TPU v7x, 128 devices: a whole 4x4x4 slice. The times are simulated.
128 devices in a mesh: row: 8 (over y, x_hi), col: 16 (over x_lo, z, core).
Axes of the slice: x: 4 (x_hi: 2, x_lo: 2; x = x_hi * 2 + x_lo), y: 4, z: 4, core: 2. Of those that a mesh axis runs over, the one named last changes fastest.
Arguments:
- traces: bfloat16 [4, 64, 4, 64, 2048], P(None, None, None, 'row', 'col'), may hold values from -6 to 6
- cell_type: int32 [64, 2048], P('row', 'col'), may hold values from 0 to 7
- port_cell: int32 [4], replicated, may hold values from 0 to 131071
- port_profile: bfloat16 [4, 64, 4], replicated, may hold values from -6 to 6
- mode_shapes: float32 [8, 256, 256], P('row', None, 'col'), may hold values from -0.375 to 0.375
- mode_values: float32 [8, 256], P('row', 'col'), may hold values from 0.3 to 1.5
- mode_weights: float32 [8, 256, 256], P('row', 'col'), may hold values from -0.375 to 0.375
Outputs:
- traces_next: bfloat16 [4, 64, 4, 64, 2048], P(None, None, None, 'row', 'col')
Inputs may be any that keep to these rules, and one draw needn't show every extreme that they name: `port_cell`: each port's cell as row * 2048 + column; two ports may share a cell.
All inputs are finite; a program needn't handle non-finite values.
Results may differ from a plain program's by a relative error of at most 0.0064.
Values may be sent and summed in bfloat16 or wider, within the bound.
No kernel may reach another device: no remote copies, remote signals or barrier semaphores. Data moves between devices by JAX's collectives and lax.ppermute only.
A program may use at most 64 MiB of HBM per device.

v0:
```python
import jax
import jax.numpy as jnp
from jax import lax
from jax.sharding import PartitionSpec as P

SWEEPS = 2


def with_halo(block, sides, width):
    for axis, dim in sides:
        count = lax.axis_size(axis)
        forward = [(i, i + 1) for i in range(count - 1)]
        backward = [(target, source) for source, target in forward]
        low = lax.ppermute(
            lax.slice_in_dim(block, block.shape[dim] - width, None, axis=dim), axis, forward
        )
        high = lax.ppermute(lax.slice_in_dim(block, 0, width, axis=dim), axis, backward)
        block = jnp.concatenate([low, block, high], axis=dim)
    return block


def received_from(outgoing):
    padded = with_halo(outgoing, (("row", 3), ("col", 4)), 1)
    north = padded[1, :, :, :-2, 1:-1]
    south = padded[0, :, :, 2:, 1:-1]
    west = padded[3, :, :, 1:-1, :-2]
    east = padded[2, :, :, 1:-1, 2:]
    return jnp.stack([north, south, west, east])


def body(traces, cell_type, port_cell, port_profile, mode_shapes, mode_values, mode_weights):
    scaled = mode_shapes * mode_values[:, None, :]
    partial_maps = jnp.einsum("tkm,tmj->tkj", scaled, mode_weights, precision=lax.Precision.HIGHEST)
    summed = lax.psum(partial_maps, "col")
    cell_maps = lax.all_gather(summed.astype(jnp.bfloat16), "row", axis=0, tiled=True)
    edges, samples, ports, tile_rows, tile_cols = traces.shape
    order = edges * samples
    ntypes = cell_maps.shape[0]
    total = tile_rows * tile_cols
    type_row = jnp.broadcast_to(cell_type.reshape(1, total), (ports, total)).reshape(
        1, ports * total
    )
    row_first = lax.axis_index("row") * tile_rows
    col_first = lax.axis_index("col") * tile_cols
    all_cols = tile_cols * lax.axis_size("col")
    local_rows = port_cell // all_cols - row_first
    local_cols = port_cell % all_cols - col_first
    inside = (
        (local_rows >= 0) & (local_rows < tile_rows) & (local_cols >= 0) & (local_cols < tile_cols)
    )
    safe_rows = jnp.clip(local_rows, 0, tile_rows - 1)
    safe_cols = jnp.clip(local_cols, 0, tile_cols - 1)
    port_index = jnp.arange(ports, dtype=jnp.int32)
    incoming = traces
    for sweep_index in range(SWEEPS):
        flat = incoming.reshape(order, ports * total)
        result = jnp.zeros((order, ports * total), jnp.float32)
        for type_index in range(ntypes):
            product = jnp.dot(cell_maps[type_index], flat, preferred_element_type=jnp.float32)
            result = jnp.where(type_row == type_index, product, result)
        outgoing = result.astype(jnp.bfloat16).reshape(incoming.shape)
        received = received_from(outgoing)
        current = received[:, :, port_index, safe_rows, safe_cols]
        added = (current.astype(jnp.float32) + port_profile.astype(jnp.float32)).astype(
            jnp.bfloat16
        )
        updated = jnp.where(inside[None, None, :], added, current)
        incoming = received.at[:, :, port_index, safe_rows, safe_cols].set(updated)
    return incoming


def solution(mesh):
    return jax.shard_map(
        body,
        mesh=mesh,
        in_specs=(
            P(None, None, None, "row", "col"),
            P("row", "col"),
            P(),
            P(),
            P("row", None, "col"),
            P("row", "col"),
            P("row", "col", None),
        ),
        out_specs=P(None, None, None, "row", "col"),
        check_vma=False,
    )
```

profile of v0, /device:TPU:0, one launch (start us, length us, event | category | flops | bytes accessed | tf_op | source)
XLA Modules:
  0.0 285.2 jit_solution(2126994691876220879)
XLA Ops:
  6.5 0.0 copy-start
  6.5 0.0 all-gather.2.cloned.1.call-start
  6.5 0.7 copy-done
  7.3 1.2 convolution_bitcast_fusion
  8.5 60.2 %all-reduce.1 = bf16[1,256,256]{2,1,0:T(8,128)(2,1)} all-reduce(f32[1,256,256]{2,1,0:T(8,128)S(1)} %convolution_bitcast_fusion), channel_id=1, replica_groups=mesh['row'=8,'col'=16] {'col'}, use_global_device_ids=true, to_apply=%region_0.0 | all-reduce | flops 65536 | bytes 393216 | tf_op jit(solution)/shard_map/psum | solution.py:34
  68.6 0.0 all-gather.2.cloned.1.call-update
  68.6 0.7 compare_bitcast_fusion.7
  69.4 2.8 reshape.116
  72.4 41.3 %all-gather.2.cloned.1.call-done = bf16[8,256,256]{2,1,0:T(8,128)(2,1)} async-done(((bf16[1,256,256]{2,1,0:T(8,128)(2,1)}), bf16[8,256,256]{2,1,0:T(8,128)(2,1)}) %all-gather.2.cloned.1.call-update) | async-done | bytes 1048592 | tf_op jit(solution)/shard_map/all_gather | solution.py:35
  113.6 1.7 convolution_select_fusion.8
  115.4 0.8 convolution_select_fusion.9
  116.2 0.8 convolution_select_fusion.10
  117.0 0.8 convolution_select_fusion.11
  117.9 0.8 convolution_select_fusion.12
  118.7 0.8 convolution_select_fusion.13
  119.6 0.8 convolution_select_fusion.14
  120.4 0.8 fusion.31
  121.2 0.5 copy.55
  121.7 0.0 copy-start.6
  121.7 3.9 %copy.33 = bf16[4,64,4,8,128]{1,0,4,3,2:T(4,128)(2,1)} copy(bf16[4,64,4,8,128]{4,3,2,1,0:T(8,128)(2,1)S(1)} %bitcast.157) | data formatting | bytes 4194304 | tf_op jit(solution)/shard_map/reshape | solution.py:61
  125.7 1.6 fusion.54
  127.2 2.5 collective-permute-start
  129.7 1.3 collective-permute-start.1
  131.0 0.0 copy-done.6
  131.0 0.0 copy-start.2
  131.1 8.4 %collective-permute-done = bf16[4,64,4,1,128]{1,0,4,3,2:T(4,128)(2,1)S(1)} collective-permute-done((bf16[4,64,4,1,128]{1,0,4,3,2:T(4,128)(2,1)S(1)}, bf16[4,64,4,1,128]{1,0,4,3,2:T(4,128)(2,1)S(1)}, u32[]{:S(2)}, u32[]{:S(2)}) %collective-permute-start) | collective-permute-done | bytes 262176 | tf_op jit(solution)/shard_map/ppermute | solution.py:14
  139.4 15.0 %collective-permute-done.1 = bf16[4,64,4,1,128]{1,0,4,3,2:T(4,128)(2,1)S(1)} collective-permute-done((bf16[4,64,4,1,128]{1,0,4,3,2:T(4,128)(2,1)S(1)}, bf16[4,64,4,1,128]{1,0,4,3,2:T(4,128)(2,1)S(1)}, u32[]{:S(2)}, u32[]{:S(2)}) %collective-permute-start.1) | collective-permute-done | bytes 262176 | tf_op jit(solution)/shard_map/ppermute | solution.py:17
  154.4 0.9 pad_maximum_fusion.5
  155.3 1.3 collective-permute-start.2
  156.6 1.5 collective-permute-start.3
  158.1 0.0 copy-start.5
  158.1 0.0 collective-permute-done.2
  158.1 3.4 %collective-permute-done.3 = bf16[4,64,4,10,1]{1,0,4,3,2:T(4,128)(2,1)S(1)} collective-permute-done((bf16[4,64,4,10,1]{1,0,4,3,2:T(4,128)(2,1)S(1)}, bf16[4,64,4,10,1]{1,0,4,3,2:T(4,128)(2,1)S(1)}, u32[]{:S(2)}, u32[]{:S(2)}) %collective-permute-start.3) | collective-permute-done | bytes 20512 | tf_op jit(solution)/shard_map/ppermute | solution.py:17
  161.5 0.0 copy-done.2
  161.5 23.4 %fusion.19 = bf16[4,64,4,8,128]{1,0,4,3,2:T(4,128)(2,1)} fusion(bf16[4,64,4,10,1]{1,0,4,3,2:T(4,128)(2,1)S(1)} %collective-permute-done.3, bf16[4,64,4,1,128]{1,0,4,3,2:T(4,128)(2,1)S(1)} %collective-permute-done.1, bf16[4,64,4,8,128]{1,0,4,3,2:T(4,128)(2,1)S(1)} %copy-done.2, bf16[4,64,4,1,128]{1,0,4,3,2:T(4,128)(2,1)S(1)} %collective-permute-done, ...), kind=kLoop, calls=%fused_computation.45 | loop fusion | flops 46137344 | bytes 4759552 | tf_op jit(solution)/shard_map/stack | solution.py:28
  184.9 2.8 gather_fusion
  187.6 0.1 fusion.40
  187.7 1.8 scatter_fusion
  189.5 6.0 %reshape.144 = bf16[256,4096]{0,1:T(8,128)(2,1)S(1)} reshape(bf16[4,64,4,8,128]{1,0,4,3,2:T(4,128)(2,1)} %scatter_fusion) | data formatting | bytes 4194304 | tf_op jit(solution)/shard_map/reshape | solution.py:56
  195.5 0.7 convolution_select_fusion
  196.2 0.8 convolution_select_fusion.1
  197.0 0.8 convolution_select_fusion.2
  197.8 0.8 convolution_select_fusion.3
  198.5 0.8 convolution_select_fusion.4
  199.3 0.8 convolution_select_fusion.5
  200.1 0.8 convolution_select_fusion.6
  200.9 0.8 fusion.30
  201.6 0.5 copy.56
  202.1 3.9 %copy.40 = bf16[4,64,4,8,128]{1,0,4,3,2:T(4,128)(2,1)} copy(bf16[4,64,4,8,128]{4,3,2,1,0:T(8,128)(2,1)S(1)} %bitcast.158) | data formatting | bytes 4194304 | tf_op jit(solution)/shard_map/reshape | solution.py:61
  206.1 1.7 fusion.53
  207.8 2.5 collective-permute-start.4
  210.3 1.3 collective-permute-start.5
  211.6 9.2 %collective-permute-done.4 = bf16[4,64,4,1,128]{1,0,4,3,2:T(4,128)(2,1)S(1)} collective-permute-done((bf16[4,64,4,1,128]{1,0,4,3,2:T(4,128)(2,1)S(1)}, bf16[4,64,4,1,128]{1,0,4,3,2:T(4,128)(2,1)S(1)}, u32[]{:S(2)}, u32[]{:S(2)}) %collective-permute-start.4) | collective-permute-done | bytes 262176 | tf_op jit(solution)/shard_map/ppermute | solution.py:14
  220.8 14.6 %collective-permute-done.5 = bf16[4,64,4,1,128]{1,0,4,3,2:T(4,128)(2,1)S(1)} collective-permute-done((bf16[4,64,4,1,128]{1,0,4,3,2:T(4,128)(2,1)S(1)}, bf16[4,64,4,1,128]{1,0,4,3,2:T(4,128)(2,1)S(1)}, u32[]{:S(2)}, u32[]{:S(2)}) %collective-permute-start.5) | collective-permute-done | bytes 262176 | tf_op jit(solution)/shard_map/ppermute | solution.py:17
  235.4 0.9 pad_maximum_fusion.2
  236.2 3.5 %collective-permute-start.6 = (bf16[4,64,4,10,1]{1,0,4,3,2:T(4,128)(2,1)S(1)}, bf16[4,64,4,10,1]{1,0,4,3,2:T(4,128)(2,1)S(1)}, u32[]{:S(2)}, u32[]{:S(2)}) collective-permute-start(bf16[4,64,4,10,1]{1,0,4,3,2:T(4,128)(2,1)S(1)} %get-tuple-element.8), channel_id=1, source_target_pairs={{0,1},{1,2},{2,3},{3,4},{4,5},{5,6},{6,7},{7,8},{8,9},{9,10},{10,1... | collective-permute-start | bytes 61448 | tf_op jit(solution)/shard_map/ppermute | solution.py:14
  239.8 1.5 collective-permute-start.7
  241.3 0.0 collective-permute-done.6
  241.3 3.3 %collective-permute-done.7 = bf16[4,64,4,10,1]{1,0,4,3,2:T(4,128)(2,1)S(1)} collective-permute-done((bf16[4,64,4,10,1]{1,0,4,3,2:T(4,128)(2,1)S(1)}, bf16[4,64,4,10,1]{1,0,4,3,2:T(4,128)(2,1)S(1)}, u32[]{:S(2)}, u32[]{:S(2)}) %collective-permute-start.7) | collective-permute-done | bytes 20512 | tf_op jit(solution)/shard_map/ppermute | solution.py:17
  244.6 23.5 %fusion.23 = bf16[4,64,4,8,128]{1,0,4,3,2:T(4,128)(2,1)} fusion(bf16[4,64,4,10,1]{1,0,4,3,2:T(4,128)(2,1)S(1)} %collective-permute-done.7, bf16[4,64,4,1,128]{1,0,4,3,2:T(4,128)(2,1)S(1)} %collective-permute-done.5, bf16[4,64,4,8,128]{1,0,4,3,2:T(4,128)(2,1)S(1)} %copy-done.3, bf16[4,64,4,1,128]{1,0,4,3,2:T(4,128)(2,1)S(1)} %collective-permute-done.4, ...), kind=kLoop, calls=%fused_computation.49 | loop fusion | flops 46137344 | bytes 4759552 | tf_op jit(solution)/shard_map/stack | solution.py:28
  268.1 2.8 gather_fusion.1
  270.9 0.1 fusion.41
  271.0 1.8 scatter_fusion.1
  272.7 5.6 %copy.45 = bf16[4,64,4,8,128]{4,3,2,1,0:T(8,128)(2,1)} copy(bf16[4,64,4,8,128]{1,0,4,3,2:T(4,128)(2,1)} %scatter_fusion.1) | data formatting | bytes 4194304 | tf_op jit(solution)/shard_map/scatter | solution.py:68
  (21 shorter events, 0.1 us)
Async XLA Ops:
  6.5 0.7 copy-start
  6.5 107.1 %all-gather.2.cloned.1.call-start = ((), (), s32[]{:S(2)}) async-start(), calls=%async_computation | async-start | bytes 1179648 | tf_op jit(solution)/shard_map/all_gather | solution.py:35
  113.6 1.7 copy-start.4
  121.7 9.3 %copy-start.6 = (s32[4]{0:T(128)S(1)}, s32[4]{0:T(128)}, u32[]{:S(2)}) copy-start(s32[4]{0:T(128)} %param.9) | copy-start | bytes 52
  127.2 12.2 %collective-permute-start = (bf16[4,64,4,1,128]{1,0,4,3,2:T(4,128)(2,1)S(1)}, bf16[4,64,4,1,128]{1,0,4,3,2:T(4,128)(2,1)S(1)}, u32[]{:S(2)}, u32[]{:S(2)}) collective-permute-start(bf16[4,64,4,1,128]{1,0,4,3,2:T(4,128)(2,1)S(1)} %get-tuple-element.14), channel_id=1, source_target_pairs={{0,16},{16,32},{32,48},{48,64},{64,80},{80,96},{96,112},{1,17},{17... | collective-permute-start | bytes 786440 | tf_op jit(solution)/shard_map/ppermute | solution.py:14
  129.7 24.7 %collective-permute-start.1 = (bf16[4,64,4,1,128]{1,0,4,3,2:T(4,128)(2,1)S(1)}, bf16[4,64,4,1,128]{1,0,4,3,2:T(4,128)(2,1)S(1)}, u32[]{:S(2)}, u32[]{:S(2)}) collective-permute-start(bf16[4,64,4,1,128]{1,0,4,3,2:T(4,128)(2,1)S(1)} %get-tuple-element.15), channel_id=1, source_target_pairs={{16,0},{32,16},{48,32},{64,48},{80,64},{96,80},{112,96},{17,1},{33... | collective-permute-start | bytes 786440 | tf_op jit(solution)/shard_map/ppermute | solution.py:17
  131.0 30.5 %copy-start.2 = (bf16[4,64,4,8,128]{1,0,4,3,2:T(4,128)(2,1)S(1)}, bf16[4,64,4,8,128]{1,0,4,3,2:T(4,128)(2,1)}, u32[]{:S(2)}) copy-start(bf16[4,64,4,8,128]{1,0,4,3,2:T(4,128)(2,1)} %copy.33) | copy-start | bytes 6291460
  155.3 2.8 collective-permute-start.2
  156.6 4.9 %collective-permute-start.3 = (bf16[4,64,4,10,1]{1,0,4,3,2:T(4,128)(2,1)S(1)}, bf16[4,64,4,10,1]{1,0,4,3,2:T(4,128)(2,1)S(1)}, u32[]{:S(2)}, u32[]{:S(2)}) collective-permute-start(bf16[4,64,4,10,1]{1,0,4,3,2:T(4,128)(2,1)S(1)} %get-tuple-element.11), channel_id=1, source_target_pairs={{1,0},{2,1},{3,2},{4,3},{5,4},{6,5},{7,6},{8,7},{9,8},{10,9},{11,1... | collective-permute-start | bytes 61448 | tf_op jit(solution)/shard_map/ppermute | solution.py:17
  158.1 29.5 %copy-start.5 = (bf16[4,64,4]{1,2,0:T(4,128)(2,1)S(1)}, bf16[4,64,4]{1,2,0:T(4,128)(2,1)}, u32[]{:S(2)}) copy-start(bf16[4,64,4]{1,2,0:T(4,128)(2,1)} %param.10) | copy-start | bytes 6148
  206.1 38.5 %copy-start.3 = (bf16[4,64,4,8,128]{1,0,4,3,2:T(4,128)(2,1)S(1)}, bf16[4,64,4,8,128]{1,0,4,3,2:T(4,128)(2,1)}, u32[]{:S(2)}) copy-start(bf16[4,64,4,8,128]{1,0,4,3,2:T(4,128)(2,1)} %copy.40) | copy-start | bytes 6291460
  207.8 13.0 %collective-permute-start.4 = (bf16[4,64,4,1,128]{1,0,4,3,2:T(4,128)(2,1)S(1)}, bf16[4,64,4,1,128]{1,0,4,3,2:T(4,128)(2,1)S(1)}, u32[]{:S(2)}, u32[]{:S(2)}) collective-permute-start(bf16[4,64,4,1,128]{1,0,4,3,2:T(4,128)(2,1)S(1)} %get-tuple-element.12), channel_id=1, source_target_pairs={{0,16},{16,32},{32,48},{48,64},{64,80},{80,96},{96,112},{1,17},{17... | collective-permute-start | bytes 786440 | tf_op jit(solution)/shard_map/ppermute | solution.py:14
  210.3 25.1 %collective-permute-start.5 = (bf16[4,64,4,1,128]{1,0,4,3,2:T(4,128)(2,1)S(1)}, bf16[4,64,4,1,128]{1,0,4,3,2:T(4,128)(2,1)S(1)}, u32[]{:S(2)}, u32[]{:S(2)}) collective-permute-start(bf16[4,64,4,1,128]{1,0,4,3,2:T(4,128)(2,1)S(1)} %get-tuple-element.13), channel_id=1, source_target_pairs={{16,0},{32,16},{48,32},{64,48},{80,64},{96,80},{112,96},{17,1},{33... | collective-permute-start | bytes 786440 | tf_op jit(solution)/shard_map/ppermute | solution.py:17
  236.2 5.1 %collective-permute-start.6 = (bf16[4,64,4,10,1]{1,0,4,3,2:T(4,128)(2,1)S(1)}, bf16[4,64,4,10,1]{1,0,4,3,2:T(4,128)(2,1)S(1)}, u32[]{:S(2)}, u32[]{:S(2)}) collective-permute-start(bf16[4,64,4,10,1]{1,0,4,3,2:T(4,128)(2,1)S(1)} %get-tuple-element.8), channel_id=1, source_target_pairs={{0,1},{1,2},{2,3},{3,4},{4,5},{5,6},{6,7},{7,8},{8,9},{9,10},{10,1... | collective-permute-start | bytes 61448 | tf_op jit(solution)/shard_map/ppermute | solution.py:14
  239.8 4.8 %collective-permute-start.7 = (bf16[4,64,4,10,1]{1,0,4,3,2:T(4,128)(2,1)S(1)}, bf16[4,64,4,10,1]{1,0,4,3,2:T(4,128)(2,1)S(1)}, u32[]{:S(2)}, u32[]{:S(2)}) collective-permute-start(bf16[4,64,4,10,1]{1,0,4,3,2:T(4,128)(2,1)S(1)} %get-tuple-element.9), channel_id=1, source_target_pairs={{1,0},{2,1},{3,2},{4,3},{5,4},{6,5},{7,6},{8,7},{9,8},{10,9},{11,1... | collective-permute-start | bytes 61448 | tf_op jit(solution)/shard_map/ppermute | solution.py:17
  244.6 33.7 %copy-start.1 = (f32[1,16,256]{2,1,0:T(8,128)S(1)}, f32[1,16,256]{2,1,0:T(8,128)}, u32[]{:S(2)}) copy-start(f32[1,16,256]{2,1,0:T(8,128)} %param.13) | copy-start | bytes 49156
Sparse Core Ops, SparseCore 0:
  68.8 44.8 all-gather.1
where the time goes:
time: 290 us; the launch traced here: 285 us
  waiting for transfers between devices  95.2 us (33%)
  blocking collectives  60.2 us (21%)
  other arithmetic  49.5 us (17%)
  local copies, waits for them, and re-layouts  36.5 us (13%)
  starting transfers between devices  15.4 us (5%)
  matrix products  14.8 us (5%)
  between operations  13.8 us (5%)
    psum x1, blocking collectives, body(): summed = lax.psum(partial_maps, 'col')  60.2 us
    another operation x2, other arithmetic, received_from(): return jnp.stack([north, south, west, east])  46.9 us
    all_gather x1, waiting for transfers between devices, body(): lax.all_gather(summed.astype(jnp.bfloat16), 'row', axis=0, tiled=True)  41.3 us
    ppermute x4, waiting for transfers between devices, with_halo(): lax.ppermute(lax.slice_in_dim(block, 0, width, axis=dim), axis, backward)  36.3 us
    ppermute x4, waiting for transfers between devices, with_halo(): lax.ppermute(lax.slice_in_dim(block, block.shape[dim] - width, None, axis...  17.5 us
    dot_general x16, matrix products, body(): jnp.dot(cell_maps[type_index], flat, preferred_element_type=jnp.float32)  13.6 us
    ppermute x4, starting transfers between devices, with_halo(): lax.ppermute(lax.slice_in_dim(block, block.shape[dim] - width, None, axis...  9.81 us
    scatter x3, local copies, waits for them, and re-layouts, body(): incoming = received.at[:, :, port_index, safe_rows, safe_cols].set(updated)  9.19 us
  transfers between devices with their start and end apart: 9, of which 7 were waited for; matrix products, arithmetic and copies ran while one was open for 1% of the time, Pallas kernels for 0%

commit v1 on v0

v1 whole, which is shorter than its diff:
```python
import functools

import jax
import jax.numpy as jnp
from jax import lax
from jax.experimental import pallas as pl
from jax.experimental.pallas import tpu as pltpu
from jax.sharding import PartitionSpec as P

BF = jnp.bfloat16
F32 = jnp.float32
LANES = 128


def gather_modes(mode_shapes, mode_values, mode_weights):
    scaled = (mode_shapes * mode_values[:, None, :])[0].T
    own = jnp.concatenate([scaled, mode_weights[0]], axis=0)
    count = lax.axis_size("col")
    spread = jnp.broadcast_to(own[None], (count,) + own.shape)
    every = lax.all_to_all(spread, "col", 0, 0, tiled=True)
    modes = scaled.shape[0]
    left = every[:, :modes].reshape(count * modes, -1)
    right = every[:, modes:].reshape(count * modes, -1)
    return left, right


def all_maps(mode_shapes, mode_values, mode_weights):
    left, right = gather_modes(mode_shapes, mode_values, mode_weights)
    own_map = lax.dot_general(
        left, right, (((0,), (0,)), ((), ())), precision=lax.Precision.HIGHEST
    ).astype(BF)
    count = lax.axis_size("row")
    maps = [own_map]
    for step in range(1, count):
        pairs = [(i, (i + step) % count) for i in range(count)]
        maps.append(lax.ppermute(own_map, "row", pairs))
    return maps


def patch(block, rows, width, port_ref, profile_ref, halo_refs):
    north, south, west, east = halo_refs
    quarter = block.shape[0] // 4
    port = pl.program_id(0)
    lane = lax.broadcasted_iota(jnp.int32, (quarter, LANES), 1)
    block[0:quarter, 0:LANES] = north[...]
    block[quarter : 2 * quarter, (rows - 1) * LANES : rows * LANES] = south[...]
    west_all = west[...].astype(F32)
    east_all = east[...].astype(F32)
    for row in range(rows):
        place = port * rows + row
        cols = slice(row * LANES, (row + 1) * LANES)
        from_west = pltpu.roll(west_all, (LANES - place) % LANES, 1)
        from_east = pltpu.roll(east_all, LANES - 1 - place, 1)
        west_part = block[2 * quarter : 3 * quarter, cols].astype(F32)
        east_part = block[3 * quarter : 4 * quarter, cols].astype(F32)
        block[2 * quarter : 3 * quarter, cols] = jnp.where(lane == 0, from_west, west_part).astype(BF)
        block[3 * quarter : 4 * quarter, cols] = jnp.where(
            lane == LANES - 1, from_east, east_part
        ).astype(BF)
    all_cols = width * lax.axis_size("col")
    cell = port_ref[port]
    row = cell // all_cols - lax.axis_index("row") * rows
    col = cell % all_cols - lax.axis_index("col") * width

    @pl.when((row >= 0) & (row < rows) & (col >= 0) & (col < width))
    def _():
        cols = pl.ds(pl.multiple_of(row * LANES, LANES), LANES)
        here = lax.broadcasted_iota(jnp.int32, (4 * quarter, LANES), 1) == col
        current = block[:, cols].astype(F32)
        added = current + profile_ref[0].astype(F32)
        block[:, cols] = jnp.where(here, added, current).astype(BF)


def apply_maps(x, types_ref, map_refs, next_ref, rim_refs, rows):
    north_out, south_out, west_out, east_out = rim_refs
    order = x.shape[0]
    quarter = order // 4
    kinds = len(map_refs)
    port = pl.program_id(0)
    mine = lax.axis_index("row")
    types = jnp.broadcast_to(types_ref[...].astype(F32).astype(BF), x.shape)
    total = None
    for step in range(kinds):
        kind = lax.rem(mine - step + kinds, kinds).astype(F32).astype(BF)
        masked = jnp.where(types == kind, x, jnp.zeros((), BF))
        product = jnp.dot(map_refs[step][...], masked, preferred_element_type=F32)
        total = product if total is None else total + product
    last = (rows - 1) * LANES
    north = total[0:quarter].astype(BF)
    south = total[quarter : 2 * quarter].astype(BF)
    north_out[...] = north[:, 0:LANES]
    south_out[...] = south[:, last:]
    next_ref[0:quarter, LANES:] = south[:, :last]
    next_ref[0:quarter, 0:LANES] = jnp.zeros((quarter, LANES), BF)
    next_ref[quarter : 2 * quarter, :last] = north[:, LANES:]
    next_ref[quarter : 2 * quarter, last:] = jnp.zeros((quarter, LANES), BF)
    lane = lax.broadcasted_iota(jnp.int32, (quarter, LANES), 1)
    west_rim = jnp.where(port == 0, 0.0, west_out[...].astype(F32))
    east_rim = jnp.where(port == 0, 0.0, east_out[...].astype(F32))
    for row in range(rows):
        place = port * rows + row
        cols = slice(row * LANES, (row + 1) * LANES)
        west = total[2 * quarter : 3 * quarter, cols]
        east = total[3 * quarter : 4 * quarter, cols]
        next_ref[2 * quarter : 3 * quarter, cols] = pltpu.roll(east, 1, 1).astype(BF)
        next_ref[3 * quarter : 4 * quarter, cols] = pltpu.roll(west, LANES - 1, 1).astype(BF)
        west_rim = jnp.where(lane == place, pltpu.roll(west, place, 1), west_rim)
        east_rim = jnp.where(lane == place, pltpu.roll(east, place + 1, 1), east_rim)
    west_out[...] = west_rim.astype(BF)
    east_out[...] = east_rim.astype(BF)


def first_kernel(rows, x_ref, types_ref, *refs):
    apply_maps(x_ref[...], types_ref, refs[:-5], refs[-5], refs[-4:], rows)


def second_kernel(rows, width, port_ref, x_ref, types_ref, profile_ref, *refs):
    halo_refs, refs = refs[:4], refs[4:]
    block = refs[-1]
    block[...] = x_ref[...]
    patch(block, rows, width, port_ref, profile_ref, halo_refs)
    apply_maps(block[...], types_ref, refs[:-6], refs[-6], refs[-5:-1], rows)


def last_kernel(rows, width, port_ref, x_ref, profile_ref, *refs):
    out_ref = refs[-1]
    out_ref[...] = x_ref[...]
    patch(out_ref, rows, width, port_ref, profile_ref, refs[:4])


def exchange(rims):
    north, south, west, east = rims

    def send(value, axis, step):
        count = lax.axis_size(axis)
        pairs = [(i, i + step) for i in range(count) if 0 <= i + step < count]
        return lax.ppermute(value, axis, pairs)

    return (
        send(south, "row", 1),
        send(north, "row", -1),
        send(east, "col", 1),
        send(west, "col", -1),
    )


def body(traces, cell_type, port_cell, port_profile, mode_shapes, mode_values, mode_weights):
    edges, samples, ports, rows, width = traces.shape
    order = edges * samples
    quarter = samples
    tile = rows * width
    maps = all_maps(mode_shapes, mode_values, mode_weights)
    x = traces.reshape(order, ports * tile)
    types = cell_type.reshape(1, tile)
    profile = jnp.broadcast_to(
        jnp.transpose(port_profile.reshape(order, ports))[:, :, None], (ports, order, LANES)
    )
    block = pl.BlockSpec((order, tile), lambda i: (0, i))
    types_spec = pl.BlockSpec((1, tile), lambda i: (0, 0))
    map_specs = [pl.BlockSpec((order, order), lambda i: (0, 0))] * len(maps)
    long_rim = pl.BlockSpec((quarter, LANES), lambda i: (0, i))
    short_rim = pl.BlockSpec((quarter, LANES), lambda i: (0, 0))
    rims = [long_rim, long_rim, short_rim, short_rim]
    ports_spec = pl.BlockSpec(memory_space=pltpu.SMEM)
    profile_spec = pl.BlockSpec((1, order, LANES), lambda i: (i, 0, 0))
    next_shape = jax.ShapeDtypeStruct((order, ports * tile), BF)
    rim_shapes = [jax.ShapeDtypeStruct((quarter, ports * LANES), BF)] * 2 + [
        jax.ShapeDtypeStruct((quarter, LANES), BF)
    ] * 2
    params = pltpu.CompilerParams(vmem_limit_bytes=40 * 2**20)
    x, *sent = pl.pallas_call(
        functools.partial(first_kernel, rows),
        grid=(ports,),
        in_specs=[block, types_spec] + map_specs,
        out_specs=[block] + rims,
        out_shape=[next_shape] + rim_shapes,
        compiler_params=params,
    )(x, types, *maps)
    halos = exchange(sent)
    x, *sent = pl.pallas_call(
        functools.partial(second_kernel, rows, width),
        grid=(ports,),
        in_specs=[ports_spec, block, types_spec, profile_spec] + rims + map_specs,
        out_specs=[block] + rims,
        out_shape=[next_shape] + rim_shapes,
        scratch_shapes=[pltpu.VMEM((order, tile), BF)],
        compiler_params=params,
    )(port_cell, x, types, profile, *halos, *maps)
    halos = exchange(sent)
    x = pl.pallas_call(
        functools.partial(last_kernel, rows, width),
        grid=(ports,),
        in_specs=[ports_spec, block, profile_spec] + rims,
        out_specs=block,
        out_shape=next_shape,
        compiler_params=params,
    )(port_cell, x, profile, *halos)
    return x.reshape(traces.shape)


def solution(mesh):
    return jax.shard_map(
        body,
        mesh=mesh,
        in_specs=(
            P(None, None, None, "row", "col"),
            P("row", "col"),
            P(),
            P(),
            P("row", None, "col"),
            P("row", "col"),
            P("row", "col", None),
        ),
        out_specs=P(None, None, None, "row", "col"),
        check_vma=False,
    )
```

time: 290 us -> 94.9 us (0.33)
  the two profiles are of different devices: /device:TPU:0 before, /device:TPU:113 now
where the time goes in v1:
time: 94.9 us; the launch traced here: 94.4 us
  starting transfers between devices  39.1 us (41%)
  waiting for transfers between devices  16 us (17%)
  Pallas kernels  14.6 us (15%)
  blocking collectives  14.4 us (15%)
  local copies, waits for them, and re-layouts  7.88 us (8%)
  other arithmetic  1.51 us (2%)
    ppermute x8, starting transfers between devices, send(): return lax.ppermute(value, axis, pairs)  26.4 us
    all_to_all x1, blocking collectives, gather_modes(): every = lax.all_to_all(spread, 'col', 0, 0, tiled=True)  14.4 us
    ppermute x7, starting transfers between devices, all_maps(): maps.append(lax.ppermute(own_map, 'row', pairs))  12.7 us
    ppermute x8, waiting for transfers between devices, send(): return lax.ppermute(value, axis, pairs)  10.4 us
    pallas_call x1, Pallas kernels, body(): pl.pallas_call(functools.partial(second_kernel, rows, width), grid=(ports...  7.16 us
    pallas_call x1, Pallas kernels, body(): pl.pallas_call(functools.partial(first_kernel, rows), grid=(ports,), in_s...  5.93 us
    ppermute x7, waiting for transfers between devices, all_maps(): maps.append(lax.ppermute(own_map, 'row', pairs))  5.67 us
    unnamed x12, local copies, waits for them, and re-layouts  4.73 us
  transfers between devices with their start and end apart: 15, of which 3 were waited for; matrix products, arithmetic and copies ran while one was open for 3% of the time, Pallas kernels for 0%

profile of v1, /device:TPU:113, one launch (start us, length us, event | category | flops | bytes accessed | tf_op | source)
XLA Modules:
  0.0 94.4 jit_solution(631076419802353040)
XLA Ops:
  0.0 0.8 multiply_bitcast_fusion
  0.8 0.7 pad_maximum_fusion
  1.6 14.4 %all_to_all.5 = f32[16,32,256]{2,1,0:T(8,128)S(1)} all-to-all(f32[16,32,256]{2,1,0:T(8,128)S(1)} %broadcast_in_dim.4), channel_id=1, replica_groups=mesh['row'=8,'col'=16] {'col'}, dimensions={0} | all-to-all | bytes 1048576 | tf_op jit(solution)/shard_map/all_to_all | solution.py:20
  16.0 0.6 fusion.refs_0_.refs_4_
  16.6 0.0 copy-start.2
  16.6 2.4 %collective-permute-start.6 = (bf16[256,256]{1,0:T(8,128)(2,1)S(1)}, bf16[256,256]{1,0:T(8,128)(2,1)S(1)}, u32[]{:S(2)}, u32[]{:S(2)}) collective-permute-start(bf16[256,256]{1,0:T(8,128)(2,1)S(1)} %fusion.refs_0_.refs_4_), channel_id=1, source_target_pairs={{0,112},{16,0},{32,16},{48,32},{64,48},{80,64},{96,80},{112,96},{1... | collective-permute-start | bytes 393224 | tf_op jit(solution)/shard_map/ppermute | solution.py:36
  19.0 0.2 collective-permute-start.5
  19.2 3.0 %collective-permute-start.4 = (bf16[256,256]{1,0:T(8,128)(2,1)S(1)}, bf16[256,256]{1,0:T(8,128)(2,1)S(1)}, u32[]{:S(2)}, u32[]{:S(2)}) collective-permute-start(bf16[256,256]{1,0:T(8,128)(2,1)S(1)} %fusion.refs_0_.refs_4_), channel_id=1, source_target_pairs={{0,80},{16,96},{32,112},{48,0},{64,16},{80,32},{96,48},{112,64},{1... | collective-permute-start | bytes 393224 | tf_op jit(solution)/shard_map/ppermute | solution.py:36
  22.1 0.3 collective-permute-start.3
  22.5 4.1 %collective-permute-start.2 = (bf16[256,256]{1,0:T(8,128)(2,1)S(1)}, bf16[256,256]{1,0:T(8,128)(2,1)S(1)}, u32[]{:S(2)}, u32[]{:S(2)}) collective-permute-start(bf16[256,256]{1,0:T(8,128)(2,1)S(1)} %fusion.refs_0_.refs_4_), channel_id=1, source_target_pairs={{0,48},{16,64},{32,80},{48,96},{64,112},{80,0},{96,16},{112,32},{1... | collective-permute-start | bytes 393224 | tf_op jit(solution)/shard_map/ppermute | solution.py:36
  26.6 0.0 collective-permute-done.6.refs_7_.refs_11_
  26.6 1.6 %collective-permute-start.1 = (bf16[256,256]{1,0:T(8,128)(2,1)S(1)}, bf16[256,256]{1,0:T(8,128)(2,1)S(1)}, u32[]{:S(2)}, u32[]{:S(2)}) collective-permute-start(bf16[256,256]{1,0:T(8,128)(2,1)S(1)} %fusion.refs_0_.refs_4_), channel_id=1, source_target_pairs={{0,32},{16,48},{32,64},{48,80},{64,96},{80,112},{96,0},{112,16},{1... | collective-permute-start | bytes 393224 | tf_op jit(solution)/shard_map/ppermute | solution.py:36
  28.2 0.0 collective-permute-done.5.refs_6_.refs_10_
  28.2 1.1 %collective-permute-start = (bf16[256,256]{1,0:T(8,128)(2,1)S(1)}, bf16[256,256]{1,0:T(8,128)(2,1)S(1)}, u32[]{:S(2)}, u32[]{:S(2)}) collective-permute-start(bf16[256,256]{1,0:T(8,128)(2,1)S(1)} %fusion.refs_0_.refs_4_), channel_id=1, source_target_pairs={{0,16},{16,32},{32,48},{48,64},{64,80},{80,96},{96,112},{112,0},{1... | collective-permute-start | bytes 393224 | tf_op jit(solution)/shard_map/ppermute | solution.py:36
  29.3 2.8 %reshape.19.x_ref = bf16[256,4096]{1,0:T(8,128)(2,1)S(1)} reshape(bf16[4,64,4,8,128]{4,3,2,1,0:T(8,128)(2,1)} %param.7) | data formatting | bytes 4194304 | tf_op jit(solution)/shard_map/reshape | solution.py:153
  32.1 0.0 copy-start.4
  32.2 0.0 copy-start.3
  32.2 0.0 collective-permute-done.4.refs_5_.refs_9_
  32.2 0.0 collective-permute-done.3.refs_4_.refs_8_
  32.2 0.0 collective-permute-done.2.refs_3_.refs_7_
  32.2 5.7 %collective-permute-done.1.refs_2_.refs_6_ = bf16[256,256]{1,0:T(8,128)(2,1)S(1)} collective-permute-done((bf16[256,256]{1,0:T(8,128)(2,1)S(1)}, bf16[256,256]{1,0:T(8,128)(2,1)S(1)}, u32[]{:S(2)}, u32[]{:S(2)}) %collective-permute-start.1) | collective-permute-done | bytes 131104 | tf_op jit(solution)/shard_map/ppermute | solution.py:36
  37.9 0.0 collective-permute-done.refs_1_.refs_5_
  37.9 0.0 copy-done.2
  37.9 5.9 %shard_map.73 = (bf16[256,4096]{1,0:T(8,128)(2,1)S(1)}, bf16[64,512]{1,0:T(8,128)(2,1)S(1)}, bf16[64,512]{1,0:T(8,128)(2,1)S(1)}, bf16[64,128]{1,0:T(8,128)(2,1)S(1)}, bf16[64,128]{1,0:T(8,128)(2,1)S(1)}) custom-call(bf16[256,4096]{1,0:T(8,128)(2,1)S(1)} %reshape.19.x_ref, s32[1,1024]{1,0:T(1,128)S(1)} %bitcast.20, ...), custom_call_target="tpu_custom_call" | custom-call | tf_op jit(solution)/shard_map/pallas_call | solution.py:171
  43.8 0.0 copy-start
  43.8 1.3 %copy-done = bf16[256,4096]{1,0:T(8,128)(2,1)} copy-done((bf16[256,4096]{1,0:T(8,128)(2,1)}, bf16[256,4096]{1,0:T(8,128)(2,1)S(1)}, u32[]{:S(2)}) %copy-start) | copy-done | bytes 2097176
  45.1 3.5 %collective-permute-start.7 = (bf16[64,512]{1,0:T(8,128)(2,1)S(1)}, bf16[64,512]{1,0:T(8,128)(2,1)S(1)}, u32[]{:S(2)}, u32[]{:S(2)}) collective-permute-start(bf16[64,512]{1,0:T(8,128)(2,1)S(1)} %get-tuple-element.16), channel_id=1, source_target_pairs={{0,16},{16,32},{32,48},{48,64},{64,80},{80,96},{96,112},{1,17},{17... | collective-permute-start | bytes 196616 | tf_op jit(solution)/shard_map/ppermute | solution.py:137
  48.6 4.2 %collective-permute-start.8 = (bf16[64,512]{1,0:T(8,128)(2,1)S(1)}, bf16[64,512]{1,0:T(8,128)(2,1)S(1)}, u32[]{:S(2)}, u32[]{:S(2)}) collective-permute-start(bf16[64,512]{1,0:T(8,128)(2,1)S(1)} %get-tuple-element.17), channel_id=1, source_target_pairs={{16,0},{32,16},{48,32},{64,48},{80,64},{96,80},{112,96},{17,1},{33... | collective-permute-start | bytes 196616 | tf_op jit(solution)/shard_map/ppermute | solution.py:137
  52.8 4.7 %collective-permute-start.9 = (bf16[64,128]{1,0:T(8,128)(2,1)S(1)}, bf16[64,128]{1,0:T(8,128)(2,1)S(1)}, u32[]{:S(2)}, u32[]{:S(2)}) collective-permute-start(bf16[64,128]{1,0:T(8,128)(2,1)S(1)} %get-tuple-element.18), channel_id=1, source_target_pairs={{0,1},{1,2},{2,3},{3,4},{4,5},{5,6},{6,7},{7,8},{8,9},{9,10},{10,1... | collective-permute-start | bytes 49160 | tf_op jit(solution)/shard_map/ppermute | solution.py:137
  57.5 1.9 %collective-permute-start.10 = (bf16[64,128]{1,0:T(8,128)(2,1)S(1)}, bf16[64,128]{1,0:T(8,128)(2,1)S(1)}, u32[]{:S(2)}, u32[]{:S(2)}) collective-permute-start(bf16[64,128]{1,0:T(8,128)(2,1)S(1)} %get-tuple-element.19), channel_id=1, source_target_pairs={{1,0},{2,1},{3,2},{4,3},{5,4},{6,5},{7,6},{8,7},{9,8},{10,9},{11,1... | collective-permute-start | bytes 49160 | tf_op jit(solution)/shard_map/ppermute | solution.py:137
  59.4 0.0 copy-done.4
  59.4 0.1 reshape.21
  59.5 0.0 collective-permute-done.9.refs_2_
  59.5 5.1 %collective-permute-done.10.refs_3_ = bf16[64,128]{1,0:T(8,128)(2,1)S(1)} collective-permute-done((bf16[64,128]{1,0:T(8,128)(2,1)S(1)}, bf16[64,128]{1,0:T(8,128)(2,1)S(1)}, u32[]{:S(2)}, u32[]{:S(2)}) %collective-permute-start.10) | collective-permute-done | bytes 16416 | tf_op jit(solution)/shard_map/ppermute | solution.py:137
  64.7 0.0 collective-permute-done.7.refs_0_
  64.7 0.0 collective-permute-done.8.refs_1_
  64.7 0.2 broadcast_in_dim.5.profile_ref
  64.9 0.0 copy-done.3
  64.9 0.0 copy-start.1
  64.9 1.6 %copy-done.1 = bf16[256,4096]{1,0:T(8,128)(2,1)S(1)} copy-done((bf16[256,4096]{1,0:T(8,128)(2,1)S(1)}, bf16[256,4096]{1,0:T(8,128)(2,1)}, u32[]{:S(2)}) %copy-start.1) | copy-done | bytes 2097176
  66.5 7.2 %shard_map.74 = (bf16[256,4096]{1,0:T(8,128)(2,1)S(1)}, bf16[64,512]{1,0:T(8,128)(2,1)S(1)}, bf16[64,512]{1,0:T(8,128)(2,1)S(1)}, bf16[64,128]{1,0:T(8,128)(2,1)S(1)}, bf16[64,128]{1,0:T(8,128)(2,1)S(1)}) custom-call(s32[4]{0:T(128)S(1)} %copy-done.3, bf16[256,4096]{1,0:T(8,128)(2,1)S(1)} %copy-done.1, s32[1,1024]{1,0:T(1,128)S(1)} %bitcast.21, ...), custom_call_target="tpu_custom_call" | custom-call | tf_op jit(solution)/shard_map/pallas_call | solution.py:180
  73.7 2.0 %collective-permute-start.11 = (bf16[64,512]{1,0:T(8,128)(2,1)S(1)}, bf16[64,512]{1,0:T(8,128)(2,1)S(1)}, u32[]{:S(2)}, u32[]{:S(2)}) collective-permute-start(bf16[64,512]{1,0:T(8,128)(2,1)S(1)} %get-tuple-element.21), channel_id=1, source_target_pairs={{0,16},{16,32},{32,48},{48,64},{64,80},{80,96},{96,112},{1,17},{17... | collective-permute-start | bytes 196616 | tf_op jit(solution)/shard_map/ppermute | solution.py:137
  75.6 5.7 %collective-permute-start.12 = (bf16[64,512]{1,0:T(8,128)(2,1)S(1)}, bf16[64,512]{1,0:T(8,128)(2,1)S(1)}, u32[]{:S(2)}, u32[]{:S(2)}) collective-permute-start(bf16[64,512]{1,0:T(8,128)(2,1)S(1)} %get-tuple-element.22), channel_id=1, source_target_pairs={{16,0},{32,16},{48,32},{64,48},{80,64},{96,80},{112,96},{17,1},{33... | collective-permute-start | bytes 196616 | tf_op jit(solution)/shard_map/ppermute | solution.py:137
  81.4 2.5 %collective-permute-start.13 = (bf16[64,128]{1,0:T(8,128)(2,1)S(1)}, bf16[64,128]{1,0:T(8,128)(2,1)S(1)}, u32[]{:S(2)}, u32[]{:S(2)}) collective-permute-start(bf16[64,128]{1,0:T(8,128)(2,1)S(1)} %get-tuple-element.23), channel_id=1, source_target_pairs={{0,1},{1,2},{2,3},{3,4},{4,5},{5,6},{6,7},{7,8},{8,9},{9,10},{10,1... | collective-permute-start | bytes 49160 | tf_op jit(solution)/shard_map/ppermute | solution.py:137
  83.9 1.9 %collective-permute-start.14 = (bf16[64,128]{1,0:T(8,128)(2,1)S(1)}, bf16[64,128]{1,0:T(8,128)(2,1)S(1)}, u32[]{:S(2)}, u32[]{:S(2)}) collective-permute-start(bf16[64,128]{1,0:T(8,128)(2,1)S(1)} %get-tuple-element.24), channel_id=1, source_target_pairs={{1,0},{2,1},{3,2},{4,3},{5,4},{6,5},{7,6},{8,7},{9,8},{10,9},{11,1... | collective-permute-start | bytes 49160 | tf_op jit(solution)/shard_map/ppermute | solution.py:137
  85.8 0.0 collective-permute-done.13.refs_2_
  85.8 5.2 %collective-permute-done.14.refs_3_ = bf16[64,128]{1,0:T(8,128)(2,1)S(1)} collective-permute-done((bf16[64,128]{1,0:T(8,128)(2,1)S(1)}, bf16[64,128]{1,0:T(8,128)(2,1)S(1)}, u32[]{:S(2)}, u32[]{:S(2)}) %collective-permute-start.14) | collective-permute-done | bytes 16416 | tf_op jit(solution)/shard_map/ppermute | solution.py:137
  91.0 0.0 collective-permute-done.11.refs_0_
  91.0 0.0 collective-permute-done.12.refs_1_
  91.0 1.5 %shard_map.75 = bf16[256,4096]{1,0:T(8,128)(2,1)S(1)} custom-call(s32[4]{0:T(128)S(1)} %copy-done.3, bf16[256,4096]{1,0:T(8,128)(2,1)S(1)} %get-tuple-element.20.x_ref, bf16[4,256,128]{2,1,0:T(8,128)(2,1)S(1)} %broadcast_in_dim.5.profile_ref, bf16[64,512]{1,0:T(8,128)(2,1)S(1)} %collective-permute-done.11.refs_0_, ...), custom_call_target="tpu_custom_call" | custom-call | tf_op jit(solution)/shard_map/pallas_call | solution.py:190
  92.6 1.8 %copy.9 = bf16[32,8,32,128]{3,2,1,0:T(8,128)(2,1)} copy(bf16[32,8,32,128]{3,1,2,0:T(8,128)(2,1)S(1)} %bitcast.19) | data formatting | bytes 4194304
  (2 shorter events, 0.0 us)
Async XLA Ops:
  16.6 21.3 %copy-start.2 = (s32[8,128]{1,0:T(8,128)S(1)}, s32[8,128]{1,0:T(8,128)}, u32[]{:S(2)}) copy-start(s32[8,128]{1,0:T(8,128)} %param.8) | copy-start | bytes 12292
  16.6 10.0 %collective-permute-start.6 = (bf16[256,256]{1,0:T(8,128)(2,1)S(1)}, bf16[256,256]{1,0:T(8,128)(2,1)S(1)}, u32[]{:S(2)}, u32[]{:S(2)}) collective-permute-start(bf16[256,256]{1,0:T(8,128)(2,1)S(1)} %fusion.refs_0_.refs_4_), channel_id=1, source_target_pairs={{0,112},{16,0},{32,16},{48,32},{64,48},{80,64},{96,80},{112,96},{1... | collective-permute-start | bytes 393224 | tf_op jit(solution)/shard_map/ppermute | solution.py:36
  19.0 9.2 %collective-permute-start.5 = (bf16[256,256]{1,0:T(8,128)(2,1)S(1)}, bf16[256,256]{1,0:T(8,128)(2,1)S(1)}, u32[]{:S(2)}, u32[]{:S(2)}) collective-permute-start(bf16[256,256]{1,0:T(8,128)(2,1)S(1)} %fusion.refs_0_.refs_4_), channel_id=1, source_target_pairs={{0,96},{16,112},{32,0},{48,16},{64,32},{80,48},{96,64},{112,80},{1... | collective-permute-start | bytes 393224 | tf_op jit(solution)/shard_map/ppermute | solution.py:36
  19.2 13.0 %collective-permute-start.4 = (bf16[256,256]{1,0:T(8,128)(2,1)S(1)}, bf16[256,256]{1,0:T(8,128)(2,1)S(1)}, u32[]{:S(2)}, u32[]{:S(2)}) collective-permute-start(bf16[256,256]{1,0:T(8,128)(2,1)S(1)} %fusion.refs_0_.refs_4_), channel_id=1, source_target_pairs={{0,80},{16,96},{32,112},{48,0},{64,16},{80,32},{96,48},{112,64},{1... | collective-permute-start | bytes 393224 | tf_op jit(solution)/shard_map/ppermute | solution.py:36
  22.1 10.0 %collective-permute-start.3 = (bf16[256,256]{1,0:T(8,128)(2,1)S(1)}, bf16[256,256]{1,0:T(8,128)(2,1)S(1)}, u32[]{:S(2)}, u32[]{:S(2)}) collective-permute-start(bf16[256,256]{1,0:T(8,128)(2,1)S(1)} %fusion.refs_0_.refs_4_), channel_id=1, source_target_pairs={{0,64},{16,80},{32,96},{48,112},{64,0},{80,16},{96,32},{112,48},{1... | collective-permute-start | bytes 393224 | tf_op jit(solution)/shard_map/ppermute | solution.py:36
  22.5 9.7 %collective-permute-start.2 = (bf16[256,256]{1,0:T(8,128)(2,1)S(1)}, bf16[256,256]{1,0:T(8,128)(2,1)S(1)}, u32[]{:S(2)}, u32[]{:S(2)}) collective-permute-start(bf16[256,256]{1,0:T(8,128)(2,1)S(1)} %fusion.refs_0_.refs_4_), channel_id=1, source_target_pairs={{0,48},{16,64},{32,80},{48,96},{64,112},{80,0},{96,16},{112,32},{1... | collective-permute-start | bytes 393224 | tf_op jit(solution)/shard_map/ppermute | solution.py:36
  26.6 11.3 %collective-permute-start.1 = (bf16[256,256]{1,0:T(8,128)(2,1)S(1)}, bf16[256,256]{1,0:T(8,128)(2,1)S(1)}, u32[]{:S(2)}, u32[]{:S(2)}) collective-permute-start(bf16[256,256]{1,0:T(8,128)(2,1)S(1)} %fusion.refs_0_.refs_4_), channel_id=1, source_target_pairs={{0,32},{16,48},{32,64},{48,80},{64,96},{80,112},{96,0},{112,16},{1... | collective-permute-start | bytes 393224 | tf_op jit(solution)/shard_map/ppermute | solution.py:36
  28.2 9.7 %collective-permute-start = (bf16[256,256]{1,0:T(8,128)(2,1)S(1)}, bf16[256,256]{1,0:T(8,128)(2,1)S(1)}, u32[]{:S(2)}, u32[]{:S(2)}) collective-permute-start(bf16[256,256]{1,0:T(8,128)(2,1)S(1)} %fusion.refs_0_.refs_4_), channel_id=1, source_target_pairs={{0,16},{16,32},{32,48},{48,64},{64,80},{80,96},{96,112},{112,0},{1... | collective-permute-start | bytes 393224 | tf_op jit(solution)/shard_map/ppermute | solution.py:36
  32.1 27.3 %copy-start.4 = (bf16[4,64,4]{1,2,0:T(4,128)(2,1)S(1)}, bf16[4,64,4]{1,2,0:T(4,128)(2,1)}, u32[]{:S(2)}) copy-start(bf16[4,64,4]{1,2,0:T(4,128)(2,1)} %param.10) | copy-start | bytes 6148
  32.2 32.7 %copy-start.3 = (s32[4]{0:T(128)S(1)}, s32[4]{0:T(128)}, u32[]{:S(2)}) copy-start(s32[4]{0:T(128)} %port_ref.3) | copy-start | bytes 52
  43.8 1.3 %copy-start = (bf16[256,4096]{1,0:T(8,128)(2,1)}, bf16[256,4096]{1,0:T(8,128)(2,1)S(1)}, u32[]{:S(2)}) copy-start(bf16[256,4096]{1,0:T(8,128)(2,1)S(1)} %get-tuple-element.15.x_ref) | copy-start | bytes 6291460
  45.1 19.5 %collective-permute-start.7 = (bf16[64,512]{1,0:T(8,128)(2,1)S(1)}, bf16[64,512]{1,0:T(8,128)(2,1)S(1)}, u32[]{:S(2)}, u32[]{:S(2)}) collective-permute-start(bf16[64,512]{1,0:T(8,128)(2,1)S(1)} %get-tuple-element.16), channel_id=1, source_target_pairs={{0,16},{16,32},{32,48},{48,64},{64,80},{80,96},{96,112},{1,17},{17... | collective-permute-start | bytes 196616 | tf_op jit(solution)/shard_map/ppermute | solution.py:137
  48.6 16.1 %collective-permute-start.8 = (bf16[64,512]{1,0:T(8,128)(2,1)S(1)}, bf16[64,512]{1,0:T(8,128)(2,1)S(1)}, u32[]{:S(2)}, u32[]{:S(2)}) collective-permute-start(bf16[64,512]{1,0:T(8,128)(2,1)S(1)} %get-tuple-element.17), channel_id=1, source_target_pairs={{16,0},{32,16},{48,32},{64,48},{80,64},{96,80},{112,96},{17,1},{33... | collective-permute-start | bytes 196616 | tf_op jit(solution)/shard_map/ppermute | solution.py:137
  52.8 6.7 %collective-permute-start.9 = (bf16[64,128]{1,0:T(8,128)(2,1)S(1)}, bf16[64,128]{1,0:T(8,128)(2,1)S(1)}, u32[]{:S(2)}, u32[]{:S(2)}) collective-permute-start(bf16[64,128]{1,0:T(8,128)(2,1)S(1)} %get-tuple-element.18), channel_id=1, source_target_pairs={{0,1},{1,2},{2,3},{3,4},{4,5},{5,6},{6,7},{7,8},{8,9},{9,10},{10,1... | collective-permute-start | bytes 49160 | tf_op jit(solution)/shard_map/ppermute | solution.py:137
  57.5 7.2 %collective-permute-start.10 = (bf16[64,128]{1,0:T(8,128)(2,1)S(1)}, bf16[64,128]{1,0:T(8,128)(2,1)S(1)}, u32[]{:S(2)}, u32[]{:S(2)}) collective-permute-start(bf16[64,128]{1,0:T(8,128)(2,1)S(1)} %get-tuple-element.19), channel_id=1, source_target_pairs={{1,0},{2,1},{3,2},{4,3},{5,4},{6,5},{7,6},{8,7},{9,8},{10,9},{11,1... | collective-permute-start | bytes 49160 | tf_op jit(solution)/shard_map/ppermute | solution.py:137
  64.9 1.6 %copy-start.1 = (bf16[256,4096]{1,0:T(8,128)(2,1)S(1)}, bf16[256,4096]{1,0:T(8,128)(2,1)}, u32[]{:S(2)}) copy-start(bf16[256,4096]{1,0:T(8,128)(2,1)} %copy-done) | copy-start | bytes 6291460
  73.7 17.4 %collective-permute-start.11 = (bf16[64,512]{1,0:T(8,128)(2,1)S(1)}, bf16[64,512]{1,0:T(8,128)(2,1)S(1)}, u32[]{:S(2)}, u32[]{:S(2)}) collective-permute-start(bf16[64,512]{1,0:T(8,128)(2,1)S(1)} %get-tuple-element.21), channel_id=1, source_target_pairs={{0,16},{16,32},{32,48},{48,64},{64,80},{80,96},{96,112},{1,17},{17... | collective-permute-start | bytes 196616 | tf_op jit(solution)/shard_map/ppermute | solution.py:137
  75.6 15.4 %collective-permute-start.12 = (bf16[64,512]{1,0:T(8,128)(2,1)S(1)}, bf16[64,512]{1,0:T(8,128)(2,1)S(1)}, u32[]{:S(2)}, u32[]{:S(2)}) collective-permute-start(bf16[64,512]{1,0:T(8,128)(2,1)S(1)} %get-tuple-element.22), channel_id=1, source_target_pairs={{16,0},{32,16},{48,32},{64,48},{80,64},{96,80},{112,96},{17,1},{33... | collective-permute-start | bytes 196616 | tf_op jit(solution)/shard_map/ppermute | solution.py:137
  81.4 4.4 %collective-permute-start.13 = (bf16[64,128]{1,0:T(8,128)(2,1)S(1)}, bf16[64,128]{1,0:T(8,128)(2,1)S(1)}, u32[]{:S(2)}, u32[]{:S(2)}) collective-permute-start(bf16[64,128]{1,0:T(8,128)(2,1)S(1)} %get-tuple-element.23), channel_id=1, source_target_pairs={{0,1},{1,2},{2,3},{3,4},{4,5},{5,6},{6,7},{7,8},{8,9},{9,10},{10,1... | collective-permute-start | bytes 49160 | tf_op jit(solution)/shard_map/ppermute | solution.py:137
  83.9 7.2 %collective-permute-start.14 = (bf16[64,128]{1,0:T(8,128)(2,1)S(1)}, bf16[64,128]{1,0:T(8,128)(2,1)S(1)}, u32[]{:S(2)}, u32[]{:S(2)}) collective-permute-start(bf16[64,128]{1,0:T(8,128)(2,1)S(1)} %get-tuple-element.24), channel_id=1, source_target_pairs={{1,0},{2,1},{3,2},{4,3},{5,4},{6,5},{7,6},{8,7},{9,8},{10,9},{11,1... | collective-permute-start | bytes 49160 | tf_op jit(solution)/shard_map/ppermute | solution.py:137

commit v2 on v1

--- a/solution.py
+++ b/solution.py
@@ -42,10 +42,15 @@
     quarter = block.shape[0] // 4
     port = pl.program_id(0)
     lane = lax.broadcasted_iota(jnp.int32, (quarter, LANES), 1)
-    block[0:quarter, 0:LANES] = north[...]
-    block[quarter : 2 * quarter, (rows - 1) * LANES : rows * LANES] = south[...]
-    west_all = west[...].astype(F32)
-    east_all = east[...].astype(F32)
+    mine, count = lax.axis_index("row"), lax.axis_size("row")
+    mine_col, count_col = lax.axis_index("col"), lax.axis_size("col")
+    zero = jnp.zeros((), BF)
+    block[0:quarter, 0:LANES] = jnp.where(mine > 0, north[...], zero)
+    block[quarter : 2 * quarter, (rows - 1) * LANES : rows * LANES] = jnp.where(
+        mine < count - 1, south[...], zero
+    )
+    west_all = jnp.where(mine_col > 0, west[...].astype(F32), 0.0)
+    east_all = jnp.where(mine_col < count_col - 1, east[...].astype(F32), 0.0)
     for row in range(rows):
         place = port * rows + row
         cols = slice(row * LANES, (row + 1) * LANES)
@@ -57,10 +62,9 @@
         block[3 * quarter : 4 * quarter, cols] = jnp.where(
             lane == LANES - 1, from_east, east_part
         ).astype(BF)
-    all_cols = width * lax.axis_size("col")
     cell = port_ref[port]
-    row = cell // all_cols - lax.axis_index("row") * rows
-    col = cell % all_cols - lax.axis_index("col") * width
+    row = cell // (width * count_col) - mine * rows
+    col = cell % (width * count_col) - mine_col * width
 
     @pl.when((row >= 0) & (row < rows) & (col >= 0) & (col < width))
     def _():
@@ -133,8 +137,7 @@
 
     def send(value, axis, step):
         count = lax.axis_size(axis)
-        pairs = [(i, i + step) for i in range(count) if 0 <= i + step < count]
-        return lax.ppermute(value, axis, pairs)
+        return lax.ppermute(value, axis, [(i, (i + step) % count) for i in range(count)])
 
     return (
         send(south, "row", 1),
@@ -167,7 +170,7 @@
     rim_shapes = [jax.ShapeDtypeStruct((quarter, ports * LANES), BF)] * 2 + [
         jax.ShapeDtypeStruct((quarter, LANES), BF)
     ] * 2
-    params = pltpu.CompilerParams(vmem_limit_bytes=40 * 2**20)
+    params = pltpu.CompilerParams(vmem_limit_bytes=20 * 2**20)
     x, *sent = pl.pallas_call(
         functools.partial(first_kernel, rows),
         grid=(ports,),

time: 94.9 us -> 86.7 us (0.914)
  the two profiles are of different devices: /device:TPU:113 before, /device:TPU:0 now
where the time goes in v2:
time: 86.7 us; the launch traced here: 86.4 us
  starting transfers between devices  32.2 us (37%)
  blocking collectives  17.1 us (20%)
  Pallas kernels  14.8 us (17%)
  waiting for transfers between devices  12.2 us (14%)
  local copies, waits for them, and re-layouts  7.88 us (9%)
  other arithmetic  1.51 us (2%)
    ppermute x8, starting transfers between devices, send(): lax.ppermute(value, axis, [(i, (i + step) % count) for i in range(count)])  19.1 us
    all_to_all x1, blocking collectives, gather_modes(): every = lax.all_to_all(spread, 'col', 0, 0, tiled=True)  17.1 us
    ppermute x7, starting transfers between devices, all_maps(): maps.append(lax.ppermute(own_map, 'row', pairs))  13.1 us
    ppermute x7, waiting for transfers between devices, all_maps(): maps.append(lax.ppermute(own_map, 'row', pairs))  9.31 us
    pallas_call x1, Pallas kernels, body(): pl.pallas_call(functools.partial(second_kernel, rows, width), grid=(ports...  7.22 us
    pallas_call x1, Pallas kernels, body(): pl.pallas_call(functools.partial(first_kernel, rows), grid=(ports,), in_s...  5.93 us
    unnamed x12, local copies, waits for them, and re-layouts  4.73 us
    ppermute x8, waiting for transfers between devices, send(): lax.ppermute(value, axis, [(i, (i + step) % count) for i in range(count)])  2.88 us
  transfers between devices with their start and end apart: 15, of which 5 were waited for; matrix products, arithmetic and copies ran while one was open for 3% of the time, Pallas kernels for 0%

profile of v2, /device:TPU:0, one launch (start us, length us, event | category | flops | bytes accessed | tf_op | source)
XLA Modules:
  0.0 86.4 jit_solution(11604411791415618831)
XLA Ops:
  0.0 0.8 multiply_bitcast_fusion
  0.8 0.7 pad_maximum_fusion
  1.6 17.1 %all_to_all.5 = f32[16,32,256]{2,1,0:T(8,128)S(1)} all-to-all(f32[16,32,256]{2,1,0:T(8,128)S(1)} %broadcast_in_dim.4), channel_id=1, replica_groups=mesh['row'=8,'col'=16] {'col'}, dimensions={0} | all-to-all | bytes 1048576 | tf_op jit(solution)/shard_map/all_to_all | solution.py:20
  18.7 0.6 fusion.refs_0_.refs_4_
  19.3 0.0 copy-start.2
  19.3 5.2 %collective-permute-start.6 = (bf16[256,256]{1,0:T(8,128)(2,1)S(1)}, bf16[256,256]{1,0:T(8,128)(2,1)S(1)}, u32[]{:S(2)}, u32[]{:S(2)}) collective-permute-start(bf16[256,256]{1,0:T(8,128)(2,1)S(1)} %fusion.refs_0_.refs_4_), channel_id=1, source_target_pairs={{0,112},{16,0},{32,16},{48,32},{64,48},{80,64},{96,80},{112,96},{1... | collective-permute-start | bytes 393224 | tf_op jit(solution)/shard_map/ppermute | solution.py:36
  24.5 0.7 collective-permute-start.5
  25.3 0.7 collective-permute-start.4
  26.0 2.9 %collective-permute-start.3 = (bf16[256,256]{1,0:T(8,128)(2,1)S(1)}, bf16[256,256]{1,0:T(8,128)(2,1)S(1)}, u32[]{:S(2)}, u32[]{:S(2)}) collective-permute-start(bf16[256,256]{1,0:T(8,128)(2,1)S(1)} %fusion.refs_0_.refs_4_), channel_id=1, source_target_pairs={{0,64},{16,80},{32,96},{48,112},{64,0},{80,16},{96,32},{112,48},{1... | collective-permute-start | bytes 393224 | tf_op jit(solution)/shard_map/ppermute | solution.py:36
  28.9 0.8 collective-permute-start.2
  29.7 0.0 collective-permute-done.6.refs_7_.refs_11_
  29.7 1.9 %collective-permute-start.1 = (bf16[256,256]{1,0:T(8,128)(2,1)S(1)}, bf16[256,256]{1,0:T(8,128)(2,1)S(1)}, u32[]{:S(2)}, u32[]{:S(2)}) collective-permute-start(bf16[256,256]{1,0:T(8,128)(2,1)S(1)} %fusion.refs_0_.refs_4_), channel_id=1, source_target_pairs={{0,32},{16,48},{32,64},{48,80},{64,96},{80,112},{96,0},{112,16},{1... | collective-permute-start | bytes 393224 | tf_op jit(solution)/shard_map/ppermute | solution.py:36
  31.6 4.4 %collective-permute-done.5.refs_6_.refs_10_ = bf16[256,256]{1,0:T(8,128)(2,1)S(1)} collective-permute-done((bf16[256,256]{1,0:T(8,128)(2,1)S(1)}, bf16[256,256]{1,0:T(8,128)(2,1)S(1)}, u32[]{:S(2)}, u32[]{:S(2)}) %collective-permute-start.5) | collective-permute-done | bytes 131104 | tf_op jit(solution)/shard_map/ppermute | solution.py:36
  36.0 0.8 collective-permute-start
  36.8 2.8 %reshape.19.x_ref = bf16[256,4096]{1,0:T(8,128)(2,1)S(1)} reshape(bf16[4,64,4,8,128]{4,3,2,1,0:T(8,128)(2,1)} %param.7) | data formatting | bytes 4194304 | tf_op jit(solution)/shard_map/reshape | solution.py:156
  39.6 0.0 copy-start.4
  39.7 0.0 copy-start.3
  39.7 0.0 collective-permute-done.4.refs_5_.refs_9_
  39.7 0.0 collective-permute-done.3.refs_4_.refs_8_
  39.7 0.0 collective-permute-done.2.refs_3_.refs_7_
  39.7 0.4 collective-permute-done.1.refs_2_.refs_6_
  40.1 4.5 %collective-permute-done.refs_1_.refs_5_ = bf16[256,256]{1,0:T(8,128)(2,1)S(1)} collective-permute-done((bf16[256,256]{1,0:T(8,128)(2,1)S(1)}, bf16[256,256]{1,0:T(8,128)(2,1)S(1)}, u32[]{:S(2)}, u32[]{:S(2)}) %collective-permute-start) | collective-permute-done | bytes 131104 | tf_op jit(solution)/shard_map/ppermute | solution.py:36
  44.6 0.0 copy-done.2
  44.6 5.9 %shard_map.73 = (bf16[256,4096]{1,0:T(8,128)(2,1)S(1)}, bf16[64,512]{1,0:T(8,128)(2,1)S(1)}, bf16[64,512]{1,0:T(8,128)(2,1)S(1)}, bf16[64,128]{1,0:T(8,128)(2,1)S(1)}, bf16[64,128]{1,0:T(8,128)(2,1)S(1)}) custom-call(bf16[256,4096]{1,0:T(8,128)(2,1)S(1)} %reshape.19.x_ref, s32[1,1024]{1,0:T(1,128)S(1)} %bitcast.20, ...), custom_call_target="tpu_custom_call" | custom-call | tf_op jit(solution)/shard_map/pallas_call | solution.py:174
  50.5 0.0 copy-start
  50.5 1.3 %copy-done = bf16[256,4096]{1,0:T(8,128)(2,1)} copy-done((bf16[256,4096]{1,0:T(8,128)(2,1)}, bf16[256,4096]{1,0:T(8,128)(2,1)S(1)}, u32[]{:S(2)}) %copy-start) | copy-done | bytes 2097176
  51.9 0.0 collective-permute-start.7
  51.9 5.6 %collective-permute-start.8 = (bf16[64,512]{1,0:T(8,128)(2,1)S(1)}, bf16[64,512]{1,0:T(8,128)(2,1)S(1)}, u32[]{:S(2)}, u32[]{:S(2)}) collective-permute-start(bf16[64,512]{1,0:T(8,128)(2,1)S(1)} %get-tuple-element.17), channel_id=1, source_target_pairs={{0,112},{16,0},{32,16},{48,32},{64,48},{80,64},{96,80},{112,96},{1... | collective-permute-start | bytes 196616 | tf_op jit(solution)/shard_map/ppermute | solution.py:140
  57.5 0.0 collective-permute-start.9
  57.5 3.9 %collective-permute-start.10 = (bf16[64,128]{1,0:T(8,128)(2,1)S(1)}, bf16[64,128]{1,0:T(8,128)(2,1)S(1)}, u32[]{:S(2)}, u32[]{:S(2)}) collective-permute-start(bf16[64,128]{1,0:T(8,128)(2,1)S(1)} %get-tuple-element.19), channel_id=1, source_target_pairs={{0,15},{1,0},{2,1},{3,2},{4,3},{5,4},{6,5},{7,6},{8,7},{9,8},{10,9... | collective-permute-start | bytes 49160 | tf_op jit(solution)/shard_map/ppermute | solution.py:140
  61.4 0.0 copy-done.4
  61.4 0.1 reshape.21
  61.4 1.3 %collective-permute-done.9.refs_2_ = bf16[64,128]{1,0:T(8,128)(2,1)S(1)} collective-permute-done((bf16[64,128]{1,0:T(8,128)(2,1)S(1)}, bf16[64,128]{1,0:T(8,128)(2,1)S(1)}, u32[]{:S(2)}, u32[]{:S(2)}) %collective-permute-start.9) | collective-permute-done | bytes 16416 | tf_op jit(solution)/shard_map/ppermute | solution.py:140
  62.8 0.0 collective-permute-done.10.refs_3_
  62.8 0.0 collective-permute-done.7.refs_0_
  62.8 0.0 collective-permute-done.8.refs_1_
  62.8 0.2 broadcast_in_dim.5.profile_ref
  63.0 0.0 copy-done.3
  63.0 0.0 copy-start.1
  63.0 1.6 %copy-done.1 = bf16[256,4096]{1,0:T(8,128)(2,1)S(1)} copy-done((bf16[256,4096]{1,0:T(8,128)(2,1)S(1)}, bf16[256,4096]{1,0:T(8,128)(2,1)}, u32[]{:S(2)}) %copy-start.1) | copy-done | bytes 2097176
  64.6 7.2 %shard_map.74 = (bf16[256,4096]{1,0:T(8,128)(2,1)S(1)}, bf16[64,512]{1,0:T(8,128)(2,1)S(1)}, bf16[64,512]{1,0:T(8,128)(2,1)S(1)}, bf16[64,128]{1,0:T(8,128)(2,1)S(1)}, bf16[64,128]{1,0:T(8,128)(2,1)S(1)}) custom-call(s32[4]{0:T(128)S(1)} %copy-done.3, bf16[256,4096]{1,0:T(8,128)(2,1)S(1)} %copy-done.1, s32[1,1024]{1,0:T(1,128)S(1)} %bitcast.21, ...), custom_call_target="tpu_custom_call" | custom-call | tf_op jit(solution)/shard_map/pallas_call | solution.py:183
  71.8 0.1 collective-permute-start.11
  71.9 5.6 %collective-permute-start.12 = (bf16[64,512]{1,0:T(8,128)(2,1)S(1)}, bf16[64,512]{1,0:T(8,128)(2,1)S(1)}, u32[]{:S(2)}, u32[]{:S(2)}) collective-permute-start(bf16[64,512]{1,0:T(8,128)(2,1)S(1)} %get-tuple-element.22), channel_id=1, source_target_pairs={{0,112},{16,0},{32,16},{48,32},{64,48},{80,64},{96,80},{112,96},{1... | collective-permute-start | bytes 196616 | tf_op jit(solution)/shard_map/ppermute | solution.py:140
  77.6 0.0 collective-permute-start.13
  77.6 3.9 %collective-permute-start.14 = (bf16[64,128]{1,0:T(8,128)(2,1)S(1)}, bf16[64,128]{1,0:T(8,128)(2,1)S(1)}, u32[]{:S(2)}, u32[]{:S(2)}) collective-permute-start(bf16[64,128]{1,0:T(8,128)(2,1)S(1)} %get-tuple-element.24), channel_id=1, source_target_pairs={{0,15},{1,0},{2,1},{3,2},{4,3},{5,4},{6,5},{7,6},{8,7},{9,8},{10,9... | collective-permute-start | bytes 49160 | tf_op jit(solution)/shard_map/ppermute | solution.py:140
  81.4 1.5 %collective-permute-done.13.refs_2_ = bf16[64,128]{1,0:T(8,128)(2,1)S(1)} collective-permute-done((bf16[64,128]{1,0:T(8,128)(2,1)S(1)}, bf16[64,128]{1,0:T(8,128)(2,1)S(1)}, u32[]{:S(2)}, u32[]{:S(2)}) %collective-permute-start.13) | collective-permute-done | bytes 16416 | tf_op jit(solution)/shard_map/ppermute | solution.py:140
  82.9 0.0 collective-permute-done.14.refs_3_
  82.9 0.0 collective-permute-done.11.refs_0_
  82.9 0.0 collective-permute-done.12.refs_1_
  82.9 1.7 %shard_map.75 = bf16[256,4096]{1,0:T(8,128)(2,1)S(1)} custom-call(s32[4]{0:T(128)S(1)} %copy-done.3, bf16[256,4096]{1,0:T(8,128)(2,1)S(1)} %get-tuple-element.20.x_ref, bf16[4,256,128]{2,1,0:T(8,128)(2,1)S(1)} %broadcast_in_dim.5.profile_ref, bf16[64,512]{1,0:T(8,128)(2,1)S(1)} %collective-permute-done.11.refs_0_, ...), custom_call_target="tpu_custom_call" | custom-call | tf_op jit(solution)/shard_map/pallas_call | solution.py:193
  84.6 1.8 %copy.9 = bf16[32,8,32,128]{3,2,1,0:T(8,128)(2,1)} copy(bf16[32,8,32,128]{3,1,2,0:T(8,128)(2,1)S(1)} %bitcast.19) | data formatting | bytes 4194304
  (2 shorter events, 0.0 us)
Async XLA Ops:
  19.3 25.3 %copy-start.2 = (s32[8,128]{1,0:T(8,128)S(1)}, s32[8,128]{1,0:T(8,128)}, u32[]{:S(2)}) copy-start(s32[8,128]{1,0:T(8,128)} %param.8) | copy-start | bytes 12292
  19.3 10.4 %collective-permute-start.6 = (bf16[256,256]{1,0:T(8,128)(2,1)S(1)}, bf16[256,256]{1,0:T(8,128)(2,1)S(1)}, u32[]{:S(2)}, u32[]{:S(2)}) collective-permute-start(bf16[256,256]{1,0:T(8,128)(2,1)S(1)} %fusion.refs_0_.refs_4_), channel_id=1, source_target_pairs={{0,112},{16,0},{32,16},{48,32},{64,48},{80,64},{96,80},{112,96},{1... | collective-permute-start | bytes 393224 | tf_op jit(solution)/shard_map/ppermute | solution.py:36
  24.5 11.5 %collective-permute-start.5 = (bf16[256,256]{1,0:T(8,128)(2,1)S(1)}, bf16[256,256]{1,0:T(8,128)(2,1)S(1)}, u32[]{:S(2)}, u32[]{:S(2)}) collective-permute-start(bf16[256,256]{1,0:T(8,128)(2,1)S(1)} %fusion.refs_0_.refs_4_), channel_id=1, source_target_pairs={{0,96},{16,112},{32,0},{48,16},{64,32},{80,48},{96,64},{112,80},{1... | collective-permute-start | bytes 393224 | tf_op jit(solution)/shard_map/ppermute | solution.py:36
  25.3 14.4 %collective-permute-start.4 = (bf16[256,256]{1,0:T(8,128)(2,1)S(1)}, bf16[256,256]{1,0:T(8,128)(2,1)S(1)}, u32[]{:S(2)}, u32[]{:S(2)}) collective-permute-start(bf16[256,256]{1,0:T(8,128)(2,1)S(1)} %fusion.refs_0_.refs_4_), channel_id=1, source_target_pairs={{0,80},{16,96},{32,112},{48,0},{64,16},{80,32},{96,48},{112,64},{1... | collective-permute-start | bytes 393224 | tf_op jit(solution)/shard_map/ppermute | solution.py:36
  26.0 13.7 %collective-permute-start.3 = (bf16[256,256]{1,0:T(8,128)(2,1)S(1)}, bf16[256,256]{1,0:T(8,128)(2,1)S(1)}, u32[]{:S(2)}, u32[]{:S(2)}) collective-permute-start(bf16[256,256]{1,0:T(8,128)(2,1)S(1)} %fusion.refs_0_.refs_4_), channel_id=1, source_target_pairs={{0,64},{16,80},{32,96},{48,112},{64,0},{80,16},{96,32},{112,48},{1... | collective-permute-start | bytes 393224 | tf_op jit(solution)/shard_map/ppermute | solution.py:36
  28.9 10.8 %collective-permute-start.2 = (bf16[256,256]{1,0:T(8,128)(2,1)S(1)}, bf16[256,256]{1,0:T(8,128)(2,1)S(1)}, u32[]{:S(2)}, u32[]{:S(2)}) collective-permute-start(bf16[256,256]{1,0:T(8,128)(2,1)S(1)} %fusion.refs_0_.refs_4_), channel_id=1, source_target_pairs={{0,48},{16,64},{32,80},{48,96},{64,112},{80,0},{96,16},{112,32},{1... | collective-permute-start | bytes 393224 | tf_op jit(solution)/shard_map/ppermute | solution.py:36
  29.7 10.4 %collective-permute-start.1 = (bf16[256,256]{1,0:T(8,128)(2,1)S(1)}, bf16[256,256]{1,0:T(8,128)(2,1)S(1)}, u32[]{:S(2)}, u32[]{:S(2)}) collective-permute-start(bf16[256,256]{1,0:T(8,128)(2,1)S(1)} %fusion.refs_0_.refs_4_), channel_id=1, source_target_pairs={{0,32},{16,48},{32,64},{48,80},{64,96},{80,112},{96,0},{112,16},{1... | collective-permute-start | bytes 393224 | tf_op jit(solution)/shard_map/ppermute | solution.py:36
  36.0 8.6 %collective-permute-start = (bf16[256,256]{1,0:T(8,128)(2,1)S(1)}, bf16[256,256]{1,0:T(8,128)(2,1)S(1)}, u32[]{:S(2)}, u32[]{:S(2)}) collective-permute-start(bf16[256,256]{1,0:T(8,128)(2,1)S(1)} %fusion.refs_0_.refs_4_), channel_id=1, source_target_pairs={{0,16},{16,32},{32,48},{48,64},{64,80},{80,96},{96,112},{112,0},{1... | collective-permute-start | bytes 393224 | tf_op jit(solution)/shard_map/ppermute | solution.py:36
  39.6 21.7 %copy-start.4 = (bf16[4,64,4]{1,2,0:T(4,128)(2,1)S(1)}, bf16[4,64,4]{1,2,0:T(4,128)(2,1)}, u32[]{:S(2)}) copy-start(bf16[4,64,4]{1,2,0:T(4,128)(2,1)} %param.10) | copy-start | bytes 6148
  39.7 23.4 %copy-start.3 = (s32[4]{0:T(128)S(1)}, s32[4]{0:T(128)}, u32[]{:S(2)}) copy-start(s32[4]{0:T(128)} %port_ref.3) | copy-start | bytes 52
  50.5 1.3 %copy-start = (bf16[256,4096]{1,0:T(8,128)(2,1)}, bf16[256,4096]{1,0:T(8,128)(2,1)S(1)}, u32[]{:S(2)}) copy-start(bf16[256,4096]{1,0:T(8,128)(2,1)S(1)} %get-tuple-element.15.x_ref) | copy-start | bytes 6291460
  51.9 10.9 %collective-permute-start.7 = (bf16[64,512]{1,0:T(8,128)(2,1)S(1)}, bf16[64,512]{1,0:T(8,128)(2,1)S(1)}, u32[]{:S(2)}, u32[]{:S(2)}) collective-permute-start(bf16[64,512]{1,0:T(8,128)(2,1)S(1)} %get-tuple-element.16), channel_id=1, source_target_pairs={{0,16},{16,32},{32,48},{48,64},{64,80},{80,96},{96,112},{112,0},{1... | collective-permute-start | bytes 196616 | tf_op jit(solution)/shard_map/ppermute | solution.py:140
  51.9 10.9 %collective-permute-start.8 = (bf16[64,512]{1,0:T(8,128)(2,1)S(1)}, bf16[64,512]{1,0:T(8,128)(2,1)S(1)}, u32[]{:S(2)}, u32[]{:S(2)}) collective-permute-start(bf16[64,512]{1,0:T(8,128)(2,1)S(1)} %get-tuple-element.17), channel_id=1, source_target_pairs={{0,112},{16,0},{32,16},{48,32},{64,48},{80,64},{96,80},{112,96},{1... | collective-permute-start | bytes 196616 | tf_op jit(solution)/shard_map/ppermute | solution.py:140
  57.5 5.3 %collective-permute-start.9 = (bf16[64,128]{1,0:T(8,128)(2,1)S(1)}, bf16[64,128]{1,0:T(8,128)(2,1)S(1)}, u32[]{:S(2)}, u32[]{:S(2)}) collective-permute-start(bf16[64,128]{1,0:T(8,128)(2,1)S(1)} %get-tuple-element.18), channel_id=1, source_target_pairs={{0,1},{1,2},{2,3},{3,4},{4,5},{5,6},{6,7},{7,8},{8,9},{9,10},{10,1... | collective-permute-start | bytes 49160 | tf_op jit(solution)/shard_map/ppermute | solution.py:140
  57.5 5.3 %collective-permute-start.10 = (bf16[64,128]{1,0:T(8,128)(2,1)S(1)}, bf16[64,128]{1,0:T(8,128)(2,1)S(1)}, u32[]{:S(2)}, u32[]{:S(2)}) collective-permute-start(bf16[64,128]{1,0:T(8,128)(2,1)S(1)} %get-tuple-element.19), channel_id=1, source_target_pairs={{0,15},{1,0},{2,1},{3,2},{4,3},{5,4},{6,5},{7,6},{8,7},{9,8},{10,9... | collective-permute-start | bytes 49160 | tf_op jit(solution)/shard_map/ppermute | solution.py:140
  63.0 1.6 %copy-start.1 = (bf16[256,4096]{1,0:T(8,128)(2,1)S(1)}, bf16[256,4096]{1,0:T(8,128)(2,1)}, u32[]{:S(2)}) copy-start(bf16[256,4096]{1,0:T(8,128)(2,1)} %copy-done) | copy-start | bytes 6291460
  71.8 11.1 %collective-permute-start.11 = (bf16[64,512]{1,0:T(8,128)(2,1)S(1)}, bf16[64,512]{1,0:T(8,128)(2,1)S(1)}, u32[]{:S(2)}, u32[]{:S(2)}) collective-permute-start(bf16[64,512]{1,0:T(8,128)(2,1)S(1)} %get-tuple-element.21), channel_id=1, source_target_pairs={{0,16},{16,32},{32,48},{48,64},{64,80},{80,96},{96,112},{112,0},{1... | collective-permute-start | bytes 196616 | tf_op jit(solution)/shard_map/ppermute | solution.py:140
  71.9 11.0 %collective-permute-start.12 = (bf16[64,512]{1,0:T(8,128)(2,1)S(1)}, bf16[64,512]{1,0:T(8,128)(2,1)S(1)}, u32[]{:S(2)}, u32[]{:S(2)}) collective-permute-start(bf16[64,512]{1,0:T(8,128)(2,1)S(1)} %get-tuple-element.22), channel_id=1, source_target_pairs={{0,112},{16,0},{32,16},{48,32},{64,48},{80,64},{96,80},{112,96},{1... | collective-permute-start | bytes 196616 | tf_op jit(solution)/shard_map/ppermute | solution.py:140
  77.6 5.4 %collective-permute-start.13 = (bf16[64,128]{1,0:T(8,128)(2,1)S(1)}, bf16[64,128]{1,0:T(8,128)(2,1)S(1)}, u32[]{:S(2)}, u32[]{:S(2)}) collective-permute-start(bf16[64,128]{1,0:T(8,128)(2,1)S(1)} %get-tuple-element.23), channel_id=1, source_target_pairs={{0,1},{1,2},{2,3},{3,4},{4,5},{5,6},{6,7},{7,8},{8,9},{9,10},{10,1... | collective-permute-start | bytes 49160 | tf_op jit(solution)/shard_map/ppermute | solution.py:140
  77.6 5.4 %collective-permute-start.14 = (bf16[64,128]{1,0:T(8,128)(2,1)S(1)}, bf16[64,128]{1,0:T(8,128)(2,1)S(1)}, u32[]{:S(2)}, u32[]{:S(2)}) collective-permute-start(bf16[64,128]{1,0:T(8,128)(2,1)S(1)} %get-tuple-element.24), channel_id=1, source_target_pairs={{0,15},{1,0},{2,1},{3,2},{4,3},{5,4},{6,5},{7,6},{8,7},{9,8},{10,9... | collective-permute-start | bytes 49160 | tf_op jit(solution)/shard_map/ppermute | solution.py:140

commit v3 on v2

--- a/solution.py
+++ b/solution.py
@@ -30,14 +30,13 @@
         left, right, (((0,), (0,)), ((), ())), precision=lax.Precision.HIGHEST
     ).astype(BF)
     count = lax.axis_size("row")
-    maps = [own_map]
-    for step in range(1, count):
-        pairs = [(i, (i + step) % count) for i in range(count)]
-        maps.append(lax.ppermute(own_map, "row", pairs))
-    return maps
-
-
-def patch(block, rows, width, port_ref, profile_ref, halo_refs):
+    return [own_map] + [
+        lax.ppermute(own_map, "row", [(i, i ^ step) for i in range(count)])
+        for step in range(1, count)
+    ]
+
+
+def patch(block, rows, width, east_lane, port_ref, profile_ref, halo_refs):
     north, south, west, east = halo_refs
     quarter = block.shape[0] // 4
     port = pl.program_id(0)
@@ -54,7 +53,7 @@
     for row in range(rows):
         place = port * rows + row
         cols = slice(row * LANES, (row + 1) * LANES)
-        from_west = pltpu.roll(west_all, (LANES - place) % LANES, 1)
+        from_west = pltpu.roll(west_all, lax.rem(2 * LANES - east_lane - place, LANES), 1)
         from_east = pltpu.roll(east_all, LANES - 1 - place, 1)
         west_part = block[2 * quarter : 3 * quarter, cols].astype(F32)
         east_part = block[3 * quarter : 4 * quarter, cols].astype(F32)
@@ -75,29 +74,90 @@
         block[:, cols] = jnp.where(here, added, current).astype(BF)
 
 
-def apply_maps(x, types_ref, map_refs, next_ref, rim_refs, rows):
-    north_out, south_out, west_out, east_out = rim_refs
-    order = x.shape[0]
-    quarter = order // 4
-    kinds = len(map_refs)
-    port = pl.program_id(0)
+def products(x, types, map_refs, first, last):
     mine = lax.axis_index("row")
-    types = jnp.broadcast_to(types_ref[...].astype(F32).astype(BF), x.shape)
+    types = jnp.broadcast_to(types, x.shape)
     total = None
-    for step in range(kinds):
-        kind = lax.rem(mine - step + kinds, kinds).astype(F32).astype(BF)
+    for step, map_ref in enumerate(map_refs):
+        kind = (mine ^ step).astype(F32).astype(BF)
         masked = jnp.where(types == kind, x, jnp.zeros((), BF))
-        product = jnp.dot(map_refs[step][...], masked, preferred_element_type=F32)
+        product = jnp.dot(map_ref[first:last, :], masked, preferred_element_type=F32)
         total = product if total is None else total + product
+    return total
+
+
+def shifted(total, next_ref, rows):
+    quarter = total.shape[0] // 4
     last = (rows - 1) * LANES
     north = total[0:quarter].astype(BF)
     south = total[quarter : 2 * quarter].astype(BF)
-    north_out[...] = north[:, 0:LANES]
-    south_out[...] = south[:, last:]
     next_ref[0:quarter, LANES:] = south[:, :last]
     next_ref[0:quarter, 0:LANES] = jnp.zeros((quarter, LANES), BF)
     next_ref[quarter : 2 * quarter, :last] = north[:, LANES:]
     next_ref[quarter : 2 * quarter, last:] = jnp.zeros((quarter, LANES), BF)
+    for row in range(rows):
+        cols = slice(row * LANES, (row + 1) * LANES)
+        west = total[2 * quarter : 3 * quarter, cols]
+        east = total[3 * quarter : 4 * quarter, cols]
+        next_ref[2 * quarter : 3 * quarter, cols] = pltpu.roll(east, 1, 1).astype(BF)
+        next_ref[3 * quarter : 4 * quarter, cols] = pltpu.roll(west, LANES - 1, 1).astype(BF)
+    return north, south
+
+
+def rim_kernel(rows, ports, x_ref, types_ref, *refs):
+    map_refs = refs[:-4]
+    north_out, south_out, west_out, east_out = refs[-4:]
+    order = x_ref.shape[0]
+    quarter = order // 4
+    tile = rows * LANES
+    types = types_ref[...].astype(F32)
+    starts = [port * tile for port in range(ports)]
+    for edge, out, offset in ((0, north_out, 0), (1, south_out, tile - LANES)):
+        cells = jnp.concatenate(
+            [x_ref[:, start + offset : start + offset + LANES] for start in starts], axis=1
+        )
+        kinds = jnp.concatenate([types[:, offset : offset + LANES]] * ports, axis=1).astype(BF)
+        out[...] = products(cells, kinds, map_refs, edge * quarter, (edge + 1) * quarter).astype(BF)
+    wide = 2 * LANES
+    spread = jnp.broadcast_to(types, (16, tile)).astype(BF)
+    place = lax.broadcasted_iota(jnp.int32, (wide, LANES), 0)
+    lane = lax.broadcasted_iota(jnp.int32, (wide, LANES), 1)
+    wanted = jnp.where(lane < 64, lane * LANES, (lane - 64) * LANES + LANES - 1)
+    picked = None
+    for start in range(0, ports * tile, wide):
+        pick = jnp.where(place + start == wanted, 1.0, 0.0).astype(BF)
+        inside = start % tile
+        both = jnp.concatenate(
+            [x_ref[:, start : start + wide], spread[:, inside : inside + wide]], axis=0
+        )
+        part = jnp.dot(both, pick, preferred_element_type=F32)
+        picked = part if picked is None else picked + part
+    cells = picked[0:order].astype(BF)
+    kinds = picked[order : order + 1].astype(BF)
+    sides = products(cells, kinds, map_refs, 2 * quarter, 4 * quarter).astype(BF)
+    west_out[...] = sides[0:quarter]
+    east_out[...] = sides[quarter : 2 * quarter]
+
+
+def first_kernel(rows, x_ref, types_ref, *refs):
+    x = x_ref[...]
+    types = types_ref[...].astype(F32).astype(BF)
+    shifted(products(x, types, refs[:-1], 0, x.shape[0]), refs[-1], rows)
+
+
+def second_kernel(rows, width, port_ref, x_ref, types_ref, profile_ref, *refs):
+    halo_refs, map_refs, next_ref = refs[:4], refs[4:-6], refs[-6]
+    north_out, south_out, west_out, east_out, block = refs[-5:]
+    block[...] = x_ref[...]
+    patch(block, rows, width, 64, port_ref, profile_ref, halo_refs)
+    order = block.shape[0]
+    quarter = order // 4
+    types = types_ref[...].astype(F32).astype(BF)
+    total = products(block[...], types, map_refs, 0, order)
+    north, south = shifted(total, next_ref, rows)
+    north_out[...] = north[:, 0:LANES]
+    south_out[...] = south[:, (rows - 1) * LANES :]
+    port = pl.program_id(0)
     lane = lax.broadcasted_iota(jnp.int32, (quarter, LANES), 1)
     west_rim = jnp.where(port == 0, 0.0, west_out[...].astype(F32))
     east_rim = jnp.where(port == 0, 0.0, east_out[...].astype(F32))
@@ -106,30 +166,17 @@
         cols = slice(row * LANES, (row + 1) * LANES)
         west = total[2 * quarter : 3 * quarter, cols]
         east = total[3 * quarter : 4 * quarter, cols]
-        next_ref[2 * quarter : 3 * quarter, cols] = pltpu.roll(east, 1, 1).astype(BF)
-        next_ref[3 * quarter : 4 * quarter, cols] = pltpu.roll(west, LANES - 1, 1).astype(BF)
         west_rim = jnp.where(lane == place, pltpu.roll(west, place, 1), west_rim)
         east_rim = jnp.where(lane == place, pltpu.roll(east, place + 1, 1), east_rim)
     west_out[...] = west_rim.astype(BF)
     east_out[...] = east_rim.astype(BF)
 
 
-def first_kernel(rows, x_ref, types_ref, *refs):
-    apply_maps(x_ref[...], types_ref, refs[:-5], refs[-5], refs[-4:], rows)
-
-
-def second_kernel(rows, width, port_ref, x_ref, types_ref, profile_ref, *refs):
-    halo_refs, refs = refs[:4], refs[4:]
-    block = refs[-1]
+def last_kernel(rows, width, port_ref, x_ref, profile_ref, *refs):
+    out_ref, block = refs[-2:]
     block[...] = x_ref[...]
-    patch(block, rows, width, port_ref, profile_ref, halo_refs)
-    apply_maps(block[...], types_ref, refs[:-6], refs[-6], refs[-5:-1], rows)
-
-
-def last_kernel(rows, width, port_ref, x_ref, profile_ref, *refs):
-    out_ref = refs[-1]
-    out_ref[...] = x_ref[...]
-    patch(out_ref, rows, width, port_ref, profile_ref, refs[:4])
+    patch(block, rows, width, 0, port_ref, profile_ref, refs[:4])
+    out_ref[...] = block[...].astype(F32).reshape(out_ref.shape).astype(BF)
 
 
 def exchange(rims):
@@ -171,15 +218,26 @@
         jax.ShapeDtypeStruct((quarter, LANES), BF)
     ] * 2
     params = pltpu.CompilerParams(vmem_limit_bytes=20 * 2**20)
-    x, *sent = pl.pallas_call(
+    whole = pl.BlockSpec(memory_space=pltpu.VMEM)
+    work = 2 * order * order * len(maps) * ports * tile
+    sent = pl.pallas_call(
+        functools.partial(rim_kernel, rows, ports),
+        in_specs=[whole] * (2 + len(maps)),
+        out_specs=[whole] * 4,
+        out_shape=rim_shapes,
+        compiler_params=params,
+        cost_estimate=pl.CostEstimate(flops=work // 8, bytes_accessed=0, transcendentals=0),
+    )(x, types, *maps)
+    halos = exchange(sent)
+    x = pl.pallas_call(
         functools.partial(first_kernel, rows),
         grid=(ports,),
         in_specs=[block, types_spec] + map_specs,
-        out_specs=[block] + rims,
-        out_shape=[next_shape] + rim_shapes,
-        compiler_params=params,
+        out_specs=block,
+        out_shape=next_shape,
+        compiler_params=params,
+        cost_estimate=pl.CostEstimate(flops=work, bytes_accessed=0, transcendentals=0),
     )(x, types, *maps)
-    halos = exchange(sent)
     x, *sent = pl.pallas_call(
         functools.partial(second_kernel, rows, width),
         grid=(ports,),
@@ -188,17 +246,19 @@
         out_shape=[next_shape] + rim_shapes,
         scratch_shapes=[pltpu.VMEM((order, tile), BF)],
         compiler_params=params,
+        cost_estimate=pl.CostEstimate(flops=work, bytes_accessed=0, transcendentals=0),
     )(port_cell, x, types, profile, *halos, *maps)
     halos = exchange(sent)
-    x = pl.pallas_call(
+    out = pl.pallas_call(
         functools.partial(last_kernel, rows, width),
         grid=(ports,),
         in_specs=[ports_spec, block, profile_spec] + rims,
-        out_specs=block,
-        out_shape=next_shape,
+        out_specs=pl.BlockSpec((order, 1, rows, LANES), lambda i: (0, i, 0, 0)),
+        out_shape=jax.ShapeDtypeStruct((order, ports, rows, width), BF),
+        scratch_shapes=[pltpu.VMEM((order, tile), BF)],
         compiler_params=params,
     )(port_cell, x, profile, *halos)
-    return x.reshape(traces.shape)
+    return out.reshape(traces.shape)
 
 
 def solution(mesh):

time: 86.7 us -> 81.6 us (0.941)
  waiting for transfers between devices: 12.2 us -> 4.5 us
  local copies, waits for them, and re-layouts: 7.88 us -> 3.18 us
  starting transfers between devices: 32.2 us -> 35.9 us
  Pallas kernels: 14.8 us -> 18.4 us
    ppermute x7, waiting for transfers between devices: 9.31 us -> 3.04 us  [all_maps(): lax.ppermute(own_map, 'row', [(i, i ^ step) for i in range(count)])]
    unnamed x12 -> x7, local copies, waits for them, and re-layouts: 4.73 us -> 0.02 us
    ppermute x7, starting transfers between devices: 13.1 us -> 16.8 us  [all_maps(): lax.ppermute(own_map, 'row', [(i, i ^ step) for i in range(count)])]
    pallas_call x0 -> x1, Pallas kernels: none -> 2.05 us  [body(): pl.pallas_call(functools.partial(rim_kernel, rows, ports), in_specs=[whol...]
    pallas_call x1, Pallas kernels: 1.66 us -> 3.49 us  [body(): pl.pallas_call(functools.partial(last_kernel, rows, width), grid=(ports,)...]
    ppermute x8, waiting for transfers between devices: 2.88 us -> 1.46 us  [send(): lax.ppermute(value, axis, [(i, (i + step) % count) for i in range(count)])]
  transfers between devices with their start and end apart: 15 -> 15, of which waited for: 5 -> 3; matrix products, arithmetic and copies ran while one was open for 3% -> 4% of each run, Pallas kernels for 0% -> 7%
where the time goes in v3:
time: 81.6 us; the launch traced here: 81.3 us
  starting transfers between devices  35.9 us (44%)
  Pallas kernels  18.4 us (23%)
  blocking collectives  17.1 us (21%)
  waiting for transfers between devices  4.5 us (6%)
  local copies, waits for them, and re-layouts  3.18 us (4%)
  other arithmetic  1.52 us (2%)
    ppermute x8, starting transfers between devices, send(): lax.ppermute(value, axis, [(i, (i + step) % count) for i in range(count)])  19.1 us
    all_to_all x1, blocking collectives, gather_modes(): every = lax.all_to_all(spread, 'col', 0, 0, tiled=True)  17.1 us
    ppermute x7, starting transfers between devices, all_maps(): lax.ppermute(own_map, 'row', [(i, i ^ step) for i in range(count)])  16.8 us
    pallas_call x1, Pallas kernels, body(): pl.pallas_call(functools.partial(second_kernel, rows, width), grid=(ports...  7.13 us
    pallas_call x1, Pallas kernels, body(): pl.pallas_call(functools.partial(first_kernel, rows), grid=(ports,), in_s...  5.68 us
    pallas_call x1, Pallas kernels, body(): pl.pallas_call(functools.partial(last_kernel, rows, width), grid=(ports,)...  3.49 us
    ppermute x7, waiting for transfers between devices, all_maps(): lax.ppermute(own_map, 'row', [(i, i ^ step) for i in range(count)])  3.04 us
    reshape x1, local copies, waits for them, and re-layouts, body(): x = traces.reshape(order, ports * tile)  2.83 us
  transfers between devices with their start and end apart: 15, of which 3 were waited for; matrix products, arithmetic and copies ran while one was open for 4% of the time, Pallas kernels for 7%

profile of v3, /device:TPU:0, one launch (start us, length us, event | category | flops | bytes accessed | tf_op | source)
XLA Modules:
  0.0 81.3 jit_solution(10548044470964467426)
XLA Ops:
  0.0 0.0 copy-start.2
  0.0 0.8 multiply_bitcast_fusion
  0.8 0.7 pad_maximum_fusion
  1.6 17.1 %all_to_all.5 = f32[16,32,256]{2,1,0:T(8,128)S(1)} all-to-all(f32[16,32,256]{2,1,0:T(8,128)S(1)} %broadcast_in_dim.4), channel_id=1, replica_groups=mesh['row'=8,'col'=16] {'col'}, dimensions={0} | all-to-all | bytes 1048576 | tf_op jit(solution)/shard_map/all_to_all | solution.py:20
  18.7 0.6 fusion.refs_0_.refs_4_
  19.3 5.3 %collective-permute-start.6 = (bf16[256,256]{1,0:T(8,128)(2,1)S(1)}, bf16[256,256]{1,0:T(8,128)(2,1)S(1)}, u32[]{:S(2)}, u32[]{:S(2)}) collective-permute-start(bf16[256,256]{1,0:T(8,128)(2,1)S(1)} %fusion.refs_0_.refs_4_), channel_id=1, source_target_pairs={{0,112},{16,96},{32,80},{48,64},{64,48},{80,32},{96,16},{112,0},{1... | collective-permute-start | bytes 393224 | tf_op jit(solution)/shard_map/ppermute | solution.py:34
  24.5 0.2 collective-permute-start.5
  24.8 2.2 %collective-permute-start.4 = (bf16[256,256]{1,0:T(8,128)(2,1)S(1)}, bf16[256,256]{1,0:T(8,128)(2,1)S(1)}, u32[]{:S(2)}, u32[]{:S(2)}) collective-permute-start(bf16[256,256]{1,0:T(8,128)(2,1)S(1)} %fusion.refs_0_.refs_4_), channel_id=1, source_target_pairs={{0,80},{16,64},{32,112},{48,96},{64,16},{80,0},{96,48},{112,32},{1... | collective-permute-start | bytes 393224 | tf_op jit(solution)/shard_map/ppermute | solution.py:34
  27.0 1.5 %collective-permute-start.3 = (bf16[256,256]{1,0:T(8,128)(2,1)S(1)}, bf16[256,256]{1,0:T(8,128)(2,1)S(1)}, u32[]{:S(2)}, u32[]{:S(2)}) collective-permute-start(bf16[256,256]{1,0:T(8,128)(2,1)S(1)} %fusion.refs_0_.refs_4_), channel_id=1, source_target_pairs={{0,64},{16,80},{32,96},{48,112},{64,0},{80,16},{96,32},{112,48},{1... | collective-permute-start | bytes 393224 | tf_op jit(solution)/shard_map/ppermute | solution.py:34
  28.5 2.5 %collective-permute-start.2 = (bf16[256,256]{1,0:T(8,128)(2,1)S(1)}, bf16[256,256]{1,0:T(8,128)(2,1)S(1)}, u32[]{:S(2)}, u32[]{:S(2)}) collective-permute-start(bf16[256,256]{1,0:T(8,128)(2,1)S(1)} %fusion.refs_0_.refs_4_), channel_id=1, source_target_pairs={{0,48},{16,32},{32,16},{48,0},{64,112},{80,96},{96,80},{112,64},{1... | collective-permute-start | bytes 393224 | tf_op jit(solution)/shard_map/ppermute | solution.py:34
  31.1 0.0 collective-permute-done.6.refs_7_.refs_11_
  31.1 1.7 %collective-permute-start.1 = (bf16[256,256]{1,0:T(8,128)(2,1)S(1)}, bf16[256,256]{1,0:T(8,128)(2,1)S(1)}, u32[]{:S(2)}, u32[]{:S(2)}) collective-permute-start(bf16[256,256]{1,0:T(8,128)(2,1)S(1)} %fusion.refs_0_.refs_4_), channel_id=1, source_target_pairs={{0,32},{16,48},{32,0},{48,16},{64,96},{80,112},{96,64},{112,80},{1... | collective-permute-start | bytes 393224 | tf_op jit(solution)/shard_map/ppermute | solution.py:34
  32.7 2.6 %collective-permute-done.5.refs_6_.refs_10_ = bf16[256,256]{1,0:T(8,128)(2,1)S(1)} collective-permute-done((bf16[256,256]{1,0:T(8,128)(2,1)S(1)}, bf16[256,256]{1,0:T(8,128)(2,1)S(1)}, u32[]{:S(2)}, u32[]{:S(2)}) %collective-permute-start.5) | collective-permute-done | bytes 131104 | tf_op jit(solution)/shard_map/ppermute | solution.py:34
  35.4 3.3 %collective-permute-start = (bf16[256,256]{1,0:T(8,128)(2,1)S(1)}, bf16[256,256]{1,0:T(8,128)(2,1)S(1)}, u32[]{:S(2)}, u32[]{:S(2)}) collective-permute-start(bf16[256,256]{1,0:T(8,128)(2,1)S(1)} %fusion.refs_0_.refs_4_), channel_id=1, source_target_pairs={{0,16},{16,0},{32,48},{48,32},{64,80},{80,64},{96,112},{112,96},{1... | collective-permute-start | bytes 393224 | tf_op jit(solution)/shard_map/ppermute | solution.py:34
  38.7 0.0 copy-done.2
  38.7 0.1 reshape.21
  38.8 0.0 copy-start
  38.8 2.8 %reshape.19.x_ref = bf16[256,4096]{1,0:T(8,128)(2,1)S(1)} reshape(bf16[4,64,4,8,128]{4,3,2,1,0:T(8,128)(2,1)} %param.7) | data formatting | bytes 4194304 | tf_op jit(solution)/shard_map/reshape | solution.py:203
  41.6 0.0 collective-permute-done.4.refs_5_.refs_9_
  41.6 0.0 collective-permute-done.3.refs_4_.refs_8_
  41.6 0.0 collective-permute-done.2.refs_3_.refs_7_
  41.7 0.0 collective-permute-done.1.refs_2_.refs_6_
  41.7 0.4 collective-permute-done.refs_1_.refs_5_
  42.1 0.0 copy-done
  42.1 2.1 %shard_map.74 = (bf16[64,512]{1,0:T(8,128)(2,1)S(1)}, bf16[64,512]{1,0:T(8,128)(2,1)S(1)}, bf16[64,128]{1,0:T(8,128)(2,1)S(1)}, bf16[64,128]{1,0:T(8,128)(2,1)S(1)}) custom-call(bf16[256,4096]{1,0:T(8,128)(2,1)S(1)} %reshape.19.x_ref, s32[1,1024]{1,0:T(1,128)S(1)} %bitcast.17, bf16[256,256]{1,0:T(8,128)(2,1)S(1)} %fusion.refs_0_.refs_4_, ...), custom_call_target="tpu_custom_call" | custom-call | flops 536870912 | tf_op jit(solution)/shard_map/pallas_call | solution.py:223
  44.1 0.1 collective-permute-start.9
  44.2 3.8 %collective-permute-start.10 = (bf16[64,128]{1,0:T(8,128)(2,1)S(1)}, bf16[64,128]{1,0:T(8,128)(2,1)S(1)}, u32[]{:S(2)}, u32[]{:S(2)}) collective-permute-start(bf16[64,128]{1,0:T(8,128)(2,1)S(1)} %get-tuple-element.17), channel_id=1, source_target_pairs={{0,15},{1,0},{2,1},{3,2},{4,3},{5,4},{6,5},{7,6},{8,7},{9,8},{10,9... | collective-permute-start | bytes 49160 | tf_op jit(solution)/shard_map/ppermute | solution.py:187
  48.1 3.2 %collective-permute-start.7 = (bf16[64,512]{1,0:T(8,128)(2,1)S(1)}, bf16[64,512]{1,0:T(8,128)(2,1)S(1)}, u32[]{:S(2)}, u32[]{:S(2)}) collective-permute-start(bf16[64,512]{1,0:T(8,128)(2,1)S(1)} %get-tuple-element.14), channel_id=1, source_target_pairs={{0,16},{16,32},{32,48},{48,64},{64,80},{80,96},{96,112},{112,0},{1... | collective-permute-start | bytes 196616 | tf_op jit(solution)/shard_map/ppermute | solution.py:187
  51.3 0.0 copy-start.1
  51.3 2.4 %collective-permute-start.8 = (bf16[64,512]{1,0:T(8,128)(2,1)S(1)}, bf16[64,512]{1,0:T(8,128)(2,1)S(1)}, u32[]{:S(2)}, u32[]{:S(2)}) collective-permute-start(bf16[64,512]{1,0:T(8,128)(2,1)S(1)} %get-tuple-element.15), channel_id=1, source_target_pairs={{0,112},{16,0},{32,16},{48,32},{64,48},{80,64},{96,80},{112,96},{1... | collective-permute-start | bytes 196616 | tf_op jit(solution)/shard_map/ppermute | solution.py:187
  53.7 5.7 %shard_map.73.x_ref = bf16[256,4096]{1,0:T(8,128)(2,1)S(1)} custom-call(bf16[256,4096]{1,0:T(8,128)(2,1)S(1)} %reshape.19.x_ref, s32[1,1024]{1,0:T(1,128)S(1)} %bitcast.18, bf16[256,256]{1,0:T(8,128)(2,1)S(1)} %fusion.refs_0_.refs_4_, bf16[256,256]{1,0:T(8,128)(2,1)S(1)} %collective-permute-done.refs_1_.refs_5_, ...), custom_call_target="tpu_custom_call" | custom-call | flops 4294967296 | tf_op jit(solution)/shard_map/pallas_call | solution.py:232
  59.4 0.0 collective-permute-done.9.refs_2_
  59.4 0.0 collective-permute-done.10.refs_3_
  59.4 0.0 collective-permute-done.7.refs_0_
  59.4 0.0 collective-permute-done.8.refs_1_
  59.4 0.2 broadcast_in_dim.5.profile_ref
  59.6 0.0 copy-done.1
  59.6 7.1 %shard_map.75 = (bf16[256,4096]{1,0:T(8,128)(2,1)S(1)}, bf16[64,512]{1,0:T(8,128)(2,1)S(1)}, bf16[64,512]{1,0:T(8,128)(2,1)S(1)}, bf16[64,128]{1,0:T(8,128)(2,1)S(1)}, bf16[64,128]{1,0:T(8,128)(2,1)S(1)}) custom-call(s32[4]{0:T(128)S(1)} %copy-done.1, bf16[256,4096]{1,0:T(8,128)(2,1)S(1)} %shard_map.73.x_ref, s32[1,1024]{1,0:T(1,128)S(1)} %bitcast.19, ...), custom_call_target="tpu_custom_call" | custom-call | flops 4294967296 | tf_op jit(solution)/shard_map/pallas_call | solution.py:241
  66.8 1.2 %collective-permute-start.11 = (bf16[64,512]{1,0:T(8,128)(2,1)S(1)}, bf16[64,512]{1,0:T(8,128)(2,1)S(1)}, u32[]{:S(2)}, u32[]{:S(2)}) collective-permute-start(bf16[64,512]{1,0:T(8,128)(2,1)S(1)} %get-tuple-element.19), channel_id=1, source_target_pairs={{0,16},{16,32},{32,48},{48,64},{64,80},{80,96},{96,112},{112,0},{1... | collective-permute-start | bytes 196616 | tf_op jit(solution)/shard_map/ppermute | solution.py:187
  68.0 4.5 %collective-permute-start.12 = (bf16[64,512]{1,0:T(8,128)(2,1)S(1)}, bf16[64,512]{1,0:T(8,128)(2,1)S(1)}, u32[]{:S(2)}, u32[]{:S(2)}) collective-permute-start(bf16[64,512]{1,0:T(8,128)(2,1)S(1)} %get-tuple-element.20), channel_id=1, source_target_pairs={{0,112},{16,0},{32,16},{48,32},{64,48},{80,64},{96,80},{112,96},{1... | collective-permute-start | bytes 196616 | tf_op jit(solution)/shard_map/ppermute | solution.py:187
  72.5 0.0 collective-permute-start.13
  72.5 3.9 %collective-permute-start.14 = (bf16[64,128]{1,0:T(8,128)(2,1)S(1)}, bf16[64,128]{1,0:T(8,128)(2,1)S(1)}, u32[]{:S(2)}, u32[]{:S(2)}) collective-permute-start(bf16[64,128]{1,0:T(8,128)(2,1)S(1)} %get-tuple-element.22), channel_id=1, source_target_pairs={{0,15},{1,0},{2,1},{3,2},{4,3},{5,4},{6,5},{7,6},{8,7},{9,8},{10,9... | collective-permute-start | bytes 49160 | tf_op jit(solution)/shard_map/ppermute | solution.py:187
  76.3 1.4 %collective-permute-done.13.refs_2_ = bf16[64,128]{1,0:T(8,128)(2,1)S(1)} collective-permute-done((bf16[64,128]{1,0:T(8,128)(2,1)S(1)}, bf16[64,128]{1,0:T(8,128)(2,1)S(1)}, u32[]{:S(2)}, u32[]{:S(2)}) %collective-permute-start.13) | collective-permute-done | bytes 16416 | tf_op jit(solution)/shard_map/ppermute | solution.py:187
  77.8 0.0 collective-permute-done.14.refs_3_
  77.8 0.0 collective-permute-done.11.refs_0_
  77.8 0.0 collective-permute-done.12.refs_1_
  77.8 3.5 %shard_map.76 = bf16[256,4,8,128]{3,2,1,0:T(8,128)(2,1)} custom-call(s32[4]{0:T(128)S(1)} %copy-done.1, bf16[256,4096]{1,0:T(8,128)(2,1)S(1)} %get-tuple-element.18.x_ref, bf16[4,256,128]{2,1,0:T(8,128)(2,1)S(1)} %broadcast_in_dim.5.profile_ref, bf16[64,512]{1,0:T(8,128)(2,1)S(1)} %collective-permute-done.11.refs_0_, ...), custom_call_target="tpu_custom_call" | custom-call | tf_op jit(solution)/shard_map/pallas_call | solution.py:252
  (2 shorter events, 0.0 us)
Async XLA Ops:
  0.0 38.7 %copy-start.2 = (bf16[4,64,4]{1,2,0:T(4,128)(2,1)S(1)}, bf16[4,64,4]{1,2,0:T(4,128)(2,1)}, u32[]{:S(2)}) copy-start(bf16[4,64,4]{1,2,0:T(4,128)(2,1)} %param.10) | copy-start | bytes 6148
  19.3 11.8 %collective-permute-start.6 = (bf16[256,256]{1,0:T(8,128)(2,1)S(1)}, bf16[256,256]{1,0:T(8,128)(2,1)S(1)}, u32[]{:S(2)}, u32[]{:S(2)}) collective-permute-start(bf16[256,256]{1,0:T(8,128)(2,1)S(1)} %fusion.refs_0_.refs_4_), channel_id=1, source_target_pairs={{0,112},{16,96},{32,80},{48,64},{64,48},{80,32},{96,16},{112,0},{1... | collective-permute-start | bytes 393224 | tf_op jit(solution)/shard_map/ppermute | solution.py:34
  24.5 10.8 %collective-permute-start.5 = (bf16[256,256]{1,0:T(8,128)(2,1)S(1)}, bf16[256,256]{1,0:T(8,128)(2,1)S(1)}, u32[]{:S(2)}, u32[]{:S(2)}) collective-permute-start(bf16[256,256]{1,0:T(8,128)(2,1)S(1)} %fusion.refs_0_.refs_4_), channel_id=1, source_target_pairs={{0,96},{16,112},{32,64},{48,80},{64,32},{80,48},{96,0},{112,16},{1... | collective-permute-start | bytes 393224 | tf_op jit(solution)/shard_map/ppermute | solution.py:34
  24.8 16.9 %collective-permute-start.4 = (bf16[256,256]{1,0:T(8,128)(2,1)S(1)}, bf16[256,256]{1,0:T(8,128)(2,1)S(1)}, u32[]{:S(2)}, u32[]{:S(2)}) collective-permute-start(bf16[256,256]{1,0:T(8,128)(2,1)S(1)} %fusion.refs_0_.refs_4_), channel_id=1, source_target_pairs={{0,80},{16,64},{32,112},{48,96},{64,16},{80,0},{96,48},{112,32},{1... | collective-permute-start | bytes 393224 | tf_op jit(solution)/shard_map/ppermute | solution.py:34
  27.0 14.7 %collective-permute-start.3 = (bf16[256,256]{1,0:T(8,128)(2,1)S(1)}, bf16[256,256]{1,0:T(8,128)(2,1)S(1)}, u32[]{:S(2)}, u32[]{:S(2)}) collective-permute-start(bf16[256,256]{1,0:T(8,128)(2,1)S(1)} %fusion.refs_0_.refs_4_), channel_id=1, source_target_pairs={{0,64},{16,80},{32,96},{48,112},{64,0},{80,16},{96,32},{112,48},{1... | collective-permute-start | bytes 393224 | tf_op jit(solution)/shard_map/ppermute | solution.py:34
  28.5 13.1 %collective-permute-start.2 = (bf16[256,256]{1,0:T(8,128)(2,1)S(1)}, bf16[256,256]{1,0:T(8,128)(2,1)S(1)}, u32[]{:S(2)}, u32[]{:S(2)}) collective-permute-start(bf16[256,256]{1,0:T(8,128)(2,1)S(1)} %fusion.refs_0_.refs_4_), channel_id=1, source_target_pairs={{0,48},{16,32},{32,16},{48,0},{64,112},{80,96},{96,80},{112,64},{1... | collective-permute-start | bytes 393224 | tf_op jit(solution)/shard_map/ppermute | solution.py:34
  31.1 10.6 %collective-permute-start.1 = (bf16[256,256]{1,0:T(8,128)(2,1)S(1)}, bf16[256,256]{1,0:T(8,128)(2,1)S(1)}, u32[]{:S(2)}, u32[]{:S(2)}) collective-permute-start(bf16[256,256]{1,0:T(8,128)(2,1)S(1)} %fusion.refs_0_.refs_4_), channel_id=1, source_target_pairs={{0,32},{16,48},{32,0},{48,16},{64,96},{80,112},{96,64},{112,80},{1... | collective-permute-start | bytes 393224 | tf_op jit(solution)/shard_map/ppermute | solution.py:34
  35.4 6.7 %collective-permute-start = (bf16[256,256]{1,0:T(8,128)(2,1)S(1)}, bf16[256,256]{1,0:T(8,128)(2,1)S(1)}, u32[]{:S(2)}, u32[]{:S(2)}) collective-permute-start(bf16[256,256]{1,0:T(8,128)(2,1)S(1)} %fusion.refs_0_.refs_4_), channel_id=1, source_target_pairs={{0,16},{16,0},{32,48},{48,32},{64,80},{80,64},{96,112},{112,96},{1... | collective-permute-start | bytes 393224 | tf_op jit(solution)/shard_map/ppermute | solution.py:34
  38.8 3.3 %copy-start = (s32[8,128]{1,0:T(8,128)S(1)}, s32[8,128]{1,0:T(8,128)}, u32[]{:S(2)}) copy-start(s32[8,128]{1,0:T(8,128)} %param.8) | copy-start | bytes 12292
  44.1 15.3 %collective-permute-start.9 = (bf16[64,128]{1,0:T(8,128)(2,1)S(1)}, bf16[64,128]{1,0:T(8,128)(2,1)S(1)}, u32[]{:S(2)}, u32[]{:S(2)}) collective-permute-start(bf16[64,128]{1,0:T(8,128)(2,1)S(1)} %get-tuple-element.16), channel_id=1, source_target_pairs={{0,1},{1,2},{2,3},{3,4},{4,5},{5,6},{6,7},{7,8},{8,9},{9,10},{10,1... | collective-permute-start | bytes 49160 | tf_op jit(solution)/shard_map/ppermute | solution.py:187
  44.2 15.2 %collective-permute-start.10 = (bf16[64,128]{1,0:T(8,128)(2,1)S(1)}, bf16[64,128]{1,0:T(8,128)(2,1)S(1)}, u32[]{:S(2)}, u32[]{:S(2)}) collective-permute-start(bf16[64,128]{1,0:T(8,128)(2,1)S(1)} %get-tuple-element.17), channel_id=1, source_target_pairs={{0,15},{1,0},{2,1},{3,2},{4,3},{5,4},{6,5},{7,6},{8,7},{9,8},{10,9... | collective-permute-start | bytes 49160 | tf_op jit(solution)/shard_map/ppermute | solution.py:187
  48.1 11.4 %collective-permute-start.7 = (bf16[64,512]{1,0:T(8,128)(2,1)S(1)}, bf16[64,512]{1,0:T(8,128)(2,1)S(1)}, u32[]{:S(2)}, u32[]{:S(2)}) collective-permute-start(bf16[64,512]{1,0:T(8,128)(2,1)S(1)} %get-tuple-element.14), channel_id=1, source_target_pairs={{0,16},{16,32},{32,48},{48,64},{64,80},{80,96},{96,112},{112,0},{1... | collective-permute-start | bytes 196616 | tf_op jit(solution)/shard_map/ppermute | solution.py:187
  51.3 8.3 %copy-start.1 = (s32[4]{0:T(128)S(1)}, s32[4]{0:T(128)}, u32[]{:S(2)}) copy-start(s32[4]{0:T(128)} %port_ref.3) | copy-start | bytes 52
  51.3 8.1 %collective-permute-start.8 = (bf16[64,512]{1,0:T(8,128)(2,1)S(1)}, bf16[64,512]{1,0:T(8,128)(2,1)S(1)}, u32[]{:S(2)}, u32[]{:S(2)}) collective-permute-start(bf16[64,512]{1,0:T(8,128)(2,1)S(1)} %get-tuple-element.15), channel_id=1, source_target_pairs={{0,112},{16,0},{32,16},{48,32},{64,48},{80,64},{96,80},{112,96},{1... | collective-permute-start | bytes 196616 | tf_op jit(solution)/shard_map/ppermute | solution.py:187
  66.8 11.0 %collective-permute-start.11 = (bf16[64,512]{1,0:T(8,128)(2,1)S(1)}, bf16[64,512]{1,0:T(8,128)(2,1)S(1)}, u32[]{:S(2)}, u32[]{:S(2)}) collective-permute-start(bf16[64,512]{1,0:T(8,128)(2,1)S(1)} %get-tuple-element.19), channel_id=1, source_target_pairs={{0,16},{16,32},{32,48},{48,64},{64,80},{80,96},{96,112},{112,0},{1... | collective-permute-start | bytes 196616 | tf_op jit(solution)/shard_map/ppermute | solution.py:187
  68.0 9.8 %collective-permute-start.12 = (bf16[64,512]{1,0:T(8,128)(2,1)S(1)}, bf16[64,512]{1,0:T(8,128)(2,1)S(1)}, u32[]{:S(2)}, u32[]{:S(2)}) collective-permute-start(bf16[64,512]{1,0:T(8,128)(2,1)S(1)} %get-tuple-element.20), channel_id=1, source_target_pairs={{0,112},{16,0},{32,16},{48,32},{64,48},{80,64},{96,80},{112,96},{1... | collective-permute-start | bytes 196616 | tf_op jit(solution)/shard_map/ppermute | solution.py:187
  72.5 5.3 %collective-permute-start.13 = (bf16[64,128]{1,0:T(8,128)(2,1)S(1)}, bf16[64,128]{1,0:T(8,128)(2,1)S(1)}, u32[]{:S(2)}, u32[]{:S(2)}) collective-permute-start(bf16[64,128]{1,0:T(8,128)(2,1)S(1)} %get-tuple-element.21), channel_id=1, source_target_pairs={{0,1},{1,2},{2,3},{3,4},{4,5},{5,6},{6,7},{7,8},{8,9},{9,10},{10,1... | collective-permute-start | bytes 49160 | tf_op jit(solution)/shard_map/ppermute | solution.py:187
  72.5 5.3 %collective-permute-start.14 = (bf16[64,128]{1,0:T(8,128)(2,1)S(1)}, bf16[64,128]{1,0:T(8,128)(2,1)S(1)}, u32[]{:S(2)}, u32[]{:S(2)}) collective-permute-start(bf16[64,128]{1,0:T(8,128)(2,1)S(1)} %get-tuple-element.22), channel_id=1, source_target_pairs={{0,15},{1,0},{2,1},{3,2},{4,3},{5,4},{6,5},{7,6},{8,7},{9,8},{10,9... | collective-permute-start | bytes 49160 | tf_op jit(solution)/shard_map/ppermute | solution.py:187

commit v4 on v3

--- a/solution.py
+++ b/solution.py
@@ -12,28 +12,44 @@
 LANES = 128
 
 
-def gather_modes(mode_shapes, mode_values, mode_weights):
+def swap(value, axis, first, second=None):
+    second = first if second is None else second
+    rows, cols = lax.axis_size("row"), lax.axis_size("col")
+    pairs = []
+    for row in range(rows):
+        for col in range(cols):
+            step = second if col % 2 else first
+            other = (row ^ step, col) if axis == "row" else (row, col ^ step)
+            pairs.append((row * cols + col, other[0] * cols + other[1]))
+    return lax.ppermute(value, ("row", "col"), pairs)
+
+
+def own_type_map(mode_shapes, mode_values, mode_weights, x):
     scaled = (mode_shapes * mode_values[:, None, :])[0].T
     own = jnp.concatenate([scaled, mode_weights[0]], axis=0)
-    count = lax.axis_size("col")
-    spread = jnp.broadcast_to(own[None], (count,) + own.shape)
-    every = lax.all_to_all(spread, "col", 0, 0, tiled=True)
-    modes = scaled.shape[0]
-    left = every[:, :modes].reshape(count * modes, -1)
-    right = every[:, modes:].reshape(count * modes, -1)
-    return left, right
-
-
-def all_maps(mode_shapes, mode_values, mode_weights):
-    left, right = gather_modes(mode_shapes, mode_values, mode_weights)
-    own_map = lax.dot_general(
+    far = swap(own, "col", 4)
+    pair = jnp.concatenate([own, swap(own, "col", 1)], axis=0)
+    got = [swap(pair, "col", 8, 10), swap(pair, "col", 2, 14), swap(pair, "col", 6, 12)]
+    *got, x = lax.optimization_barrier((*got, x))
+    every = jnp.concatenate([own, far] + got, axis=0).reshape((-1, 2) + scaled.shape)
+    left = every[:, 0].reshape(-1, scaled.shape[1])
+    right = every[:, 1].reshape(-1, scaled.shape[1])
+    partial = lax.dot_general(
         left, right, (((0,), (0,)), ((), ())), precision=lax.Precision.HIGHEST
-    ).astype(BF)
-    count = lax.axis_size("row")
-    return [own_map] + [
-        lax.ppermute(own_map, "row", [(i, i ^ step) for i in range(count)])
-        for step in range(1, count)
-    ]
+    )
+    partial = lax.optimization_barrier(partial)
+    return (partial + swap(partial, "col", 1)).astype(BF), x
+
+
+MAP_STEPS = ((0, 0), (1, 3), (2, 7), (6, 5), (3, 1), (7, 2), (5, 6), (4, 4))
+
+
+def all_maps(own_map):
+    core = lax.rem(lax.axis_index("col"), 2)
+    half = own_map.shape[0] // 2
+    mine = swap(lax.dynamic_slice_in_dim(own_map, core * half, half), "row", 4)
+    got = [swap(own_map, "row", first, second) for first, second in MAP_STEPS[1:4]]
+    return [own_map] + got + [swap(value, "col", 1) for value in got + [mine]] + [mine]
 
 
 def patch(block, rows, width, east_lane, port_ref, profile_ref, halo_refs):
@@ -78,10 +94,17 @@
     mine = lax.axis_index("row")
     types = jnp.broadcast_to(types, x.shape)
     total = None
-    for step, map_ref in enumerate(map_refs):
-        kind = (mine ^ step).astype(F32).astype(BF)
+    core = lax.rem(lax.axis_index("col"), 2)
+    for number, (even, odd) in enumerate(MAP_STEPS):
+        kind = (mine ^ jnp.where(core == 0, even, odd)).astype(F32).astype(BF)
         masked = jnp.where(types == kind, x, jnp.zeros((), BF))
-        product = jnp.dot(map_ref[first:last, :], masked, preferred_element_type=F32)
+        if number + 1 < len(MAP_STEPS):
+            part = map_refs[number][first:last, :]
+        else:
+            swapped, own = map_refs[number][...], map_refs[number + 1][...]
+            low, high = jnp.where(core == 0, own, swapped), jnp.where(core == 0, swapped, own)
+            part = jnp.concatenate([low, high], axis=0)[first:last]
+        product = jnp.dot(part, masked, preferred_element_type=F32)
         total = product if total is None else total + product
     return total
 
@@ -199,15 +222,16 @@
     order = edges * samples
     quarter = samples
     tile = rows * width
-    maps = all_maps(mode_shapes, mode_values, mode_weights)
     x = traces.reshape(order, ports * tile)
+    own_map, x = own_type_map(mode_shapes, mode_values, mode_weights, x)
+    maps = all_maps(own_map)
     types = cell_type.reshape(1, tile)
     profile = jnp.broadcast_to(
         jnp.transpose(port_profile.reshape(order, ports))[:, :, None], (ports, order, LANES)
     )
     block = pl.BlockSpec((order, tile), lambda i: (0, i))
     types_spec = pl.BlockSpec((1, tile), lambda i: (0, 0))
-    map_specs = [pl.BlockSpec((order, order), lambda i: (0, 0))] * len(maps)
+    map_specs = [pl.BlockSpec(value.shape, lambda i: (0, 0)) for value in maps]
     long_rim = pl.BlockSpec((quarter, LANES), lambda i: (0, i))
     short_rim = pl.BlockSpec((quarter, LANES), lambda i: (0, 0))
     rims = [long_rim, long_rim, short_rim, short_rim]
@@ -219,7 +243,7 @@
     ] * 2
     params = pltpu.CompilerParams(vmem_limit_bytes=20 * 2**20)
     whole = pl.BlockSpec(memory_space=pltpu.VMEM)
-    work = 2 * order * order * len(maps) * ports * tile
+    work = 2 * order * order * len(MAP_STEPS) * ports * tile
     sent = pl.pallas_call(
         functools.partial(rim_kernel, rows, ports),
         in_specs=[whole] * (2 + len(maps)),

time: 81.6 us -> 75.2 us (0.922)
  blocking collectives: 17.1 us -> 0 us
  starting transfers between devices: 35.9 us -> 44 us
  waiting for transfers between devices: 4.5 us -> 6.32 us
    all_to_all x1 -> x0, blocking collectives: 17.1 us -> none  [gather_modes(): every = lax.all_to_all(spread, 'col', 0, 0, tiled=True)]
    ppermute x7 -> x14, starting transfers between devices: 16.8 us -> 24.9 us  [swap(): return lax.ppermute(value, ('row', 'col'), pairs)]
    ppermute x7 -> x14, waiting for transfers between devices: 3.04 us -> 4.86 us  [swap(): return lax.ppermute(value, ('row', 'col'), pairs)]
  transfers between devices with their start and end apart: 15 -> 22, of which waited for: 3 -> 4; matrix products, arithmetic and copies ran while one was open for 4% -> 5% of each run, Pallas kernels for 7% -> 8%
where the time goes in v4:
time: 75.2 us; the launch traced here: 74.8 us
  starting transfers between devices  44 us (59%)
  Pallas kernels  18.5 us (25%)
  waiting for transfers between devices  6.32 us (8%)
  local copies, waits for them, and re-layouts  3.89 us (5%)
  other arithmetic  1.55 us (2%)
    ppermute x14, starting transfers between devices, swap(): return lax.ppermute(value, ('row', 'col'), pairs)  24.9 us
    ppermute x8, starting transfers between devices, send(): lax.ppermute(value, axis, [(i, (i + step) % count) for i in range(count)])  19.1 us
    pallas_call x1, Pallas kernels, body(): pl.pallas_call(functools.partial(second_kernel, rows, width), grid=(ports...  7.2 us
    pallas_call x1, Pallas kernels, body(): pl.pallas_call(functools.partial(first_kernel, rows), grid=(ports,), in_s...  5.75 us
    ppermute x14, waiting for transfers between devices, swap(): return lax.ppermute(value, ('row', 'col'), pairs)  4.86 us
    pallas_call x1, Pallas kernels, body(): pl.pallas_call(functools.partial(last_kernel, rows, width), grid=(ports,)...  3.48 us
    reshape x1, local copies, waits for them, and re-layouts, body(): x = traces.reshape(order, ports * tile)  2.83 us
    pallas_call x1, Pallas kernels, body(): pl.pallas_call(functools.partial(rim_kernel, rows, ports), in_specs=[whol...  2.07 us
  transfers between devices with their start and end apart: 22, of which 4 were waited for; matrix products, arithmetic and copies ran while one was open for 5% of the time, Pallas kernels for 8%

profile of v4, /device:TPU:0, one launch (start us, length us, event | category | flops | bytes accessed | tf_op | source)
XLA Modules:
  0.0 74.8 jit_solution(17464275482723789667)
XLA Ops:
  0.0 0.8 %constant_dynamic-update-slice_fusion.5 = (f32[256,256]{1,0:T(8,128)S(1)}, f32[16,256]{1,0:T(8,128)S(1)}) fusion(f32[1,256,16]{1,2,0:T(8,128)} %param.11, f32[16]{0:T(128)} %bitcast.35), kind=kLoop, calls=%fused_computation.12 | loop fusion | flops 4095 | bytes 49216
  0.8 0.7 pad_maximum_fusion.1
  1.5 4.0 %collective-permute-start.4 = (f32[32,256]{1,0:T(8,128)S(1)}, f32[32,256]{1,0:T(8,128)S(1)}, u32[]{:S(2)}, u32[]{:S(2)}) collective-permute-start(f32[32,256]{1,0:T(8,128)S(1)} %pad_maximum_fusion.1), channel_id=1, source_target_pairs={{0,4},{1,5},{2,6},{3,7},{4,0},{5,1},{6,2},{7,3},{8,12},{9,13},{10,... | collective-permute-start | bytes 98312 | tf_op jit(solution)/shard_map/ppermute | solution.py:24
  5.5 0.0 collective-permute-start
  5.5 0.7 constant_dynamic-update-slice_fusion.4
  6.2 0.0 copy-start.2
  6.2 2.8 %reshape.25.x_ref = bf16[256,4096]{1,0:T(8,128)(2,1)S(1)} reshape(bf16[4,64,4,8,128]{4,3,2,1,0:T(8,128)(2,1)} %param.7) | data formatting | bytes 4194304 | tf_op jit(solution)/shard_map/reshape | solution.py:225
  9.0 0.0 copy-start.3
  9.1 0.0 copy-start
  9.1 0.0 collective-permute-done
  9.1 0.0 copy-done.2
  9.1 0.8 %collective-permute-start.3 = (f32[64,256]{1,0:T(8,128)S(1)}, f32[64,256]{1,0:T(8,128)S(1)}, u32[]{:S(2)}, u32[]{:S(2)}) collective-permute-start(f32[64,256]{1,0:T(8,128)S(1)} %pad_maximum_fusion), channel_id=1, source_target_pairs={{0,6},{1,13},{2,4},{3,15},{4,2},{5,9},{6,0},{7,11},{8,14},{9,5},{1... | collective-permute-start | bytes 196616 | tf_op jit(solution)/shard_map/ppermute | solution.py:24
  9.9 0.4 collective-permute-start.2
  10.3 1.5 %collective-permute-start.1 = (f32[64,256]{1,0:T(8,128)S(1)}, f32[64,256]{1,0:T(8,128)S(1)}, u32[]{:S(2)}, u32[]{:S(2)}) collective-permute-start(f32[64,256]{1,0:T(8,128)S(1)} %pad_maximum_fusion), channel_id=1, source_target_pairs={{0,8},{1,11},{2,10},{3,9},{4,12},{5,15},{6,14},{7,13},{8,0},{9,3},... | collective-permute-start | bytes 196616 | tf_op jit(solution)/shard_map/ppermute | solution.py:24
  11.8 0.0 collective-permute-done.4
  11.8 2.9 %collective-permute-done.3 = f32[64,256]{1,0:T(8,128)S(1)} collective-permute-done((f32[64,256]{1,0:T(8,128)S(1)}, f32[64,256]{1,0:T(8,128)S(1)}, u32[]{:S(2)}, u32[]{:S(2)}) %collective-permute-start.3) | collective-permute-done | bytes 65568 | tf_op jit(solution)/shard_map/ppermute | solution.py:24
  14.7 0.0 collective-permute-done.2
  14.7 0.0 collective-permute-done.1
  14.7 0.4 convolution_bitcast_fusion
  15.1 3.1 %collective-permute-start.5 = (f32[256,256]{1,0:T(8,128)S(1)}, f32[256,256]{1,0:T(8,128)S(1)}, u32[]{:S(2)}, u32[]{:S(2)}) collective-permute-start(f32[256,256]{1,0:T(8,128)S(1)} %convolution_bitcast_fusion), channel_id=1, source_target_pairs={{0,1},{1,0},{2,3},{3,2},{4,5},{5,4},{6,7},{7,6},{8,9},{9,8},{10,11... | collective-permute-start | bytes 786440 | tf_op jit(solution)/shard_map/ppermute | solution.py:24
  18.3 1.2 %collective-permute-done.5 = f32[256,256]{1,0:T(8,128)S(1)} collective-permute-done((f32[256,256]{1,0:T(8,128)S(1)}, f32[256,256]{1,0:T(8,128)S(1)}, u32[]{:S(2)}, u32[]{:S(2)}) %collective-permute-start.5) | collective-permute-done | bytes 262176 | tf_op jit(solution)/shard_map/ppermute | solution.py:24
  19.5 3.1 %collective-permute-start.8 = (bf16[256,256]{1,0:T(8,128)(2,1)S(1)}, bf16[256,256]{1,0:T(8,128)(2,1)S(1)}, u32[]{:S(2)}, u32[]{:S(2)}) collective-permute-start(bf16[256,256]{1,0:T(8,128)(2,1)S(1)} %add_convert_fusion.refs_0_.refs_4_), channel_id=1, source_target_pairs={{0,96},{1,81},{2,98},{3,83},{4,100},{5,85},{6,102},{7,87},{8,104},... | collective-permute-start | bytes 393224 | tf_op jit(solution)/shard_map/ppermute | solution.py:24
  22.6 0.1 collective-permute-start.7
  22.7 3.0 %collective-permute-start.6 = (bf16[256,256]{1,0:T(8,128)(2,1)S(1)}, bf16[256,256]{1,0:T(8,128)(2,1)S(1)}, u32[]{:S(2)}, u32[]{:S(2)}) collective-permute-start(bf16[256,256]{1,0:T(8,128)(2,1)S(1)} %add_convert_fusion.refs_0_.refs_4_), channel_id=1, source_target_pairs={{0,16},{1,49},{2,18},{3,51},{4,20},{5,53},{6,22},{7,55},{8,24},{9,... | collective-permute-start | bytes 393224 | tf_op jit(solution)/shard_map/ppermute | solution.py:24
  25.7 1.5 %collective-permute-start.12 = (bf16[128,256]{1,0:T(8,128)(2,1)S(1)}, bf16[128,256]{1,0:T(8,128)(2,1)S(1)}, u32[]{:S(2)}, u32[]{:S(2)}) collective-permute-start(bf16[128,256]{1,0:T(8,128)(2,1)S(1)} %constant_dynamic-slice_fusion), channel_id=1, source_target_pairs={{0,64},{1,65},{2,66},{3,67},{4,68},{5,69},{6,70},{7,71},{8,72},{9,... | collective-permute-start | bytes 196616 | tf_op jit(solution)/shard_map/ppermute | solution.py:24
  27.3 0.0 collective-permute-done.8.refs_3_.refs_7_
  27.3 4.3 %collective-permute-start.11 = (bf16[256,256]{1,0:T(8,128)(2,1)S(1)}, bf16[256,256]{1,0:T(8,128)(2,1)S(1)}, u32[]{:S(2)}, u32[]{:S(2)}) collective-permute-start(bf16[256,256]{1,0:T(8,128)(2,1)S(1)} %collective-permute-done.8.refs_3_.refs_7_), channel_id=1, source_target_pairs={{0,1},{1,0},{2,3},{3,2},{4,5},{5,4},{6,7},{7,6},{8,9},{9,8},{10,11... | collective-permute-start | bytes 393224 | tf_op jit(solution)/shard_map/ppermute | solution.py:24
  31.6 0.0 collective-permute-done.7.refs_2_.refs_6_
  31.6 1.2 %collective-permute-start.10 = (bf16[256,256]{1,0:T(8,128)(2,1)S(1)}, bf16[256,256]{1,0:T(8,128)(2,1)S(1)}, u32[]{:S(2)}, u32[]{:S(2)}) collective-permute-start(bf16[256,256]{1,0:T(8,128)(2,1)S(1)} %collective-permute-done.7.refs_2_.refs_6_), channel_id=1, source_target_pairs={{0,1},{1,0},{2,3},{3,2},{4,5},{5,4},{6,7},{7,6},{8,9},{9,8},{10,11... | collective-permute-start | bytes 393224 | tf_op jit(solution)/shard_map/ppermute | solution.py:24
  32.7 0.0 collective-permute-done.6.refs_1_.refs_5_
  32.7 0.0 collective-permute-start.9
  32.7 0.0 collective-permute-done.12.refs_8_.refs_12_
  32.7 1.8 %collective-permute-start.13 = (bf16[128,256]{1,0:T(8,128)(2,1)S(1)}, bf16[128,256]{1,0:T(8,128)(2,1)S(1)}, u32[]{:S(2)}, u32[]{:S(2)}) collective-permute-start(bf16[128,256]{1,0:T(8,128)(2,1)S(1)} %collective-permute-done.12.refs_8_.refs_12_), channel_id=1, source_target_pairs={{0,1},{1,0},{2,3},{3,2},{4,5},{5,4},{6,7},{7,6},{8,9},{9,8},{10,11... | collective-permute-start | bytes 196616 | tf_op jit(solution)/shard_map/ppermute | solution.py:24
  34.6 0.0 copy-done.3
  34.6 0.1 reshape.30
  34.6 0.8 %collective-permute-done.13.refs_7_.refs_11_ = bf16[128,256]{1,0:T(8,128)(2,1)S(1)} collective-permute-done((bf16[128,256]{1,0:T(8,128)(2,1)S(1)}, bf16[128,256]{1,0:T(8,128)(2,1)S(1)}, u32[]{:S(2)}, u32[]{:S(2)}) %collective-permute-start.13) | collective-permute-done | bytes 65568 | tf_op jit(solution)/shard_map/ppermute | solution.py:24
  35.5 0.0 collective-permute-done.11.refs_6_.refs_10_
  35.5 0.0 collective-permute-done.10.refs_5_.refs_9_
  35.5 0.0 collective-permute-done.9.refs_4_.refs_8_
  35.5 0.0 copy-done
  35.5 2.1 %shard_map.74 = (bf16[64,512]{1,0:T(8,128)(2,1)S(1)}, bf16[64,512]{1,0:T(8,128)(2,1)S(1)}, bf16[64,128]{1,0:T(8,128)(2,1)S(1)}, bf16[64,128]{1,0:T(8,128)(2,1)S(1)}) custom-call(bf16[256,4096]{1,0:T(8,128)(2,1)S(1)} %reshape.25.x_ref, s32[1,1024]{1,0:T(1,128)S(1)} %bitcast.28, bf16[256,256]{1,0:T(8,128)(2,1)S(1)} %add_convert_fusion.refs_0_.refs_4_, ...), custom_call_target="tpu_custom_call" | custom-call | flops 536870912 | tf_op jit(solution)/shard_map/pallas_call | solution.py:247
  37.5 0.4 collective-permute-start.16
  38.0 3.5 %collective-permute-start.17 = (bf16[64,128]{1,0:T(8,128)(2,1)S(1)}, bf16[64,128]{1,0:T(8,128)(2,1)S(1)}, u32[]{:S(2)}, u32[]{:S(2)}) collective-permute-start(bf16[64,128]{1,0:T(8,128)(2,1)S(1)} %get-tuple-element.25), channel_id=1, source_target_pairs={{0,15},{1,0},{2,1},{3,2},{4,3},{5,4},{6,5},{7,6},{8,7},{9,8},{10,9... | collective-permute-start | bytes 49160 | tf_op jit(solution)/shard_map/ppermute | solution.py:210
  41.5 1.1 %collective-permute-start.14 = (bf16[64,512]{1,0:T(8,128)(2,1)S(1)}, bf16[64,512]{1,0:T(8,128)(2,1)S(1)}, u32[]{:S(2)}, u32[]{:S(2)}) collective-permute-start(bf16[64,512]{1,0:T(8,128)(2,1)S(1)} %get-tuple-element.22), channel_id=1, source_target_pairs={{0,16},{16,32},{32,48},{48,64},{64,80},{80,96},{96,112},{112,0},{1... | collective-permute-start | bytes 196616 | tf_op jit(solution)/shard_map/ppermute | solution.py:210
  42.5 0.0 copy-start.1
  42.5 4.6 %collective-permute-start.15 = (bf16[64,512]{1,0:T(8,128)(2,1)S(1)}, bf16[64,512]{1,0:T(8,128)(2,1)S(1)}, u32[]{:S(2)}, u32[]{:S(2)}) collective-permute-start(bf16[64,512]{1,0:T(8,128)(2,1)S(1)} %get-tuple-element.23), channel_id=1, source_target_pairs={{0,112},{16,0},{32,16},{48,32},{64,48},{80,64},{96,80},{112,96},{1... | collective-permute-start | bytes 196616 | tf_op jit(solution)/shard_map/ppermute | solution.py:210
  47.1 5.8 %shard_map.73.x_ref = bf16[256,4096]{1,0:T(8,128)(2,1)S(1)} custom-call(bf16[256,4096]{1,0:T(8,128)(2,1)S(1)} %reshape.25.x_ref, s32[1,1024]{1,0:T(1,128)S(1)} %bitcast.29, bf16[256,256]{1,0:T(8,128)(2,1)S(1)} %add_convert_fusion.refs_0_.refs_4_, bf16[256,256]{1,0:T(8,128)(2,1)S(1)} %collective-permute-done.6.refs_1_.refs_5_, ...), custom_call_target="tpu_custom_call" | custom-call | flops 4294967296 | tf_op jit(solution)/shard_map/pallas_call | solution.py:256
  52.9 0.0 collective-permute-done.16.refs_2_
  52.9 0.0 collective-permute-done.17.refs_3_
  52.9 0.0 collective-permute-done.14.refs_0_
  52.9 0.0 collective-permute-done.15.refs_1_
  52.9 0.2 broadcast_in_dim.2.profile_ref
  53.1 0.0 copy-done.1
  53.1 7.2 %shard_map.75 = (bf16[256,4096]{1,0:T(8,128)(2,1)S(1)}, bf16[64,512]{1,0:T(8,128)(2,1)S(1)}, bf16[64,512]{1,0:T(8,128)(2,1)S(1)}, bf16[64,128]{1,0:T(8,128)(2,1)S(1)}, bf16[64,128]{1,0:T(8,128)(2,1)S(1)}) custom-call(s32[4]{0:T(128)S(1)} %copy-done.1, bf16[256,4096]{1,0:T(8,128)(2,1)S(1)} %shard_map.73.x_ref, s32[1,1024]{1,0:T(1,128)S(1)} %bitcast.30, ...), custom_call_target="tpu_custom_call" | custom-call | flops 4294967296 | tf_op jit(solution)/shard_map/pallas_call | solution.py:265
  60.3 0.1 collective-permute-start.18
  60.4 5.6 %collective-permute-start.19 = (bf16[64,512]{1,0:T(8,128)(2,1)S(1)}, bf16[64,512]{1,0:T(8,128)(2,1)S(1)}, u32[]{:S(2)}, u32[]{:S(2)}) collective-permute-start(bf16[64,512]{1,0:T(8,128)(2,1)S(1)} %get-tuple-element.28), channel_id=1, source_target_pairs={{0,112},{16,0},{32,16},{48,32},{64,48},{80,64},{96,80},{112,96},{1... | collective-permute-start | bytes 196616 | tf_op jit(solution)/shard_map/ppermute | solution.py:210
  66.0 0.0 collective-permute-start.20
  66.1 3.9 %collective-permute-start.21 = (bf16[64,128]{1,0:T(8,128)(2,1)S(1)}, bf16[64,128]{1,0:T(8,128)(2,1)S(1)}, u32[]{:S(2)}, u32[]{:S(2)}) collective-permute-start(bf16[64,128]{1,0:T(8,128)(2,1)S(1)} %get-tuple-element.30), channel_id=1, source_target_pairs={{0,15},{1,0},{2,1},{3,2},{4,3},{5,4},{6,5},{7,6},{8,7},{9,8},{10,9... | collective-permute-start | bytes 49160 | tf_op jit(solution)/shard_map/ppermute | solution.py:210
  69.9 1.4 %collective-permute-done.20.refs_2_ = bf16[64,128]{1,0:T(8,128)(2,1)S(1)} collective-permute-done((bf16[64,128]{1,0:T(8,128)(2,1)S(1)}, bf16[64,128]{1,0:T(8,128)(2,1)S(1)}, u32[]{:S(2)}, u32[]{:S(2)}) %collective-permute-start.20) | collective-permute-done | bytes 16416 | tf_op jit(solution)/shard_map/ppermute | solution.py:210
  71.3 0.0 collective-permute-done.21.refs_3_
  71.3 0.0 collective-permute-done.18.refs_0_
  71.4 0.0 collective-permute-done.19.refs_1_
  71.4 3.5 %shard_map.76 = bf16[256,4,8,128]{3,2,1,0:T(8,128)(2,1)} custom-call(s32[4]{0:T(128)S(1)} %copy-done.1, bf16[256,4096]{1,0:T(8,128)(2,1)S(1)} %get-tuple-element.26.x_ref, bf16[4,256,128]{2,1,0:T(8,128)(2,1)S(1)} %broadcast_in_dim.2.profile_ref, bf16[64,512]{1,0:T(8,128)(2,1)S(1)} %collective-permute-done.18.refs_0_, ...), custom_call_target="tpu_custom_call" | custom-call | tf_op jit(solution)/shard_map/pallas_call | solution.py:276
  (8 shorter events, 0.1 us)
Async XLA Ops:
  1.5 10.3 %collective-permute-start.4 = (f32[32,256]{1,0:T(8,128)S(1)}, f32[32,256]{1,0:T(8,128)S(1)}, u32[]{:S(2)}, u32[]{:S(2)}) collective-permute-start(f32[32,256]{1,0:T(8,128)S(1)} %pad_maximum_fusion.1), channel_id=1, source_target_pairs={{0,4},{1,5},{2,6},{3,7},{4,0},{5,1},{6,2},{7,3},{8,12},{9,13},{10,... | collective-permute-start | bytes 98312 | tf_op jit(solution)/shard_map/ppermute | solution.py:24
  5.5 3.6 %collective-permute-start = (f32[32,256]{1,0:T(8,128)S(1)}, f32[32,256]{1,0:T(8,128)S(1)}, u32[]{:S(2)}, u32[]{:S(2)}) collective-permute-start(f32[32,256]{1,0:T(8,128)S(1)} %pad_maximum_fusion.1), channel_id=1, source_target_pairs={{0,1},{1,0},{2,3},{3,2},{4,5},{5,4},{6,7},{7,6},{8,9},{9,8},{10,11... | collective-permute-start | bytes 98312 | tf_op jit(solution)/shard_map/ppermute | solution.py:24
  6.2 2.9 %copy-start.2 = (f32[1,16,256]{2,1,0:T(8,128)S(1)}, f32[1,16,256]{2,1,0:T(8,128)}, u32[]{:S(2)}) copy-start(f32[1,16,256]{2,1,0:T(8,128)} %param.13) | copy-start | bytes 49156
  9.0 25.5 %copy-start.3 = (bf16[4,64,4]{1,2,0:T(4,128)(2,1)S(1)}, bf16[4,64,4]{1,2,0:T(4,128)(2,1)}, u32[]{:S(2)}) copy-start(bf16[4,64,4]{1,2,0:T(4,128)(2,1)} %param.10) | copy-start | bytes 6148
  9.1 26.4 %copy-start = (s32[8,128]{1,0:T(8,128)S(1)}, s32[8,128]{1,0:T(8,128)}, u32[]{:S(2)}) copy-start(s32[8,128]{1,0:T(8,128)} %param.8) | copy-start | bytes 12292
  9.1 5.6 %collective-permute-start.3 = (f32[64,256]{1,0:T(8,128)S(1)}, f32[64,256]{1,0:T(8,128)S(1)}, u32[]{:S(2)}, u32[]{:S(2)}) collective-permute-start(f32[64,256]{1,0:T(8,128)S(1)} %pad_maximum_fusion), channel_id=1, source_target_pairs={{0,6},{1,13},{2,4},{3,15},{4,2},{5,9},{6,0},{7,11},{8,14},{9,5},{1... | collective-permute-start | bytes 196616 | tf_op jit(solution)/shard_map/ppermute | solution.py:24
  9.9 4.8 %collective-permute-start.2 = (f32[64,256]{1,0:T(8,128)S(1)}, f32[64,256]{1,0:T(8,128)S(1)}, u32[]{:S(2)}, u32[]{:S(2)}) collective-permute-start(f32[64,256]{1,0:T(8,128)S(1)} %pad_maximum_fusion), channel_id=1, source_target_pairs={{0,2},{1,15},{2,0},{3,13},{4,6},{5,11},{6,4},{7,9},{8,10},{9,7},{1... | collective-permute-start | bytes 196616 | tf_op jit(solution)/shard_map/ppermute | solution.py:24
  10.3 4.4 %collective-permute-start.1 = (f32[64,256]{1,0:T(8,128)S(1)}, f32[64,256]{1,0:T(8,128)S(1)}, u32[]{:S(2)}, u32[]{:S(2)}) collective-permute-start(f32[64,256]{1,0:T(8,128)S(1)} %pad_maximum_fusion), channel_id=1, source_target_pairs={{0,8},{1,11},{2,10},{3,9},{4,12},{5,15},{6,14},{7,13},{8,0},{9,3},... | collective-permute-start | bytes 196616 | tf_op jit(solution)/shard_map/ppermute | solution.py:24
  15.1 4.3 %collective-permute-start.5 = (f32[256,256]{1,0:T(8,128)S(1)}, f32[256,256]{1,0:T(8,128)S(1)}, u32[]{:S(2)}, u32[]{:S(2)}) collective-permute-start(f32[256,256]{1,0:T(8,128)S(1)} %convolution_bitcast_fusion), channel_id=1, source_target_pairs={{0,1},{1,0},{2,3},{3,2},{4,5},{5,4},{6,7},{7,6},{8,9},{9,8},{10,11... | collective-permute-start | bytes 786440 | tf_op jit(solution)/shard_map/ppermute | solution.py:24
  19.5 7.8 %collective-permute-start.8 = (bf16[256,256]{1,0:T(8,128)(2,1)S(1)}, bf16[256,256]{1,0:T(8,128)(2,1)S(1)}, u32[]{:S(2)}, u32[]{:S(2)}) collective-permute-start(bf16[256,256]{1,0:T(8,128)(2,1)S(1)} %add_convert_fusion.refs_0_.refs_4_), channel_id=1, source_target_pairs={{0,96},{1,81},{2,98},{3,83},{4,100},{5,85},{6,102},{7,87},{8,104},... | collective-permute-start | bytes 393224 | tf_op jit(solution)/shard_map/ppermute | solution.py:24
  22.6 9.0 %collective-permute-start.7 = (bf16[256,256]{1,0:T(8,128)(2,1)S(1)}, bf16[256,256]{1,0:T(8,128)(2,1)S(1)}, u32[]{:S(2)}, u32[]{:S(2)}) collective-permute-start(bf16[256,256]{1,0:T(8,128)(2,1)S(1)} %add_convert_fusion.refs_0_.refs_4_), channel_id=1, source_target_pairs={{0,32},{1,113},{2,34},{3,115},{4,36},{5,117},{6,38},{7,119},{8,40}... | collective-permute-start | bytes 393224 | tf_op jit(solution)/shard_map/ppermute | solution.py:24
  22.7 10.0 %collective-permute-start.6 = (bf16[256,256]{1,0:T(8,128)(2,1)S(1)}, bf16[256,256]{1,0:T(8,128)(2,1)S(1)}, u32[]{:S(2)}, u32[]{:S(2)}) collective-permute-start(bf16[256,256]{1,0:T(8,128)(2,1)S(1)} %add_convert_fusion.refs_0_.refs_4_), channel_id=1, source_target_pairs={{0,16},{1,49},{2,18},{3,51},{4,20},{5,53},{6,22},{7,55},{8,24},{9,... | collective-permute-start | bytes 393224 | tf_op jit(solution)/shard_map/ppermute | solution.py:24
  25.7 7.0 %collective-permute-start.12 = (bf16[128,256]{1,0:T(8,128)(2,1)S(1)}, bf16[128,256]{1,0:T(8,128)(2,1)S(1)}, u32[]{:S(2)}, u32[]{:S(2)}) collective-permute-start(bf16[128,256]{1,0:T(8,128)(2,1)S(1)} %constant_dynamic-slice_fusion), channel_id=1, source_target_pairs={{0,64},{1,65},{2,66},{3,67},{4,68},{5,69},{6,70},{7,71},{8,72},{9,... | collective-permute-start | bytes 196616 | tf_op jit(solution)/shard_map/ppermute | solution.py:24
  27.3 8.2 %collective-permute-start.11 = (bf16[256,256]{1,0:T(8,128)(2,1)S(1)}, bf16[256,256]{1,0:T(8,128)(2,1)S(1)}, u32[]{:S(2)}, u32[]{:S(2)}) collective-permute-start(bf16[256,256]{1,0:T(8,128)(2,1)S(1)} %collective-permute-done.8.refs_3_.refs_7_), channel_id=1, source_target_pairs={{0,1},{1,0},{2,3},{3,2},{4,5},{5,4},{6,7},{7,6},{8,9},{9,8},{10,11... | collective-permute-start | bytes 393224 | tf_op jit(solution)/shard_map/ppermute | solution.py:24
  31.6 3.9 %collective-permute-start.10 = (bf16[256,256]{1,0:T(8,128)(2,1)S(1)}, bf16[256,256]{1,0:T(8,128)(2,1)S(1)}, u32[]{:S(2)}, u32[]{:S(2)}) collective-permute-start(bf16[256,256]{1,0:T(8,128)(2,1)S(1)} %collective-permute-done.7.refs_2_.refs_6_), channel_id=1, source_target_pairs={{0,1},{1,0},{2,3},{3,2},{4,5},{5,4},{6,7},{7,6},{8,9},{9,8},{10,11... | collective-permute-start | bytes 393224 | tf_op jit(solution)/shard_map/ppermute | solution.py:24
  32.7 2.7 %collective-permute-start.9 = (bf16[256,256]{1,0:T(8,128)(2,1)S(1)}, bf16[256,256]{1,0:T(8,128)(2,1)S(1)}, u32[]{:S(2)}, u32[]{:S(2)}) collective-permute-start(bf16[256,256]{1,0:T(8,128)(2,1)S(1)} %collective-permute-done.6.refs_1_.refs_5_), channel_id=1, source_target_pairs={{0,1},{1,0},{2,3},{3,2},{4,5},{5,4},{6,7},{7,6},{8,9},{9,8},{10,11... | collective-permute-start | bytes 393224 | tf_op jit(solution)/shard_map/ppermute | solution.py:24
  32.7 2.7 %collective-permute-start.13 = (bf16[128,256]{1,0:T(8,128)(2,1)S(1)}, bf16[128,256]{1,0:T(8,128)(2,1)S(1)}, u32[]{:S(2)}, u32[]{:S(2)}) collective-permute-start(bf16[128,256]{1,0:T(8,128)(2,1)S(1)} %collective-permute-done.12.refs_8_.refs_12_), channel_id=1, source_target_pairs={{0,1},{1,0},{2,3},{3,2},{4,5},{5,4},{6,7},{7,6},{8,9},{9,8},{10,11... | collective-permute-start | bytes 196616 | tf_op jit(solution)/shard_map/ppermute | solution.py:24
  37.5 15.3 %collective-permute-start.16 = (bf16[64,128]{1,0:T(8,128)(2,1)S(1)}, bf16[64,128]{1,0:T(8,128)(2,1)S(1)}, u32[]{:S(2)}, u32[]{:S(2)}) collective-permute-start(bf16[64,128]{1,0:T(8,128)(2,1)S(1)} %get-tuple-element.24), channel_id=1, source_target_pairs={{0,1},{1,2},{2,3},{3,4},{4,5},{5,6},{6,7},{7,8},{8,9},{9,10},{10,1... | collective-permute-start | bytes 49160 | tf_op jit(solution)/shard_map/ppermute | solution.py:210
  38.0 14.9 %collective-permute-start.17 = (bf16[64,128]{1,0:T(8,128)(2,1)S(1)}, bf16[64,128]{1,0:T(8,128)(2,1)S(1)}, u32[]{:S(2)}, u32[]{:S(2)}) collective-permute-start(bf16[64,128]{1,0:T(8,128)(2,1)S(1)} %get-tuple-element.25), channel_id=1, source_target_pairs={{0,15},{1,0},{2,1},{3,2},{4,3},{5,4},{6,5},{7,6},{8,7},{9,8},{10,9... | collective-permute-start | bytes 49160 | tf_op jit(solution)/shard_map/ppermute | solution.py:210
  41.5 11.4 %collective-permute-start.14 = (bf16[64,512]{1,0:T(8,128)(2,1)S(1)}, bf16[64,512]{1,0:T(8,128)(2,1)S(1)}, u32[]{:S(2)}, u32[]{:S(2)}) collective-permute-start(bf16[64,512]{1,0:T(8,128)(2,1)S(1)} %get-tuple-element.22), channel_id=1, source_target_pairs={{0,16},{16,32},{32,48},{48,64},{64,80},{80,96},{96,112},{112,0},{1... | collective-permute-start | bytes 196616 | tf_op jit(solution)/shard_map/ppermute | solution.py:210
  42.5 10.6 %copy-start.1 = (s32[4]{0:T(128)S(1)}, s32[4]{0:T(128)}, u32[]{:S(2)}) copy-start(s32[4]{0:T(128)} %port_ref.3) | copy-start | bytes 52
  42.5 10.4 %collective-permute-start.15 = (bf16[64,512]{1,0:T(8,128)(2,1)S(1)}, bf16[64,512]{1,0:T(8,128)(2,1)S(1)}, u32[]{:S(2)}, u32[]{:S(2)}) collective-permute-start(bf16[64,512]{1,0:T(8,128)(2,1)S(1)} %get-tuple-element.23), channel_id=1, source_target_pairs={{0,112},{16,0},{32,16},{48,32},{64,48},{80,64},{96,80},{112,96},{1... | collective-permute-start | bytes 196616 | tf_op jit(solution)/shard_map/ppermute | solution.py:210
  60.3 11.0 %collective-permute-start.18 = (bf16[64,512]{1,0:T(8,128)(2,1)S(1)}, bf16[64,512]{1,0:T(8,128)(2,1)S(1)}, u32[]{:S(2)}, u32[]{:S(2)}) collective-permute-start(bf16[64,512]{1,0:T(8,128)(2,1)S(1)} %get-tuple-element.27), channel_id=1, source_target_pairs={{0,16},{16,32},{32,48},{48,64},{64,80},{80,96},{96,112},{112,0},{1... | collective-permute-start | bytes 196616 | tf_op jit(solution)/shard_map/ppermute | solution.py:210
  60.4 10.9 %collective-permute-start.19 = (bf16[64,512]{1,0:T(8,128)(2,1)S(1)}, bf16[64,512]{1,0:T(8,128)(2,1)S(1)}, u32[]{:S(2)}, u32[]{:S(2)}) collective-permute-start(bf16[64,512]{1,0:T(8,128)(2,1)S(1)} %get-tuple-element.28), channel_id=1, source_target_pairs={{0,112},{16,0},{32,16},{48,32},{64,48},{80,64},{96,80},{112,96},{1... | collective-permute-start | bytes 196616 | tf_op jit(solution)/shard_map/ppermute | solution.py:210
  66.0 5.3 %collective-permute-start.20 = (bf16[64,128]{1,0:T(8,128)(2,1)S(1)}, bf16[64,128]{1,0:T(8,128)(2,1)S(1)}, u32[]{:S(2)}, u32[]{:S(2)}) collective-permute-start(bf16[64,128]{1,0:T(8,128)(2,1)S(1)} %get-tuple-element.29), channel_id=1, source_target_pairs={{0,1},{1,2},{2,3},{3,4},{4,5},{5,6},{6,7},{7,8},{8,9},{9,10},{10,1... | collective-permute-start | bytes 49160 | tf_op jit(solution)/shard_map/ppermute | solution.py:210
  66.1 5.3 %collective-permute-start.21 = (bf16[64,128]{1,0:T(8,128)(2,1)S(1)}, bf16[64,128]{1,0:T(8,128)(2,1)S(1)}, u32[]{:S(2)}, u32[]{:S(2)}) collective-permute-start(bf16[64,128]{1,0:T(8,128)(2,1)S(1)} %get-tuple-element.30), channel_id=1, source_target_pairs={{0,15},{1,0},{2,1},{3,2},{4,3},{5,4},{6,5},{7,6},{8,7},{9,8},{10,9... | collective-permute-start | bytes 49160 | tf_op jit(solution)/shard_map/ppermute | solution.py:210

commit v5 on v4

--- a/solution.py
+++ b/solution.py
@@ -10,6 +10,7 @@
 BF = jnp.bfloat16
 F32 = jnp.float32
 LANES = 128
+PARAMS = pltpu.CompilerParams(vmem_limit_bytes=20 * 2**20)
 
 
 def swap(value, axis, first, second=None):
@@ -24,32 +25,71 @@
     return lax.ppermute(value, ("row", "col"), pairs)
 
 
-def own_type_map(mode_shapes, mode_values, mode_weights, x):
-    scaled = (mode_shapes * mode_values[:, None, :])[0].T
-    own = jnp.concatenate([scaled, mode_weights[0]], axis=0)
+def pack_kernel(shapes_ref, values_ref, weights_ref, out_ref):
+    modes = shapes_ref.shape[0]
+    row = lax.broadcasted_iota(jnp.int32, (modes, modes), 0)
+    col = lax.broadcasted_iota(jnp.int32, (modes, modes), 1)
+    values = jnp.broadcast_to(values_ref[...], (modes, modes))
+    column = jnp.sum(jnp.where(row == col, values, 0.0), axis=1, keepdims=True)
+    out_ref[0:modes] = shapes_ref[...] * column
+    out_ref[modes:] = weights_ref[...]
+
+
+def partial_kernel(modes, *refs):
+    left, right = [], []
+    for ref in refs[:-1]:
+        for start in range(0, ref.shape[0], 2 * modes):
+            left.append(ref[start : start + modes])
+            right.append(ref[start + modes : start + 2 * modes])
+    refs[-1][...] = lax.dot_general(
+        jnp.concatenate(left, axis=0),
+        jnp.concatenate(right, axis=0),
+        (((0,), (0,)), ((), ())),
+        precision=lax.Precision.HIGHEST,
+        preferred_element_type=F32,
+    )
+
+
+WHOLE = pl.BlockSpec(memory_space=pltpu.VMEM)
+
+
+def whole_call(kernel, shapes, *operands, flops=0):
+    return pl.pallas_call(
+        kernel,
+        in_specs=[WHOLE] * len(operands),
+        out_specs=[WHOLE] * len(shapes),
+        out_shape=shapes,
+        compiler_params=PARAMS,
+        cost_estimate=pl.CostEstimate(flops=flops, bytes_accessed=0, transcendentals=0),
+    )(*operands)
+
+
+def own_type_map(mode_shapes, mode_values, mode_weights, traces):
+    modes, order = mode_weights.shape[1:]
+    (own,) = whole_call(
+        pack_kernel,
+        [jax.ShapeDtypeStruct((2 * modes, order), F32)],
+        mode_shapes[0].T,
+        mode_values,
+        mode_weights[0],
+    )
     far = swap(own, "col", 4)
     pair = jnp.concatenate([own, swap(own, "col", 1)], axis=0)
+    pair, traces = lax.optimization_barrier((pair, traces))
     got = [swap(pair, "col", 8, 10), swap(pair, "col", 2, 14), swap(pair, "col", 6, 12)]
+    x = traces.reshape(order, -1)
     *got, x = lax.optimization_barrier((*got, x))
-    every = jnp.concatenate([own, far] + got, axis=0).reshape((-1, 2) + scaled.shape)
-    left = every[:, 0].reshape(-1, scaled.shape[1])
-    right = every[:, 1].reshape(-1, scaled.shape[1])
-    partial = lax.dot_general(
-        left, right, (((0,), (0,)), ((), ())), precision=lax.Precision.HIGHEST
-    )
-    partial = lax.optimization_barrier(partial)
+    (partial,) = whole_call(
+        functools.partial(partial_kernel, modes),
+        [jax.ShapeDtypeStruct((order, order), F32)],
+        own,
+        far,
+        *got,
+    )
     return (partial + swap(partial, "col", 1)).astype(BF), x
 
 
 MAP_STEPS = ((0, 0), (1, 3), (2, 7), (6, 5), (3, 1), (7, 2), (5, 6), (4, 4))
-
-
-def all_maps(own_map):
-    core = lax.rem(lax.axis_index("col"), 2)
-    half = own_map.shape[0] // 2
-    mine = swap(lax.dynamic_slice_in_dim(own_map, core * half, half), "row", 4)
-    got = [swap(own_map, "row", first, second) for first, second in MAP_STEPS[1:4]]
-    return [own_map] + got + [swap(value, "col", 1) for value in got + [mine]] + [mine]
 
 
 def patch(block, rows, width, east_lane, port_ref, profile_ref, halo_refs):
@@ -90,23 +130,33 @@
         block[:, cols] = jnp.where(here, added, current).astype(BF)
 
 
-def products(x, types, map_refs, first, last):
+def map_rows(map_refs, first, last):
+    if len(map_refs) == 1:
+        return map_refs[0][first:last, :]
+    core = lax.rem(lax.axis_index("col"), 2)
+    swapped, own = map_refs[0][...], map_refs[1][...]
+    low, high = jnp.where(core == 0, own, swapped), jnp.where(core == 0, swapped, own)
+    return jnp.concatenate([low, high], axis=0)[first:last]
+
+
+def products(x, types, maps, first, last, total=None):
     mine = lax.axis_index("row")
+    core = lax.rem(lax.axis_index("col"), 2)
     types = jnp.broadcast_to(types, x.shape)
-    total = None
-    core = lax.rem(lax.axis_index("col"), 2)
-    for number, (even, odd) in enumerate(MAP_STEPS):
+    for (even, odd), map_refs in maps:
         kind = (mine ^ jnp.where(core == 0, even, odd)).astype(F32).astype(BF)
         masked = jnp.where(types == kind, x, jnp.zeros((), BF))
-        if number + 1 < len(MAP_STEPS):
-            part = map_refs[number][first:last, :]
-        else:
-            swapped, own = map_refs[number][...], map_refs[number + 1][...]
-            low, high = jnp.where(core == 0, own, swapped), jnp.where(core == 0, swapped, own)
-            part = jnp.concatenate([low, high], axis=0)[first:last]
+        part = map_rows(map_refs, first, last)
         product = jnp.dot(part, masked, preferred_element_type=F32)
         total = product if total is None else total + product
     return total
+
+
+def with_steps(map_refs, first, last):
+    refs = [(ref,) for ref in map_refs]
+    if last == len(MAP_STEPS):
+        refs[-2:] = [refs[-2] + refs[-1]]
+    return list(zip(MAP_STEPS[first:last], refs, strict=True))
 
 
 def shifted(total, next_ref, rows):
@@ -127,20 +177,15 @@
     return north, south
 
 
-def rim_kernel(rows, ports, x_ref, types_ref, *refs):
-    map_refs = refs[:-4]
-    north_out, south_out, west_out, east_out = refs[-4:]
-    order = x_ref.shape[0]
-    quarter = order // 4
-    tile = rows * LANES
-    types = types_ref[...].astype(F32)
-    starts = [port * tile for port in range(ports)]
-    for edge, out, offset in ((0, north_out, 0), (1, south_out, tile - LANES)):
-        cells = jnp.concatenate(
-            [x_ref[:, start + offset : start + offset + LANES] for start in starts], axis=1
-        )
-        kinds = jnp.concatenate([types[:, offset : offset + LANES]] * ports, axis=1).astype(BF)
-        out[...] = products(cells, kinds, map_refs, edge * quarter, (edge + 1) * quarter).astype(BF)
+def rim_columns(x_ref, types, ports, offset):
+    tile = types.shape[1]
+    starts = [port * tile + offset for port in range(ports)]
+    cells = jnp.concatenate([x_ref[:, start : start + LANES] for start in starts], axis=1)
+    return cells, jnp.concatenate([types[:, offset : offset + LANES]] * ports, axis=1).astype(BF)
+
+
+def side_columns(x_ref, types, ports):
+    order, tile = x_ref.shape[0], types.shape[1]
     wide = 2 * LANES
     spread = jnp.broadcast_to(types, (16, tile)).astype(BF)
     place = lax.broadcasted_iota(jnp.int32, (wide, LANES), 0)
@@ -155,17 +200,64 @@
         )
         part = jnp.dot(both, pick, preferred_element_type=F32)
         picked = part if picked is None else picked + part
-    cells = picked[0:order].astype(BF)
-    kinds = picked[order : order + 1].astype(BF)
-    sides = products(cells, kinds, map_refs, 2 * quarter, 4 * quarter).astype(BF)
-    west_out[...] = sides[0:quarter]
-    east_out[...] = sides[quarter : 2 * quarter]
-
-
-def first_kernel(rows, x_ref, types_ref, *refs):
-    x = x_ref[...]
+    return picked[0:order].astype(BF), picked[order:].astype(BF)
+
+
+def rims(x_ref, types, ports, sides, kinds, maps, so_far):
+    order, tile = x_ref.shape[0], types.shape[1]
+    quarter = order // 4
+    before = [None if ref is None else ref[...].astype(F32) for ref in so_far]
+    cells, cell_kinds = rim_columns(x_ref, types, ports, 0)
+    north = products(cells, cell_kinds, maps, 0, quarter, before[0])
+    cells, cell_kinds = rim_columns(x_ref, types, ports, tile - LANES)
+    south = products(cells, cell_kinds, maps, quarter, 2 * quarter, before[1])
+    side = products(sides, kinds, maps, 2 * quarter, order, before[2])
+    return north.astype(BF), south.astype(BF), side.astype(BF)
+
+
+def early_kernel(ports, first, last, x_ref, types_ref, *refs):
+    maps = with_steps(refs[: last - first], first, last)
+    refs = refs[last - first :]
+    types = types_ref[...].astype(F32)
+    tile = types.shape[1]
+    if first == 0:
+        done_ref, so_far = None, [None] * 3
+        sides, kinds = side_columns(x_ref, types, ports)
+        refs[4][...] = sides
+        refs[5][...] = kinds
+    else:
+        done_ref, so_far = refs[0], refs[1:4]
+        sides, kinds = refs[4][...], refs[5][...]
+        refs = refs[6:]
+    outs = rims(x_ref, types, ports, sides, kinds[0:1], maps, so_far)
+    for ref, value in zip(refs[1:4], outs):
+        ref[...] = value
+    for port in range(ports):
+        cols = slice(port * tile, (port + 1) * tile)
+        before = None if done_ref is None else done_ref[:, cols].astype(F32)
+        total = products(x_ref[:, cols], types.astype(BF), maps, 0, x_ref.shape[0], before)
+        refs[0][:, cols] = total.astype(BF)
+
+
+def rim_kernel(ports, first, x_ref, types_ref, *refs):
+    maps = with_steps(refs[:-9], first, len(MAP_STEPS))
+    so_far, (sides, kinds) = refs[-9:-6], refs[-6:-4]
+    outs = rims(
+        x_ref, types_ref[...].astype(F32), ports, sides[...], kinds[0:1, :], maps, so_far
+    )
+    quarter = x_ref.shape[0] // 4
+    refs[-4][...] = outs[0]
+    refs[-3][...] = outs[1]
+    refs[-2][...] = outs[2][0:quarter]
+    refs[-1][...] = outs[2][quarter:]
+
+
+def first_kernel(rows, first, x_ref, types_ref, done_ref, *refs):
+    maps = with_steps(refs[:-1], first, len(MAP_STEPS))
     types = types_ref[...].astype(F32).astype(BF)
-    shifted(products(x, types, refs[:-1], 0, x.shape[0]), refs[-1], rows)
+    before = done_ref[...].astype(F32)
+    total = products(x_ref[...], types, maps, 0, x_ref.shape[0], before)
+    shifted(total, refs[-1], rows)
 
 
 def second_kernel(rows, width, port_ref, x_ref, types_ref, profile_ref, *refs):
@@ -176,7 +268,8 @@
     order = block.shape[0]
     quarter = order // 4
     types = types_ref[...].astype(F32).astype(BF)
-    total = products(block[...], types, map_refs, 0, order)
+    maps = with_steps(map_refs, 0, len(MAP_STEPS))
+    total = products(block[...], types, maps, 0, order)
     north, south = shifted(total, next_ref, rows)
     north_out[...] = north[:, 0:LANES]
     south_out[...] = south[:, (rows - 1) * LANES :]
@@ -222,16 +315,18 @@
     order = edges * samples
     quarter = samples
     tile = rows * width
-    x = traces.reshape(order, ports * tile)
-    own_map, x = own_type_map(mode_shapes, mode_values, mode_weights, x)
-    maps = all_maps(own_map)
+    own_map, x = own_type_map(mode_shapes, mode_values, mode_weights, traces)
+    core = lax.rem(lax.axis_index("col"), 2)
+    half = lax.dynamic_slice_in_dim(own_map, core * (order // 2), order // 2)
+    fetched = [swap(own_map, "row", *steps) for steps in MAP_STEPS[1:4]]
+    half = swap(half, "row", 4)
+    swapped = [swap(fetched[0], "col", 1)]
     types = cell_type.reshape(1, tile)
     profile = jnp.broadcast_to(
         jnp.transpose(port_profile.reshape(order, ports))[:, :, None], (ports, order, LANES)
     )
     block = pl.BlockSpec((order, tile), lambda i: (0, i))
     types_spec = pl.BlockSpec((1, tile), lambda i: (0, 0))
-    map_specs = [pl.BlockSpec(value.shape, lambda i: (0, 0)) for value in maps]
     long_rim = pl.BlockSpec((quarter, LANES), lambda i: (0, i))
     short_rim = pl.BlockSpec((quarter, LANES), lambda i: (0, 0))
     rims = [long_rim, long_rim, short_rim, short_rim]
@@ -241,27 +336,60 @@
     rim_shapes = [jax.ShapeDtypeStruct((quarter, ports * LANES), BF)] * 2 + [
         jax.ShapeDtypeStruct((quarter, LANES), BF)
     ] * 2
-    params = pltpu.CompilerParams(vmem_limit_bytes=20 * 2**20)
-    whole = pl.BlockSpec(memory_space=pltpu.VMEM)
     work = 2 * order * order * len(MAP_STEPS) * ports * tile
-    sent = pl.pallas_call(
-        functools.partial(rim_kernel, rows, ports),
-        in_specs=[whole] * (2 + len(maps)),
-        out_specs=[whole] * 4,
-        out_shape=rim_shapes,
-        compiler_params=params,
-        cost_estimate=pl.CostEstimate(flops=work // 8, bytes_accessed=0, transcendentals=0),
-    )(x, types, *maps)
+    early = (0, 2, 4)
+    side_shapes = [
+        jax.ShapeDtypeStruct((order, LANES), BF),
+        jax.ShapeDtypeStruct((16, LANES), BF),
+    ]
+    part_shapes = [next_shape] + rim_shapes[:2] + [jax.ShapeDtypeStruct((2 * quarter, LANES), BF)]
+    *parts, sides, kinds = whole_call(
+        functools.partial(early_kernel, ports, early[0], early[1]),
+        part_shapes + side_shapes,
+        x,
+        types,
+        own_map,
+        fetched[0],
+        flops=work // 3,
+    )
+    parts, rest, half = lax.optimization_barrier((parts, fetched[1:], half))
+    swapped += [swap(value, "col", 1) for value in rest + [half]]
+    parts = whole_call(
+        functools.partial(early_kernel, ports, early[1], early[2]),
+        part_shapes,
+        x,
+        types,
+        *rest,
+        *parts,
+        sides,
+        kinds,
+        flops=work // 3,
+    )
+    done, *parts = parts
+    late = swapped + [half]
+    maps = [own_map, fetched[0]] + rest + late
+    map_specs = [pl.BlockSpec(value.shape, lambda i: (0, 0)) for value in maps]
+    sent = whole_call(
+        functools.partial(rim_kernel, ports, early[2]),
+        rim_shapes,
+        x,
+        types,
+        *late,
+        *parts,
+        sides,
+        kinds,
+        flops=work // 8,
+    )
     halos = exchange(sent)
     x = pl.pallas_call(
-        functools.partial(first_kernel, rows),
+        functools.partial(first_kernel, rows, early[2]),
         grid=(ports,),
-        in_specs=[block, types_spec] + map_specs,
+        in_specs=[block, types_spec, block] + map_specs[early[2] :],
         out_specs=block,
         out_shape=next_shape,
-        compiler_params=params,
-        cost_estimate=pl.CostEstimate(flops=work, bytes_accessed=0, transcendentals=0),
-    )(x, types, *maps)
+        compiler_params=PARAMS,
+        cost_estimate=pl.CostEstimate(flops=work // 2, bytes_accessed=0, transcendentals=0),
+    )(x, types, done, *late)
     x, *sent = pl.pallas_call(
         functools.partial(second_kernel, rows, width),
         grid=(ports,),
@@ -269,7 +397,7 @@
         out_specs=[block] + rims,
         out_shape=[next_shape] + rim_shapes,
         scratch_shapes=[pltpu.VMEM((order, tile), BF)],
-        compiler_params=params,
+        compiler_params=PARAMS,
         cost_estimate=pl.CostEstimate(flops=work, bytes_accessed=0, transcendentals=0),
     )(port_cell, x, types, profile, *halos, *maps)
     halos = exchange(sent)
@@ -280,7 +408,7 @@
         out_specs=pl.BlockSpec((order, 1, rows, LANES), lambda i: (0, i, 0, 0)),
         out_shape=jax.ShapeDtypeStruct((order, ports, rows, width), BF),
         scratch_shapes=[pltpu.VMEM((order, tile), BF)],
-        compiler_params=params,
+        compiler_params=PARAMS,
     )(port_cell, x, profile, *halos)
     return out.reshape(traces.shape)
 

time: 75.2 us -> 70.9 us (0.943)
  starting transfers between devices: 44 us -> 35.4 us
  waiting for transfers between devices: 6.32 us -> 9.69 us
  Pallas kernels: 18.5 us -> 20.1 us
  other arithmetic: 1.55 us -> 0.05 us
  local copies, waits for them, and re-layouts: 3.89 us -> 5.22 us
    ppermute x14, starting transfers between devices: 24.9 us -> 16.3 us  [swap(): return lax.ppermute(value, ('row', 'col'), pairs)]
    ppermute x14, waiting for transfers between devices: 4.86 us -> 8.23 us  [swap(): return lax.ppermute(value, ('row', 'col'), pairs)]
    pallas_call x2 -> x6, Pallas kernels: 7.82 us -> 9.37 us  [the longest x5 5.7 us: whole_call(): pl.pallas_call(kernel, in_specs=[WHOLE] * len(operands), out_specs=[WHOLE...]
    unnamed x13, local copies, waits for them, and re-layouts: 0.76 us -> 2.11 us
    unnamed x1 -> x0, other arithmetic: 0.79 us -> none
  transfers between devices with their start and end apart: 22 -> 22, of which waited for: 4 -> 6; matrix products, arithmetic and copies ran while one was open for 5% -> 4% of each run, Pallas kernels for 8% -> 12%
where the time goes in v5:
time: 70.9 us; the launch traced here: 70.6 us
  starting transfers between devices  35.4 us (50%)
  Pallas kernels  20.1 us (28%)
  waiting for transfers between devices  9.69 us (14%)
  local copies, waits for them, and re-layouts  5.22 us (7%)
    ppermute x8, starting transfers between devices, send(): lax.ppermute(value, axis, [(i, (i + step) % count) for i in range(count)])  19.1 us
    ppermute x14, starting transfers between devices, swap(): return lax.ppermute(value, ('row', 'col'), pairs)  16.3 us
    ppermute x14, waiting for transfers between devices, swap(): return lax.ppermute(value, ('row', 'col'), pairs)  8.23 us
    pallas_call x1, Pallas kernels, body(): pl.pallas_call(functools.partial(second_kernel, rows, width), grid=(ports...  7.2 us
    pallas_call x5, Pallas kernels, whole_call(): pl.pallas_call(kernel, in_specs=[WHOLE] * len(operands), out_specs=[WHOLE...  5.7 us
    pallas_call x1, Pallas kernels, body(): pl.pallas_call(functools.partial(first_kernel, rows, early[2]), grid=(por...  3.67 us
    pallas_call x1, Pallas kernels, body(): pl.pallas_call(functools.partial(last_kernel, rows, width), grid=(ports,)...  3.48 us
    reshape x1, local copies, waits for them, and re-layouts, own_type_map(): x = traces.reshape(order, -1)  2.82 us
  transfers between devices with their start and end apart: 22, of which 6 were waited for; matrix products, arithmetic and copies ran while one was open for 4% of the time, Pallas kernels for 12%

profile of v5, /device:TPU:0, one launch (start us, length us, event | category | flops | bytes accessed | tf_op | source)
XLA Modules:
  0.0 70.6 jit_solution(954741525844917591)
XLA Ops:
  0.0 0.0 copy-start
  0.0 0.7 %copy-done = f32[1,256,16]{1,2,0:T(8,128)S(1)} copy-done((f32[1,256,16]{1,2,0:T(8,128)S(1)}, f32[1,256,16]{1,2,0:T(8,128)}, u32[]{:S(2)}) %copy-start) | copy-done | bytes 16408
  0.7 0.0 copy-start.1
  0.7 0.7 %copy-done.1 = f32[1,16,256]{2,1,0:T(8,128)S(1)} copy-done((f32[1,16,256]{2,1,0:T(8,128)S(1)}, f32[1,16,256]{2,1,0:T(8,128)}, u32[]{:S(2)}) %copy-start.1) | copy-done | bytes 16408
  1.4 0.7 copy-done.3
  2.1 0.1 shard_map.73.refs_0_
  2.2 0.0 collective-permute-start
  2.2 1.2 %collective-permute-done = f32[32,256]{1,0:T(8,128)S(1)} collective-permute-done((f32[32,256]{1,0:T(8,128)S(1)}, f32[32,256]{1,0:T(8,128)S(1)}, u32[]{:S(2)}, u32[]{:S(2)}) %collective-permute-start) | collective-permute-done | bytes 32800 | tf_op jit(solution)/shard_map/ppermute | solution.py:25
  3.4 0.0 copy-start.2
  3.4 1.7 %collective-permute-start.1 = (f32[64,256]{1,0:T(8,128)S(1)}, f32[64,256]{1,0:T(8,128)S(1)}, u32[]{:S(2)}, u32[]{:S(2)}) collective-permute-start(f32[64,256]{1,0:T(8,128)S(1)} %pad_maximum_fusion), channel_id=1, source_target_pairs={{0,8},{1,11},{2,10},{3,9},{4,12},{5,15},{6,14},{7,13},{8,0},{9,3},... | collective-permute-start | bytes 196616 | tf_op jit(solution)/shard_map/ppermute | solution.py:25
  5.1 1.9 %collective-permute-start.2 = (f32[64,256]{1,0:T(8,128)S(1)}, f32[64,256]{1,0:T(8,128)S(1)}, u32[]{:S(2)}, u32[]{:S(2)}) collective-permute-start(f32[64,256]{1,0:T(8,128)S(1)} %pad_maximum_fusion), channel_id=1, source_target_pairs={{0,2},{1,15},{2,0},{3,13},{4,6},{5,11},{6,4},{7,9},{8,10},{9,7},{1... | collective-permute-start | bytes 196616 | tf_op jit(solution)/shard_map/ppermute | solution.py:25
  7.0 2.5 %collective-permute-start.3 = (f32[64,256]{1,0:T(8,128)S(1)}, f32[64,256]{1,0:T(8,128)S(1)}, u32[]{:S(2)}, u32[]{:S(2)}) collective-permute-start(f32[64,256]{1,0:T(8,128)S(1)} %pad_maximum_fusion), channel_id=1, source_target_pairs={{0,6},{1,13},{2,4},{3,15},{4,2},{5,9},{6,0},{7,11},{8,14},{9,5},{1... | collective-permute-start | bytes 196616 | tf_op jit(solution)/shard_map/ppermute | solution.py:25
  9.5 1.1 %collective-permute-start.4 = (f32[32,256]{1,0:T(8,128)S(1)}, f32[32,256]{1,0:T(8,128)S(1)}, u32[]{:S(2)}, u32[]{:S(2)}) collective-permute-start(f32[32,256]{1,0:T(8,128)S(1)} %shard_map.73.refs_0_), channel_id=1, source_target_pairs={{0,4},{1,5},{2,6},{3,7},{4,0},{5,1},{6,2},{7,3},{8,12},{9,13},{10,... | collective-permute-start | bytes 98312 | tf_op jit(solution)/shard_map/ppermute | solution.py:25
  10.6 2.8 %reshape.13.x_ref = bf16[256,4096]{1,0:T(8,128)(2,1)S(1)} reshape(bf16[4,64,4,8,128]{4,3,2,1,0:T(8,128)(2,1)} %param.7) | data formatting | bytes 4194304 | tf_op jit(solution)/shard_map/reshape | solution.py:80
  13.4 0.0 collective-permute-done.1.refs_2_
  13.4 0.0 collective-permute-done.2.refs_3_
  13.4 0.0 collective-permute-done.3.refs_4_
  13.4 1.5 %collective-permute-done.4.refs_1_ = f32[32,256]{1,0:T(8,128)S(1)} collective-permute-done((f32[32,256]{1,0:T(8,128)S(1)}, f32[32,256]{1,0:T(8,128)S(1)}, u32[]{:S(2)}, u32[]{:S(2)}) %collective-permute-start.4) | collective-permute-done | bytes 32800 | tf_op jit(solution)/shard_map/ppermute | solution.py:25
  14.9 0.4 shard_map.74
  15.4 0.4 collective-permute-start.5
  15.8 1.2 %collective-permute-done.5 = f32[256,256]{1,0:T(8,128)S(1)} collective-permute-done((f32[256,256]{1,0:T(8,128)S(1)}, f32[256,256]{1,0:T(8,128)S(1)}, u32[]{:S(2)}, u32[]{:S(2)}) %collective-permute-start.5) | collective-permute-done | bytes 262176 | tf_op jit(solution)/shard_map/ppermute | solution.py:25
  17.0 3.1 %collective-permute-start.6 = (bf16[256,256]{1,0:T(8,128)(2,1)S(1)}, bf16[256,256]{1,0:T(8,128)(2,1)S(1)}, u32[]{:S(2)}, u32[]{:S(2)}) collective-permute-start(bf16[256,256]{1,0:T(8,128)(2,1)S(1)} %add_convert_fusion.refs_0_.refs_4_), channel_id=1, source_target_pairs={{0,16},{1,49},{2,18},{3,51},{4,20},{5,53},{6,22},{7,55},{8,24},{9,... | collective-permute-start | bytes 393224 | tf_op jit(solution)/shard_map/ppermute | solution.py:25
  20.1 0.0 copy-done.5
  20.1 0.1 reshape.15
  20.2 1.6 %collective-permute-start.7 = (bf16[256,256]{1,0:T(8,128)(2,1)S(1)}, bf16[256,256]{1,0:T(8,128)(2,1)S(1)}, u32[]{:S(2)}, u32[]{:S(2)}) collective-permute-start(bf16[256,256]{1,0:T(8,128)(2,1)S(1)} %add_convert_fusion.refs_0_.refs_4_), channel_id=1, source_target_pairs={{0,32},{1,113},{2,34},{3,115},{4,36},{5,117},{6,38},{7,119},{8,40}... | collective-permute-start | bytes 393224 | tf_op jit(solution)/shard_map/ppermute | solution.py:25
  21.8 2.2 %collective-permute-start.8 = (bf16[256,256]{1,0:T(8,128)(2,1)S(1)}, bf16[256,256]{1,0:T(8,128)(2,1)S(1)}, u32[]{:S(2)}, u32[]{:S(2)}) collective-permute-start(bf16[256,256]{1,0:T(8,128)(2,1)S(1)} %add_convert_fusion.refs_0_.refs_4_), channel_id=1, source_target_pairs={{0,96},{1,81},{2,98},{3,83},{4,100},{5,85},{6,102},{7,87},{8,104},... | collective-permute-start | bytes 393224 | tf_op jit(solution)/shard_map/ppermute | solution.py:25
  24.0 0.8 %collective-permute-start.9 = (bf16[128,256]{1,0:T(8,128)(2,1)S(1)}, bf16[128,256]{1,0:T(8,128)(2,1)S(1)}, u32[]{:S(2)}, u32[]{:S(2)}) collective-permute-start(bf16[128,256]{1,0:T(8,128)(2,1)S(1)} %constant_dynamic-slice_fusion), channel_id=1, source_target_pairs={{0,64},{1,65},{2,66},{3,67},{4,68},{5,69},{6,70},{7,71},{8,72},{9,... | collective-permute-start | bytes 196616 | tf_op jit(solution)/shard_map/ppermute | solution.py:25
  24.8 0.0 collective-permute-done.6.refs_1_.refs_5_
  24.8 0.0 copy-done.2
  24.8 3.0 %shard_map.75 = (bf16[256,4096]{1,0:T(8,128)(2,1)S(1)}, bf16[64,512]{1,0:T(8,128)(2,1)S(1)}, bf16[64,512]{1,0:T(8,128)(2,1)S(1)}, bf16[128,128]{1,0:T(8,128)(2,1...) custom-call(bf16[256,4096]{1,0:T(8,128)(2,1)S(1)} %reshape.13.x_ref, s32[1,1024]{1,0:T(1,128)S(1)} %bitcast.13, ...), custom_call_target="tpu_custom_call" | custom-call | flops 1431655808 | tf_op jit(solution)/shard_map/pallas_call | solution.py:57
  27.8 3.6 %collective-permute-done.9.refs_4_.refs_12_ = bf16[128,256]{1,0:T(8,128)(2,1)S(1)} collective-permute-done((bf16[128,256]{1,0:T(8,128)(2,1)S(1)}, bf16[128,256]{1,0:T(8,128)(2,1)S(1)}, u32[]{:S(2)}, u32[]{:S(2)}) %collective-permute-start.9) | collective-permute-done | bytes 65568 | tf_op jit(solution)/shard_map/ppermute | solution.py:25
  31.5 0.0 collective-permute-done.7.refs_0_.refs_6_
  31.5 0.7 collective-permute-done.8.refs_1_.refs_7_
  32.2 0.0 collective-permute-start.11
  32.2 0.5 collective-permute-start.12
  32.7 0.0 collective-permute-start.13
  32.7 0.5 collective-permute-start.10
  33.2 1.5 %shard_map.76 = (bf16[256,4096]{1,0:T(8,128)(2,1)S(1)}, bf16[64,512]{1,0:T(8,128)(2,1)S(1)}, bf16[64,512]{1,0:T(8,128)(2,1)S(1)}, bf16[128,128]{1,0:T(8,128)(2,1)S(1)}) custom-call(bf16[256,4096]{1,0:T(8,128)(2,1)S(1)} %reshape.13.x_ref, s32[1,1024]{1,0:T(1,128)S(1)} %bitcast.14, bf16[256,256]{1,0:T(8,128)(2,1)S(1)} %collective-permute-done.7.refs_0_.refs_6_, ...), custom_call_target="tpu_custom_call" | custom-call | flops 1431655808 | tf_op jit(solution)/shard_map/pallas_call | solution.py:57
  34.7 0.0 collective-permute-done.13.refs_3_.refs_11_
  34.7 0.0 collective-permute-done.11.refs_1_.refs_9_
  34.7 0.0 collective-permute-done.12.refs_2_.refs_10_
  34.8 0.0 collective-permute-done.10.refs_0_.refs_8_
  34.8 0.6 shard_map.78
  35.4 1.1 %collective-permute-start.14 = (bf16[64,512]{1,0:T(8,128)(2,1)S(1)}, bf16[64,512]{1,0:T(8,128)(2,1)S(1)}, u32[]{:S(2)}, u32[]{:S(2)}) collective-permute-start(bf16[64,512]{1,0:T(8,128)(2,1)S(1)} %get-tuple-element.60), channel_id=1, source_target_pairs={{0,16},{16,32},{32,48},{48,64},{64,80},{80,96},{96,112},{112,0},{1... | collective-permute-start | bytes 196616 | tf_op jit(solution)/shard_map/ppermute | solution.py:303
  36.5 4.7 %collective-permute-start.15 = (bf16[64,512]{1,0:T(8,128)(2,1)S(1)}, bf16[64,512]{1,0:T(8,128)(2,1)S(1)}, u32[]{:S(2)}, u32[]{:S(2)}) collective-permute-start(bf16[64,512]{1,0:T(8,128)(2,1)S(1)} %get-tuple-element.61), channel_id=1, source_target_pairs={{0,112},{16,0},{32,16},{48,32},{64,48},{80,64},{96,80},{112,96},{1... | collective-permute-start | bytes 196616 | tf_op jit(solution)/shard_map/ppermute | solution.py:303
  41.1 0.0 collective-permute-start.16
  41.1 3.9 %collective-permute-start.17 = (bf16[64,128]{1,0:T(8,128)(2,1)S(1)}, bf16[64,128]{1,0:T(8,128)(2,1)S(1)}, u32[]{:S(2)}, u32[]{:S(2)}) collective-permute-start(bf16[64,128]{1,0:T(8,128)(2,1)S(1)} %get-tuple-element.63), channel_id=1, source_target_pairs={{0,15},{1,0},{2,1},{3,2},{4,3},{5,4},{6,5},{7,6},{8,7},{9,8},{10,9... | collective-permute-start | bytes 49160 | tf_op jit(solution)/shard_map/ppermute | solution.py:303
  45.0 3.7 %shard_map.77.x_ref = bf16[256,4096]{1,0:T(8,128)(2,1)S(1)} custom-call(bf16[256,4096]{1,0:T(8,128)(2,1)S(1)} %reshape.13.x_ref, s32[1,1024]{1,0:T(1,128)S(1)} %bitcast.16, bf16[256,4096]{1,0:T(8,128)(2,1)S(1)} %get-tuple-element.55.done_ref, bf16[256,256]{1,0:T(8,128)(2,1)S(1)} %collective-permute-done.10.refs_0_.refs_8_, ...), custom_call_target="tpu_custom_call" | custom-call | flops 2147483648 | tf_op jit(solution)/shard_map/pallas_call | solution.py:384
  48.6 0.0 collective-permute-done.16.refs_2_
  48.6 0.0 collective-permute-done.17.refs_3_
  48.7 0.0 collective-permute-done.14.refs_0_
  48.7 0.0 collective-permute-done.15.refs_1_
  48.7 0.2 broadcast_in_dim.2.profile_ref
  48.9 0.0 copy-done.4
  48.9 7.2 %shard_map.79 = (bf16[256,4096]{1,0:T(8,128)(2,1)S(1)}, bf16[64,512]{1,0:T(8,128)(2,1)S(1)}, bf16[64,512]{1,0:T(8,128)(2,1)S(1)}, bf16[64,128]{1,0:T(8,128)(2,1)S(1)}, bf16[64,128]{1,0:T(8,128)(2,1)S(1)}) custom-call(s32[4]{0:T(128)S(1)} %copy-done.4, bf16[256,4096]{1,0:T(8,128)(2,1)S(1)} %shard_map.77.x_ref, s32[1,1024]{1,0:T(1,128)S(1)} %bitcast.17, ...), custom_call_target="tpu_custom_call" | custom-call | flops 4294967296 | tf_op jit(solution)/shard_map/pallas_call | solution.py:393
  56.1 0.1 collective-permute-start.18
  56.2 5.6 %collective-permute-start.19 = (bf16[64,512]{1,0:T(8,128)(2,1)S(1)}, bf16[64,512]{1,0:T(8,128)(2,1)S(1)}, u32[]{:S(2)}, u32[]{:S(2)}) collective-permute-start(bf16[64,512]{1,0:T(8,128)(2,1)S(1)} %get-tuple-element.66), channel_id=1, source_target_pairs={{0,112},{16,0},{32,16},{48,32},{64,48},{80,64},{96,80},{112,96},{1... | collective-permute-start | bytes 196616 | tf_op jit(solution)/shard_map/ppermute | solution.py:303
  61.8 0.0 collective-permute-start.20
  61.8 3.9 %collective-permute-start.21 = (bf16[64,128]{1,0:T(8,128)(2,1)S(1)}, bf16[64,128]{1,0:T(8,128)(2,1)S(1)}, u32[]{:S(2)}, u32[]{:S(2)}) collective-permute-start(bf16[64,128]{1,0:T(8,128)(2,1)S(1)} %get-tuple-element.68), channel_id=1, source_target_pairs={{0,15},{1,0},{2,1},{3,2},{4,3},{5,4},{6,5},{7,6},{8,7},{9,8},{10,9... | collective-permute-start | bytes 49160 | tf_op jit(solution)/shard_map/ppermute | solution.py:303
  65.7 1.4 %collective-permute-done.20.refs_2_ = bf16[64,128]{1,0:T(8,128)(2,1)S(1)} collective-permute-done((bf16[64,128]{1,0:T(8,128)(2,1)S(1)}, bf16[64,128]{1,0:T(8,128)(2,1)S(1)}, u32[]{:S(2)}, u32[]{:S(2)}) %collective-permute-start.20) | collective-permute-done | bytes 16416 | tf_op jit(solution)/shard_map/ppermute | solution.py:303
  67.1 0.0 collective-permute-done.21.refs_3_
  67.1 0.0 collective-permute-done.18.refs_0_
  67.1 0.0 collective-permute-done.19.refs_1_
  67.1 3.5 %shard_map.80 = bf16[256,4,8,128]{3,2,1,0:T(8,128)(2,1)} custom-call(s32[4]{0:T(128)S(1)} %copy-done.4, bf16[256,4096]{1,0:T(8,128)(2,1)S(1)} %get-tuple-element.64.x_ref, bf16[4,256,128]{2,1,0:T(8,128)(2,1)S(1)} %broadcast_in_dim.2.profile_ref, bf16[64,512]{1,0:T(8,128)(2,1)S(1)} %collective-permute-done.18.refs_0_, ...), custom_call_target="tpu_custom_call" | custom-call | tf_op jit(solution)/shard_map/pallas_call | solution.py:404
  (7 shorter events, 0.1 us)
Async XLA Ops:
  0.0 0.7 %copy-start = (f32[1,256,16]{1,2,0:T(8,128)S(1)}, f32[1,256,16]{1,2,0:T(8,128)}, u32[]{:S(2)}) copy-start(f32[1,256,16]{1,2,0:T(8,128)} %param.11) | copy-start | bytes 49156
  0.7 0.7 %copy-start.1 = (f32[1,16,256]{2,1,0:T(8,128)S(1)}, f32[1,16,256]{2,1,0:T(8,128)}, u32[]{:S(2)}) copy-start(f32[1,16,256]{2,1,0:T(8,128)} %param.13) | copy-start | bytes 49156
  1.4 0.7 copy-start.3
  2.2 1.2 %collective-permute-start = (f32[32,256]{1,0:T(8,128)S(1)}, f32[32,256]{1,0:T(8,128)S(1)}, u32[]{:S(2)}, u32[]{:S(2)}) collective-permute-start(f32[32,256]{1,0:T(8,128)S(1)} %shard_map.73.refs_0_), channel_id=1, source_target_pairs={{0,1},{1,0},{2,3},{3,2},{4,5},{5,4},{6,7},{7,6},{8,9},{9,8},{10,11... | collective-permute-start | bytes 98312 | tf_op jit(solution)/shard_map/ppermute | solution.py:25
  3.4 16.7 %copy-start.5 = (bf16[4,64,4]{1,2,0:T(4,128)(2,1)S(1)}, bf16[4,64,4]{1,2,0:T(4,128)(2,1)}, u32[]{:S(2)}) copy-start(bf16[4,64,4]{1,2,0:T(4,128)(2,1)} %param.10) | copy-start | bytes 6148
  3.4 21.4 %copy-start.2 = (s32[8,128]{1,0:T(8,128)S(1)}, s32[8,128]{1,0:T(8,128)}, u32[]{:S(2)}) copy-start(s32[8,128]{1,0:T(8,128)} %param.8) | copy-start | bytes 12292
  3.4 10.0 %collective-permute-start.1 = (f32[64,256]{1,0:T(8,128)S(1)}, f32[64,256]{1,0:T(8,128)S(1)}, u32[]{:S(2)}, u32[]{:S(2)}) collective-permute-start(f32[64,256]{1,0:T(8,128)S(1)} %pad_maximum_fusion), channel_id=1, source_target_pairs={{0,8},{1,11},{2,10},{3,9},{4,12},{5,15},{6,14},{7,13},{8,0},{9,3},... | collective-permute-start | bytes 196616 | tf_op jit(solution)/shard_map/ppermute | solution.py:25
  5.1 8.3 %collective-permute-start.2 = (f32[64,256]{1,0:T(8,128)S(1)}, f32[64,256]{1,0:T(8,128)S(1)}, u32[]{:S(2)}, u32[]{:S(2)}) collective-permute-start(f32[64,256]{1,0:T(8,128)S(1)} %pad_maximum_fusion), channel_id=1, source_target_pairs={{0,2},{1,15},{2,0},{3,13},{4,6},{5,11},{6,4},{7,9},{8,10},{9,7},{1... | collective-permute-start | bytes 196616 | tf_op jit(solution)/shard_map/ppermute | solution.py:25
  7.0 6.4 %collective-permute-start.3 = (f32[64,256]{1,0:T(8,128)S(1)}, f32[64,256]{1,0:T(8,128)S(1)}, u32[]{:S(2)}, u32[]{:S(2)}) collective-permute-start(f32[64,256]{1,0:T(8,128)S(1)} %pad_maximum_fusion), channel_id=1, source_target_pairs={{0,6},{1,13},{2,4},{3,15},{4,2},{5,9},{6,0},{7,11},{8,14},{9,5},{1... | collective-permute-start | bytes 196616 | tf_op jit(solution)/shard_map/ppermute | solution.py:25
  9.5 5.4 %collective-permute-start.4 = (f32[32,256]{1,0:T(8,128)S(1)}, f32[32,256]{1,0:T(8,128)S(1)}, u32[]{:S(2)}, u32[]{:S(2)}) collective-permute-start(f32[32,256]{1,0:T(8,128)S(1)} %shard_map.73.refs_0_), channel_id=1, source_target_pairs={{0,4},{1,5},{2,6},{3,7},{4,0},{5,1},{6,2},{7,3},{8,12},{9,13},{10,... | collective-permute-start | bytes 98312 | tf_op jit(solution)/shard_map/ppermute | solution.py:25
  15.4 1.6 %collective-permute-start.5 = (f32[256,256]{1,0:T(8,128)S(1)}, f32[256,256]{1,0:T(8,128)S(1)}, u32[]{:S(2)}, u32[]{:S(2)}) collective-permute-start(f32[256,256]{1,0:T(8,128)S(1)} %shard_map.74), channel_id=1, source_target_pairs={{0,1},{1,0},{2,3},{3,2},{4,5},{5,4},{6,7},{7,6},{8,9},{9,8},{10,11... | collective-permute-start | bytes 786440 | tf_op jit(solution)/shard_map/ppermute | solution.py:25
  17.0 7.8 %collective-permute-start.6 = (bf16[256,256]{1,0:T(8,128)(2,1)S(1)}, bf16[256,256]{1,0:T(8,128)(2,1)S(1)}, u32[]{:S(2)}, u32[]{:S(2)}) collective-permute-start(bf16[256,256]{1,0:T(8,128)(2,1)S(1)} %add_convert_fusion.refs_0_.refs_4_), channel_id=1, source_target_pairs={{0,16},{1,49},{2,18},{3,51},{4,20},{5,53},{6,22},{7,55},{8,24},{9,... | collective-permute-start | bytes 393224 | tf_op jit(solution)/shard_map/ppermute | solution.py:25
  20.2 11.3 %collective-permute-start.7 = (bf16[256,256]{1,0:T(8,128)(2,1)S(1)}, bf16[256,256]{1,0:T(8,128)(2,1)S(1)}, u32[]{:S(2)}, u32[]{:S(2)}) collective-permute-start(bf16[256,256]{1,0:T(8,128)(2,1)S(1)} %add_convert_fusion.refs_0_.refs_4_), channel_id=1, source_target_pairs={{0,32},{1,113},{2,34},{3,115},{4,36},{5,117},{6,38},{7,119},{8,40}... | collective-permute-start | bytes 393224 | tf_op jit(solution)/shard_map/ppermute | solution.py:25
  21.8 10.4 %collective-permute-start.8 = (bf16[256,256]{1,0:T(8,128)(2,1)S(1)}, bf16[256,256]{1,0:T(8,128)(2,1)S(1)}, u32[]{:S(2)}, u32[]{:S(2)}) collective-permute-start(bf16[256,256]{1,0:T(8,128)(2,1)S(1)} %add_convert_fusion.refs_0_.refs_4_), channel_id=1, source_target_pairs={{0,96},{1,81},{2,98},{3,83},{4,100},{5,85},{6,102},{7,87},{8,104},... | collective-permute-start | bytes 393224 | tf_op jit(solution)/shard_map/ppermute | solution.py:25
  24.0 7.5 %collective-permute-start.9 = (bf16[128,256]{1,0:T(8,128)(2,1)S(1)}, bf16[128,256]{1,0:T(8,128)(2,1)S(1)}, u32[]{:S(2)}, u32[]{:S(2)}) collective-permute-start(bf16[128,256]{1,0:T(8,128)(2,1)S(1)} %constant_dynamic-slice_fusion), channel_id=1, source_target_pairs={{0,64},{1,65},{2,66},{3,67},{4,68},{5,69},{6,70},{7,71},{8,72},{9,... | collective-permute-start | bytes 196616 | tf_op jit(solution)/shard_map/ppermute | solution.py:25
  32.2 2.6 %collective-permute-start.11 = (bf16[256,256]{1,0:T(8,128)(2,1)S(1)}, bf16[256,256]{1,0:T(8,128)(2,1)S(1)}, u32[]{:S(2)}, u32[]{:S(2)}) collective-permute-start(bf16[256,256]{1,0:T(8,128)(2,1)S(1)} %collective-permute-done.7.refs_0_.refs_6_), channel_id=1, source_target_pairs={{0,1},{1,0},{2,3},{3,2},{4,5},{5,4},{6,7},{7,6},{8,9},{9,8},{10,11... | collective-permute-start | bytes 393224 | tf_op jit(solution)/shard_map/ppermute | solution.py:25
  32.2 2.6 %collective-permute-start.12 = (bf16[256,256]{1,0:T(8,128)(2,1)S(1)}, bf16[256,256]{1,0:T(8,128)(2,1)S(1)}, u32[]{:S(2)}, u32[]{:S(2)}) collective-permute-start(bf16[256,256]{1,0:T(8,128)(2,1)S(1)} %collective-permute-done.8.refs_1_.refs_7_), channel_id=1, source_target_pairs={{0,1},{1,0},{2,3},{3,2},{4,5},{5,4},{6,7},{7,6},{8,9},{9,8},{10,11... | collective-permute-start | bytes 393224 | tf_op jit(solution)/shard_map/ppermute | solution.py:25
  32.7 2.1 %collective-permute-start.13 = (bf16[128,256]{1,0:T(8,128)(2,1)S(1)}, bf16[128,256]{1,0:T(8,128)(2,1)S(1)}, u32[]{:S(2)}, u32[]{:S(2)}) collective-permute-start(bf16[128,256]{1,0:T(8,128)(2,1)S(1)} %collective-permute-done.9.refs_4_.refs_12_), channel_id=1, source_target_pairs={{0,1},{1,0},{2,3},{3,2},{4,5},{5,4},{6,7},{7,6},{8,9},{9,8},{10,11... | collective-permute-start | bytes 196616 | tf_op jit(solution)/shard_map/ppermute | solution.py:25
  32.7 2.1 %collective-permute-start.10 = (bf16[256,256]{1,0:T(8,128)(2,1)S(1)}, bf16[256,256]{1,0:T(8,128)(2,1)S(1)}, u32[]{:S(2)}, u32[]{:S(2)}) collective-permute-start(bf16[256,256]{1,0:T(8,128)(2,1)S(1)} %collective-permute-done.6.refs_1_.refs_5_), channel_id=1, source_target_pairs={{0,1},{1,0},{2,3},{3,2},{4,5},{5,4},{6,7},{7,6},{8,9},{9,8},{10,11... | collective-permute-start | bytes 393224 | tf_op jit(solution)/shard_map/ppermute | solution.py:25
  35.4 13.3 %collective-permute-start.14 = (bf16[64,512]{1,0:T(8,128)(2,1)S(1)}, bf16[64,512]{1,0:T(8,128)(2,1)S(1)}, u32[]{:S(2)}, u32[]{:S(2)}) collective-permute-start(bf16[64,512]{1,0:T(8,128)(2,1)S(1)} %get-tuple-element.60), channel_id=1, source_target_pairs={{0,16},{16,32},{32,48},{48,64},{64,80},{80,96},{96,112},{112,0},{1... | collective-permute-start | bytes 196616 | tf_op jit(solution)/shard_map/ppermute | solution.py:303
  36.5 12.2 %collective-permute-start.15 = (bf16[64,512]{1,0:T(8,128)(2,1)S(1)}, bf16[64,512]{1,0:T(8,128)(2,1)S(1)}, u32[]{:S(2)}, u32[]{:S(2)}) collective-permute-start(bf16[64,512]{1,0:T(8,128)(2,1)S(1)} %get-tuple-element.61), channel_id=1, source_target_pairs={{0,112},{16,0},{32,16},{48,32},{64,48},{80,64},{96,80},{112,96},{1... | collective-permute-start | bytes 196616 | tf_op jit(solution)/shard_map/ppermute | solution.py:303
  41.1 7.5 %collective-permute-start.16 = (bf16[64,128]{1,0:T(8,128)(2,1)S(1)}, bf16[64,128]{1,0:T(8,128)(2,1)S(1)}, u32[]{:S(2)}, u32[]{:S(2)}) collective-permute-start(bf16[64,128]{1,0:T(8,128)(2,1)S(1)} %get-tuple-element.62), channel_id=1, source_target_pairs={{0,1},{1,2},{2,3},{3,4},{4,5},{5,6},{6,7},{7,8},{8,9},{9,10},{10,1... | collective-permute-start | bytes 49160 | tf_op jit(solution)/shard_map/ppermute | solution.py:303
  41.1 7.5 %collective-permute-start.17 = (bf16[64,128]{1,0:T(8,128)(2,1)S(1)}, bf16[64,128]{1,0:T(8,128)(2,1)S(1)}, u32[]{:S(2)}, u32[]{:S(2)}) collective-permute-start(bf16[64,128]{1,0:T(8,128)(2,1)S(1)} %get-tuple-element.63), channel_id=1, source_target_pairs={{0,15},{1,0},{2,1},{3,2},{4,3},{5,4},{6,5},{7,6},{8,7},{9,8},{10,9... | collective-permute-start | bytes 49160 | tf_op jit(solution)/shard_map/ppermute | solution.py:303
  45.0 3.9 %copy-start.4 = (s32[4]{0:T(128)S(1)}, s32[4]{0:T(128)}, u32[]{:S(2)}) copy-start(s32[4]{0:T(128)} %port_ref.3) | copy-start | bytes 52
  56.1 11.0 %collective-permute-start.18 = (bf16[64,512]{1,0:T(8,128)(2,1)S(1)}, bf16[64,512]{1,0:T(8,128)(2,1)S(1)}, u32[]{:S(2)}, u32[]{:S(2)}) collective-permute-start(bf16[64,512]{1,0:T(8,128)(2,1)S(1)} %get-tuple-element.65), channel_id=1, source_target_pairs={{0,16},{16,32},{32,48},{48,64},{64,80},{80,96},{96,112},{112,0},{1... | collective-permute-start | bytes 196616 | tf_op jit(solution)/shard_map/ppermute | solution.py:303
  56.2 10.9 %collective-permute-start.19 = (bf16[64,512]{1,0:T(8,128)(2,1)S(1)}, bf16[64,512]{1,0:T(8,128)(2,1)S(1)}, u32[]{:S(2)}, u32[]{:S(2)}) collective-permute-start(bf16[64,512]{1,0:T(8,128)(2,1)S(1)} %get-tuple-element.66), channel_id=1, source_target_pairs={{0,112},{16,0},{32,16},{48,32},{64,48},{80,64},{96,80},{112,96},{1... | collective-permute-start | bytes 196616 | tf_op jit(solution)/shard_map/ppermute | solution.py:303
  61.8 5.3 %collective-permute-start.20 = (bf16[64,128]{1,0:T(8,128)(2,1)S(1)}, bf16[64,128]{1,0:T(8,128)(2,1)S(1)}, u32[]{:S(2)}, u32[]{:S(2)}) collective-permute-start(bf16[64,128]{1,0:T(8,128)(2,1)S(1)} %get-tuple-element.67), channel_id=1, source_target_pairs={{0,1},{1,2},{2,3},{3,4},{4,5},{5,6},{6,7},{7,8},{8,9},{9,10},{10,1... | collective-permute-start | bytes 49160 | tf_op jit(solution)/shard_map/ppermute | solution.py:303
  61.8 5.3 %collective-permute-start.21 = (bf16[64,128]{1,0:T(8,128)(2,1)S(1)}, bf16[64,128]{1,0:T(8,128)(2,1)S(1)}, u32[]{:S(2)}, u32[]{:S(2)}) collective-permute-start(bf16[64,128]{1,0:T(8,128)(2,1)S(1)} %get-tuple-element.68), channel_id=1, source_target_pairs={{0,15},{1,0},{2,1},{3,2},{4,3},{5,4},{6,5},{7,6},{8,7},{9,8},{10,9... | collective-permute-start | bytes 49160 | tf_op jit(solution)/shard_map/ppermute | solution.py:303

commit v6 on v5

--- a/solution.py
+++ b/solution.py
@@ -1,4 +1,5 @@
 import functools
+import math
 
 import jax
 import jax.numpy as jnp
@@ -11,6 +12,7 @@
 F32 = jnp.float32
 LANES = 128
 PARAMS = pltpu.CompilerParams(vmem_limit_bytes=20 * 2**20)
+WIDE_PARAMS = pltpu.CompilerParams(vmem_limit_bytes=50 * 2**20)
 
 
 def swap(value, axis, first, second=None):
@@ -25,14 +27,21 @@
     return lax.ppermute(value, ("row", "col"), pairs)
 
 
-def pack_kernel(shapes_ref, values_ref, weights_ref, out_ref):
-    modes = shapes_ref.shape[0]
-    row = lax.broadcasted_iota(jnp.int32, (modes, modes), 0)
-    col = lax.broadcasted_iota(jnp.int32, (modes, modes), 1)
-    values = jnp.broadcast_to(values_ref[...], (modes, modes))
-    column = jnp.sum(jnp.where(row == col, values, 0.0), axis=1, keepdims=True)
-    out_ref[0:modes] = shapes_ref[...] * column
-    out_ref[modes:] = weights_ref[...]
+def flat_kernel(x_hbm, out_ref, x_ref, sems):
+    order, ports, rows, width = x_ref.shape
+    quarter, tile = order // 4, rows * width
+    edges = [slice(edge * quarter, (edge + 1) * quarter) for edge in range(4)]
+    copies = [
+        pltpu.make_async_copy(x_hbm.at[lines], x_ref.at[lines], sems.at[edge])
+        for edge, lines in enumerate(edges)
+    ]
+    for copy in copies:
+        copy.start()
+    for copy, lines in zip(copies, edges):
+        copy.wait()
+        for port in range(ports):
+            value = x_ref[lines, port].astype(F32).reshape(quarter, tile)
+            out_ref[lines, port * tile : (port + 1) * tile] = value.astype(BF)
 
 
 def partial_kernel(modes, *refs):
@@ -66,18 +75,22 @@
 
 def own_type_map(mode_shapes, mode_values, mode_weights, traces):
     modes, order = mode_weights.shape[1:]
-    (own,) = whole_call(
-        pack_kernel,
-        [jax.ShapeDtypeStruct((2 * modes, order), F32)],
-        mode_shapes[0].T,
-        mode_values,
-        mode_weights[0],
-    )
+    own = jnp.concatenate([mode_shapes[0].T, mode_weights[0]], axis=0)
+    own = own * jnp.concatenate([mode_values[0], jnp.ones((modes,), F32)])[:, None]
     far = swap(own, "col", 4)
     pair = jnp.concatenate([own, swap(own, "col", 1)], axis=0)
     pair, traces = lax.optimization_barrier((pair, traces))
     got = [swap(pair, "col", 8, 10), swap(pair, "col", 2, 14), swap(pair, "col", 6, 12)]
-    x = traces.reshape(order, -1)
+    shape = (order,) + traces.shape[2:]
+    x = pl.pallas_call(
+        flat_kernel,
+        in_specs=[pl.BlockSpec(memory_space=pltpu.HBM)],
+        out_specs=WHOLE,
+        out_shape=jax.ShapeDtypeStruct((order, math.prod(shape[1:])), BF),
+        scratch_shapes=[pltpu.VMEM(shape, BF), pltpu.SemaphoreType.DMA((4,))],
+        compiler_params=WIDE_PARAMS,
+        cost_estimate=pl.CostEstimate(flops=2**30, bytes_accessed=0, transcendentals=0),
+    )(traces.reshape(shape))
     *got, x = lax.optimization_barrier((*got, x))
     (partial,) = whole_call(
         functools.partial(partial_kernel, modes),
@@ -92,42 +105,28 @@
 MAP_STEPS = ((0, 0), (1, 3), (2, 7), (6, 5), (3, 1), (7, 2), (5, 6), (4, 4))
 
 
-def patch(block, rows, width, east_lane, port_ref, profile_ref, halo_refs):
-    north, south, west, east = halo_refs
-    quarter = block.shape[0] // 4
-    port = pl.program_id(0)
-    lane = lax.broadcasted_iota(jnp.int32, (quarter, LANES), 1)
-    mine, count = lax.axis_index("row"), lax.axis_size("row")
-    mine_col, count_col = lax.axis_index("col"), lax.axis_size("col")
-    zero = jnp.zeros((), BF)
-    block[0:quarter, 0:LANES] = jnp.where(mine > 0, north[...], zero)
-    block[quarter : 2 * quarter, (rows - 1) * LANES : rows * LANES] = jnp.where(
-        mine < count - 1, south[...], zero
-    )
-    west_all = jnp.where(mine_col > 0, west[...].astype(F32), 0.0)
-    east_all = jnp.where(mine_col < count_col - 1, east[...].astype(F32), 0.0)
-    for row in range(rows):
-        place = port * rows + row
-        cols = slice(row * LANES, (row + 1) * LANES)
-        from_west = pltpu.roll(west_all, lax.rem(2 * LANES - east_lane - place, LANES), 1)
-        from_east = pltpu.roll(east_all, LANES - 1 - place, 1)
-        west_part = block[2 * quarter : 3 * quarter, cols].astype(F32)
-        east_part = block[3 * quarter : 4 * quarter, cols].astype(F32)
-        block[2 * quarter : 3 * quarter, cols] = jnp.where(lane == 0, from_west, west_part).astype(BF)
-        block[3 * quarter : 4 * quarter, cols] = jnp.where(
-            lane == LANES - 1, from_east, east_part
-        ).astype(BF)
+def halos_inside(halo_refs):
+    north, south, west, east = (ref[...].astype(F32) for ref in halo_refs)
+    row, rows = lax.axis_index("row"), lax.axis_size("row")
+    col, cols = lax.axis_index("col"), lax.axis_size("col")
+    return (
+        jnp.where(row > 0, north, 0.0),
+        jnp.where(row < rows - 1, south, 0.0),
+        jnp.where(col > 0, west, 0.0),
+        jnp.where(col < cols - 1, east, 0.0),
+    )
+
+
+def lane_of(value, lane):
+    return jnp.broadcast_to(value[:, lane : lane + 1], (value.shape[0], LANES))
+
+
+def port_place(port_ref, port, rows, width):
+    all_cols = width * lax.axis_size("col")
     cell = port_ref[port]
-    row = cell // (width * count_col) - mine * rows
-    col = cell % (width * count_col) - mine_col * width
-
-    @pl.when((row >= 0) & (row < rows) & (col >= 0) & (col < width))
-    def _():
-        cols = pl.ds(pl.multiple_of(row * LANES, LANES), LANES)
-        here = lax.broadcasted_iota(jnp.int32, (4 * quarter, LANES), 1) == col
-        current = block[:, cols].astype(F32)
-        added = current + profile_ref[0].astype(F32)
-        block[:, cols] = jnp.where(here, added, current).astype(BF)
+    row = cell // all_cols - lax.axis_index("row") * rows
+    col = cell % all_cols - lax.axis_index("col") * width
+    return row, col, (row >= 0) & (row < rows) & (col >= 0) & (col < width)
 
 
 def map_rows(map_refs, first, last):
@@ -186,21 +185,32 @@
 
 def side_columns(x_ref, types, ports):
     order, tile = x_ref.shape[0], types.shape[1]
-    wide = 2 * LANES
-    spread = jnp.broadcast_to(types, (16, tile)).astype(BF)
-    place = lax.broadcasted_iota(jnp.int32, (wide, LANES), 0)
-    lane = lax.broadcasted_iota(jnp.int32, (wide, LANES), 1)
-    wanted = jnp.where(lane < 64, lane * LANES, (lane - 64) * LANES + LANES - 1)
-    picked = None
-    for start in range(0, ports * tile, wide):
-        pick = jnp.where(place + start == wanted, 1.0, 0.0).astype(BF)
-        inside = start % tile
-        both = jnp.concatenate(
-            [x_ref[:, start : start + wide], spread[:, inside : inside + wide]], axis=0
+    rows = tile // LANES
+
+    def pick(block_of, lines):
+        lane = lax.broadcasted_iota(jnp.int32, (lines, LANES), 1)
+        first = last = jnp.zeros((lines, LANES), F32)
+        for place in range(ports * rows):
+            turned = pltpu.roll(block_of(place), place + 1, 1)
+            first = jnp.where(lane == place + 1, turned, first)
+            last = jnp.where(lane == place, turned, last)
+        first = pltpu.roll(first, LANES - 1, 1)
+        return jnp.where(lane < 64, first, pltpu.roll(last, 64, 1)).astype(BF)
+
+    def types_of(place):
+        start = place % rows * LANES
+        return jnp.broadcast_to(types[:, start : start + LANES], (16, LANES))
+
+    quarter = order // 4
+    sides = [
+        pick(
+            lambda place: x_ref[edge * quarter : (edge + 1) * quarter,
+                                place * LANES : (place + 1) * LANES].astype(F32),
+            quarter,
         )
-        part = jnp.dot(both, pick, preferred_element_type=F32)
-        picked = part if picked is None else picked + part
-    return picked[0:order].astype(BF), picked[order:].astype(BF)
+        for edge in range(4)
+    ]
+    return jnp.concatenate(sides, axis=0), pick(types_of, 16)
 
 
 def rims(x_ref, types, ports, sides, kinds, maps, so_far):
@@ -252,47 +262,116 @@
     refs[-1][...] = outs[2][quarter:]
 
 
-def first_kernel(rows, first, x_ref, types_ref, done_ref, *refs):
+def first_kernel(rows, ports, first, x_ref, types_ref, done_ref, *refs):
     maps = with_steps(refs[:-1], first, len(MAP_STEPS))
     types = types_ref[...].astype(F32).astype(BF)
-    before = done_ref[...].astype(F32)
-    total = products(x_ref[...], types, maps, 0, x_ref.shape[0], before)
-    shifted(total, refs[-1], rows)
+    tile = types.shape[1]
+    for port in range(ports):
+        cols = slice(port * tile, (port + 1) * tile)
+        before = done_ref[:, cols].astype(F32)
+        total = products(x_ref[:, cols], types, maps, 0, x_ref.shape[0], before)
+        shifted(total, refs[-1].at[:, cols], rows)
 
 
 def second_kernel(rows, width, port_ref, x_ref, types_ref, profile_ref, *refs):
     halo_refs, map_refs, next_ref = refs[:4], refs[4:-6], refs[-6]
-    north_out, south_out, west_out, east_out, block = refs[-5:]
-    block[...] = x_ref[...]
-    patch(block, rows, width, 64, port_ref, profile_ref, halo_refs)
-    order = block.shape[0]
+    north_out, south_out, west_out, east_out, blocks = refs[-5:]
+    types = types_ref[...].astype(F32).astype(BF)
+    tile = types.shape[1]
+    order = x_ref.shape[0]
     quarter = order // 4
-    types = types_ref[...].astype(F32).astype(BF)
     maps = with_steps(map_refs, 0, len(MAP_STEPS))
-    total = products(block[...], types, maps, 0, order)
-    north, south = shifted(total, next_ref, rows)
-    north_out[...] = north[:, 0:LANES]
-    south_out[...] = south[:, (rows - 1) * LANES :]
-    port = pl.program_id(0)
+    north_in, south_in, west_in, east_in = halos_inside(halo_refs)
     lane = lax.broadcasted_iota(jnp.int32, (quarter, LANES), 1)
-    west_rim = jnp.where(port == 0, 0.0, west_out[...].astype(F32))
-    east_rim = jnp.where(port == 0, 0.0, east_out[...].astype(F32))
-    for row in range(rows):
-        place = port * rows + row
-        cols = slice(row * LANES, (row + 1) * LANES)
-        west = total[2 * quarter : 3 * quarter, cols]
-        east = total[3 * quarter : 4 * quarter, cols]
-        west_rim = jnp.where(lane == place, pltpu.roll(west, place, 1), west_rim)
-        east_rim = jnp.where(lane == place, pltpu.roll(east, place + 1, 1), east_rim)
+    west_rim = east_rim = jnp.zeros((quarter, LANES), F32)
+    for port in range(x_ref.shape[1] // tile):
+        own = slice(port * tile, (port + 1) * tile)
+        rim = slice(port * LANES, (port + 1) * LANES)
+        block = blocks.at[port % 2]
+        block[...] = x_ref[:, own]
+        block[0:quarter, 0:LANES] = north_in[:, rim].astype(BF)
+        block[quarter : 2 * quarter, tile - LANES :] = south_in[:, rim].astype(BF)
+        for row in range(rows):
+            place = port * rows + row
+            cols = slice(row * LANES, (row + 1) * LANES)
+            west = block[2 * quarter : 3 * quarter, cols].astype(F32)
+            east = block[3 * quarter :, cols].astype(F32)
+            west = jnp.where(lane == 0, lane_of(west_in, 64 + place), west)
+            east = jnp.where(lane == LANES - 1, lane_of(east_in, place), east)
+            block[2 * quarter : 3 * quarter, cols] = west.astype(BF)
+            block[3 * quarter :, cols] = east.astype(BF)
+        row, col, inside = port_place(port_ref, port, rows, width)
+
+        @pl.when(inside)
+        def _():
+            cols = pl.ds(pl.multiple_of(row * LANES, LANES), LANES)
+            here = lax.broadcasted_iota(jnp.int32, (order, LANES), 1) == col
+            current = block[:, cols].astype(F32)
+            added = current + profile_ref[port].astype(F32)
+            block[:, cols] = jnp.where(here, added, current).astype(BF)
+
+        total = products(block[...], types, maps, 0, order)
+        north, south = shifted(total, next_ref.at[:, own], rows)
+        north_out[:, rim] = north[:, 0:LANES]
+        south_out[:, rim] = south[:, tile - LANES :]
+        for row in range(rows):
+            place = port * rows + row
+            west = lane_of(total[2 * quarter : 3 * quarter], row * LANES)
+            east = lane_of(total[3 * quarter :], (row + 1) * LANES - 1)
+            west_rim = jnp.where(lane == place, west, west_rim)
+            east_rim = jnp.where(lane == place, east, east_rim)
     west_out[...] = west_rim.astype(BF)
     east_out[...] = east_rim.astype(BF)
 
 
 def last_kernel(rows, width, port_ref, x_ref, profile_ref, *refs):
-    out_ref, block = refs[-2:]
-    block[...] = x_ref[...]
-    patch(block, rows, width, 0, port_ref, profile_ref, refs[:4])
-    out_ref[...] = block[...].astype(F32).reshape(out_ref.shape).astype(BF)
+    out_ref, buffer, sems = refs[4:]
+    order, ports = buffer.shape[:2]
+    quarter, tile = order // 4, rows * width
+    north_in, south_in, west_in, east_in = halos_inside(refs[:4])
+    lane = lax.broadcasted_iota(jnp.int32, (quarter, LANES), 1)
+    copies = []
+    for edge in (2, 3, 0, 1):
+        lines = slice(edge * quarter, (edge + 1) * quarter)
+        for port in range(ports):
+            rim = slice(port * LANES, (port + 1) * LANES)
+            starts = [port * tile + row * LANES for row in range(rows)]
+            parts = [x_ref[lines, start : start + LANES].astype(F32) for start in starts]
+            places = range(port * rows, (port + 1) * rows)
+            if edge == 0:
+                parts[0] = north_in[:, rim]
+            elif edge == 1:
+                parts[-1] = south_in[:, rim]
+            elif edge == 2:
+                parts = [
+                    jnp.where(lane == 0, lane_of(west_in, place), part)
+                    for place, part in zip(places, parts)
+                ]
+            else:
+                parts = [
+                    jnp.where(lane == LANES - 1, lane_of(east_in, place), part)
+                    for place, part in zip(places, parts)
+                ]
+            value = jnp.concatenate(parts, axis=1).reshape(quarter, rows, LANES)
+            buffer[lines, port] = value.astype(BF)
+        for port in range(ports):
+            row, col, inside = port_place(port_ref, port, rows, width)
+
+            @pl.when(inside)
+            def _():
+                current = buffer[lines, port].astype(F32)
+                here = (lax.broadcasted_iota(jnp.int32, current.shape, 1) == row) & (
+                    lax.broadcasted_iota(jnp.int32, current.shape, 2) == col
+                )
+                profile = profile_ref[port, lines, :].astype(F32).reshape(quarter, 1, LANES)
+                added = current + jnp.broadcast_to(profile, current.shape)
+                buffer[lines, port] = jnp.where(here, added, current).astype(BF)
+
+        copy = pltpu.make_async_copy(buffer.at[lines], out_ref.at[lines], sems.at[edge])
+        copy.start()
+        copies.append(copy)
+    for copy in copies:
+        copy.wait()
 
 
 def exchange(rims):
@@ -325,13 +404,7 @@
     profile = jnp.broadcast_to(
         jnp.transpose(port_profile.reshape(order, ports))[:, :, None], (ports, order, LANES)
     )
-    block = pl.BlockSpec((order, tile), lambda i: (0, i))
-    types_spec = pl.BlockSpec((1, tile), lambda i: (0, 0))
-    long_rim = pl.BlockSpec((quarter, LANES), lambda i: (0, i))
-    short_rim = pl.BlockSpec((quarter, LANES), lambda i: (0, 0))
-    rims = [long_rim, long_rim, short_rim, short_rim]
     ports_spec = pl.BlockSpec(memory_space=pltpu.SMEM)
-    profile_spec = pl.BlockSpec((1, order, LANES), lambda i: (i, 0, 0))
     next_shape = jax.ShapeDtypeStruct((order, ports * tile), BF)
     rim_shapes = [jax.ShapeDtypeStruct((quarter, ports * LANES), BF)] * 2 + [
         jax.ShapeDtypeStruct((quarter, LANES), BF)
@@ -368,7 +441,6 @@
     done, *parts = parts
     late = swapped + [half]
     maps = [own_map, fetched[0]] + rest + late
-    map_specs = [pl.BlockSpec(value.shape, lambda i: (0, 0)) for value in maps]
     sent = whole_call(
         functools.partial(rim_kernel, ports, early[2]),
         rim_shapes,
@@ -381,35 +453,37 @@
         flops=work // 8,
     )
     halos = exchange(sent)
-    x = pl.pallas_call(
-        functools.partial(first_kernel, rows, early[2]),
-        grid=(ports,),
-        in_specs=[block, types_spec, block] + map_specs[early[2] :],
-        out_specs=block,
-        out_shape=next_shape,
-        compiler_params=PARAMS,
-        cost_estimate=pl.CostEstimate(flops=work // 2, bytes_accessed=0, transcendentals=0),
-    )(x, types, done, *late)
+    (x,) = whole_call(
+        functools.partial(first_kernel, rows, ports, early[2]),
+        [next_shape],
+        x,
+        types,
+        done,
+        *late,
+        flops=work // 2,
+    )
+    operands = [port_cell, x, types, profile, *halos, *maps]
     x, *sent = pl.pallas_call(
         functools.partial(second_kernel, rows, width),
-        grid=(ports,),
-        in_specs=[ports_spec, block, types_spec, profile_spec] + rims + map_specs,
-        out_specs=[block] + rims,
+        in_specs=[ports_spec] + [WHOLE] * (len(operands) - 1),
+        out_specs=[WHOLE] * 5,
         out_shape=[next_shape] + rim_shapes,
-        scratch_shapes=[pltpu.VMEM((order, tile), BF)],
+        scratch_shapes=[pltpu.VMEM((2, order, tile), BF)],
         compiler_params=PARAMS,
         cost_estimate=pl.CostEstimate(flops=work, bytes_accessed=0, transcendentals=0),
-    )(port_cell, x, types, profile, *halos, *maps)
-    halos = exchange(sent)
+    )(*operands)
+    operands = [port_cell, x, profile, *exchange(sent)]
     out = pl.pallas_call(
         functools.partial(last_kernel, rows, width),
-        grid=(ports,),
-        in_specs=[ports_spec, block, profile_spec] + rims,
-        out_specs=pl.BlockSpec((order, 1, rows, LANES), lambda i: (0, i, 0, 0)),
+        in_specs=[ports_spec] + [WHOLE] * (len(operands) - 1),
+        out_specs=pl.BlockSpec(memory_space=pl.ANY),
         out_shape=jax.ShapeDtypeStruct((order, ports, rows, width), BF),
-        scratch_shapes=[pltpu.VMEM((order, tile), BF)],
+        scratch_shapes=[
+            pltpu.VMEM((order, ports, rows, width), BF),
+            pltpu.SemaphoreType.DMA((4,)),
+        ],
         compiler_params=PARAMS,
-    )(port_cell, x, profile, *halos)
+    )(*operands)
     return out.reshape(traces.shape)
 
 

time: 70.9 us -> 68 us (0.959)
  local copies, waits for them, and re-layouts: 5.22 us -> 0.96 us
  waiting for transfers between devices: 9.69 us -> 11.7 us
  Pallas kernels: 20.1 us -> 19 us
  other arithmetic: 0.05 us -> 0.85 us
    reshape x1 -> x0, local copies, waits for them, and re-layouts: 2.82 us -> none  [own_type_map(): x = traces.reshape(order, -1)]
    pallas_call x3, Pallas kernels: 14.4 us -> 11.7 us  [the longest x1 6.66 us: body(): pl.pallas_call(functools.partial(second_kernel, rows, width), in_specs=[p...]
    unnamed x13 -> x7, local copies, waits for them, and re-layouts: 2.11 us -> 0.02 us
    ppermute x14, waiting for transfers between devices: 8.23 us -> 10.3 us  [swap(): return lax.ppermute(value, ('row', 'col'), pairs)]
    pallas_call x5, Pallas kernels: 5.7 us -> 7.27 us  [whole_call(): pl.pallas_call(kernel, in_specs=[WHOLE] * len(operands), out_specs=[WHOLE...]
    mul x0 -> x1, other arithmetic: none -> 0.81 us  [own_type_map(): own * jnp.concatenate([mode_values[0], jnp.ones((modes,), F32)])[:, None]]
  transfers between devices with their start and end apart: 22 -> 22, of which waited for: 6 -> 7; matrix products, arithmetic and copies ran while one was open for 4% -> 0% of each run, Pallas kernels for 12% -> 12%
where the time goes in v6:
time: 68 us; the launch traced here: 67.7 us
  starting transfers between devices  34.8 us (51%)
  Pallas kernels  19 us (28%)
  waiting for transfers between devices  11.7 us (17%)
  local copies, waits for them, and re-layouts  0.96 us (1%)
  other arithmetic  0.85 us (1%)
    ppermute x8, starting transfers between devices, send(): lax.ppermute(value, axis, [(i, (i + step) % count) for i in range(count)])  19.1 us
    ppermute x14, starting transfers between devices, swap(): return lax.ppermute(value, ('row', 'col'), pairs)  15.7 us
    ppermute x14, waiting for transfers between devices, swap(): return lax.ppermute(value, ('row', 'col'), pairs)  10.3 us
    pallas_call x5, Pallas kernels, whole_call(): pl.pallas_call(kernel, in_specs=[WHOLE] * len(operands), out_specs=[WHOLE...  7.27 us
    pallas_call x1, Pallas kernels, body(): pl.pallas_call(functools.partial(second_kernel, rows, width), in_specs=[p...  6.66 us
    pallas_call x1, Pallas kernels, body(): pl.pallas_call(functools.partial(last_kernel, rows, width), in_specs=[por...  3.08 us
    pallas_call x1, Pallas kernels, own_type_map(): pl.pallas_call(flat_kernel, in_specs=[pl.BlockSpec(memory_space=pltpu.HBM...  2 us
    ppermute x8, waiting for transfers between devices, send(): lax.ppermute(value, axis, [(i, (i + step) % count) for i in range(count)])  1.46 us
  transfers between devices with their start and end apart: 22, of which 7 were waited for; matrix products, arithmetic and copies ran while one was open for 0% of the time, Pallas kernels for 12%

profile of v6, /device:TPU:0, one launch (start us, length us, event | category | flops | bytes accessed | tf_op | source)
XLA Modules:
  0.0 67.7 jit_solution(8590110244478553222)
XLA Ops:
  0.0 0.7 concatenate.10
  0.7 0.8 %maximum_multiply_fusion.refs_0_ = f32[32,256]{1,0:T(8,128)S(1)} fusion(f32[16,256]{1,0:T(8,128)} %bitcast.17, f32[16,256]{1,0:T(8,128)} %bitcast.18, f32[32]{0:T(128)S(1)} %concatenate.10), kind=kLoop, calls=%fused_computation.2 | loop fusion | flops 16384 | bytes 65664 | tf_op jit(solution)/shard_map/mul | solution.py:79
  1.5 0.0 collective-permute-start
  1.5 4.0 %collective-permute-start.4 = (f32[32,256]{1,0:T(8,128)S(1)}, f32[32,256]{1,0:T(8,128)S(1)}, u32[]{:S(2)}, u32[]{:S(2)}) collective-permute-start(f32[32,256]{1,0:T(8,128)S(1)} %maximum_multiply_fusion.refs_0_), channel_id=1, source_target_pairs={{0,4},{1,5},{2,6},{3,7},{4,0},{5,1},{6,2},{7,3},{8,12},{9,13},{10,... | collective-permute-start | bytes 98312 | tf_op jit(solution)/shard_map/ppermute | solution.py:27
  5.5 0.0 collective-permute-done
  5.5 1.6 %collective-permute-start.1 = (f32[64,256]{1,0:T(8,128)S(1)}, f32[64,256]{1,0:T(8,128)S(1)}, u32[]{:S(2)}, u32[]{:S(2)}) collective-permute-start(f32[64,256]{1,0:T(8,128)S(1)} %pad_maximum_fusion), channel_id=1, source_target_pairs={{0,8},{1,11},{2,10},{3,9},{4,12},{5,15},{6,14},{7,13},{8,0},{9,3},... | collective-permute-start | bytes 196616 | tf_op jit(solution)/shard_map/ppermute | solution.py:27
  7.0 1.0 %collective-permute-start.2 = (f32[64,256]{1,0:T(8,128)S(1)}, f32[64,256]{1,0:T(8,128)S(1)}, u32[]{:S(2)}, u32[]{:S(2)}) collective-permute-start(f32[64,256]{1,0:T(8,128)S(1)} %pad_maximum_fusion), channel_id=1, source_target_pairs={{0,2},{1,15},{2,0},{3,13},{4,6},{5,11},{6,4},{7,9},{8,10},{9,7},{1... | collective-permute-start | bytes 196616 | tf_op jit(solution)/shard_map/ppermute | solution.py:27
  8.1 0.6 collective-permute-start.3
  8.7 0.0 copy-start.2
  8.7 0.0 copy-start
  8.7 2.0 %shard_map.73.x_ref = bf16[256,4096]{1,0:T(8,128)(2,1)S(1)} custom-call(bf16[256,4,8,128]{3,2,1,0:T(8,128)(2,1)} %bitcast.16), custom_call_target="tpu_custom_call" | custom-call | flops 1073741824 | tf_op jit(solution)/shard_map/pallas_call | solution.py:85
  10.7 0.0 collective-permute-done.1.refs_2_
  10.7 0.6 collective-permute-done.2.refs_3_
  11.3 2.9 %collective-permute-done.3.refs_4_ = f32[64,256]{1,0:T(8,128)S(1)} collective-permute-done((f32[64,256]{1,0:T(8,128)S(1)}, f32[64,256]{1,0:T(8,128)S(1)}, u32[]{:S(2)}, u32[]{:S(2)}) %collective-permute-start.3) | collective-permute-done | bytes 65568 | tf_op jit(solution)/shard_map/ppermute | solution.py:27
  14.2 0.0 collective-permute-done.4.refs_1_
  14.2 0.4 shard_map.74
  14.6 0.1 collective-permute-start.5
  14.7 1.5 %collective-permute-done.5 = f32[256,256]{1,0:T(8,128)S(1)} collective-permute-done((f32[256,256]{1,0:T(8,128)S(1)}, f32[256,256]{1,0:T(8,128)S(1)}, u32[]{:S(2)}, u32[]{:S(2)}) %collective-permute-start.5) | collective-permute-done | bytes 262176 | tf_op jit(solution)/shard_map/ppermute | solution.py:27
  16.3 2.8 %collective-permute-start.6 = (bf16[256,256]{1,0:T(8,128)(2,1)S(1)}, bf16[256,256]{1,0:T(8,128)(2,1)S(1)}, u32[]{:S(2)}, u32[]{:S(2)}) collective-permute-start(bf16[256,256]{1,0:T(8,128)(2,1)S(1)} %add_convert_fusion.refs_0_.refs_4_), channel_id=1, source_target_pairs={{0,16},{1,49},{2,18},{3,51},{4,20},{5,53},{6,22},{7,55},{8,24},{9,... | collective-permute-start | bytes 393224 | tf_op jit(solution)/shard_map/ppermute | solution.py:27
  19.1 0.0 copy-done.2
  19.1 0.1 reshape.16
  19.2 1.6 %collective-permute-start.7 = (bf16[256,256]{1,0:T(8,128)(2,1)S(1)}, bf16[256,256]{1,0:T(8,128)(2,1)S(1)}, u32[]{:S(2)}, u32[]{:S(2)}) collective-permute-start(bf16[256,256]{1,0:T(8,128)(2,1)S(1)} %add_convert_fusion.refs_0_.refs_4_), channel_id=1, source_target_pairs={{0,32},{1,113},{2,34},{3,115},{4,36},{5,117},{6,38},{7,119},{8,40}... | collective-permute-start | bytes 393224 | tf_op jit(solution)/shard_map/ppermute | solution.py:27
  20.8 2.2 %collective-permute-start.8 = (bf16[256,256]{1,0:T(8,128)(2,1)S(1)}, bf16[256,256]{1,0:T(8,128)(2,1)S(1)}, u32[]{:S(2)}, u32[]{:S(2)}) collective-permute-start(bf16[256,256]{1,0:T(8,128)(2,1)S(1)} %add_convert_fusion.refs_0_.refs_4_), channel_id=1, source_target_pairs={{0,96},{1,81},{2,98},{3,83},{4,100},{5,85},{6,102},{7,87},{8,104},... | collective-permute-start | bytes 393224 | tf_op jit(solution)/shard_map/ppermute | solution.py:27
  23.0 0.8 %collective-permute-start.9 = (bf16[128,256]{1,0:T(8,128)(2,1)S(1)}, bf16[128,256]{1,0:T(8,128)(2,1)S(1)}, u32[]{:S(2)}, u32[]{:S(2)}) collective-permute-start(bf16[128,256]{1,0:T(8,128)(2,1)S(1)} %constant_dynamic-slice_fusion), channel_id=1, source_target_pairs={{0,64},{1,65},{2,66},{3,67},{4,68},{5,69},{6,70},{7,71},{8,72},{9,... | collective-permute-start | bytes 196616 | tf_op jit(solution)/shard_map/ppermute | solution.py:27
  23.8 0.3 collective-permute-done.6.refs_1_.refs_5_
  24.1 0.0 copy-done
  24.1 2.2 %shard_map.75 = (bf16[256,4096]{1,0:T(8,128)(2,1)S(1)}, bf16[64,512]{1,0:T(8,128)(2,1)S(1)}, bf16[64,512]{1,0:T(8,128)(2,1)S(1)}, bf16[128,128]{1,0:T(8,128)(2,1...) custom-call(bf16[256,4096]{1,0:T(8,128)(2,1)S(1)} %shard_map.73.x_ref, s32[1,1024]{1,0:T(1,128)S(1)} %bitcast.11, ...), custom_call_target="tpu_custom_call" | custom-call | flops 1431655808 | tf_op jit(solution)/shard_map/pallas_call | solution.py:66
  26.3 4.2 %collective-permute-done.9.refs_4_.refs_12_ = bf16[128,256]{1,0:T(8,128)(2,1)S(1)} collective-permute-done((bf16[128,256]{1,0:T(8,128)(2,1)S(1)}, bf16[128,256]{1,0:T(8,128)(2,1)S(1)}, u32[]{:S(2)}, u32[]{:S(2)}) %collective-permute-start.9) | collective-permute-done | bytes 65568 | tf_op jit(solution)/shard_map/ppermute | solution.py:27
  30.5 0.0 collective-permute-done.7.refs_0_.refs_6_
  30.5 0.7 %collective-permute-done.8.refs_1_.refs_7_ = bf16[256,256]{1,0:T(8,128)(2,1)S(1)} collective-permute-done((bf16[256,256]{1,0:T(8,128)(2,1)S(1)}, bf16[256,256]{1,0:T(8,128)(2,1)S(1)}, u32[]{:S(2)}, u32[]{:S(2)}) %collective-permute-start.8) | collective-permute-done | bytes 131104 | tf_op jit(solution)/shard_map/ppermute | solution.py:27
  31.2 0.0 collective-permute-start.11
  31.2 0.5 collective-permute-start.12
  31.7 0.0 collective-permute-start.13
  31.7 0.5 collective-permute-start.10
  32.2 1.5 %shard_map.76 = (bf16[256,4096]{1,0:T(8,128)(2,1)S(1)}, bf16[64,512]{1,0:T(8,128)(2,1)S(1)}, bf16[64,512]{1,0:T(8,128)(2,1)S(1)}, bf16[128,128]{1,0:T(8,128)(2,1)S(1)}) custom-call(bf16[256,4096]{1,0:T(8,128)(2,1)S(1)} %shard_map.73.x_ref, s32[1,1024]{1,0:T(1,128)S(1)} %bitcast.12, bf16[256,256]{1,0:T(8,128)(2,1)S(1)} %collective-permute-done.7.refs_0_.refs_6_, ...), custom_call_target="tpu_custom_call" | custom-call | flops 1431655808 | tf_op jit(solution)/shard_map/pallas_call | solution.py:66
  33.8 0.0 collective-permute-done.13.refs_3_.refs_11_
  33.8 0.0 collective-permute-done.11.refs_1_.refs_9_
  33.8 0.0 collective-permute-done.12.refs_2_.refs_10_
  33.8 0.0 collective-permute-done.10.refs_0_.refs_8_
  33.8 0.6 shard_map.78
  34.5 1.1 %collective-permute-start.14 = (bf16[64,512]{1,0:T(8,128)(2,1)S(1)}, bf16[64,512]{1,0:T(8,128)(2,1)S(1)}, u32[]{:S(2)}, u32[]{:S(2)}) collective-permute-start(bf16[64,512]{1,0:T(8,128)(2,1)S(1)} %get-tuple-element.60), channel_id=1, source_target_pairs={{0,16},{16,32},{32,48},{48,64},{64,80},{80,96},{96,112},{112,0},{1... | collective-permute-start | bytes 196616 | tf_op jit(solution)/shard_map/ppermute | solution.py:382
  35.5 4.7 %collective-permute-start.15 = (bf16[64,512]{1,0:T(8,128)(2,1)S(1)}, bf16[64,512]{1,0:T(8,128)(2,1)S(1)}, u32[]{:S(2)}, u32[]{:S(2)}) collective-permute-start(bf16[64,512]{1,0:T(8,128)(2,1)S(1)} %get-tuple-element.61), channel_id=1, source_target_pairs={{0,112},{16,0},{32,16},{48,32},{64,48},{80,64},{96,80},{112,96},{1... | collective-permute-start | bytes 196616 | tf_op jit(solution)/shard_map/ppermute | solution.py:382
  40.2 0.0 collective-permute-start.16
  40.2 3.9 %collective-permute-start.17 = (bf16[64,128]{1,0:T(8,128)(2,1)S(1)}, bf16[64,128]{1,0:T(8,128)(2,1)S(1)}, u32[]{:S(2)}, u32[]{:S(2)}) collective-permute-start(bf16[64,128]{1,0:T(8,128)(2,1)S(1)} %get-tuple-element.63), channel_id=1, source_target_pairs={{0,15},{1,0},{2,1},{3,2},{4,3},{5,4},{6,5},{7,6},{8,7},{9,8},{10,9... | collective-permute-start | bytes 49160 | tf_op jit(solution)/shard_map/ppermute | solution.py:382
  44.0 0.0 copy-start.1
  44.0 2.5 %shard_map.77.x_ref = bf16[256,4096]{1,0:T(8,128)(2,1)S(1)} custom-call(bf16[256,4096]{1,0:T(8,128)(2,1)S(1)} %shard_map.73.x_ref, s32[1,1024]{1,0:T(1,128)S(1)} %bitcast.14, bf16[256,4096]{1,0:T(8,128)(2,1)S(1)} %get-tuple-element.55.done_ref, bf16[256,256]{1,0:T(8,128)(2,1)S(1)} %collective-permute-done.10.refs_0_.refs_8_, ...), custom_call_target="tpu_custom_call" | custom-call | flops 2147483648 | tf_op jit(solution)/shard_map/pallas_call | solution.py:66
  46.5 0.0 collective-permute-done.16.refs_2_
  46.6 0.0 collective-permute-done.17.refs_3_
  46.6 0.0 collective-permute-done.14.refs_0_
  46.6 0.0 collective-permute-done.15.refs_1_
  46.6 0.2 broadcast_in_dim.2.profile_ref
  46.8 0.0 copy-done.1
  46.8 6.7 %shard_map.79 = (bf16[256,4096]{1,0:T(8,128)(2,1)S(1)}, bf16[64,512]{1,0:T(8,128)(2,1)S(1)}, bf16[64,512]{1,0:T(8,128)(2,1)S(1)}, bf16[64,128]{1,0:T(8,128)(2,1)S(1)}, bf16[64,128]{1,0:T(8,128)(2,1)S(1)}) custom-call(s32[4]{0:T(128)S(1)} %copy-done.1, bf16[256,4096]{1,0:T(8,128)(2,1)S(1)} %shard_map.77.x_ref, s32[1,1024]{1,0:T(1,128)S(1)} %bitcast.15, ...), custom_call_target="tpu_custom_call" | custom-call | flops 4294967296 | tf_op jit(solution)/shard_map/pallas_call | solution.py:466
  53.5 0.1 collective-permute-start.18
  53.6 5.6 %collective-permute-start.19 = (bf16[64,512]{1,0:T(8,128)(2,1)S(1)}, bf16[64,512]{1,0:T(8,128)(2,1)S(1)}, u32[]{:S(2)}, u32[]{:S(2)}) collective-permute-start(bf16[64,512]{1,0:T(8,128)(2,1)S(1)} %get-tuple-element.66), channel_id=1, source_target_pairs={{0,112},{16,0},{32,16},{48,32},{64,48},{80,64},{96,80},{112,96},{1... | collective-permute-start | bytes 196616 | tf_op jit(solution)/shard_map/ppermute | solution.py:382
  59.2 0.0 collective-permute-start.20
  59.2 3.9 %collective-permute-start.21 = (bf16[64,128]{1,0:T(8,128)(2,1)S(1)}, bf16[64,128]{1,0:T(8,128)(2,1)S(1)}, u32[]{:S(2)}, u32[]{:S(2)}) collective-permute-start(bf16[64,128]{1,0:T(8,128)(2,1)S(1)} %get-tuple-element.68), channel_id=1, source_target_pairs={{0,15},{1,0},{2,1},{3,2},{4,3},{5,4},{6,5},{7,6},{8,7},{9,8},{10,9... | collective-permute-start | bytes 49160 | tf_op jit(solution)/shard_map/ppermute | solution.py:382
  63.0 1.4 %collective-permute-done.20.refs_2_ = bf16[64,128]{1,0:T(8,128)(2,1)S(1)} collective-permute-done((bf16[64,128]{1,0:T(8,128)(2,1)S(1)}, bf16[64,128]{1,0:T(8,128)(2,1)S(1)}, u32[]{:S(2)}, u32[]{:S(2)}) %collective-permute-start.20) | collective-permute-done | bytes 16416 | tf_op jit(solution)/shard_map/ppermute | solution.py:382
  64.5 0.0 collective-permute-done.21.refs_3_
  64.5 0.0 collective-permute-done.18.refs_0_
  64.5 0.0 collective-permute-done.19.refs_1_
  64.5 3.1 %shard_map.80 = bf16[256,4,8,128]{3,2,1,0:T(8,128)(2,1)} custom-call(s32[4]{0:T(128)S(1)} %copy-done.1, bf16[256,4096]{1,0:T(8,128)(2,1)S(1)} %get-tuple-element.64.x_ref, bf16[4,256,128]{2,1,0:T(8,128)(2,1)S(1)} %broadcast_in_dim.2.profile_ref, bf16[64,512]{1,0:T(8,128)(2,1)S(1)} %collective-permute-done.18.refs_0_, ...), custom_call_target="tpu_custom_call" | custom-call | tf_op jit(solution)/shard_map/pallas_call | solution.py:476
  (4 shorter events, 0.1 us)
Async XLA Ops:
  1.5 4.0 %collective-permute-start = (f32[32,256]{1,0:T(8,128)S(1)}, f32[32,256]{1,0:T(8,128)S(1)}, u32[]{:S(2)}, u32[]{:S(2)}) collective-permute-start(f32[32,256]{1,0:T(8,128)S(1)} %maximum_multiply_fusion.refs_0_), channel_id=1, source_target_pairs={{0,1},{1,0},{2,3},{3,2},{4,5},{5,4},{6,7},{7,6},{8,9},{9,8},{10,11... | collective-permute-start | bytes 98312 | tf_op jit(solution)/shard_map/ppermute | solution.py:27
  1.5 12.8 %collective-permute-start.4 = (f32[32,256]{1,0:T(8,128)S(1)}, f32[32,256]{1,0:T(8,128)S(1)}, u32[]{:S(2)}, u32[]{:S(2)}) collective-permute-start(f32[32,256]{1,0:T(8,128)S(1)} %maximum_multiply_fusion.refs_0_), channel_id=1, source_target_pairs={{0,4},{1,5},{2,6},{3,7},{4,0},{5,1},{6,2},{7,3},{8,12},{9,13},{10,... | collective-permute-start | bytes 98312 | tf_op jit(solution)/shard_map/ppermute | solution.py:27
  5.5 5.2 %collective-permute-start.1 = (f32[64,256]{1,0:T(8,128)S(1)}, f32[64,256]{1,0:T(8,128)S(1)}, u32[]{:S(2)}, u32[]{:S(2)}) collective-permute-start(f32[64,256]{1,0:T(8,128)S(1)} %pad_maximum_fusion), channel_id=1, source_target_pairs={{0,8},{1,11},{2,10},{3,9},{4,12},{5,15},{6,14},{7,13},{8,0},{9,3},... | collective-permute-start | bytes 196616 | tf_op jit(solution)/shard_map/ppermute | solution.py:27
  7.0 4.3 %collective-permute-start.2 = (f32[64,256]{1,0:T(8,128)S(1)}, f32[64,256]{1,0:T(8,128)S(1)}, u32[]{:S(2)}, u32[]{:S(2)}) collective-permute-start(f32[64,256]{1,0:T(8,128)S(1)} %pad_maximum_fusion), channel_id=1, source_target_pairs={{0,2},{1,15},{2,0},{3,13},{4,6},{5,11},{6,4},{7,9},{8,10},{9,7},{1... | collective-permute-start | bytes 196616 | tf_op jit(solution)/shard_map/ppermute | solution.py:27
  8.1 6.2 %collective-permute-start.3 = (f32[64,256]{1,0:T(8,128)S(1)}, f32[64,256]{1,0:T(8,128)S(1)}, u32[]{:S(2)}, u32[]{:S(2)}) collective-permute-start(f32[64,256]{1,0:T(8,128)S(1)} %pad_maximum_fusion), channel_id=1, source_target_pairs={{0,6},{1,13},{2,4},{3,15},{4,2},{5,9},{6,0},{7,11},{8,14},{9,5},{1... | collective-permute-start | bytes 196616 | tf_op jit(solution)/shard_map/ppermute | solution.py:27
  8.7 10.4 %copy-start.2 = (bf16[4,64,4]{1,2,0:T(4,128)(2,1)S(1)}, bf16[4,64,4]{1,2,0:T(4,128)(2,1)}, u32[]{:S(2)}) copy-start(bf16[4,64,4]{1,2,0:T(4,128)(2,1)} %param.10) | copy-start | bytes 6148
  8.7 15.4 %copy-start = (s32[8,128]{1,0:T(8,128)S(1)}, s32[8,128]{1,0:T(8,128)}, u32[]{:S(2)}) copy-start(s32[8,128]{1,0:T(8,128)} %param.8) | copy-start | bytes 12292
  14.6 1.6 %collective-permute-start.5 = (f32[256,256]{1,0:T(8,128)S(1)}, f32[256,256]{1,0:T(8,128)S(1)}, u32[]{:S(2)}, u32[]{:S(2)}) collective-permute-start(f32[256,256]{1,0:T(8,128)S(1)} %shard_map.74), channel_id=1, source_target_pairs={{0,1},{1,0},{2,3},{3,2},{4,5},{5,4},{6,7},{7,6},{8,9},{9,8},{10,11... | collective-permute-start | bytes 786440 | tf_op jit(solution)/shard_map/ppermute | solution.py:27
  16.3 7.8 %collective-permute-start.6 = (bf16[256,256]{1,0:T(8,128)(2,1)S(1)}, bf16[256,256]{1,0:T(8,128)(2,1)S(1)}, u32[]{:S(2)}, u32[]{:S(2)}) collective-permute-start(bf16[256,256]{1,0:T(8,128)(2,1)S(1)} %add_convert_fusion.refs_0_.refs_4_), channel_id=1, source_target_pairs={{0,16},{1,49},{2,18},{3,51},{4,20},{5,53},{6,22},{7,55},{8,24},{9,... | collective-permute-start | bytes 393224 | tf_op jit(solution)/shard_map/ppermute | solution.py:27
  19.2 11.3 %collective-permute-start.7 = (bf16[256,256]{1,0:T(8,128)(2,1)S(1)}, bf16[256,256]{1,0:T(8,128)(2,1)S(1)}, u32[]{:S(2)}, u32[]{:S(2)}) collective-permute-start(bf16[256,256]{1,0:T(8,128)(2,1)S(1)} %add_convert_fusion.refs_0_.refs_4_), channel_id=1, source_target_pairs={{0,32},{1,113},{2,34},{3,115},{4,36},{5,117},{6,38},{7,119},{8,40}... | collective-permute-start | bytes 393224 | tf_op jit(solution)/shard_map/ppermute | solution.py:27
  20.8 10.4 %collective-permute-start.8 = (bf16[256,256]{1,0:T(8,128)(2,1)S(1)}, bf16[256,256]{1,0:T(8,128)(2,1)S(1)}, u32[]{:S(2)}, u32[]{:S(2)}) collective-permute-start(bf16[256,256]{1,0:T(8,128)(2,1)S(1)} %add_convert_fusion.refs_0_.refs_4_), channel_id=1, source_target_pairs={{0,96},{1,81},{2,98},{3,83},{4,100},{5,85},{6,102},{7,87},{8,104},... | collective-permute-start | bytes 393224 | tf_op jit(solution)/shard_map/ppermute | solution.py:27
  23.0 7.5 %collective-permute-start.9 = (bf16[128,256]{1,0:T(8,128)(2,1)S(1)}, bf16[128,256]{1,0:T(8,128)(2,1)S(1)}, u32[]{:S(2)}, u32[]{:S(2)}) collective-permute-start(bf16[128,256]{1,0:T(8,128)(2,1)S(1)} %constant_dynamic-slice_fusion), channel_id=1, source_target_pairs={{0,64},{1,65},{2,66},{3,67},{4,68},{5,69},{6,70},{7,71},{8,72},{9,... | collective-permute-start | bytes 196616 | tf_op jit(solution)/shard_map/ppermute | solution.py:27
  31.2 2.6 %collective-permute-start.11 = (bf16[256,256]{1,0:T(8,128)(2,1)S(1)}, bf16[256,256]{1,0:T(8,128)(2,1)S(1)}, u32[]{:S(2)}, u32[]{:S(2)}) collective-permute-start(bf16[256,256]{1,0:T(8,128)(2,1)S(1)} %collective-permute-done.7.refs_0_.refs_6_), channel_id=1, source_target_pairs={{0,1},{1,0},{2,3},{3,2},{4,5},{5,4},{6,7},{7,6},{8,9},{9,8},{10,11... | collective-permute-start | bytes 393224 | tf_op jit(solution)/shard_map/ppermute | solution.py:27
  31.2 2.6 %collective-permute-start.12 = (bf16[256,256]{1,0:T(8,128)(2,1)S(1)}, bf16[256,256]{1,0:T(8,128)(2,1)S(1)}, u32[]{:S(2)}, u32[]{:S(2)}) collective-permute-start(bf16[256,256]{1,0:T(8,128)(2,1)S(1)} %collective-permute-done.8.refs_1_.refs_7_), channel_id=1, source_target_pairs={{0,1},{1,0},{2,3},{3,2},{4,5},{5,4},{6,7},{7,6},{8,9},{9,8},{10,11... | collective-permute-start | bytes 393224 | tf_op jit(solution)/shard_map/ppermute | solution.py:27
  31.7 2.1 %collective-permute-start.13 = (bf16[128,256]{1,0:T(8,128)(2,1)S(1)}, bf16[128,256]{1,0:T(8,128)(2,1)S(1)}, u32[]{:S(2)}, u32[]{:S(2)}) collective-permute-start(bf16[128,256]{1,0:T(8,128)(2,1)S(1)} %collective-permute-done.9.refs_4_.refs_12_), channel_id=1, source_target_pairs={{0,1},{1,0},{2,3},{3,2},{4,5},{5,4},{6,7},{7,6},{8,9},{9,8},{10,11... | collective-permute-start | bytes 196616 | tf_op jit(solution)/shard_map/ppermute | solution.py:27
  31.7 2.1 %collective-permute-start.10 = (bf16[256,256]{1,0:T(8,128)(2,1)S(1)}, bf16[256,256]{1,0:T(8,128)(2,1)S(1)}, u32[]{:S(2)}, u32[]{:S(2)}) collective-permute-start(bf16[256,256]{1,0:T(8,128)(2,1)S(1)} %collective-permute-done.6.refs_1_.refs_5_), channel_id=1, source_target_pairs={{0,1},{1,0},{2,3},{3,2},{4,5},{5,4},{6,7},{7,6},{8,9},{9,8},{10,11... | collective-permute-start | bytes 393224 | tf_op jit(solution)/shard_map/ppermute | solution.py:27
  34.5 12.1 %collective-permute-start.14 = (bf16[64,512]{1,0:T(8,128)(2,1)S(1)}, bf16[64,512]{1,0:T(8,128)(2,1)S(1)}, u32[]{:S(2)}, u32[]{:S(2)}) collective-permute-start(bf16[64,512]{1,0:T(8,128)(2,1)S(1)} %get-tuple-element.60), channel_id=1, source_target_pairs={{0,16},{16,32},{32,48},{48,64},{64,80},{80,96},{96,112},{112,0},{1... | collective-permute-start | bytes 196616 | tf_op jit(solution)/shard_map/ppermute | solution.py:382
  35.5 11.1 %collective-permute-start.15 = (bf16[64,512]{1,0:T(8,128)(2,1)S(1)}, bf16[64,512]{1,0:T(8,128)(2,1)S(1)}, u32[]{:S(2)}, u32[]{:S(2)}) collective-permute-start(bf16[64,512]{1,0:T(8,128)(2,1)S(1)} %get-tuple-element.61), channel_id=1, source_target_pairs={{0,112},{16,0},{32,16},{48,32},{64,48},{80,64},{96,80},{112,96},{1... | collective-permute-start | bytes 196616 | tf_op jit(solution)/shard_map/ppermute | solution.py:382
  40.2 6.4 %collective-permute-start.16 = (bf16[64,128]{1,0:T(8,128)(2,1)S(1)}, bf16[64,128]{1,0:T(8,128)(2,1)S(1)}, u32[]{:S(2)}, u32[]{:S(2)}) collective-permute-start(bf16[64,128]{1,0:T(8,128)(2,1)S(1)} %get-tuple-element.62), channel_id=1, source_target_pairs={{0,1},{1,2},{2,3},{3,4},{4,5},{5,6},{6,7},{7,8},{8,9},{9,10},{10,1... | collective-permute-start | bytes 49160 | tf_op jit(solution)/shard_map/ppermute | solution.py:382
  40.2 6.4 %collective-permute-start.17 = (bf16[64,128]{1,0:T(8,128)(2,1)S(1)}, bf16[64,128]{1,0:T(8,128)(2,1)S(1)}, u32[]{:S(2)}, u32[]{:S(2)}) collective-permute-start(bf16[64,128]{1,0:T(8,128)(2,1)S(1)} %get-tuple-element.63), channel_id=1, source_target_pairs={{0,15},{1,0},{2,1},{3,2},{4,3},{5,4},{6,5},{7,6},{8,7},{9,8},{10,9... | collective-permute-start | bytes 49160 | tf_op jit(solution)/shard_map/ppermute | solution.py:382
  44.0 2.8 %copy-start.1 = (s32[4]{0:T(128)S(1)}, s32[4]{0:T(128)}, u32[]{:S(2)}) copy-start(s32[4]{0:T(128)} %port_ref.3) | copy-start | bytes 52
  53.5 11.0 %collective-permute-start.18 = (bf16[64,512]{1,0:T(8,128)(2,1)S(1)}, bf16[64,512]{1,0:T(8,128)(2,1)S(1)}, u32[]{:S(2)}, u32[]{:S(2)}) collective-permute-start(bf16[64,512]{1,0:T(8,128)(2,1)S(1)} %get-tuple-element.65), channel_id=1, source_target_pairs={{0,16},{16,32},{32,48},{48,64},{64,80},{80,96},{96,112},{112,0},{1... | collective-permute-start | bytes 196616 | tf_op jit(solution)/shard_map/ppermute | solution.py:382
  53.6 10.9 %collective-permute-start.19 = (bf16[64,512]{1,0:T(8,128)(2,1)S(1)}, bf16[64,512]{1,0:T(8,128)(2,1)S(1)}, u32[]{:S(2)}, u32[]{:S(2)}) collective-permute-start(bf16[64,512]{1,0:T(8,128)(2,1)S(1)} %get-tuple-element.66), channel_id=1, source_target_pairs={{0,112},{16,0},{32,16},{48,32},{64,48},{80,64},{96,80},{112,96},{1... | collective-permute-start | bytes 196616 | tf_op jit(solution)/shard_map/ppermute | solution.py:382
  59.2 5.3 %collective-permute-start.20 = (bf16[64,128]{1,0:T(8,128)(2,1)S(1)}, bf16[64,128]{1,0:T(8,128)(2,1)S(1)}, u32[]{:S(2)}, u32[]{:S(2)}) collective-permute-start(bf16[64,128]{1,0:T(8,128)(2,1)S(1)} %get-tuple-element.67), channel_id=1, source_target_pairs={{0,1},{1,2},{2,3},{3,4},{4,5},{5,6},{6,7},{7,8},{8,9},{9,10},{10,1... | collective-permute-start | bytes 49160 | tf_op jit(solution)/shard_map/ppermute | solution.py:382
  59.2 5.3 %collective-permute-start.21 = (bf16[64,128]{1,0:T(8,128)(2,1)S(1)}, bf16[64,128]{1,0:T(8,128)(2,1)S(1)}, u32[]{:S(2)}, u32[]{:S(2)}) collective-permute-start(bf16[64,128]{1,0:T(8,128)(2,1)S(1)} %get-tuple-element.68), channel_id=1, source_target_pairs={{0,15},{1,0},{2,1},{3,2},{4,3},{5,4},{6,5},{7,6},{8,7},{9,8},{10,9... | collective-permute-start | bytes 49160 | tf_op jit(solution)/shard_map/ppermute | solution.py:382

commit v7 on v6

--- a/solution.py
+++ b/solution.py
@@ -76,7 +76,9 @@
 def own_type_map(mode_shapes, mode_values, mode_weights, traces):
     modes, order = mode_weights.shape[1:]
     own = jnp.concatenate([mode_shapes[0].T, mode_weights[0]], axis=0)
-    own = own * jnp.concatenate([mode_values[0], jnp.ones((modes,), F32)])[:, None]
+    values = jnp.broadcast_to(mode_values[0][None, :, None], (2, modes, order)).reshape(own.shape)
+    line = lax.broadcasted_iota(jnp.int32, own.shape, 0)
+    own = jnp.where(line < modes, own * values, own)
     far = swap(own, "col", 4)
     pair = jnp.concatenate([own, swap(own, "col", 1)], axis=0)
     pair, traces = lax.optimization_barrier((pair, traces))
@@ -105,16 +107,32 @@
 MAP_STEPS = ((0, 0), (1, 3), (2, 7), (6, 5), (3, 1), (7, 2), (5, 6), (4, 4))
 
 
+def even(axis):
+    return lax.rem(lax.axis_index(axis), 2) == 0
+
+
 def halos_inside(halo_refs):
-    north, south, west, east = (ref[...].astype(F32) for ref in halo_refs)
+    row_one, row_two, col_one, col_two = (ref[...].astype(F32) for ref in halo_refs)
     row, rows = lax.axis_index("row"), lax.axis_size("row")
     col, cols = lax.axis_index("col"), lax.axis_size("col")
+    north = jnp.where(even("row"), row_two, row_one)
+    south = jnp.where(even("row"), row_one, row_two)
+    west = jnp.where(even("col"), col_two, col_one)
+    east = jnp.where(even("col"), col_one, col_two)
     return (
         jnp.where(row > 0, north, 0.0),
         jnp.where(row < rows - 1, south, 0.0),
         jnp.where(col > 0, west, 0.0),
         jnp.where(col < cols - 1, east, 0.0),
     )
+
+
+def store_rims(out_refs, north, south, west, east):
+    first, second, third, fourth = out_refs
+    first[...] = jnp.where(even("row"), south, north).astype(BF)
+    second[...] = jnp.where(even("row"), north, south).astype(BF)
+    third[...] = jnp.where(even("col"), east, west).astype(BF)
+    fourth[...] = jnp.where(even("col"), west, east).astype(BF)
 
 
 def lane_of(value, lane):
@@ -256,10 +274,7 @@
         x_ref, types_ref[...].astype(F32), ports, sides[...], kinds[0:1, :], maps, so_far
     )
     quarter = x_ref.shape[0] // 4
-    refs[-4][...] = outs[0]
-    refs[-3][...] = outs[1]
-    refs[-2][...] = outs[2][0:quarter]
-    refs[-1][...] = outs[2][quarter:]
+    store_rims(refs[-4:], outs[0], outs[1], outs[2][0:quarter], outs[2][quarter:])
 
 
 def first_kernel(rows, ports, first, x_ref, types_ref, done_ref, *refs):
@@ -275,7 +290,7 @@
 
 def second_kernel(rows, width, port_ref, x_ref, types_ref, profile_ref, *refs):
     halo_refs, map_refs, next_ref = refs[:4], refs[4:-6], refs[-6]
-    north_out, south_out, west_out, east_out, blocks = refs[-5:]
+    rim_refs, blocks = refs[-5:-1], refs[-1]
     types = types_ref[...].astype(F32).astype(BF)
     tile = types.shape[1]
     order = x_ref.shape[0]
@@ -284,6 +299,7 @@
     north_in, south_in, west_in, east_in = halos_inside(halo_refs)
     lane = lax.broadcasted_iota(jnp.int32, (quarter, LANES), 1)
     west_rim = east_rim = jnp.zeros((quarter, LANES), F32)
+    north_rim, south_rim = [], []
     for port in range(x_ref.shape[1] // tile):
         own = slice(port * tile, (port + 1) * tile)
         rim = slice(port * LANES, (port + 1) * LANES)
@@ -312,16 +328,16 @@
 
         total = products(block[...], types, maps, 0, order)
         north, south = shifted(total, next_ref.at[:, own], rows)
-        north_out[:, rim] = north[:, 0:LANES]
-        south_out[:, rim] = south[:, tile - LANES :]
+        north_rim.append(north[:, 0:LANES])
+        south_rim.append(south[:, tile - LANES :])
         for row in range(rows):
             place = port * rows + row
             west = lane_of(total[2 * quarter : 3 * quarter], row * LANES)
             east = lane_of(total[3 * quarter :], (row + 1) * LANES - 1)
             west_rim = jnp.where(lane == place, west, west_rim)
             east_rim = jnp.where(lane == place, east, east_rim)
-    west_out[...] = west_rim.astype(BF)
-    east_out[...] = east_rim.astype(BF)
+    north_rim, south_rim = (jnp.concatenate(value, axis=1) for value in (north_rim, south_rim))
+    store_rims(rim_refs, north_rim, south_rim, west_rim, east_rim)
 
 
 def last_kernel(rows, width, port_ref, x_ref, profile_ref, *refs):
@@ -375,18 +391,13 @@
 
 
 def exchange(rims):
-    north, south, west, east = rims
-
-    def send(value, axis, step):
+    def pairs(axis, first):
         count = lax.axis_size(axis)
-        return lax.ppermute(value, axis, [(i, (i + step) % count) for i in range(count)])
-
-    return (
-        send(south, "row", 1),
-        send(north, "row", -1),
-        send(east, "col", 1),
-        send(west, "col", -1),
-    )
+        near = [(i, (i + 1) % count) for i in range(first, count, 2)]
+        return near + [(target, source) for source, target in near]
+
+    axes = (("row", 0), ("row", 1), ("col", 0), ("col", 1))
+    return [lax.ppermute(rim, axis, pairs(axis, first)) for rim, (axis, first) in zip(rims, axes)]
 
 
 def body(traces, cell_type, port_cell, port_profile, mode_shapes, mode_values, mode_weights):

time: 68 us -> 64 us (0.941)
  starting transfers between devices: 34.8 us -> 27 us
  waiting for transfers between devices: 11.7 us -> 15.4 us
    ppermute x8, starting transfers between devices: 19.1 us -> 11.3 us  [exchange(): lax.ppermute(rim, axis, pairs(axis, first))]
    ppermute x8, waiting for transfers between devices: 1.46 us -> 5.08 us  [exchange(): lax.ppermute(rim, axis, pairs(axis, first))]
    select_n x0 -> x1, other arithmetic: none -> 0.81 us  [own_type_map(): own = jnp.where(line < modes, own * values, own)]
    mul x1 -> x0, other arithmetic: 0.81 us -> none  [own_type_map(): own * jnp.concatenate([mode_values[0], jnp.ones((modes,), F32)])[:, None]]
    broadcast_in_dim x0 -> x2, local copies, waits for them, and re-layouts: none -> 0.74 us  [own_type_map(): jnp.broadcast_to(mode_values[0][None, :, None], (2, modes, order))]
  transfers between devices with their start and end apart: 22 -> 22, of which waited for: 7 -> 8; matrix products, arithmetic and copies ran while one was open for 0% -> 0% of each run, Pallas kernels for 12% -> 13%
where the time goes in v7:
time: 64 us; the launch traced here: 63.7 us
  starting transfers between devices  27 us (42%)
  Pallas kernels  19.1 us (30%)
  waiting for transfers between devices  15.4 us (24%)
  local copies, waits for them, and re-layouts  1.05 us (2%)
  other arithmetic  0.86 us (1%)
    ppermute x14, starting transfers between devices, swap(): return lax.ppermute(value, ('row', 'col'), pairs)  15.8 us
    ppermute x8, starting transfers between devices, exchange(): lax.ppermute(rim, axis, pairs(axis, first))  11.3 us
    ppermute x14, waiting for transfers between devices, swap(): return lax.ppermute(value, ('row', 'col'), pairs)  10.3 us
    pallas_call x5, Pallas kernels, whole_call(): pl.pallas_call(kernel, in_specs=[WHOLE] * len(operands), out_specs=[WHOLE...  7.27 us
    pallas_call x1, Pallas kernels, body(): pl.pallas_call(functools.partial(second_kernel, rows, width), in_specs=[p...  6.67 us
    ppermute x8, waiting for transfers between devices, exchange(): lax.ppermute(rim, axis, pairs(axis, first))  5.08 us
    pallas_call x1, Pallas kernels, body(): pl.pallas_call(functools.partial(last_kernel, rows, width), in_specs=[por...  3.11 us
    pallas_call x1, Pallas kernels, own_type_map(): pl.pallas_call(flat_kernel, in_specs=[pl.BlockSpec(memory_space=pltpu.HBM...  2 us
  transfers between devices with their start and end apart: 22, of which 8 were waited for; matrix products, arithmetic and copies ran while one was open for 0% of the time, Pallas kernels for 13%

profile of v7, /device:TPU:0, one launch (start us, length us, event | category | flops | bytes accessed | tf_op | source)
XLA Modules:
  0.0 63.7 jit_solution(8089103392325857582)
XLA Ops:
  0.0 0.7 %broadcast_in_dim.18 = f32[2,16]{1,0:T(2,128)S(1)} broadcast(f32[16]{0:T(128)} %bitcast.20), dimensions={1} | broadcast | bytes 192 | tf_op jit(solution)/shard_map/broadcast_in_dim | solution.py:79
  0.7 0.1 broadcast_in_dim.19
  0.7 0.8 %multiply_select_fusion.refs_0_ = f32[32,256]{1,0:T(8,128)S(1)} fusion(f32[16,256]{1,0:T(8,128)} %bitcast.17, f32[16,256]{1,0:T(8,128)} %bitcast.18, f32[32]{0:T(128)S(1)} %broadcast_in_dim.19, pred[32]{0:T(512)(128)(4,1)S(1)} %iota_compare_fusion), kind=kLoop, calls=%fused_computation.2 | loop fusion | flops 24576 | bytes 65696 | tf_op jit(solution)/shard_map/jit(_where)/select_n | solution.py:81
  1.6 0.0 collective-permute-start
  1.6 4.0 %collective-permute-start.4 = (f32[32,256]{1,0:T(8,128)S(1)}, f32[32,256]{1,0:T(8,128)S(1)}, u32[]{:S(2)}, u32[]{:S(2)}) collective-permute-start(f32[32,256]{1,0:T(8,128)S(1)} %multiply_select_fusion.refs_0_), channel_id=1, source_target_pairs={{0,4},{1,5},{2,6},{3,7},{4,0},{5,1},{6,2},{7,3},{8,12},{9,13},{10,... | collective-permute-start | bytes 98312 | tf_op jit(solution)/shard_map/ppermute | solution.py:27
  5.6 0.0 collective-permute-done
  5.7 1.6 %collective-permute-start.1 = (f32[64,256]{1,0:T(8,128)S(1)}, f32[64,256]{1,0:T(8,128)S(1)}, u32[]{:S(2)}, u32[]{:S(2)}) collective-permute-start(f32[64,256]{1,0:T(8,128)S(1)} %pad_maximum_fusion), channel_id=1, source_target_pairs={{0,8},{1,11},{2,10},{3,9},{4,12},{5,15},{6,14},{7,13},{8,0},{9,3},... | collective-permute-start | bytes 196616 | tf_op jit(solution)/shard_map/ppermute | solution.py:27
  7.2 1.0 %collective-permute-start.2 = (f32[64,256]{1,0:T(8,128)S(1)}, f32[64,256]{1,0:T(8,128)S(1)}, u32[]{:S(2)}, u32[]{:S(2)}) collective-permute-start(f32[64,256]{1,0:T(8,128)S(1)} %pad_maximum_fusion), channel_id=1, source_target_pairs={{0,2},{1,15},{2,0},{3,13},{4,6},{5,11},{6,4},{7,9},{8,10},{9,7},{1... | collective-permute-start | bytes 196616 | tf_op jit(solution)/shard_map/ppermute | solution.py:27
  8.2 0.6 collective-permute-start.3
  8.8 0.0 copy-start.2
  8.8 0.0 copy-start
  8.8 2.0 %shard_map.73.x_ref = bf16[256,4096]{1,0:T(8,128)(2,1)S(1)} custom-call(bf16[256,4,8,128]{3,2,1,0:T(8,128)(2,1)} %bitcast.16), custom_call_target="tpu_custom_call" | custom-call | flops 1073741824 | tf_op jit(solution)/shard_map/pallas_call | solution.py:87
  10.8 0.0 collective-permute-done.1.refs_2_
  10.8 0.7 %collective-permute-done.2.refs_3_ = f32[64,256]{1,0:T(8,128)S(1)} collective-permute-done((f32[64,256]{1,0:T(8,128)S(1)}, f32[64,256]{1,0:T(8,128)S(1)}, u32[]{:S(2)}, u32[]{:S(2)}) %collective-permute-start.2) | collective-permute-done | bytes 65568 | tf_op jit(solution)/shard_map/ppermute | solution.py:27
  11.5 2.9 %collective-permute-done.3.refs_4_ = f32[64,256]{1,0:T(8,128)S(1)} collective-permute-done((f32[64,256]{1,0:T(8,128)S(1)}, f32[64,256]{1,0:T(8,128)S(1)}, u32[]{:S(2)}, u32[]{:S(2)}) %collective-permute-start.3) | collective-permute-done | bytes 65568 | tf_op jit(solution)/shard_map/ppermute | solution.py:27
  14.4 0.0 collective-permute-done.4.refs_1_
  14.4 0.4 shard_map.74
  14.8 0.1 collective-permute-start.5
  14.9 1.5 %collective-permute-done.5 = f32[256,256]{1,0:T(8,128)S(1)} collective-permute-done((f32[256,256]{1,0:T(8,128)S(1)}, f32[256,256]{1,0:T(8,128)S(1)}, u32[]{:S(2)}, u32[]{:S(2)}) %collective-permute-start.5) | collective-permute-done | bytes 262176 | tf_op jit(solution)/shard_map/ppermute | solution.py:27
  16.4 2.9 %collective-permute-start.6 = (bf16[256,256]{1,0:T(8,128)(2,1)S(1)}, bf16[256,256]{1,0:T(8,128)(2,1)S(1)}, u32[]{:S(2)}, u32[]{:S(2)}) collective-permute-start(bf16[256,256]{1,0:T(8,128)(2,1)S(1)} %add_convert_fusion.refs_0_.refs_4_), channel_id=1, source_target_pairs={{0,16},{1,49},{2,18},{3,51},{4,20},{5,53},{6,22},{7,55},{8,24},{9,... | collective-permute-start | bytes 393224 | tf_op jit(solution)/shard_map/ppermute | solution.py:27
  19.3 0.0 copy-done.2
  19.3 0.1 reshape.18
  19.4 1.6 %collective-permute-start.7 = (bf16[256,256]{1,0:T(8,128)(2,1)S(1)}, bf16[256,256]{1,0:T(8,128)(2,1)S(1)}, u32[]{:S(2)}, u32[]{:S(2)}) collective-permute-start(bf16[256,256]{1,0:T(8,128)(2,1)S(1)} %add_convert_fusion.refs_0_.refs_4_), channel_id=1, source_target_pairs={{0,32},{1,113},{2,34},{3,115},{4,36},{5,117},{6,38},{7,119},{8,40}... | collective-permute-start | bytes 393224 | tf_op jit(solution)/shard_map/ppermute | solution.py:27
  21.0 2.2 %collective-permute-start.8 = (bf16[256,256]{1,0:T(8,128)(2,1)S(1)}, bf16[256,256]{1,0:T(8,128)(2,1)S(1)}, u32[]{:S(2)}, u32[]{:S(2)}) collective-permute-start(bf16[256,256]{1,0:T(8,128)(2,1)S(1)} %add_convert_fusion.refs_0_.refs_4_), channel_id=1, source_target_pairs={{0,96},{1,81},{2,98},{3,83},{4,100},{5,85},{6,102},{7,87},{8,104},... | collective-permute-start | bytes 393224 | tf_op jit(solution)/shard_map/ppermute | solution.py:27
  23.2 0.8 %collective-permute-start.9 = (bf16[128,256]{1,0:T(8,128)(2,1)S(1)}, bf16[128,256]{1,0:T(8,128)(2,1)S(1)}, u32[]{:S(2)}, u32[]{:S(2)}) collective-permute-start(bf16[128,256]{1,0:T(8,128)(2,1)S(1)} %constant_dynamic-slice_fusion), channel_id=1, source_target_pairs={{0,64},{1,65},{2,66},{3,67},{4,68},{5,69},{6,70},{7,71},{8,72},{9,... | collective-permute-start | bytes 196616 | tf_op jit(solution)/shard_map/ppermute | solution.py:27
  24.0 0.2 collective-permute-done.6.refs_1_.refs_5_
  24.2 0.0 copy-done
  24.2 2.2 %shard_map.75 = (bf16[256,4096]{1,0:T(8,128)(2,1)S(1)}, bf16[64,512]{1,0:T(8,128)(2,1)S(1)}, bf16[64,512]{1,0:T(8,128)(2,1)S(1)}, bf16[128,128]{1,0:T(8,128)(2,1...) custom-call(bf16[256,4096]{1,0:T(8,128)(2,1)S(1)} %shard_map.73.x_ref, s32[1,1024]{1,0:T(1,128)S(1)} %bitcast.11, ...), custom_call_target="tpu_custom_call" | custom-call | flops 1431655808 | tf_op jit(solution)/shard_map/pallas_call | solution.py:66
  26.4 4.3 %collective-permute-done.9.refs_4_.refs_12_ = bf16[128,256]{1,0:T(8,128)(2,1)S(1)} collective-permute-done((bf16[128,256]{1,0:T(8,128)(2,1)S(1)}, bf16[128,256]{1,0:T(8,128)(2,1)S(1)}, u32[]{:S(2)}, u32[]{:S(2)}) %collective-permute-start.9) | collective-permute-done | bytes 65568 | tf_op jit(solution)/shard_map/ppermute | solution.py:27
  30.7 0.0 collective-permute-done.7.refs_0_.refs_6_
  30.7 0.7 %collective-permute-done.8.refs_1_.refs_7_ = bf16[256,256]{1,0:T(8,128)(2,1)S(1)} collective-permute-done((bf16[256,256]{1,0:T(8,128)(2,1)S(1)}, bf16[256,256]{1,0:T(8,128)(2,1)S(1)}, u32[]{:S(2)}, u32[]{:S(2)}) %collective-permute-start.8) | collective-permute-done | bytes 131104 | tf_op jit(solution)/shard_map/ppermute | solution.py:27
  31.4 0.0 collective-permute-start.11
  31.4 0.5 collective-permute-start.12
  31.9 0.0 collective-permute-start.13
  31.9 0.5 collective-permute-start.10
  32.4 1.5 %shard_map.76 = (bf16[256,4096]{1,0:T(8,128)(2,1)S(1)}, bf16[64,512]{1,0:T(8,128)(2,1)S(1)}, bf16[64,512]{1,0:T(8,128)(2,1)S(1)}, bf16[128,128]{1,0:T(8,128)(2,1)S(1)}) custom-call(bf16[256,4096]{1,0:T(8,128)(2,1)S(1)} %shard_map.73.x_ref, s32[1,1024]{1,0:T(1,128)S(1)} %bitcast.12, bf16[256,256]{1,0:T(8,128)(2,1)S(1)} %collective-permute-done.7.refs_0_.refs_6_, ...), custom_call_target="tpu_custom_call" | custom-call | flops 1431655808 | tf_op jit(solution)/shard_map/pallas_call | solution.py:66
  34.0 0.0 collective-permute-done.13.refs_3_.refs_11_
  34.0 0.0 collective-permute-done.11.refs_1_.refs_9_
  34.0 0.0 collective-permute-done.12.refs_2_.refs_10_
  34.0 0.0 collective-permute-done.10.refs_0_.refs_8_
  34.0 0.6 shard_map.78
  34.6 1.1 %collective-permute-start.14 = (bf16[64,512]{1,0:T(8,128)(2,1)S(1)}, bf16[64,512]{1,0:T(8,128)(2,1)S(1)}, u32[]{:S(2)}, u32[]{:S(2)}) collective-permute-start(bf16[64,512]{1,0:T(8,128)(2,1)S(1)} %get-tuple-element.60), channel_id=1, source_target_pairs={{0,16},{32,48},{64,80},{96,112},{16,0},{48,32},{80,64},{112,96},{1... | collective-permute-start | bytes 196616 | tf_op jit(solution)/shard_map/ppermute | solution.py:400
  35.7 4.2 %collective-permute-start.15 = (bf16[64,512]{1,0:T(8,128)(2,1)S(1)}, bf16[64,512]{1,0:T(8,128)(2,1)S(1)}, u32[]{:S(2)}, u32[]{:S(2)}) collective-permute-start(bf16[64,512]{1,0:T(8,128)(2,1)S(1)} %get-tuple-element.61), channel_id=1, source_target_pairs={{16,32},{48,64},{80,96},{112,0},{32,16},{64,48},{96,80},{0,112},{1... | collective-permute-start | bytes 196616 | tf_op jit(solution)/shard_map/ppermute | solution.py:400
  39.9 0.0 collective-permute-start.16
  39.9 1.6 %collective-permute-start.17 = (bf16[64,128]{1,0:T(8,128)(2,1)S(1)}, bf16[64,128]{1,0:T(8,128)(2,1)S(1)}, u32[]{:S(2)}, u32[]{:S(2)}) collective-permute-start(bf16[64,128]{1,0:T(8,128)(2,1)S(1)} %get-tuple-element.63), channel_id=1, source_target_pairs={{1,2},{3,4},{5,6},{7,8},{9,10},{11,12},{13,14},{15,0},{2,1},{4,3},... | collective-permute-start | bytes 49160 | tf_op jit(solution)/shard_map/ppermute | solution.py:400
  41.5 0.0 copy-start.1
  41.5 2.5 %shard_map.77.x_ref = bf16[256,4096]{1,0:T(8,128)(2,1)S(1)} custom-call(bf16[256,4096]{1,0:T(8,128)(2,1)S(1)} %shard_map.73.x_ref, s32[1,1024]{1,0:T(1,128)S(1)} %bitcast.14, bf16[256,4096]{1,0:T(8,128)(2,1)S(1)} %get-tuple-element.55.done_ref, bf16[256,256]{1,0:T(8,128)(2,1)S(1)} %collective-permute-done.10.refs_0_.refs_8_, ...), custom_call_target="tpu_custom_call" | custom-call | flops 2147483648 | tf_op jit(solution)/shard_map/pallas_call | solution.py:66
  44.0 0.0 collective-permute-done.16.refs_2_
  44.1 1.1 %collective-permute-done.17.refs_3_ = bf16[64,128]{1,0:T(8,128)(2,1)S(1)} collective-permute-done((bf16[64,128]{1,0:T(8,128)(2,1)S(1)}, bf16[64,128]{1,0:T(8,128)(2,1)S(1)}, u32[]{:S(2)}, u32[]{:S(2)}) %collective-permute-start.17) | collective-permute-done | bytes 16416 | tf_op jit(solution)/shard_map/ppermute | solution.py:400
  45.1 0.0 collective-permute-done.14.refs_0_
  45.1 0.0 collective-permute-done.15.refs_1_
  45.1 0.2 broadcast_in_dim.21.profile_ref
  45.3 0.0 copy-done.1
  45.4 6.7 %shard_map.79 = (bf16[256,4096]{1,0:T(8,128)(2,1)S(1)}, bf16[64,512]{1,0:T(8,128)(2,1)S(1)}, bf16[64,512]{1,0:T(8,128)(2,1)S(1)}, bf16[64,128]{1,0:T(8,128)(2,1)S(1)}, bf16[64,128]{1,0:T(8,128)(2,1)S(1)}) custom-call(s32[4]{0:T(128)S(1)} %copy-done.1, bf16[256,4096]{1,0:T(8,128)(2,1)S(1)} %shard_map.77.x_ref, s32[1,1024]{1,0:T(1,128)S(1)} %bitcast.15, ...), custom_call_target="tpu_custom_call" | custom-call | flops 4294967296 | tf_op jit(solution)/shard_map/pallas_call | solution.py:477
  52.0 0.1 collective-permute-start.18
  52.1 3.0 %collective-permute-start.19 = (bf16[64,512]{1,0:T(8,128)(2,1)S(1)}, bf16[64,512]{1,0:T(8,128)(2,1)S(1)}, u32[]{:S(2)}, u32[]{:S(2)}) collective-permute-start(bf16[64,512]{1,0:T(8,128)(2,1)S(1)} %get-tuple-element.66), channel_id=1, source_target_pairs={{16,32},{48,64},{80,96},{112,0},{32,16},{64,48},{96,80},{0,112},{1... | collective-permute-start | bytes 196616 | tf_op jit(solution)/shard_map/ppermute | solution.py:400
  55.1 0.0 collective-permute-start.20
  55.1 1.3 %collective-permute-start.21 = (bf16[64,128]{1,0:T(8,128)(2,1)S(1)}, bf16[64,128]{1,0:T(8,128)(2,1)S(1)}, u32[]{:S(2)}, u32[]{:S(2)}) collective-permute-start(bf16[64,128]{1,0:T(8,128)(2,1)S(1)} %get-tuple-element.68), channel_id=1, source_target_pairs={{1,2},{3,4},{5,6},{7,8},{9,10},{11,12},{13,14},{15,0},{2,1},{4,3},... | collective-permute-start | bytes 49160 | tf_op jit(solution)/shard_map/ppermute | solution.py:400
  56.4 0.0 collective-permute-done.20.refs_2_
  56.4 4.0 %collective-permute-done.21.refs_3_ = bf16[64,128]{1,0:T(8,128)(2,1)S(1)} collective-permute-done((bf16[64,128]{1,0:T(8,128)(2,1)S(1)}, bf16[64,128]{1,0:T(8,128)(2,1)S(1)}, u32[]{:S(2)}, u32[]{:S(2)}) %collective-permute-start.21) | collective-permute-done | bytes 16416 | tf_op jit(solution)/shard_map/ppermute | solution.py:400
  60.4 0.0 collective-permute-done.18.refs_0_
  60.4 0.0 collective-permute-done.19.refs_1_
  60.4 3.1 %shard_map.80 = bf16[256,4,8,128]{3,2,1,0:T(8,128)(2,1)} custom-call(s32[4]{0:T(128)S(1)} %copy-done.1, bf16[256,4096]{1,0:T(8,128)(2,1)S(1)} %get-tuple-element.64.x_ref, bf16[4,256,128]{2,1,0:T(8,128)(2,1)S(1)} %broadcast_in_dim.21.profile_ref, bf16[64,512]{1,0:T(8,128)(2,1)S(1)} %collective-permute-done.18.refs_0_, ...), custom_call_target="tpu_custom_call" | custom-call | tf_op jit(solution)/shard_map/pallas_call | solution.py:487
  (5 shorter events, 0.1 us)
Async XLA Ops:
  1.6 4.1 %collective-permute-start = (f32[32,256]{1,0:T(8,128)S(1)}, f32[32,256]{1,0:T(8,128)S(1)}, u32[]{:S(2)}, u32[]{:S(2)}) collective-permute-start(f32[32,256]{1,0:T(8,128)S(1)} %multiply_select_fusion.refs_0_), channel_id=1, source_target_pairs={{0,1},{1,0},{2,3},{3,2},{4,5},{5,4},{6,7},{7,6},{8,9},{9,8},{10,11... | collective-permute-start | bytes 98312 | tf_op jit(solution)/shard_map/ppermute | solution.py:27
  1.6 12.8 %collective-permute-start.4 = (f32[32,256]{1,0:T(8,128)S(1)}, f32[32,256]{1,0:T(8,128)S(1)}, u32[]{:S(2)}, u32[]{:S(2)}) collective-permute-start(f32[32,256]{1,0:T(8,128)S(1)} %multiply_select_fusion.refs_0_), channel_id=1, source_target_pairs={{0,4},{1,5},{2,6},{3,7},{4,0},{5,1},{6,2},{7,3},{8,12},{9,13},{10,... | collective-permute-start | bytes 98312 | tf_op jit(solution)/shard_map/ppermute | solution.py:27
  5.7 5.2 %collective-permute-start.1 = (f32[64,256]{1,0:T(8,128)S(1)}, f32[64,256]{1,0:T(8,128)S(1)}, u32[]{:S(2)}, u32[]{:S(2)}) collective-permute-start(f32[64,256]{1,0:T(8,128)S(1)} %pad_maximum_fusion), channel_id=1, source_target_pairs={{0,8},{1,11},{2,10},{3,9},{4,12},{5,15},{6,14},{7,13},{8,0},{9,3},... | collective-permute-start | bytes 196616 | tf_op jit(solution)/shard_map/ppermute | solution.py:27
  7.2 4.3 %collective-permute-start.2 = (f32[64,256]{1,0:T(8,128)S(1)}, f32[64,256]{1,0:T(8,128)S(1)}, u32[]{:S(2)}, u32[]{:S(2)}) collective-permute-start(f32[64,256]{1,0:T(8,128)S(1)} %pad_maximum_fusion), channel_id=1, source_target_pairs={{0,2},{1,15},{2,0},{3,13},{4,6},{5,11},{6,4},{7,9},{8,10},{9,7},{1... | collective-permute-start | bytes 196616 | tf_op jit(solution)/shard_map/ppermute | solution.py:27
  8.2 6.1 %collective-permute-start.3 = (f32[64,256]{1,0:T(8,128)S(1)}, f32[64,256]{1,0:T(8,128)S(1)}, u32[]{:S(2)}, u32[]{:S(2)}) collective-permute-start(f32[64,256]{1,0:T(8,128)S(1)} %pad_maximum_fusion), channel_id=1, source_target_pairs={{0,6},{1,13},{2,4},{3,15},{4,2},{5,9},{6,0},{7,11},{8,14},{9,5},{1... | collective-permute-start | bytes 196616 | tf_op jit(solution)/shard_map/ppermute | solution.py:27
  8.8 10.5 %copy-start.2 = (bf16[4,64,4]{1,2,0:T(4,128)(2,1)S(1)}, bf16[4,64,4]{1,2,0:T(4,128)(2,1)}, u32[]{:S(2)}) copy-start(bf16[4,64,4]{1,2,0:T(4,128)(2,1)} %param.10) | copy-start | bytes 6148
  8.8 15.4 %copy-start = (s32[8,128]{1,0:T(8,128)S(1)}, s32[8,128]{1,0:T(8,128)}, u32[]{:S(2)}) copy-start(s32[8,128]{1,0:T(8,128)} %param.8) | copy-start | bytes 12292
  14.8 1.6 %collective-permute-start.5 = (f32[256,256]{1,0:T(8,128)S(1)}, f32[256,256]{1,0:T(8,128)S(1)}, u32[]{:S(2)}, u32[]{:S(2)}) collective-permute-start(f32[256,256]{1,0:T(8,128)S(1)} %shard_map.74), channel_id=1, source_target_pairs={{0,1},{1,0},{2,3},{3,2},{4,5},{5,4},{6,7},{7,6},{8,9},{9,8},{10,11... | collective-permute-start | bytes 786440 | tf_op jit(solution)/shard_map/ppermute | solution.py:27
  16.4 7.8 %collective-permute-start.6 = (bf16[256,256]{1,0:T(8,128)(2,1)S(1)}, bf16[256,256]{1,0:T(8,128)(2,1)S(1)}, u32[]{:S(2)}, u32[]{:S(2)}) collective-permute-start(bf16[256,256]{1,0:T(8,128)(2,1)S(1)} %add_convert_fusion.refs_0_.refs_4_), channel_id=1, source_target_pairs={{0,16},{1,49},{2,18},{3,51},{4,20},{5,53},{6,22},{7,55},{8,24},{9,... | collective-permute-start | bytes 393224 | tf_op jit(solution)/shard_map/ppermute | solution.py:27
  19.4 11.3 %collective-permute-start.7 = (bf16[256,256]{1,0:T(8,128)(2,1)S(1)}, bf16[256,256]{1,0:T(8,128)(2,1)S(1)}, u32[]{:S(2)}, u32[]{:S(2)}) collective-permute-start(bf16[256,256]{1,0:T(8,128)(2,1)S(1)} %add_convert_fusion.refs_0_.refs_4_), channel_id=1, source_target_pairs={{0,32},{1,113},{2,34},{3,115},{4,36},{5,117},{6,38},{7,119},{8,40}... | collective-permute-start | bytes 393224 | tf_op jit(solution)/shard_map/ppermute | solution.py:27
  21.0 10.4 %collective-permute-start.8 = (bf16[256,256]{1,0:T(8,128)(2,1)S(1)}, bf16[256,256]{1,0:T(8,128)(2,1)S(1)}, u32[]{:S(2)}, u32[]{:S(2)}) collective-permute-start(bf16[256,256]{1,0:T(8,128)(2,1)S(1)} %add_convert_fusion.refs_0_.refs_4_), channel_id=1, source_target_pairs={{0,96},{1,81},{2,98},{3,83},{4,100},{5,85},{6,102},{7,87},{8,104},... | collective-permute-start | bytes 393224 | tf_op jit(solution)/shard_map/ppermute | solution.py:27
  23.2 7.5 %collective-permute-start.9 = (bf16[128,256]{1,0:T(8,128)(2,1)S(1)}, bf16[128,256]{1,0:T(8,128)(2,1)S(1)}, u32[]{:S(2)}, u32[]{:S(2)}) collective-permute-start(bf16[128,256]{1,0:T(8,128)(2,1)S(1)} %constant_dynamic-slice_fusion), channel_id=1, source_target_pairs={{0,64},{1,65},{2,66},{3,67},{4,68},{5,69},{6,70},{7,71},{8,72},{9,... | collective-permute-start | bytes 196616 | tf_op jit(solution)/shard_map/ppermute | solution.py:27
  31.4 2.6 %collective-permute-start.11 = (bf16[256,256]{1,0:T(8,128)(2,1)S(1)}, bf16[256,256]{1,0:T(8,128)(2,1)S(1)}, u32[]{:S(2)}, u32[]{:S(2)}) collective-permute-start(bf16[256,256]{1,0:T(8,128)(2,1)S(1)} %collective-permute-done.7.refs_0_.refs_6_), channel_id=1, source_target_pairs={{0,1},{1,0},{2,3},{3,2},{4,5},{5,4},{6,7},{7,6},{8,9},{9,8},{10,11... | collective-permute-start | bytes 393224 | tf_op jit(solution)/shard_map/ppermute | solution.py:27
  31.4 2.6 %collective-permute-start.12 = (bf16[256,256]{1,0:T(8,128)(2,1)S(1)}, bf16[256,256]{1,0:T(8,128)(2,1)S(1)}, u32[]{:S(2)}, u32[]{:S(2)}) collective-permute-start(bf16[256,256]{1,0:T(8,128)(2,1)S(1)} %collective-permute-done.8.refs_1_.refs_7_), channel_id=1, source_target_pairs={{0,1},{1,0},{2,3},{3,2},{4,5},{5,4},{6,7},{7,6},{8,9},{9,8},{10,11... | collective-permute-start | bytes 393224 | tf_op jit(solution)/shard_map/ppermute | solution.py:27
  31.9 2.1 %collective-permute-start.13 = (bf16[128,256]{1,0:T(8,128)(2,1)S(1)}, bf16[128,256]{1,0:T(8,128)(2,1)S(1)}, u32[]{:S(2)}, u32[]{:S(2)}) collective-permute-start(bf16[128,256]{1,0:T(8,128)(2,1)S(1)} %collective-permute-done.9.refs_4_.refs_12_), channel_id=1, source_target_pairs={{0,1},{1,0},{2,3},{3,2},{4,5},{5,4},{6,7},{7,6},{8,9},{9,8},{10,11... | collective-permute-start | bytes 196616 | tf_op jit(solution)/shard_map/ppermute | solution.py:27
  31.9 2.1 %collective-permute-start.10 = (bf16[256,256]{1,0:T(8,128)(2,1)S(1)}, bf16[256,256]{1,0:T(8,128)(2,1)S(1)}, u32[]{:S(2)}, u32[]{:S(2)}) collective-permute-start(bf16[256,256]{1,0:T(8,128)(2,1)S(1)} %collective-permute-done.6.refs_1_.refs_5_), channel_id=1, source_target_pairs={{0,1},{1,0},{2,3},{3,2},{4,5},{5,4},{6,7},{7,6},{8,9},{9,8},{10,11... | collective-permute-start | bytes 393224 | tf_op jit(solution)/shard_map/ppermute | solution.py:27
  34.6 10.5 %collective-permute-start.14 = (bf16[64,512]{1,0:T(8,128)(2,1)S(1)}, bf16[64,512]{1,0:T(8,128)(2,1)S(1)}, u32[]{:S(2)}, u32[]{:S(2)}) collective-permute-start(bf16[64,512]{1,0:T(8,128)(2,1)S(1)} %get-tuple-element.60), channel_id=1, source_target_pairs={{0,16},{32,48},{64,80},{96,112},{16,0},{48,32},{80,64},{112,96},{1... | collective-permute-start | bytes 196616 | tf_op jit(solution)/shard_map/ppermute | solution.py:400
  35.7 9.4 %collective-permute-start.15 = (bf16[64,512]{1,0:T(8,128)(2,1)S(1)}, bf16[64,512]{1,0:T(8,128)(2,1)S(1)}, u32[]{:S(2)}, u32[]{:S(2)}) collective-permute-start(bf16[64,512]{1,0:T(8,128)(2,1)S(1)} %get-tuple-element.61), channel_id=1, source_target_pairs={{16,32},{48,64},{80,96},{112,0},{32,16},{64,48},{96,80},{0,112},{1... | collective-permute-start | bytes 196616 | tf_op jit(solution)/shard_map/ppermute | solution.py:400
  39.9 4.2 %collective-permute-start.16 = (bf16[64,128]{1,0:T(8,128)(2,1)S(1)}, bf16[64,128]{1,0:T(8,128)(2,1)S(1)}, u32[]{:S(2)}, u32[]{:S(2)}) collective-permute-start(bf16[64,128]{1,0:T(8,128)(2,1)S(1)} %get-tuple-element.62), channel_id=1, source_target_pairs={{0,1},{2,3},{4,5},{6,7},{8,9},{10,11},{12,13},{14,15},{1,0},{3,2},... | collective-permute-start | bytes 49160 | tf_op jit(solution)/shard_map/ppermute | solution.py:400
  39.9 5.3 %collective-permute-start.17 = (bf16[64,128]{1,0:T(8,128)(2,1)S(1)}, bf16[64,128]{1,0:T(8,128)(2,1)S(1)}, u32[]{:S(2)}, u32[]{:S(2)}) collective-permute-start(bf16[64,128]{1,0:T(8,128)(2,1)S(1)} %get-tuple-element.63), channel_id=1, source_target_pairs={{1,2},{3,4},{5,6},{7,8},{9,10},{11,12},{13,14},{15,0},{2,1},{4,3},... | collective-permute-start | bytes 49160 | tf_op jit(solution)/shard_map/ppermute | solution.py:400
  41.5 3.8 %copy-start.1 = (s32[4]{0:T(128)S(1)}, s32[4]{0:T(128)}, u32[]{:S(2)}) copy-start(s32[4]{0:T(128)} %port_ref.3) | copy-start | bytes 52
  52.0 8.4 %collective-permute-start.18 = (bf16[64,512]{1,0:T(8,128)(2,1)S(1)}, bf16[64,512]{1,0:T(8,128)(2,1)S(1)}, u32[]{:S(2)}, u32[]{:S(2)}) collective-permute-start(bf16[64,512]{1,0:T(8,128)(2,1)S(1)} %get-tuple-element.65), channel_id=1, source_target_pairs={{0,16},{32,48},{64,80},{96,112},{16,0},{48,32},{80,64},{112,96},{1... | collective-permute-start | bytes 196616 | tf_op jit(solution)/shard_map/ppermute | solution.py:400
  52.1 8.3 %collective-permute-start.19 = (bf16[64,512]{1,0:T(8,128)(2,1)S(1)}, bf16[64,512]{1,0:T(8,128)(2,1)S(1)}, u32[]{:S(2)}, u32[]{:S(2)}) collective-permute-start(bf16[64,512]{1,0:T(8,128)(2,1)S(1)} %get-tuple-element.66), channel_id=1, source_target_pairs={{16,32},{48,64},{80,96},{112,0},{32,16},{64,48},{96,80},{0,112},{1... | collective-permute-start | bytes 196616 | tf_op jit(solution)/shard_map/ppermute | solution.py:400
  55.1 1.3 %collective-permute-start.20 = (bf16[64,128]{1,0:T(8,128)(2,1)S(1)}, bf16[64,128]{1,0:T(8,128)(2,1)S(1)}, u32[]{:S(2)}, u32[]{:S(2)}) collective-permute-start(bf16[64,128]{1,0:T(8,128)(2,1)S(1)} %get-tuple-element.67), channel_id=1, source_target_pairs={{0,1},{2,3},{4,5},{6,7},{8,9},{10,11},{12,13},{14,15},{1,0},{3,2},... | collective-permute-start | bytes 49160 | tf_op jit(solution)/shard_map/ppermute | solution.py:400
  55.1 5.3 %collective-permute-start.21 = (bf16[64,128]{1,0:T(8,128)(2,1)S(1)}, bf16[64,128]{1,0:T(8,128)(2,1)S(1)}, u32[]{:S(2)}, u32[]{:S(2)}) collective-permute-start(bf16[64,128]{1,0:T(8,128)(2,1)S(1)} %get-tuple-element.68), channel_id=1, source_target_pairs={{1,2},{3,4},{5,6},{7,8},{9,10},{11,12},{13,14},{15,0},{2,1},{4,3},... | collective-permute-start | bytes 49160 | tf_op jit(solution)/shard_map/ppermute | solution.py:400

commit v8 on v7

--- a/solution.py
+++ b/solution.py
@@ -73,12 +73,11 @@
     )(*operands)
 
 
-def own_type_map(mode_shapes, mode_values, mode_weights, traces):
+def own_type_map(mode_shapes, mode_values, mode_weights, traces, types):
     modes, order = mode_weights.shape[1:]
-    own = jnp.concatenate([mode_shapes[0].T, mode_weights[0]], axis=0)
-    values = jnp.broadcast_to(mode_values[0][None, :, None], (2, modes, order)).reshape(own.shape)
-    line = lax.broadcasted_iota(jnp.int32, own.shape, 0)
-    own = jnp.where(line < modes, own * values, own)
+    scaled = mode_shapes[0].T * mode_values[0][:, None]
+    part = lax.broadcasted_iota(jnp.int32, (2, modes, order), 0)
+    own = jnp.where(part == 0, scaled[None], mode_weights).reshape(2 * modes, order)
     far = swap(own, "col", 4)
     pair = jnp.concatenate([own, swap(own, "col", 1)], axis=0)
     pair, traces = lax.optimization_barrier((pair, traces))
@@ -101,7 +100,17 @@
         far,
         *got,
     )
-    return (partial + swap(partial, "col", 1)).astype(BF), x
+    partial, x = lax.optimization_barrier((partial, x))
+    other = swap(partial, "col", 1)
+    sides = whole_call(
+        functools.partial(sides_kernel, traces.shape[2]),
+        [jax.ShapeDtypeStruct((order, LANES), BF), jax.ShapeDtypeStruct((16, LANES), BF)],
+        x,
+        types,
+        flops=2**30,
+    )
+    other, sides = lax.optimization_barrier((other, sides))
+    return (partial + other).astype(BF), x, sides
 
 
 MAP_STEPS = ((0, 0), (1, 3), (2, 7), (6, 5), (3, 1), (7, 2), (5, 6), (4, 4))
@@ -111,20 +120,12 @@
     return lax.rem(lax.axis_index(axis), 2) == 0
 
 
-def halos_inside(halo_refs):
-    row_one, row_two, col_one, col_two = (ref[...].astype(F32) for ref in halo_refs)
-    row, rows = lax.axis_index("row"), lax.axis_size("row")
-    col, cols = lax.axis_index("col"), lax.axis_size("col")
-    north = jnp.where(even("row"), row_two, row_one)
-    south = jnp.where(even("row"), row_one, row_two)
-    west = jnp.where(even("col"), col_two, col_one)
-    east = jnp.where(even("col"), col_one, col_two)
-    return (
-        jnp.where(row > 0, north, 0.0),
-        jnp.where(row < rows - 1, south, 0.0),
-        jnp.where(col > 0, west, 0.0),
-        jnp.where(col < cols - 1, east, 0.0),
-    )
+def halos_inside(axis, one, two):
+    one, two = one[...].astype(F32), two[...].astype(F32)
+    index, count = lax.axis_index(axis), lax.axis_size(axis)
+    low = jnp.where(even(axis), two, one)
+    high = jnp.where(even(axis), one, two)
+    return jnp.where(index > 0, low, 0.0), jnp.where(index < count - 1, high, 0.0)
 
 
 def store_rims(out_refs, north, south, west, east):
@@ -243,38 +244,32 @@
     return north.astype(BF), south.astype(BF), side.astype(BF)
 
 
-def early_kernel(ports, first, last, x_ref, types_ref, *refs):
+def sides_kernel(ports, x_ref, types_ref, sides_ref, kinds_ref):
+    sides_ref[...], kinds_ref[...] = side_columns(x_ref, types_ref[...].astype(F32), ports)
+
+
+def early_kernel(ports, first, last, x_ref, types_ref, sides_ref, kinds_ref, *refs):
     maps = with_steps(refs[: last - first], first, last)
-    refs = refs[last - first :]
     types = types_ref[...].astype(F32)
     tile = types.shape[1]
-    if first == 0:
-        done_ref, so_far = None, [None] * 3
-        sides, kinds = side_columns(x_ref, types, ports)
-        refs[4][...] = sides
-        refs[5][...] = kinds
-    else:
-        done_ref, so_far = refs[0], refs[1:4]
-        sides, kinds = refs[4][...], refs[5][...]
-        refs = refs[6:]
-    outs = rims(x_ref, types, ports, sides, kinds[0:1], maps, so_far)
-    for ref, value in zip(refs[1:4], outs):
+    so_far, outs = refs[last - first : -4], refs[-4:]
+    done_ref, *so_far = so_far if first else [None] * 4
+    values = rims(x_ref, types, ports, sides_ref[...], kinds_ref[0:1, :], maps, so_far)
+    for ref, value in zip(outs[1:], values):
         ref[...] = value
     for port in range(ports):
         cols = slice(port * tile, (port + 1) * tile)
         before = None if done_ref is None else done_ref[:, cols].astype(F32)
         total = products(x_ref[:, cols], types.astype(BF), maps, 0, x_ref.shape[0], before)
-        refs[0][:, cols] = total.astype(BF)
-
-
-def rim_kernel(ports, first, x_ref, types_ref, *refs):
-    maps = with_steps(refs[:-9], first, len(MAP_STEPS))
-    so_far, (sides, kinds) = refs[-9:-6], refs[-6:-4]
-    outs = rims(
-        x_ref, types_ref[...].astype(F32), ports, sides[...], kinds[0:1, :], maps, so_far
-    )
+        outs[0][:, cols] = total.astype(BF)
+
+
+def rim_kernel(ports, first, x_ref, types_ref, sides_ref, kinds_ref, *refs):
+    maps = with_steps(refs[:-7], first, len(MAP_STEPS))
+    types = types_ref[...].astype(F32)
     quarter = x_ref.shape[0] // 4
-    store_rims(refs[-4:], outs[0], outs[1], outs[2][0:quarter], outs[2][quarter:])
+    values = rims(x_ref, types, ports, sides_ref[...], kinds_ref[0:1, :], maps, refs[-7:-4])
+    store_rims(refs[-4:], values[0], values[1], values[2][0:quarter], values[2][quarter:])
 
 
 def first_kernel(rows, ports, first, x_ref, types_ref, done_ref, *refs):
@@ -296,7 +291,8 @@
     order = x_ref.shape[0]
     quarter = order // 4
     maps = with_steps(map_refs, 0, len(MAP_STEPS))
-    north_in, south_in, west_in, east_in = halos_inside(halo_refs)
+    north_in, south_in = halos_inside("row", *halo_refs[:2])
+    west_in, east_in = halos_inside("col", *halo_refs[2:])
     lane = lax.broadcasted_iota(jnp.int32, (quarter, LANES), 1)
     west_rim = east_rim = jnp.zeros((quarter, LANES), F32)
     north_rim, south_rim = [], []
@@ -340,50 +336,51 @@
     store_rims(rim_refs, north_rim, south_rim, west_rim, east_rim)
 
 
-def last_kernel(rows, width, port_ref, x_ref, profile_ref, *refs):
-    out_ref, buffer, sems = refs[4:]
-    order, ports = buffer.shape[:2]
-    quarter, tile = order // 4, rows * width
-    north_in, south_in, west_in, east_in = halos_inside(refs[:4])
+def last_kernel(rows, width, axis, port_ref, x_ref, profile_ref, one_ref, two_ref, *refs):
+    out_ref, buffer, sems = refs[-3:]
+    ports = buffer.shape[1]
+    quarter, tile = x_ref.shape[0] // 4, rows * width
+    low, high = halos_inside(axis, one_ref, two_ref)
     lane = lax.broadcasted_iota(jnp.int32, (quarter, LANES), 1)
     copies = []
-    for edge in (2, 3, 0, 1):
+    for edge in (0, 1) if axis == "row" else (2, 3):
         lines = slice(edge * quarter, (edge + 1) * quarter)
+        local = slice(edge % 2 * quarter, (edge % 2 + 1) * quarter)
         for port in range(ports):
             rim = slice(port * LANES, (port + 1) * LANES)
             starts = [port * tile + row * LANES for row in range(rows)]
             parts = [x_ref[lines, start : start + LANES].astype(F32) for start in starts]
             places = range(port * rows, (port + 1) * rows)
             if edge == 0:
-                parts[0] = north_in[:, rim]
+                parts[0] = low[:, rim]
             elif edge == 1:
-                parts[-1] = south_in[:, rim]
+                parts[-1] = high[:, rim]
             elif edge == 2:
                 parts = [
-                    jnp.where(lane == 0, lane_of(west_in, place), part)
+                    jnp.where(lane == 0, lane_of(low, place), part)
                     for place, part in zip(places, parts)
                 ]
             else:
                 parts = [
-                    jnp.where(lane == LANES - 1, lane_of(east_in, place), part)
+                    jnp.where(lane == LANES - 1, lane_of(high, place), part)
                     for place, part in zip(places, parts)
                 ]
             value = jnp.concatenate(parts, axis=1).reshape(quarter, rows, LANES)
-            buffer[lines, port] = value.astype(BF)
+            buffer[local, port] = value.astype(BF)
         for port in range(ports):
             row, col, inside = port_place(port_ref, port, rows, width)
 
             @pl.when(inside)
             def _():
-                current = buffer[lines, port].astype(F32)
+                current = buffer[local, port].astype(F32)
                 here = (lax.broadcasted_iota(jnp.int32, current.shape, 1) == row) & (
                     lax.broadcasted_iota(jnp.int32, current.shape, 2) == col
                 )
                 profile = profile_ref[port, lines, :].astype(F32).reshape(quarter, 1, LANES)
                 added = current + jnp.broadcast_to(profile, current.shape)
-                buffer[lines, port] = jnp.where(here, added, current).astype(BF)
-
-        copy = pltpu.make_async_copy(buffer.at[lines], out_ref.at[lines], sems.at[edge])
+                buffer[local, port] = jnp.where(here, added, current).astype(BF)
+
+        copy = pltpu.make_async_copy(buffer.at[local], out_ref.at[lines], sems.at[edge % 2])
         copy.start()
         copies.append(copy)
     for copy in copies:
@@ -405,13 +402,13 @@
     order = edges * samples
     quarter = samples
     tile = rows * width
-    own_map, x = own_type_map(mode_shapes, mode_values, mode_weights, traces)
+    types = cell_type.reshape(1, tile)
+    own_map, x, sides = own_type_map(mode_shapes, mode_values, mode_weights, traces, types)
     core = lax.rem(lax.axis_index("col"), 2)
     half = lax.dynamic_slice_in_dim(own_map, core * (order // 2), order // 2)
     fetched = [swap(own_map, "row", *steps) for steps in MAP_STEPS[1:4]]
     half = swap(half, "row", 4)
     swapped = [swap(fetched[0], "col", 1)]
-    types = cell_type.reshape(1, tile)
     profile = jnp.broadcast_to(
         jnp.transpose(port_profile.reshape(order, ports))[:, :, None], (ports, order, LANES)
     )
@@ -421,51 +418,38 @@
         jax.ShapeDtypeStruct((quarter, LANES), BF)
     ] * 2
     work = 2 * order * order * len(MAP_STEPS) * ports * tile
-    early = (0, 2, 4)
-    side_shapes = [
-        jax.ShapeDtypeStruct((order, LANES), BF),
-        jax.ShapeDtypeStruct((16, LANES), BF),
-    ]
     part_shapes = [next_shape] + rim_shapes[:2] + [jax.ShapeDtypeStruct((2 * quarter, LANES), BF)]
-    *parts, sides, kinds = whole_call(
-        functools.partial(early_kernel, ports, early[0], early[1]),
-        part_shapes + side_shapes,
-        x,
-        types,
-        own_map,
-        fetched[0],
-        flops=work // 3,
-    )
-    parts, rest, half = lax.optimization_barrier((parts, fetched[1:], half))
-    swapped += [swap(value, "col", 1) for value in rest + [half]]
-    parts = whole_call(
-        functools.partial(early_kernel, ports, early[1], early[2]),
-        part_shapes,
-        x,
-        types,
-        *rest,
-        *parts,
-        sides,
-        kinds,
-        flops=work // 3,
-    )
+
+    def early(first, maps, parts=()):
+        last = first + len(maps)
+        kernel = functools.partial(early_kernel, ports, first, last)
+        flops = work * len(maps) // 7
+        return whole_call(kernel, part_shapes, x, types, *sides, *maps, *parts, flops=flops)
+
+    parts = early(0, [own_map, fetched[0]])
+    parts, rest = lax.optimization_barrier((parts, fetched[1:]))
+    swapped += [swap(value, "col", 1) for value in rest]
+    parts = early(2, rest, parts)
+    parts, half = lax.optimization_barrier((parts, half))
+    swapped += [swap(half, "col", 1)]
+    parts = early(4, swapped[:1], parts)
+    parts, swapped[3] = lax.optimization_barrier((parts, swapped[3]))
     done, *parts = parts
-    late = swapped + [half]
-    maps = [own_map, fetched[0]] + rest + late
+    maps = [own_map, fetched[0]] + rest + swapped + [half]
+    late = maps[5:]
     sent = whole_call(
-        functools.partial(rim_kernel, ports, early[2]),
+        functools.partial(rim_kernel, ports, 5),
         rim_shapes,
         x,
         types,
+        *sides,
         *late,
         *parts,
-        sides,
-        kinds,
         flops=work // 8,
     )
     halos = exchange(sent)
     (x,) = whole_call(
-        functools.partial(first_kernel, rows, ports, early[2]),
+        functools.partial(first_kernel, rows, ports, 5),
         [next_shape],
         x,
         types,
@@ -483,19 +467,26 @@
         compiler_params=PARAMS,
         cost_estimate=pl.CostEstimate(flops=work, bytes_accessed=0, transcendentals=0),
     )(*operands)
-    operands = [port_cell, x, profile, *exchange(sent)]
-    out = pl.pallas_call(
-        functools.partial(last_kernel, rows, width),
-        in_specs=[ports_spec] + [WHOLE] * (len(operands) - 1),
-        out_specs=pl.BlockSpec(memory_space=pl.ANY),
-        out_shape=jax.ShapeDtypeStruct((order, ports, rows, width), BF),
-        scratch_shapes=[
-            pltpu.VMEM((order, ports, rows, width), BF),
-            pltpu.SemaphoreType.DMA((4,)),
-        ],
-        compiler_params=PARAMS,
-    )(*operands)
-    return out.reshape(traces.shape)
+    halos = exchange(sent)
+    out = []
+    for axis, pair in (("row", halos[:2]), ("col", halos[2:])):
+        operands = [port_cell, x, profile, *pair, *out]
+        out = [
+            pl.pallas_call(
+                functools.partial(last_kernel, rows, width, axis),
+                in_specs=[ports_spec] + [WHOLE] * 4 + [pl.BlockSpec(memory_space=pl.ANY)] * len(out),
+                out_specs=pl.BlockSpec(memory_space=pl.ANY),
+                out_shape=jax.ShapeDtypeStruct((order, ports, rows, width), BF),
+                scratch_shapes=[
+                    pltpu.VMEM((order // 2, ports, rows, width), BF),
+                    pltpu.SemaphoreType.DMA((2,)),
+                ],
+                input_output_aliases={5: 0} if out else {},
+                compiler_params=PARAMS,
+                cost_estimate=pl.CostEstimate(flops=2**30, bytes_accessed=0, transcendentals=0),
+            )(*operands)
+        ]
+    return out[0].reshape(traces.shape)
 
 
 def solution(mesh):

time: 64 us -> 68.2 us (1.066)
  waiting for transfers between devices: 15.4 us -> 11.7 us
  starting transfers between devices: 27 us -> 29.9 us
  local copies, waits for them, and re-layouts: 1.05 us -> 3.37 us
  Pallas kernels: 19.1 us -> 21 us
  other arithmetic: 0.86 us -> 1.62 us
    ppermute x14, waiting for transfers between devices: 10.3 us -> 6.49 us  [swap(): return lax.ppermute(value, ('row', 'col'), pairs)]
    unnamed x7 -> x11, local copies, waits for them, and re-layouts: 0.02 us -> 2.92 us
    ppermute x14, starting transfers between devices: 15.8 us -> 18.5 us  [swap(): return lax.ppermute(value, ('row', 'col'), pairs)]
    pallas_call x1 -> x2, Pallas kernels: 3.11 us -> 4.43 us  [body(): pl.pallas_call(functools.partial(last_kernel, rows, width, axis), in_spec...]
    mul x0 -> x1, other arithmetic: none -> 0.79 us  [own_type_map(): scaled = mode_shapes[0].T * mode_values[0][:, None]]
    broadcast_in_dim x2 -> x0, local copies, waits for them, and re-layouts: 0.74 us -> none  [own_type_map(): jnp.broadcast_to(mode_values[0][None, :, None], (2, modes, order))]
    pallas_call x5 -> x7, Pallas kernels: 7.27 us -> 7.94 us  [whole_call(): pl.pallas_call(kernel, in_specs=[WHOLE] * len(operands), out_specs=[WHOLE...]
  transfers between devices with their start and end apart: 22 -> 22, of which waited for: 8 -> 8; matrix products, arithmetic and copies ran while one was open for 0% -> 0% of each run, Pallas kernels for 13% -> 16%
where the time goes in v8:
time: 68.2 us; the launch traced here: 67.9 us
  starting transfers between devices  29.9 us (44%)
  Pallas kernels  21 us (31%)
  waiting for transfers between devices  11.7 us (17%)
  local copies, waits for them, and re-layouts  3.37 us (5%)
  other arithmetic  1.62 us (2%)
    ppermute x14, starting transfers between devices, swap(): return lax.ppermute(value, ('row', 'col'), pairs)  18.5 us
    ppermute x8, starting transfers between devices, exchange(): lax.ppermute(rim, axis, pairs(axis, first))  11.4 us
    pallas_call x7, Pallas kernels, whole_call(): pl.pallas_call(kernel, in_specs=[WHOLE] * len(operands), out_specs=[WHOLE...  7.94 us
    pallas_call x1, Pallas kernels, body(): pl.pallas_call(functools.partial(second_kernel, rows, width), in_specs=[p...  6.6 us
    ppermute x14, waiting for transfers between devices, swap(): return lax.ppermute(value, ('row', 'col'), pairs)  6.49 us
    ppermute x8, waiting for transfers between devices, exchange(): lax.ppermute(rim, axis, pairs(axis, first))  5.24 us
    pallas_call x2, Pallas kernels, body(): pl.pallas_call(functools.partial(last_kernel, rows, width, axis), in_spec...  4.43 us
    unnamed x11, local copies, waits for them, and re-layouts  2.92 us
  transfers between devices with their start and end apart: 22, of which 8 were waited for; matrix products, arithmetic and copies ran while one was open for 0% of the time, Pallas kernels for 16%

profile of v8, /device:TPU:0, one launch (start us, length us, event | category | flops | bytes accessed | tf_op | source)
XLA Modules:
  0.0 67.9 jit_solution(3571265536256445225)
XLA Ops:
  0.0 0.1 iota.11
  0.1 0.1 iota.12
  0.2 0.8 %fusion = f32[16,256]{1,0:T(8,128)S(1)} fusion(f32[1,256,16]{1,2,0:T(8,128)} %param.11, f32[16]{0:T(128)} %bitcast.28), kind=kLoop, calls=%fused_computation.4 | loop fusion | flops 4096 | bytes 32832 | tf_op jit(solution)/shard_map/mul | solution.py:78
  1.0 0.8 %bitcast_select_fusion.refs_0_ = f32[32,256]{1,0:T(8,128)S(1)} fusion(f32[16,256]{1,0:T(8,128)} %bitcast.26, f32[16,256]{1,0:T(8,128)S(1)} %fusion, pred[32]{0:T(512)(128)(4,1)S(1)} %iota.12), kind=kLoop, calls=%fused_computation.2 | loop fusion | flops 8192 | bytes 65568 | tf_op jit(solution)/shard_map/jit(_where)/select_n | solution.py:80
  1.8 0.0 collective-permute-start.1
  1.8 4.0 %collective-permute-start = (f32[32,256]{1,0:T(8,128)S(1)}, f32[32,256]{1,0:T(8,128)S(1)}, u32[]{:S(2)}, u32[]{:S(2)}) collective-permute-start(f32[32,256]{1,0:T(8,128)S(1)} %bitcast_select_fusion.refs_0_), channel_id=1, source_target_pairs={{0,4},{1,5},{2,6},{3,7},{4,0},{5,1},{6,2},{7,3},{8,12},{9,13},{10,... | collective-permute-start | bytes 98312 | tf_op jit(solution)/shard_map/ppermute | solution.py:27
  5.8 0.0 collective-permute-done.1
  5.8 1.6 %collective-permute-start.2 = (f32[64,256]{1,0:T(8,128)S(1)}, f32[64,256]{1,0:T(8,128)S(1)}, u32[]{:S(2)}, u32[]{:S(2)}) collective-permute-start(f32[64,256]{1,0:T(8,128)S(1)} %pad_maximum_fusion), channel_id=1, source_target_pairs={{0,8},{1,11},{2,10},{3,9},{4,12},{5,15},{6,14},{7,13},{8,0},{9,3},... | collective-permute-start | bytes 196616 | tf_op jit(solution)/shard_map/ppermute | solution.py:27
  7.3 1.0 %collective-permute-start.3 = (f32[64,256]{1,0:T(8,128)S(1)}, f32[64,256]{1,0:T(8,128)S(1)}, u32[]{:S(2)}, u32[]{:S(2)}) collective-permute-start(f32[64,256]{1,0:T(8,128)S(1)} %pad_maximum_fusion), channel_id=1, source_target_pairs={{0,2},{1,15},{2,0},{3,13},{4,6},{5,11},{6,4},{7,9},{8,10},{9,7},{1... | collective-permute-start | bytes 196616 | tf_op jit(solution)/shard_map/ppermute | solution.py:27
  8.4 0.6 collective-permute-start.4
  9.0 2.0 %shard_map.73.x_ref = bf16[256,4096]{1,0:T(8,128)(2,1)S(1)} custom-call(bf16[256,4,8,128]{3,2,1,0:T(8,128)(2,1)} %bitcast.25), custom_call_target="tpu_custom_call" | custom-call | flops 1073741824 | tf_op jit(solution)/shard_map/pallas_call | solution.py:86
  11.0 0.0 collective-permute-done.2.refs_2_
  11.0 0.6 collective-permute-done.3.refs_3_
  11.6 2.9 %collective-permute-done.4.refs_4_ = f32[64,256]{1,0:T(8,128)S(1)} collective-permute-done((f32[64,256]{1,0:T(8,128)S(1)}, f32[64,256]{1,0:T(8,128)S(1)}, u32[]{:S(2)}, u32[]{:S(2)}) %collective-permute-start.4) | collective-permute-done | bytes 65568 | tf_op jit(solution)/shard_map/ppermute | solution.py:27
  14.5 0.0 collective-permute-done.refs_1_
  14.5 0.4 shard_map.74
  14.9 0.1 collective-permute-start.5
  15.0 1.2 %shard_map.75 = (bf16[256,128]{1,0:T(8,128)(2,1)S(1)}, bf16[16,128]{1,0:T(8,128)(2,1)S(1)}) custom-call(bf16[256,4096]{1,0:T(8,128)(2,1)S(1)} %shard_map.73.x_ref, s32[1,1024]{1,0:T(1,128)S(1)} %bitcast.18), custom_call_target="tpu_custom_call" | custom-call | flops 1073741824 | tf_op jit(solution)/shard_map/pallas_call | solution.py:66
  16.2 0.3 collective-permute-done.5
  16.6 2.8 %collective-permute-start.6 = (bf16[256,256]{1,0:T(8,128)(2,1)S(1)}, bf16[256,256]{1,0:T(8,128)(2,1)S(1)}, u32[]{:S(2)}, u32[]{:S(2)}) collective-permute-start(bf16[256,256]{1,0:T(8,128)(2,1)S(1)} %add_convert_fusion.refs_0_.refs_4_), channel_id=1, source_target_pairs={{0,16},{1,49},{2,18},{3,51},{4,20},{5,53},{6,22},{7,55},{8,24},{9,... | collective-permute-start | bytes 393224 | tf_op jit(solution)/shard_map/ppermute | solution.py:27
  19.4 1.6 %collective-permute-start.8 = (bf16[256,256]{1,0:T(8,128)(2,1)S(1)}, bf16[256,256]{1,0:T(8,128)(2,1)S(1)}, u32[]{:S(2)}, u32[]{:S(2)}) collective-permute-start(bf16[256,256]{1,0:T(8,128)(2,1)S(1)} %add_convert_fusion.refs_0_.refs_4_), channel_id=1, source_target_pairs={{0,32},{1,113},{2,34},{3,115},{4,36},{5,117},{6,38},{7,119},{8,40}... | collective-permute-start | bytes 393224 | tf_op jit(solution)/shard_map/ppermute | solution.py:27
  21.0 2.2 %collective-permute-start.9 = (bf16[256,256]{1,0:T(8,128)(2,1)S(1)}, bf16[256,256]{1,0:T(8,128)(2,1)S(1)}, u32[]{:S(2)}, u32[]{:S(2)}) collective-permute-start(bf16[256,256]{1,0:T(8,128)(2,1)S(1)} %add_convert_fusion.refs_0_.refs_4_), channel_id=1, source_target_pairs={{0,96},{1,81},{2,98},{3,83},{4,100},{5,85},{6,102},{7,87},{8,104},... | collective-permute-start | bytes 393224 | tf_op jit(solution)/shard_map/ppermute | solution.py:27
  23.2 0.8 %collective-permute-start.10 = (bf16[128,256]{1,0:T(8,128)(2,1)S(1)}, bf16[128,256]{1,0:T(8,128)(2,1)S(1)}, u32[]{:S(2)}, u32[]{:S(2)}) collective-permute-start(bf16[128,256]{1,0:T(8,128)(2,1)S(1)} %constant_dynamic-slice_fusion), channel_id=1, source_target_pairs={{0,64},{1,65},{2,66},{3,67},{4,68},{5,69},{6,70},{7,71},{8,72},{9,... | collective-permute-start | bytes 196616 | tf_op jit(solution)/shard_map/ppermute | solution.py:27
  24.0 0.3 collective-permute-done.6.refs_1_.refs_5_
  24.3 3.3 %collective-permute-start.7 = (bf16[256,256]{1,0:T(8,128)(2,1)S(1)}, bf16[256,256]{1,0:T(8,128)(2,1)S(1)}, u32[]{:S(2)}, u32[]{:S(2)}) collective-permute-start(bf16[256,256]{1,0:T(8,128)(2,1)S(1)} %collective-permute-done.6.refs_1_.refs_5_), channel_id=1, source_target_pairs={{0,1},{1,0},{2,3},{3,2},{4,5},{5,4},{6,7},{7,6},{8,9},{9,8},{10,11... | collective-permute-start | bytes 393224 | tf_op jit(solution)/shard_map/ppermute | solution.py:27
  27.6 1.5 %shard_map.76 = (bf16[256,4096]{1,0:T(8,128)(2,1)S(1)}, bf16[64,512]{1,0:T(8,128)(2,1)S(1)}, bf16[64,512]{1,0:T(8,128)(2,1)S(1)}, bf16[128,128]{1,0:T(8,128)(2,1)S(1)}) custom-call(bf16[256,4096]{1,0:T(8,128)(2,1)S(1)} %shard_map.73.x_ref, s32[1,1024]{1,0:T(1,128)S(1)} %bitcast.19, bf16[256,128]{1,0:T(8,128)(2,1)S(1)} %get-tuple-element.65.sides_ref, ...), custom_call_target="tpu_custom_call" | custom-call | flops 1227133568 | tf_op jit(solution)/shard_map/pallas_call | solution.py:66
  29.1 0.0 collective-permute-done.8.refs_0_.refs_6_
  29.1 2.3 %collective-permute-done.9.refs_1_.refs_7_ = bf16[256,256]{1,0:T(8,128)(2,1)S(1)} collective-permute-done((bf16[256,256]{1,0:T(8,128)(2,1)S(1)}, bf16[256,256]{1,0:T(8,128)(2,1)S(1)}, u32[]{:S(2)}, u32[]{:S(2)}) %collective-permute-start.9) | collective-permute-done | bytes 131104 | tf_op jit(solution)/shard_map/ppermute | solution.py:27
  31.4 0.0 collective-permute-start.12
  31.4 0.5 collective-permute-start.13
  31.9 1.5 %shard_map.77 = (bf16[256,4096]{1,0:T(8,128)(2,1)S(1)}, bf16[64,512]{1,0:T(8,128)(2,1)S(1)}, bf16[64,512]{1,0:T(8,128)(2,1)S(1)}, bf16[128,128]{1,0:T(8,128)(2,1)S(1)}) custom-call(bf16[256,4096]{1,0:T(8,128)(2,1)S(1)} %shard_map.73.x_ref, s32[1,1024]{1,0:T(1,128)S(1)} %bitcast.20, bf16[256,128]{1,0:T(8,128)(2,1)S(1)} %get-tuple-element.65.sides_ref, ...), custom_call_target="tpu_custom_call" | custom-call | flops 1227133568 | tf_op jit(solution)/shard_map/pallas_call | solution.py:66
  33.5 0.0 copy-start
  33.5 1.3 %copy-done = bf16[256,4096]{1,0:T(8,128)(2,1)} copy-done((bf16[256,4096]{1,0:T(8,128)(2,1)}, bf16[256,4096]{1,0:T(8,128)(2,1)S(1)}, u32[]{:S(2)}) %copy-start) | copy-done | bytes 2097176
  34.8 0.0 collective-permute-done.10.refs_3_.refs_12_
  34.8 0.0 collective-permute-start.11
  34.8 0.1 reshape.21
  34.9 0.0 collective-permute-done.7.refs_0_.refs_8_
  34.9 1.6 %copy-done.1 = bf16[256,4096]{1,0:T(8,128)(2,1)S(1)} copy-done((bf16[256,4096]{1,0:T(8,128)(2,1)S(1)}, bf16[256,4096]{1,0:T(8,128)(2,1)}, u32[]{:S(2)}) %copy-start.1) | copy-done | bytes 2097176
  36.5 0.8 %shard_map.78 = (bf16[256,4096]{1,0:T(8,128)(2,1)S(1)}, bf16[64,512]{1,0:T(8,128)(2,1)S(1)}, bf16[64,512]{1,0:T(8,128)(2,1)S(1)}, bf16[128,128]{1,0:T(8,128)(2,1)S(1)}) custom-call(bf16[256,4096]{1,0:T(8,128)(2,1)S(1)} %shard_map.73.x_ref, s32[1,1024]{1,0:T(1,128)S(1)} %bitcast.21, bf16[256,128]{1,0:T(8,128)(2,1)S(1)} %get-tuple-element.65.sides_ref, ...), custom_call_target="tpu_custom_call" | custom-call | flops 613566784 | tf_op jit(solution)/shard_map/pallas_call | solution.py:66
  37.3 0.0 collective-permute-done.11.refs_2_.refs_11_
  37.4 0.0 collective-permute-done.12.refs_0_.refs_9_
  37.4 0.0 collective-permute-done.13.refs_1_.refs_10_
  37.4 0.5 shard_map.80
  37.9 1.6 %collective-permute-start.14 = (bf16[64,512]{1,0:T(8,128)(2,1)S(1)}, bf16[64,512]{1,0:T(8,128)(2,1)S(1)}, u32[]{:S(2)}, u32[]{:S(2)}) collective-permute-start(bf16[64,512]{1,0:T(8,128)(2,1)S(1)} %get-tuple-element.96), channel_id=1, source_target_pairs={{0,16},{32,48},{64,80},{96,112},{16,0},{48,32},{80,64},{112,96},{1... | collective-permute-start | bytes 196616 | tf_op jit(solution)/shard_map/ppermute | solution.py:397
  39.5 3.6 %collective-permute-start.15 = (bf16[64,512]{1,0:T(8,128)(2,1)S(1)}, bf16[64,512]{1,0:T(8,128)(2,1)S(1)}, u32[]{:S(2)}, u32[]{:S(2)}) collective-permute-start(bf16[64,512]{1,0:T(8,128)(2,1)S(1)} %get-tuple-element.97), channel_id=1, source_target_pairs={{16,32},{48,64},{80,96},{112,0},{32,16},{64,48},{96,80},{0,112},{1... | collective-permute-start | bytes 196616 | tf_op jit(solution)/shard_map/ppermute | solution.py:397
  43.1 0.0 collective-permute-start.16
  43.1 1.7 %collective-permute-start.17 = (bf16[64,128]{1,0:T(8,128)(2,1)S(1)}, bf16[64,128]{1,0:T(8,128)(2,1)S(1)}, u32[]{:S(2)}, u32[]{:S(2)}) collective-permute-start(bf16[64,128]{1,0:T(8,128)(2,1)S(1)} %get-tuple-element.99), channel_id=1, source_target_pairs={{1,2},{3,4},{5,6},{7,8},{9,10},{11,12},{13,14},{15,0},{2,1},{4,3},... | collective-permute-start | bytes 49160 | tf_op jit(solution)/shard_map/ppermute | solution.py:397
  44.8 1.9 %shard_map.79.x_ref = bf16[256,4096]{1,0:T(8,128)(2,1)S(1)} custom-call(bf16[256,4096]{1,0:T(8,128)(2,1)S(1)} %shard_map.73.x_ref, s32[1,1024]{1,0:T(1,128)S(1)} %bitcast.23, bf16[256,4096]{1,0:T(8,128)(2,1)S(1)} %get-tuple-element.91.done_ref, bf16[256,256]{1,0:T(8,128)(2,1)S(1)} %collective-permute-done.12.refs_0_.refs_9_, ...), custom_call_target="tpu_custom_call" | custom-call | flops 2147483648 | tf_op jit(solution)/shard_map/pallas_call | solution.py:66
  46.8 0.0 collective-permute-done.16.refs_2_
  46.8 1.6 %collective-permute-done.17.refs_3_ = bf16[64,128]{1,0:T(8,128)(2,1)S(1)} collective-permute-done((bf16[64,128]{1,0:T(8,128)(2,1)S(1)}, bf16[64,128]{1,0:T(8,128)(2,1)S(1)}, u32[]{:S(2)}, u32[]{:S(2)}) %collective-permute-start.17) | collective-permute-done | bytes 16416 | tf_op jit(solution)/shard_map/ppermute | solution.py:397
  48.4 0.0 collective-permute-done.14.refs_0_
  48.4 0.0 collective-permute-done.15.refs_1_
  48.4 0.2 broadcast_in_dim.34.profile_ref
  48.6 6.6 %shard_map.81 = (bf16[256,4096]{1,0:T(8,128)(2,1)S(1)}, bf16[64,512]{1,0:T(8,128)(2,1)S(1)}, bf16[64,512]{1,0:T(8,128)(2,1)S(1)}, bf16[64,128]{1,0:T(8,128)(2,1)S(1)}, bf16[64,128]{1,0:T(8,128)(2,1)S(1)}) custom-call(s32[4]{0:T(128)S(1)} %copy-done.3, bf16[256,4096]{1,0:T(8,128)(2,1)S(1)} %shard_map.79.x_ref, s32[1,1024]{1,0:T(1,128)S(1)} %bitcast.24, ...), custom_call_target="tpu_custom_call" | custom-call | flops 4294967296 | tf_op jit(solution)/shard_map/pallas_call | solution.py:461
  55.2 0.2 collective-permute-start.20
  55.4 2.9 %collective-permute-start.21 = (bf16[64,512]{1,0:T(8,128)(2,1)S(1)}, bf16[64,512]{1,0:T(8,128)(2,1)S(1)}, u32[]{:S(2)}, u32[]{:S(2)}) collective-permute-start(bf16[64,512]{1,0:T(8,128)(2,1)S(1)} %get-tuple-element.104), channel_id=1, source_target_pairs={{16,32},{48,64},{80,96},{112,0},{32,16},{64,48},{96,80},{0,112},{1... | collective-permute-start | bytes 196616 | tf_op jit(solution)/shard_map/ppermute | solution.py:397
  58.3 0.0 collective-permute-start.18
  58.3 1.3 %collective-permute-start.19 = (bf16[64,128]{1,0:T(8,128)(2,1)S(1)}, bf16[64,128]{1,0:T(8,128)(2,1)S(1)}, u32[]{:S(2)}, u32[]{:S(2)}) collective-permute-start(bf16[64,128]{1,0:T(8,128)(2,1)S(1)} %get-tuple-element.102), channel_id=1, source_target_pairs={{1,2},{3,4},{5,6},{7,8},{9,10},{11,12},{13,14},{15,0},{2,1},{4,3},... | collective-permute-start | bytes 49160 | tf_op jit(solution)/shard_map/ppermute | solution.py:397
  59.7 1.4 %collective-permute-done.20.one_ref = bf16[64,512]{1,0:T(8,128)(2,1)S(1)} collective-permute-done((bf16[64,512]{1,0:T(8,128)(2,1)S(1)}, bf16[64,512]{1,0:T(8,128)(2,1)S(1)}, u32[]{:S(2)}, u32[]{:S(2)}) %collective-permute-start.20) | collective-permute-done | bytes 65568 | tf_op jit(solution)/shard_map/ppermute | solution.py:397
  61.1 2.2 %collective-permute-done.21.two_ref = bf16[64,512]{1,0:T(8,128)(2,1)S(1)} collective-permute-done((bf16[64,512]{1,0:T(8,128)(2,1)S(1)}, bf16[64,512]{1,0:T(8,128)(2,1)S(1)}, u32[]{:S(2)}, u32[]{:S(2)}) %collective-permute-start.21) | collective-permute-done | bytes 65568 | tf_op jit(solution)/shard_map/ppermute | solution.py:397
  63.3 2.1 %shard_map.82.refs_0_ = bf16[256,4,8,128]{3,2,1,0:T(8,128)(2,1)} custom-call(s32[4]{0:T(128)S(1)} %copy-done.3, bf16[256,4096]{1,0:T(8,128)(2,1)S(1)} %get-tuple-element.100.x_ref, bf16[4,256,128]{2,1,0:T(8,128)(2,1)S(1)} %broadcast_in_dim.34.profile_ref, bf16[64,512]{1,0:T(8,128)(2,1)S(1)} %collective-permute-done.20.one_ref, ...), custom_call_target="tpu_custom_call" | custom-call | flops 1073741824 | tf_op jit(solution)/shard_map/pallas_call | solution.py:475
  65.4 0.0 collective-permute-done.18.one_ref
  65.4 0.0 collective-permute-done.19.two_ref
  65.4 2.4 %shard_map.83 = bf16[256,4,8,128]{3,2,1,0:T(8,128)(2,1)} custom-call(s32[4]{0:T(128)S(1)} %copy-done.3, bf16[256,4096]{1,0:T(8,128)(2,1)S(1)} %get-tuple-element.100.x_ref, bf16[4,256,128]{2,1,0:T(8,128)(2,1)S(1)} %broadcast_in_dim.34.profile_ref, bf16[64,128]{1,0:T(8,128)(2,1)S(1)} %collective-permute-done.18.one_ref, ...), custom_call_target="tpu_custom_call", output_to_operand_aliasing={{}: (5, {})} | custom-call | flops 1073741824 | tf_op jit(solution)/shard_map/pallas_call | solution.py:475
  (12 shorter events, 0.1 us)
Async XLA Ops:
  1.8 4.0 %collective-permute-start.1 = (f32[32,256]{1,0:T(8,128)S(1)}, f32[32,256]{1,0:T(8,128)S(1)}, u32[]{:S(2)}, u32[]{:S(2)}) collective-permute-start(f32[32,256]{1,0:T(8,128)S(1)} %bitcast_select_fusion.refs_0_), channel_id=1, source_target_pairs={{0,1},{1,0},{2,3},{3,2},{4,5},{5,4},{6,7},{7,6},{8,9},{9,8},{10,11... | collective-permute-start | bytes 98312 | tf_op jit(solution)/shard_map/ppermute | solution.py:27
  1.8 12.8 %collective-permute-start = (f32[32,256]{1,0:T(8,128)S(1)}, f32[32,256]{1,0:T(8,128)S(1)}, u32[]{:S(2)}, u32[]{:S(2)}) collective-permute-start(f32[32,256]{1,0:T(8,128)S(1)} %bitcast_select_fusion.refs_0_), channel_id=1, source_target_pairs={{0,4},{1,5},{2,6},{3,7},{4,0},{5,1},{6,2},{7,3},{8,12},{9,13},{10,... | collective-permute-start | bytes 98312 | tf_op jit(solution)/shard_map/ppermute | solution.py:27
  5.8 5.2 %collective-permute-start.2 = (f32[64,256]{1,0:T(8,128)S(1)}, f32[64,256]{1,0:T(8,128)S(1)}, u32[]{:S(2)}, u32[]{:S(2)}) collective-permute-start(f32[64,256]{1,0:T(8,128)S(1)} %pad_maximum_fusion), channel_id=1, source_target_pairs={{0,8},{1,11},{2,10},{3,9},{4,12},{5,15},{6,14},{7,13},{8,0},{9,3},... | collective-permute-start | bytes 196616 | tf_op jit(solution)/shard_map/ppermute | solution.py:27
  7.3 4.3 %collective-permute-start.3 = (f32[64,256]{1,0:T(8,128)S(1)}, f32[64,256]{1,0:T(8,128)S(1)}, u32[]{:S(2)}, u32[]{:S(2)}) collective-permute-start(f32[64,256]{1,0:T(8,128)S(1)} %pad_maximum_fusion), channel_id=1, source_target_pairs={{0,2},{1,15},{2,0},{3,13},{4,6},{5,11},{6,4},{7,9},{8,10},{9,7},{1... | collective-permute-start | bytes 196616 | tf_op jit(solution)/shard_map/ppermute | solution.py:27
  8.4 6.1 %collective-permute-start.4 = (f32[64,256]{1,0:T(8,128)S(1)}, f32[64,256]{1,0:T(8,128)S(1)}, u32[]{:S(2)}, u32[]{:S(2)}) collective-permute-start(f32[64,256]{1,0:T(8,128)S(1)} %pad_maximum_fusion), channel_id=1, source_target_pairs={{0,6},{1,13},{2,4},{3,15},{4,2},{5,9},{6,0},{7,11},{8,14},{9,5},{1... | collective-permute-start | bytes 196616 | tf_op jit(solution)/shard_map/ppermute | solution.py:27
  9.0 6.0 %copy-start.2 = (s32[8,128]{1,0:T(8,128)S(1)}, s32[8,128]{1,0:T(8,128)}, u32[]{:S(2)}) copy-start(s32[8,128]{1,0:T(8,128)} %param.8) | copy-start | bytes 12292
  14.9 1.6 %collective-permute-start.5 = (f32[256,256]{1,0:T(8,128)S(1)}, f32[256,256]{1,0:T(8,128)S(1)}, u32[]{:S(2)}, u32[]{:S(2)}) collective-permute-start(f32[256,256]{1,0:T(8,128)S(1)} %shard_map.74), channel_id=1, source_target_pairs={{0,1},{1,0},{2,3},{3,2},{4,5},{5,4},{6,7},{7,6},{8,9},{9,8},{10,11... | collective-permute-start | bytes 786440 | tf_op jit(solution)/shard_map/ppermute | solution.py:27
  16.6 7.7 %collective-permute-start.6 = (bf16[256,256]{1,0:T(8,128)(2,1)S(1)}, bf16[256,256]{1,0:T(8,128)(2,1)S(1)}, u32[]{:S(2)}, u32[]{:S(2)}) collective-permute-start(bf16[256,256]{1,0:T(8,128)(2,1)S(1)} %add_convert_fusion.refs_0_.refs_4_), channel_id=1, source_target_pairs={{0,16},{1,49},{2,18},{3,51},{4,20},{5,53},{6,22},{7,55},{8,24},{9,... | collective-permute-start | bytes 393224 | tf_op jit(solution)/shard_map/ppermute | solution.py:27
  19.4 9.7 %collective-permute-start.8 = (bf16[256,256]{1,0:T(8,128)(2,1)S(1)}, bf16[256,256]{1,0:T(8,128)(2,1)S(1)}, u32[]{:S(2)}, u32[]{:S(2)}) collective-permute-start(bf16[256,256]{1,0:T(8,128)(2,1)S(1)} %add_convert_fusion.refs_0_.refs_4_), channel_id=1, source_target_pairs={{0,32},{1,113},{2,34},{3,115},{4,36},{5,117},{6,38},{7,119},{8,40}... | collective-permute-start | bytes 393224 | tf_op jit(solution)/shard_map/ppermute | solution.py:27
  21.0 10.4 %collective-permute-start.9 = (bf16[256,256]{1,0:T(8,128)(2,1)S(1)}, bf16[256,256]{1,0:T(8,128)(2,1)S(1)}, u32[]{:S(2)}, u32[]{:S(2)}) collective-permute-start(bf16[256,256]{1,0:T(8,128)(2,1)S(1)} %add_convert_fusion.refs_0_.refs_4_), channel_id=1, source_target_pairs={{0,96},{1,81},{2,98},{3,83},{4,100},{5,85},{6,102},{7,87},{8,104},... | collective-permute-start | bytes 393224 | tf_op jit(solution)/shard_map/ppermute | solution.py:27
  23.2 11.6 %collective-permute-start.10 = (bf16[128,256]{1,0:T(8,128)(2,1)S(1)}, bf16[128,256]{1,0:T(8,128)(2,1)S(1)}, u32[]{:S(2)}, u32[]{:S(2)}) collective-permute-start(bf16[128,256]{1,0:T(8,128)(2,1)S(1)} %constant_dynamic-slice_fusion), channel_id=1, source_target_pairs={{0,64},{1,65},{2,66},{3,67},{4,68},{5,69},{6,70},{7,71},{8,72},{9,... | collective-permute-start | bytes 196616 | tf_op jit(solution)/shard_map/ppermute | solution.py:27
  24.3 10.6 %collective-permute-start.7 = (bf16[256,256]{1,0:T(8,128)(2,1)S(1)}, bf16[256,256]{1,0:T(8,128)(2,1)S(1)}, u32[]{:S(2)}, u32[]{:S(2)}) collective-permute-start(bf16[256,256]{1,0:T(8,128)(2,1)S(1)} %collective-permute-done.6.refs_1_.refs_5_), channel_id=1, source_target_pairs={{0,1},{1,0},{2,3},{3,2},{4,5},{5,4},{6,7},{7,6},{8,9},{9,8},{10,11... | collective-permute-start | bytes 393224 | tf_op jit(solution)/shard_map/ppermute | solution.py:27
  31.4 3.4 %copy-start.4 = (bf16[4,64,4]{1,2,0:T(4,128)(2,1)S(1)}, bf16[4,64,4]{1,2,0:T(4,128)(2,1)}, u32[]{:S(2)}) copy-start(bf16[4,64,4]{1,2,0:T(4,128)(2,1)} %param.10) | copy-start | bytes 6148
  31.4 5.9 %collective-permute-start.12 = (bf16[256,256]{1,0:T(8,128)(2,1)S(1)}, bf16[256,256]{1,0:T(8,128)(2,1)S(1)}, u32[]{:S(2)}, u32[]{:S(2)}) collective-permute-start(bf16[256,256]{1,0:T(8,128)(2,1)S(1)} %collective-permute-done.8.refs_0_.refs_6_), channel_id=1, source_target_pairs={{0,1},{1,0},{2,3},{3,2},{4,5},{5,4},{6,7},{7,6},{8,9},{9,8},{10,11... | collective-permute-start | bytes 393224 | tf_op jit(solution)/shard_map/ppermute | solution.py:27
  31.4 6.0 %collective-permute-start.13 = (bf16[256,256]{1,0:T(8,128)(2,1)S(1)}, bf16[256,256]{1,0:T(8,128)(2,1)S(1)}, u32[]{:S(2)}, u32[]{:S(2)}) collective-permute-start(bf16[256,256]{1,0:T(8,128)(2,1)S(1)} %collective-permute-done.9.refs_1_.refs_7_), channel_id=1, source_target_pairs={{0,1},{1,0},{2,3},{3,2},{4,5},{5,4},{6,7},{7,6},{8,9},{9,8},{10,11... | collective-permute-start | bytes 393224 | tf_op jit(solution)/shard_map/ppermute | solution.py:27
  33.5 1.3 %copy-start = (bf16[256,4096]{1,0:T(8,128)(2,1)}, bf16[256,4096]{1,0:T(8,128)(2,1)S(1)}, u32[]{:S(2)}) copy-start(bf16[256,4096]{1,0:T(8,128)(2,1)S(1)} %get-tuple-element.82.refs_1_) | copy-start | bytes 6291460
  34.8 2.6 %collective-permute-start.11 = (bf16[128,256]{1,0:T(8,128)(2,1)S(1)}, bf16[128,256]{1,0:T(8,128)(2,1)S(1)}, u32[]{:S(2)}, u32[]{:S(2)}) collective-permute-start(bf16[128,256]{1,0:T(8,128)(2,1)S(1)} %collective-permute-done.10.refs_3_.refs_12_), channel_id=1, source_target_pairs={{0,1},{1,0},{2,3},{3,2},{4,5},{5,4},{6,7},{7,6},{8,9},{9,8},{10,11... | collective-permute-start | bytes 196616 | tf_op jit(solution)/shard_map/ppermute | solution.py:27
  34.9 1.6 %copy-start.1 = (bf16[256,4096]{1,0:T(8,128)(2,1)S(1)}, bf16[256,4096]{1,0:T(8,128)(2,1)}, u32[]{:S(2)}) copy-start(bf16[256,4096]{1,0:T(8,128)(2,1)} %copy-done) | copy-start | bytes 6291460
  37.9 10.5 %collective-permute-start.14 = (bf16[64,512]{1,0:T(8,128)(2,1)S(1)}, bf16[64,512]{1,0:T(8,128)(2,1)S(1)}, u32[]{:S(2)}, u32[]{:S(2)}) collective-permute-start(bf16[64,512]{1,0:T(8,128)(2,1)S(1)} %get-tuple-element.96), channel_id=1, source_target_pairs={{0,16},{32,48},{64,80},{96,112},{16,0},{48,32},{80,64},{112,96},{1... | collective-permute-start | bytes 196616 | tf_op jit(solution)/shard_map/ppermute | solution.py:397
  39.5 8.9 %collective-permute-start.15 = (bf16[64,512]{1,0:T(8,128)(2,1)S(1)}, bf16[64,512]{1,0:T(8,128)(2,1)S(1)}, u32[]{:S(2)}, u32[]{:S(2)}) collective-permute-start(bf16[64,512]{1,0:T(8,128)(2,1)S(1)} %get-tuple-element.97), channel_id=1, source_target_pairs={{16,32},{48,64},{80,96},{112,0},{32,16},{64,48},{96,80},{0,112},{1... | collective-permute-start | bytes 196616 | tf_op jit(solution)/shard_map/ppermute | solution.py:397
  43.1 3.7 %collective-permute-start.16 = (bf16[64,128]{1,0:T(8,128)(2,1)S(1)}, bf16[64,128]{1,0:T(8,128)(2,1)S(1)}, u32[]{:S(2)}, u32[]{:S(2)}) collective-permute-start(bf16[64,128]{1,0:T(8,128)(2,1)S(1)} %get-tuple-element.98), channel_id=1, source_target_pairs={{0,1},{2,3},{4,5},{6,7},{8,9},{10,11},{12,13},{14,15},{1,0},{3,2},... | collective-permute-start | bytes 49160 | tf_op jit(solution)/shard_map/ppermute | solution.py:397
  43.1 5.5 %copy-start.3 = (s32[4]{0:T(128)S(1)}, s32[4]{0:T(128)}, u32[]{:S(2)}) copy-start(s32[4]{0:T(128)} %port_ref.5) | copy-start | bytes 52
  43.1 5.3 %collective-permute-start.17 = (bf16[64,128]{1,0:T(8,128)(2,1)S(1)}, bf16[64,128]{1,0:T(8,128)(2,1)S(1)}, u32[]{:S(2)}, u32[]{:S(2)}) collective-permute-start(bf16[64,128]{1,0:T(8,128)(2,1)S(1)} %get-tuple-element.99), channel_id=1, source_target_pairs={{1,2},{3,4},{5,6},{7,8},{9,10},{11,12},{13,14},{15,0},{2,1},{4,3},... | collective-permute-start | bytes 49160 | tf_op jit(solution)/shard_map/ppermute | solution.py:397
  55.2 5.8 %collective-permute-start.20 = (bf16[64,512]{1,0:T(8,128)(2,1)S(1)}, bf16[64,512]{1,0:T(8,128)(2,1)S(1)}, u32[]{:S(2)}, u32[]{:S(2)}) collective-permute-start(bf16[64,512]{1,0:T(8,128)(2,1)S(1)} %get-tuple-element.103), channel_id=1, source_target_pairs={{0,16},{32,48},{64,80},{96,112},{16,0},{48,32},{80,64},{112,96},{1... | collective-permute-start | bytes 196616 | tf_op jit(solution)/shard_map/ppermute | solution.py:397
  55.4 7.9 %collective-permute-start.21 = (bf16[64,512]{1,0:T(8,128)(2,1)S(1)}, bf16[64,512]{1,0:T(8,128)(2,1)S(1)}, u32[]{:S(2)}, u32[]{:S(2)}) collective-permute-start(bf16[64,512]{1,0:T(8,128)(2,1)S(1)} %get-tuple-element.104), channel_id=1, source_target_pairs={{16,32},{48,64},{80,96},{112,0},{32,16},{64,48},{96,80},{0,112},{1... | collective-permute-start | bytes 196616 | tf_op jit(solution)/shard_map/ppermute | solution.py:397
  58.3 7.1 %collective-permute-start.18 = (bf16[64,128]{1,0:T(8,128)(2,1)S(1)}, bf16[64,128]{1,0:T(8,128)(2,1)S(1)}, u32[]{:S(2)}, u32[]{:S(2)}) collective-permute-start(bf16[64,128]{1,0:T(8,128)(2,1)S(1)} %get-tuple-element.101), channel_id=1, source_target_pairs={{0,1},{2,3},{4,5},{6,7},{8,9},{10,11},{12,13},{14,15},{1,0},{3,2},... | collective-permute-start | bytes 49160 | tf_op jit(solution)/shard_map/ppermute | solution.py:397
  58.3 7.1 %collective-permute-start.19 = (bf16[64,128]{1,0:T(8,128)(2,1)S(1)}, bf16[64,128]{1,0:T(8,128)(2,1)S(1)}, u32[]{:S(2)}, u32[]{:S(2)}) collective-permute-start(bf16[64,128]{1,0:T(8,128)(2,1)S(1)} %get-tuple-element.102), channel_id=1, source_target_pairs={{1,2},{3,4},{5,6},{7,8},{9,10},{11,12},{13,14},{15,0},{2,1},{4,3},... | collective-permute-start | bytes 49160 | tf_op jit(solution)/shard_map/ppermute | solution.py:397

commit v9 on v8

--- a/solution.py
+++ b/solution.py
@@ -75,9 +75,10 @@
 
 def own_type_map(mode_shapes, mode_values, mode_weights, traces, types):
     modes, order = mode_weights.shape[1:]
-    scaled = mode_shapes[0].T * mode_values[0][:, None]
-    part = lax.broadcasted_iota(jnp.int32, (2, modes, order), 0)
-    own = jnp.where(part == 0, scaled[None], mode_weights).reshape(2 * modes, order)
+    own = jnp.concatenate([mode_shapes[0].T, mode_weights[0]], axis=0).reshape(2, modes, order)
+    part = lax.broadcasted_iota(jnp.int32, own.shape, 0)
+    own = own * jnp.where(part == 0, mode_values[0][None, :, None], 1.0)
+    own = own.reshape(2 * modes, order)
     far = swap(own, "col", 4)
     pair = jnp.concatenate([own, swap(own, "col", 1)], axis=0)
     pair, traces = lax.optimization_barrier((pair, traces))
@@ -336,51 +337,51 @@
     store_rims(rim_refs, north_rim, south_rim, west_rim, east_rim)
 
 
-def last_kernel(rows, width, axis, port_ref, x_ref, profile_ref, one_ref, two_ref, *refs):
-    out_ref, buffer, sems = refs[-3:]
-    ports = buffer.shape[1]
-    quarter, tile = x_ref.shape[0] // 4, rows * width
-    low, high = halos_inside(axis, one_ref, two_ref)
+def last_kernel(rows, width, port_ref, x_ref, profile_ref, *refs):
+    out_ref, buffer, sems = refs[4:]
+    order, ports = buffer.shape[:2]
+    quarter, tile = order // 4, rows * width
+    north_in, south_in = halos_inside("row", *refs[:2])
+    west_in, east_in = halos_inside("col", *refs[2:4])
     lane = lax.broadcasted_iota(jnp.int32, (quarter, LANES), 1)
     copies = []
-    for edge in (0, 1) if axis == "row" else (2, 3):
+    for edge in (2, 3, 0, 1):
         lines = slice(edge * quarter, (edge + 1) * quarter)
-        local = slice(edge % 2 * quarter, (edge % 2 + 1) * quarter)
         for port in range(ports):
             rim = slice(port * LANES, (port + 1) * LANES)
             starts = [port * tile + row * LANES for row in range(rows)]
             parts = [x_ref[lines, start : start + LANES].astype(F32) for start in starts]
             places = range(port * rows, (port + 1) * rows)
             if edge == 0:
-                parts[0] = low[:, rim]
+                parts[0] = north_in[:, rim]
             elif edge == 1:
-                parts[-1] = high[:, rim]
+                parts[-1] = south_in[:, rim]
             elif edge == 2:
                 parts = [
-                    jnp.where(lane == 0, lane_of(low, place), part)
+                    jnp.where(lane == 0, lane_of(west_in, place), part)
                     for place, part in zip(places, parts)
                 ]
             else:
                 parts = [
-                    jnp.where(lane == LANES - 1, lane_of(high, place), part)
+                    jnp.where(lane == LANES - 1, lane_of(east_in, place), part)
                     for place, part in zip(places, parts)
                 ]
             value = jnp.concatenate(parts, axis=1).reshape(quarter, rows, LANES)
-            buffer[local, port] = value.astype(BF)
+            buffer[lines, port] = value.astype(BF)
         for port in range(ports):
             row, col, inside = port_place(port_ref, port, rows, width)
 
             @pl.when(inside)
             def _():
-                current = buffer[local, port].astype(F32)
+                current = buffer[lines, port].astype(F32)
                 here = (lax.broadcasted_iota(jnp.int32, current.shape, 1) == row) & (
                     lax.broadcasted_iota(jnp.int32, current.shape, 2) == col
                 )
                 profile = profile_ref[port, lines, :].astype(F32).reshape(quarter, 1, LANES)
                 added = current + jnp.broadcast_to(profile, current.shape)
-                buffer[local, port] = jnp.where(here, added, current).astype(BF)
-
-        copy = pltpu.make_async_copy(buffer.at[local], out_ref.at[lines], sems.at[edge % 2])
+                buffer[lines, port] = jnp.where(here, added, current).astype(BF)
+
+        copy = pltpu.make_async_copy(buffer.at[lines], out_ref.at[lines], sems.at[edge])
         copy.start()
         copies.append(copy)
     for copy in copies:
@@ -408,7 +409,6 @@
     half = lax.dynamic_slice_in_dim(own_map, core * (order // 2), order // 2)
     fetched = [swap(own_map, "row", *steps) for steps in MAP_STEPS[1:4]]
     half = swap(half, "row", 4)
-    swapped = [swap(fetched[0], "col", 1)]
     profile = jnp.broadcast_to(
         jnp.transpose(port_profile.reshape(order, ports))[:, :, None], (ports, order, LANES)
     )
@@ -427,18 +427,16 @@
         return whole_call(kernel, part_shapes, x, types, *sides, *maps, *parts, flops=flops)
 
     parts = early(0, [own_map, fetched[0]])
-    parts, rest = lax.optimization_barrier((parts, fetched[1:]))
-    swapped += [swap(value, "col", 1) for value in rest]
-    parts = early(2, rest, parts)
+    parts, fetched = lax.optimization_barrier((parts, fetched))
+    swapped = [swap(value, "col", 1) for value in fetched]
+    parts = early(2, fetched[1:], parts)
     parts, half = lax.optimization_barrier((parts, half))
-    swapped += [swap(half, "col", 1)]
-    parts = early(4, swapped[:1], parts)
-    parts, swapped[3] = lax.optimization_barrier((parts, swapped[3]))
+    swapped.append(swap(half, "col", 1))
     done, *parts = parts
-    maps = [own_map, fetched[0]] + rest + swapped + [half]
-    late = maps[5:]
+    late = swapped + [half]
+    maps = [own_map] + fetched + late
     sent = whole_call(
-        functools.partial(rim_kernel, ports, 5),
+        functools.partial(rim_kernel, ports, 4),
         rim_shapes,
         x,
         types,
@@ -449,7 +447,7 @@
     )
     halos = exchange(sent)
     (x,) = whole_call(
-        functools.partial(first_kernel, rows, ports, 5),
+        functools.partial(first_kernel, rows, ports, 4),
         [next_shape],
         x,
         types,
@@ -467,26 +465,19 @@
         compiler_params=PARAMS,
         cost_estimate=pl.CostEstimate(flops=work, bytes_accessed=0, transcendentals=0),
     )(*operands)
-    halos = exchange(sent)
-    out = []
-    for axis, pair in (("row", halos[:2]), ("col", halos[2:])):
-        operands = [port_cell, x, profile, *pair, *out]
-        out = [
-            pl.pallas_call(
-                functools.partial(last_kernel, rows, width, axis),
-                in_specs=[ports_spec] + [WHOLE] * 4 + [pl.BlockSpec(memory_space=pl.ANY)] * len(out),
-                out_specs=pl.BlockSpec(memory_space=pl.ANY),
-                out_shape=jax.ShapeDtypeStruct((order, ports, rows, width), BF),
-                scratch_shapes=[
-                    pltpu.VMEM((order // 2, ports, rows, width), BF),
-                    pltpu.SemaphoreType.DMA((2,)),
-                ],
-                input_output_aliases={5: 0} if out else {},
-                compiler_params=PARAMS,
-                cost_estimate=pl.CostEstimate(flops=2**30, bytes_accessed=0, transcendentals=0),
-            )(*operands)
-        ]
-    return out[0].reshape(traces.shape)
+    operands = [port_cell, x, profile, *exchange(sent)]
+    out = pl.pallas_call(
+        functools.partial(last_kernel, rows, width),
+        in_specs=[ports_spec] + [WHOLE] * (len(operands) - 1),
+        out_specs=pl.BlockSpec(memory_space=pl.ANY),
+        out_shape=jax.ShapeDtypeStruct((order, ports, rows, width), BF),
+        scratch_shapes=[
+            pltpu.VMEM((order, ports, rows, width), BF),
+            pltpu.SemaphoreType.DMA((4,)),
+        ],
+        compiler_params=PARAMS,
+    )(*operands)
+    return out.reshape(traces.shape)
 
 
 def solution(mesh):

time: 68.2 us -> 66.2 us (0.971)
  waiting for transfers between devices: 11.7 us -> 15.7 us
  starting transfers between devices: 29.9 us -> 27.1 us
  Pallas kernels: 21 us -> 19.3 us
  local copies, waits for them, and re-layouts: 3.37 us -> 2.52 us
  other arithmetic: 1.62 us -> 0.85 us
    ppermute x14, waiting for transfers between devices: 6.49 us -> 10.6 us  [swap(): return lax.ppermute(value, ('row', 'col'), pairs)]
    ppermute x14, starting transfers between devices: 18.5 us -> 15.8 us  [swap(): return lax.ppermute(value, ('row', 'col'), pairs)]
    unnamed x11, local copies, waits for them, and re-layouts: 2.92 us -> 1.33 us
    pallas_call x2 -> x1, Pallas kernels: 4.43 us -> 3.08 us  [body(): pl.pallas_call(functools.partial(last_kernel, rows, width), in_specs=[por...]
    select_n x1 -> x0, other arithmetic: 0.79 us -> none  [own_type_map(): jnp.where(part == 0, scaled[None], mode_weights).reshape(2 * modes, order)]
    broadcast_in_dim x0 -> x2, local copies, waits for them, and re-layouts: none -> 0.74 us  [own_type_map(): own = own * jnp.where(part == 0, mode_values[0][None, :, None], 1.0)]
    pallas_call x7 -> x6, Pallas kernels: 7.94 us -> 7.66 us  [whole_call(): pl.pallas_call(kernel, in_specs=[WHOLE] * len(operands), out_specs=[WHOLE...]
  transfers between devices with their start and end apart: 22 -> 22, of which waited for: 8 -> 8; matrix products, arithmetic and copies ran while one was open for 0% -> 0% of each run, Pallas kernels for 16% -> 13%
where the time goes in v9:
time: 66.2 us; the launch traced here: 65.8 us
  starting transfers between devices  27.1 us (41%)
  Pallas kernels  19.3 us (29%)
  waiting for transfers between devices  15.7 us (24%)
  local copies, waits for them, and re-layouts  2.52 us (4%)
  other arithmetic  0.85 us (1%)
    ppermute x14, starting transfers between devices, swap(): return lax.ppermute(value, ('row', 'col'), pairs)  15.8 us
    ppermute x8, starting transfers between devices, exchange(): lax.ppermute(rim, axis, pairs(axis, first))  11.3 us
    ppermute x14, waiting for transfers between devices, swap(): return lax.ppermute(value, ('row', 'col'), pairs)  10.6 us
    pallas_call x6, Pallas kernels, whole_call(): pl.pallas_call(kernel, in_specs=[WHOLE] * len(operands), out_specs=[WHOLE...  7.66 us
    pallas_call x1, Pallas kernels, body(): pl.pallas_call(functools.partial(second_kernel, rows, width), in_specs=[p...  6.61 us
    ppermute x8, waiting for transfers between devices, exchange(): lax.ppermute(rim, axis, pairs(axis, first))  5.11 us
    pallas_call x1, Pallas kernels, body(): pl.pallas_call(functools.partial(last_kernel, rows, width), in_specs=[por...  3.08 us
    pallas_call x1, Pallas kernels, own_type_map(): pl.pallas_call(flat_kernel, in_specs=[pl.BlockSpec(memory_space=pltpu.HBM...  1.98 us
  transfers between devices with their start and end apart: 22, of which 8 were waited for; matrix products, arithmetic and copies ran while one was open for 0% of the time, Pallas kernels for 13%

profile of v9, /device:TPU:0, one launch (start us, length us, event | category | flops | bytes accessed | tf_op | source)
XLA Modules:
  0.0 65.8 jit_solution(17843445246196985496)
XLA Ops:
  0.0 0.7 broadcast_in_dim.25
  0.7 0.1 broadcast_in_dim.26
  0.7 0.1 iota.11
  0.8 0.1 iota.12
  0.9 0.8 %maximum_multiply_fusion.refs_0_ = f32[32,256]{1,0:T(8,128)S(1)} fusion(f32[16,256]{1,0:T(8,128)} %bitcast.18, f32[16,256]{1,0:T(8,128)} %bitcast.19, f32[32]{0:T(128)S(1)} %broadcast_in_dim.26, pred[32]{0:T(512)(128)(4,1)S(1)} %iota.12), kind=kLoop, calls=%fused_computation.2 | loop fusion | flops 24576 | bytes 65696 | tf_op jit(solution)/shard_map/mul | solution.py:80
  1.7 0.1 collective-permute-start.1
  1.8 4.0 %collective-permute-start = (f32[32,256]{1,0:T(8,128)S(1)}, f32[32,256]{1,0:T(8,128)S(1)}, u32[]{:S(2)}, u32[]{:S(2)}) collective-permute-start(f32[32,256]{1,0:T(8,128)S(1)} %maximum_multiply_fusion.refs_0_), channel_id=1, source_target_pairs={{0,4},{1,5},{2,6},{3,7},{4,0},{5,1},{6,2},{7,3},{8,12},{9,13},{10,... | collective-permute-start | bytes 98312 | tf_op jit(solution)/shard_map/ppermute | solution.py:27
  5.8 0.0 collective-permute-done.1
  5.8 1.6 %collective-permute-start.2 = (f32[64,256]{1,0:T(8,128)S(1)}, f32[64,256]{1,0:T(8,128)S(1)}, u32[]{:S(2)}, u32[]{:S(2)}) collective-permute-start(f32[64,256]{1,0:T(8,128)S(1)} %pad_maximum_fusion), channel_id=1, source_target_pairs={{0,8},{1,11},{2,10},{3,9},{4,12},{5,15},{6,14},{7,13},{8,0},{9,3},... | collective-permute-start | bytes 196616 | tf_op jit(solution)/shard_map/ppermute | solution.py:27
  7.4 1.0 %collective-permute-start.3 = (f32[64,256]{1,0:T(8,128)S(1)}, f32[64,256]{1,0:T(8,128)S(1)}, u32[]{:S(2)}, u32[]{:S(2)}) collective-permute-start(f32[64,256]{1,0:T(8,128)S(1)} %pad_maximum_fusion), channel_id=1, source_target_pairs={{0,2},{1,15},{2,0},{3,13},{4,6},{5,11},{6,4},{7,9},{8,10},{9,7},{1... | collective-permute-start | bytes 196616 | tf_op jit(solution)/shard_map/ppermute | solution.py:27
  8.4 0.6 collective-permute-start.4
  9.0 2.0 %shard_map.73.x_ref = bf16[256,4096]{1,0:T(8,128)(2,1)S(1)} custom-call(bf16[256,4,8,128]{3,2,1,0:T(8,128)(2,1)} %bitcast.17), custom_call_target="tpu_custom_call" | custom-call | flops 1073741824 | tf_op jit(solution)/shard_map/pallas_call | solution.py:87
  11.0 0.0 collective-permute-done.2.refs_2_
  11.0 0.7 %collective-permute-done.3.refs_3_ = f32[64,256]{1,0:T(8,128)S(1)} collective-permute-done((f32[64,256]{1,0:T(8,128)S(1)}, f32[64,256]{1,0:T(8,128)S(1)}, u32[]{:S(2)}, u32[]{:S(2)}) %collective-permute-start.3) | collective-permute-done | bytes 65568 | tf_op jit(solution)/shard_map/ppermute | solution.py:27
  11.7 2.9 %collective-permute-done.4.refs_4_ = f32[64,256]{1,0:T(8,128)S(1)} collective-permute-done((f32[64,256]{1,0:T(8,128)S(1)}, f32[64,256]{1,0:T(8,128)S(1)}, u32[]{:S(2)}, u32[]{:S(2)}) %collective-permute-start.4) | collective-permute-done | bytes 65568 | tf_op jit(solution)/shard_map/ppermute | solution.py:27
  14.5 0.0 collective-permute-done.refs_1_
  14.5 0.4 shard_map.74
  15.0 0.1 collective-permute-start.5
  15.0 0.0 copy-done
  15.1 1.2 %shard_map.75 = (bf16[256,128]{1,0:T(8,128)(2,1)S(1)}, bf16[16,128]{1,0:T(8,128)(2,1)S(1)}) custom-call(bf16[256,4096]{1,0:T(8,128)(2,1)S(1)} %shard_map.73.x_ref, s32[1,1024]{1,0:T(1,128)S(1)} %bitcast.11), custom_call_target="tpu_custom_call" | custom-call | flops 1073741824 | tf_op jit(solution)/shard_map/pallas_call | solution.py:66
  16.2 0.3 collective-permute-done.5
  16.6 2.9 %collective-permute-start.6 = (bf16[256,256]{1,0:T(8,128)(2,1)S(1)}, bf16[256,256]{1,0:T(8,128)(2,1)S(1)}, u32[]{:S(2)}, u32[]{:S(2)}) collective-permute-start(bf16[256,256]{1,0:T(8,128)(2,1)S(1)} %add_convert_fusion.refs_0_.refs_4_), channel_id=1, source_target_pairs={{0,16},{1,49},{2,18},{3,51},{4,20},{5,53},{6,22},{7,55},{8,24},{9,... | collective-permute-start | bytes 393224 | tf_op jit(solution)/shard_map/ppermute | solution.py:27
  19.5 1.6 %collective-permute-start.7 = (bf16[256,256]{1,0:T(8,128)(2,1)S(1)}, bf16[256,256]{1,0:T(8,128)(2,1)S(1)}, u32[]{:S(2)}, u32[]{:S(2)}) collective-permute-start(bf16[256,256]{1,0:T(8,128)(2,1)S(1)} %add_convert_fusion.refs_0_.refs_4_), channel_id=1, source_target_pairs={{0,32},{1,113},{2,34},{3,115},{4,36},{5,117},{6,38},{7,119},{8,40}... | collective-permute-start | bytes 393224 | tf_op jit(solution)/shard_map/ppermute | solution.py:27
  21.1 2.2 %collective-permute-start.8 = (bf16[256,256]{1,0:T(8,128)(2,1)S(1)}, bf16[256,256]{1,0:T(8,128)(2,1)S(1)}, u32[]{:S(2)}, u32[]{:S(2)}) collective-permute-start(bf16[256,256]{1,0:T(8,128)(2,1)S(1)} %add_convert_fusion.refs_0_.refs_4_), channel_id=1, source_target_pairs={{0,96},{1,81},{2,98},{3,83},{4,100},{5,85},{6,102},{7,87},{8,104},... | collective-permute-start | bytes 393224 | tf_op jit(solution)/shard_map/ppermute | solution.py:27
  23.2 0.8 %collective-permute-start.9 = (bf16[128,256]{1,0:T(8,128)(2,1)S(1)}, bf16[128,256]{1,0:T(8,128)(2,1)S(1)}, u32[]{:S(2)}, u32[]{:S(2)}) collective-permute-start(bf16[128,256]{1,0:T(8,128)(2,1)S(1)} %constant_dynamic-slice_fusion), channel_id=1, source_target_pairs={{0,64},{1,65},{2,66},{3,67},{4,68},{5,69},{6,70},{7,71},{8,72},{9,... | collective-permute-start | bytes 196616 | tf_op jit(solution)/shard_map/ppermute | solution.py:27
  24.1 0.3 collective-permute-done.6.refs_1_.refs_5_
  24.3 1.5 %shard_map.76 = (bf16[256,4096]{1,0:T(8,128)(2,1)S(1)}, bf16[64,512]{1,0:T(8,128)(2,1)S(1)}, bf16[64,512]{1,0:T(8,128)(2,1)S(1)}, bf16[128,128]{1,0:T(8,128)(2,1)S(1)}) custom-call(bf16[256,4096]{1,0:T(8,128)(2,1)S(1)} %shard_map.73.x_ref, s32[1,1024]{1,0:T(1,128)S(1)} %bitcast.12, bf16[256,128]{1,0:T(8,128)(2,1)S(1)} %get-tuple-element.57.sides_ref, ...), custom_call_target="tpu_custom_call" | custom-call | flops 1227133568 | tf_op jit(solution)/shard_map/pallas_call | solution.py:66
  25.9 0.0 collective-permute-done.7.refs_0_.refs_6_
  25.9 5.6 %collective-permute-done.8.refs_1_.refs_7_ = bf16[256,256]{1,0:T(8,128)(2,1)S(1)} collective-permute-done((bf16[256,256]{1,0:T(8,128)(2,1)S(1)}, bf16[256,256]{1,0:T(8,128)(2,1)S(1)}, u32[]{:S(2)}, u32[]{:S(2)}) %collective-permute-start.8) | collective-permute-done | bytes 131104 | tf_op jit(solution)/shard_map/ppermute | solution.py:27
  31.4 0.0 collective-permute-start.10
  31.5 0.5 collective-permute-start.11
  32.0 0.0 collective-permute-start.12
  32.0 1.5 %shard_map.77 = (bf16[256,4096]{1,0:T(8,128)(2,1)S(1)}, bf16[64,512]{1,0:T(8,128)(2,1)S(1)}, bf16[64,512]{1,0:T(8,128)(2,1)S(1)}, bf16[128,128]{1,0:T(8,128)(2,1)S(1)}) custom-call(bf16[256,4096]{1,0:T(8,128)(2,1)S(1)} %shard_map.73.x_ref, s32[1,1024]{1,0:T(1,128)S(1)} %bitcast.13, bf16[256,128]{1,0:T(8,128)(2,1)S(1)} %get-tuple-element.57.sides_ref, ...), custom_call_target="tpu_custom_call" | custom-call | flops 1227133568 | tf_op jit(solution)/shard_map/pallas_call | solution.py:66
  33.5 0.0 copy-start.2
  33.5 1.3 %copy-done.2 = bf16[256,4096]{1,0:T(8,128)(2,1)} copy-done((bf16[256,4096]{1,0:T(8,128)(2,1)}, bf16[256,4096]{1,0:T(8,128)(2,1)S(1)}, u32[]{:S(2)}) %copy-start.2) | copy-done | bytes 2097176
  34.8 0.0 collective-permute-done.9.refs_4_.refs_12_
  34.8 0.5 collective-permute-start.13
  35.3 0.1 reshape.20
  35.4 0.8 %collective-permute-done.13.refs_3_.refs_11_ = bf16[128,256]{1,0:T(8,128)(2,1)S(1)} collective-permute-done((bf16[128,256]{1,0:T(8,128)(2,1)S(1)}, bf16[128,256]{1,0:T(8,128)(2,1)S(1)}, u32[]{:S(2)}, u32[]{:S(2)}) %collective-permute-start.13) | collective-permute-done | bytes 65568 | tf_op jit(solution)/shard_map/ppermute | solution.py:27
  36.2 0.0 collective-permute-done.10.refs_0_.refs_8_
  36.2 0.0 collective-permute-done.11.refs_1_.refs_9_
  36.2 0.0 collective-permute-done.12.refs_2_.refs_10_
  36.2 0.6 shard_map.79
  36.8 1.5 %collective-permute-start.14 = (bf16[64,512]{1,0:T(8,128)(2,1)S(1)}, bf16[64,512]{1,0:T(8,128)(2,1)S(1)}, u32[]{:S(2)}, u32[]{:S(2)}) collective-permute-start(bf16[64,512]{1,0:T(8,128)(2,1)S(1)} %get-tuple-element.80), channel_id=1, source_target_pairs={{0,16},{32,48},{64,80},{96,112},{16,0},{48,32},{80,64},{112,96},{1... | collective-permute-start | bytes 196616 | tf_op jit(solution)/shard_map/ppermute | solution.py:398
  38.3 3.8 %collective-permute-start.15 = (bf16[64,512]{1,0:T(8,128)(2,1)S(1)}, bf16[64,512]{1,0:T(8,128)(2,1)S(1)}, u32[]{:S(2)}, u32[]{:S(2)}) collective-permute-start(bf16[64,512]{1,0:T(8,128)(2,1)S(1)} %get-tuple-element.81), channel_id=1, source_target_pairs={{16,32},{48,64},{80,96},{112,0},{32,16},{64,48},{96,80},{0,112},{1... | collective-permute-start | bytes 196616 | tf_op jit(solution)/shard_map/ppermute | solution.py:398
  42.1 0.0 collective-permute-start.16
  42.1 1.7 %collective-permute-start.17 = (bf16[64,128]{1,0:T(8,128)(2,1)S(1)}, bf16[64,128]{1,0:T(8,128)(2,1)S(1)}, u32[]{:S(2)}, u32[]{:S(2)}) collective-permute-start(bf16[64,128]{1,0:T(8,128)(2,1)S(1)} %get-tuple-element.83), channel_id=1, source_target_pairs={{1,2},{3,4},{5,6},{7,8},{9,10},{11,12},{13,14},{15,0},{2,1},{4,3},... | collective-permute-start | bytes 49160 | tf_op jit(solution)/shard_map/ppermute | solution.py:398
  43.8 0.0 copy-done.3
  43.8 2.5 %shard_map.78.x_ref = bf16[256,4096]{1,0:T(8,128)(2,1)S(1)} custom-call(bf16[256,4096]{1,0:T(8,128)(2,1)S(1)} %shard_map.73.x_ref, s32[1,1024]{1,0:T(1,128)S(1)} %bitcast.15, bf16[256,4096]{1,0:T(8,128)(2,1)S(1)} %copy-done.3, bf16[256,256]{1,0:T(8,128)(2,1)S(1)} %collective-permute-done.10.refs_0_.refs_8_, ...), custom_call_target="tpu_custom_call" | custom-call | flops 2147483648 | tf_op jit(solution)/shard_map/pallas_call | solution.py:66
  46.2 0.0 collective-permute-done.16.refs_2_
  46.2 1.1 %collective-permute-done.17.refs_3_ = bf16[64,128]{1,0:T(8,128)(2,1)S(1)} collective-permute-done((bf16[64,128]{1,0:T(8,128)(2,1)S(1)}, bf16[64,128]{1,0:T(8,128)(2,1)S(1)}, u32[]{:S(2)}, u32[]{:S(2)}) %collective-permute-start.17) | collective-permute-done | bytes 16416 | tf_op jit(solution)/shard_map/ppermute | solution.py:398
  47.4 0.0 collective-permute-done.14.refs_0_
  47.4 0.0 collective-permute-done.15.refs_1_
  47.4 0.2 broadcast_in_dim.29.profile_ref
  47.6 6.6 %shard_map.80 = (bf16[256,4096]{1,0:T(8,128)(2,1)S(1)}, bf16[64,512]{1,0:T(8,128)(2,1)S(1)}, bf16[64,512]{1,0:T(8,128)(2,1)S(1)}, bf16[64,128]{1,0:T(8,128)(2,1)S(1)}, bf16[64,128]{1,0:T(8,128)(2,1)S(1)}) custom-call(s32[4]{0:T(128)S(1)} %copy-done.1, bf16[256,4096]{1,0:T(8,128)(2,1)S(1)} %shard_map.78.x_ref, s32[1,1024]{1,0:T(1,128)S(1)} %bitcast.16, ...), custom_call_target="tpu_custom_call" | custom-call | flops 4294967296 | tf_op jit(solution)/shard_map/pallas_call | solution.py:459
  54.2 0.1 collective-permute-start.18
  54.3 3.0 %collective-permute-start.19 = (bf16[64,512]{1,0:T(8,128)(2,1)S(1)}, bf16[64,512]{1,0:T(8,128)(2,1)S(1)}, u32[]{:S(2)}, u32[]{:S(2)}) collective-permute-start(bf16[64,512]{1,0:T(8,128)(2,1)S(1)} %get-tuple-element.86), channel_id=1, source_target_pairs={{16,32},{48,64},{80,96},{112,0},{32,16},{64,48},{96,80},{0,112},{1... | collective-permute-start | bytes 196616 | tf_op jit(solution)/shard_map/ppermute | solution.py:398
  57.3 0.0 collective-permute-start.20
  57.3 1.3 %collective-permute-start.21 = (bf16[64,128]{1,0:T(8,128)(2,1)S(1)}, bf16[64,128]{1,0:T(8,128)(2,1)S(1)}, u32[]{:S(2)}, u32[]{:S(2)}) collective-permute-start(bf16[64,128]{1,0:T(8,128)(2,1)S(1)} %get-tuple-element.88), channel_id=1, source_target_pairs={{1,2},{3,4},{5,6},{7,8},{9,10},{11,12},{13,14},{15,0},{2,1},{4,3},... | collective-permute-start | bytes 49160 | tf_op jit(solution)/shard_map/ppermute | solution.py:398
  58.6 0.0 collective-permute-done.20.refs_2_
  58.6 4.0 %collective-permute-done.21.refs_3_ = bf16[64,128]{1,0:T(8,128)(2,1)S(1)} collective-permute-done((bf16[64,128]{1,0:T(8,128)(2,1)S(1)}, bf16[64,128]{1,0:T(8,128)(2,1)S(1)}, u32[]{:S(2)}, u32[]{:S(2)}) %collective-permute-start.21) | collective-permute-done | bytes 16416 | tf_op jit(solution)/shard_map/ppermute | solution.py:398
  62.6 0.0 collective-permute-done.18.refs_0_
  62.6 0.0 collective-permute-done.19.refs_1_
  62.6 3.1 %shard_map.81 = bf16[256,4,8,128]{3,2,1,0:T(8,128)(2,1)} custom-call(s32[4]{0:T(128)S(1)} %copy-done.1, bf16[256,4096]{1,0:T(8,128)(2,1)S(1)} %get-tuple-element.84.x_ref, bf16[4,256,128]{2,1,0:T(8,128)(2,1)S(1)} %broadcast_in_dim.29.profile_ref, bf16[64,512]{1,0:T(8,128)(2,1)S(1)} %collective-permute-done.18.refs_0_, ...), custom_call_target="tpu_custom_call" | custom-call | tf_op jit(solution)/shard_map/pallas_call | solution.py:469
  (11 shorter events, 0.1 us)
Async XLA Ops:
  1.7 4.1 %collective-permute-start.1 = (f32[32,256]{1,0:T(8,128)S(1)}, f32[32,256]{1,0:T(8,128)S(1)}, u32[]{:S(2)}, u32[]{:S(2)}) collective-permute-start(f32[32,256]{1,0:T(8,128)S(1)} %maximum_multiply_fusion.refs_0_), channel_id=1, source_target_pairs={{0,1},{1,0},{2,3},{3,2},{4,5},{5,4},{6,7},{7,6},{8,9},{9,8},{10,11... | collective-permute-start | bytes 98312 | tf_op jit(solution)/shard_map/ppermute | solution.py:27
  1.8 12.8 %collective-permute-start = (f32[32,256]{1,0:T(8,128)S(1)}, f32[32,256]{1,0:T(8,128)S(1)}, u32[]{:S(2)}, u32[]{:S(2)}) collective-permute-start(f32[32,256]{1,0:T(8,128)S(1)} %maximum_multiply_fusion.refs_0_), channel_id=1, source_target_pairs={{0,4},{1,5},{2,6},{3,7},{4,0},{5,1},{6,2},{7,3},{8,12},{9,13},{10,... | collective-permute-start | bytes 98312 | tf_op jit(solution)/shard_map/ppermute | solution.py:27
  5.8 5.2 %collective-permute-start.2 = (f32[64,256]{1,0:T(8,128)S(1)}, f32[64,256]{1,0:T(8,128)S(1)}, u32[]{:S(2)}, u32[]{:S(2)}) collective-permute-start(f32[64,256]{1,0:T(8,128)S(1)} %pad_maximum_fusion), channel_id=1, source_target_pairs={{0,8},{1,11},{2,10},{3,9},{4,12},{5,15},{6,14},{7,13},{8,0},{9,3},... | collective-permute-start | bytes 196616 | tf_op jit(solution)/shard_map/ppermute | solution.py:27
  7.4 4.3 %collective-permute-start.3 = (f32[64,256]{1,0:T(8,128)S(1)}, f32[64,256]{1,0:T(8,128)S(1)}, u32[]{:S(2)}, u32[]{:S(2)}) collective-permute-start(f32[64,256]{1,0:T(8,128)S(1)} %pad_maximum_fusion), channel_id=1, source_target_pairs={{0,2},{1,15},{2,0},{3,13},{4,6},{5,11},{6,4},{7,9},{8,10},{9,7},{1... | collective-permute-start | bytes 196616 | tf_op jit(solution)/shard_map/ppermute | solution.py:27
  8.4 6.1 %collective-permute-start.4 = (f32[64,256]{1,0:T(8,128)S(1)}, f32[64,256]{1,0:T(8,128)S(1)}, u32[]{:S(2)}, u32[]{:S(2)}) collective-permute-start(f32[64,256]{1,0:T(8,128)S(1)} %pad_maximum_fusion), channel_id=1, source_target_pairs={{0,6},{1,13},{2,4},{3,15},{4,2},{5,9},{6,0},{7,11},{8,14},{9,5},{1... | collective-permute-start | bytes 196616 | tf_op jit(solution)/shard_map/ppermute | solution.py:27
  9.0 6.1 %copy-start = (s32[8,128]{1,0:T(8,128)S(1)}, s32[8,128]{1,0:T(8,128)}, u32[]{:S(2)}) copy-start(s32[8,128]{1,0:T(8,128)} %param.8) | copy-start | bytes 12292
  15.0 1.6 %collective-permute-start.5 = (f32[256,256]{1,0:T(8,128)S(1)}, f32[256,256]{1,0:T(8,128)S(1)}, u32[]{:S(2)}, u32[]{:S(2)}) collective-permute-start(f32[256,256]{1,0:T(8,128)S(1)} %shard_map.74), channel_id=1, source_target_pairs={{0,1},{1,0},{2,3},{3,2},{4,5},{5,4},{6,7},{7,6},{8,9},{9,8},{10,11... | collective-permute-start | bytes 786440 | tf_op jit(solution)/shard_map/ppermute | solution.py:27
  16.6 7.7 %collective-permute-start.6 = (bf16[256,256]{1,0:T(8,128)(2,1)S(1)}, bf16[256,256]{1,0:T(8,128)(2,1)S(1)}, u32[]{:S(2)}, u32[]{:S(2)}) collective-permute-start(bf16[256,256]{1,0:T(8,128)(2,1)S(1)} %add_convert_fusion.refs_0_.refs_4_), channel_id=1, source_target_pairs={{0,16},{1,49},{2,18},{3,51},{4,20},{5,53},{6,22},{7,55},{8,24},{9,... | collective-permute-start | bytes 393224 | tf_op jit(solution)/shard_map/ppermute | solution.py:27
  19.5 6.4 %collective-permute-start.7 = (bf16[256,256]{1,0:T(8,128)(2,1)S(1)}, bf16[256,256]{1,0:T(8,128)(2,1)S(1)}, u32[]{:S(2)}, u32[]{:S(2)}) collective-permute-start(bf16[256,256]{1,0:T(8,128)(2,1)S(1)} %add_convert_fusion.refs_0_.refs_4_), channel_id=1, source_target_pairs={{0,32},{1,113},{2,34},{3,115},{4,36},{5,117},{6,38},{7,119},{8,40}... | collective-permute-start | bytes 393224 | tf_op jit(solution)/shard_map/ppermute | solution.py:27
  21.1 10.4 %collective-permute-start.8 = (bf16[256,256]{1,0:T(8,128)(2,1)S(1)}, bf16[256,256]{1,0:T(8,128)(2,1)S(1)}, u32[]{:S(2)}, u32[]{:S(2)}) collective-permute-start(bf16[256,256]{1,0:T(8,128)(2,1)S(1)} %add_convert_fusion.refs_0_.refs_4_), channel_id=1, source_target_pairs={{0,96},{1,81},{2,98},{3,83},{4,100},{5,85},{6,102},{7,87},{8,104},... | collective-permute-start | bytes 393224 | tf_op jit(solution)/shard_map/ppermute | solution.py:27
  23.2 11.5 %collective-permute-start.9 = (bf16[128,256]{1,0:T(8,128)(2,1)S(1)}, bf16[128,256]{1,0:T(8,128)(2,1)S(1)}, u32[]{:S(2)}, u32[]{:S(2)}) collective-permute-start(bf16[128,256]{1,0:T(8,128)(2,1)S(1)} %constant_dynamic-slice_fusion), channel_id=1, source_target_pairs={{0,64},{1,65},{2,66},{3,67},{4,68},{5,69},{6,70},{7,71},{8,72},{9,... | collective-permute-start | bytes 196616 | tf_op jit(solution)/shard_map/ppermute | solution.py:27
  31.4 3.9 %copy-start.4 = (bf16[4,64,4]{1,2,0:T(4,128)(2,1)S(1)}, bf16[4,64,4]{1,2,0:T(4,128)(2,1)}, u32[]{:S(2)}) copy-start(bf16[4,64,4]{1,2,0:T(4,128)(2,1)} %param.10) | copy-start | bytes 6148
  31.4 4.8 %collective-permute-start.10 = (bf16[256,256]{1,0:T(8,128)(2,1)S(1)}, bf16[256,256]{1,0:T(8,128)(2,1)S(1)}, u32[]{:S(2)}, u32[]{:S(2)}) collective-permute-start(bf16[256,256]{1,0:T(8,128)(2,1)S(1)} %collective-permute-done.6.refs_1_.refs_5_), channel_id=1, source_target_pairs={{0,1},{1,0},{2,3},{3,2},{4,5},{5,4},{6,7},{7,6},{8,9},{9,8},{10,11... | collective-permute-start | bytes 393224 | tf_op jit(solution)/shard_map/ppermute | solution.py:27
  31.5 4.8 %collective-permute-start.11 = (bf16[256,256]{1,0:T(8,128)(2,1)S(1)}, bf16[256,256]{1,0:T(8,128)(2,1)S(1)}, u32[]{:S(2)}, u32[]{:S(2)}) collective-permute-start(bf16[256,256]{1,0:T(8,128)(2,1)S(1)} %collective-permute-done.7.refs_0_.refs_6_), channel_id=1, source_target_pairs={{0,1},{1,0},{2,3},{3,2},{4,5},{5,4},{6,7},{7,6},{8,9},{9,8},{10,11... | collective-permute-start | bytes 393224 | tf_op jit(solution)/shard_map/ppermute | solution.py:27
  32.0 4.3 %collective-permute-start.12 = (bf16[256,256]{1,0:T(8,128)(2,1)S(1)}, bf16[256,256]{1,0:T(8,128)(2,1)S(1)}, u32[]{:S(2)}, u32[]{:S(2)}) collective-permute-start(bf16[256,256]{1,0:T(8,128)(2,1)S(1)} %collective-permute-done.8.refs_1_.refs_7_), channel_id=1, source_target_pairs={{0,1},{1,0},{2,3},{3,2},{4,5},{5,4},{6,7},{7,6},{8,9},{9,8},{10,11... | collective-permute-start | bytes 393224 | tf_op jit(solution)/shard_map/ppermute | solution.py:27
  33.5 1.3 %copy-start.2 = (bf16[256,4096]{1,0:T(8,128)(2,1)}, bf16[256,4096]{1,0:T(8,128)(2,1)S(1)}, u32[]{:S(2)}) copy-start(bf16[256,4096]{1,0:T(8,128)(2,1)S(1)} %get-tuple-element.74.done_ref) | copy-start | bytes 6291460
  34.8 1.4 %collective-permute-start.13 = (bf16[128,256]{1,0:T(8,128)(2,1)S(1)}, bf16[128,256]{1,0:T(8,128)(2,1)S(1)}, u32[]{:S(2)}, u32[]{:S(2)}) collective-permute-start(bf16[128,256]{1,0:T(8,128)(2,1)S(1)} %collective-permute-done.9.refs_4_.refs_12_), channel_id=1, source_target_pairs={{0,1},{1,0},{2,3},{3,2},{4,5},{5,4},{6,7},{7,6},{8,9},{9,8},{10,11... | collective-permute-start | bytes 196616 | tf_op jit(solution)/shard_map/ppermute | solution.py:27
  35.4 8.4 %copy-start.3 = (bf16[256,4096]{1,0:T(8,128)(2,1)S(1)}, bf16[256,4096]{1,0:T(8,128)(2,1)}, u32[]{:S(2)}) copy-start(bf16[256,4096]{1,0:T(8,128)(2,1)} %copy-done.2) | copy-start | bytes 6291460
  36.8 10.5 %collective-permute-start.14 = (bf16[64,512]{1,0:T(8,128)(2,1)S(1)}, bf16[64,512]{1,0:T(8,128)(2,1)S(1)}, u32[]{:S(2)}, u32[]{:S(2)}) collective-permute-start(bf16[64,512]{1,0:T(8,128)(2,1)S(1)} %get-tuple-element.80), channel_id=1, source_target_pairs={{0,16},{32,48},{64,80},{96,112},{16,0},{48,32},{80,64},{112,96},{1... | collective-permute-start | bytes 196616 | tf_op jit(solution)/shard_map/ppermute | solution.py:398
  38.3 9.1 %collective-permute-start.15 = (bf16[64,512]{1,0:T(8,128)(2,1)S(1)}, bf16[64,512]{1,0:T(8,128)(2,1)S(1)}, u32[]{:S(2)}, u32[]{:S(2)}) collective-permute-start(bf16[64,512]{1,0:T(8,128)(2,1)S(1)} %get-tuple-element.81), channel_id=1, source_target_pairs={{16,32},{48,64},{80,96},{112,0},{32,16},{64,48},{96,80},{0,112},{1... | collective-permute-start | bytes 196616 | tf_op jit(solution)/shard_map/ppermute | solution.py:398
  42.1 4.1 %collective-permute-start.16 = (bf16[64,128]{1,0:T(8,128)(2,1)S(1)}, bf16[64,128]{1,0:T(8,128)(2,1)S(1)}, u32[]{:S(2)}, u32[]{:S(2)}) collective-permute-start(bf16[64,128]{1,0:T(8,128)(2,1)S(1)} %get-tuple-element.82), channel_id=1, source_target_pairs={{0,1},{2,3},{4,5},{6,7},{8,9},{10,11},{12,13},{14,15},{1,0},{3,2},... | collective-permute-start | bytes 49160 | tf_op jit(solution)/shard_map/ppermute | solution.py:398
  42.1 5.5 %copy-start.1 = (s32[4]{0:T(128)S(1)}, s32[4]{0:T(128)}, u32[]{:S(2)}) copy-start(s32[4]{0:T(128)} %port_ref.3) | copy-start | bytes 52
  42.1 5.3 %collective-permute-start.17 = (bf16[64,128]{1,0:T(8,128)(2,1)S(1)}, bf16[64,128]{1,0:T(8,128)(2,1)S(1)}, u32[]{:S(2)}, u32[]{:S(2)}) collective-permute-start(bf16[64,128]{1,0:T(8,128)(2,1)S(1)} %get-tuple-element.83), channel_id=1, source_target_pairs={{1,2},{3,4},{5,6},{7,8},{9,10},{11,12},{13,14},{15,0},{2,1},{4,3},... | collective-permute-start | bytes 49160 | tf_op jit(solution)/shard_map/ppermute | solution.py:398
  54.2 8.4 %collective-permute-start.18 = (bf16[64,512]{1,0:T(8,128)(2,1)S(1)}, bf16[64,512]{1,0:T(8,128)(2,1)S(1)}, u32[]{:S(2)}, u32[]{:S(2)}) collective-permute-start(bf16[64,512]{1,0:T(8,128)(2,1)S(1)} %get-tuple-element.85), channel_id=1, source_target_pairs={{0,16},{32,48},{64,80},{96,112},{16,0},{48,32},{80,64},{112,96},{1... | collective-permute-start | bytes 196616 | tf_op jit(solution)/shard_map/ppermute | solution.py:398
  54.3 8.3 %collective-permute-start.19 = (bf16[64,512]{1,0:T(8,128)(2,1)S(1)}, bf16[64,512]{1,0:T(8,128)(2,1)S(1)}, u32[]{:S(2)}, u32[]{:S(2)}) collective-permute-start(bf16[64,512]{1,0:T(8,128)(2,1)S(1)} %get-tuple-element.86), channel_id=1, source_target_pairs={{16,32},{48,64},{80,96},{112,0},{32,16},{64,48},{96,80},{0,112},{1... | collective-permute-start | bytes 196616 | tf_op jit(solution)/shard_map/ppermute | solution.py:398
  57.3 1.3 %collective-permute-start.20 = (bf16[64,128]{1,0:T(8,128)(2,1)S(1)}, bf16[64,128]{1,0:T(8,128)(2,1)S(1)}, u32[]{:S(2)}, u32[]{:S(2)}) collective-permute-start(bf16[64,128]{1,0:T(8,128)(2,1)S(1)} %get-tuple-element.87), channel_id=1, source_target_pairs={{0,1},{2,3},{4,5},{6,7},{8,9},{10,11},{12,13},{14,15},{1,0},{3,2},... | collective-permute-start | bytes 49160 | tf_op jit(solution)/shard_map/ppermute | solution.py:398
  57.3 5.3 %collective-permute-start.21 = (bf16[64,128]{1,0:T(8,128)(2,1)S(1)}, bf16[64,128]{1,0:T(8,128)(2,1)S(1)}, u32[]{:S(2)}, u32[]{:S(2)}) collective-permute-start(bf16[64,128]{1,0:T(8,128)(2,1)S(1)} %get-tuple-element.88), channel_id=1, source_target_pairs={{1,2},{3,4},{5,6},{7,8},{9,10},{11,12},{13,14},{15,0},{2,1},{4,3},... | collective-permute-start | bytes 49160 | tf_op jit(solution)/shard_map/ppermute | solution.py:398

commit v10 on v9

--- a/solution.py
+++ b/solution.py
@@ -15,16 +15,19 @@
 WIDE_PARAMS = pltpu.CompilerParams(vmem_limit_bytes=50 * 2**20)
 
 
-def swap(value, axis, first, second=None):
+def swap(value, first, second=None):
     second = first if second is None else second
     rows, cols = lax.axis_size("row"), lax.axis_size("col")
     pairs = []
     for row in range(rows):
         for col in range(cols):
-            step = second if col % 2 else first
-            other = (row ^ step, col) if axis == "row" else (row, col ^ step)
-            pairs.append((row * cols + col, other[0] * cols + other[1]))
+            down, along = second if col % 2 else first
+            pairs.append((row * cols + col, (row ^ down) * cols + (col ^ along)))
     return lax.ppermute(value, ("row", "col"), pairs)
+
+
+def swap_cores(value):
+    return swap(value, (0, 1))
 
 
 def flat_kernel(x_hbm, out_ref, x_ref, sems):
@@ -79,10 +82,11 @@
     part = lax.broadcasted_iota(jnp.int32, own.shape, 0)
     own = own * jnp.where(part == 0, mode_values[0][None, :, None], 1.0)
     own = own.reshape(2 * modes, order)
-    far = swap(own, "col", 4)
-    pair = jnp.concatenate([own, swap(own, "col", 1)], axis=0)
+    far = swap(own, (0, 4))
+    pair = jnp.concatenate([own, swap_cores(own)], axis=0)
     pair, traces = lax.optimization_barrier((pair, traces))
-    got = [swap(pair, "col", 8, 10), swap(pair, "col", 2, 14), swap(pair, "col", 6, 12)]
+    steps = (((0, 8), (0, 10)), ((0, 2), (0, 14)), ((0, 6), (0, 12)))
+    got = [swap(pair, *step) for step in steps]
     shape = (order,) + traces.shape[2:]
     x = pl.pallas_call(
         flat_kernel,
@@ -102,7 +106,7 @@
         *got,
     )
     partial, x = lax.optimization_barrier((partial, x))
-    other = swap(partial, "col", 1)
+    other = swap_cores(partial)
     sides = whole_call(
         functools.partial(sides_kernel, traces.shape[2]),
         [jax.ShapeDtypeStruct((order, LANES), BF), jax.ShapeDtypeStruct((16, LANES), BF)],
@@ -407,8 +411,10 @@
     own_map, x, sides = own_type_map(mode_shapes, mode_values, mode_weights, traces, types)
     core = lax.rem(lax.axis_index("col"), 2)
     half = lax.dynamic_slice_in_dim(own_map, core * (order // 2), order // 2)
-    fetched = [swap(own_map, "row", *steps) for steps in MAP_STEPS[1:4]]
-    half = swap(half, "row", 4)
+    fetched = [
+        swap(own_map, *((step, 8 * (step % 2)) for step in steps)) for steps in MAP_STEPS[1:4]
+    ]
+    half = swap(half, (4, 0))
     profile = jnp.broadcast_to(
         jnp.transpose(port_profile.reshape(order, ports))[:, :, None], (ports, order, LANES)
     )
@@ -426,12 +432,12 @@
         flops = work * len(maps) // 7
         return whole_call(kernel, part_shapes, x, types, *sides, *maps, *parts, flops=flops)
 
-    parts = early(0, [own_map, fetched[0]])
-    parts, fetched = lax.optimization_barrier((parts, fetched))
-    swapped = [swap(value, "col", 1) for value in fetched]
-    parts = early(2, fetched[1:], parts)
-    parts, half = lax.optimization_barrier((parts, half))
-    swapped.append(swap(half, "col", 1))
+    parts = list(early(0, [own_map, fetched[0]]))
+    parts[1], fetched = lax.optimization_barrier((parts[1], fetched))
+    swapped = [swap_cores(value) for value in fetched]
+    parts = list(early(2, fetched[1:], parts))
+    parts[1], half = lax.optimization_barrier((parts[1], half))
+    swapped.append(swap_cores(half))
     done, *parts = parts
     late = swapped + [half]
     maps = [own_map] + fetched + late

time: 66.2 us -> 65.5 us (0.989)
  starting transfers between devices: 27.1 us -> 25.3 us
  waiting for transfers between devices: 15.7 us -> 16.8 us
    ppermute x8, starting transfers between devices: 11.3 us -> 10.2 us  [exchange(): lax.ppermute(rim, axis, pairs(axis, first))]
    ppermute x8, waiting for transfers between devices: 5.11 us -> 6.22 us  [exchange(): lax.ppermute(rim, axis, pairs(axis, first))]
  transfers between devices with their start and end apart: 22 -> 22, of which waited for: 8 -> 9; matrix products, arithmetic and copies ran while one was open for 0% -> 0% of each run, Pallas kernels for 13% -> 13%
where the time goes in v10:
time: 65.5 us; the launch traced here: 65.2 us
  starting transfers between devices  25.3 us (39%)
  Pallas kernels  19.3 us (29%)
  waiting for transfers between devices  16.8 us (26%)
  local copies, waits for them, and re-layouts  2.52 us (4%)
  other arithmetic  0.85 us (1%)
    ppermute x14, starting transfers between devices, swap(): return lax.ppermute(value, ('row', 'col'), pairs)  15.2 us
    ppermute x14, waiting for transfers between devices, swap(): return lax.ppermute(value, ('row', 'col'), pairs)  10.6 us
    ppermute x8, starting transfers between devices, exchange(): lax.ppermute(rim, axis, pairs(axis, first))  10.2 us
    pallas_call x6, Pallas kernels, whole_call(): pl.pallas_call(kernel, in_specs=[WHOLE] * len(operands), out_specs=[WHOLE...  7.66 us
    pallas_call x1, Pallas kernels, body(): pl.pallas_call(functools.partial(second_kernel, rows, width), in_specs=[p...  6.62 us
    ppermute x8, waiting for transfers between devices, exchange(): lax.ppermute(rim, axis, pairs(axis, first))  6.22 us
    pallas_call x1, Pallas kernels, body(): pl.pallas_call(functools.partial(last_kernel, rows, width), in_specs=[por...  3.08 us
    pallas_call x1, Pallas kernels, own_type_map(): pl.pallas_call(flat_kernel, in_specs=[pl.BlockSpec(memory_space=pltpu.HBM...  1.98 us
  transfers between devices with their start and end apart: 22, of which 9 were waited for; matrix products, arithmetic and copies ran while one was open for 0% of the time, Pallas kernels for 13%

profile of v10, /device:TPU:0, one launch (start us, length us, event | category | flops | bytes accessed | tf_op | source)
XLA Modules:
  0.0 65.2 jit_solution(6765570634275089713)
XLA Ops:
  0.0 0.7 %broadcast_in_dim.25 = f32[2,16]{1,0:T(2,128)S(1)} broadcast(f32[16]{0:T(128)} %bitcast.21), dimensions={1} | broadcast | bytes 192 | tf_op jit(solution)/shard_map/jit(_where)/broadcast_in_dim | solution.py:83
  0.7 0.1 broadcast_in_dim.26
  0.7 0.1 iota.11
  0.8 0.1 iota.12
  0.9 0.8 %maximum_multiply_fusion.refs_0_ = f32[32,256]{1,0:T(8,128)S(1)} fusion(f32[16,256]{1,0:T(8,128)} %bitcast.18, f32[16,256]{1,0:T(8,128)} %bitcast.19, f32[32]{0:T(128)S(1)} %broadcast_in_dim.26, pred[32]{0:T(512)(128)(4,1)S(1)} %iota.12), kind=kLoop, calls=%fused_computation.2 | loop fusion | flops 24576 | bytes 65696 | tf_op jit(solution)/shard_map/mul | solution.py:83
  1.7 0.1 collective-permute-start.1
  1.8 4.0 %collective-permute-start = (f32[32,256]{1,0:T(8,128)S(1)}, f32[32,256]{1,0:T(8,128)S(1)}, u32[]{:S(2)}, u32[]{:S(2)}) collective-permute-start(f32[32,256]{1,0:T(8,128)S(1)} %maximum_multiply_fusion.refs_0_), channel_id=1, source_target_pairs={{0,4},{1,5},{2,6},{3,7},{4,0},{5,1},{6,2},{7,3},{8,12},{9,13},{10,... | collective-permute-start | bytes 98312 | tf_op jit(solution)/shard_map/ppermute | solution.py:26
  5.8 0.0 collective-permute-done.1
  5.8 1.6 %collective-permute-start.2 = (f32[64,256]{1,0:T(8,128)S(1)}, f32[64,256]{1,0:T(8,128)S(1)}, u32[]{:S(2)}, u32[]{:S(2)}) collective-permute-start(f32[64,256]{1,0:T(8,128)S(1)} %pad_maximum_fusion), channel_id=1, source_target_pairs={{0,8},{1,11},{2,10},{3,9},{4,12},{5,15},{6,14},{7,13},{8,0},{9,3},... | collective-permute-start | bytes 196616 | tf_op jit(solution)/shard_map/ppermute | solution.py:26
  7.4 1.0 %collective-permute-start.3 = (f32[64,256]{1,0:T(8,128)S(1)}, f32[64,256]{1,0:T(8,128)S(1)}, u32[]{:S(2)}, u32[]{:S(2)}) collective-permute-start(f32[64,256]{1,0:T(8,128)S(1)} %pad_maximum_fusion), channel_id=1, source_target_pairs={{0,2},{1,15},{2,0},{3,13},{4,6},{5,11},{6,4},{7,9},{8,10},{9,7},{1... | collective-permute-start | bytes 196616 | tf_op jit(solution)/shard_map/ppermute | solution.py:26
  8.4 0.6 collective-permute-start.4
  9.0 2.0 %shard_map.73.x_ref = bf16[256,4096]{1,0:T(8,128)(2,1)S(1)} custom-call(bf16[256,4,8,128]{3,2,1,0:T(8,128)(2,1)} %bitcast.17), custom_call_target="tpu_custom_call" | custom-call | flops 1073741824 | tf_op jit(solution)/shard_map/pallas_call | solution.py:91
  11.0 0.0 collective-permute-done.2.refs_2_
  11.0 0.7 %collective-permute-done.3.refs_3_ = f32[64,256]{1,0:T(8,128)S(1)} collective-permute-done((f32[64,256]{1,0:T(8,128)S(1)}, f32[64,256]{1,0:T(8,128)S(1)}, u32[]{:S(2)}, u32[]{:S(2)}) %collective-permute-start.3) | collective-permute-done | bytes 65568 | tf_op jit(solution)/shard_map/ppermute | solution.py:26
  11.7 2.9 %collective-permute-done.4.refs_4_ = f32[64,256]{1,0:T(8,128)S(1)} collective-permute-done((f32[64,256]{1,0:T(8,128)S(1)}, f32[64,256]{1,0:T(8,128)S(1)}, u32[]{:S(2)}, u32[]{:S(2)}) %collective-permute-start.4) | collective-permute-done | bytes 65568 | tf_op jit(solution)/shard_map/ppermute | solution.py:26
  14.5 0.0 collective-permute-done.refs_1_
  14.5 0.4 shard_map.74
  15.0 0.1 collective-permute-start.5
  15.0 0.0 copy-done
  15.1 1.2 %shard_map.75 = (bf16[256,128]{1,0:T(8,128)(2,1)S(1)}, bf16[16,128]{1,0:T(8,128)(2,1)S(1)}) custom-call(bf16[256,4096]{1,0:T(8,128)(2,1)S(1)} %shard_map.73.x_ref, s32[1,1024]{1,0:T(1,128)S(1)} %bitcast.11), custom_call_target="tpu_custom_call" | custom-call | flops 1073741824 | tf_op jit(solution)/shard_map/pallas_call | solution.py:69
  16.2 0.3 collective-permute-done.5
  16.6 2.2 %collective-permute-start.6 = (bf16[256,256]{1,0:T(8,128)(2,1)S(1)}, bf16[256,256]{1,0:T(8,128)(2,1)S(1)}, u32[]{:S(2)}, u32[]{:S(2)}) collective-permute-start(bf16[256,256]{1,0:T(8,128)(2,1)S(1)} %add_convert_fusion.refs_0_.refs_4_), channel_id=1, source_target_pairs={{0,24},{1,57},{2,26},{3,59},{4,28},{5,61},{6,30},{7,63},{8,16},{9,... | collective-permute-start | bytes 393224 | tf_op jit(solution)/shard_map/ppermute | solution.py:26
  18.9 1.6 %collective-permute-start.7 = (bf16[256,256]{1,0:T(8,128)(2,1)S(1)}, bf16[256,256]{1,0:T(8,128)(2,1)S(1)}, u32[]{:S(2)}, u32[]{:S(2)}) collective-permute-start(bf16[256,256]{1,0:T(8,128)(2,1)S(1)} %add_convert_fusion.refs_0_.refs_4_), channel_id=1, source_target_pairs={{0,32},{1,121},{2,34},{3,123},{4,36},{5,125},{6,38},{7,127},{8,40}... | collective-permute-start | bytes 393224 | tf_op jit(solution)/shard_map/ppermute | solution.py:26
  20.4 2.2 %collective-permute-start.8 = (bf16[256,256]{1,0:T(8,128)(2,1)S(1)}, bf16[256,256]{1,0:T(8,128)(2,1)S(1)}, u32[]{:S(2)}, u32[]{:S(2)}) collective-permute-start(bf16[256,256]{1,0:T(8,128)(2,1)S(1)} %add_convert_fusion.refs_0_.refs_4_), channel_id=1, source_target_pairs={{0,96},{1,89},{2,98},{3,91},{4,100},{5,93},{6,102},{7,95},{8,104},... | collective-permute-start | bytes 393224 | tf_op jit(solution)/shard_map/ppermute | solution.py:26
  22.6 0.8 %collective-permute-start.12 = (bf16[128,256]{1,0:T(8,128)(2,1)S(1)}, bf16[128,256]{1,0:T(8,128)(2,1)S(1)}, u32[]{:S(2)}, u32[]{:S(2)}) collective-permute-start(bf16[128,256]{1,0:T(8,128)(2,1)S(1)} %constant_dynamic-slice_fusion), channel_id=1, source_target_pairs={{0,64},{1,65},{2,66},{3,67},{4,68},{5,69},{6,70},{7,71},{8,72},{9,... | collective-permute-start | bytes 196616 | tf_op jit(solution)/shard_map/ppermute | solution.py:26
  23.4 0.6 collective-permute-done.6.refs_1_.refs_5_
  24.1 1.5 %shard_map.76 = (bf16[256,4096]{1,0:T(8,128)(2,1)S(1)}, bf16[64,512]{1,0:T(8,128)(2,1)S(1)}, bf16[64,512]{1,0:T(8,128)(2,1)S(1)}, bf16[128,128]{1,0:T(8,128)(2,1)S(1)}) custom-call(bf16[256,4096]{1,0:T(8,128)(2,1)S(1)} %shard_map.73.x_ref, s32[1,1024]{1,0:T(1,128)S(1)} %bitcast.12, bf16[256,128]{1,0:T(8,128)(2,1)S(1)} %get-tuple-element.51.sides_ref, ...), custom_call_target="tpu_custom_call" | custom-call | flops 1227133568 | tf_op jit(solution)/shard_map/pallas_call | solution.py:69
  25.6 0.0 collective-permute-done.7.refs_0_.refs_6_
  25.6 5.2 %collective-permute-done.8.refs_1_.refs_7_ = bf16[256,256]{1,0:T(8,128)(2,1)S(1)} collective-permute-done((bf16[256,256]{1,0:T(8,128)(2,1)S(1)}, bf16[256,256]{1,0:T(8,128)(2,1)S(1)}, u32[]{:S(2)}, u32[]{:S(2)}) %collective-permute-start.8) | collective-permute-done | bytes 131104 | tf_op jit(solution)/shard_map/ppermute | solution.py:26
  30.8 0.0 collective-permute-start.10
  30.8 0.5 collective-permute-start.11
  31.3 0.0 collective-permute-start.9
  31.3 1.5 %shard_map.77 = (bf16[256,4096]{1,0:T(8,128)(2,1)S(1)}, bf16[64,512]{1,0:T(8,128)(2,1)S(1)}, bf16[64,512]{1,0:T(8,128)(2,1)S(1)}, bf16[128,128]{1,0:T(8,128)(2,1)S(1)}) custom-call(bf16[256,4096]{1,0:T(8,128)(2,1)S(1)} %shard_map.73.x_ref, s32[1,1024]{1,0:T(1,128)S(1)} %bitcast.13, bf16[256,128]{1,0:T(8,128)(2,1)S(1)} %get-tuple-element.51.sides_ref, ...), custom_call_target="tpu_custom_call" | custom-call | flops 1227133568 | tf_op jit(solution)/shard_map/pallas_call | solution.py:69
  32.8 0.0 copy-start.2
  32.9 1.3 %copy-done.2 = bf16[256,4096]{1,0:T(8,128)(2,1)} copy-done((bf16[256,4096]{1,0:T(8,128)(2,1)}, bf16[256,4096]{1,0:T(8,128)(2,1)S(1)}, u32[]{:S(2)}) %copy-start.2) | copy-done | bytes 2097176
  34.2 0.0 collective-permute-done.12.refs_4_.refs_12_
  34.2 0.5 collective-permute-start.13
  34.7 0.0 copy-done.4
  34.7 0.1 reshape.20
  34.8 0.8 %collective-permute-done.13.refs_3_.refs_11_ = bf16[128,256]{1,0:T(8,128)(2,1)S(1)} collective-permute-done((bf16[128,256]{1,0:T(8,128)(2,1)S(1)}, bf16[128,256]{1,0:T(8,128)(2,1)S(1)}, u32[]{:S(2)}, u32[]{:S(2)}) %collective-permute-start.13) | collective-permute-done | bytes 65568 | tf_op jit(solution)/shard_map/ppermute | solution.py:26
  35.6 0.0 collective-permute-done.10.refs_1_.refs_9_
  35.6 0.0 collective-permute-done.11.refs_2_.refs_10_
  35.6 0.0 collective-permute-done.9.refs_0_.refs_8_
  35.6 0.6 shard_map.79
  36.2 0.7 %collective-permute-start.14 = (bf16[64,512]{1,0:T(8,128)(2,1)S(1)}, bf16[64,512]{1,0:T(8,128)(2,1)S(1)}, u32[]{:S(2)}, u32[]{:S(2)}) collective-permute-start(bf16[64,512]{1,0:T(8,128)(2,1)S(1)} %get-tuple-element.68), channel_id=1, source_target_pairs={{0,16},{32,48},{64,80},{96,112},{16,0},{48,32},{80,64},{112,96},{1... | collective-permute-start | bytes 196616 | tf_op jit(solution)/shard_map/ppermute | solution.py:402
  37.0 4.5 %collective-permute-start.15 = (bf16[64,512]{1,0:T(8,128)(2,1)S(1)}, bf16[64,512]{1,0:T(8,128)(2,1)S(1)}, u32[]{:S(2)}, u32[]{:S(2)}) collective-permute-start(bf16[64,512]{1,0:T(8,128)(2,1)S(1)} %get-tuple-element.69), channel_id=1, source_target_pairs={{16,32},{48,64},{80,96},{112,0},{32,16},{64,48},{96,80},{0,112},{1... | collective-permute-start | bytes 196616 | tf_op jit(solution)/shard_map/ppermute | solution.py:402
  41.4 0.0 collective-permute-start.16
  41.4 1.1 %collective-permute-start.17 = (bf16[64,128]{1,0:T(8,128)(2,1)S(1)}, bf16[64,128]{1,0:T(8,128)(2,1)S(1)}, u32[]{:S(2)}, u32[]{:S(2)}) collective-permute-start(bf16[64,128]{1,0:T(8,128)(2,1)S(1)} %get-tuple-element.71), channel_id=1, source_target_pairs={{1,2},{3,4},{5,6},{7,8},{9,10},{11,12},{13,14},{15,0},{2,1},{4,3},... | collective-permute-start | bytes 49160 | tf_op jit(solution)/shard_map/ppermute | solution.py:402
  42.5 2.5 %shard_map.78.x_ref = bf16[256,4096]{1,0:T(8,128)(2,1)S(1)} custom-call(bf16[256,4096]{1,0:T(8,128)(2,1)S(1)} %shard_map.73.x_ref, s32[1,1024]{1,0:T(1,128)S(1)} %bitcast.15, bf16[256,4096]{1,0:T(8,128)(2,1)S(1)} %copy-done.3, bf16[256,256]{1,0:T(8,128)(2,1)S(1)} %collective-permute-done.9.refs_0_.refs_8_, ...), custom_call_target="tpu_custom_call" | custom-call | flops 2147483648 | tf_op jit(solution)/shard_map/pallas_call | solution.py:69
  45.0 0.0 collective-permute-done.16.refs_2_
  45.0 1.7 %collective-permute-done.17.refs_3_ = bf16[64,128]{1,0:T(8,128)(2,1)S(1)} collective-permute-done((bf16[64,128]{1,0:T(8,128)(2,1)S(1)}, bf16[64,128]{1,0:T(8,128)(2,1)S(1)}, u32[]{:S(2)}, u32[]{:S(2)}) %collective-permute-start.17) | collective-permute-done | bytes 16416 | tf_op jit(solution)/shard_map/ppermute | solution.py:402
  46.7 0.0 collective-permute-done.14.refs_0_
  46.7 0.0 collective-permute-done.15.refs_1_
  46.7 0.2 broadcast_in_dim.29.profile_ref
  46.9 6.6 %shard_map.80 = (bf16[256,4096]{1,0:T(8,128)(2,1)S(1)}, bf16[64,512]{1,0:T(8,128)(2,1)S(1)}, bf16[64,512]{1,0:T(8,128)(2,1)S(1)}, bf16[64,128]{1,0:T(8,128)(2,1)S(1)}, bf16[64,128]{1,0:T(8,128)(2,1)S(1)}) custom-call(s32[4]{0:T(128)S(1)} %copy-done.1, bf16[256,4096]{1,0:T(8,128)(2,1)S(1)} %shard_map.78.x_ref, s32[1,1024]{1,0:T(1,128)S(1)} %bitcast.16, ...), custom_call_target="tpu_custom_call" | custom-call | flops 4294967296 | tf_op jit(solution)/shard_map/pallas_call | solution.py:465
  53.6 0.1 collective-permute-start.18
  53.7 3.0 %collective-permute-start.19 = (bf16[64,512]{1,0:T(8,128)(2,1)S(1)}, bf16[64,512]{1,0:T(8,128)(2,1)S(1)}, u32[]{:S(2)}, u32[]{:S(2)}) collective-permute-start(bf16[64,512]{1,0:T(8,128)(2,1)S(1)} %get-tuple-element.74), channel_id=1, source_target_pairs={{16,32},{48,64},{80,96},{112,0},{32,16},{64,48},{96,80},{0,112},{1... | collective-permute-start | bytes 196616 | tf_op jit(solution)/shard_map/ppermute | solution.py:402
  56.6 0.0 collective-permute-start.20
  56.6 0.8 %collective-permute-start.21 = (bf16[64,128]{1,0:T(8,128)(2,1)S(1)}, bf16[64,128]{1,0:T(8,128)(2,1)S(1)}, u32[]{:S(2)}, u32[]{:S(2)}) collective-permute-start(bf16[64,128]{1,0:T(8,128)(2,1)S(1)} %get-tuple-element.76), channel_id=1, source_target_pairs={{1,2},{3,4},{5,6},{7,8},{9,10},{11,12},{13,14},{15,0},{2,1},{4,3},... | collective-permute-start | bytes 49160 | tf_op jit(solution)/shard_map/ppermute | solution.py:402
  57.4 0.4 collective-permute-done.20.refs_2_
  57.8 4.1 %collective-permute-done.21.refs_3_ = bf16[64,128]{1,0:T(8,128)(2,1)S(1)} collective-permute-done((bf16[64,128]{1,0:T(8,128)(2,1)S(1)}, bf16[64,128]{1,0:T(8,128)(2,1)S(1)}, u32[]{:S(2)}, u32[]{:S(2)}) %collective-permute-start.21) | collective-permute-done | bytes 16416 | tf_op jit(solution)/shard_map/ppermute | solution.py:402
  61.9 0.0 collective-permute-done.18.refs_0_
  61.9 0.0 collective-permute-done.19.refs_1_
  61.9 3.1 %shard_map.81 = bf16[256,4,8,128]{3,2,1,0:T(8,128)(2,1)} custom-call(s32[4]{0:T(128)S(1)} %copy-done.1, bf16[256,4096]{1,0:T(8,128)(2,1)S(1)} %get-tuple-element.72.x_ref, bf16[4,256,128]{2,1,0:T(8,128)(2,1)S(1)} %broadcast_in_dim.29.profile_ref, bf16[64,512]{1,0:T(8,128)(2,1)S(1)} %collective-permute-done.18.refs_0_, ...), custom_call_target="tpu_custom_call" | custom-call | tf_op jit(solution)/shard_map/pallas_call | solution.py:475
  (11 shorter events, 0.1 us)
Async XLA Ops:
  1.7 4.1 %collective-permute-start.1 = (f32[32,256]{1,0:T(8,128)S(1)}, f32[32,256]{1,0:T(8,128)S(1)}, u32[]{:S(2)}, u32[]{:S(2)}) collective-permute-start(f32[32,256]{1,0:T(8,128)S(1)} %maximum_multiply_fusion.refs_0_), channel_id=1, source_target_pairs={{0,1},{1,0},{2,3},{3,2},{4,5},{5,4},{6,7},{7,6},{8,9},{9,8},{10,11... | collective-permute-start | bytes 98312 | tf_op jit(solution)/shard_map/ppermute | solution.py:26
  1.8 12.8 %collective-permute-start = (f32[32,256]{1,0:T(8,128)S(1)}, f32[32,256]{1,0:T(8,128)S(1)}, u32[]{:S(2)}, u32[]{:S(2)}) collective-permute-start(f32[32,256]{1,0:T(8,128)S(1)} %maximum_multiply_fusion.refs_0_), channel_id=1, source_target_pairs={{0,4},{1,5},{2,6},{3,7},{4,0},{5,1},{6,2},{7,3},{8,12},{9,13},{10,... | collective-permute-start | bytes 98312 | tf_op jit(solution)/shard_map/ppermute | solution.py:26
  5.8 5.2 %collective-permute-start.2 = (f32[64,256]{1,0:T(8,128)S(1)}, f32[64,256]{1,0:T(8,128)S(1)}, u32[]{:S(2)}, u32[]{:S(2)}) collective-permute-start(f32[64,256]{1,0:T(8,128)S(1)} %pad_maximum_fusion), channel_id=1, source_target_pairs={{0,8},{1,11},{2,10},{3,9},{4,12},{5,15},{6,14},{7,13},{8,0},{9,3},... | collective-permute-start | bytes 196616 | tf_op jit(solution)/shard_map/ppermute | solution.py:26
  7.4 4.3 %collective-permute-start.3 = (f32[64,256]{1,0:T(8,128)S(1)}, f32[64,256]{1,0:T(8,128)S(1)}, u32[]{:S(2)}, u32[]{:S(2)}) collective-permute-start(f32[64,256]{1,0:T(8,128)S(1)} %pad_maximum_fusion), channel_id=1, source_target_pairs={{0,2},{1,15},{2,0},{3,13},{4,6},{5,11},{6,4},{7,9},{8,10},{9,7},{1... | collective-permute-start | bytes 196616 | tf_op jit(solution)/shard_map/ppermute | solution.py:26
  8.4 6.1 %collective-permute-start.4 = (f32[64,256]{1,0:T(8,128)S(1)}, f32[64,256]{1,0:T(8,128)S(1)}, u32[]{:S(2)}, u32[]{:S(2)}) collective-permute-start(f32[64,256]{1,0:T(8,128)S(1)} %pad_maximum_fusion), channel_id=1, source_target_pairs={{0,6},{1,13},{2,4},{3,15},{4,2},{5,9},{6,0},{7,11},{8,14},{9,5},{1... | collective-permute-start | bytes 196616 | tf_op jit(solution)/shard_map/ppermute | solution.py:26
  9.0 6.1 %copy-start = (s32[8,128]{1,0:T(8,128)S(1)}, s32[8,128]{1,0:T(8,128)}, u32[]{:S(2)}) copy-start(s32[8,128]{1,0:T(8,128)} %param.8) | copy-start | bytes 12292
  15.0 1.6 %collective-permute-start.5 = (f32[256,256]{1,0:T(8,128)S(1)}, f32[256,256]{1,0:T(8,128)S(1)}, u32[]{:S(2)}, u32[]{:S(2)}) collective-permute-start(f32[256,256]{1,0:T(8,128)S(1)} %shard_map.74), channel_id=1, source_target_pairs={{0,1},{1,0},{2,3},{3,2},{4,5},{5,4},{6,7},{7,6},{8,9},{9,8},{10,11... | collective-permute-start | bytes 786440 | tf_op jit(solution)/shard_map/ppermute | solution.py:26
  16.6 7.4 %collective-permute-start.6 = (bf16[256,256]{1,0:T(8,128)(2,1)S(1)}, bf16[256,256]{1,0:T(8,128)(2,1)S(1)}, u32[]{:S(2)}, u32[]{:S(2)}) collective-permute-start(bf16[256,256]{1,0:T(8,128)(2,1)S(1)} %add_convert_fusion.refs_0_.refs_4_), channel_id=1, source_target_pairs={{0,24},{1,57},{2,26},{3,59},{4,28},{5,61},{6,30},{7,63},{8,16},{9,... | collective-permute-start | bytes 393224 | tf_op jit(solution)/shard_map/ppermute | solution.py:26
  18.9 6.7 %collective-permute-start.7 = (bf16[256,256]{1,0:T(8,128)(2,1)S(1)}, bf16[256,256]{1,0:T(8,128)(2,1)S(1)}, u32[]{:S(2)}, u32[]{:S(2)}) collective-permute-start(bf16[256,256]{1,0:T(8,128)(2,1)S(1)} %add_convert_fusion.refs_0_.refs_4_), channel_id=1, source_target_pairs={{0,32},{1,121},{2,34},{3,123},{4,36},{5,125},{6,38},{7,127},{8,40}... | collective-permute-start | bytes 393224 | tf_op jit(solution)/shard_map/ppermute | solution.py:26
  20.4 10.4 %collective-permute-start.8 = (bf16[256,256]{1,0:T(8,128)(2,1)S(1)}, bf16[256,256]{1,0:T(8,128)(2,1)S(1)}, u32[]{:S(2)}, u32[]{:S(2)}) collective-permute-start(bf16[256,256]{1,0:T(8,128)(2,1)S(1)} %add_convert_fusion.refs_0_.refs_4_), channel_id=1, source_target_pairs={{0,96},{1,89},{2,98},{3,91},{4,100},{5,93},{6,102},{7,95},{8,104},... | collective-permute-start | bytes 393224 | tf_op jit(solution)/shard_map/ppermute | solution.py:26
  22.6 11.6 %collective-permute-start.12 = (bf16[128,256]{1,0:T(8,128)(2,1)S(1)}, bf16[128,256]{1,0:T(8,128)(2,1)S(1)}, u32[]{:S(2)}, u32[]{:S(2)}) collective-permute-start(bf16[128,256]{1,0:T(8,128)(2,1)S(1)} %constant_dynamic-slice_fusion), channel_id=1, source_target_pairs={{0,64},{1,65},{2,66},{3,67},{4,68},{5,69},{6,70},{7,71},{8,72},{9,... | collective-permute-start | bytes 196616 | tf_op jit(solution)/shard_map/ppermute | solution.py:26
  30.8 4.8 %collective-permute-start.10 = (bf16[256,256]{1,0:T(8,128)(2,1)S(1)}, bf16[256,256]{1,0:T(8,128)(2,1)S(1)}, u32[]{:S(2)}, u32[]{:S(2)}) collective-permute-start(bf16[256,256]{1,0:T(8,128)(2,1)S(1)} %collective-permute-done.7.refs_0_.refs_6_), channel_id=1, source_target_pairs={{0,1},{1,0},{2,3},{3,2},{4,5},{5,4},{6,7},{7,6},{8,9},{9,8},{10,11... | collective-permute-start | bytes 393224 | tf_op jit(solution)/shard_map/ppermute | solution.py:26
  30.8 4.8 %collective-permute-start.11 = (bf16[256,256]{1,0:T(8,128)(2,1)S(1)}, bf16[256,256]{1,0:T(8,128)(2,1)S(1)}, u32[]{:S(2)}, u32[]{:S(2)}) collective-permute-start(bf16[256,256]{1,0:T(8,128)(2,1)S(1)} %collective-permute-done.8.refs_1_.refs_7_), channel_id=1, source_target_pairs={{0,1},{1,0},{2,3},{3,2},{4,5},{5,4},{6,7},{7,6},{8,9},{9,8},{10,11... | collective-permute-start | bytes 393224 | tf_op jit(solution)/shard_map/ppermute | solution.py:26
  31.3 4.3 %collective-permute-start.9 = (bf16[256,256]{1,0:T(8,128)(2,1)S(1)}, bf16[256,256]{1,0:T(8,128)(2,1)S(1)}, u32[]{:S(2)}, u32[]{:S(2)}) collective-permute-start(bf16[256,256]{1,0:T(8,128)(2,1)S(1)} %collective-permute-done.6.refs_1_.refs_5_), channel_id=1, source_target_pairs={{0,1},{1,0},{2,3},{3,2},{4,5},{5,4},{6,7},{7,6},{8,9},{9,8},{10,11... | collective-permute-start | bytes 393224 | tf_op jit(solution)/shard_map/ppermute | solution.py:26
  31.3 3.3 %copy-start.4 = (bf16[4,64,4]{1,2,0:T(4,128)(2,1)S(1)}, bf16[4,64,4]{1,2,0:T(4,128)(2,1)}, u32[]{:S(2)}) copy-start(bf16[4,64,4]{1,2,0:T(4,128)(2,1)} %param.10) | copy-start | bytes 6148
  32.8 1.3 %copy-start.2 = (bf16[256,4096]{1,0:T(8,128)(2,1)}, bf16[256,4096]{1,0:T(8,128)(2,1)S(1)}, u32[]{:S(2)}) copy-start(bf16[256,4096]{1,0:T(8,128)(2,1)S(1)} %get-tuple-element.61.done_ref) | copy-start | bytes 6291460
  34.2 1.4 %collective-permute-start.13 = (bf16[128,256]{1,0:T(8,128)(2,1)S(1)}, bf16[128,256]{1,0:T(8,128)(2,1)S(1)}, u32[]{:S(2)}, u32[]{:S(2)}) collective-permute-start(bf16[128,256]{1,0:T(8,128)(2,1)S(1)} %collective-permute-done.12.refs_4_.refs_12_), channel_id=1, source_target_pairs={{0,1},{1,0},{2,3},{3,2},{4,5},{5,4},{6,7},{7,6},{8,9},{9,8},{10,11... | collective-permute-start | bytes 196616 | tf_op jit(solution)/shard_map/ppermute | solution.py:26
  34.8 7.8 %copy-start.3 = (bf16[256,4096]{1,0:T(8,128)(2,1)S(1)}, bf16[256,4096]{1,0:T(8,128)(2,1)}, u32[]{:S(2)}) copy-start(bf16[256,4096]{1,0:T(8,128)(2,1)} %copy-done.2) | copy-start | bytes 6291460
  36.2 10.5 %collective-permute-start.14 = (bf16[64,512]{1,0:T(8,128)(2,1)S(1)}, bf16[64,512]{1,0:T(8,128)(2,1)S(1)}, u32[]{:S(2)}, u32[]{:S(2)}) collective-permute-start(bf16[64,512]{1,0:T(8,128)(2,1)S(1)} %get-tuple-element.68), channel_id=1, source_target_pairs={{0,16},{32,48},{64,80},{96,112},{16,0},{48,32},{80,64},{112,96},{1... | collective-permute-start | bytes 196616 | tf_op jit(solution)/shard_map/ppermute | solution.py:402
  37.0 9.8 %collective-permute-start.15 = (bf16[64,512]{1,0:T(8,128)(2,1)S(1)}, bf16[64,512]{1,0:T(8,128)(2,1)S(1)}, u32[]{:S(2)}, u32[]{:S(2)}) collective-permute-start(bf16[64,512]{1,0:T(8,128)(2,1)S(1)} %get-tuple-element.69), channel_id=1, source_target_pairs={{16,32},{48,64},{80,96},{112,0},{32,16},{64,48},{96,80},{0,112},{1... | collective-permute-start | bytes 196616 | tf_op jit(solution)/shard_map/ppermute | solution.py:402
  41.4 3.6 %collective-permute-start.16 = (bf16[64,128]{1,0:T(8,128)(2,1)S(1)}, bf16[64,128]{1,0:T(8,128)(2,1)S(1)}, u32[]{:S(2)}, u32[]{:S(2)}) collective-permute-start(bf16[64,128]{1,0:T(8,128)(2,1)S(1)} %get-tuple-element.70), channel_id=1, source_target_pairs={{0,1},{2,3},{4,5},{6,7},{8,9},{10,11},{12,13},{14,15},{1,0},{3,2},... | collective-permute-start | bytes 49160 | tf_op jit(solution)/shard_map/ppermute | solution.py:402
  41.4 5.3 %collective-permute-start.17 = (bf16[64,128]{1,0:T(8,128)(2,1)S(1)}, bf16[64,128]{1,0:T(8,128)(2,1)S(1)}, u32[]{:S(2)}, u32[]{:S(2)}) collective-permute-start(bf16[64,128]{1,0:T(8,128)(2,1)S(1)} %get-tuple-element.71), channel_id=1, source_target_pairs={{1,2},{3,4},{5,6},{7,8},{9,10},{11,12},{13,14},{15,0},{2,1},{4,3},... | collective-permute-start | bytes 49160 | tf_op jit(solution)/shard_map/ppermute | solution.py:402
  42.5 4.4 %copy-start.1 = (s32[4]{0:T(128)S(1)}, s32[4]{0:T(128)}, u32[]{:S(2)}) copy-start(s32[4]{0:T(128)} %port_ref.3) | copy-start | bytes 52
  53.6 8.4 %collective-permute-start.18 = (bf16[64,512]{1,0:T(8,128)(2,1)S(1)}, bf16[64,512]{1,0:T(8,128)(2,1)S(1)}, u32[]{:S(2)}, u32[]{:S(2)}) collective-permute-start(bf16[64,512]{1,0:T(8,128)(2,1)S(1)} %get-tuple-element.73), channel_id=1, source_target_pairs={{0,16},{32,48},{64,80},{96,112},{16,0},{48,32},{80,64},{112,96},{1... | collective-permute-start | bytes 196616 | tf_op jit(solution)/shard_map/ppermute | solution.py:402
  53.7 8.3 %collective-permute-start.19 = (bf16[64,512]{1,0:T(8,128)(2,1)S(1)}, bf16[64,512]{1,0:T(8,128)(2,1)S(1)}, u32[]{:S(2)}, u32[]{:S(2)}) collective-permute-start(bf16[64,512]{1,0:T(8,128)(2,1)S(1)} %get-tuple-element.74), channel_id=1, source_target_pairs={{16,32},{48,64},{80,96},{112,0},{32,16},{64,48},{96,80},{0,112},{1... | collective-permute-start | bytes 196616 | tf_op jit(solution)/shard_map/ppermute | solution.py:402
  56.6 1.2 %collective-permute-start.20 = (bf16[64,128]{1,0:T(8,128)(2,1)S(1)}, bf16[64,128]{1,0:T(8,128)(2,1)S(1)}, u32[]{:S(2)}, u32[]{:S(2)}) collective-permute-start(bf16[64,128]{1,0:T(8,128)(2,1)S(1)} %get-tuple-element.75), channel_id=1, source_target_pairs={{0,1},{2,3},{4,5},{6,7},{8,9},{10,11},{12,13},{14,15},{1,0},{3,2},... | collective-permute-start | bytes 49160 | tf_op jit(solution)/shard_map/ppermute | solution.py:402
  56.6 5.3 %collective-permute-start.21 = (bf16[64,128]{1,0:T(8,128)(2,1)S(1)}, bf16[64,128]{1,0:T(8,128)(2,1)S(1)}, u32[]{:S(2)}, u32[]{:S(2)}) collective-permute-start(bf16[64,128]{1,0:T(8,128)(2,1)S(1)} %get-tuple-element.76), channel_id=1, source_target_pairs={{1,2},{3,4},{5,6},{7,8},{9,10},{11,12},{13,14},{15,0},{2,1},{4,3},... | collective-permute-start | bytes 49160 | tf_op jit(solution)/shard_map/ppermute | solution.py:402

commit v11 on v10

--- a/solution.py
+++ b/solution.py
@@ -78,10 +78,8 @@
 
 def own_type_map(mode_shapes, mode_values, mode_weights, traces, types):
     modes, order = mode_weights.shape[1:]
-    own = jnp.concatenate([mode_shapes[0].T, mode_weights[0]], axis=0).reshape(2, modes, order)
-    part = lax.broadcasted_iota(jnp.int32, own.shape, 0)
-    own = own * jnp.where(part == 0, mode_values[0][None, :, None], 1.0)
-    own = own.reshape(2 * modes, order)
+    own = jnp.concatenate([mode_shapes[0].T, mode_weights[0]], axis=0)
+    own = own * jnp.concatenate([mode_values[0], jnp.ones((modes,), F32)])[:, None]
     far = swap(own, (0, 4))
     pair = jnp.concatenate([own, swap_cores(own)], axis=0)
     pair, traces = lax.optimization_barrier((pair, traces))
@@ -145,6 +143,17 @@
     return jnp.broadcast_to(value[:, lane : lane + 1], (value.shape[0], LANES))
 
 
+def port_profile_column(profile_ref, port):
+    edges, _, samples = profile_ref.shape
+    row = lax.broadcasted_iota(jnp.int32, (samples, samples), 0)
+    col = lax.broadcasted_iota(jnp.int32, (samples, samples), 1)
+    columns = []
+    for edge in range(edges):
+        line = jnp.broadcast_to(profile_ref[edge].astype(F32)[port : port + 1], row.shape)
+        columns.append(jnp.sum(jnp.where(row == col, line, 0.0), axis=1, keepdims=True))
+    return jnp.concatenate(columns, axis=0)
+
+
 def port_place(port_ref, port, rows, width):
     all_cols = width * lax.axis_size("col")
     cell = port_ref[port]
@@ -289,8 +298,8 @@
 
 
 def second_kernel(rows, width, port_ref, x_ref, types_ref, profile_ref, *refs):
-    halo_refs, map_refs, next_ref = refs[:4], refs[4:-6], refs[-6]
-    rim_refs, blocks = refs[-5:-1], refs[-1]
+    halo_refs, map_refs, next_ref = refs[:4], refs[4:-5], refs[-5]
+    rim_refs = refs[-4:]
     types = types_ref[...].astype(F32).astype(BF)
     tile = types.shape[1]
     order = x_ref.shape[0]
@@ -301,33 +310,38 @@
     lane = lax.broadcasted_iota(jnp.int32, (quarter, LANES), 1)
     west_rim = east_rim = jnp.zeros((quarter, LANES), F32)
     north_rim, south_rim = [], []
+    place_in_tile = lax.broadcasted_iota(jnp.int32, (1, tile), 1)
     for port in range(x_ref.shape[1] // tile):
         own = slice(port * tile, (port + 1) * tile)
         rim = slice(port * LANES, (port + 1) * LANES)
-        block = blocks.at[port % 2]
-        block[...] = x_ref[:, own]
-        block[0:quarter, 0:LANES] = north_in[:, rim].astype(BF)
-        block[quarter : 2 * quarter, tile - LANES :] = south_in[:, rim].astype(BF)
+        north = jnp.concatenate(
+            [north_in[:, rim].astype(BF), x_ref[0:quarter, port * tile + LANES : (port + 1) * tile]],
+            axis=1,
+        )
+        south = jnp.concatenate(
+            [
+                x_ref[quarter : 2 * quarter, port * tile : (port + 1) * tile - LANES],
+                south_in[:, rim].astype(BF),
+            ],
+            axis=1,
+        )
+        west, east = [], []
         for row in range(rows):
             place = port * rows + row
-            cols = slice(row * LANES, (row + 1) * LANES)
-            west = block[2 * quarter : 3 * quarter, cols].astype(F32)
-            east = block[3 * quarter :, cols].astype(F32)
-            west = jnp.where(lane == 0, lane_of(west_in, 64 + place), west)
-            east = jnp.where(lane == LANES - 1, lane_of(east_in, place), east)
-            block[2 * quarter : 3 * quarter, cols] = west.astype(BF)
-            block[3 * quarter :, cols] = east.astype(BF)
+            cols = slice(place * LANES, (place + 1) * LANES)
+            value = x_ref[2 * quarter : 3 * quarter, cols].astype(F32)
+            west.append(jnp.where(lane == 0, lane_of(west_in, 64 + place), value))
+            value = x_ref[3 * quarter :, cols].astype(F32)
+            east.append(jnp.where(lane == LANES - 1, lane_of(east_in, place), value))
+        west = jnp.concatenate(west, axis=1).astype(BF)
+        east = jnp.concatenate(east, axis=1).astype(BF)
+        block = jnp.concatenate([north, south, west, east], axis=0)
         row, col, inside = port_place(port_ref, port, rows, width)
-
-        @pl.when(inside)
-        def _():
-            cols = pl.ds(pl.multiple_of(row * LANES, LANES), LANES)
-            here = lax.broadcasted_iota(jnp.int32, (order, LANES), 1) == col
-            current = block[:, cols].astype(F32)
-            added = current + profile_ref[port].astype(F32)
-            block[:, cols] = jnp.where(here, added, current).astype(BF)
-
-        total = products(block[...], types, maps, 0, order)
+        here = place_in_tile == jnp.where(inside, row * width + col, -1)
+        current = block.astype(F32)
+        added = current + port_profile_column(profile_ref, port)
+        block = jnp.where(here, added, current).astype(BF)
+        total = products(block, types, maps, 0, order)
         north, south = shifted(total, next_ref.at[:, own], rows)
         north_rim.append(north[:, 0:LANES])
         south_rim.append(south[:, tile - LANES :])
@@ -381,7 +395,8 @@
                 here = (lax.broadcasted_iota(jnp.int32, current.shape, 1) == row) & (
                     lax.broadcasted_iota(jnp.int32, current.shape, 2) == col
                 )
-                profile = profile_ref[port, lines, :].astype(F32).reshape(quarter, 1, LANES)
+                profile = port_profile_column(profile_ref, port)[lines]
+                profile = jnp.broadcast_to(profile, (quarter, LANES)).reshape(quarter, 1, LANES)
                 added = current + jnp.broadcast_to(profile, current.shape)
                 buffer[lines, port] = jnp.where(here, added, current).astype(BF)
 
@@ -415,9 +430,7 @@
         swap(own_map, *((step, 8 * (step % 2)) for step in steps)) for steps in MAP_STEPS[1:4]
     ]
     half = swap(half, (4, 0))
-    profile = jnp.broadcast_to(
-        jnp.transpose(port_profile.reshape(order, ports))[:, :, None], (ports, order, LANES)
-    )
+    profile = jnp.transpose(port_profile, (0, 2, 1))
     ports_spec = pl.BlockSpec(memory_space=pltpu.SMEM)
     next_shape = jax.ShapeDtypeStruct((order, ports * tile), BF)
     rim_shapes = [jax.ShapeDtypeStruct((quarter, ports * LANES), BF)] * 2 + [
@@ -467,7 +480,6 @@
         in_specs=[ports_spec] + [WHOLE] * (len(operands) - 1),
         out_specs=[WHOLE] * 5,
         out_shape=[next_shape] + rim_shapes,
-        scratch_shapes=[pltpu.VMEM((2, order, tile), BF)],
         compiler_params=PARAMS,
         cost_estimate=pl.CostEstimate(flops=work, bytes_accessed=0, transcendentals=0),
     )(*operands)

time: 65.5 us -> 63.5 us (0.969)
  local copies, waits for them, and re-layouts: 2.52 us -> 0.67 us
    unnamed x11 -> x6, local copies, waits for them, and re-layouts: 1.33 us -> 0.01 us
    broadcast_in_dim x3 -> x0, local copies, waits for them, and re-layouts: 0.94 us -> none  [the longest x2 0.74 us: own_type_map(): own = own * jnp.where(part == 0, mode_values[0][None, :, None], 1.0)]
    pallas_call x1, Pallas kernels: 6.62 us -> 5.83 us  [body(): pl.pallas_call(functools.partial(second_kernel, rows, width), in_specs=[p...]
    concatenate x0 -> x1, local copies, waits for them, and re-layouts: none -> 0.66 us  [own_type_map(): jnp.concatenate([mode_values[0], jnp.ones((modes,), F32)])[:, None]]
  transfers between devices with their start and end apart: 22 -> 22, of which waited for: 9 -> 9; matrix products, arithmetic and copies ran while one was open for 0% -> 0% of each run, Pallas kernels for 13% -> 14%
where the time goes in v11:
time: 63.5 us; the launch traced here: 63.2 us
  starting transfers between devices  25.4 us (40%)
  Pallas kernels  19.2 us (30%)
  waiting for transfers between devices  16.7 us (26%)
  other arithmetic  0.85 us (1%)
  local copies, waits for them, and re-layouts  0.67 us (1%)
    ppermute x14, starting transfers between devices, swap(): return lax.ppermute(value, ('row', 'col'), pairs)  15.2 us
    ppermute x14, waiting for transfers between devices, swap(): return lax.ppermute(value, ('row', 'col'), pairs)  10.7 us
    ppermute x8, starting transfers between devices, exchange(): lax.ppermute(rim, axis, pairs(axis, first))  10.3 us
    pallas_call x6, Pallas kernels, whole_call(): pl.pallas_call(kernel, in_specs=[WHOLE] * len(operands), out_specs=[WHOLE...  7.77 us
    ppermute x8, waiting for transfers between devices, exchange(): lax.ppermute(rim, axis, pairs(axis, first))  6.07 us
    pallas_call x1, Pallas kernels, body(): pl.pallas_call(functools.partial(second_kernel, rows, width), in_specs=[p...  5.83 us
    pallas_call x1, Pallas kernels, body(): pl.pallas_call(functools.partial(last_kernel, rows, width), in_specs=[por...  3.65 us
    pallas_call x1, Pallas kernels, own_type_map(): pl.pallas_call(flat_kernel, in_specs=[pl.BlockSpec(memory_space=pltpu.HBM...  1.98 us
  transfers between devices with their start and end apart: 22, of which 9 were waited for; matrix products, arithmetic and copies ran while one was open for 0% of the time, Pallas kernels for 14%

profile of v11, /device:TPU:0, one launch (start us, length us, event | category | flops | bytes accessed | tf_op | source)
XLA Modules:
  0.0 63.2 jit_solution(11371030554486752736)
XLA Ops:
  0.0 0.7 %concatenate.10 = f32[32]{0:T(128)S(1)} pad(f32[16]{0:T(128)} %bitcast.20, f32[]{:T(128)} %constant.6.clone.1), padding=0_16 | pad | bytes 196 | tf_op jit(solution)/shard_map/concatenate | solution.py:82
  0.7 0.8 %maximum_multiply_fusion.refs_0_ = f32[32,256]{1,0:T(8,128)S(1)} fusion(f32[16,256]{1,0:T(8,128)} %bitcast.18, f32[16,256]{1,0:T(8,128)} %bitcast.19, f32[32]{0:T(128)S(1)} %concatenate.10), kind=kLoop, calls=%fused_computation.2 | loop fusion | flops 16384 | bytes 65664 | tf_op jit(solution)/shard_map/mul | solution.py:82
  1.5 0.0 collective-permute-start.1
  1.5 4.0 %collective-permute-start = (f32[32,256]{1,0:T(8,128)S(1)}, f32[32,256]{1,0:T(8,128)S(1)}, u32[]{:S(2)}, u32[]{:S(2)}) collective-permute-start(f32[32,256]{1,0:T(8,128)S(1)} %maximum_multiply_fusion.refs_0_), channel_id=1, source_target_pairs={{0,4},{1,5},{2,6},{3,7},{4,0},{5,1},{6,2},{7,3},{8,12},{9,13},{10,... | collective-permute-start | bytes 98312 | tf_op jit(solution)/shard_map/ppermute | solution.py:26
  5.5 0.0 collective-permute-done.1
  5.5 1.6 %collective-permute-start.2 = (f32[64,256]{1,0:T(8,128)S(1)}, f32[64,256]{1,0:T(8,128)S(1)}, u32[]{:S(2)}, u32[]{:S(2)}) collective-permute-start(f32[64,256]{1,0:T(8,128)S(1)} %pad_maximum_fusion), channel_id=1, source_target_pairs={{0,8},{1,11},{2,10},{3,9},{4,12},{5,15},{6,14},{7,13},{8,0},{9,3},... | collective-permute-start | bytes 196616 | tf_op jit(solution)/shard_map/ppermute | solution.py:26
  7.0 1.0 %collective-permute-start.3 = (f32[64,256]{1,0:T(8,128)S(1)}, f32[64,256]{1,0:T(8,128)S(1)}, u32[]{:S(2)}, u32[]{:S(2)}) collective-permute-start(f32[64,256]{1,0:T(8,128)S(1)} %pad_maximum_fusion), channel_id=1, source_target_pairs={{0,2},{1,15},{2,0},{3,13},{4,6},{5,11},{6,4},{7,9},{8,10},{9,7},{1... | collective-permute-start | bytes 196616 | tf_op jit(solution)/shard_map/ppermute | solution.py:26
  8.1 0.6 %collective-permute-start.4 = (f32[64,256]{1,0:T(8,128)S(1)}, f32[64,256]{1,0:T(8,128)S(1)}, u32[]{:S(2)}, u32[]{:S(2)}) collective-permute-start(f32[64,256]{1,0:T(8,128)S(1)} %pad_maximum_fusion), channel_id=1, source_target_pairs={{0,6},{1,13},{2,4},{3,15},{4,2},{5,9},{6,0},{7,11},{8,14},{9,5},{1... | collective-permute-start | bytes 196616 | tf_op jit(solution)/shard_map/ppermute | solution.py:26
  8.7 0.0 copy-start
  8.7 2.0 %shard_map.73.x_ref = bf16[256,4096]{1,0:T(8,128)(2,1)S(1)} custom-call(bf16[256,4,8,128]{3,2,1,0:T(8,128)(2,1)} %bitcast.17), custom_call_target="tpu_custom_call" | custom-call | flops 1073741824 | tf_op jit(solution)/shard_map/pallas_call | solution.py:89
  10.7 0.0 collective-permute-done.2.refs_2_
  10.7 0.6 collective-permute-done.3.refs_3_
  11.3 2.9 %collective-permute-done.4.refs_4_ = f32[64,256]{1,0:T(8,128)S(1)} collective-permute-done((f32[64,256]{1,0:T(8,128)S(1)}, f32[64,256]{1,0:T(8,128)S(1)}, u32[]{:S(2)}, u32[]{:S(2)}) %collective-permute-start.4) | collective-permute-done | bytes 65568 | tf_op jit(solution)/shard_map/ppermute | solution.py:26
  14.2 0.0 collective-permute-done.refs_1_
  14.2 0.4 shard_map.74
  14.6 0.1 collective-permute-start.5
  14.7 0.0 copy-done
  14.7 1.2 %shard_map.75 = (bf16[256,128]{1,0:T(8,128)(2,1)S(1)}, bf16[16,128]{1,0:T(8,128)(2,1)S(1)}) custom-call(bf16[256,4096]{1,0:T(8,128)(2,1)S(1)} %shard_map.73.x_ref, s32[1,1024]{1,0:T(1,128)S(1)} %bitcast.9), custom_call_target="tpu_custom_call" | custom-call | flops 1073741824 | tf_op jit(solution)/shard_map/pallas_call | solution.py:69
  15.9 0.3 collective-permute-done.5
  16.3 2.2 %collective-permute-start.6 = (bf16[256,256]{1,0:T(8,128)(2,1)S(1)}, bf16[256,256]{1,0:T(8,128)(2,1)S(1)}, u32[]{:S(2)}, u32[]{:S(2)}) collective-permute-start(bf16[256,256]{1,0:T(8,128)(2,1)S(1)} %add_convert_fusion.refs_0_.refs_4_), channel_id=1, source_target_pairs={{0,24},{1,57},{2,26},{3,59},{4,28},{5,61},{6,30},{7,63},{8,16},{9,... | collective-permute-start | bytes 393224 | tf_op jit(solution)/shard_map/ppermute | solution.py:26
  18.5 1.6 %collective-permute-start.7 = (bf16[256,256]{1,0:T(8,128)(2,1)S(1)}, bf16[256,256]{1,0:T(8,128)(2,1)S(1)}, u32[]{:S(2)}, u32[]{:S(2)}) collective-permute-start(bf16[256,256]{1,0:T(8,128)(2,1)S(1)} %add_convert_fusion.refs_0_.refs_4_), channel_id=1, source_target_pairs={{0,32},{1,121},{2,34},{3,123},{4,36},{5,125},{6,38},{7,127},{8,40}... | collective-permute-start | bytes 393224 | tf_op jit(solution)/shard_map/ppermute | solution.py:26
  20.1 2.2 %collective-permute-start.8 = (bf16[256,256]{1,0:T(8,128)(2,1)S(1)}, bf16[256,256]{1,0:T(8,128)(2,1)S(1)}, u32[]{:S(2)}, u32[]{:S(2)}) collective-permute-start(bf16[256,256]{1,0:T(8,128)(2,1)S(1)} %add_convert_fusion.refs_0_.refs_4_), channel_id=1, source_target_pairs={{0,96},{1,89},{2,98},{3,91},{4,100},{5,93},{6,102},{7,95},{8,104},... | collective-permute-start | bytes 393224 | tf_op jit(solution)/shard_map/ppermute | solution.py:26
  22.3 0.8 %collective-permute-start.12 = (bf16[128,256]{1,0:T(8,128)(2,1)S(1)}, bf16[128,256]{1,0:T(8,128)(2,1)S(1)}, u32[]{:S(2)}, u32[]{:S(2)}) collective-permute-start(bf16[128,256]{1,0:T(8,128)(2,1)S(1)} %constant_dynamic-slice_fusion), channel_id=1, source_target_pairs={{0,64},{1,65},{2,66},{3,67},{4,68},{5,69},{6,70},{7,71},{8,72},{9,... | collective-permute-start | bytes 196616 | tf_op jit(solution)/shard_map/ppermute | solution.py:26
  23.1 0.7 %collective-permute-done.6.refs_1_.refs_5_ = bf16[256,256]{1,0:T(8,128)(2,1)S(1)} collective-permute-done((bf16[256,256]{1,0:T(8,128)(2,1)S(1)}, bf16[256,256]{1,0:T(8,128)(2,1)S(1)}, u32[]{:S(2)}, u32[]{:S(2)}) %collective-permute-start.6) | collective-permute-done | bytes 131104 | tf_op jit(solution)/shard_map/ppermute | solution.py:26
  23.7 1.5 %shard_map.76 = (bf16[256,4096]{1,0:T(8,128)(2,1)S(1)}, bf16[64,512]{1,0:T(8,128)(2,1)S(1)}, bf16[64,512]{1,0:T(8,128)(2,1)S(1)}, bf16[128,128]{1,0:T(8,128)(2,1)S(1)}) custom-call(bf16[256,4096]{1,0:T(8,128)(2,1)S(1)} %shard_map.73.x_ref, s32[1,1024]{1,0:T(1,128)S(1)} %bitcast.10, bf16[256,128]{1,0:T(8,128)(2,1)S(1)} %get-tuple-element.51.sides_ref, ...), custom_call_target="tpu_custom_call" | custom-call | flops 1227133568 | tf_op jit(solution)/shard_map/pallas_call | solution.py:69
  25.3 0.0 collective-permute-done.7.refs_0_.refs_6_
  25.3 5.2 %collective-permute-done.8.refs_1_.refs_7_ = bf16[256,256]{1,0:T(8,128)(2,1)S(1)} collective-permute-done((bf16[256,256]{1,0:T(8,128)(2,1)S(1)}, bf16[256,256]{1,0:T(8,128)(2,1)S(1)}, u32[]{:S(2)}, u32[]{:S(2)}) %collective-permute-start.8) | collective-permute-done | bytes 131104 | tf_op jit(solution)/shard_map/ppermute | solution.py:26
  30.5 0.0 collective-permute-start.10
  30.5 0.5 collective-permute-start.11
  31.0 0.0 collective-permute-start.9
  31.0 1.5 %shard_map.77 = (bf16[256,4096]{1,0:T(8,128)(2,1)S(1)}, bf16[64,512]{1,0:T(8,128)(2,1)S(1)}, bf16[64,512]{1,0:T(8,128)(2,1)S(1)}, bf16[128,128]{1,0:T(8,128)(2,1)S(1)}) custom-call(bf16[256,4096]{1,0:T(8,128)(2,1)S(1)} %shard_map.73.x_ref, s32[1,1024]{1,0:T(1,128)S(1)} %bitcast.11, bf16[256,128]{1,0:T(8,128)(2,1)S(1)} %get-tuple-element.51.sides_ref, ...), custom_call_target="tpu_custom_call" | custom-call | flops 1227133568 | tf_op jit(solution)/shard_map/pallas_call | solution.py:69
  32.5 0.0 collective-permute-done.12.refs_4_.refs_12_
  32.5 0.6 collective-permute-start.13
  33.1 0.9 %collective-permute-done.13.refs_3_.refs_11_ = bf16[128,256]{1,0:T(8,128)(2,1)S(1)} collective-permute-done((bf16[128,256]{1,0:T(8,128)(2,1)S(1)}, bf16[128,256]{1,0:T(8,128)(2,1)S(1)}, u32[]{:S(2)}, u32[]{:S(2)}) %collective-permute-start.13) | collective-permute-done | bytes 65568 | tf_op jit(solution)/shard_map/ppermute | solution.py:26
  34.0 0.0 collective-permute-done.10.refs_1_.refs_9_
  34.0 0.0 collective-permute-done.11.refs_2_.refs_10_
  34.0 0.0 collective-permute-done.9.refs_0_.refs_8_
  34.0 0.6 shard_map.79
  34.7 0.7 %collective-permute-start.14 = (bf16[64,512]{1,0:T(8,128)(2,1)S(1)}, bf16[64,512]{1,0:T(8,128)(2,1)S(1)}, u32[]{:S(2)}, u32[]{:S(2)}) collective-permute-start(bf16[64,512]{1,0:T(8,128)(2,1)S(1)} %get-tuple-element.68), channel_id=1, source_target_pairs={{0,16},{32,48},{64,80},{96,112},{16,0},{48,32},{80,64},{112,96},{1... | collective-permute-start | bytes 196616 | tf_op jit(solution)/shard_map/ppermute | solution.py:417
  35.4 4.5 %collective-permute-start.15 = (bf16[64,512]{1,0:T(8,128)(2,1)S(1)}, bf16[64,512]{1,0:T(8,128)(2,1)S(1)}, u32[]{:S(2)}, u32[]{:S(2)}) collective-permute-start(bf16[64,512]{1,0:T(8,128)(2,1)S(1)} %get-tuple-element.69), channel_id=1, source_target_pairs={{16,32},{48,64},{80,96},{112,0},{32,16},{64,48},{96,80},{0,112},{1... | collective-permute-start | bytes 196616 | tf_op jit(solution)/shard_map/ppermute | solution.py:417
  39.9 0.0 collective-permute-start.16
  39.9 1.1 %collective-permute-start.17 = (bf16[64,128]{1,0:T(8,128)(2,1)S(1)}, bf16[64,128]{1,0:T(8,128)(2,1)S(1)}, u32[]{:S(2)}, u32[]{:S(2)}) collective-permute-start(bf16[64,128]{1,0:T(8,128)(2,1)S(1)} %get-tuple-element.71), channel_id=1, source_target_pairs={{1,2},{3,4},{5,6},{7,8},{9,10},{11,12},{13,14},{15,0},{2,1},{4,3},... | collective-permute-start | bytes 49160 | tf_op jit(solution)/shard_map/ppermute | solution.py:417
  41.0 0.0 copy-start.1
  41.0 0.0 copy-start.2
  41.0 2.5 %shard_map.78.x_ref = bf16[256,4096]{1,0:T(8,128)(2,1)S(1)} custom-call(bf16[256,4096]{1,0:T(8,128)(2,1)S(1)} %shard_map.73.x_ref, s32[1,1024]{1,0:T(1,128)S(1)} %bitcast.13, bf16[256,4096]{1,0:T(8,128)(2,1)S(1)} %get-tuple-element.61.done_ref, bf16[256,256]{1,0:T(8,128)(2,1)S(1)} %collective-permute-done.9.refs_0_.refs_8_, ...), custom_call_target="tpu_custom_call" | custom-call | flops 2147483648 | tf_op jit(solution)/shard_map/pallas_call | solution.py:69
  43.6 0.0 collective-permute-done.16.refs_2_
  43.6 1.6 %collective-permute-done.17.refs_3_ = bf16[64,128]{1,0:T(8,128)(2,1)S(1)} collective-permute-done((bf16[64,128]{1,0:T(8,128)(2,1)S(1)}, bf16[64,128]{1,0:T(8,128)(2,1)S(1)}, u32[]{:S(2)}, u32[]{:S(2)}) %collective-permute-start.17) | collective-permute-done | bytes 16416 | tf_op jit(solution)/shard_map/ppermute | solution.py:417
  45.2 0.0 collective-permute-done.14.refs_0_
  45.2 0.0 collective-permute-done.15.refs_1_
  45.2 0.0 copy-done.1
  45.2 0.0 copy-done.2
  45.2 5.8 %shard_map.80 = (bf16[256,4096]{1,0:T(8,128)(2,1)S(1)}, bf16[64,512]{1,0:T(8,128)(2,1)S(1)}, bf16[64,512]{1,0:T(8,128)(2,1)S(1)}, bf16[64,128]{1,0:T(8,128)(2,1)S(1)}, bf16[64,128]{1,0:T(8,128)(2,1)S(1)}) custom-call(s32[4]{0:T(128)S(1)} %copy-done.2, bf16[256,4096]{1,0:T(8,128)(2,1)S(1)} %shard_map.78.x_ref, s32[1,1024]{1,0:T(1,128)S(1)} %bitcast.14, ...), custom_call_target="tpu_custom_call" | custom-call | flops 4294967296 | tf_op jit(solution)/shard_map/pallas_call | solution.py:478
  51.0 0.1 collective-permute-start.18
  51.1 3.0 %collective-permute-start.19 = (bf16[64,512]{1,0:T(8,128)(2,1)S(1)}, bf16[64,512]{1,0:T(8,128)(2,1)S(1)}, u32[]{:S(2)}, u32[]{:S(2)}) collective-permute-start(bf16[64,512]{1,0:T(8,128)(2,1)S(1)} %get-tuple-element.74), channel_id=1, source_target_pairs={{16,32},{48,64},{80,96},{112,0},{32,16},{64,48},{96,80},{0,112},{1... | collective-permute-start | bytes 196616 | tf_op jit(solution)/shard_map/ppermute | solution.py:417
  54.1 0.0 collective-permute-start.20
  54.1 0.8 %collective-permute-start.21 = (bf16[64,128]{1,0:T(8,128)(2,1)S(1)}, bf16[64,128]{1,0:T(8,128)(2,1)S(1)}, u32[]{:S(2)}, u32[]{:S(2)}) collective-permute-start(bf16[64,128]{1,0:T(8,128)(2,1)S(1)} %get-tuple-element.76), channel_id=1, source_target_pairs={{1,2},{3,4},{5,6},{7,8},{9,10},{11,12},{13,14},{15,0},{2,1},{4,3},... | collective-permute-start | bytes 49160 | tf_op jit(solution)/shard_map/ppermute | solution.py:417
  54.9 0.4 collective-permute-done.20.refs_2_
  55.3 4.1 %collective-permute-done.21.refs_3_ = bf16[64,128]{1,0:T(8,128)(2,1)S(1)} collective-permute-done((bf16[64,128]{1,0:T(8,128)(2,1)S(1)}, bf16[64,128]{1,0:T(8,128)(2,1)S(1)}, u32[]{:S(2)}, u32[]{:S(2)}) %collective-permute-start.21) | collective-permute-done | bytes 16416 | tf_op jit(solution)/shard_map/ppermute | solution.py:417
  59.4 0.0 collective-permute-done.18.refs_0_
  59.4 0.0 collective-permute-done.19.refs_1_
  59.4 3.6 %shard_map.81 = bf16[256,4,8,128]{3,2,1,0:T(8,128)(2,1)} custom-call(s32[4]{0:T(128)S(1)} %copy-done.2, bf16[256,4096]{1,0:T(8,128)(2,1)S(1)} %get-tuple-element.72.x_ref, bf16[4,4,64]{2,1,0:T(4,128)(2,1)S(1)} %bitcast.16, bf16[64,512]{1,0:T(8,128)(2,1)S(1)} %collective-permute-done.18.refs_0_, bf16[64,512]{1,0:T(8,128)(2,1)S(1)} %collective-permute-done.19.refs_1_, ...), custom_call_target="tpu_custom_call" | custom-call | tf_op jit(solution)/shard_map/pallas_call | solution.py:487
  (3 shorter events, 0.0 us)
Async XLA Ops:
  1.5 4.0 %collective-permute-start.1 = (f32[32,256]{1,0:T(8,128)S(1)}, f32[32,256]{1,0:T(8,128)S(1)}, u32[]{:S(2)}, u32[]{:S(2)}) collective-permute-start(f32[32,256]{1,0:T(8,128)S(1)} %maximum_multiply_fusion.refs_0_), channel_id=1, source_target_pairs={{0,1},{1,0},{2,3},{3,2},{4,5},{5,4},{6,7},{7,6},{8,9},{9,8},{10,11... | collective-permute-start | bytes 98312 | tf_op jit(solution)/shard_map/ppermute | solution.py:26
  1.5 12.8 %collective-permute-start = (f32[32,256]{1,0:T(8,128)S(1)}, f32[32,256]{1,0:T(8,128)S(1)}, u32[]{:S(2)}, u32[]{:S(2)}) collective-permute-start(f32[32,256]{1,0:T(8,128)S(1)} %maximum_multiply_fusion.refs_0_), channel_id=1, source_target_pairs={{0,4},{1,5},{2,6},{3,7},{4,0},{5,1},{6,2},{7,3},{8,12},{9,13},{10,... | collective-permute-start | bytes 98312 | tf_op jit(solution)/shard_map/ppermute | solution.py:26
  5.5 5.2 %collective-permute-start.2 = (f32[64,256]{1,0:T(8,128)S(1)}, f32[64,256]{1,0:T(8,128)S(1)}, u32[]{:S(2)}, u32[]{:S(2)}) collective-permute-start(f32[64,256]{1,0:T(8,128)S(1)} %pad_maximum_fusion), channel_id=1, source_target_pairs={{0,8},{1,11},{2,10},{3,9},{4,12},{5,15},{6,14},{7,13},{8,0},{9,3},... | collective-permute-start | bytes 196616 | tf_op jit(solution)/shard_map/ppermute | solution.py:26
  7.0 4.3 %collective-permute-start.3 = (f32[64,256]{1,0:T(8,128)S(1)}, f32[64,256]{1,0:T(8,128)S(1)}, u32[]{:S(2)}, u32[]{:S(2)}) collective-permute-start(f32[64,256]{1,0:T(8,128)S(1)} %pad_maximum_fusion), channel_id=1, source_target_pairs={{0,2},{1,15},{2,0},{3,13},{4,6},{5,11},{6,4},{7,9},{8,10},{9,7},{1... | collective-permute-start | bytes 196616 | tf_op jit(solution)/shard_map/ppermute | solution.py:26
  8.1 6.2 %collective-permute-start.4 = (f32[64,256]{1,0:T(8,128)S(1)}, f32[64,256]{1,0:T(8,128)S(1)}, u32[]{:S(2)}, u32[]{:S(2)}) collective-permute-start(f32[64,256]{1,0:T(8,128)S(1)} %pad_maximum_fusion), channel_id=1, source_target_pairs={{0,6},{1,13},{2,4},{3,15},{4,2},{5,9},{6,0},{7,11},{8,14},{9,5},{1... | collective-permute-start | bytes 196616 | tf_op jit(solution)/shard_map/ppermute | solution.py:26
  8.7 6.0 %copy-start = (s32[8,128]{1,0:T(8,128)S(1)}, s32[8,128]{1,0:T(8,128)}, u32[]{:S(2)}) copy-start(s32[8,128]{1,0:T(8,128)} %param.8) | copy-start | bytes 12292
  14.6 1.6 %collective-permute-start.5 = (f32[256,256]{1,0:T(8,128)S(1)}, f32[256,256]{1,0:T(8,128)S(1)}, u32[]{:S(2)}, u32[]{:S(2)}) collective-permute-start(f32[256,256]{1,0:T(8,128)S(1)} %shard_map.74), channel_id=1, source_target_pairs={{0,1},{1,0},{2,3},{3,2},{4,5},{5,4},{6,7},{7,6},{8,9},{9,8},{10,11... | collective-permute-start | bytes 786440 | tf_op jit(solution)/shard_map/ppermute | solution.py:26
  16.3 7.4 %collective-permute-start.6 = (bf16[256,256]{1,0:T(8,128)(2,1)S(1)}, bf16[256,256]{1,0:T(8,128)(2,1)S(1)}, u32[]{:S(2)}, u32[]{:S(2)}) collective-permute-start(bf16[256,256]{1,0:T(8,128)(2,1)S(1)} %add_convert_fusion.refs_0_.refs_4_), channel_id=1, source_target_pairs={{0,24},{1,57},{2,26},{3,59},{4,28},{5,61},{6,30},{7,63},{8,16},{9,... | collective-permute-start | bytes 393224 | tf_op jit(solution)/shard_map/ppermute | solution.py:26
  18.5 6.8 %collective-permute-start.7 = (bf16[256,256]{1,0:T(8,128)(2,1)S(1)}, bf16[256,256]{1,0:T(8,128)(2,1)S(1)}, u32[]{:S(2)}, u32[]{:S(2)}) collective-permute-start(bf16[256,256]{1,0:T(8,128)(2,1)S(1)} %add_convert_fusion.refs_0_.refs_4_), channel_id=1, source_target_pairs={{0,32},{1,121},{2,34},{3,123},{4,36},{5,125},{6,38},{7,127},{8,40}... | collective-permute-start | bytes 393224 | tf_op jit(solution)/shard_map/ppermute | solution.py:26
  20.1 10.4 %collective-permute-start.8 = (bf16[256,256]{1,0:T(8,128)(2,1)S(1)}, bf16[256,256]{1,0:T(8,128)(2,1)S(1)}, u32[]{:S(2)}, u32[]{:S(2)}) collective-permute-start(bf16[256,256]{1,0:T(8,128)(2,1)S(1)} %add_convert_fusion.refs_0_.refs_4_), channel_id=1, source_target_pairs={{0,96},{1,89},{2,98},{3,91},{4,100},{5,93},{6,102},{7,95},{8,104},... | collective-permute-start | bytes 393224 | tf_op jit(solution)/shard_map/ppermute | solution.py:26
  22.3 10.3 %collective-permute-start.12 = (bf16[128,256]{1,0:T(8,128)(2,1)S(1)}, bf16[128,256]{1,0:T(8,128)(2,1)S(1)}, u32[]{:S(2)}, u32[]{:S(2)}) collective-permute-start(bf16[128,256]{1,0:T(8,128)(2,1)S(1)} %constant_dynamic-slice_fusion), channel_id=1, source_target_pairs={{0,64},{1,65},{2,66},{3,67},{4,68},{5,69},{6,70},{7,71},{8,72},{9,... | collective-permute-start | bytes 196616 | tf_op jit(solution)/shard_map/ppermute | solution.py:26
  30.5 3.6 %collective-permute-start.10 = (bf16[256,256]{1,0:T(8,128)(2,1)S(1)}, bf16[256,256]{1,0:T(8,128)(2,1)S(1)}, u32[]{:S(2)}, u32[]{:S(2)}) collective-permute-start(bf16[256,256]{1,0:T(8,128)(2,1)S(1)} %collective-permute-done.7.refs_0_.refs_6_), channel_id=1, source_target_pairs={{0,1},{1,0},{2,3},{3,2},{4,5},{5,4},{6,7},{7,6},{8,9},{9,8},{10,11... | collective-permute-start | bytes 393224 | tf_op jit(solution)/shard_map/ppermute | solution.py:26
  30.5 3.6 %collective-permute-start.11 = (bf16[256,256]{1,0:T(8,128)(2,1)S(1)}, bf16[256,256]{1,0:T(8,128)(2,1)S(1)}, u32[]{:S(2)}, u32[]{:S(2)}) collective-permute-start(bf16[256,256]{1,0:T(8,128)(2,1)S(1)} %collective-permute-done.8.refs_1_.refs_7_), channel_id=1, source_target_pairs={{0,1},{1,0},{2,3},{3,2},{4,5},{5,4},{6,7},{7,6},{8,9},{9,8},{10,11... | collective-permute-start | bytes 393224 | tf_op jit(solution)/shard_map/ppermute | solution.py:26
  31.0 3.1 %collective-permute-start.9 = (bf16[256,256]{1,0:T(8,128)(2,1)S(1)}, bf16[256,256]{1,0:T(8,128)(2,1)S(1)}, u32[]{:S(2)}, u32[]{:S(2)}) collective-permute-start(bf16[256,256]{1,0:T(8,128)(2,1)S(1)} %collective-permute-done.6.refs_1_.refs_5_), channel_id=1, source_target_pairs={{0,1},{1,0},{2,3},{3,2},{4,5},{5,4},{6,7},{7,6},{8,9},{9,8},{10,11... | collective-permute-start | bytes 393224 | tf_op jit(solution)/shard_map/ppermute | solution.py:26
  32.5 1.5 %collective-permute-start.13 = (bf16[128,256]{1,0:T(8,128)(2,1)S(1)}, bf16[128,256]{1,0:T(8,128)(2,1)S(1)}, u32[]{:S(2)}, u32[]{:S(2)}) collective-permute-start(bf16[128,256]{1,0:T(8,128)(2,1)S(1)} %collective-permute-done.12.refs_4_.refs_12_), channel_id=1, source_target_pairs={{0,1},{1,0},{2,3},{3,2},{4,5},{5,4},{6,7},{7,6},{8,9},{9,8},{10,11... | collective-permute-start | bytes 196616 | tf_op jit(solution)/shard_map/ppermute | solution.py:26
  34.7 10.5 %collective-permute-start.14 = (bf16[64,512]{1,0:T(8,128)(2,1)S(1)}, bf16[64,512]{1,0:T(8,128)(2,1)S(1)}, u32[]{:S(2)}, u32[]{:S(2)}) collective-permute-start(bf16[64,512]{1,0:T(8,128)(2,1)S(1)} %get-tuple-element.68), channel_id=1, source_target_pairs={{0,16},{32,48},{64,80},{96,112},{16,0},{48,32},{80,64},{112,96},{1... | collective-permute-start | bytes 196616 | tf_op jit(solution)/shard_map/ppermute | solution.py:417
  35.4 9.8 %collective-permute-start.15 = (bf16[64,512]{1,0:T(8,128)(2,1)S(1)}, bf16[64,512]{1,0:T(8,128)(2,1)S(1)}, u32[]{:S(2)}, u32[]{:S(2)}) collective-permute-start(bf16[64,512]{1,0:T(8,128)(2,1)S(1)} %get-tuple-element.69), channel_id=1, source_target_pairs={{16,32},{48,64},{80,96},{112,0},{32,16},{64,48},{96,80},{0,112},{1... | collective-permute-start | bytes 196616 | tf_op jit(solution)/shard_map/ppermute | solution.py:417
  39.9 3.7 %collective-permute-start.16 = (bf16[64,128]{1,0:T(8,128)(2,1)S(1)}, bf16[64,128]{1,0:T(8,128)(2,1)S(1)}, u32[]{:S(2)}, u32[]{:S(2)}) collective-permute-start(bf16[64,128]{1,0:T(8,128)(2,1)S(1)} %get-tuple-element.70), channel_id=1, source_target_pairs={{0,1},{2,3},{4,5},{6,7},{8,9},{10,11},{12,13},{14,15},{1,0},{3,2},... | collective-permute-start | bytes 49160 | tf_op jit(solution)/shard_map/ppermute | solution.py:417
  39.9 5.3 %collective-permute-start.17 = (bf16[64,128]{1,0:T(8,128)(2,1)S(1)}, bf16[64,128]{1,0:T(8,128)(2,1)S(1)}, u32[]{:S(2)}, u32[]{:S(2)}) collective-permute-start(bf16[64,128]{1,0:T(8,128)(2,1)S(1)} %get-tuple-element.71), channel_id=1, source_target_pairs={{1,2},{3,4},{5,6},{7,8},{9,10},{11,12},{13,14},{15,0},{2,1},{4,3},... | collective-permute-start | bytes 49160 | tf_op jit(solution)/shard_map/ppermute | solution.py:417
  41.0 4.1 %copy-start.1 = (bf16[4,64,4]{1,2,0:T(4,128)(2,1)S(1)}, bf16[4,64,4]{1,2,0:T(4,128)(2,1)}, u32[]{:S(2)}) copy-start(bf16[4,64,4]{1,2,0:T(4,128)(2,1)} %param.10) | copy-start | bytes 6148
  41.0 4.1 %copy-start.2 = (s32[4]{0:T(128)S(1)}, s32[4]{0:T(128)}, u32[]{:S(2)}) copy-start(s32[4]{0:T(128)} %port_ref.3) | copy-start | bytes 52
  51.0 8.4 %collective-permute-start.18 = (bf16[64,512]{1,0:T(8,128)(2,1)S(1)}, bf16[64,512]{1,0:T(8,128)(2,1)S(1)}, u32[]{:S(2)}, u32[]{:S(2)}) collective-permute-start(bf16[64,512]{1,0:T(8,128)(2,1)S(1)} %get-tuple-element.73), channel_id=1, source_target_pairs={{0,16},{32,48},{64,80},{96,112},{16,0},{48,32},{80,64},{112,96},{1... | collective-permute-start | bytes 196616 | tf_op jit(solution)/shard_map/ppermute | solution.py:417
  51.1 8.3 %collective-permute-start.19 = (bf16[64,512]{1,0:T(8,128)(2,1)S(1)}, bf16[64,512]{1,0:T(8,128)(2,1)S(1)}, u32[]{:S(2)}, u32[]{:S(2)}) collective-permute-start(bf16[64,512]{1,0:T(8,128)(2,1)S(1)} %get-tuple-element.74), channel_id=1, source_target_pairs={{16,32},{48,64},{80,96},{112,0},{32,16},{64,48},{96,80},{0,112},{1... | collective-permute-start | bytes 196616 | tf_op jit(solution)/shard_map/ppermute | solution.py:417
  54.1 1.2 %collective-permute-start.20 = (bf16[64,128]{1,0:T(8,128)(2,1)S(1)}, bf16[64,128]{1,0:T(8,128)(2,1)S(1)}, u32[]{:S(2)}, u32[]{:S(2)}) collective-permute-start(bf16[64,128]{1,0:T(8,128)(2,1)S(1)} %get-tuple-element.75), channel_id=1, source_target_pairs={{0,1},{2,3},{4,5},{6,7},{8,9},{10,11},{12,13},{14,15},{1,0},{3,2},... | collective-permute-start | bytes 49160 | tf_op jit(solution)/shard_map/ppermute | solution.py:417
  54.1 5.3 %collective-permute-start.21 = (bf16[64,128]{1,0:T(8,128)(2,1)S(1)}, bf16[64,128]{1,0:T(8,128)(2,1)S(1)}, u32[]{:S(2)}, u32[]{:S(2)}) collective-permute-start(bf16[64,128]{1,0:T(8,128)(2,1)S(1)} %get-tuple-element.76), channel_id=1, source_target_pairs={{1,2},{3,4},{5,6},{7,8},{9,10},{11,12},{13,14},{15,0},{2,1},{4,3},... | collective-permute-start | bytes 49160 | tf_op jit(solution)/shard_map/ppermute | solution.py:417

commit v12 on v11

--- a/solution.py
+++ b/solution.py
@@ -116,7 +116,12 @@
     return (partial + other).astype(BF), x, sides
 
 
-MAP_STEPS = ((0, 0), (1, 3), (2, 7), (6, 5), (3, 1), (7, 2), (5, 6), (4, 4))
+MAP_STEPS = ((0, 0), (2, 3), (6, 7), (3, 2), (7, 6), (4, 5), (5, 4), (1, 1))
+
+
+def relay_kernel(first_ref, second_ref, out_ref):
+    core = lax.rem(lax.axis_index("col"), 2)
+    out_ref[...] = jnp.where(core == 0, second_ref[...], first_ref[...])
 
 
 def even(axis):
@@ -143,15 +148,12 @@
     return jnp.broadcast_to(value[:, lane : lane + 1], (value.shape[0], LANES))
 
 
-def port_profile_column(profile_ref, port):
-    edges, _, samples = profile_ref.shape
+def port_profile_column(profile_ref, port, edge):
+    samples = profile_ref.shape[2]
     row = lax.broadcasted_iota(jnp.int32, (samples, samples), 0)
     col = lax.broadcasted_iota(jnp.int32, (samples, samples), 1)
-    columns = []
-    for edge in range(edges):
-        line = jnp.broadcast_to(profile_ref[edge].astype(F32)[port : port + 1], row.shape)
-        columns.append(jnp.sum(jnp.where(row == col, line, 0.0), axis=1, keepdims=True))
-    return jnp.concatenate(columns, axis=0)
+    line = jnp.broadcast_to(profile_ref[edge].astype(F32)[port : port + 1], row.shape)
+    return jnp.sum(jnp.where(row == col, line, 0.0), axis=1, keepdims=True)
 
 
 def port_place(port_ref, port, rows, width):
@@ -339,7 +341,8 @@
         row, col, inside = port_place(port_ref, port, rows, width)
         here = place_in_tile == jnp.where(inside, row * width + col, -1)
         current = block.astype(F32)
-        added = current + port_profile_column(profile_ref, port)
+        columns = [port_profile_column(profile_ref, port, edge) for edge in range(4)]
+        added = current + jnp.concatenate(columns, axis=0)
         block = jnp.where(here, added, current).astype(BF)
         total = products(block, types, maps, 0, order)
         north, south = shifted(total, next_ref.at[:, own], rows)
@@ -395,7 +398,7 @@
                 here = (lax.broadcasted_iota(jnp.int32, current.shape, 1) == row) & (
                     lax.broadcasted_iota(jnp.int32, current.shape, 2) == col
                 )
-                profile = port_profile_column(profile_ref, port)[lines]
+                profile = port_profile_column(profile_ref, port, edge)
                 profile = jnp.broadcast_to(profile, (quarter, LANES)).reshape(quarter, 1, LANES)
                 added = current + jnp.broadcast_to(profile, current.shape)
                 buffer[lines, port] = jnp.where(here, added, current).astype(BF)
@@ -426,10 +429,9 @@
     own_map, x, sides = own_type_map(mode_shapes, mode_values, mode_weights, traces, types)
     core = lax.rem(lax.axis_index("col"), 2)
     half = lax.dynamic_slice_in_dim(own_map, core * (order // 2), order // 2)
-    fetched = [
-        swap(own_map, *((step, 8 * (step % 2)) for step in steps)) for steps in MAP_STEPS[1:4]
-    ]
-    half = swap(half, (4, 0))
+    first = swap(own_map, (2, 0), (3, 8))
+    second = swap(own_map, (6, 0), (7, 8))
+    half = swap(half, (1, 8))
     profile = jnp.transpose(port_profile, (0, 2, 1))
     ports_spec = pl.BlockSpec(memory_space=pltpu.SMEM)
     next_shape = jax.ShapeDtypeStruct((order, ports * tile), BF)
@@ -445,17 +447,18 @@
         flops = work * len(maps) // 7
         return whole_call(kernel, part_shapes, x, types, *sides, *maps, *parts, flops=flops)
 
-    parts = list(early(0, [own_map, fetched[0]]))
-    parts[1], fetched = lax.optimization_barrier((parts[1], fetched))
-    swapped = [swap_cores(value) for value in fetched]
-    parts = list(early(2, fetched[1:], parts))
-    parts[1], half = lax.optimization_barrier((parts[1], half))
-    swapped.append(swap_cores(half))
+    parts = list(early(0, [own_map, first]))
+    parts[1], first, second = lax.optimization_barrier((parts[1], first, second))
+    map_shape = jax.ShapeDtypeStruct(own_map.shape, BF)
+    third = swap(whole_call(relay_kernel, [map_shape], first, second)[0], (2, 0), (6, 0))
+    maps = [own_map, first, second, swap_cores(first), swap_cores(second)]
+    parts = list(early(2, maps[2:], parts))
+    parts[1], third, half = lax.optimization_barrier((parts[1], third, half))
     done, *parts = parts
-    late = swapped + [half]
-    maps = [own_map] + fetched + late
+    late = [third, swap_cores(third), swap_cores(half), half]
+    maps += late
     sent = whole_call(
-        functools.partial(rim_kernel, ports, 4),
+        functools.partial(rim_kernel, ports, 5),
         rim_shapes,
         x,
         types,
@@ -466,7 +469,7 @@
     )
     halos = exchange(sent)
     (x,) = whole_call(
-        functools.partial(first_kernel, rows, ports, 4),
+        functools.partial(first_kernel, rows, ports, 5),
         [next_shape],
         x,
         types,

time: 63.5 us -> 64.8 us (1.020)
  waiting for transfers between devices: 16.7 us -> 10.8 us
  starting transfers between devices: 25.4 us -> 30.2 us
  local copies, waits for them, and re-layouts: 0.67 us -> 3.58 us
    ppermute x14, waiting for transfers between devices: 10.7 us -> 6.27 us  [swap(): return lax.ppermute(value, ('row', 'col'), pairs)]
    unnamed x6 -> x10, local copies, waits for them, and re-layouts: 0.01 us -> 2.91 us
    ppermute x14, starting transfers between devices: 15.2 us -> 17.7 us  [swap(): return lax.ppermute(value, ('row', 'col'), pairs)]
    ppermute x8, starting transfers between devices: 10.3 us -> 12.5 us  [exchange(): lax.ppermute(rim, axis, pairs(axis, first))]
    ppermute x8, waiting for transfers between devices: 6.07 us -> 4.52 us  [exchange(): lax.ppermute(rim, axis, pairs(axis, first))]
    pallas_call x6 -> x7, Pallas kernels: 7.77 us -> 7.8 us  [whole_call(): pl.pallas_call(kernel, in_specs=[WHOLE] * len(operands), out_specs=[WHOLE...]
  transfers between devices with their start and end apart: 22 -> 22, of which waited for: 9 -> 7; matrix products, arithmetic and copies ran while one was open for 0% -> 0% of each run, Pallas kernels for 14% -> 14%
where the time goes in v12:
time: 64.8 us; the launch traced here: 64.5 us
  starting transfers between devices  30.2 us (47%)
  Pallas kernels  18.8 us (29%)
  waiting for transfers between devices  10.8 us (17%)
  local copies, waits for them, and re-layouts  3.58 us (6%)
  other arithmetic  0.85 us (1%)
    ppermute x14, starting transfers between devices, swap(): return lax.ppermute(value, ('row', 'col'), pairs)  17.7 us
    ppermute x8, starting transfers between devices, exchange(): lax.ppermute(rim, axis, pairs(axis, first))  12.5 us
    pallas_call x7, Pallas kernels, whole_call(): pl.pallas_call(kernel, in_specs=[WHOLE] * len(operands), out_specs=[WHOLE...  7.8 us
    ppermute x14, waiting for transfers between devices, swap(): return lax.ppermute(value, ('row', 'col'), pairs)  6.27 us
    pallas_call x1, Pallas kernels, body(): pl.pallas_call(functools.partial(second_kernel, rows, width), in_specs=[p...  5.75 us
    ppermute x8, waiting for transfers between devices, exchange(): lax.ppermute(rim, axis, pairs(axis, first))  4.52 us
    pallas_call x1, Pallas kernels, body(): pl.pallas_call(functools.partial(last_kernel, rows, width), in_specs=[por...  3.32 us
    unnamed x10, local copies, waits for them, and re-layouts  2.91 us
  transfers between devices with their start and end apart: 22, of which 7 were waited for; matrix products, arithmetic and copies ran while one was open for 0% of the time, Pallas kernels for 14%

profile of v12, /device:TPU:0, one launch (start us, length us, event | category | flops | bytes accessed | tf_op | source)
XLA Modules:
  0.0 64.5 jit_solution(5646195778943228730)
XLA Ops:
  0.0 0.7 %concatenate.10 = f32[32]{0:T(128)S(1)} pad(f32[16]{0:T(128)} %bitcast.20, f32[]{:T(128)} %constant.6.clone.1), padding=0_16 | pad | bytes 196 | tf_op jit(solution)/shard_map/concatenate | solution.py:82
  0.7 0.8 %maximum_multiply_fusion.refs_0_ = f32[32,256]{1,0:T(8,128)S(1)} fusion(f32[16,256]{1,0:T(8,128)} %bitcast.18, f32[16,256]{1,0:T(8,128)} %bitcast.19, f32[32]{0:T(128)S(1)} %concatenate.10), kind=kLoop, calls=%fused_computation.2 | loop fusion | flops 16384 | bytes 65664 | tf_op jit(solution)/shard_map/mul | solution.py:82
  1.5 0.0 collective-permute-start.1
  1.5 4.0 %collective-permute-start = (f32[32,256]{1,0:T(8,128)S(1)}, f32[32,256]{1,0:T(8,128)S(1)}, u32[]{:S(2)}, u32[]{:S(2)}) collective-permute-start(f32[32,256]{1,0:T(8,128)S(1)} %maximum_multiply_fusion.refs_0_), channel_id=1, source_target_pairs={{0,4},{1,5},{2,6},{3,7},{4,0},{5,1},{6,2},{7,3},{8,12},{9,13},{10,... | collective-permute-start | bytes 98312 | tf_op jit(solution)/shard_map/ppermute | solution.py:26
  5.5 0.0 collective-permute-done.1
  5.5 1.6 %collective-permute-start.2 = (f32[64,256]{1,0:T(8,128)S(1)}, f32[64,256]{1,0:T(8,128)S(1)}, u32[]{:S(2)}, u32[]{:S(2)}) collective-permute-start(f32[64,256]{1,0:T(8,128)S(1)} %pad_maximum_fusion), channel_id=1, source_target_pairs={{0,8},{1,11},{2,10},{3,9},{4,12},{5,15},{6,14},{7,13},{8,0},{9,3},... | collective-permute-start | bytes 196616 | tf_op jit(solution)/shard_map/ppermute | solution.py:26
  7.0 1.0 %collective-permute-start.3 = (f32[64,256]{1,0:T(8,128)S(1)}, f32[64,256]{1,0:T(8,128)S(1)}, u32[]{:S(2)}, u32[]{:S(2)}) collective-permute-start(f32[64,256]{1,0:T(8,128)S(1)} %pad_maximum_fusion), channel_id=1, source_target_pairs={{0,2},{1,15},{2,0},{3,13},{4,6},{5,11},{6,4},{7,9},{8,10},{9,7},{1... | collective-permute-start | bytes 196616 | tf_op jit(solution)/shard_map/ppermute | solution.py:26
  8.1 0.6 collective-permute-start.4
  8.7 0.0 copy-start
  8.7 2.0 %shard_map.73.x_ref = bf16[256,4096]{1,0:T(8,128)(2,1)S(1)} custom-call(bf16[256,4,8,128]{3,2,1,0:T(8,128)(2,1)} %bitcast.17), custom_call_target="tpu_custom_call" | custom-call | flops 1073741824 | tf_op jit(solution)/shard_map/pallas_call | solution.py:89
  10.7 0.0 collective-permute-done.2.refs_2_
  10.7 0.6 collective-permute-done.3.refs_3_
  11.3 2.9 %collective-permute-done.4.refs_4_ = f32[64,256]{1,0:T(8,128)S(1)} collective-permute-done((f32[64,256]{1,0:T(8,128)S(1)}, f32[64,256]{1,0:T(8,128)S(1)}, u32[]{:S(2)}, u32[]{:S(2)}) %collective-permute-start.4) | collective-permute-done | bytes 65568 | tf_op jit(solution)/shard_map/ppermute | solution.py:26
  14.2 0.0 collective-permute-done.refs_1_
  14.2 0.4 shard_map.74
  14.6 0.1 collective-permute-start.5
  14.7 0.0 copy-done
  14.7 1.2 %shard_map.75 = (bf16[256,128]{1,0:T(8,128)(2,1)S(1)}, bf16[16,128]{1,0:T(8,128)(2,1)S(1)}) custom-call(bf16[256,4096]{1,0:T(8,128)(2,1)S(1)} %shard_map.73.x_ref, s32[1,1024]{1,0:T(1,128)S(1)} %bitcast.9), custom_call_target="tpu_custom_call" | custom-call | flops 1073741824 | tf_op jit(solution)/shard_map/pallas_call | solution.py:69
  15.9 0.3 collective-permute-done.5
  16.3 1.7 %collective-permute-start.6 = (bf16[256,256]{1,0:T(8,128)(2,1)S(1)}, bf16[256,256]{1,0:T(8,128)(2,1)S(1)}, u32[]{:S(2)}, u32[]{:S(2)}) collective-permute-start(bf16[256,256]{1,0:T(8,128)(2,1)S(1)} %add_convert_fusion.refs_0_.refs_4_), channel_id=1, source_target_pairs={{0,32},{1,57},{2,34},{3,59},{4,36},{5,61},{6,38},{7,63},{8,40},{9,... | collective-permute-start | bytes 393224 | tf_op jit(solution)/shard_map/ppermute | solution.py:26
  18.0 2.2 %collective-permute-start.7 = (bf16[256,256]{1,0:T(8,128)(2,1)S(1)}, bf16[256,256]{1,0:T(8,128)(2,1)S(1)}, u32[]{:S(2)}, u32[]{:S(2)}) collective-permute-start(bf16[256,256]{1,0:T(8,128)(2,1)S(1)} %add_convert_fusion.refs_0_.refs_4_), channel_id=1, source_target_pairs={{0,96},{1,121},{2,98},{3,123},{4,100},{5,125},{6,102},{7,127},{8,1... | collective-permute-start | bytes 393224 | tf_op jit(solution)/shard_map/ppermute | solution.py:26
  20.1 1.2 %collective-permute-done.6.refs_1_.first_ref.refs_5_ = bf16[256,256]{1,0:T(8,128)(2,1)S(1)} collective-permute-done((bf16[256,256]{1,0:T(8,128)(2,1)S(1)}, bf16[256,256]{1,0:T(8,128)(2,1)S(1)}, u32[]{:S(2)}, u32[]{:S(2)}) %collective-permute-start.6) | collective-permute-done | bytes 131104 | tf_op jit(solution)/shard_map/ppermute | solution.py:26
  21.4 1.5 %shard_map.76 = (bf16[256,4096]{1,0:T(8,128)(2,1)S(1)}, bf16[64,512]{1,0:T(8,128)(2,1)S(1)}, bf16[64,512]{1,0:T(8,128)(2,1)S(1)}, bf16[128,128]{1,0:T(8,128)(2,1)S(1)}) custom-call(bf16[256,4096]{1,0:T(8,128)(2,1)S(1)} %shard_map.73.x_ref, s32[1,1024]{1,0:T(1,128)S(1)} %bitcast.10, bf16[256,128]{1,0:T(8,128)(2,1)S(1)} %get-tuple-element.51.sides_ref, ...), custom_call_target="tpu_custom_call" | custom-call | flops 1227133568 | tf_op jit(solution)/shard_map/pallas_call | solution.py:69
  22.9 0.0 copy-start.3
  22.9 1.3 %copy-done.3 = bf16[256,4096]{1,0:T(8,128)(2,1)} copy-done((bf16[256,4096]{1,0:T(8,128)(2,1)}, bf16[256,4096]{1,0:T(8,128)(2,1)S(1)}, u32[]{:S(2)}) %copy-start.3) | copy-done | bytes 2097176
  24.2 0.0 collective-permute-done.7.refs_0_.second_ref.refs_6_
  24.2 2.4 %collective-permute-start.8 = (bf16[256,256]{1,0:T(8,128)(2,1)S(1)}, bf16[256,256]{1,0:T(8,128)(2,1)S(1)}, u32[]{:S(2)}, u32[]{:S(2)}) collective-permute-start(bf16[256,256]{1,0:T(8,128)(2,1)S(1)} %collective-permute-done.6.refs_1_.first_ref.refs_5_), channel_id=1, source_target_pairs={{0,1},{1,0},{2,3},{3,2},{4,5},{5,4},{6,7},{7,6},{8,9},{9,8},{10,11... | collective-permute-start | bytes 393224 | tf_op jit(solution)/shard_map/ppermute | solution.py:26
  26.5 0.0 collective-permute-start.9
  26.5 1.3 %collective-permute-start.11 = (bf16[128,256]{1,0:T(8,128)(2,1)S(1)}, bf16[128,256]{1,0:T(8,128)(2,1)S(1)}, u32[]{:S(2)}, u32[]{:S(2)}) collective-permute-start(bf16[128,256]{1,0:T(8,128)(2,1)S(1)} %constant_dynamic-slice_fusion), channel_id=1, source_target_pairs={{0,24},{1,25},{2,26},{3,27},{4,28},{5,29},{6,30},{7,31},{8,16},{9,... | collective-permute-start | bytes 196616 | tf_op jit(solution)/shard_map/ppermute | solution.py:26
  27.8 1.4 %collective-permute-start.10 = (bf16[256,256]{1,0:T(8,128)(2,1)S(1)}, bf16[256,256]{1,0:T(8,128)(2,1)S(1)}, u32[]{:S(2)}, u32[]{:S(2)}) collective-permute-start(bf16[256,256]{1,0:T(8,128)(2,1)S(1)} %shard_map.78), channel_id=1, source_target_pairs={{0,32},{1,97},{2,34},{3,99},{4,36},{5,101},{6,38},{7,103},{8,40},{... | collective-permute-start | bytes 393224 | tf_op jit(solution)/shard_map/ppermute | solution.py:26
  29.3 0.0 collective-permute-done.8.refs_1_.refs_7_
  29.3 0.0 collective-permute-done.9.refs_2_.refs_8_
  29.3 0.0 copy-start.4
  29.3 1.6 %copy-done.4 = bf16[256,4096]{1,0:T(8,128)(2,1)S(1)} copy-done((bf16[256,4096]{1,0:T(8,128)(2,1)S(1)}, bf16[256,4096]{1,0:T(8,128)(2,1)}, u32[]{:S(2)}) %copy-start.4) | copy-done | bytes 2097176
  30.9 2.2 %shard_map.77 = (bf16[256,4096]{1,0:T(8,128)(2,1)S(1)}, bf16[64,512]{1,0:T(8,128)(2,1)S(1)}, bf16[64,512]{1,0:T(8,128)(2,1)S(1)}, bf16[128,128]{1,0:T(8,128)(2,1)S(1)}) custom-call(bf16[256,4096]{1,0:T(8,128)(2,1)S(1)} %shard_map.73.x_ref, s32[1,1024]{1,0:T(1,128)S(1)} %bitcast.11, bf16[256,128]{1,0:T(8,128)(2,1)S(1)} %get-tuple-element.51.sides_ref, ...), custom_call_target="tpu_custom_call" | custom-call | flops 1840700288 | tf_op jit(solution)/shard_map/pallas_call | solution.py:69
  33.1 0.0 collective-permute-done.11.refs_3_.refs_12_
  33.1 0.0 collective-permute-done.10.refs_0_.refs_9_
  33.1 1.4 %collective-permute-start.12 = (bf16[256,256]{1,0:T(8,128)(2,1)S(1)}, bf16[256,256]{1,0:T(8,128)(2,1)S(1)}, u32[]{:S(2)}, u32[]{:S(2)}) collective-permute-start(bf16[256,256]{1,0:T(8,128)(2,1)S(1)} %collective-permute-done.10.refs_0_.refs_9_), channel_id=1, source_target_pairs={{0,1},{1,0},{2,3},{3,2},{4,5},{5,4},{6,7},{7,6},{8,9},{9,8},{10,11... | collective-permute-start | bytes 393224 | tf_op jit(solution)/shard_map/ppermute | solution.py:26
  34.5 0.1 collective-permute-start.13
  34.6 1.2 %collective-permute-done.13.refs_2_.refs_11_ = bf16[128,256]{1,0:T(8,128)(2,1)S(1)} collective-permute-done((bf16[128,256]{1,0:T(8,128)(2,1)S(1)}, bf16[128,256]{1,0:T(8,128)(2,1)S(1)}, u32[]{:S(2)}, u32[]{:S(2)}) %collective-permute-start.13) | collective-permute-done | bytes 65568 | tf_op jit(solution)/shard_map/ppermute | solution.py:26
  35.8 0.0 collective-permute-done.12.refs_1_.refs_10_
  35.8 0.5 shard_map.80
  36.3 1.3 %collective-permute-start.14 = (bf16[64,512]{1,0:T(8,128)(2,1)S(1)}, bf16[64,512]{1,0:T(8,128)(2,1)S(1)}, u32[]{:S(2)}, u32[]{:S(2)}) collective-permute-start(bf16[64,512]{1,0:T(8,128)(2,1)S(1)} %get-tuple-element.68), channel_id=1, source_target_pairs={{0,16},{32,48},{64,80},{96,112},{16,0},{48,32},{80,64},{112,96},{1... | collective-permute-start | bytes 196616 | tf_op jit(solution)/shard_map/ppermute | solution.py:420
  37.6 3.2 %collective-permute-start.15 = (bf16[64,512]{1,0:T(8,128)(2,1)S(1)}, bf16[64,512]{1,0:T(8,128)(2,1)S(1)}, u32[]{:S(2)}, u32[]{:S(2)}) collective-permute-start(bf16[64,512]{1,0:T(8,128)(2,1)S(1)} %get-tuple-element.69), channel_id=1, source_target_pairs={{16,32},{48,64},{80,96},{112,0},{32,16},{64,48},{96,80},{0,112},{1... | collective-permute-start | bytes 196616 | tf_op jit(solution)/shard_map/ppermute | solution.py:420
  40.7 0.0 collective-permute-start.16
  40.7 2.3 %collective-permute-start.17 = (bf16[64,128]{1,0:T(8,128)(2,1)S(1)}, bf16[64,128]{1,0:T(8,128)(2,1)S(1)}, u32[]{:S(2)}, u32[]{:S(2)}) collective-permute-start(bf16[64,128]{1,0:T(8,128)(2,1)S(1)} %get-tuple-element.71), channel_id=1, source_target_pairs={{1,2},{3,4},{5,6},{7,8},{9,10},{11,12},{13,14},{15,0},{2,1},{4,3},... | collective-permute-start | bytes 49160 | tf_op jit(solution)/shard_map/ppermute | solution.py:420
  43.0 0.0 copy-start.1
  43.0 2.0 %shard_map.79.x_ref = bf16[256,4096]{1,0:T(8,128)(2,1)S(1)} custom-call(bf16[256,4096]{1,0:T(8,128)(2,1)S(1)} %shard_map.73.x_ref, s32[1,1024]{1,0:T(1,128)S(1)} %bitcast.13, bf16[256,4096]{1,0:T(8,128)(2,1)S(1)} %get-tuple-element.61.done_ref, bf16[256,256]{1,0:T(8,128)(2,1)S(1)} %collective-permute-done.10.refs_0_.refs_9_, ...), custom_call_target="tpu_custom_call" | custom-call | flops 2147483648 | tf_op jit(solution)/shard_map/pallas_call | solution.py:69
  45.0 0.0 collective-permute-done.16.refs_2_
  45.0 1.0 %collective-permute-done.17.refs_3_ = bf16[64,128]{1,0:T(8,128)(2,1)S(1)} collective-permute-done((bf16[64,128]{1,0:T(8,128)(2,1)S(1)}, bf16[64,128]{1,0:T(8,128)(2,1)S(1)}, u32[]{:S(2)}, u32[]{:S(2)}) %collective-permute-start.17) | collective-permute-done | bytes 16416 | tf_op jit(solution)/shard_map/ppermute | solution.py:420
  46.0 0.0 collective-permute-done.14.refs_0_
  46.0 0.0 collective-permute-done.15.refs_1_
  46.0 0.0 copy-done.1
  46.0 0.0 copy-done.2
  46.0 5.7 %shard_map.81 = (bf16[256,4096]{1,0:T(8,128)(2,1)S(1)}, bf16[64,512]{1,0:T(8,128)(2,1)S(1)}, bf16[64,512]{1,0:T(8,128)(2,1)S(1)}, bf16[64,128]{1,0:T(8,128)(2,1)S(1)}, bf16[64,128]{1,0:T(8,128)(2,1)S(1)}) custom-call(s32[4]{0:T(128)S(1)} %copy-done.2, bf16[256,4096]{1,0:T(8,128)(2,1)S(1)} %shard_map.79.x_ref, s32[1,1024]{1,0:T(1,128)S(1)} %bitcast.14, ...), custom_call_target="tpu_custom_call" | custom-call | flops 4294967296 | tf_op jit(solution)/shard_map/pallas_call | solution.py:481
  51.8 0.6 collective-permute-start.18
  52.4 3.4 %collective-permute-start.19 = (bf16[64,512]{1,0:T(8,128)(2,1)S(1)}, bf16[64,512]{1,0:T(8,128)(2,1)S(1)}, u32[]{:S(2)}, u32[]{:S(2)}) collective-permute-start(bf16[64,512]{1,0:T(8,128)(2,1)S(1)} %get-tuple-element.74), channel_id=1, source_target_pairs={{16,32},{48,64},{80,96},{112,0},{32,16},{64,48},{96,80},{0,112},{1... | collective-permute-start | bytes 196616 | tf_op jit(solution)/shard_map/ppermute | solution.py:420
  55.8 0.0 collective-permute-start.20
  55.8 1.8 %collective-permute-start.21 = (bf16[64,128]{1,0:T(8,128)(2,1)S(1)}, bf16[64,128]{1,0:T(8,128)(2,1)S(1)}, u32[]{:S(2)}, u32[]{:S(2)}) collective-permute-start(bf16[64,128]{1,0:T(8,128)(2,1)S(1)} %get-tuple-element.76), channel_id=1, source_target_pairs={{1,2},{3,4},{5,6},{7,8},{9,10},{11,12},{13,14},{15,0},{2,1},{4,3},... | collective-permute-start | bytes 49160 | tf_op jit(solution)/shard_map/ppermute | solution.py:420
  57.5 0.0 collective-permute-done.20.refs_2_
  57.5 3.5 %collective-permute-done.21.refs_3_ = bf16[64,128]{1,0:T(8,128)(2,1)S(1)} collective-permute-done((bf16[64,128]{1,0:T(8,128)(2,1)S(1)}, bf16[64,128]{1,0:T(8,128)(2,1)S(1)}, u32[]{:S(2)}, u32[]{:S(2)}) %collective-permute-start.21) | collective-permute-done | bytes 16416 | tf_op jit(solution)/shard_map/ppermute | solution.py:420
  61.1 0.0 collective-permute-done.18.refs_0_
  61.1 0.0 collective-permute-done.19.refs_1_
  61.1 3.3 %shard_map.82 = bf16[256,4,8,128]{3,2,1,0:T(8,128)(2,1)} custom-call(s32[4]{0:T(128)S(1)} %copy-done.2, bf16[256,4096]{1,0:T(8,128)(2,1)S(1)} %get-tuple-element.72.x_ref, bf16[4,4,64]{2,1,0:T(4,128)(2,1)S(1)} %bitcast.16, bf16[64,512]{1,0:T(8,128)(2,1)S(1)} %collective-permute-done.18.refs_0_, bf16[64,512]{1,0:T(8,128)(2,1)S(1)} %collective-permute-done.19.refs_1_, ...), custom_call_target="tpu_custom_call" | custom-call | tf_op jit(solution)/shard_map/pallas_call | solution.py:490
  (5 shorter events, 0.1 us)
Async XLA Ops:
  1.5 4.0 %collective-permute-start.1 = (f32[32,256]{1,0:T(8,128)S(1)}, f32[32,256]{1,0:T(8,128)S(1)}, u32[]{:S(2)}, u32[]{:S(2)}) collective-permute-start(f32[32,256]{1,0:T(8,128)S(1)} %maximum_multiply_fusion.refs_0_), channel_id=1, source_target_pairs={{0,1},{1,0},{2,3},{3,2},{4,5},{5,4},{6,7},{7,6},{8,9},{9,8},{10,11... | collective-permute-start | bytes 98312 | tf_op jit(solution)/shard_map/ppermute | solution.py:26
  1.5 12.8 %collective-permute-start = (f32[32,256]{1,0:T(8,128)S(1)}, f32[32,256]{1,0:T(8,128)S(1)}, u32[]{:S(2)}, u32[]{:S(2)}) collective-permute-start(f32[32,256]{1,0:T(8,128)S(1)} %maximum_multiply_fusion.refs_0_), channel_id=1, source_target_pairs={{0,4},{1,5},{2,6},{3,7},{4,0},{5,1},{6,2},{7,3},{8,12},{9,13},{10,... | collective-permute-start | bytes 98312 | tf_op jit(solution)/shard_map/ppermute | solution.py:26
  5.5 5.2 %collective-permute-start.2 = (f32[64,256]{1,0:T(8,128)S(1)}, f32[64,256]{1,0:T(8,128)S(1)}, u32[]{:S(2)}, u32[]{:S(2)}) collective-permute-start(f32[64,256]{1,0:T(8,128)S(1)} %pad_maximum_fusion), channel_id=1, source_target_pairs={{0,8},{1,11},{2,10},{3,9},{4,12},{5,15},{6,14},{7,13},{8,0},{9,3},... | collective-permute-start | bytes 196616 | tf_op jit(solution)/shard_map/ppermute | solution.py:26
  7.0 4.3 %collective-permute-start.3 = (f32[64,256]{1,0:T(8,128)S(1)}, f32[64,256]{1,0:T(8,128)S(1)}, u32[]{:S(2)}, u32[]{:S(2)}) collective-permute-start(f32[64,256]{1,0:T(8,128)S(1)} %pad_maximum_fusion), channel_id=1, source_target_pairs={{0,2},{1,15},{2,0},{3,13},{4,6},{5,11},{6,4},{7,9},{8,10},{9,7},{1... | collective-permute-start | bytes 196616 | tf_op jit(solution)/shard_map/ppermute | solution.py:26
  8.1 6.2 %collective-permute-start.4 = (f32[64,256]{1,0:T(8,128)S(1)}, f32[64,256]{1,0:T(8,128)S(1)}, u32[]{:S(2)}, u32[]{:S(2)}) collective-permute-start(f32[64,256]{1,0:T(8,128)S(1)} %pad_maximum_fusion), channel_id=1, source_target_pairs={{0,6},{1,13},{2,4},{3,15},{4,2},{5,9},{6,0},{7,11},{8,14},{9,5},{1... | collective-permute-start | bytes 196616 | tf_op jit(solution)/shard_map/ppermute | solution.py:26
  8.7 6.0 %copy-start = (s32[8,128]{1,0:T(8,128)S(1)}, s32[8,128]{1,0:T(8,128)}, u32[]{:S(2)}) copy-start(s32[8,128]{1,0:T(8,128)} %param.8) | copy-start | bytes 12292
  14.6 1.6 %collective-permute-start.5 = (f32[256,256]{1,0:T(8,128)S(1)}, f32[256,256]{1,0:T(8,128)S(1)}, u32[]{:S(2)}, u32[]{:S(2)}) collective-permute-start(f32[256,256]{1,0:T(8,128)S(1)} %shard_map.74), channel_id=1, source_target_pairs={{0,1},{1,0},{2,3},{3,2},{4,5},{5,4},{6,7},{7,6},{8,9},{9,8},{10,11... | collective-permute-start | bytes 786440 | tf_op jit(solution)/shard_map/ppermute | solution.py:26
  16.3 5.1 %collective-permute-start.6 = (bf16[256,256]{1,0:T(8,128)(2,1)S(1)}, bf16[256,256]{1,0:T(8,128)(2,1)S(1)}, u32[]{:S(2)}, u32[]{:S(2)}) collective-permute-start(bf16[256,256]{1,0:T(8,128)(2,1)S(1)} %add_convert_fusion.refs_0_.refs_4_), channel_id=1, source_target_pairs={{0,32},{1,57},{2,34},{3,59},{4,36},{5,61},{6,38},{7,63},{8,40},{9,... | collective-permute-start | bytes 393224 | tf_op jit(solution)/shard_map/ppermute | solution.py:26
  18.0 6.2 %collective-permute-start.7 = (bf16[256,256]{1,0:T(8,128)(2,1)S(1)}, bf16[256,256]{1,0:T(8,128)(2,1)S(1)}, u32[]{:S(2)}, u32[]{:S(2)}) collective-permute-start(bf16[256,256]{1,0:T(8,128)(2,1)S(1)} %add_convert_fusion.refs_0_.refs_4_), channel_id=1, source_target_pairs={{0,96},{1,121},{2,98},{3,123},{4,100},{5,125},{6,102},{7,127},{8,1... | collective-permute-start | bytes 393224 | tf_op jit(solution)/shard_map/ppermute | solution.py:26
  22.9 1.3 %copy-start.3 = (bf16[256,4096]{1,0:T(8,128)(2,1)}, bf16[256,4096]{1,0:T(8,128)(2,1)S(1)}, u32[]{:S(2)}) copy-start(bf16[256,4096]{1,0:T(8,128)(2,1)S(1)} %get-tuple-element.57.refs_3_) | copy-start | bytes 6291460
  24.2 5.1 %collective-permute-start.8 = (bf16[256,256]{1,0:T(8,128)(2,1)S(1)}, bf16[256,256]{1,0:T(8,128)(2,1)S(1)}, u32[]{:S(2)}, u32[]{:S(2)}) collective-permute-start(bf16[256,256]{1,0:T(8,128)(2,1)S(1)} %collective-permute-done.6.refs_1_.first_ref.refs_5_), channel_id=1, source_target_pairs={{0,1},{1,0},{2,3},{3,2},{4,5},{5,4},{6,7},{7,6},{8,9},{9,8},{10,11... | collective-permute-start | bytes 393224 | tf_op jit(solution)/shard_map/ppermute | solution.py:26
  26.5 2.8 %collective-permute-start.9 = (bf16[256,256]{1,0:T(8,128)(2,1)S(1)}, bf16[256,256]{1,0:T(8,128)(2,1)S(1)}, u32[]{:S(2)}, u32[]{:S(2)}) collective-permute-start(bf16[256,256]{1,0:T(8,128)(2,1)S(1)} %collective-permute-done.7.refs_0_.second_ref.refs_6_), channel_id=1, source_target_pairs={{0,1},{1,0},{2,3},{3,2},{4,5},{5,4},{6,7},{7,6},{8,9},{9,8},{10,11... | collective-permute-start | bytes 393224 | tf_op jit(solution)/shard_map/ppermute | solution.py:26
  26.5 6.6 %collective-permute-start.11 = (bf16[128,256]{1,0:T(8,128)(2,1)S(1)}, bf16[128,256]{1,0:T(8,128)(2,1)S(1)}, u32[]{:S(2)}, u32[]{:S(2)}) collective-permute-start(bf16[128,256]{1,0:T(8,128)(2,1)S(1)} %constant_dynamic-slice_fusion), channel_id=1, source_target_pairs={{0,24},{1,25},{2,26},{3,27},{4,28},{5,29},{6,30},{7,31},{8,16},{9,... | collective-permute-start | bytes 196616 | tf_op jit(solution)/shard_map/ppermute | solution.py:26
  27.8 5.3 %collective-permute-start.10 = (bf16[256,256]{1,0:T(8,128)(2,1)S(1)}, bf16[256,256]{1,0:T(8,128)(2,1)S(1)}, u32[]{:S(2)}, u32[]{:S(2)}) collective-permute-start(bf16[256,256]{1,0:T(8,128)(2,1)S(1)} %shard_map.78), channel_id=1, source_target_pairs={{0,32},{1,97},{2,34},{3,99},{4,36},{5,101},{6,38},{7,103},{8,40},{... | collective-permute-start | bytes 393224 | tf_op jit(solution)/shard_map/ppermute | solution.py:26
  29.3 1.6 %copy-start.4 = (bf16[256,4096]{1,0:T(8,128)(2,1)S(1)}, bf16[256,4096]{1,0:T(8,128)(2,1)}, u32[]{:S(2)}) copy-start(bf16[256,4096]{1,0:T(8,128)(2,1)} %copy-done.3) | copy-start | bytes 6291460
  33.1 2.7 %collective-permute-start.12 = (bf16[256,256]{1,0:T(8,128)(2,1)S(1)}, bf16[256,256]{1,0:T(8,128)(2,1)S(1)}, u32[]{:S(2)}, u32[]{:S(2)}) collective-permute-start(bf16[256,256]{1,0:T(8,128)(2,1)S(1)} %collective-permute-done.10.refs_0_.refs_9_), channel_id=1, source_target_pairs={{0,1},{1,0},{2,3},{3,2},{4,5},{5,4},{6,7},{7,6},{8,9},{9,8},{10,11... | collective-permute-start | bytes 393224 | tf_op jit(solution)/shard_map/ppermute | solution.py:26
  34.5 1.3 %collective-permute-start.13 = (bf16[128,256]{1,0:T(8,128)(2,1)S(1)}, bf16[128,256]{1,0:T(8,128)(2,1)S(1)}, u32[]{:S(2)}, u32[]{:S(2)}) collective-permute-start(bf16[128,256]{1,0:T(8,128)(2,1)S(1)} %collective-permute-done.11.refs_3_.refs_12_), channel_id=1, source_target_pairs={{0,1},{1,0},{2,3},{3,2},{4,5},{5,4},{6,7},{7,6},{8,9},{9,8},{10,11... | collective-permute-start | bytes 196616 | tf_op jit(solution)/shard_map/ppermute | solution.py:26
  36.3 9.7 %collective-permute-start.14 = (bf16[64,512]{1,0:T(8,128)(2,1)S(1)}, bf16[64,512]{1,0:T(8,128)(2,1)S(1)}, u32[]{:S(2)}, u32[]{:S(2)}) collective-permute-start(bf16[64,512]{1,0:T(8,128)(2,1)S(1)} %get-tuple-element.68), channel_id=1, source_target_pairs={{0,16},{32,48},{64,80},{96,112},{16,0},{48,32},{80,64},{112,96},{1... | collective-permute-start | bytes 196616 | tf_op jit(solution)/shard_map/ppermute | solution.py:420
  37.6 8.5 %collective-permute-start.15 = (bf16[64,512]{1,0:T(8,128)(2,1)S(1)}, bf16[64,512]{1,0:T(8,128)(2,1)S(1)}, u32[]{:S(2)}, u32[]{:S(2)}) collective-permute-start(bf16[64,512]{1,0:T(8,128)(2,1)S(1)} %get-tuple-element.69), channel_id=1, source_target_pairs={{16,32},{48,64},{80,96},{112,0},{32,16},{64,48},{96,80},{0,112},{1... | collective-permute-start | bytes 196616 | tf_op jit(solution)/shard_map/ppermute | solution.py:420
  40.7 4.3 %collective-permute-start.16 = (bf16[64,128]{1,0:T(8,128)(2,1)S(1)}, bf16[64,128]{1,0:T(8,128)(2,1)S(1)}, u32[]{:S(2)}, u32[]{:S(2)}) collective-permute-start(bf16[64,128]{1,0:T(8,128)(2,1)S(1)} %get-tuple-element.70), channel_id=1, source_target_pairs={{0,1},{2,3},{4,5},{6,7},{8,9},{10,11},{12,13},{14,15},{1,0},{3,2},... | collective-permute-start | bytes 49160 | tf_op jit(solution)/shard_map/ppermute | solution.py:420
  40.7 5.3 %collective-permute-start.17 = (bf16[64,128]{1,0:T(8,128)(2,1)S(1)}, bf16[64,128]{1,0:T(8,128)(2,1)S(1)}, u32[]{:S(2)}, u32[]{:S(2)}) collective-permute-start(bf16[64,128]{1,0:T(8,128)(2,1)S(1)} %get-tuple-element.71), channel_id=1, source_target_pairs={{1,2},{3,4},{5,6},{7,8},{9,10},{11,12},{13,14},{15,0},{2,1},{4,3},... | collective-permute-start | bytes 49160 | tf_op jit(solution)/shard_map/ppermute | solution.py:420
  43.0 3.0 %copy-start.1 = (bf16[4,64,4]{1,2,0:T(4,128)(2,1)S(1)}, bf16[4,64,4]{1,2,0:T(4,128)(2,1)}, u32[]{:S(2)}) copy-start(bf16[4,64,4]{1,2,0:T(4,128)(2,1)} %param.10) | copy-start | bytes 6148
  43.0 3.0 %copy-start.2 = (s32[4]{0:T(128)S(1)}, s32[4]{0:T(128)}, u32[]{:S(2)}) copy-start(s32[4]{0:T(128)} %port_ref.3) | copy-start | bytes 52
  51.8 9.3 %collective-permute-start.18 = (bf16[64,512]{1,0:T(8,128)(2,1)S(1)}, bf16[64,512]{1,0:T(8,128)(2,1)S(1)}, u32[]{:S(2)}, u32[]{:S(2)}) collective-permute-start(bf16[64,512]{1,0:T(8,128)(2,1)S(1)} %get-tuple-element.73), channel_id=1, source_target_pairs={{0,16},{32,48},{64,80},{96,112},{16,0},{48,32},{80,64},{112,96},{1... | collective-permute-start | bytes 196616 | tf_op jit(solution)/shard_map/ppermute | solution.py:420
  52.4 8.7 %collective-permute-start.19 = (bf16[64,512]{1,0:T(8,128)(2,1)S(1)}, bf16[64,512]{1,0:T(8,128)(2,1)S(1)}, u32[]{:S(2)}, u32[]{:S(2)}) collective-permute-start(bf16[64,512]{1,0:T(8,128)(2,1)S(1)} %get-tuple-element.74), channel_id=1, source_target_pairs={{16,32},{48,64},{80,96},{112,0},{32,16},{64,48},{96,80},{0,112},{1... | collective-permute-start | bytes 196616 | tf_op jit(solution)/shard_map/ppermute | solution.py:420
  55.8 1.8 %collective-permute-start.20 = (bf16[64,128]{1,0:T(8,128)(2,1)S(1)}, bf16[64,128]{1,0:T(8,128)(2,1)S(1)}, u32[]{:S(2)}, u32[]{:S(2)}) collective-permute-start(bf16[64,128]{1,0:T(8,128)(2,1)S(1)} %get-tuple-element.75), channel_id=1, source_target_pairs={{0,1},{2,3},{4,5},{6,7},{8,9},{10,11},{12,13},{14,15},{1,0},{3,2},... | collective-permute-start | bytes 49160 | tf_op jit(solution)/shard_map/ppermute | solution.py:420
  55.8 5.3 %collective-permute-start.21 = (bf16[64,128]{1,0:T(8,128)(2,1)S(1)}, bf16[64,128]{1,0:T(8,128)(2,1)S(1)}, u32[]{:S(2)}, u32[]{:S(2)}) collective-permute-start(bf16[64,128]{1,0:T(8,128)(2,1)S(1)} %get-tuple-element.76), channel_id=1, source_target_pairs={{1,2},{3,4},{5,6},{7,8},{9,10},{11,12},{13,14},{15,0},{2,1},{4,3},... | collective-permute-start | bytes 49160 | tf_op jit(solution)/shard_map/ppermute | solution.py:420

commit v13 on v12

--- a/solution.py
+++ b/solution.py
@@ -113,10 +113,20 @@
         flops=2**30,
     )
     other, sides = lax.optimization_barrier((other, sides))
-    return (partial + other).astype(BF), x, sides
-
-
-MAP_STEPS = ((0, 0), (2, 3), (6, 7), (3, 2), (7, 6), (4, 5), (5, 4), (1, 1))
+    shapes = [jax.ShapeDtypeStruct((lines, order), BF) for lines in (order, order // 2)]
+    return *whole_call(own_kernel, shapes, partial, other), x, sides
+
+
+MAP_STEPS = ((0, 0), (2, 3), (6, 7), (3, 2), (7, 6), (1, 1), (4, 5), (5, 4))
+HALVES = 5
+
+
+def own_kernel(one_ref, two_ref, out_ref, half_ref):
+    core = lax.rem(lax.axis_index("col"), 2)
+    half = half_ref.shape[0]
+    total = (one_ref[...] + two_ref[...]).astype(BF)
+    out_ref[...] = total
+    half_ref[...] = jnp.where(core == 0, total[0:half], total[half:])
 
 
 def relay_kernel(first_ref, second_ref, out_ref):
@@ -186,11 +196,14 @@
     return total
 
 
-def with_steps(map_refs, first, last):
-    refs = [(ref,) for ref in map_refs]
-    if last == len(MAP_STEPS):
-        refs[-2:] = [refs[-2] + refs[-1]]
-    return list(zip(MAP_STEPS[first:last], refs, strict=True))
+def with_steps(map_refs, first):
+    map_refs, maps = list(map_refs), []
+    while map_refs:
+        number = first + len(maps)
+        count = 2 if number == HALVES else 1
+        maps.append((MAP_STEPS[number], map_refs[:count]))
+        del map_refs[:count]
+    return maps
 
 
 def shifted(total, next_ref, rows):
@@ -264,11 +277,11 @@
     sides_ref[...], kinds_ref[...] = side_columns(x_ref, types_ref[...].astype(F32), ports)
 
 
-def early_kernel(ports, first, last, x_ref, types_ref, sides_ref, kinds_ref, *refs):
-    maps = with_steps(refs[: last - first], first, last)
+def early_kernel(ports, first, count, x_ref, types_ref, sides_ref, kinds_ref, *refs):
+    maps = with_steps(refs[:count], first)
     types = types_ref[...].astype(F32)
     tile = types.shape[1]
-    so_far, outs = refs[last - first : -4], refs[-4:]
+    so_far, outs = refs[count:-4], refs[-4:]
     done_ref, *so_far = so_far if first else [None] * 4
     values = rims(x_ref, types, ports, sides_ref[...], kinds_ref[0:1, :], maps, so_far)
     for ref, value in zip(outs[1:], values):
@@ -281,7 +294,7 @@
 
 
 def rim_kernel(ports, first, x_ref, types_ref, sides_ref, kinds_ref, *refs):
-    maps = with_steps(refs[:-7], first, len(MAP_STEPS))
+    maps = with_steps(refs[:-7], first)
     types = types_ref[...].astype(F32)
     quarter = x_ref.shape[0] // 4
     values = rims(x_ref, types, ports, sides_ref[...], kinds_ref[0:1, :], maps, refs[-7:-4])
@@ -289,7 +302,7 @@
 
 
 def first_kernel(rows, ports, first, x_ref, types_ref, done_ref, *refs):
-    maps = with_steps(refs[:-1], first, len(MAP_STEPS))
+    maps = with_steps(refs[:-1], first)
     types = types_ref[...].astype(F32).astype(BF)
     tile = types.shape[1]
     for port in range(ports):
@@ -306,7 +319,7 @@
     tile = types.shape[1]
     order = x_ref.shape[0]
     quarter = order // 4
-    maps = with_steps(map_refs, 0, len(MAP_STEPS))
+    maps = with_steps(map_refs, 0)
     north_in, south_in = halos_inside("row", *halo_refs[:2])
     west_in, east_in = halos_inside("col", *halo_refs[2:])
     lane = lax.broadcasted_iota(jnp.int32, (quarter, LANES), 1)
@@ -426,9 +439,7 @@
     quarter = samples
     tile = rows * width
     types = cell_type.reshape(1, tile)
-    own_map, x, sides = own_type_map(mode_shapes, mode_values, mode_weights, traces, types)
-    core = lax.rem(lax.axis_index("col"), 2)
-    half = lax.dynamic_slice_in_dim(own_map, core * (order // 2), order // 2)
+    own_map, half, x, sides = own_type_map(mode_shapes, mode_values, mode_weights, traces, types)
     first = swap(own_map, (2, 0), (3, 8))
     second = swap(own_map, (6, 0), (7, 8))
     half = swap(half, (1, 8))
@@ -442,23 +453,24 @@
     part_shapes = [next_shape] + rim_shapes[:2] + [jax.ShapeDtypeStruct((2 * quarter, LANES), BF)]
 
     def early(first, maps, parts=()):
-        last = first + len(maps)
-        kernel = functools.partial(early_kernel, ports, first, last)
+        kernel = functools.partial(early_kernel, ports, first, len(maps))
         flops = work * len(maps) // 7
         return whole_call(kernel, part_shapes, x, types, *sides, *maps, *parts, flops=flops)
 
     parts = list(early(0, [own_map, first]))
-    parts[1], first, second = lax.optimization_barrier((parts[1], first, second))
+    parts[1], first, second, half = lax.optimization_barrier((parts[1], first, second, half))
     map_shape = jax.ShapeDtypeStruct(own_map.shape, BF)
-    third = swap(whole_call(relay_kernel, [map_shape], first, second)[0], (2, 0), (6, 0))
-    maps = [own_map, first, second, swap_cores(first), swap_cores(second)]
-    parts = list(early(2, maps[2:], parts))
-    parts[1], third, half = lax.optimization_barrier((parts[1], third, half))
+    (relay,) = whole_call(relay_kernel, [map_shape], first, second)
+    relay, first, second, half = lax.optimization_barrier((relay, first, second, half))
+    third = swap(relay, (2, 0), (6, 0))
+    maps = [second, swap_cores(first), swap_cores(second), swap_cores(half), half]
+    parts = list(early(2, maps, parts))
+    parts[1], third = lax.optimization_barrier((parts[1], third))
     done, *parts = parts
-    late = [third, swap_cores(third), swap_cores(half), half]
-    maps += late
+    late = [third, swap_cores(third)]
+    maps = [own_map, first] + maps + late
     sent = whole_call(
-        functools.partial(rim_kernel, ports, 5),
+        functools.partial(rim_kernel, ports, 6),
         rim_shapes,
         x,
         types,
@@ -469,7 +481,7 @@
     )
     halos = exchange(sent)
     (x,) = whole_call(
-        functools.partial(first_kernel, rows, ports, 5),
+        functools.partial(first_kernel, rows, ports, 6),
         [next_shape],
         x,
         types,

time: 64.8 us -> 64 us (0.988)
  waiting for transfers between devices: 10.8 us -> 14.3 us
  local copies, waits for them, and re-layouts: 3.58 us -> 0.67 us
  starting transfers between devices: 30.2 us -> 28.8 us
    ppermute x8, waiting for transfers between devices: 4.52 us -> 8.97 us  [exchange(): lax.ppermute(rim, axis, pairs(axis, first))]
    unnamed x10 -> x6, local copies, waits for them, and re-layouts: 2.91 us -> 0.01 us
    ppermute x8, starting transfers between devices: 12.5 us -> 9.86 us  [exchange(): lax.ppermute(rim, axis, pairs(axis, first))]
    ppermute x14, starting transfers between devices: 17.7 us -> 18.9 us  [swap(): return lax.ppermute(value, ('row', 'col'), pairs)]
    ppermute x14, waiting for transfers between devices: 6.27 us -> 5.3 us  [swap(): return lax.ppermute(value, ('row', 'col'), pairs)]
    pallas_call x7 -> x8, Pallas kernels: 7.8 us -> 7.83 us  [whole_call(): pl.pallas_call(kernel, in_specs=[WHOLE] * len(operands), out_specs=[WHOLE...]
  transfers between devices with their start and end apart: 22 -> 22, of which waited for: 7 -> 9; matrix products, arithmetic and copies ran while one was open for 0% -> 0% of each run, Pallas kernels for 14% -> 14%
where the time goes in v13:
time: 64 us; the launch traced here: 63.7 us
  starting transfers between devices  28.8 us (45%)
  Pallas kernels  18.9 us (30%)
  waiting for transfers between devices  14.3 us (22%)
  other arithmetic  0.81 us (1%)
  local copies, waits for them, and re-layouts  0.67 us (1%)
    ppermute x14, starting transfers between devices, swap(): return lax.ppermute(value, ('row', 'col'), pairs)  18.9 us
    ppermute x8, starting transfers between devices, exchange(): lax.ppermute(rim, axis, pairs(axis, first))  9.86 us
    ppermute x8, waiting for transfers between devices, exchange(): lax.ppermute(rim, axis, pairs(axis, first))  8.97 us
    pallas_call x8, Pallas kernels, whole_call(): pl.pallas_call(kernel, in_specs=[WHOLE] * len(operands), out_specs=[WHOLE...  7.83 us
    pallas_call x1, Pallas kernels, body(): pl.pallas_call(functools.partial(second_kernel, rows, width), in_specs=[p...  5.77 us
    ppermute x14, waiting for transfers between devices, swap(): return lax.ppermute(value, ('row', 'col'), pairs)  5.3 us
    pallas_call x1, Pallas kernels, body(): pl.pallas_call(functools.partial(last_kernel, rows, width), in_specs=[por...  3.33 us
    pallas_call x1, Pallas kernels, own_type_map(): pl.pallas_call(flat_kernel, in_specs=[pl.BlockSpec(memory_space=pltpu.HBM...  1.98 us
  transfers between devices with their start and end apart: 22, of which 9 were waited for; matrix products, arithmetic and copies ran while one was open for 0% of the time, Pallas kernels for 14%

profile of v13, /device:TPU:0, one launch (start us, length us, event | category | flops | bytes accessed | tf_op | source)
XLA Modules:
  0.0 63.7 jit_solution(11767296328908473421)
XLA Ops:
  0.0 0.7 %concatenate.10 = f32[32]{0:T(128)S(1)} pad(f32[16]{0:T(128)} %bitcast.20, f32[]{:T(128)} %constant.0.clone.1), padding=0_16 | pad | bytes 196 | tf_op jit(solution)/shard_map/concatenate | solution.py:82
  0.7 0.8 %maximum_multiply_fusion.refs_0_ = f32[32,256]{1,0:T(8,128)S(1)} fusion(f32[16,256]{1,0:T(8,128)} %bitcast.18, f32[16,256]{1,0:T(8,128)} %bitcast.19, f32[32]{0:T(128)S(1)} %concatenate.10), kind=kLoop, calls=%fused_computation.1 | loop fusion | flops 16384 | bytes 65664 | tf_op jit(solution)/shard_map/mul | solution.py:82
  1.5 0.0 collective-permute-start.1
  1.5 4.0 %collective-permute-start = (f32[32,256]{1,0:T(8,128)S(1)}, f32[32,256]{1,0:T(8,128)S(1)}, u32[]{:S(2)}, u32[]{:S(2)}) collective-permute-start(f32[32,256]{1,0:T(8,128)S(1)} %maximum_multiply_fusion.refs_0_), channel_id=1, source_target_pairs={{0,4},{1,5},{2,6},{3,7},{4,0},{5,1},{6,2},{7,3},{8,12},{9,13},{10,... | collective-permute-start | bytes 98312 | tf_op jit(solution)/shard_map/ppermute | solution.py:26
  5.5 0.0 collective-permute-done.1
  5.5 1.3 %collective-permute-start.4 = (f32[64,256]{1,0:T(8,128)S(1)}, f32[64,256]{1,0:T(8,128)S(1)}, u32[]{:S(2)}, u32[]{:S(2)}) collective-permute-start(f32[64,256]{1,0:T(8,128)S(1)} %pad_maximum_fusion), channel_id=1, source_target_pairs={{0,6},{1,13},{2,4},{3,15},{4,2},{5,9},{6,0},{7,11},{8,14},{9,5},{1... | collective-permute-start | bytes 196616 | tf_op jit(solution)/shard_map/ppermute | solution.py:26
  6.8 0.0 collective-permute-start.3
  6.8 1.5 %collective-permute-start.2 = (f32[64,256]{1,0:T(8,128)S(1)}, f32[64,256]{1,0:T(8,128)S(1)}, u32[]{:S(2)}, u32[]{:S(2)}) collective-permute-start(f32[64,256]{1,0:T(8,128)S(1)} %pad_maximum_fusion), channel_id=1, source_target_pairs={{0,8},{1,11},{2,10},{3,9},{4,12},{5,15},{6,14},{7,13},{8,0},{9,3},... | collective-permute-start | bytes 196616 | tf_op jit(solution)/shard_map/ppermute | solution.py:26
  8.3 0.0 copy-start
  8.3 2.0 %shard_map.73.x_ref = bf16[256,4096]{1,0:T(8,128)(2,1)S(1)} custom-call(bf16[256,4,8,128]{3,2,1,0:T(8,128)(2,1)} %bitcast.17), custom_call_target="tpu_custom_call" | custom-call | flops 1073741824 | tf_op jit(solution)/shard_map/pallas_call | solution.py:89
  10.3 1.4 %collective-permute-done.4.refs_4_ = f32[64,256]{1,0:T(8,128)S(1)} collective-permute-done((f32[64,256]{1,0:T(8,128)S(1)}, f32[64,256]{1,0:T(8,128)S(1)}, u32[]{:S(2)}, u32[]{:S(2)}) %collective-permute-start.4) | collective-permute-done | bytes 65568 | tf_op jit(solution)/shard_map/ppermute | solution.py:26
  11.7 0.0 collective-permute-done.3.refs_3_
  11.7 0.0 collective-permute-done.2.refs_2_
  11.7 0.0 collective-permute-done.refs_1_
  11.7 0.4 shard_map.74.one_ref
  12.2 2.1 %collective-permute-start.5 = (f32[256,256]{1,0:T(8,128)S(1)}, f32[256,256]{1,0:T(8,128)S(1)}, u32[]{:S(2)}, u32[]{:S(2)}) collective-permute-start(f32[256,256]{1,0:T(8,128)S(1)} %shard_map.74.one_ref), channel_id=1, source_target_pairs={{0,1},{1,0},{2,3},{3,2},{4,5},{5,4},{6,7},{7,6},{8,9},{9,8},{10,11... | collective-permute-start | bytes 786440 | tf_op jit(solution)/shard_map/ppermute | solution.py:26
  14.3 0.0 copy-done
  14.3 1.2 %shard_map.75 = (bf16[256,128]{1,0:T(8,128)(2,1)S(1)}, bf16[16,128]{1,0:T(8,128)(2,1)S(1)}) custom-call(bf16[256,4096]{1,0:T(8,128)(2,1)S(1)} %shard_map.73.x_ref, s32[1,1024]{1,0:T(1,128)S(1)} %bitcast.9), custom_call_target="tpu_custom_call" | custom-call | flops 1073741824 | tf_op jit(solution)/shard_map/pallas_call | solution.py:69
  15.5 0.0 collective-permute-done.5.two_ref
  15.5 1.7 %collective-permute-start.6 = (bf16[256,256]{1,0:T(8,128)(2,1)S(1)}, bf16[256,256]{1,0:T(8,128)(2,1)S(1)}, u32[]{:S(2)}, u32[]{:S(2)}) collective-permute-start(bf16[256,256]{1,0:T(8,128)(2,1)S(1)} %get-tuple-element.60.refs_0_.refs_4_), channel_id=1, source_target_pairs={{0,32},{1,57},{2,34},{3,59},{4,36},{5,61},{6,38},{7,63},{8,40},{9,... | collective-permute-start | bytes 393224 | tf_op jit(solution)/shard_map/ppermute | solution.py:26
  17.2 2.2 %collective-permute-start.7 = (bf16[256,256]{1,0:T(8,128)(2,1)S(1)}, bf16[256,256]{1,0:T(8,128)(2,1)S(1)}, u32[]{:S(2)}, u32[]{:S(2)}) collective-permute-start(bf16[256,256]{1,0:T(8,128)(2,1)S(1)} %get-tuple-element.60.refs_0_.refs_4_), channel_id=1, source_target_pairs={{0,96},{1,121},{2,98},{3,123},{4,100},{5,125},{6,102},{7,127},{8,1... | collective-permute-start | bytes 393224 | tf_op jit(solution)/shard_map/ppermute | solution.py:26
  19.4 2.7 %collective-permute-start.8 = (bf16[128,256]{1,0:T(8,128)(2,1)S(1)}, bf16[128,256]{1,0:T(8,128)(2,1)S(1)}, u32[]{:S(2)}, u32[]{:S(2)}) collective-permute-start(bf16[128,256]{1,0:T(8,128)(2,1)S(1)} %get-tuple-element.62), channel_id=1, source_target_pairs={{0,24},{1,25},{2,26},{3,27},{4,28},{5,29},{6,30},{7,31},{8,16},{9,... | collective-permute-start | bytes 196616 | tf_op jit(solution)/shard_map/ppermute | solution.py:26
  22.1 0.0 collective-permute-done.6.refs_1_.first_ref.refs_5_
  22.1 1.5 %shard_map.77 = (bf16[256,4096]{1,0:T(8,128)(2,1)S(1)}, bf16[64,512]{1,0:T(8,128)(2,1)S(1)}, bf16[64,512]{1,0:T(8,128)(2,1)S(1)}, bf16[128,128]{1,0:T(8,128)(2,1)S(1)}) custom-call(bf16[256,4096]{1,0:T(8,128)(2,1)S(1)} %shard_map.73.x_ref, s32[1,1024]{1,0:T(1,128)S(1)} %bitcast.10, bf16[256,128]{1,0:T(8,128)(2,1)S(1)} %get-tuple-element.57.sides_ref, ...), custom_call_target="tpu_custom_call" | custom-call | flops 1227133568 | tf_op jit(solution)/shard_map/pallas_call | solution.py:69
  23.6 1.2 %collective-permute-done.8.refs_4_.refs_10_ = bf16[128,256]{1,0:T(8,128)(2,1)S(1)} collective-permute-done((bf16[128,256]{1,0:T(8,128)(2,1)S(1)}, bf16[128,256]{1,0:T(8,128)(2,1)S(1)}, u32[]{:S(2)}, u32[]{:S(2)}) %collective-permute-start.8) | collective-permute-done | bytes 65568 | tf_op jit(solution)/shard_map/ppermute | solution.py:26
  24.8 0.0 collective-permute-done.7.second_ref.refs_0_.refs_6_
  24.9 2.0 %collective-permute-start.9 = (bf16[256,256]{1,0:T(8,128)(2,1)S(1)}, bf16[256,256]{1,0:T(8,128)(2,1)S(1)}, u32[]{:S(2)}, u32[]{:S(2)}) collective-permute-start(bf16[256,256]{1,0:T(8,128)(2,1)S(1)} %collective-permute-done.6.refs_1_.first_ref.refs_5_), channel_id=1, source_target_pairs={{0,1},{1,0},{2,3},{3,2},{4,5},{5,4},{6,7},{7,6},{8,9},{9,8},{10,11... | collective-permute-start | bytes 393224 | tf_op jit(solution)/shard_map/ppermute | solution.py:26
  26.9 0.1 collective-permute-start.10
  27.0 0.4 collective-permute-start.11
  27.4 0.7 %collective-permute-start.12 = (bf16[256,256]{1,0:T(8,128)(2,1)S(1)}, bf16[256,256]{1,0:T(8,128)(2,1)S(1)}, u32[]{:S(2)}, u32[]{:S(2)}) collective-permute-start(bf16[256,256]{1,0:T(8,128)(2,1)S(1)} %shard_map.78), channel_id=1, source_target_pairs={{0,32},{1,97},{2,34},{3,99},{4,36},{5,101},{6,38},{7,103},{8,40},{... | collective-permute-start | bytes 393224 | tf_op jit(solution)/shard_map/ppermute | solution.py:26
  28.1 0.3 collective-permute-done.11.refs_3_.refs_9_
  28.3 0.0 collective-permute-done.9.refs_1_.refs_7_
  28.3 0.0 collective-permute-done.10.refs_2_.refs_8_
  28.3 2.8 %shard_map.79 = (bf16[256,4096]{1,0:T(8,128)(2,1)S(1)}, bf16[64,512]{1,0:T(8,128)(2,1)S(1)}, bf16[64,512]{1,0:T(8,128)(2,1)S(1)}, bf16[128,128]{1,0:T(8,128)(2,1)S(1)}) custom-call(bf16[256,4096]{1,0:T(8,128)(2,1)S(1)} %shard_map.73.x_ref, s32[1,1024]{1,0:T(1,128)S(1)} %bitcast.11, bf16[256,128]{1,0:T(8,128)(2,1)S(1)} %get-tuple-element.57.sides_ref, ...), custom_call_target="tpu_custom_call" | custom-call | flops 3067833856 | tf_op jit(solution)/shard_map/pallas_call | solution.py:69
  31.2 1.2 %collective-permute-done.12.refs_0_.refs_11_ = bf16[256,256]{1,0:T(8,128)(2,1)S(1)} collective-permute-done((bf16[256,256]{1,0:T(8,128)(2,1)S(1)}, bf16[256,256]{1,0:T(8,128)(2,1)S(1)}, u32[]{:S(2)}, u32[]{:S(2)}) %collective-permute-start.12) | collective-permute-done | bytes 131104 | tf_op jit(solution)/shard_map/ppermute | solution.py:26
  32.4 0.2 collective-permute-start.13
  32.5 1.2 %collective-permute-done.13.refs_1_.refs_12_ = bf16[256,256]{1,0:T(8,128)(2,1)S(1)} collective-permute-done((bf16[256,256]{1,0:T(8,128)(2,1)S(1)}, bf16[256,256]{1,0:T(8,128)(2,1)S(1)}, u32[]{:S(2)}, u32[]{:S(2)}) %collective-permute-start.13) | collective-permute-done | bytes 131104 | tf_op jit(solution)/shard_map/ppermute | solution.py:26
  33.7 0.4 shard_map.81
  34.2 0.2 collective-permute-start.16
  34.4 0.4 collective-permute-start.17
  34.8 3.3 %collective-permute-start.14 = (bf16[64,512]{1,0:T(8,128)(2,1)S(1)}, bf16[64,512]{1,0:T(8,128)(2,1)S(1)}, u32[]{:S(2)}, u32[]{:S(2)}) collective-permute-start(bf16[64,512]{1,0:T(8,128)(2,1)S(1)} %get-tuple-element.80), channel_id=1, source_target_pairs={{0,16},{32,48},{64,80},{96,112},{16,0},{48,32},{80,64},{112,96},{1... | collective-permute-start | bytes 196616 | tf_op jit(solution)/shard_map/ppermute | solution.py:433
  38.0 1.6 %collective-permute-start.15 = (bf16[64,512]{1,0:T(8,128)(2,1)S(1)}, bf16[64,512]{1,0:T(8,128)(2,1)S(1)}, u32[]{:S(2)}, u32[]{:S(2)}) collective-permute-start(bf16[64,512]{1,0:T(8,128)(2,1)S(1)} %get-tuple-element.81), channel_id=1, source_target_pairs={{16,32},{48,64},{80,96},{112,0},{32,16},{64,48},{96,80},{0,112},{1... | collective-permute-start | bytes 196616 | tf_op jit(solution)/shard_map/ppermute | solution.py:433
  39.7 0.0 copy-start.1
  39.7 0.0 copy-start.2
  39.7 1.4 %shard_map.80.x_ref = bf16[256,4096]{1,0:T(8,128)(2,1)S(1)} custom-call(bf16[256,4096]{1,0:T(8,128)(2,1)S(1)} %shard_map.73.x_ref, s32[1,1024]{1,0:T(1,128)S(1)} %bitcast.13, bf16[256,4096]{1,0:T(8,128)(2,1)S(1)} %get-tuple-element.73.done_ref, bf16[256,256]{1,0:T(8,128)(2,1)S(1)} %collective-permute-done.12.refs_0_.refs_11_, ...), custom_call_target="tpu_custom_call" | custom-call | flops 2147483648 | tf_op jit(solution)/shard_map/pallas_call | solution.py:69
  41.1 0.0 collective-permute-done.16.refs_2_
  41.1 0.0 collective-permute-done.17.refs_3_
  41.1 0.2 collective-permute-done.14.refs_0_
  41.3 4.6 %collective-permute-done.15.refs_1_ = bf16[64,512]{1,0:T(8,128)(2,1)S(1)} collective-permute-done((bf16[64,512]{1,0:T(8,128)(2,1)S(1)}, bf16[64,512]{1,0:T(8,128)(2,1)S(1)}, u32[]{:S(2)}, u32[]{:S(2)}) %collective-permute-start.15) | collective-permute-done | bytes 65568 | tf_op jit(solution)/shard_map/ppermute | solution.py:433
  45.9 0.0 copy-done.1
  45.9 0.0 copy-done.2
  45.9 5.8 %shard_map.82 = (bf16[256,4096]{1,0:T(8,128)(2,1)S(1)}, bf16[64,512]{1,0:T(8,128)(2,1)S(1)}, bf16[64,512]{1,0:T(8,128)(2,1)S(1)}, bf16[64,128]{1,0:T(8,128)(2,1)S(1)}, bf16[64,128]{1,0:T(8,128)(2,1)S(1)}) custom-call(s32[4]{0:T(128)S(1)} %copy-done.2, bf16[256,4096]{1,0:T(8,128)(2,1)S(1)} %shard_map.80.x_ref, s32[1,1024]{1,0:T(1,128)S(1)} %bitcast.14, ...), custom_call_target="tpu_custom_call" | custom-call | flops 4294967296 | tf_op jit(solution)/shard_map/pallas_call | solution.py:493
  51.7 0.1 collective-permute-start.18
  51.8 3.1 %collective-permute-start.19 = (bf16[64,512]{1,0:T(8,128)(2,1)S(1)}, bf16[64,512]{1,0:T(8,128)(2,1)S(1)}, u32[]{:S(2)}, u32[]{:S(2)}) collective-permute-start(bf16[64,512]{1,0:T(8,128)(2,1)S(1)} %get-tuple-element.86), channel_id=1, source_target_pairs={{16,32},{48,64},{80,96},{112,0},{32,16},{64,48},{96,80},{0,112},{1... | collective-permute-start | bytes 196616 | tf_op jit(solution)/shard_map/ppermute | solution.py:433
  54.9 0.0 collective-permute-start.20
  54.9 1.1 %collective-permute-start.21 = (bf16[64,128]{1,0:T(8,128)(2,1)S(1)}, bf16[64,128]{1,0:T(8,128)(2,1)S(1)}, u32[]{:S(2)}, u32[]{:S(2)}) collective-permute-start(bf16[64,128]{1,0:T(8,128)(2,1)S(1)} %get-tuple-element.88), channel_id=1, source_target_pairs={{1,2},{3,4},{5,6},{7,8},{9,10},{11,12},{13,14},{15,0},{2,1},{4,3},... | collective-permute-start | bytes 49160 | tf_op jit(solution)/shard_map/ppermute | solution.py:433
  56.0 0.1 collective-permute-done.20.refs_2_
  56.1 4.1 %collective-permute-done.21.refs_3_ = bf16[64,128]{1,0:T(8,128)(2,1)S(1)} collective-permute-done((bf16[64,128]{1,0:T(8,128)(2,1)S(1)}, bf16[64,128]{1,0:T(8,128)(2,1)S(1)}, u32[]{:S(2)}, u32[]{:S(2)}) %collective-permute-start.21) | collective-permute-done | bytes 16416 | tf_op jit(solution)/shard_map/ppermute | solution.py:433
  60.2 0.0 collective-permute-done.18.refs_0_
  60.2 0.0 collective-permute-done.19.refs_1_
  60.2 3.3 %shard_map.83 = bf16[256,4,8,128]{3,2,1,0:T(8,128)(2,1)} custom-call(s32[4]{0:T(128)S(1)} %copy-done.2, bf16[256,4096]{1,0:T(8,128)(2,1)S(1)} %get-tuple-element.84.x_ref, bf16[4,4,64]{2,1,0:T(4,128)(2,1)S(1)} %bitcast.16, bf16[64,512]{1,0:T(8,128)(2,1)S(1)} %collective-permute-done.18.refs_0_, bf16[64,512]{1,0:T(8,128)(2,1)S(1)} %collective-permute-done.19.refs_1_, ...), custom_call_target="tpu_custom_call" | custom-call | tf_op jit(solution)/shard_map/pallas_call | solution.py:502
  (3 shorter events, 0.1 us)
Async XLA Ops:
  1.5 4.0 %collective-permute-start.1 = (f32[32,256]{1,0:T(8,128)S(1)}, f32[32,256]{1,0:T(8,128)S(1)}, u32[]{:S(2)}, u32[]{:S(2)}) collective-permute-start(f32[32,256]{1,0:T(8,128)S(1)} %maximum_multiply_fusion.refs_0_), channel_id=1, source_target_pairs={{0,1},{1,0},{2,3},{3,2},{4,5},{5,4},{6,7},{7,6},{8,9},{9,8},{10,11... | collective-permute-start | bytes 98312 | tf_op jit(solution)/shard_map/ppermute | solution.py:26
  1.5 10.3 %collective-permute-start = (f32[32,256]{1,0:T(8,128)S(1)}, f32[32,256]{1,0:T(8,128)S(1)}, u32[]{:S(2)}, u32[]{:S(2)}) collective-permute-start(f32[32,256]{1,0:T(8,128)S(1)} %maximum_multiply_fusion.refs_0_), channel_id=1, source_target_pairs={{0,4},{1,5},{2,6},{3,7},{4,0},{5,1},{6,2},{7,3},{8,12},{9,13},{10,... | collective-permute-start | bytes 98312 | tf_op jit(solution)/shard_map/ppermute | solution.py:26
  5.5 6.3 %collective-permute-start.4 = (f32[64,256]{1,0:T(8,128)S(1)}, f32[64,256]{1,0:T(8,128)S(1)}, u32[]{:S(2)}, u32[]{:S(2)}) collective-permute-start(f32[64,256]{1,0:T(8,128)S(1)} %pad_maximum_fusion), channel_id=1, source_target_pairs={{0,6},{1,13},{2,4},{3,15},{4,2},{5,9},{6,0},{7,11},{8,14},{9,5},{1... | collective-permute-start | bytes 196616 | tf_op jit(solution)/shard_map/ppermute | solution.py:26
  6.8 4.9 %collective-permute-start.3 = (f32[64,256]{1,0:T(8,128)S(1)}, f32[64,256]{1,0:T(8,128)S(1)}, u32[]{:S(2)}, u32[]{:S(2)}) collective-permute-start(f32[64,256]{1,0:T(8,128)S(1)} %pad_maximum_fusion), channel_id=1, source_target_pairs={{0,2},{1,15},{2,0},{3,13},{4,6},{5,11},{6,4},{7,9},{8,10},{9,7},{1... | collective-permute-start | bytes 196616 | tf_op jit(solution)/shard_map/ppermute | solution.py:26
  6.8 4.9 %collective-permute-start.2 = (f32[64,256]{1,0:T(8,128)S(1)}, f32[64,256]{1,0:T(8,128)S(1)}, u32[]{:S(2)}, u32[]{:S(2)}) collective-permute-start(f32[64,256]{1,0:T(8,128)S(1)} %pad_maximum_fusion), channel_id=1, source_target_pairs={{0,8},{1,11},{2,10},{3,9},{4,12},{5,15},{6,14},{7,13},{8,0},{9,3},... | collective-permute-start | bytes 196616 | tf_op jit(solution)/shard_map/ppermute | solution.py:26
  8.3 6.0 %copy-start = (s32[8,128]{1,0:T(8,128)S(1)}, s32[8,128]{1,0:T(8,128)}, u32[]{:S(2)}) copy-start(s32[8,128]{1,0:T(8,128)} %param.8) | copy-start | bytes 12292
  12.2 3.3 %collective-permute-start.5 = (f32[256,256]{1,0:T(8,128)S(1)}, f32[256,256]{1,0:T(8,128)S(1)}, u32[]{:S(2)}, u32[]{:S(2)}) collective-permute-start(f32[256,256]{1,0:T(8,128)S(1)} %shard_map.74.one_ref), channel_id=1, source_target_pairs={{0,1},{1,0},{2,3},{3,2},{4,5},{5,4},{6,7},{7,6},{8,9},{9,8},{10,11... | collective-permute-start | bytes 786440 | tf_op jit(solution)/shard_map/ppermute | solution.py:26
  15.5 6.6 %collective-permute-start.6 = (bf16[256,256]{1,0:T(8,128)(2,1)S(1)}, bf16[256,256]{1,0:T(8,128)(2,1)S(1)}, u32[]{:S(2)}, u32[]{:S(2)}) collective-permute-start(bf16[256,256]{1,0:T(8,128)(2,1)S(1)} %get-tuple-element.60.refs_0_.refs_4_), channel_id=1, source_target_pairs={{0,32},{1,57},{2,34},{3,59},{4,36},{5,61},{6,38},{7,63},{8,40},{9,... | collective-permute-start | bytes 393224 | tf_op jit(solution)/shard_map/ppermute | solution.py:26
  17.2 7.7 %collective-permute-start.7 = (bf16[256,256]{1,0:T(8,128)(2,1)S(1)}, bf16[256,256]{1,0:T(8,128)(2,1)S(1)}, u32[]{:S(2)}, u32[]{:S(2)}) collective-permute-start(bf16[256,256]{1,0:T(8,128)(2,1)S(1)} %get-tuple-element.60.refs_0_.refs_4_), channel_id=1, source_target_pairs={{0,96},{1,121},{2,98},{3,123},{4,100},{5,125},{6,102},{7,127},{8,1... | collective-permute-start | bytes 393224 | tf_op jit(solution)/shard_map/ppermute | solution.py:26
  19.4 5.5 %collective-permute-start.8 = (bf16[128,256]{1,0:T(8,128)(2,1)S(1)}, bf16[128,256]{1,0:T(8,128)(2,1)S(1)}, u32[]{:S(2)}, u32[]{:S(2)}) collective-permute-start(bf16[128,256]{1,0:T(8,128)(2,1)S(1)} %get-tuple-element.62), channel_id=1, source_target_pairs={{0,24},{1,25},{2,26},{3,27},{4,28},{5,29},{6,30},{7,31},{8,16},{9,... | collective-permute-start | bytes 196616 | tf_op jit(solution)/shard_map/ppermute | solution.py:26
  24.9 3.5 %collective-permute-start.9 = (bf16[256,256]{1,0:T(8,128)(2,1)S(1)}, bf16[256,256]{1,0:T(8,128)(2,1)S(1)}, u32[]{:S(2)}, u32[]{:S(2)}) collective-permute-start(bf16[256,256]{1,0:T(8,128)(2,1)S(1)} %collective-permute-done.6.refs_1_.first_ref.refs_5_), channel_id=1, source_target_pairs={{0,1},{1,0},{2,3},{3,2},{4,5},{5,4},{6,7},{7,6},{8,9},{9,8},{10,11... | collective-permute-start | bytes 393224 | tf_op jit(solution)/shard_map/ppermute | solution.py:26
  26.9 1.4 %collective-permute-start.10 = (bf16[256,256]{1,0:T(8,128)(2,1)S(1)}, bf16[256,256]{1,0:T(8,128)(2,1)S(1)}, u32[]{:S(2)}, u32[]{:S(2)}) collective-permute-start(bf16[256,256]{1,0:T(8,128)(2,1)S(1)} %collective-permute-done.7.second_ref.refs_0_.refs_6_), channel_id=1, source_target_pairs={{0,1},{1,0},{2,3},{3,2},{4,5},{5,4},{6,7},{7,6},{8,9},{9,8},{10,11... | collective-permute-start | bytes 393224 | tf_op jit(solution)/shard_map/ppermute | solution.py:26
  27.0 1.3 %collective-permute-start.11 = (bf16[128,256]{1,0:T(8,128)(2,1)S(1)}, bf16[128,256]{1,0:T(8,128)(2,1)S(1)}, u32[]{:S(2)}, u32[]{:S(2)}) collective-permute-start(bf16[128,256]{1,0:T(8,128)(2,1)S(1)} %collective-permute-done.8.refs_4_.refs_10_), channel_id=1, source_target_pairs={{0,1},{1,0},{2,3},{3,2},{4,5},{5,4},{6,7},{7,6},{8,9},{9,8},{10,11... | collective-permute-start | bytes 196616 | tf_op jit(solution)/shard_map/ppermute | solution.py:26
  27.4 5.0 %collective-permute-start.12 = (bf16[256,256]{1,0:T(8,128)(2,1)S(1)}, bf16[256,256]{1,0:T(8,128)(2,1)S(1)}, u32[]{:S(2)}, u32[]{:S(2)}) collective-permute-start(bf16[256,256]{1,0:T(8,128)(2,1)S(1)} %shard_map.78), channel_id=1, source_target_pairs={{0,32},{1,97},{2,34},{3,99},{4,36},{5,101},{6,38},{7,103},{8,40},{... | collective-permute-start | bytes 393224 | tf_op jit(solution)/shard_map/ppermute | solution.py:26
  32.4 1.3 %collective-permute-start.13 = (bf16[256,256]{1,0:T(8,128)(2,1)S(1)}, bf16[256,256]{1,0:T(8,128)(2,1)S(1)}, u32[]{:S(2)}, u32[]{:S(2)}) collective-permute-start(bf16[256,256]{1,0:T(8,128)(2,1)S(1)} %collective-permute-done.12.refs_0_.refs_11_), channel_id=1, source_target_pairs={{0,1},{1,0},{2,3},{3,2},{4,5},{5,4},{6,7},{7,6},{8,9},{9,8},{10,11... | collective-permute-start | bytes 393224 | tf_op jit(solution)/shard_map/ppermute | solution.py:26
  34.2 7.0 %collective-permute-start.16 = (bf16[64,128]{1,0:T(8,128)(2,1)S(1)}, bf16[64,128]{1,0:T(8,128)(2,1)S(1)}, u32[]{:S(2)}, u32[]{:S(2)}) collective-permute-start(bf16[64,128]{1,0:T(8,128)(2,1)S(1)} %get-tuple-element.82), channel_id=1, source_target_pairs={{0,1},{2,3},{4,5},{6,7},{8,9},{10,11},{12,13},{14,15},{1,0},{3,2},... | collective-permute-start | bytes 49160 | tf_op jit(solution)/shard_map/ppermute | solution.py:433
  34.4 6.7 %collective-permute-start.17 = (bf16[64,128]{1,0:T(8,128)(2,1)S(1)}, bf16[64,128]{1,0:T(8,128)(2,1)S(1)}, u32[]{:S(2)}, u32[]{:S(2)}) collective-permute-start(bf16[64,128]{1,0:T(8,128)(2,1)S(1)} %get-tuple-element.83), channel_id=1, source_target_pairs={{1,2},{3,4},{5,6},{7,8},{9,10},{11,12},{13,14},{15,0},{2,1},{4,3},... | collective-permute-start | bytes 49160 | tf_op jit(solution)/shard_map/ppermute | solution.py:433
  34.8 6.6 %collective-permute-start.14 = (bf16[64,512]{1,0:T(8,128)(2,1)S(1)}, bf16[64,512]{1,0:T(8,128)(2,1)S(1)}, u32[]{:S(2)}, u32[]{:S(2)}) collective-permute-start(bf16[64,512]{1,0:T(8,128)(2,1)S(1)} %get-tuple-element.80), channel_id=1, source_target_pairs={{0,16},{32,48},{64,80},{96,112},{16,0},{48,32},{80,64},{112,96},{1... | collective-permute-start | bytes 196616 | tf_op jit(solution)/shard_map/ppermute | solution.py:433
  38.0 7.9 %collective-permute-start.15 = (bf16[64,512]{1,0:T(8,128)(2,1)S(1)}, bf16[64,512]{1,0:T(8,128)(2,1)S(1)}, u32[]{:S(2)}, u32[]{:S(2)}) collective-permute-start(bf16[64,512]{1,0:T(8,128)(2,1)S(1)} %get-tuple-element.81), channel_id=1, source_target_pairs={{16,32},{48,64},{80,96},{112,0},{32,16},{64,48},{96,80},{0,112},{1... | collective-permute-start | bytes 196616 | tf_op jit(solution)/shard_map/ppermute | solution.py:433
  39.7 6.2 %copy-start.1 = (bf16[4,64,4]{1,2,0:T(4,128)(2,1)S(1)}, bf16[4,64,4]{1,2,0:T(4,128)(2,1)}, u32[]{:S(2)}) copy-start(bf16[4,64,4]{1,2,0:T(4,128)(2,1)} %param.10) | copy-start | bytes 6148
  39.7 6.2 %copy-start.2 = (s32[4]{0:T(128)S(1)}, s32[4]{0:T(128)}, u32[]{:S(2)}) copy-start(s32[4]{0:T(128)} %port_ref.3) | copy-start | bytes 52
  51.7 8.5 %collective-permute-start.18 = (bf16[64,512]{1,0:T(8,128)(2,1)S(1)}, bf16[64,512]{1,0:T(8,128)(2,1)S(1)}, u32[]{:S(2)}, u32[]{:S(2)}) collective-permute-start(bf16[64,512]{1,0:T(8,128)(2,1)S(1)} %get-tuple-element.85), channel_id=1, source_target_pairs={{0,16},{32,48},{64,80},{96,112},{16,0},{48,32},{80,64},{112,96},{1... | collective-permute-start | bytes 196616 | tf_op jit(solution)/shard_map/ppermute | solution.py:433
  51.8 8.4 %collective-permute-start.19 = (bf16[64,512]{1,0:T(8,128)(2,1)S(1)}, bf16[64,512]{1,0:T(8,128)(2,1)S(1)}, u32[]{:S(2)}, u32[]{:S(2)}) collective-permute-start(bf16[64,512]{1,0:T(8,128)(2,1)S(1)} %get-tuple-element.86), channel_id=1, source_target_pairs={{16,32},{48,64},{80,96},{112,0},{32,16},{64,48},{96,80},{0,112},{1... | collective-permute-start | bytes 196616 | tf_op jit(solution)/shard_map/ppermute | solution.py:433
  54.9 1.2 %collective-permute-start.20 = (bf16[64,128]{1,0:T(8,128)(2,1)S(1)}, bf16[64,128]{1,0:T(8,128)(2,1)S(1)}, u32[]{:S(2)}, u32[]{:S(2)}) collective-permute-start(bf16[64,128]{1,0:T(8,128)(2,1)S(1)} %get-tuple-element.87), channel_id=1, source_target_pairs={{0,1},{2,3},{4,5},{6,7},{8,9},{10,11},{12,13},{14,15},{1,0},{3,2},... | collective-permute-start | bytes 49160 | tf_op jit(solution)/shard_map/ppermute | solution.py:433
  54.9 5.3 %collective-permute-start.21 = (bf16[64,128]{1,0:T(8,128)(2,1)S(1)}, bf16[64,128]{1,0:T(8,128)(2,1)S(1)}, u32[]{:S(2)}, u32[]{:S(2)}) collective-permute-start(bf16[64,128]{1,0:T(8,128)(2,1)S(1)} %get-tuple-element.88), channel_id=1, source_target_pairs={{1,2},{3,4},{5,6},{7,8},{9,10},{11,12},{13,14},{15,0},{2,1},{4,3},... | collective-permute-start | bytes 49160 | tf_op jit(solution)/shard_map/ppermute | solution.py:433

commit v14 on v11

--- a/solution.py
+++ b/solution.py
@@ -143,15 +143,12 @@
     return jnp.broadcast_to(value[:, lane : lane + 1], (value.shape[0], LANES))
 
 
-def port_profile_column(profile_ref, port):
-    edges, _, samples = profile_ref.shape
+def port_profile_column(profile_ref, port, edge):
+    samples = profile_ref.shape[2]
     row = lax.broadcasted_iota(jnp.int32, (samples, samples), 0)
     col = lax.broadcasted_iota(jnp.int32, (samples, samples), 1)
-    columns = []
-    for edge in range(edges):
-        line = jnp.broadcast_to(profile_ref[edge].astype(F32)[port : port + 1], row.shape)
-        columns.append(jnp.sum(jnp.where(row == col, line, 0.0), axis=1, keepdims=True))
-    return jnp.concatenate(columns, axis=0)
+    line = jnp.broadcast_to(profile_ref[edge].astype(F32)[port : port + 1], row.shape)
+    return jnp.sum(jnp.where(row == col, line, 0.0), axis=1, keepdims=True)
 
 
 def port_place(port_ref, port, rows, width):
@@ -339,7 +336,8 @@
         row, col, inside = port_place(port_ref, port, rows, width)
         here = place_in_tile == jnp.where(inside, row * width + col, -1)
         current = block.astype(F32)
-        added = current + port_profile_column(profile_ref, port)
+        columns = [port_profile_column(profile_ref, port, edge) for edge in range(4)]
+        added = current + jnp.concatenate(columns, axis=0)
         block = jnp.where(here, added, current).astype(BF)
         total = products(block, types, maps, 0, order)
         north, south = shifted(total, next_ref.at[:, own], rows)
@@ -395,7 +393,7 @@
                 here = (lax.broadcasted_iota(jnp.int32, current.shape, 1) == row) & (
                     lax.broadcasted_iota(jnp.int32, current.shape, 2) == col
                 )
-                profile = port_profile_column(profile_ref, port)[lines]
+                profile = port_profile_column(profile_ref, port, edge)
                 profile = jnp.broadcast_to(profile, (quarter, LANES)).reshape(quarter, 1, LANES)
                 added = current + jnp.broadcast_to(profile, current.shape)
                 buffer[lines, port] = jnp.where(here, added, current).astype(BF)
@@ -410,8 +408,9 @@
 def exchange(rims):
     def pairs(axis, first):
         count = lax.axis_size(axis)
-        near = [(i, (i + 1) % count) for i in range(first, count, 2)]
-        return near + [(target, source) for source, target in near]
+        near = [(i, i + 1) for i in range(first, count - 1, 2)]
+        alone = [(0, 0), (count - 1, count - 1)] if first else []
+        return near + [(target, source) for source, target in near] + alone
 
     axes = (("row", 0), ("row", 1), ("col", 0), ("col", 1))
     return [lax.ppermute(rim, axis, pairs(axis, first)) for rim, (axis, first) in zip(rims, axes)]

time: 63.5 us -> 68.7 us (1.082)
  the two profiles are of different devices: /device:TPU:0 before, /device:TPU:18 now
where the time goes in v14:
time: 68.7 us; the launch traced here: 68.3 us
  starting transfers between devices  36.7 us (53%)
  Pallas kernels  18.4 us (27%)
  waiting for transfers between devices  11.2 us (16%)
  other arithmetic  0.85 us (1%)
    ppermute x8, starting transfers between devices, exchange(): lax.ppermute(rim, axis, pairs(axis, first))  22 us
    ppermute x14, starting transfers between devices, swap(): return lax.ppermute(value, ('row', 'col'), pairs)  14.7 us
    ppermute x14, waiting for transfers between devices, swap(): return lax.ppermute(value, ('row', 'col'), pairs)  7.87 us
    pallas_call x6, Pallas kernels, whole_call(): pl.pallas_call(kernel, in_specs=[WHOLE] * len(operands), out_specs=[WHOLE...  7.78 us
    pallas_call x1, Pallas kernels, body(): pl.pallas_call(functools.partial(second_kernel, rows, width), in_specs=[p...  5.83 us
    ppermute x8, waiting for transfers between devices, exchange(): lax.ppermute(rim, axis, pairs(axis, first))  3.38 us
    pallas_call x1, Pallas kernels, body(): pl.pallas_call(functools.partial(last_kernel, rows, width), in_specs=[por...  2.86 us
    pallas_call x1, Pallas kernels, own_type_map(): pl.pallas_call(flat_kernel, in_specs=[pl.BlockSpec(memory_space=pltpu.HBM...  1.98 us
  transfers between devices with their start and end apart: 22, of which 7 were waited for; matrix products, arithmetic and copies ran while one was open for 0% of the time, Pallas kernels for 13%

profile of v14, /device:TPU:18, one launch (start us, length us, event | category | flops | bytes accessed | tf_op | source)
XLA Modules:
  0.0 68.3 jit_solution(88140465728690869)
XLA Ops:
  0.0 0.7 concatenate.10
  0.7 0.8 %maximum_multiply_fusion.refs_0_ = f32[32,256]{1,0:T(8,128)S(1)} fusion(f32[16,256]{1,0:T(8,128)} %bitcast.18, f32[16,256]{1,0:T(8,128)} %bitcast.19, f32[32]{0:T(128)S(1)} %concatenate.10), kind=kLoop, calls=%fused_computation.2 | loop fusion | flops 16384 | bytes 65664 | tf_op jit(solution)/shard_map/mul | solution.py:82
  1.5 0.0 collective-permute-start.1
  1.5 3.9 %collective-permute-start = (f32[32,256]{1,0:T(8,128)S(1)}, f32[32,256]{1,0:T(8,128)S(1)}, u32[]{:S(2)}, u32[]{:S(2)}) collective-permute-start(f32[32,256]{1,0:T(8,128)S(1)} %maximum_multiply_fusion.refs_0_), channel_id=1, source_target_pairs={{0,4},{1,5},{2,6},{3,7},{4,0},{5,1},{6,2},{7,3},{8,12},{9,13},{10,... | collective-permute-start | bytes 98312 | tf_op jit(solution)/shard_map/ppermute | solution.py:26
  5.4 0.0 collective-permute-done.1
  5.4 0.6 collective-permute-start.2
  6.0 1.0 %collective-permute-start.3 = (f32[64,256]{1,0:T(8,128)S(1)}, f32[64,256]{1,0:T(8,128)S(1)}, u32[]{:S(2)}, u32[]{:S(2)}) collective-permute-start(f32[64,256]{1,0:T(8,128)S(1)} %pad_maximum_fusion), channel_id=1, source_target_pairs={{0,2},{1,15},{2,0},{3,13},{4,6},{5,11},{6,4},{7,9},{8,10},{9,7},{1... | collective-permute-start | bytes 196616 | tf_op jit(solution)/shard_map/ppermute | solution.py:26
  7.0 0.6 collective-permute-start.4
  7.7 0.0 copy-start
  7.7 2.0 %shard_map.73.x_ref = bf16[256,4096]{1,0:T(8,128)(2,1)S(1)} custom-call(bf16[256,4,8,128]{3,2,1,0:T(8,128)(2,1)} %bitcast.17), custom_call_target="tpu_custom_call" | custom-call | flops 1073741824 | tf_op jit(solution)/shard_map/pallas_call | solution.py:89
  9.7 0.8 %collective-permute-done.2.refs_2_ = f32[64,256]{1,0:T(8,128)S(1)} collective-permute-done((f32[64,256]{1,0:T(8,128)S(1)}, f32[64,256]{1,0:T(8,128)S(1)}, u32[]{:S(2)}, u32[]{:S(2)}) %collective-permute-start.2) | collective-permute-done | bytes 65568 | tf_op jit(solution)/shard_map/ppermute | solution.py:26
  10.4 0.2 collective-permute-done.3.refs_3_
  10.6 1.9 %collective-permute-done.4.refs_4_ = f32[64,256]{1,0:T(8,128)S(1)} collective-permute-done((f32[64,256]{1,0:T(8,128)S(1)}, f32[64,256]{1,0:T(8,128)S(1)}, u32[]{:S(2)}, u32[]{:S(2)}) %collective-permute-start.4) | collective-permute-done | bytes 65568 | tf_op jit(solution)/shard_map/ppermute | solution.py:26
  12.5 0.0 collective-permute-done.refs_1_
  12.5 0.4 shard_map.74
  12.9 0.7 %collective-permute-start.5 = (f32[256,256]{1,0:T(8,128)S(1)}, f32[256,256]{1,0:T(8,128)S(1)}, u32[]{:S(2)}, u32[]{:S(2)}) collective-permute-start(f32[256,256]{1,0:T(8,128)S(1)} %shard_map.74), channel_id=1, source_target_pairs={{0,1},{1,0},{2,3},{3,2},{4,5},{5,4},{6,7},{7,6},{8,9},{9,8},{10,11... | collective-permute-start | bytes 786440 | tf_op jit(solution)/shard_map/ppermute | solution.py:26
  13.6 0.0 copy-done
  13.6 1.2 %shard_map.75 = (bf16[256,128]{1,0:T(8,128)(2,1)S(1)}, bf16[16,128]{1,0:T(8,128)(2,1)S(1)}) custom-call(bf16[256,4096]{1,0:T(8,128)(2,1)S(1)} %shard_map.73.x_ref, s32[1,1024]{1,0:T(1,128)S(1)} %bitcast.9), custom_call_target="tpu_custom_call" | custom-call | flops 1073741824 | tf_op jit(solution)/shard_map/pallas_call | solution.py:69
  14.8 0.0 collective-permute-done.5
  14.9 2.6 %collective-permute-start.6 = (bf16[256,256]{1,0:T(8,128)(2,1)S(1)}, bf16[256,256]{1,0:T(8,128)(2,1)S(1)}, u32[]{:S(2)}, u32[]{:S(2)}) collective-permute-start(bf16[256,256]{1,0:T(8,128)(2,1)S(1)} %add_convert_fusion.refs_0_.refs_4_), channel_id=1, source_target_pairs={{0,24},{1,57},{2,26},{3,59},{4,28},{5,61},{6,30},{7,63},{8,16},{9,... | collective-permute-start | bytes 393224 | tf_op jit(solution)/shard_map/ppermute | solution.py:26
  17.5 1.3 %collective-permute-start.7 = (bf16[256,256]{1,0:T(8,128)(2,1)S(1)}, bf16[256,256]{1,0:T(8,128)(2,1)S(1)}, u32[]{:S(2)}, u32[]{:S(2)}) collective-permute-start(bf16[256,256]{1,0:T(8,128)(2,1)S(1)} %add_convert_fusion.refs_0_.refs_4_), channel_id=1, source_target_pairs={{0,32},{1,121},{2,34},{3,123},{4,36},{5,125},{6,38},{7,127},{8,40}... | collective-permute-start | bytes 393224 | tf_op jit(solution)/shard_map/ppermute | solution.py:26
  18.8 0.0 collective-permute-start.8
  18.8 2.8 %collective-permute-start.12 = (bf16[128,256]{1,0:T(8,128)(2,1)S(1)}, bf16[128,256]{1,0:T(8,128)(2,1)S(1)}, u32[]{:S(2)}, u32[]{:S(2)}) collective-permute-start(bf16[128,256]{1,0:T(8,128)(2,1)S(1)} %constant_dynamic-slice_fusion), channel_id=1, source_target_pairs={{0,64},{1,65},{2,66},{3,67},{4,68},{5,69},{6,70},{7,71},{8,72},{9,... | collective-permute-start | bytes 196616 | tf_op jit(solution)/shard_map/ppermute | solution.py:26
  21.6 0.2 collective-permute-done.6.refs_1_.refs_5_
  21.8 1.5 %shard_map.76 = (bf16[256,4096]{1,0:T(8,128)(2,1)S(1)}, bf16[64,512]{1,0:T(8,128)(2,1)S(1)}, bf16[64,512]{1,0:T(8,128)(2,1)S(1)}, bf16[128,128]{1,0:T(8,128)(2,1)S(1)}) custom-call(bf16[256,4096]{1,0:T(8,128)(2,1)S(1)} %shard_map.73.x_ref, s32[1,1024]{1,0:T(1,128)S(1)} %bitcast.10, bf16[256,128]{1,0:T(8,128)(2,1)S(1)} %get-tuple-element.51.sides_ref, ...), custom_call_target="tpu_custom_call" | custom-call | flops 1227133568 | tf_op jit(solution)/shard_map/pallas_call | solution.py:69
  23.3 0.0 collective-permute-done.7.refs_0_.refs_6_
  23.3 3.9 %collective-permute-done.8.refs_1_.refs_7_ = bf16[256,256]{1,0:T(8,128)(2,1)S(1)} collective-permute-done((bf16[256,256]{1,0:T(8,128)(2,1)S(1)}, bf16[256,256]{1,0:T(8,128)(2,1)S(1)}, u32[]{:S(2)}, u32[]{:S(2)}) %collective-permute-start.8) | collective-permute-done | bytes 131104 | tf_op jit(solution)/shard_map/ppermute | solution.py:26
  27.2 0.0 collective-permute-start.10
  27.2 0.5 collective-permute-start.11
  27.7 0.0 collective-permute-start.9
  27.7 1.5 %shard_map.77 = (bf16[256,4096]{1,0:T(8,128)(2,1)S(1)}, bf16[64,512]{1,0:T(8,128)(2,1)S(1)}, bf16[64,512]{1,0:T(8,128)(2,1)S(1)}, bf16[128,128]{1,0:T(8,128)(2,1)S(1)}) custom-call(bf16[256,4096]{1,0:T(8,128)(2,1)S(1)} %shard_map.73.x_ref, s32[1,1024]{1,0:T(1,128)S(1)} %bitcast.11, bf16[256,128]{1,0:T(8,128)(2,1)S(1)} %get-tuple-element.51.sides_ref, ...), custom_call_target="tpu_custom_call" | custom-call | flops 1227133568 | tf_op jit(solution)/shard_map/pallas_call | solution.py:69
  29.3 0.0 collective-permute-done.12.refs_4_.refs_12_
  29.3 0.6 collective-permute-start.13
  29.9 0.9 %collective-permute-done.13.refs_3_.refs_11_ = bf16[128,256]{1,0:T(8,128)(2,1)S(1)} collective-permute-done((bf16[128,256]{1,0:T(8,128)(2,1)S(1)}, bf16[128,256]{1,0:T(8,128)(2,1)S(1)}, u32[]{:S(2)}, u32[]{:S(2)}) %collective-permute-start.13) | collective-permute-done | bytes 65568 | tf_op jit(solution)/shard_map/ppermute | solution.py:26
  30.8 0.0 collective-permute-done.10.refs_1_.refs_9_
  30.8 0.0 collective-permute-done.11.refs_2_.refs_10_
  30.8 0.0 collective-permute-done.9.refs_0_.refs_8_
  30.8 0.6 shard_map.79
  31.4 2.2 %collective-permute-start.14 = (bf16[64,512]{1,0:T(8,128)(2,1)S(1)}, bf16[64,512]{1,0:T(8,128)(2,1)S(1)}, u32[]{:S(2)}, u32[]{:S(2)}) collective-permute-start(bf16[64,512]{1,0:T(8,128)(2,1)S(1)} %get-tuple-element.68), channel_id=1, source_target_pairs={{0,16},{32,48},{64,80},{96,112},{16,0},{48,32},{80,64},{112,96},{1... | collective-permute-start | bytes 196616 | tf_op jit(solution)/shard_map/ppermute | solution.py:416
  33.6 3.5 %collective-permute-start.15 = (bf16[64,512]{1,0:T(8,128)(2,1)S(1)}, bf16[64,512]{1,0:T(8,128)(2,1)S(1)}, u32[]{:S(2)}, u32[]{:S(2)}) collective-permute-start(bf16[64,512]{1,0:T(8,128)(2,1)S(1)} %get-tuple-element.69), channel_id=1, source_target_pairs={{16,32},{48,64},{80,96},{32,16},{64,48},{96,80},{0,0},{112,112},{1... | collective-permute-start | bytes 196616 | tf_op jit(solution)/shard_map/ppermute | solution.py:416
  37.1 0.1 collective-permute-start.16
  37.2 4.6 %collective-permute-start.17 = (bf16[64,128]{1,0:T(8,128)(2,1)S(1)}, bf16[64,128]{1,0:T(8,128)(2,1)S(1)}, u32[]{:S(2)}, u32[]{:S(2)}) collective-permute-start(bf16[64,128]{1,0:T(8,128)(2,1)S(1)} %get-tuple-element.71), channel_id=1, source_target_pairs={{1,2},{3,4},{5,6},{7,8},{9,10},{11,12},{13,14},{2,1},{4,3},{6,5},{... | collective-permute-start | bytes 49160 | tf_op jit(solution)/shard_map/ppermute | solution.py:416
  41.8 0.0 copy-start.1
  41.8 0.0 copy-start.2
  41.8 2.5 %shard_map.78.x_ref = bf16[256,4096]{1,0:T(8,128)(2,1)S(1)} custom-call(bf16[256,4096]{1,0:T(8,128)(2,1)S(1)} %shard_map.73.x_ref, s32[1,1024]{1,0:T(1,128)S(1)} %bitcast.13, bf16[256,4096]{1,0:T(8,128)(2,1)S(1)} %get-tuple-element.61.done_ref, bf16[256,256]{1,0:T(8,128)(2,1)S(1)} %collective-permute-done.9.refs_0_.refs_8_, ...), custom_call_target="tpu_custom_call" | custom-call | flops 2147483648 | tf_op jit(solution)/shard_map/pallas_call | solution.py:69
  44.4 0.0 collective-permute-done.16.refs_2_
  44.4 0.0 collective-permute-done.17.refs_3_
  44.4 0.0 collective-permute-done.14.refs_0_
  44.4 0.0 collective-permute-done.15.refs_1_
  44.4 0.0 copy-done.1
  44.4 0.0 copy-done.2
  44.4 5.8 %shard_map.80 = (bf16[256,4096]{1,0:T(8,128)(2,1)S(1)}, bf16[64,512]{1,0:T(8,128)(2,1)S(1)}, bf16[64,512]{1,0:T(8,128)(2,1)S(1)}, bf16[64,128]{1,0:T(8,128)(2,1)S(1)}, bf16[64,128]{1,0:T(8,128)(2,1)S(1)}) custom-call(s32[4]{0:T(128)S(1)} %copy-done.2, bf16[256,4096]{1,0:T(8,128)(2,1)S(1)} %shard_map.78.x_ref, s32[1,1024]{1,0:T(1,128)S(1)} %bitcast.14, ...), custom_call_target="tpu_custom_call" | custom-call | flops 4294967296 | tf_op jit(solution)/shard_map/pallas_call | solution.py:477
  50.3 3.4 %collective-permute-start.18 = (bf16[64,512]{1,0:T(8,128)(2,1)S(1)}, bf16[64,512]{1,0:T(8,128)(2,1)S(1)}, u32[]{:S(2)}, u32[]{:S(2)}) collective-permute-start(bf16[64,512]{1,0:T(8,128)(2,1)S(1)} %get-tuple-element.73), channel_id=1, source_target_pairs={{0,16},{32,48},{64,80},{96,112},{16,0},{48,32},{80,64},{112,96},{1... | collective-permute-start | bytes 196616 | tf_op jit(solution)/shard_map/ppermute | solution.py:416
  53.7 4.4 %collective-permute-start.19 = (bf16[64,512]{1,0:T(8,128)(2,1)S(1)}, bf16[64,512]{1,0:T(8,128)(2,1)S(1)}, u32[]{:S(2)}, u32[]{:S(2)}) collective-permute-start(bf16[64,512]{1,0:T(8,128)(2,1)S(1)} %get-tuple-element.74), channel_id=1, source_target_pairs={{16,32},{48,64},{80,96},{32,16},{64,48},{96,80},{0,0},{112,112},{1... | collective-permute-start | bytes 196616 | tf_op jit(solution)/shard_map/ppermute | solution.py:416
  58.0 0.1 collective-permute-start.20
  58.1 3.8 %collective-permute-start.21 = (bf16[64,128]{1,0:T(8,128)(2,1)S(1)}, bf16[64,128]{1,0:T(8,128)(2,1)S(1)}, u32[]{:S(2)}, u32[]{:S(2)}) collective-permute-start(bf16[64,128]{1,0:T(8,128)(2,1)S(1)} %get-tuple-element.76), channel_id=1, source_target_pairs={{1,2},{3,4},{5,6},{7,8},{9,10},{11,12},{13,14},{2,1},{4,3},{6,5},{... | collective-permute-start | bytes 49160 | tf_op jit(solution)/shard_map/ppermute | solution.py:416
  62.0 0.0 collective-permute-done.20.refs_2_
  62.0 3.3 %collective-permute-done.21.refs_3_ = bf16[64,128]{1,0:T(8,128)(2,1)S(1)} collective-permute-done((bf16[64,128]{1,0:T(8,128)(2,1)S(1)}, bf16[64,128]{1,0:T(8,128)(2,1)S(1)}, u32[]{:S(2)}, u32[]{:S(2)}) %collective-permute-start.21) | collective-permute-done | bytes 16416 | tf_op jit(solution)/shard_map/ppermute | solution.py:416
  65.3 0.0 collective-permute-done.18.refs_0_
  65.3 0.0 collective-permute-done.19.refs_1_
  65.3 2.9 %shard_map.81 = bf16[256,4,8,128]{3,2,1,0:T(8,128)(2,1)} custom-call(s32[4]{0:T(128)S(1)} %copy-done.2, bf16[256,4096]{1,0:T(8,128)(2,1)S(1)} %get-tuple-element.72.x_ref, bf16[4,4,64]{2,1,0:T(4,128)(2,1)S(1)} %bitcast.16, bf16[64,512]{1,0:T(8,128)(2,1)S(1)} %collective-permute-done.18.refs_0_, bf16[64,512]{1,0:T(8,128)(2,1)S(1)} %collective-permute-done.19.refs_1_, ...), custom_call_target="tpu_custom_call" | custom-call | tf_op jit(solution)/shard_map/pallas_call | solution.py:486
  (3 shorter events, 0.0 us)
Async XLA Ops:
  1.5 3.9 %collective-permute-start.1 = (f32[32,256]{1,0:T(8,128)S(1)}, f32[32,256]{1,0:T(8,128)S(1)}, u32[]{:S(2)}, u32[]{:S(2)}) collective-permute-start(f32[32,256]{1,0:T(8,128)S(1)} %maximum_multiply_fusion.refs_0_), channel_id=1, source_target_pairs={{0,1},{1,0},{2,3},{3,2},{4,5},{5,4},{6,7},{7,6},{8,9},{9,8},{10,11... | collective-permute-start | bytes 98312 | tf_op jit(solution)/shard_map/ppermute | solution.py:26
  1.5 11.0 %collective-permute-start = (f32[32,256]{1,0:T(8,128)S(1)}, f32[32,256]{1,0:T(8,128)S(1)}, u32[]{:S(2)}, u32[]{:S(2)}) collective-permute-start(f32[32,256]{1,0:T(8,128)S(1)} %maximum_multiply_fusion.refs_0_), channel_id=1, source_target_pairs={{0,4},{1,5},{2,6},{3,7},{4,0},{5,1},{6,2},{7,3},{8,12},{9,13},{10,... | collective-permute-start | bytes 98312 | tf_op jit(solution)/shard_map/ppermute | solution.py:26
  5.4 5.0 %collective-permute-start.2 = (f32[64,256]{1,0:T(8,128)S(1)}, f32[64,256]{1,0:T(8,128)S(1)}, u32[]{:S(2)}, u32[]{:S(2)}) collective-permute-start(f32[64,256]{1,0:T(8,128)S(1)} %pad_maximum_fusion), channel_id=1, source_target_pairs={{0,8},{1,11},{2,10},{3,9},{4,12},{5,15},{6,14},{7,13},{8,0},{9,3},... | collective-permute-start | bytes 196616 | tf_op jit(solution)/shard_map/ppermute | solution.py:26
  6.0 4.6 %collective-permute-start.3 = (f32[64,256]{1,0:T(8,128)S(1)}, f32[64,256]{1,0:T(8,128)S(1)}, u32[]{:S(2)}, u32[]{:S(2)}) collective-permute-start(f32[64,256]{1,0:T(8,128)S(1)} %pad_maximum_fusion), channel_id=1, source_target_pairs={{0,2},{1,15},{2,0},{3,13},{4,6},{5,11},{6,4},{7,9},{8,10},{9,7},{1... | collective-permute-start | bytes 196616 | tf_op jit(solution)/shard_map/ppermute | solution.py:26
  7.0 5.5 %collective-permute-start.4 = (f32[64,256]{1,0:T(8,128)S(1)}, f32[64,256]{1,0:T(8,128)S(1)}, u32[]{:S(2)}, u32[]{:S(2)}) collective-permute-start(f32[64,256]{1,0:T(8,128)S(1)} %pad_maximum_fusion), channel_id=1, source_target_pairs={{0,6},{1,13},{2,4},{3,15},{4,2},{5,9},{6,0},{7,11},{8,14},{9,5},{1... | collective-permute-start | bytes 196616 | tf_op jit(solution)/shard_map/ppermute | solution.py:26
  7.7 6.0 %copy-start = (s32[8,128]{1,0:T(8,128)S(1)}, s32[8,128]{1,0:T(8,128)}, u32[]{:S(2)}) copy-start(s32[8,128]{1,0:T(8,128)} %param.8) | copy-start | bytes 12292
  12.9 1.9 %collective-permute-start.5 = (f32[256,256]{1,0:T(8,128)S(1)}, f32[256,256]{1,0:T(8,128)S(1)}, u32[]{:S(2)}, u32[]{:S(2)}) collective-permute-start(f32[256,256]{1,0:T(8,128)S(1)} %shard_map.74), channel_id=1, source_target_pairs={{0,1},{1,0},{2,3},{3,2},{4,5},{5,4},{6,7},{7,6},{8,9},{9,8},{10,11... | collective-permute-start | bytes 786440 | tf_op jit(solution)/shard_map/ppermute | solution.py:26
  14.9 6.9 %collective-permute-start.6 = (bf16[256,256]{1,0:T(8,128)(2,1)S(1)}, bf16[256,256]{1,0:T(8,128)(2,1)S(1)}, u32[]{:S(2)}, u32[]{:S(2)}) collective-permute-start(bf16[256,256]{1,0:T(8,128)(2,1)S(1)} %add_convert_fusion.refs_0_.refs_4_), channel_id=1, source_target_pairs={{0,24},{1,57},{2,26},{3,59},{4,28},{5,61},{6,30},{7,63},{8,16},{9,... | collective-permute-start | bytes 393224 | tf_op jit(solution)/shard_map/ppermute | solution.py:26
  17.5 5.8 %collective-permute-start.7 = (bf16[256,256]{1,0:T(8,128)(2,1)S(1)}, bf16[256,256]{1,0:T(8,128)(2,1)S(1)}, u32[]{:S(2)}, u32[]{:S(2)}) collective-permute-start(bf16[256,256]{1,0:T(8,128)(2,1)S(1)} %add_convert_fusion.refs_0_.refs_4_), channel_id=1, source_target_pairs={{0,32},{1,121},{2,34},{3,123},{4,36},{5,125},{6,38},{7,127},{8,40}... | collective-permute-start | bytes 393224 | tf_op jit(solution)/shard_map/ppermute | solution.py:26
  18.8 8.4 %collective-permute-start.8 = (bf16[256,256]{1,0:T(8,128)(2,1)S(1)}, bf16[256,256]{1,0:T(8,128)(2,1)S(1)}, u32[]{:S(2)}, u32[]{:S(2)}) collective-permute-start(bf16[256,256]{1,0:T(8,128)(2,1)S(1)} %add_convert_fusion.refs_0_.refs_4_), channel_id=1, source_target_pairs={{0,96},{1,89},{2,98},{3,91},{4,100},{5,93},{6,102},{7,95},{8,104},... | collective-permute-start | bytes 393224 | tf_op jit(solution)/shard_map/ppermute | solution.py:26
  18.8 10.5 %collective-permute-start.12 = (bf16[128,256]{1,0:T(8,128)(2,1)S(1)}, bf16[128,256]{1,0:T(8,128)(2,1)S(1)}, u32[]{:S(2)}, u32[]{:S(2)}) collective-permute-start(bf16[128,256]{1,0:T(8,128)(2,1)S(1)} %constant_dynamic-slice_fusion), channel_id=1, source_target_pairs={{0,64},{1,65},{2,66},{3,67},{4,68},{5,69},{6,70},{7,71},{8,72},{9,... | collective-permute-start | bytes 196616 | tf_op jit(solution)/shard_map/ppermute | solution.py:26
  27.2 3.6 %collective-permute-start.10 = (bf16[256,256]{1,0:T(8,128)(2,1)S(1)}, bf16[256,256]{1,0:T(8,128)(2,1)S(1)}, u32[]{:S(2)}, u32[]{:S(2)}) collective-permute-start(bf16[256,256]{1,0:T(8,128)(2,1)S(1)} %collective-permute-done.7.refs_0_.refs_6_), channel_id=1, source_target_pairs={{0,1},{1,0},{2,3},{3,2},{4,5},{5,4},{6,7},{7,6},{8,9},{9,8},{10,11... | collective-permute-start | bytes 393224 | tf_op jit(solution)/shard_map/ppermute | solution.py:26
  27.2 3.6 %collective-permute-start.11 = (bf16[256,256]{1,0:T(8,128)(2,1)S(1)}, bf16[256,256]{1,0:T(8,128)(2,1)S(1)}, u32[]{:S(2)}, u32[]{:S(2)}) collective-permute-start(bf16[256,256]{1,0:T(8,128)(2,1)S(1)} %collective-permute-done.8.refs_1_.refs_7_), channel_id=1, source_target_pairs={{0,1},{1,0},{2,3},{3,2},{4,5},{5,4},{6,7},{7,6},{8,9},{9,8},{10,11... | collective-permute-start | bytes 393224 | tf_op jit(solution)/shard_map/ppermute | solution.py:26
  27.7 3.1 %collective-permute-start.9 = (bf16[256,256]{1,0:T(8,128)(2,1)S(1)}, bf16[256,256]{1,0:T(8,128)(2,1)S(1)}, u32[]{:S(2)}, u32[]{:S(2)}) collective-permute-start(bf16[256,256]{1,0:T(8,128)(2,1)S(1)} %collective-permute-done.6.refs_1_.refs_5_), channel_id=1, source_target_pairs={{0,1},{1,0},{2,3},{3,2},{4,5},{5,4},{6,7},{7,6},{8,9},{9,8},{10,11... | collective-permute-start | bytes 393224 | tf_op jit(solution)/shard_map/ppermute | solution.py:26
  29.3 1.5 %collective-permute-start.13 = (bf16[128,256]{1,0:T(8,128)(2,1)S(1)}, bf16[128,256]{1,0:T(8,128)(2,1)S(1)}, u32[]{:S(2)}, u32[]{:S(2)}) collective-permute-start(bf16[128,256]{1,0:T(8,128)(2,1)S(1)} %collective-permute-done.12.refs_4_.refs_12_), channel_id=1, source_target_pairs={{0,1},{1,0},{2,3},{3,2},{4,5},{5,4},{6,7},{7,6},{8,9},{9,8},{10,11... | collective-permute-start | bytes 196616 | tf_op jit(solution)/shard_map/ppermute | solution.py:26
  31.4 13.0 %collective-permute-start.14 = (bf16[64,512]{1,0:T(8,128)(2,1)S(1)}, bf16[64,512]{1,0:T(8,128)(2,1)S(1)}, u32[]{:S(2)}, u32[]{:S(2)}) collective-permute-start(bf16[64,512]{1,0:T(8,128)(2,1)S(1)} %get-tuple-element.68), channel_id=1, source_target_pairs={{0,16},{32,48},{64,80},{96,112},{16,0},{48,32},{80,64},{112,96},{1... | collective-permute-start | bytes 196616 | tf_op jit(solution)/shard_map/ppermute | solution.py:416
  33.6 10.8 %collective-permute-start.15 = (bf16[64,512]{1,0:T(8,128)(2,1)S(1)}, bf16[64,512]{1,0:T(8,128)(2,1)S(1)}, u32[]{:S(2)}, u32[]{:S(2)}) collective-permute-start(bf16[64,512]{1,0:T(8,128)(2,1)S(1)} %get-tuple-element.69), channel_id=1, source_target_pairs={{16,32},{48,64},{80,96},{32,16},{64,48},{96,80},{0,0},{112,112},{1... | collective-permute-start | bytes 196616 | tf_op jit(solution)/shard_map/ppermute | solution.py:416
  37.1 7.2 %collective-permute-start.16 = (bf16[64,128]{1,0:T(8,128)(2,1)S(1)}, bf16[64,128]{1,0:T(8,128)(2,1)S(1)}, u32[]{:S(2)}, u32[]{:S(2)}) collective-permute-start(bf16[64,128]{1,0:T(8,128)(2,1)S(1)} %get-tuple-element.70), channel_id=1, source_target_pairs={{0,1},{2,3},{4,5},{6,7},{8,9},{10,11},{12,13},{14,15},{1,0},{3,2},... | collective-permute-start | bytes 49160 | tf_op jit(solution)/shard_map/ppermute | solution.py:416
  37.2 7.2 %collective-permute-start.17 = (bf16[64,128]{1,0:T(8,128)(2,1)S(1)}, bf16[64,128]{1,0:T(8,128)(2,1)S(1)}, u32[]{:S(2)}, u32[]{:S(2)}) collective-permute-start(bf16[64,128]{1,0:T(8,128)(2,1)S(1)} %get-tuple-element.71), channel_id=1, source_target_pairs={{1,2},{3,4},{5,6},{7,8},{9,10},{11,12},{13,14},{2,1},{4,3},{6,5},{... | collective-permute-start | bytes 49160 | tf_op jit(solution)/shard_map/ppermute | solution.py:416
  41.8 2.6 %copy-start.1 = (bf16[4,64,4]{1,2,0:T(4,128)(2,1)S(1)}, bf16[4,64,4]{1,2,0:T(4,128)(2,1)}, u32[]{:S(2)}) copy-start(bf16[4,64,4]{1,2,0:T(4,128)(2,1)} %param.10) | copy-start | bytes 6148
  41.8 2.6 %copy-start.2 = (s32[4]{0:T(128)S(1)}, s32[4]{0:T(128)}, u32[]{:S(2)}) copy-start(s32[4]{0:T(128)} %port_ref.3) | copy-start | bytes 52
  50.3 15.0 %collective-permute-start.18 = (bf16[64,512]{1,0:T(8,128)(2,1)S(1)}, bf16[64,512]{1,0:T(8,128)(2,1)S(1)}, u32[]{:S(2)}, u32[]{:S(2)}) collective-permute-start(bf16[64,512]{1,0:T(8,128)(2,1)S(1)} %get-tuple-element.73), channel_id=1, source_target_pairs={{0,16},{32,48},{64,80},{96,112},{16,0},{48,32},{80,64},{112,96},{1... | collective-permute-start | bytes 196616 | tf_op jit(solution)/shard_map/ppermute | solution.py:416
  53.7 11.6 %collective-permute-start.19 = (bf16[64,512]{1,0:T(8,128)(2,1)S(1)}, bf16[64,512]{1,0:T(8,128)(2,1)S(1)}, u32[]{:S(2)}, u32[]{:S(2)}) collective-permute-start(bf16[64,512]{1,0:T(8,128)(2,1)S(1)} %get-tuple-element.74), channel_id=1, source_target_pairs={{16,32},{48,64},{80,96},{32,16},{64,48},{96,80},{0,0},{112,112},{1... | collective-permute-start | bytes 196616 | tf_op jit(solution)/shard_map/ppermute | solution.py:416
  58.0 3.9 %collective-permute-start.20 = (bf16[64,128]{1,0:T(8,128)(2,1)S(1)}, bf16[64,128]{1,0:T(8,128)(2,1)S(1)}, u32[]{:S(2)}, u32[]{:S(2)}) collective-permute-start(bf16[64,128]{1,0:T(8,128)(2,1)S(1)} %get-tuple-element.75), channel_id=1, source_target_pairs={{0,1},{2,3},{4,5},{6,7},{8,9},{10,11},{12,13},{14,15},{1,0},{3,2},... | collective-permute-start | bytes 49160 | tf_op jit(solution)/shard_map/ppermute | solution.py:416
  58.1 7.2 %collective-permute-start.21 = (bf16[64,128]{1,0:T(8,128)(2,1)S(1)}, bf16[64,128]{1,0:T(8,128)(2,1)S(1)}, u32[]{:S(2)}, u32[]{:S(2)}) collective-permute-start(bf16[64,128]{1,0:T(8,128)(2,1)S(1)} %get-tuple-element.76), channel_id=1, source_target_pairs={{1,2},{3,4},{5,6},{7,8},{9,10},{11,12},{13,14},{2,1},{4,3},{6,5},{... | collective-permute-start | bytes 49160 | tf_op jit(solution)/shard_map/ppermute | solution.py:416

commit v15 on v14

--- a/solution.py
+++ b/solution.py
@@ -131,12 +131,10 @@
     return jnp.where(index > 0, low, 0.0), jnp.where(index < count - 1, high, 0.0)
 
 
-def store_rims(out_refs, north, south, west, east):
-    first, second, third, fourth = out_refs
-    first[...] = jnp.where(even("row"), south, north).astype(BF)
-    second[...] = jnp.where(even("row"), north, south).astype(BF)
-    third[...] = jnp.where(even("col"), east, west).astype(BF)
-    fourth[...] = jnp.where(even("col"), west, east).astype(BF)
+def store_rims(out_refs, axis, low, high):
+    first, second = out_refs
+    first[...] = jnp.where(even(axis), high, low).astype(BF)
+    second[...] = jnp.where(even(axis), low, high).astype(BF)
 
 
 def lane_of(value, lane):
@@ -280,7 +278,8 @@
     types = types_ref[...].astype(F32)
     quarter = x_ref.shape[0] // 4
     values = rims(x_ref, types, ports, sides_ref[...], kinds_ref[0:1, :], maps, refs[-7:-4])
-    store_rims(refs[-4:], values[0], values[1], values[2][0:quarter], values[2][quarter:])
+    store_rims(refs[-4:-2], "row", values[0], values[1])
+    store_rims(refs[-2:], "col", values[2][0:quarter], values[2][quarter:])
 
 
 def first_kernel(rows, ports, first, x_ref, types_ref, done_ref, *refs):
@@ -294,63 +293,72 @@
         shifted(total, refs[-1].at[:, cols], rows)
 
 
-def second_kernel(rows, width, port_ref, x_ref, types_ref, profile_ref, *refs):
-    halo_refs, map_refs, next_ref = refs[:4], refs[4:-5], refs[-5]
-    rim_refs = refs[-4:]
-    types = types_ref[...].astype(F32).astype(BF)
-    tile = types.shape[1]
+def patched(rows, width, x_ref, port_ref, profile_ref, halo_refs, places):
     order = x_ref.shape[0]
     quarter = order // 4
-    maps = with_steps(map_refs, 0, len(MAP_STEPS))
     north_in, south_in = halos_inside("row", *halo_refs[:2])
     west_in, east_in = halos_inside("col", *halo_refs[2:])
     lane = lax.broadcasted_iota(jnp.int32, (quarter, LANES), 1)
+    blocks = []
+    for port, row in places:
+        place = port * rows + row
+        rim = slice(port * LANES, (port + 1) * LANES)
+        value = x_ref[:, place * LANES : (place + 1) * LANES].astype(F32)
+        north, south, west, east = (value[i * quarter : (i + 1) * quarter] for i in range(4))
+        north = north_in[:, rim] if row == 0 else north
+        south = south_in[:, rim] if row == rows - 1 else south
+        west = jnp.where(lane == 0, lane_of(west_in, 64 + place), west)
+        east = jnp.where(lane == LANES - 1, lane_of(east_in, place), east)
+        source_row, col, inside = port_place(port_ref, port, rows, width)
+        here = lane == jnp.where(inside & (source_row == row), col, -1)
+        columns = [
+            jnp.where(here, part + port_profile_column(profile_ref, port, edge), part)
+            for edge, part in enumerate((north, south, west, east))
+        ]
+        blocks.append(jnp.concatenate(columns, axis=0).astype(BF))
+    return jnp.concatenate(blocks, axis=1)
+
+
+def types_of_rows(types_ref, rows):
+    types = types_ref[...].astype(F32)
+    return jnp.concatenate([types[:, row * LANES : (row + 1) * LANES] for row in rows], axis=1)
+
+
+def ends_kernel(rows, ports, width, port_ref, x_ref, types_ref, profile_ref, *refs):
+    halo_refs, map_refs, ends_ref = refs[:4], refs[4:-3], refs[-3]
+    quarter = x_ref.shape[0] // 4
+    places = [(port, row) for row in (0, rows - 1) for port in range(ports)]
+    block = patched(rows, width, x_ref, port_ref, profile_ref, halo_refs, places)
+    types = types_of_rows(types_ref, [row for _, row in places]).astype(BF)
+    total = products(block, types, with_steps(map_refs, 0, len(MAP_STEPS)), 0, x_ref.shape[0])
+    ends_ref[...] = total.astype(BF)
+    wide = ports * LANES
+    store_rims(refs[-2:], "row", total[0:quarter, :wide], total[quarter : 2 * quarter, wide:])
+
+
+def second_kernel(rows, ports, width, port_ref, x_ref, types_ref, profile_ref, ends_ref, *refs):
+    halo_refs, map_refs, next_ref = refs[:4], refs[4:-3], refs[-3]
+    order, tile = x_ref.shape[0], rows * width
+    quarter = order // 4
+    maps = with_steps(map_refs, 0, len(MAP_STEPS))
+    types = types_of_rows(types_ref, range(1, rows - 1)).astype(BF)
+    lane = lax.broadcasted_iota(jnp.int32, (quarter, LANES), 1)
     west_rim = east_rim = jnp.zeros((quarter, LANES), F32)
-    north_rim, south_rim = [], []
-    place_in_tile = lax.broadcasted_iota(jnp.int32, (1, tile), 1)
-    for port in range(x_ref.shape[1] // tile):
-        own = slice(port * tile, (port + 1) * tile)
-        rim = slice(port * LANES, (port + 1) * LANES)
-        north = jnp.concatenate(
-            [north_in[:, rim].astype(BF), x_ref[0:quarter, port * tile + LANES : (port + 1) * tile]],
-            axis=1,
-        )
-        south = jnp.concatenate(
-            [
-                x_ref[quarter : 2 * quarter, port * tile : (port + 1) * tile - LANES],
-                south_in[:, rim].astype(BF),
-            ],
-            axis=1,
-        )
-        west, east = [], []
-        for row in range(rows):
-            place = port * rows + row
-            cols = slice(place * LANES, (place + 1) * LANES)
-            value = x_ref[2 * quarter : 3 * quarter, cols].astype(F32)
-            west.append(jnp.where(lane == 0, lane_of(west_in, 64 + place), value))
-            value = x_ref[3 * quarter :, cols].astype(F32)
-            east.append(jnp.where(lane == LANES - 1, lane_of(east_in, place), value))
-        west = jnp.concatenate(west, axis=1).astype(BF)
-        east = jnp.concatenate(east, axis=1).astype(BF)
-        block = jnp.concatenate([north, south, west, east], axis=0)
-        row, col, inside = port_place(port_ref, port, rows, width)
-        here = place_in_tile == jnp.where(inside, row * width + col, -1)
-        current = block.astype(F32)
-        columns = [port_profile_column(profile_ref, port, edge) for edge in range(4)]
-        added = current + jnp.concatenate(columns, axis=0)
-        block = jnp.where(here, added, current).astype(BF)
-        total = products(block, types, maps, 0, order)
-        north, south = shifted(total, next_ref.at[:, own], rows)
-        north_rim.append(north[:, 0:LANES])
-        south_rim.append(south[:, tile - LANES :])
+    for port in range(ports):
+        places = [(port, row) for row in range(1, rows - 1)]
+        block = patched(rows, width, x_ref, port_ref, profile_ref, halo_refs, places)
+        middle = products(block, types, maps, 0, order)
+        top = ends_ref[:, port * LANES : (port + 1) * LANES].astype(F32)
+        bottom = ends_ref[:, (ports + port) * LANES : (ports + port + 1) * LANES].astype(F32)
+        total = jnp.concatenate([top, middle, bottom], axis=1)
+        shifted(total, next_ref.at[:, port * tile : (port + 1) * tile], rows)
         for row in range(rows):
             place = port * rows + row
             west = lane_of(total[2 * quarter : 3 * quarter], row * LANES)
             east = lane_of(total[3 * quarter :], (row + 1) * LANES - 1)
             west_rim = jnp.where(lane == place, west, west_rim)
             east_rim = jnp.where(lane == place, east, east_rim)
-    north_rim, south_rim = (jnp.concatenate(value, axis=1) for value in (north_rim, south_rim))
-    store_rims(rim_refs, north_rim, south_rim, west_rim, east_rim)
+    store_rims(refs[-2:], "col", west_rim, east_rim)
 
 
 def last_kernel(rows, width, port_ref, x_ref, profile_ref, *refs):
@@ -405,15 +413,13 @@
         copy.wait()
 
 
-def exchange(rims):
-    def pairs(axis, first):
+def exchange(rims, axis):
+    def pairs(first):
         count = lax.axis_size(axis)
-        near = [(i, i + 1) for i in range(first, count - 1, 2)]
-        alone = [(0, 0), (count - 1, count - 1)] if first else []
-        return near + [(target, source) for source, target in near] + alone
-
-    axes = (("row", 0), ("row", 1), ("col", 0), ("col", 1))
-    return [lax.ppermute(rim, axis, pairs(axis, first)) for rim, (axis, first) in zip(rims, axes)]
+        near = [(i, (i + 1) % count) for i in range(first, count, 2)]
+        return near + [(target, source) for source, target in near]
+
+    return [lax.ppermute(rim, axis, pairs(first)) for first, rim in enumerate(rims)]
 
 
 def body(traces, cell_type, port_cell, port_profile, mode_shapes, mode_values, mode_weights):
@@ -463,7 +469,7 @@
         *parts,
         flops=work // 8,
     )
-    halos = exchange(sent)
+    halos = exchange(sent[:2], "row") + exchange(sent[2:], "col")
     (x,) = whole_call(
         functools.partial(first_kernel, rows, ports, 4),
         [next_shape],
@@ -473,16 +479,25 @@
         *late,
         flops=work // 2,
     )
-    operands = [port_cell, x, types, profile, *halos, *maps]
-    x, *sent = pl.pallas_call(
-        functools.partial(second_kernel, rows, width),
-        in_specs=[ports_spec] + [WHOLE] * (len(operands) - 1),
-        out_specs=[WHOLE] * 5,
-        out_shape=[next_shape] + rim_shapes,
-        compiler_params=PARAMS,
-        cost_estimate=pl.CostEstimate(flops=work, bytes_accessed=0, transcendentals=0),
-    )(*operands)
-    operands = [port_cell, x, profile, *exchange(sent)]
+    def sweep(kernel, shapes, operands, share):
+        return pl.pallas_call(
+            functools.partial(kernel, rows, ports, width),
+            in_specs=[ports_spec] + [WHOLE] * (len(operands) - 1),
+            out_specs=[WHOLE] * len(shapes),
+            out_shape=shapes,
+            compiler_params=PARAMS,
+            cost_estimate=pl.CostEstimate(
+                flops=work * share // rows, bytes_accessed=0, transcendentals=0
+            ),
+        )(*operands)
+
+    ends_shape = jax.ShapeDtypeStruct((order, 2 * ports * LANES), BF)
+    operands = [port_cell, x, types, profile]
+    ends, *sent = sweep(ends_kernel, [ends_shape] + rim_shapes[:2], operands + halos + maps, 2)
+    row_halos = exchange(sent, "row")
+    operands = operands + [ends] + halos + maps
+    x, *sent = sweep(second_kernel, [next_shape] + rim_shapes[2:], operands, rows - 2)
+    operands = [port_cell, x, profile, *row_halos, *exchange(sent, "col")]
     out = pl.pallas_call(
         functools.partial(last_kernel, rows, width),
         in_specs=[ports_spec] + [WHOLE] * (len(operands) - 1),

time: 68.7 us -> 64.7 us (0.942)
  the two profiles are of different devices: /device:TPU:18 before, /device:TPU:0 now
where the time goes in v15:
time: 64.7 us; the launch traced here: 64.5 us
  starting transfers between devices  25.6 us (40%)
  Pallas kernels  20.3 us (31%)
  waiting for transfers between devices  16.7 us (26%)
  other arithmetic  0.85 us (1%)
  local copies, waits for them, and re-layouts  0.67 us (1%)
    ppermute x14, starting transfers between devices, swap(): return lax.ppermute(value, ('row', 'col'), pairs)  15.2 us
    ppermute x14, waiting for transfers between devices, swap(): return lax.ppermute(value, ('row', 'col'), pairs)  10.7 us
    ppermute x8, starting transfers between devices, exchange(): lax.ppermute(rim, axis, pairs(first))  10.5 us
    pallas_call x6, Pallas kernels, whole_call(): pl.pallas_call(kernel, in_specs=[WHOLE] * len(operands), out_specs=[WHOLE...  7.77 us
    pallas_call x2, Pallas kernels, sweep(): pl.pallas_call(functools.partial(kernel, rows, ports, width), in_specs=[p...  7.19 us
    ppermute x8, waiting for transfers between devices, exchange(): lax.ppermute(rim, axis, pairs(first))  6.07 us
    pallas_call x1, Pallas kernels, body(): pl.pallas_call(functools.partial(last_kernel, rows, width), in_specs=[por...  3.33 us
    pallas_call x1, Pallas kernels, own_type_map(): pl.pallas_call(flat_kernel, in_specs=[pl.BlockSpec(memory_space=pltpu.HBM...  1.98 us
  transfers between devices with their start and end apart: 22, of which 9 were waited for; matrix products, arithmetic and copies ran while one was open for 0% of the time, Pallas kernels for 21%

profile of v15, /device:TPU:0, one launch (start us, length us, event | category | flops | bytes accessed | tf_op | source)
XLA Modules:
  0.0 64.5 jit_solution(18332257894972714095)
XLA Ops:
  0.0 0.7 %concatenate.10 = f32[32]{0:T(128)S(1)} pad(f32[16]{0:T(128)} %bitcast.22, f32[]{:T(128)} %constant.6.clone.1), padding=0_16 | pad | bytes 196 | tf_op jit(solution)/shard_map/concatenate | solution.py:82
  0.7 0.8 %maximum_multiply_fusion.refs_0_ = f32[32,256]{1,0:T(8,128)S(1)} fusion(f32[16,256]{1,0:T(8,128)} %bitcast.20, f32[16,256]{1,0:T(8,128)} %bitcast.21, f32[32]{0:T(128)S(1)} %concatenate.10), kind=kLoop, calls=%fused_computation.2 | loop fusion | flops 16384 | bytes 65664 | tf_op jit(solution)/shard_map/mul | solution.py:82
  1.5 0.0 collective-permute-start.1
  1.5 4.0 %collective-permute-start = (f32[32,256]{1,0:T(8,128)S(1)}, f32[32,256]{1,0:T(8,128)S(1)}, u32[]{:S(2)}, u32[]{:S(2)}) collective-permute-start(f32[32,256]{1,0:T(8,128)S(1)} %maximum_multiply_fusion.refs_0_), channel_id=1, source_target_pairs={{0,4},{1,5},{2,6},{3,7},{4,0},{5,1},{6,2},{7,3},{8,12},{9,13},{10,... | collective-permute-start | bytes 98312 | tf_op jit(solution)/shard_map/ppermute | solution.py:26
  5.5 0.0 collective-permute-done.1
  5.5 1.6 %collective-permute-start.2 = (f32[64,256]{1,0:T(8,128)S(1)}, f32[64,256]{1,0:T(8,128)S(1)}, u32[]{:S(2)}, u32[]{:S(2)}) collective-permute-start(f32[64,256]{1,0:T(8,128)S(1)} %pad_maximum_fusion), channel_id=1, source_target_pairs={{0,8},{1,11},{2,10},{3,9},{4,12},{5,15},{6,14},{7,13},{8,0},{9,3},... | collective-permute-start | bytes 196616 | tf_op jit(solution)/shard_map/ppermute | solution.py:26
  7.0 1.0 %collective-permute-start.3 = (f32[64,256]{1,0:T(8,128)S(1)}, f32[64,256]{1,0:T(8,128)S(1)}, u32[]{:S(2)}, u32[]{:S(2)}) collective-permute-start(f32[64,256]{1,0:T(8,128)S(1)} %pad_maximum_fusion), channel_id=1, source_target_pairs={{0,2},{1,15},{2,0},{3,13},{4,6},{5,11},{6,4},{7,9},{8,10},{9,7},{1... | collective-permute-start | bytes 196616 | tf_op jit(solution)/shard_map/ppermute | solution.py:26
  8.1 0.6 collective-permute-start.4
  8.7 0.0 copy-start
  8.7 2.0 %shard_map.73.x_ref = bf16[256,4096]{1,0:T(8,128)(2,1)S(1)} custom-call(bf16[256,4,8,128]{3,2,1,0:T(8,128)(2,1)} %bitcast.19), custom_call_target="tpu_custom_call" | custom-call | flops 1073741824 | tf_op jit(solution)/shard_map/pallas_call | solution.py:89
  10.7 0.0 collective-permute-done.2.refs_2_
  10.7 0.6 collective-permute-done.3.refs_3_
  11.3 2.9 %collective-permute-done.4.refs_4_ = f32[64,256]{1,0:T(8,128)S(1)} collective-permute-done((f32[64,256]{1,0:T(8,128)S(1)}, f32[64,256]{1,0:T(8,128)S(1)}, u32[]{:S(2)}, u32[]{:S(2)}) %collective-permute-start.4) | collective-permute-done | bytes 65568 | tf_op jit(solution)/shard_map/ppermute | solution.py:26
  14.2 0.0 collective-permute-done.refs_1_
  14.2 0.4 shard_map.74
  14.6 0.1 collective-permute-start.5
  14.7 0.0 copy-done
  14.7 1.2 %shard_map.75 = (bf16[256,128]{1,0:T(8,128)(2,1)S(1)}, bf16[16,128]{1,0:T(8,128)(2,1)S(1)}) custom-call(bf16[256,4096]{1,0:T(8,128)(2,1)S(1)} %shard_map.73.x_ref, s32[1,1024]{1,0:T(1,128)S(1)} %bitcast.9), custom_call_target="tpu_custom_call" | custom-call | flops 1073741824 | tf_op jit(solution)/shard_map/pallas_call | solution.py:69
  15.9 0.3 collective-permute-done.5
  16.3 2.2 %collective-permute-start.6 = (bf16[256,256]{1,0:T(8,128)(2,1)S(1)}, bf16[256,256]{1,0:T(8,128)(2,1)S(1)}, u32[]{:S(2)}, u32[]{:S(2)}) collective-permute-start(bf16[256,256]{1,0:T(8,128)(2,1)S(1)} %add_convert_fusion.refs_0_.refs_4_), channel_id=1, source_target_pairs={{0,24},{1,57},{2,26},{3,59},{4,28},{5,61},{6,30},{7,63},{8,16},{9,... | collective-permute-start | bytes 393224 | tf_op jit(solution)/shard_map/ppermute | solution.py:26
  18.5 1.6 %collective-permute-start.7 = (bf16[256,256]{1,0:T(8,128)(2,1)S(1)}, bf16[256,256]{1,0:T(8,128)(2,1)S(1)}, u32[]{:S(2)}, u32[]{:S(2)}) collective-permute-start(bf16[256,256]{1,0:T(8,128)(2,1)S(1)} %add_convert_fusion.refs_0_.refs_4_), channel_id=1, source_target_pairs={{0,32},{1,121},{2,34},{3,123},{4,36},{5,125},{6,38},{7,127},{8,40}... | collective-permute-start | bytes 393224 | tf_op jit(solution)/shard_map/ppermute | solution.py:26
  20.1 2.2 %collective-permute-start.8 = (bf16[256,256]{1,0:T(8,128)(2,1)S(1)}, bf16[256,256]{1,0:T(8,128)(2,1)S(1)}, u32[]{:S(2)}, u32[]{:S(2)}) collective-permute-start(bf16[256,256]{1,0:T(8,128)(2,1)S(1)} %add_convert_fusion.refs_0_.refs_4_), channel_id=1, source_target_pairs={{0,96},{1,89},{2,98},{3,91},{4,100},{5,93},{6,102},{7,95},{8,104},... | collective-permute-start | bytes 393224 | tf_op jit(solution)/shard_map/ppermute | solution.py:26
  22.3 0.8 %collective-permute-start.12 = (bf16[128,256]{1,0:T(8,128)(2,1)S(1)}, bf16[128,256]{1,0:T(8,128)(2,1)S(1)}, u32[]{:S(2)}, u32[]{:S(2)}) collective-permute-start(bf16[128,256]{1,0:T(8,128)(2,1)S(1)} %constant_dynamic-slice_fusion), channel_id=1, source_target_pairs={{0,64},{1,65},{2,66},{3,67},{4,68},{5,69},{6,70},{7,71},{8,72},{9,... | collective-permute-start | bytes 196616 | tf_op jit(solution)/shard_map/ppermute | solution.py:26
  23.1 0.7 %collective-permute-done.6.refs_1_.refs_5_ = bf16[256,256]{1,0:T(8,128)(2,1)S(1)} collective-permute-done((bf16[256,256]{1,0:T(8,128)(2,1)S(1)}, bf16[256,256]{1,0:T(8,128)(2,1)S(1)}, u32[]{:S(2)}, u32[]{:S(2)}) %collective-permute-start.6) | collective-permute-done | bytes 131104 | tf_op jit(solution)/shard_map/ppermute | solution.py:26
  23.7 1.5 %shard_map.76 = (bf16[256,4096]{1,0:T(8,128)(2,1)S(1)}, bf16[64,512]{1,0:T(8,128)(2,1)S(1)}, bf16[64,512]{1,0:T(8,128)(2,1)S(1)}, bf16[128,128]{1,0:T(8,128)(2,1)S(1)}) custom-call(bf16[256,4096]{1,0:T(8,128)(2,1)S(1)} %shard_map.73.x_ref, s32[1,1024]{1,0:T(1,128)S(1)} %bitcast.10, bf16[256,128]{1,0:T(8,128)(2,1)S(1)} %get-tuple-element.52.sides_ref, ...), custom_call_target="tpu_custom_call" | custom-call | flops 1227133568 | tf_op jit(solution)/shard_map/pallas_call | solution.py:69
  25.3 0.0 collective-permute-done.7.refs_0_.refs_6_
  25.3 5.2 %collective-permute-done.8.refs_1_.refs_7_ = bf16[256,256]{1,0:T(8,128)(2,1)S(1)} collective-permute-done((bf16[256,256]{1,0:T(8,128)(2,1)S(1)}, bf16[256,256]{1,0:T(8,128)(2,1)S(1)}, u32[]{:S(2)}, u32[]{:S(2)}) %collective-permute-start.8) | collective-permute-done | bytes 131104 | tf_op jit(solution)/shard_map/ppermute | solution.py:26
  30.5 0.0 collective-permute-start.10
  30.5 0.5 collective-permute-start.11
  31.0 0.0 collective-permute-start.9
  31.0 1.5 %shard_map.77 = (bf16[256,4096]{1,0:T(8,128)(2,1)S(1)}, bf16[64,512]{1,0:T(8,128)(2,1)S(1)}, bf16[64,512]{1,0:T(8,128)(2,1)S(1)}, bf16[128,128]{1,0:T(8,128)(2,1)S(1)}) custom-call(bf16[256,4096]{1,0:T(8,128)(2,1)S(1)} %shard_map.73.x_ref, s32[1,1024]{1,0:T(1,128)S(1)} %bitcast.11, bf16[256,128]{1,0:T(8,128)(2,1)S(1)} %get-tuple-element.52.sides_ref, ...), custom_call_target="tpu_custom_call" | custom-call | flops 1227133568 | tf_op jit(solution)/shard_map/pallas_call | solution.py:69
  32.5 0.0 collective-permute-done.12.refs_4_.refs_12_
  32.5 0.6 collective-permute-start.13
  33.1 0.9 %collective-permute-done.13.refs_3_.refs_11_ = bf16[128,256]{1,0:T(8,128)(2,1)S(1)} collective-permute-done((bf16[128,256]{1,0:T(8,128)(2,1)S(1)}, bf16[128,256]{1,0:T(8,128)(2,1)S(1)}, u32[]{:S(2)}, u32[]{:S(2)}) %collective-permute-start.13) | collective-permute-done | bytes 65568 | tf_op jit(solution)/shard_map/ppermute | solution.py:26
  34.0 0.0 collective-permute-done.10.refs_1_.refs_9_
  34.0 0.0 collective-permute-done.11.refs_2_.refs_10_
  34.0 0.0 collective-permute-done.9.refs_0_.refs_8_
  34.0 0.6 shard_map.79
  34.7 0.7 %collective-permute-start.14 = (bf16[64,512]{1,0:T(8,128)(2,1)S(1)}, bf16[64,512]{1,0:T(8,128)(2,1)S(1)}, u32[]{:S(2)}, u32[]{:S(2)}) collective-permute-start(bf16[64,512]{1,0:T(8,128)(2,1)S(1)} %get-tuple-element.69), channel_id=1, source_target_pairs={{0,16},{32,48},{64,80},{96,112},{16,0},{48,32},{80,64},{112,96},{1... | collective-permute-start | bytes 196616 | tf_op jit(solution)/shard_map/ppermute | solution.py:422
  35.4 4.5 %collective-permute-start.15 = (bf16[64,512]{1,0:T(8,128)(2,1)S(1)}, bf16[64,512]{1,0:T(8,128)(2,1)S(1)}, u32[]{:S(2)}, u32[]{:S(2)}) collective-permute-start(bf16[64,512]{1,0:T(8,128)(2,1)S(1)} %get-tuple-element.70), channel_id=1, source_target_pairs={{16,32},{48,64},{80,96},{112,0},{32,16},{64,48},{96,80},{0,112},{1... | collective-permute-start | bytes 196616 | tf_op jit(solution)/shard_map/ppermute | solution.py:422
  39.9 0.0 collective-permute-start.16
  39.9 1.1 %collective-permute-start.17 = (bf16[64,128]{1,0:T(8,128)(2,1)S(1)}, bf16[64,128]{1,0:T(8,128)(2,1)S(1)}, u32[]{:S(2)}, u32[]{:S(2)}) collective-permute-start(bf16[64,128]{1,0:T(8,128)(2,1)S(1)} %get-tuple-element.72), channel_id=1, source_target_pairs={{1,2},{3,4},{5,6},{7,8},{9,10},{11,12},{13,14},{15,0},{2,1},{4,3},... | collective-permute-start | bytes 49160 | tf_op jit(solution)/shard_map/ppermute | solution.py:422
  41.0 0.0 copy-start.1
  41.0 0.0 copy-start.2
  41.0 2.5 %shard_map.78.x_ref = bf16[256,4096]{1,0:T(8,128)(2,1)S(1)} custom-call(bf16[256,4096]{1,0:T(8,128)(2,1)S(1)} %shard_map.73.x_ref, s32[1,1024]{1,0:T(1,128)S(1)} %bitcast.13, bf16[256,4096]{1,0:T(8,128)(2,1)S(1)} %get-tuple-element.62.done_ref, bf16[256,256]{1,0:T(8,128)(2,1)S(1)} %collective-permute-done.9.refs_0_.refs_8_, ...), custom_call_target="tpu_custom_call" | custom-call | flops 2147483648 | tf_op jit(solution)/shard_map/pallas_call | solution.py:69
  43.6 0.0 collective-permute-done.16.refs_2_
  43.6 1.6 %collective-permute-done.17.refs_3_ = bf16[64,128]{1,0:T(8,128)(2,1)S(1)} collective-permute-done((bf16[64,128]{1,0:T(8,128)(2,1)S(1)}, bf16[64,128]{1,0:T(8,128)(2,1)S(1)}, u32[]{:S(2)}, u32[]{:S(2)}) %collective-permute-start.17) | collective-permute-done | bytes 16416 | tf_op jit(solution)/shard_map/ppermute | solution.py:422
  45.2 0.0 collective-permute-done.14.refs_0_
  45.2 0.0 collective-permute-done.15.refs_1_
  45.2 0.0 copy-done.1
  45.2 0.0 copy-done.2
  45.2 2.3 %shard_map.80 = (bf16[256,1024]{1,0:T(8,128)(2,1)S(1)}, bf16[64,512]{1,0:T(8,128)(2,1)S(1)}, bf16[64,512]{1,0:T(8,128)(2,1)S(1)}) custom-call(s32[4]{0:T(128)S(1)} %copy-done.2, bf16[256,4096]{1,0:T(8,128)(2,1)S(1)} %shard_map.78.x_ref, s32[1,1024]{1,0:T(1,128)S(1)} %bitcast.14, bf16[4,4,64]{2,1,0:T(4,128)(2,1)S(1)} %bitcast.16, ...), custom_call_target="tpu_custom_call" | custom-call | flops 1073741824 | tf_op jit(solution)/shard_map/pallas_call | solution.py:483
  47.5 0.1 collective-permute-start.18
  47.6 3.0 %collective-permute-start.19 = (bf16[64,512]{1,0:T(8,128)(2,1)S(1)}, bf16[64,512]{1,0:T(8,128)(2,1)S(1)}, u32[]{:S(2)}, u32[]{:S(2)}) collective-permute-start(bf16[64,512]{1,0:T(8,128)(2,1)S(1)} %get-tuple-element.76), channel_id=1, source_target_pairs={{16,32},{48,64},{80,96},{112,0},{32,16},{64,48},{96,80},{0,112},{1... | collective-permute-start | bytes 196616 | tf_op jit(solution)/shard_map/ppermute | solution.py:422
  50.6 4.9 %shard_map.81 = (bf16[256,4096]{1,0:T(8,128)(2,1)S(1)}, bf16[64,128]{1,0:T(8,128)(2,1)S(1)}, bf16[64,128]{1,0:T(8,128)(2,1)S(1)}) custom-call(s32[4]{0:T(128)S(1)} %copy-done.2, bf16[256,4096]{1,0:T(8,128)(2,1)S(1)} %shard_map.78.x_ref, s32[1,1024]{1,0:T(1,128)S(1)} %bitcast.15, bf16[4,4,64]{2,1,0:T(4,128)(2,1)S(1)} %bitcast.17, ...), custom_call_target="tpu_custom_call" | custom-call | flops 3221225472 | tf_op jit(solution)/shard_map/pallas_call | solution.py:483
  55.5 0.1 collective-permute-start.20
  55.6 0.9 %collective-permute-start.21 = (bf16[64,128]{1,0:T(8,128)(2,1)S(1)}, bf16[64,128]{1,0:T(8,128)(2,1)S(1)}, u32[]{:S(2)}, u32[]{:S(2)}) collective-permute-start(bf16[64,128]{1,0:T(8,128)(2,1)S(1)} %get-tuple-element.78), channel_id=1, source_target_pairs={{1,2},{3,4},{5,6},{7,8},{9,10},{11,12},{13,14},{15,0},{2,1},{4,3},... | collective-permute-start | bytes 49160 | tf_op jit(solution)/shard_map/ppermute | solution.py:422
  56.5 0.3 collective-permute-done.20.refs_2_
  56.8 4.2 %collective-permute-done.21.refs_3_ = bf16[64,128]{1,0:T(8,128)(2,1)S(1)} collective-permute-done((bf16[64,128]{1,0:T(8,128)(2,1)S(1)}, bf16[64,128]{1,0:T(8,128)(2,1)S(1)}, u32[]{:S(2)}, u32[]{:S(2)}) %collective-permute-start.21) | collective-permute-done | bytes 16416 | tf_op jit(solution)/shard_map/ppermute | solution.py:422
  61.0 0.0 collective-permute-done.18.refs_0_
  61.0 0.0 collective-permute-done.19.refs_1_
  61.0 3.3 %shard_map.82 = bf16[256,4,8,128]{3,2,1,0:T(8,128)(2,1)} custom-call(s32[4]{0:T(128)S(1)} %copy-done.2, bf16[256,4096]{1,0:T(8,128)(2,1)S(1)} %get-tuple-element.74.x_ref, bf16[4,4,64]{2,1,0:T(4,128)(2,1)S(1)} %bitcast.18, bf16[64,512]{1,0:T(8,128)(2,1)S(1)} %collective-permute-done.18.refs_0_, bf16[64,512]{1,0:T(8,128)(2,1)S(1)} %collective-permute-done.19.refs_1_, ...), custom_call_target="tpu_custom_call" | custom-call | tf_op jit(solution)/shard_map/pallas_call | solution.py:501
  (3 shorter events, 0.0 us)
Async XLA Ops:
  1.5 4.0 %collective-permute-start.1 = (f32[32,256]{1,0:T(8,128)S(1)}, f32[32,256]{1,0:T(8,128)S(1)}, u32[]{:S(2)}, u32[]{:S(2)}) collective-permute-start(f32[32,256]{1,0:T(8,128)S(1)} %maximum_multiply_fusion.refs_0_), channel_id=1, source_target_pairs={{0,1},{1,0},{2,3},{3,2},{4,5},{5,4},{6,7},{7,6},{8,9},{9,8},{10,11... | collective-permute-start | bytes 98312 | tf_op jit(solution)/shard_map/ppermute | solution.py:26
  1.5 12.8 %collective-permute-start = (f32[32,256]{1,0:T(8,128)S(1)}, f32[32,256]{1,0:T(8,128)S(1)}, u32[]{:S(2)}, u32[]{:S(2)}) collective-permute-start(f32[32,256]{1,0:T(8,128)S(1)} %maximum_multiply_fusion.refs_0_), channel_id=1, source_target_pairs={{0,4},{1,5},{2,6},{3,7},{4,0},{5,1},{6,2},{7,3},{8,12},{9,13},{10,... | collective-permute-start | bytes 98312 | tf_op jit(solution)/shard_map/ppermute | solution.py:26
  5.5 5.2 %collective-permute-start.2 = (f32[64,256]{1,0:T(8,128)S(1)}, f32[64,256]{1,0:T(8,128)S(1)}, u32[]{:S(2)}, u32[]{:S(2)}) collective-permute-start(f32[64,256]{1,0:T(8,128)S(1)} %pad_maximum_fusion), channel_id=1, source_target_pairs={{0,8},{1,11},{2,10},{3,9},{4,12},{5,15},{6,14},{7,13},{8,0},{9,3},... | collective-permute-start | bytes 196616 | tf_op jit(solution)/shard_map/ppermute | solution.py:26
  7.0 4.3 %collective-permute-start.3 = (f32[64,256]{1,0:T(8,128)S(1)}, f32[64,256]{1,0:T(8,128)S(1)}, u32[]{:S(2)}, u32[]{:S(2)}) collective-permute-start(f32[64,256]{1,0:T(8,128)S(1)} %pad_maximum_fusion), channel_id=1, source_target_pairs={{0,2},{1,15},{2,0},{3,13},{4,6},{5,11},{6,4},{7,9},{8,10},{9,7},{1... | collective-permute-start | bytes 196616 | tf_op jit(solution)/shard_map/ppermute | solution.py:26
  8.1 6.2 %collective-permute-start.4 = (f32[64,256]{1,0:T(8,128)S(1)}, f32[64,256]{1,0:T(8,128)S(1)}, u32[]{:S(2)}, u32[]{:S(2)}) collective-permute-start(f32[64,256]{1,0:T(8,128)S(1)} %pad_maximum_fusion), channel_id=1, source_target_pairs={{0,6},{1,13},{2,4},{3,15},{4,2},{5,9},{6,0},{7,11},{8,14},{9,5},{1... | collective-permute-start | bytes 196616 | tf_op jit(solution)/shard_map/ppermute | solution.py:26
  8.7 6.0 %copy-start = (s32[8,128]{1,0:T(8,128)S(1)}, s32[8,128]{1,0:T(8,128)}, u32[]{:S(2)}) copy-start(s32[8,128]{1,0:T(8,128)} %param.8) | copy-start | bytes 12292
  14.6 1.6 %collective-permute-start.5 = (f32[256,256]{1,0:T(8,128)S(1)}, f32[256,256]{1,0:T(8,128)S(1)}, u32[]{:S(2)}, u32[]{:S(2)}) collective-permute-start(f32[256,256]{1,0:T(8,128)S(1)} %shard_map.74), channel_id=1, source_target_pairs={{0,1},{1,0},{2,3},{3,2},{4,5},{5,4},{6,7},{7,6},{8,9},{9,8},{10,11... | collective-permute-start | bytes 786440 | tf_op jit(solution)/shard_map/ppermute | solution.py:26
  16.3 7.4 %collective-permute-start.6 = (bf16[256,256]{1,0:T(8,128)(2,1)S(1)}, bf16[256,256]{1,0:T(8,128)(2,1)S(1)}, u32[]{:S(2)}, u32[]{:S(2)}) collective-permute-start(bf16[256,256]{1,0:T(8,128)(2,1)S(1)} %add_convert_fusion.refs_0_.refs_4_), channel_id=1, source_target_pairs={{0,24},{1,57},{2,26},{3,59},{4,28},{5,61},{6,30},{7,63},{8,16},{9,... | collective-permute-start | bytes 393224 | tf_op jit(solution)/shard_map/ppermute | solution.py:26
  18.5 6.8 %collective-permute-start.7 = (bf16[256,256]{1,0:T(8,128)(2,1)S(1)}, bf16[256,256]{1,0:T(8,128)(2,1)S(1)}, u32[]{:S(2)}, u32[]{:S(2)}) collective-permute-start(bf16[256,256]{1,0:T(8,128)(2,1)S(1)} %add_convert_fusion.refs_0_.refs_4_), channel_id=1, source_target_pairs={{0,32},{1,121},{2,34},{3,123},{4,36},{5,125},{6,38},{7,127},{8,40}... | collective-permute-start | bytes 393224 | tf_op jit(solution)/shard_map/ppermute | solution.py:26
  20.1 10.4 %collective-permute-start.8 = (bf16[256,256]{1,0:T(8,128)(2,1)S(1)}, bf16[256,256]{1,0:T(8,128)(2,1)S(1)}, u32[]{:S(2)}, u32[]{:S(2)}) collective-permute-start(bf16[256,256]{1,0:T(8,128)(2,1)S(1)} %add_convert_fusion.refs_0_.refs_4_), channel_id=1, source_target_pairs={{0,96},{1,89},{2,98},{3,91},{4,100},{5,93},{6,102},{7,95},{8,104},... | collective-permute-start | bytes 393224 | tf_op jit(solution)/shard_map/ppermute | solution.py:26
  22.3 10.3 %collective-permute-start.12 = (bf16[128,256]{1,0:T(8,128)(2,1)S(1)}, bf16[128,256]{1,0:T(8,128)(2,1)S(1)}, u32[]{:S(2)}, u32[]{:S(2)}) collective-permute-start(bf16[128,256]{1,0:T(8,128)(2,1)S(1)} %constant_dynamic-slice_fusion), channel_id=1, source_target_pairs={{0,64},{1,65},{2,66},{3,67},{4,68},{5,69},{6,70},{7,71},{8,72},{9,... | collective-permute-start | bytes 196616 | tf_op jit(solution)/shard_map/ppermute | solution.py:26
  30.5 3.6 %collective-permute-start.10 = (bf16[256,256]{1,0:T(8,128)(2,1)S(1)}, bf16[256,256]{1,0:T(8,128)(2,1)S(1)}, u32[]{:S(2)}, u32[]{:S(2)}) collective-permute-start(bf16[256,256]{1,0:T(8,128)(2,1)S(1)} %collective-permute-done.7.refs_0_.refs_6_), channel_id=1, source_target_pairs={{0,1},{1,0},{2,3},{3,2},{4,5},{5,4},{6,7},{7,6},{8,9},{9,8},{10,11... | collective-permute-start | bytes 393224 | tf_op jit(solution)/shard_map/ppermute | solution.py:26
  30.5 3.6 %collective-permute-start.11 = (bf16[256,256]{1,0:T(8,128)(2,1)S(1)}, bf16[256,256]{1,0:T(8,128)(2,1)S(1)}, u32[]{:S(2)}, u32[]{:S(2)}) collective-permute-start(bf16[256,256]{1,0:T(8,128)(2,1)S(1)} %collective-permute-done.8.refs_1_.refs_7_), channel_id=1, source_target_pairs={{0,1},{1,0},{2,3},{3,2},{4,5},{5,4},{6,7},{7,6},{8,9},{9,8},{10,11... | collective-permute-start | bytes 393224 | tf_op jit(solution)/shard_map/ppermute | solution.py:26
  31.0 3.1 %collective-permute-start.9 = (bf16[256,256]{1,0:T(8,128)(2,1)S(1)}, bf16[256,256]{1,0:T(8,128)(2,1)S(1)}, u32[]{:S(2)}, u32[]{:S(2)}) collective-permute-start(bf16[256,256]{1,0:T(8,128)(2,1)S(1)} %collective-permute-done.6.refs_1_.refs_5_), channel_id=1, source_target_pairs={{0,1},{1,0},{2,3},{3,2},{4,5},{5,4},{6,7},{7,6},{8,9},{9,8},{10,11... | collective-permute-start | bytes 393224 | tf_op jit(solution)/shard_map/ppermute | solution.py:26
  32.5 1.5 %collective-permute-start.13 = (bf16[128,256]{1,0:T(8,128)(2,1)S(1)}, bf16[128,256]{1,0:T(8,128)(2,1)S(1)}, u32[]{:S(2)}, u32[]{:S(2)}) collective-permute-start(bf16[128,256]{1,0:T(8,128)(2,1)S(1)} %collective-permute-done.12.refs_4_.refs_12_), channel_id=1, source_target_pairs={{0,1},{1,0},{2,3},{3,2},{4,5},{5,4},{6,7},{7,6},{8,9},{9,8},{10,11... | collective-permute-start | bytes 196616 | tf_op jit(solution)/shard_map/ppermute | solution.py:26
  34.7 10.5 %collective-permute-start.14 = (bf16[64,512]{1,0:T(8,128)(2,1)S(1)}, bf16[64,512]{1,0:T(8,128)(2,1)S(1)}, u32[]{:S(2)}, u32[]{:S(2)}) collective-permute-start(bf16[64,512]{1,0:T(8,128)(2,1)S(1)} %get-tuple-element.69), channel_id=1, source_target_pairs={{0,16},{32,48},{64,80},{96,112},{16,0},{48,32},{80,64},{112,96},{1... | collective-permute-start | bytes 196616 | tf_op jit(solution)/shard_map/ppermute | solution.py:422
  35.4 9.8 %collective-permute-start.15 = (bf16[64,512]{1,0:T(8,128)(2,1)S(1)}, bf16[64,512]{1,0:T(8,128)(2,1)S(1)}, u32[]{:S(2)}, u32[]{:S(2)}) collective-permute-start(bf16[64,512]{1,0:T(8,128)(2,1)S(1)} %get-tuple-element.70), channel_id=1, source_target_pairs={{16,32},{48,64},{80,96},{112,0},{32,16},{64,48},{96,80},{0,112},{1... | collective-permute-start | bytes 196616 | tf_op jit(solution)/shard_map/ppermute | solution.py:422
  39.9 3.7 %collective-permute-start.16 = (bf16[64,128]{1,0:T(8,128)(2,1)S(1)}, bf16[64,128]{1,0:T(8,128)(2,1)S(1)}, u32[]{:S(2)}, u32[]{:S(2)}) collective-permute-start(bf16[64,128]{1,0:T(8,128)(2,1)S(1)} %get-tuple-element.71), channel_id=1, source_target_pairs={{0,1},{2,3},{4,5},{6,7},{8,9},{10,11},{12,13},{14,15},{1,0},{3,2},... | collective-permute-start | bytes 49160 | tf_op jit(solution)/shard_map/ppermute | solution.py:422
  39.9 5.3 %collective-permute-start.17 = (bf16[64,128]{1,0:T(8,128)(2,1)S(1)}, bf16[64,128]{1,0:T(8,128)(2,1)S(1)}, u32[]{:S(2)}, u32[]{:S(2)}) collective-permute-start(bf16[64,128]{1,0:T(8,128)(2,1)S(1)} %get-tuple-element.72), channel_id=1, source_target_pairs={{1,2},{3,4},{5,6},{7,8},{9,10},{11,12},{13,14},{15,0},{2,1},{4,3},... | collective-permute-start | bytes 49160 | tf_op jit(solution)/shard_map/ppermute | solution.py:422
  41.0 4.1 %copy-start.1 = (bf16[4,64,4]{1,2,0:T(4,128)(2,1)S(1)}, bf16[4,64,4]{1,2,0:T(4,128)(2,1)}, u32[]{:S(2)}) copy-start(bf16[4,64,4]{1,2,0:T(4,128)(2,1)} %param.10) | copy-start | bytes 6148
  41.0 4.1 %copy-start.2 = (s32[4]{0:T(128)S(1)}, s32[4]{0:T(128)}, u32[]{:S(2)}) copy-start(s32[4]{0:T(128)} %port_ref.5) | copy-start | bytes 52
  47.5 13.5 %collective-permute-start.18 = (bf16[64,512]{1,0:T(8,128)(2,1)S(1)}, bf16[64,512]{1,0:T(8,128)(2,1)S(1)}, u32[]{:S(2)}, u32[]{:S(2)}) collective-permute-start(bf16[64,512]{1,0:T(8,128)(2,1)S(1)} %get-tuple-element.75), channel_id=1, source_target_pairs={{0,16},{32,48},{64,80},{96,112},{16,0},{48,32},{80,64},{112,96},{1... | collective-permute-start | bytes 196616 | tf_op jit(solution)/shard_map/ppermute | solution.py:422
  47.6 13.4 %collective-permute-start.19 = (bf16[64,512]{1,0:T(8,128)(2,1)S(1)}, bf16[64,512]{1,0:T(8,128)(2,1)S(1)}, u32[]{:S(2)}, u32[]{:S(2)}) collective-permute-start(bf16[64,512]{1,0:T(8,128)(2,1)S(1)} %get-tuple-element.76), channel_id=1, source_target_pairs={{16,32},{48,64},{80,96},{112,0},{32,16},{64,48},{96,80},{0,112},{1... | collective-permute-start | bytes 196616 | tf_op jit(solution)/shard_map/ppermute | solution.py:422
  55.5 1.3 %collective-permute-start.20 = (bf16[64,128]{1,0:T(8,128)(2,1)S(1)}, bf16[64,128]{1,0:T(8,128)(2,1)S(1)}, u32[]{:S(2)}, u32[]{:S(2)}) collective-permute-start(bf16[64,128]{1,0:T(8,128)(2,1)S(1)} %get-tuple-element.77), channel_id=1, source_target_pairs={{0,1},{2,3},{4,5},{6,7},{8,9},{10,11},{12,13},{14,15},{1,0},{3,2},... | collective-permute-start | bytes 49160 | tf_op jit(solution)/shard_map/ppermute | solution.py:422
  55.6 5.4 %collective-permute-start.21 = (bf16[64,128]{1,0:T(8,128)(2,1)S(1)}, bf16[64,128]{1,0:T(8,128)(2,1)S(1)}, u32[]{:S(2)}, u32[]{:S(2)}) collective-permute-start(bf16[64,128]{1,0:T(8,128)(2,1)S(1)} %get-tuple-element.78), channel_id=1, source_target_pairs={{1,2},{3,4},{5,6},{7,8},{9,10},{11,12},{13,14},{15,0},{2,1},{4,3},... | collective-permute-start | bytes 49160 | tf_op jit(solution)/shard_map/ppermute | solution.py:422

commit v16 on v15

--- a/solution.py
+++ b/solution.py
@@ -325,40 +325,38 @@
 
 
 def ends_kernel(rows, ports, width, port_ref, x_ref, types_ref, profile_ref, *refs):
-    halo_refs, map_refs, ends_ref = refs[:4], refs[4:-3], refs[-3]
-    quarter = x_ref.shape[0] // 4
-    places = [(port, row) for row in (0, rows - 1) for port in range(ports)]
-    block = patched(rows, width, x_ref, port_ref, profile_ref, halo_refs, places)
-    types = types_of_rows(types_ref, [row for _, row in places]).astype(BF)
-    total = products(block, types, with_steps(map_refs, 0, len(MAP_STEPS)), 0, x_ref.shape[0])
-    ends_ref[...] = total.astype(BF)
-    wide = ports * LANES
-    store_rims(refs[-2:], "row", total[0:quarter, :wide], total[quarter : 2 * quarter, wide:])
-
-
-def second_kernel(rows, ports, width, port_ref, x_ref, types_ref, profile_ref, ends_ref, *refs):
-    halo_refs, map_refs, next_ref = refs[:4], refs[4:-3], refs[-3]
+    halo_refs, map_refs, patched_ref, ends_ref = refs[:4], refs[4:-6], refs[-6], refs[-5]
     order, tile = x_ref.shape[0], rows * width
     quarter = order // 4
     maps = with_steps(map_refs, 0, len(MAP_STEPS))
+    for port in range(ports):
+        places = [(port, row) for row in range(rows)]
+        value = patched(rows, width, x_ref, port_ref, profile_ref, halo_refs, places)
+        patched_ref[:, port * tile : (port + 1) * tile] = value
+    starts = [port * tile + row * width for row in (0, rows - 1) for port in range(ports)]
+    block = jnp.concatenate([patched_ref[:, start : start + width] for start in starts], axis=1)
+    types = types_of_rows(types_ref, [0] * ports + [rows - 1] * ports).astype(BF)
+    total = products(block, types, maps, 0, order)
+    ends_ref[...] = total.astype(BF)
+    wide = ports * LANES
+    store_rims(refs[-4:-2], "row", total[0:quarter, :wide], total[quarter : 2 * quarter, wide:])
+    sides, kinds = side_columns(patched_ref, types_ref[...].astype(F32), ports)
+    sides = products(sides, kinds[0:1], maps, 2 * quarter, order)
+    store_rims(refs[-2:], "col", sides[0:quarter], sides[quarter:])
+
+
+def second_kernel(rows, ports, width, x_ref, types_ref, ends_ref, *refs):
+    map_refs, next_ref = refs[:-1], refs[-1]
+    order, tile = x_ref.shape[0], rows * width
+    maps = with_steps(map_refs, 0, len(MAP_STEPS))
     types = types_of_rows(types_ref, range(1, rows - 1)).astype(BF)
-    lane = lax.broadcasted_iota(jnp.int32, (quarter, LANES), 1)
-    west_rim = east_rim = jnp.zeros((quarter, LANES), F32)
     for port in range(ports):
-        places = [(port, row) for row in range(1, rows - 1)]
-        block = patched(rows, width, x_ref, port_ref, profile_ref, halo_refs, places)
-        middle = products(block, types, maps, 0, order)
+        start = port * tile
+        middle = products(x_ref[:, start + width : start + tile - width], types, maps, 0, order)
         top = ends_ref[:, port * LANES : (port + 1) * LANES].astype(F32)
         bottom = ends_ref[:, (ports + port) * LANES : (ports + port + 1) * LANES].astype(F32)
         total = jnp.concatenate([top, middle, bottom], axis=1)
-        shifted(total, next_ref.at[:, port * tile : (port + 1) * tile], rows)
-        for row in range(rows):
-            place = port * rows + row
-            west = lane_of(total[2 * quarter : 3 * quarter], row * LANES)
-            east = lane_of(total[3 * quarter :], (row + 1) * LANES - 1)
-            west_rim = jnp.where(lane == place, west, west_rim)
-            east_rim = jnp.where(lane == place, east, east_rim)
-    store_rims(refs[-2:], "col", west_rim, east_rim)
+        shifted(total, next_ref.at[:, start : start + tile], rows)
 
 
 def last_kernel(rows, width, port_ref, x_ref, profile_ref, *refs):
@@ -382,7 +380,7 @@
                 parts[-1] = south_in[:, rim]
             elif edge == 2:
                 parts = [
-                    jnp.where(lane == 0, lane_of(west_in, place), part)
+                    jnp.where(lane == 0, lane_of(west_in, 64 + place), part)
                     for place, part in zip(places, parts)
                 ]
             else:
@@ -414,12 +412,23 @@
 
 
 def exchange(rims, axis):
+    sizes = lax.axis_size("row"), lax.axis_size("col")
+    at = ("row", "col").index(axis)
+
+    def partner(place, first):
+        place = list(place)
+        other = place[at] + (1 if place[at] % 2 == first else -1)
+        if 0 <= other < sizes[at]:
+            place[at] = other
+        else:
+            place[1 - at] ^= 2
+        return place[0] * sizes[1] + place[1]
+
     def pairs(first):
-        count = lax.axis_size(axis)
-        near = [(i, (i + 1) % count) for i in range(first, count, 2)]
-        return near + [(target, source) for source, target in near]
-
-    return [lax.ppermute(rim, axis, pairs(first)) for first, rim in enumerate(rims)]
+        places = [(row, col) for row in range(sizes[0]) for col in range(sizes[1])]
+        return [(row * sizes[1] + col, partner((row, col), first)) for row, col in places]
+
+    return [lax.ppermute(rim, ("row", "col"), pairs(first)) for first, rim in enumerate(rims)]
 
 
 def body(traces, cell_type, port_cell, port_profile, mode_shapes, mode_values, mode_weights):
@@ -479,25 +488,27 @@
         *late,
         flops=work // 2,
     )
-    def sweep(kernel, shapes, operands, share):
-        return pl.pallas_call(
-            functools.partial(kernel, rows, ports, width),
-            in_specs=[ports_spec] + [WHOLE] * (len(operands) - 1),
-            out_specs=[WHOLE] * len(shapes),
-            out_shape=shapes,
-            compiler_params=PARAMS,
-            cost_estimate=pl.CostEstimate(
-                flops=work * share // rows, bytes_accessed=0, transcendentals=0
-            ),
-        )(*operands)
-
     ends_shape = jax.ShapeDtypeStruct((order, 2 * ports * LANES), BF)
-    operands = [port_cell, x, types, profile]
-    ends, *sent = sweep(ends_kernel, [ends_shape] + rim_shapes[:2], operands + halos + maps, 2)
-    row_halos = exchange(sent, "row")
-    operands = operands + [ends] + halos + maps
-    x, *sent = sweep(second_kernel, [next_shape] + rim_shapes[2:], operands, rows - 2)
-    operands = [port_cell, x, profile, *row_halos, *exchange(sent, "col")]
+    operands = [port_cell, x, types, profile, *halos, *maps]
+    x, ends, *sent = pl.pallas_call(
+        functools.partial(ends_kernel, rows, ports, width),
+        in_specs=[ports_spec] + [WHOLE] * (len(operands) - 1),
+        out_specs=[WHOLE] * 6,
+        out_shape=[next_shape, ends_shape] + rim_shapes,
+        compiler_params=PARAMS,
+        cost_estimate=pl.CostEstimate(flops=work // 3, bytes_accessed=0, transcendentals=0),
+    )(*operands)
+    halos = exchange(sent[:2], "row") + exchange(sent[2:], "col")
+    (x,) = whole_call(
+        functools.partial(second_kernel, rows, ports, width),
+        [next_shape],
+        x,
+        types,
+        ends,
+        *maps,
+        flops=work * (rows - 2) // rows,
+    )
+    operands = [port_cell, x, profile, *halos]
     out = pl.pallas_call(
         functools.partial(last_kernel, rows, width),
         in_specs=[ports_spec] + [WHOLE] * (len(operands) - 1),

time: 64.7 us -> 58.5 us (0.904)
  waiting for transfers between devices: 16.7 us -> 10.7 us
    ppermute x8, waiting for transfers between devices: 6.07 us -> 0.02 us  [exchange(): lax.ppermute(rim, ('row', 'col'), pairs(first))]
    pallas_call x2 -> x1, Pallas kernels: 7.19 us -> 3.26 us  [body(): pl.pallas_call(functools.partial(ends_kernel, rows, ports, width), in_spe...]
    pallas_call x6 -> x7, Pallas kernels: 7.77 us -> 11.3 us  [whole_call(): pl.pallas_call(kernel, in_specs=[WHOLE] * len(operands), out_specs=[WHOLE...]
  transfers between devices with their start and end apart: 22 -> 22, of which waited for: 9 -> 6; matrix products, arithmetic and copies ran while one was open for 0% -> 0% of each run, Pallas kernels for 21% -> 21%
where the time goes in v16:
time: 58.5 us; the launch traced here: 57.8 us
  starting transfers between devices  25.3 us (43%)
  Pallas kernels  19.9 us (34%)
  waiting for transfers between devices  10.7 us (18%)
  other arithmetic  0.85 us (1%)
  local copies, waits for them, and re-layouts  0.67 us (1%)
    ppermute x14, starting transfers between devices, swap(): return lax.ppermute(value, ('row', 'col'), pairs)  15.2 us
    pallas_call x7, Pallas kernels, whole_call(): pl.pallas_call(kernel, in_specs=[WHOLE] * len(operands), out_specs=[WHOLE...  11.3 us
    ppermute x14, waiting for transfers between devices, swap(): return lax.ppermute(value, ('row', 'col'), pairs)  10.7 us
    ppermute x8, starting transfers between devices, exchange(): lax.ppermute(rim, ('row', 'col'), pairs(first))  10.1 us
    pallas_call x1, Pallas kernels, body(): pl.pallas_call(functools.partial(last_kernel, rows, width), in_specs=[por...  3.32 us
    pallas_call x1, Pallas kernels, body(): pl.pallas_call(functools.partial(ends_kernel, rows, ports, width), in_spe...  3.26 us
    pallas_call x1, Pallas kernels, own_type_map(): pl.pallas_call(flat_kernel, in_specs=[pl.BlockSpec(memory_space=pltpu.HBM...  1.98 us
  transfers between devices with their start and end apart: 22, of which 6 were waited for; matrix products, arithmetic and copies ran while one was open for 0% of the time, Pallas kernels for 21%

profile of v16, /device:TPU:0, one launch (start us, length us, event | category | flops | bytes accessed | tf_op | source)
XLA Modules:
  0.0 57.8 jit_solution(16151767194811376411)
XLA Ops:
  0.0 0.7 %concatenate.10 = f32[32]{0:T(128)S(1)} pad(f32[16]{0:T(128)} %bitcast.21, f32[]{:T(128)} %constant.6.clone.1), padding=0_16 | pad | bytes 196 | tf_op jit(solution)/shard_map/concatenate | solution.py:82
  0.7 0.8 %maximum_multiply_fusion.refs_0_ = f32[32,256]{1,0:T(8,128)S(1)} fusion(f32[16,256]{1,0:T(8,128)} %bitcast.19, f32[16,256]{1,0:T(8,128)} %bitcast.20, f32[32]{0:T(128)S(1)} %concatenate.10), kind=kLoop, calls=%fused_computation.2 | loop fusion | flops 16384 | bytes 65664 | tf_op jit(solution)/shard_map/mul | solution.py:82
  1.5 0.0 collective-permute-start.1
  1.5 4.0 %collective-permute-start = (f32[32,256]{1,0:T(8,128)S(1)}, f32[32,256]{1,0:T(8,128)S(1)}, u32[]{:S(2)}, u32[]{:S(2)}) collective-permute-start(f32[32,256]{1,0:T(8,128)S(1)} %maximum_multiply_fusion.refs_0_), channel_id=1, source_target_pairs={{0,4},{1,5},{2,6},{3,7},{4,0},{5,1},{6,2},{7,3},{8,12},{9,13},{10,... | collective-permute-start | bytes 98312 | tf_op jit(solution)/shard_map/ppermute | solution.py:26
  5.5 0.0 collective-permute-done.1
  5.5 1.6 %collective-permute-start.2 = (f32[64,256]{1,0:T(8,128)S(1)}, f32[64,256]{1,0:T(8,128)S(1)}, u32[]{:S(2)}, u32[]{:S(2)}) collective-permute-start(f32[64,256]{1,0:T(8,128)S(1)} %pad_maximum_fusion), channel_id=1, source_target_pairs={{0,8},{1,11},{2,10},{3,9},{4,12},{5,15},{6,14},{7,13},{8,0},{9,3},... | collective-permute-start | bytes 196616 | tf_op jit(solution)/shard_map/ppermute | solution.py:26
  7.0 1.0 %collective-permute-start.3 = (f32[64,256]{1,0:T(8,128)S(1)}, f32[64,256]{1,0:T(8,128)S(1)}, u32[]{:S(2)}, u32[]{:S(2)}) collective-permute-start(f32[64,256]{1,0:T(8,128)S(1)} %pad_maximum_fusion), channel_id=1, source_target_pairs={{0,2},{1,15},{2,0},{3,13},{4,6},{5,11},{6,4},{7,9},{8,10},{9,7},{1... | collective-permute-start | bytes 196616 | tf_op jit(solution)/shard_map/ppermute | solution.py:26
  8.1 0.6 %collective-permute-start.4 = (f32[64,256]{1,0:T(8,128)S(1)}, f32[64,256]{1,0:T(8,128)S(1)}, u32[]{:S(2)}, u32[]{:S(2)}) collective-permute-start(f32[64,256]{1,0:T(8,128)S(1)} %pad_maximum_fusion), channel_id=1, source_target_pairs={{0,6},{1,13},{2,4},{3,15},{4,2},{5,9},{6,0},{7,11},{8,14},{9,5},{1... | collective-permute-start | bytes 196616 | tf_op jit(solution)/shard_map/ppermute | solution.py:26
  8.7 0.0 copy-start
  8.7 2.0 %shard_map.73.x_ref = bf16[256,4096]{1,0:T(8,128)(2,1)S(1)} custom-call(bf16[256,4,8,128]{3,2,1,0:T(8,128)(2,1)} %bitcast.18), custom_call_target="tpu_custom_call" | custom-call | flops 1073741824 | tf_op jit(solution)/shard_map/pallas_call | solution.py:89
  10.7 0.0 collective-permute-done.2.refs_2_
  10.7 0.6 %collective-permute-done.3.refs_3_ = f32[64,256]{1,0:T(8,128)S(1)} collective-permute-done((f32[64,256]{1,0:T(8,128)S(1)}, f32[64,256]{1,0:T(8,128)S(1)}, u32[]{:S(2)}, u32[]{:S(2)}) %collective-permute-start.3) | collective-permute-done | bytes 65568 | tf_op jit(solution)/shard_map/ppermute | solution.py:26
  11.3 2.9 %collective-permute-done.4.refs_4_ = f32[64,256]{1,0:T(8,128)S(1)} collective-permute-done((f32[64,256]{1,0:T(8,128)S(1)}, f32[64,256]{1,0:T(8,128)S(1)}, u32[]{:S(2)}, u32[]{:S(2)}) %collective-permute-start.4) | collective-permute-done | bytes 65568 | tf_op jit(solution)/shard_map/ppermute | solution.py:26
  14.2 0.0 collective-permute-done.refs_1_
  14.2 0.4 shard_map.74
  14.6 0.1 collective-permute-start.5
  14.7 0.0 copy-done
  14.7 1.2 %shard_map.75 = (bf16[256,128]{1,0:T(8,128)(2,1)S(1)}, bf16[16,128]{1,0:T(8,128)(2,1)S(1)}) custom-call(bf16[256,4096]{1,0:T(8,128)(2,1)S(1)} %shard_map.73.x_ref, s32[1,1024]{1,0:T(1,128)S(1)} %bitcast.9), custom_call_target="tpu_custom_call" | custom-call | flops 1073741824 | tf_op jit(solution)/shard_map/pallas_call | solution.py:69
  15.9 0.3 collective-permute-done.5
  16.3 2.2 %collective-permute-start.6 = (bf16[256,256]{1,0:T(8,128)(2,1)S(1)}, bf16[256,256]{1,0:T(8,128)(2,1)S(1)}, u32[]{:S(2)}, u32[]{:S(2)}) collective-permute-start(bf16[256,256]{1,0:T(8,128)(2,1)S(1)} %add_convert_fusion.refs_0_.refs_4_), channel_id=1, source_target_pairs={{0,24},{1,57},{2,26},{3,59},{4,28},{5,61},{6,30},{7,63},{8,16},{9,... | collective-permute-start | bytes 393224 | tf_op jit(solution)/shard_map/ppermute | solution.py:26
  18.5 1.6 %collective-permute-start.7 = (bf16[256,256]{1,0:T(8,128)(2,1)S(1)}, bf16[256,256]{1,0:T(8,128)(2,1)S(1)}, u32[]{:S(2)}, u32[]{:S(2)}) collective-permute-start(bf16[256,256]{1,0:T(8,128)(2,1)S(1)} %add_convert_fusion.refs_0_.refs_4_), channel_id=1, source_target_pairs={{0,32},{1,121},{2,34},{3,123},{4,36},{5,125},{6,38},{7,127},{8,40}... | collective-permute-start | bytes 393224 | tf_op jit(solution)/shard_map/ppermute | solution.py:26
  20.1 2.2 %collective-permute-start.8 = (bf16[256,256]{1,0:T(8,128)(2,1)S(1)}, bf16[256,256]{1,0:T(8,128)(2,1)S(1)}, u32[]{:S(2)}, u32[]{:S(2)}) collective-permute-start(bf16[256,256]{1,0:T(8,128)(2,1)S(1)} %add_convert_fusion.refs_0_.refs_4_), channel_id=1, source_target_pairs={{0,96},{1,89},{2,98},{3,91},{4,100},{5,93},{6,102},{7,95},{8,104},... | collective-permute-start | bytes 393224 | tf_op jit(solution)/shard_map/ppermute | solution.py:26
  22.3 0.8 %collective-permute-start.12 = (bf16[128,256]{1,0:T(8,128)(2,1)S(1)}, bf16[128,256]{1,0:T(8,128)(2,1)S(1)}, u32[]{:S(2)}, u32[]{:S(2)}) collective-permute-start(bf16[128,256]{1,0:T(8,128)(2,1)S(1)} %constant_dynamic-slice_fusion), channel_id=1, source_target_pairs={{0,64},{1,65},{2,66},{3,67},{4,68},{5,69},{6,70},{7,71},{8,72},{9,... | collective-permute-start | bytes 196616 | tf_op jit(solution)/shard_map/ppermute | solution.py:26
  23.1 0.7 %collective-permute-done.6.refs_1_.refs_5_ = bf16[256,256]{1,0:T(8,128)(2,1)S(1)} collective-permute-done((bf16[256,256]{1,0:T(8,128)(2,1)S(1)}, bf16[256,256]{1,0:T(8,128)(2,1)S(1)}, u32[]{:S(2)}, u32[]{:S(2)}) %collective-permute-start.6) | collective-permute-done | bytes 131104 | tf_op jit(solution)/shard_map/ppermute | solution.py:26
  23.7 1.5 %shard_map.76 = (bf16[256,4096]{1,0:T(8,128)(2,1)S(1)}, bf16[64,512]{1,0:T(8,128)(2,1)S(1)}, bf16[64,512]{1,0:T(8,128)(2,1)S(1)}, bf16[128,128]{1,0:T(8,128)(2,1)S(1)}) custom-call(bf16[256,4096]{1,0:T(8,128)(2,1)S(1)} %shard_map.73.x_ref, s32[1,1024]{1,0:T(1,128)S(1)} %bitcast.10, bf16[256,128]{1,0:T(8,128)(2,1)S(1)} %get-tuple-element.52.sides_ref, ...), custom_call_target="tpu_custom_call" | custom-call | flops 1227133568 | tf_op jit(solution)/shard_map/pallas_call | solution.py:69
  25.3 0.0 collective-permute-done.7.refs_0_.refs_6_.refs_2_
  25.3 5.2 %collective-permute-done.8.refs_1_.refs_7_.refs_3_ = bf16[256,256]{1,0:T(8,128)(2,1)S(1)} collective-permute-done((bf16[256,256]{1,0:T(8,128)(2,1)S(1)}, bf16[256,256]{1,0:T(8,128)(2,1)S(1)}, u32[]{:S(2)}, u32[]{:S(2)}) %collective-permute-start.8) | collective-permute-done | bytes 131104 | tf_op jit(solution)/shard_map/ppermute | solution.py:26
  30.5 0.0 collective-permute-start.10
  30.5 0.5 collective-permute-start.11
  31.0 0.0 collective-permute-start.9
  31.0 1.5 %shard_map.77 = (bf16[256,4096]{1,0:T(8,128)(2,1)S(1)}, bf16[64,512]{1,0:T(8,128)(2,1)S(1)}, bf16[64,512]{1,0:T(8,128)(2,1)S(1)}, bf16[128,128]{1,0:T(8,128)(2,1)S(1)}) custom-call(bf16[256,4096]{1,0:T(8,128)(2,1)S(1)} %shard_map.73.x_ref, s32[1,1024]{1,0:T(1,128)S(1)} %bitcast.11, bf16[256,128]{1,0:T(8,128)(2,1)S(1)} %get-tuple-element.52.sides_ref, ...), custom_call_target="tpu_custom_call" | custom-call | flops 1227133568 | tf_op jit(solution)/shard_map/pallas_call | solution.py:69
  32.5 0.0 collective-permute-done.12.refs_4_.refs_12_.refs_8_
  32.5 0.6 %collective-permute-start.13 = (bf16[128,256]{1,0:T(8,128)(2,1)S(1)}, bf16[128,256]{1,0:T(8,128)(2,1)S(1)}, u32[]{:S(2)}, u32[]{:S(2)}) collective-permute-start(bf16[128,256]{1,0:T(8,128)(2,1)S(1)} %collective-permute-done.12.refs_4_.refs_12_.refs_8_), channel_id=1, source_target_pairs={{0,1},{1,0},{2,3},{3,2},{4,5},{5,4},{6,7},{7,6},{8,9},{9,8},{10,11... | collective-permute-start | bytes 196616 | tf_op jit(solution)/shard_map/ppermute | solution.py:26
  33.1 0.9 %collective-permute-done.13.refs_3_.refs_11_.refs_7_ = bf16[128,256]{1,0:T(8,128)(2,1)S(1)} collective-permute-done((bf16[128,256]{1,0:T(8,128)(2,1)S(1)}, bf16[128,256]{1,0:T(8,128)(2,1)S(1)}, u32[]{:S(2)}, u32[]{:S(2)}) %collective-permute-start.13) | collective-permute-done | bytes 65568 | tf_op jit(solution)/shard_map/ppermute | solution.py:26
  34.0 0.0 collective-permute-done.10.refs_1_.refs_9_.refs_5_
  34.0 0.0 collective-permute-done.11.refs_2_.refs_10_.refs_6_
  34.0 0.0 collective-permute-done.9.refs_0_.refs_8_.refs_4_
  34.0 0.6 %shard_map.79 = (bf16[64,512]{1,0:T(8,128)(2,1)S(1)}, bf16[64,512]{1,0:T(8,128)(2,1)S(1)}, bf16[64,128]{1,0:T(8,128)(2,1)S(1)}, bf16[64,128]{1,0:T(8,128)(2,1)S(1)}) custom-call(bf16[256,4096]{1,0:T(8,128)(2,1)S(1)} %shard_map.73.x_ref, s32[1,1024]{1,0:T(1,128)S(1)} %bitcast.12, bf16[256,128]{1,0:T(8,128)(2,1)S(1)} %get-tuple-element.52.sides_ref, ...), custom_call_target="tpu_custom_call" | custom-call | flops 536870912 | tf_op jit(solution)/shard_map/pallas_call | solution.py:69
  34.7 0.7 %collective-permute-start.14 = (bf16[64,512]{1,0:T(8,128)(2,1)S(1)}, bf16[64,512]{1,0:T(8,128)(2,1)S(1)}, u32[]{:S(2)}, u32[]{:S(2)}) collective-permute-start(bf16[64,512]{1,0:T(8,128)(2,1)S(1)} %get-tuple-element.69), channel_id=1, source_target_pairs={{0,16},{1,17},{2,18},{3,19},{4,20},{5,21},{6,22},{7,23},{8,24},{9,... | collective-permute-start | bytes 196616 | tf_op jit(solution)/shard_map/ppermute | solution.py:431
  35.4 0.0 collective-permute-start.15
  35.4 0.0 collective-permute-start.16
  35.4 4.3 %collective-permute-start.17 = (bf16[64,128]{1,0:T(8,128)(2,1)S(1)}, bf16[64,128]{1,0:T(8,128)(2,1)S(1)}, u32[]{:S(2)}, u32[]{:S(2)}) collective-permute-start(bf16[64,128]{1,0:T(8,128)(2,1)S(1)} %get-tuple-element.72), channel_id=1, source_target_pairs={{0,32},{1,2},{2,1},{3,4},{4,3},{5,6},{6,5},{7,8},{8,7},{9,10},{10,... | collective-permute-start | bytes 49160 | tf_op jit(solution)/shard_map/ppermute | solution.py:431
  39.7 0.0 copy-start.1
  39.7 0.0 copy-start.2
  39.7 2.5 %shard_map.78.x_ref = bf16[256,4096]{1,0:T(8,128)(2,1)S(1)} custom-call(bf16[256,4096]{1,0:T(8,128)(2,1)S(1)} %shard_map.73.x_ref, s32[1,1024]{1,0:T(1,128)S(1)} %bitcast.13, bf16[256,4096]{1,0:T(8,128)(2,1)S(1)} %get-tuple-element.62.done_ref, bf16[256,256]{1,0:T(8,128)(2,1)S(1)} %collective-permute-done.9.refs_0_.refs_8_.refs_4_, ...), custom_call_target="tpu_custom_call" | custom-call | flops 2147483648 | tf_op jit(solution)/shard_map/pallas_call | solution.py:69
  42.3 0.0 collective-permute-done.16.refs_2_
  42.3 0.0 collective-permute-done.17.refs_3_
  42.3 0.0 collective-permute-done.14.refs_0_
  42.3 0.0 collective-permute-done.15.refs_1_
  42.3 0.0 copy-done.1
  42.3 0.0 copy-done.2
  42.3 3.3 %shard_map.80 = (bf16[256,4096]{1,0:T(8,128)(2,1)S(1)}, bf16[256,1024]{1,0:T(8,128)(2,1)S(1)}, bf16[64,512]{1,0:T(8,128)(2,1)S(1)}, bf16[64,512]{1,0:T(8,128)(2,...) custom-call(s32[4]{0:T(128)S(1)} %copy-done.2, bf16[256,4096]{1,0:T(8,128)(2,1)S(1)} %shard_map.78.x_ref, ...), custom_call_target="tpu_custom_call" | custom-call | flops 1431655808 | tf_op jit(solution)/shard_map/pallas_call | solution.py:493
  45.6 2.7 %collective-permute-start.18 = (bf16[64,512]{1,0:T(8,128)(2,1)S(1)}, bf16[64,512]{1,0:T(8,128)(2,1)S(1)}, u32[]{:S(2)}, u32[]{:S(2)}) collective-permute-start(bf16[64,512]{1,0:T(8,128)(2,1)S(1)} %get-tuple-element.75), channel_id=1, source_target_pairs={{0,16},{1,17},{2,18},{3,19},{4,20},{5,21},{6,22},{7,23},{8,24},{9,... | collective-permute-start | bytes 196616 | tf_op jit(solution)/shard_map/ppermute | solution.py:431
  48.3 0.3 collective-permute-start.19
  48.6 0.0 collective-permute-start.20
  48.6 2.1 %collective-permute-start.21 = (bf16[64,128]{1,0:T(8,128)(2,1)S(1)}, bf16[64,128]{1,0:T(8,128)(2,1)S(1)}, u32[]{:S(2)}, u32[]{:S(2)}) collective-permute-start(bf16[64,128]{1,0:T(8,128)(2,1)S(1)} %get-tuple-element.78), channel_id=1, source_target_pairs={{0,32},{1,2},{2,1},{3,4},{4,3},{5,6},{6,5},{7,8},{8,7},{9,10},{10,... | collective-permute-start | bytes 49160 | tf_op jit(solution)/shard_map/ppermute | solution.py:431
  50.7 3.6 %shard_map.81.x_ref = bf16[256,4096]{1,0:T(8,128)(2,1)S(1)} custom-call(bf16[256,4096]{1,0:T(8,128)(2,1)S(1)} %get-tuple-element.73.x_ref, s32[1,1024]{1,0:T(1,128)S(1)} %bitcast.15, bf16[256,1024]{1,0:T(8,128)(2,1)S(1)} %get-tuple-element.74.ends_ref, bf16[256,256]{1,0:T(8,128)(2,1)S(1)} %add_convert_fusion.refs_0_.refs_4_, ...), custom_call_target="tpu_custom_call" | custom-call | flops 3221225472 | tf_op jit(solution)/shard_map/pallas_call | solution.py:69
  54.2 0.0 collective-permute-done.20.refs_2_
  54.3 0.0 collective-permute-done.21.refs_3_
  54.3 0.0 collective-permute-done.18.refs_0_
  54.3 0.0 collective-permute-done.19.refs_1_
  54.3 3.3 %shard_map.82 = bf16[256,4,8,128]{3,2,1,0:T(8,128)(2,1)} custom-call(s32[4]{0:T(128)S(1)} %copy-done.2, bf16[256,4096]{1,0:T(8,128)(2,1)S(1)} %shard_map.81.x_ref, bf16[4,4,64]{2,1,0:T(4,128)(2,1)S(1)} %bitcast.17, bf16[64,512]{1,0:T(8,128)(2,1)S(1)} %collective-permute-done.18.refs_0_, bf16[64,512]{1,0:T(8,128)(2,1)S(1)} %collective-permute-done.19.refs_1_, ...), custom_call_target="tpu_custom_call" | custom-call | tf_op jit(solution)/shard_map/pallas_call | solution.py:512
  (3 shorter events, 0.0 us)
Async XLA Ops:
  1.5 4.0 %collective-permute-start.1 = (f32[32,256]{1,0:T(8,128)S(1)}, f32[32,256]{1,0:T(8,128)S(1)}, u32[]{:S(2)}, u32[]{:S(2)}) collective-permute-start(f32[32,256]{1,0:T(8,128)S(1)} %maximum_multiply_fusion.refs_0_), channel_id=1, source_target_pairs={{0,1},{1,0},{2,3},{3,2},{4,5},{5,4},{6,7},{7,6},{8,9},{9,8},{10,11... | collective-permute-start | bytes 98312 | tf_op jit(solution)/shard_map/ppermute | solution.py:26
  1.5 12.8 %collective-permute-start = (f32[32,256]{1,0:T(8,128)S(1)}, f32[32,256]{1,0:T(8,128)S(1)}, u32[]{:S(2)}, u32[]{:S(2)}) collective-permute-start(f32[32,256]{1,0:T(8,128)S(1)} %maximum_multiply_fusion.refs_0_), channel_id=1, source_target_pairs={{0,4},{1,5},{2,6},{3,7},{4,0},{5,1},{6,2},{7,3},{8,12},{9,13},{10,... | collective-permute-start | bytes 98312 | tf_op jit(solution)/shard_map/ppermute | solution.py:26
  5.5 5.2 %collective-permute-start.2 = (f32[64,256]{1,0:T(8,128)S(1)}, f32[64,256]{1,0:T(8,128)S(1)}, u32[]{:S(2)}, u32[]{:S(2)}) collective-permute-start(f32[64,256]{1,0:T(8,128)S(1)} %pad_maximum_fusion), channel_id=1, source_target_pairs={{0,8},{1,11},{2,10},{3,9},{4,12},{5,15},{6,14},{7,13},{8,0},{9,3},... | collective-permute-start | bytes 196616 | tf_op jit(solution)/shard_map/ppermute | solution.py:26
  7.0 4.3 %collective-permute-start.3 = (f32[64,256]{1,0:T(8,128)S(1)}, f32[64,256]{1,0:T(8,128)S(1)}, u32[]{:S(2)}, u32[]{:S(2)}) collective-permute-start(f32[64,256]{1,0:T(8,128)S(1)} %pad_maximum_fusion), channel_id=1, source_target_pairs={{0,2},{1,15},{2,0},{3,13},{4,6},{5,11},{6,4},{7,9},{8,10},{9,7},{1... | collective-permute-start | bytes 196616 | tf_op jit(solution)/shard_map/ppermute | solution.py:26
  8.1 6.2 %collective-permute-start.4 = (f32[64,256]{1,0:T(8,128)S(1)}, f32[64,256]{1,0:T(8,128)S(1)}, u32[]{:S(2)}, u32[]{:S(2)}) collective-permute-start(f32[64,256]{1,0:T(8,128)S(1)} %pad_maximum_fusion), channel_id=1, source_target_pairs={{0,6},{1,13},{2,4},{3,15},{4,2},{5,9},{6,0},{7,11},{8,14},{9,5},{1... | collective-permute-start | bytes 196616 | tf_op jit(solution)/shard_map/ppermute | solution.py:26
  8.7 6.0 %copy-start = (s32[8,128]{1,0:T(8,128)S(1)}, s32[8,128]{1,0:T(8,128)}, u32[]{:S(2)}) copy-start(s32[8,128]{1,0:T(8,128)} %param.8) | copy-start | bytes 12292
  14.6 1.6 %collective-permute-start.5 = (f32[256,256]{1,0:T(8,128)S(1)}, f32[256,256]{1,0:T(8,128)S(1)}, u32[]{:S(2)}, u32[]{:S(2)}) collective-permute-start(f32[256,256]{1,0:T(8,128)S(1)} %shard_map.74), channel_id=1, source_target_pairs={{0,1},{1,0},{2,3},{3,2},{4,5},{5,4},{6,7},{7,6},{8,9},{9,8},{10,11... | collective-permute-start | bytes 786440 | tf_op jit(solution)/shard_map/ppermute | solution.py:26
  16.3 7.4 %collective-permute-start.6 = (bf16[256,256]{1,0:T(8,128)(2,1)S(1)}, bf16[256,256]{1,0:T(8,128)(2,1)S(1)}, u32[]{:S(2)}, u32[]{:S(2)}) collective-permute-start(bf16[256,256]{1,0:T(8,128)(2,1)S(1)} %add_convert_fusion.refs_0_.refs_4_), channel_id=1, source_target_pairs={{0,24},{1,57},{2,26},{3,59},{4,28},{5,61},{6,30},{7,63},{8,16},{9,... | collective-permute-start | bytes 393224 | tf_op jit(solution)/shard_map/ppermute | solution.py:26
  18.5 6.8 %collective-permute-start.7 = (bf16[256,256]{1,0:T(8,128)(2,1)S(1)}, bf16[256,256]{1,0:T(8,128)(2,1)S(1)}, u32[]{:S(2)}, u32[]{:S(2)}) collective-permute-start(bf16[256,256]{1,0:T(8,128)(2,1)S(1)} %add_convert_fusion.refs_0_.refs_4_), channel_id=1, source_target_pairs={{0,32},{1,121},{2,34},{3,123},{4,36},{5,125},{6,38},{7,127},{8,40}... | collective-permute-start | bytes 393224 | tf_op jit(solution)/shard_map/ppermute | solution.py:26
  20.1 10.4 %collective-permute-start.8 = (bf16[256,256]{1,0:T(8,128)(2,1)S(1)}, bf16[256,256]{1,0:T(8,128)(2,1)S(1)}, u32[]{:S(2)}, u32[]{:S(2)}) collective-permute-start(bf16[256,256]{1,0:T(8,128)(2,1)S(1)} %add_convert_fusion.refs_0_.refs_4_), channel_id=1, source_target_pairs={{0,96},{1,89},{2,98},{3,91},{4,100},{5,93},{6,102},{7,95},{8,104},... | collective-permute-start | bytes 393224 | tf_op jit(solution)/shard_map/ppermute | solution.py:26
  22.3 10.3 %collective-permute-start.12 = (bf16[128,256]{1,0:T(8,128)(2,1)S(1)}, bf16[128,256]{1,0:T(8,128)(2,1)S(1)}, u32[]{:S(2)}, u32[]{:S(2)}) collective-permute-start(bf16[128,256]{1,0:T(8,128)(2,1)S(1)} %constant_dynamic-slice_fusion), channel_id=1, source_target_pairs={{0,64},{1,65},{2,66},{3,67},{4,68},{5,69},{6,70},{7,71},{8,72},{9,... | collective-permute-start | bytes 196616 | tf_op jit(solution)/shard_map/ppermute | solution.py:26
  30.5 3.6 %collective-permute-start.10 = (bf16[256,256]{1,0:T(8,128)(2,1)S(1)}, bf16[256,256]{1,0:T(8,128)(2,1)S(1)}, u32[]{:S(2)}, u32[]{:S(2)}) collective-permute-start(bf16[256,256]{1,0:T(8,128)(2,1)S(1)} %collective-permute-done.7.refs_0_.refs_6_.refs_2_), channel_id=1, source_target_pairs={{0,1},{1,0},{2,3},{3,2},{4,5},{5,4},{6,7},{7,6},{8,9},{9,8},{10,11... | collective-permute-start | bytes 393224 | tf_op jit(solution)/shard_map/ppermute | solution.py:26
  30.5 3.6 %collective-permute-start.11 = (bf16[256,256]{1,0:T(8,128)(2,1)S(1)}, bf16[256,256]{1,0:T(8,128)(2,1)S(1)}, u32[]{:S(2)}, u32[]{:S(2)}) collective-permute-start(bf16[256,256]{1,0:T(8,128)(2,1)S(1)} %collective-permute-done.8.refs_1_.refs_7_.refs_3_), channel_id=1, source_target_pairs={{0,1},{1,0},{2,3},{3,2},{4,5},{5,4},{6,7},{7,6},{8,9},{9,8},{10,11... | collective-permute-start | bytes 393224 | tf_op jit(solution)/shard_map/ppermute | solution.py:26
  31.0 3.1 %collective-permute-start.9 = (bf16[256,256]{1,0:T(8,128)(2,1)S(1)}, bf16[256,256]{1,0:T(8,128)(2,1)S(1)}, u32[]{:S(2)}, u32[]{:S(2)}) collective-permute-start(bf16[256,256]{1,0:T(8,128)(2,1)S(1)} %collective-permute-done.6.refs_1_.refs_5_), channel_id=1, source_target_pairs={{0,1},{1,0},{2,3},{3,2},{4,5},{5,4},{6,7},{7,6},{8,9},{9,8},{10,11... | collective-permute-start | bytes 393224 | tf_op jit(solution)/shard_map/ppermute | solution.py:26
  32.5 1.5 %collective-permute-start.13 = (bf16[128,256]{1,0:T(8,128)(2,1)S(1)}, bf16[128,256]{1,0:T(8,128)(2,1)S(1)}, u32[]{:S(2)}, u32[]{:S(2)}) collective-permute-start(bf16[128,256]{1,0:T(8,128)(2,1)S(1)} %collective-permute-done.12.refs_4_.refs_12_.refs_8_), channel_id=1, source_target_pairs={{0,1},{1,0},{2,3},{3,2},{4,5},{5,4},{6,7},{7,6},{8,9},{9,8},{10,11... | collective-permute-start | bytes 196616 | tf_op jit(solution)/shard_map/ppermute | solution.py:26
  34.7 7.6 %collective-permute-start.14 = (bf16[64,512]{1,0:T(8,128)(2,1)S(1)}, bf16[64,512]{1,0:T(8,128)(2,1)S(1)}, u32[]{:S(2)}, u32[]{:S(2)}) collective-permute-start(bf16[64,512]{1,0:T(8,128)(2,1)S(1)} %get-tuple-element.69), channel_id=1, source_target_pairs={{0,16},{1,17},{2,18},{3,19},{4,20},{5,21},{6,22},{7,23},{8,24},{9,... | collective-permute-start | bytes 196616 | tf_op jit(solution)/shard_map/ppermute | solution.py:431
  35.4 6.9 %collective-permute-start.15 = (bf16[64,512]{1,0:T(8,128)(2,1)S(1)}, bf16[64,512]{1,0:T(8,128)(2,1)S(1)}, u32[]{:S(2)}, u32[]{:S(2)}) collective-permute-start(bf16[64,512]{1,0:T(8,128)(2,1)S(1)} %get-tuple-element.70), channel_id=1, source_target_pairs={{0,2},{1,3},{2,0},{3,1},{4,6},{5,7},{6,4},{7,5},{8,10},{9,11},{10,... | collective-permute-start | bytes 196616 | tf_op jit(solution)/shard_map/ppermute | solution.py:431
  35.4 6.9 %collective-permute-start.16 = (bf16[64,128]{1,0:T(8,128)(2,1)S(1)}, bf16[64,128]{1,0:T(8,128)(2,1)S(1)}, u32[]{:S(2)}, u32[]{:S(2)}) collective-permute-start(bf16[64,128]{1,0:T(8,128)(2,1)S(1)} %get-tuple-element.71), channel_id=1, source_target_pairs={{0,1},{1,0},{2,3},{3,2},{4,5},{5,4},{6,7},{7,6},{8,9},{9,8},{10,11... | collective-permute-start | bytes 49160 | tf_op jit(solution)/shard_map/ppermute | solution.py:431
  35.4 6.9 %collective-permute-start.17 = (bf16[64,128]{1,0:T(8,128)(2,1)S(1)}, bf16[64,128]{1,0:T(8,128)(2,1)S(1)}, u32[]{:S(2)}, u32[]{:S(2)}) collective-permute-start(bf16[64,128]{1,0:T(8,128)(2,1)S(1)} %get-tuple-element.72), channel_id=1, source_target_pairs={{0,32},{1,2},{2,1},{3,4},{4,3},{5,6},{6,5},{7,8},{8,7},{9,10},{10,... | collective-permute-start | bytes 49160 | tf_op jit(solution)/shard_map/ppermute | solution.py:431
  39.7 2.6 %copy-start.1 = (bf16[4,64,4]{1,2,0:T(4,128)(2,1)S(1)}, bf16[4,64,4]{1,2,0:T(4,128)(2,1)}, u32[]{:S(2)}) copy-start(bf16[4,64,4]{1,2,0:T(4,128)(2,1)} %param.10) | copy-start | bytes 6148
  39.7 2.6 %copy-start.2 = (s32[4]{0:T(128)S(1)}, s32[4]{0:T(128)}, u32[]{:S(2)}) copy-start(s32[4]{0:T(128)} %port_ref.3) | copy-start | bytes 52
  45.6 8.7 %collective-permute-start.18 = (bf16[64,512]{1,0:T(8,128)(2,1)S(1)}, bf16[64,512]{1,0:T(8,128)(2,1)S(1)}, u32[]{:S(2)}, u32[]{:S(2)}) collective-permute-start(bf16[64,512]{1,0:T(8,128)(2,1)S(1)} %get-tuple-element.75), channel_id=1, source_target_pairs={{0,16},{1,17},{2,18},{3,19},{4,20},{5,21},{6,22},{7,23},{8,24},{9,... | collective-permute-start | bytes 196616 | tf_op jit(solution)/shard_map/ppermute | solution.py:431
  48.3 6.0 %collective-permute-start.19 = (bf16[64,512]{1,0:T(8,128)(2,1)S(1)}, bf16[64,512]{1,0:T(8,128)(2,1)S(1)}, u32[]{:S(2)}, u32[]{:S(2)}) collective-permute-start(bf16[64,512]{1,0:T(8,128)(2,1)S(1)} %get-tuple-element.76), channel_id=1, source_target_pairs={{0,2},{1,3},{2,0},{3,1},{4,6},{5,7},{6,4},{7,5},{8,10},{9,11},{10,... | collective-permute-start | bytes 196616 | tf_op jit(solution)/shard_map/ppermute | solution.py:431
  48.6 5.6 %collective-permute-start.20 = (bf16[64,128]{1,0:T(8,128)(2,1)S(1)}, bf16[64,128]{1,0:T(8,128)(2,1)S(1)}, u32[]{:S(2)}, u32[]{:S(2)}) collective-permute-start(bf16[64,128]{1,0:T(8,128)(2,1)S(1)} %get-tuple-element.77), channel_id=1, source_target_pairs={{0,1},{1,0},{2,3},{3,2},{4,5},{5,4},{6,7},{7,6},{8,9},{9,8},{10,11... | collective-permute-start | bytes 49160 | tf_op jit(solution)/shard_map/ppermute | solution.py:431
  48.6 5.7 %collective-permute-start.21 = (bf16[64,128]{1,0:T(8,128)(2,1)S(1)}, bf16[64,128]{1,0:T(8,128)(2,1)S(1)}, u32[]{:S(2)}, u32[]{:S(2)}) collective-permute-start(bf16[64,128]{1,0:T(8,128)(2,1)S(1)} %get-tuple-element.78), channel_id=1, source_target_pairs={{0,32},{1,2},{2,1},{3,4},{4,3},{5,6},{6,5},{7,8},{8,7},{9,10},{10,... | collective-permute-start | bytes 49160 | tf_op jit(solution)/shard_map/ppermute | solution.py:431

commit v17 on v16

--- a/solution.py
+++ b/solution.py
@@ -113,10 +113,25 @@
         flops=2**30,
     )
     other, sides = lax.optimization_barrier((other, sides))
-    return (partial + other).astype(BF), x, sides
-
-
-MAP_STEPS = ((0, 0), (1, 3), (2, 7), (6, 5), (3, 1), (7, 2), (5, 6), (4, 4))
+    shapes = [jax.ShapeDtypeStruct((lines, order), BF) for lines in (order, order // 2)]
+    return *whole_call(own_kernel, shapes, partial, other), x, sides
+
+
+MAP_STEPS = ((0, 0), (2, 3), (6, 7), (3, 2), (7, 6), (1, 1), (4, 5), (5, 4))
+HALVES = 5
+
+
+def own_kernel(one_ref, two_ref, out_ref, half_ref):
+    core = lax.rem(lax.axis_index("col"), 2)
+    half = half_ref.shape[0]
+    total = (one_ref[...] + two_ref[...]).astype(BF)
+    out_ref[...] = total
+    half_ref[...] = jnp.where(core == 0, total[0:half], total[half:])
+
+
+def relay_kernel(first_ref, second_ref, out_ref):
+    core = lax.rem(lax.axis_index("col"), 2)
+    out_ref[...] = jnp.where(core == 0, second_ref[...], first_ref[...])
 
 
 def even(axis):
@@ -179,11 +194,14 @@
     return total
 
 
-def with_steps(map_refs, first, last):
-    refs = [(ref,) for ref in map_refs]
-    if last == len(MAP_STEPS):
-        refs[-2:] = [refs[-2] + refs[-1]]
-    return list(zip(MAP_STEPS[first:last], refs, strict=True))
+def with_steps(map_refs, first):
+    map_refs, maps = list(map_refs), []
+    while map_refs:
+        number = first + len(maps)
+        count = 2 if number == HALVES else 1
+        maps.append((MAP_STEPS[number], map_refs[:count]))
+        del map_refs[:count]
+    return maps
 
 
 def shifted(total, next_ref, rows):
@@ -257,11 +275,11 @@
     sides_ref[...], kinds_ref[...] = side_columns(x_ref, types_ref[...].astype(F32), ports)
 
 
-def early_kernel(ports, first, last, x_ref, types_ref, sides_ref, kinds_ref, *refs):
-    maps = with_steps(refs[: last - first], first, last)
+def early_kernel(ports, first, count, x_ref, types_ref, sides_ref, kinds_ref, *refs):
+    maps = with_steps(refs[:count], first)
     types = types_ref[...].astype(F32)
     tile = types.shape[1]
-    so_far, outs = refs[last - first : -4], refs[-4:]
+    so_far, outs = refs[count:-4], refs[-4:]
     done_ref, *so_far = so_far if first else [None] * 4
     values = rims(x_ref, types, ports, sides_ref[...], kinds_ref[0:1, :], maps, so_far)
     for ref, value in zip(outs[1:], values):
@@ -274,7 +292,7 @@
 
 
 def rim_kernel(ports, first, x_ref, types_ref, sides_ref, kinds_ref, *refs):
-    maps = with_steps(refs[:-7], first, len(MAP_STEPS))
+    maps = with_steps(refs[:-7], first)
     types = types_ref[...].astype(F32)
     quarter = x_ref.shape[0] // 4
     values = rims(x_ref, types, ports, sides_ref[...], kinds_ref[0:1, :], maps, refs[-7:-4])
@@ -283,7 +301,7 @@
 
 
 def first_kernel(rows, ports, first, x_ref, types_ref, done_ref, *refs):
-    maps = with_steps(refs[:-1], first, len(MAP_STEPS))
+    maps = with_steps(refs[:-1], first)
     types = types_ref[...].astype(F32).astype(BF)
     tile = types.shape[1]
     for port in range(ports):
@@ -328,7 +346,7 @@
     halo_refs, map_refs, patched_ref, ends_ref = refs[:4], refs[4:-6], refs[-6], refs[-5]
     order, tile = x_ref.shape[0], rows * width
     quarter = order // 4
-    maps = with_steps(map_refs, 0, len(MAP_STEPS))
+    maps = with_steps(map_refs, 0)
     for port in range(ports):
         places = [(port, row) for row in range(rows)]
         value = patched(rows, width, x_ref, port_ref, profile_ref, halo_refs, places)
@@ -348,7 +366,7 @@
 def second_kernel(rows, ports, width, x_ref, types_ref, ends_ref, *refs):
     map_refs, next_ref = refs[:-1], refs[-1]
     order, tile = x_ref.shape[0], rows * width
-    maps = with_steps(map_refs, 0, len(MAP_STEPS))
+    maps = with_steps(map_refs, 0)
     types = types_of_rows(types_ref, range(1, rows - 1)).astype(BF)
     for port in range(ports):
         start = port * tile
@@ -437,13 +455,10 @@
     quarter = samples
     tile = rows * width
     types = cell_type.reshape(1, tile)
-    own_map, x, sides = own_type_map(mode_shapes, mode_values, mode_weights, traces, types)
-    core = lax.rem(lax.axis_index("col"), 2)
-    half = lax.dynamic_slice_in_dim(own_map, core * (order // 2), order // 2)
-    fetched = [
-        swap(own_map, *((step, 8 * (step % 2)) for step in steps)) for steps in MAP_STEPS[1:4]
-    ]
-    half = swap(half, (4, 0))
+    own_map, half, x, sides = own_type_map(mode_shapes, mode_values, mode_weights, traces, types)
+    first = swap(own_map, (2, 0), (3, 8))
+    second = swap(own_map, (6, 0), (7, 8))
+    half = swap(half, (1, 8))
     profile = jnp.transpose(port_profile, (0, 2, 1))
     ports_spec = pl.BlockSpec(memory_space=pltpu.SMEM)
     next_shape = jax.ShapeDtypeStruct((order, ports * tile), BF)
@@ -454,22 +469,24 @@
     part_shapes = [next_shape] + rim_shapes[:2] + [jax.ShapeDtypeStruct((2 * quarter, LANES), BF)]
 
     def early(first, maps, parts=()):
-        last = first + len(maps)
-        kernel = functools.partial(early_kernel, ports, first, last)
+        kernel = functools.partial(early_kernel, ports, first, len(maps))
         flops = work * len(maps) // 7
         return whole_call(kernel, part_shapes, x, types, *sides, *maps, *parts, flops=flops)
 
-    parts = list(early(0, [own_map, fetched[0]]))
-    parts[1], fetched = lax.optimization_barrier((parts[1], fetched))
-    swapped = [swap_cores(value) for value in fetched]
-    parts = list(early(2, fetched[1:], parts))
-    parts[1], half = lax.optimization_barrier((parts[1], half))
-    swapped.append(swap_cores(half))
+    parts = list(early(0, [own_map, first]))
+    parts[1], first, second, half = lax.optimization_barrier((parts[1], first, second, half))
+    map_shape = jax.ShapeDtypeStruct(own_map.shape, BF)
+    (relay,) = whole_call(relay_kernel, [map_shape], first, second)
+    relay, first, second, half = lax.optimization_barrier((relay, first, second, half))
+    third = swap(relay, (2, 0), (6, 0))
+    maps = [second, swap_cores(first), swap_cores(second), swap_cores(half), half]
+    parts = list(early(2, maps, parts))
+    parts[1], third = lax.optimization_barrier((parts[1], third))
     done, *parts = parts
-    late = swapped + [half]
-    maps = [own_map] + fetched + late
+    late = [third, swap_cores(third)]
+    maps = [own_map, first] + maps + late
     sent = whole_call(
-        functools.partial(rim_kernel, ports, 4),
+        functools.partial(rim_kernel, ports, 6),
         rim_shapes,
         x,
         types,
@@ -480,7 +497,7 @@
     )
     halos = exchange(sent[:2], "row") + exchange(sent[2:], "col")
     (x,) = whole_call(
-        functools.partial(first_kernel, rows, ports, 4),
+        functools.partial(first_kernel, rows, ports, 6),
         [next_shape],
         x,
         types,

time: 58.5 us -> 59 us (level)
  the two profiles are of different devices: /device:TPU:0 before, /device:TPU:10 now
where the time goes in v17:
time: 59 us; the launch traced here: 58.7 us
  starting transfers between devices  26 us (44%)
  Pallas kernels  19.4 us (33%)
  waiting for transfers between devices  11.4 us (19%)
  other arithmetic  0.81 us (1%)
  local copies, waits for them, and re-layouts  0.67 us (1%)
    ppermute x14, starting transfers between devices, swap(): return lax.ppermute(value, ('row', 'col'), pairs)  14.2 us
    ppermute x8, starting transfers between devices, exchange(): lax.ppermute(rim, ('row', 'col'), pairs(first))  11.9 us
    pallas_call x9, Pallas kernels, whole_call(): pl.pallas_call(kernel, in_specs=[WHOLE] * len(operands), out_specs=[WHOLE...  11.4 us
    ppermute x14, waiting for transfers between devices, swap(): return lax.ppermute(value, ('row', 'col'), pairs)  7.25 us
    ppermute x8, waiting for transfers between devices, exchange(): lax.ppermute(rim, ('row', 'col'), pairs(first))  4.19 us
    pallas_call x1, Pallas kernels, body(): pl.pallas_call(functools.partial(ends_kernel, rows, ports, width), in_spe...  3.2 us
    pallas_call x1, Pallas kernels, body(): pl.pallas_call(functools.partial(last_kernel, rows, width), in_specs=[por...  2.86 us
    pallas_call x1, Pallas kernels, own_type_map(): pl.pallas_call(flat_kernel, in_specs=[pl.BlockSpec(memory_space=pltpu.HBM...  1.98 us
  transfers between devices with their start and end apart: 22, of which 8 were waited for; matrix products, arithmetic and copies ran while one was open for 0% of the time, Pallas kernels for 21%

profile of v17, /device:TPU:10, one launch (start us, length us, event | category | flops | bytes accessed | tf_op | source)
XLA Modules:
  0.0 58.7 jit_solution(16290575511707974006)
XLA Ops:
  0.0 0.7 %concatenate.10 = f32[32]{0:T(128)S(1)} pad(f32[16]{0:T(128)} %bitcast.21, f32[]{:T(128)} %constant.0.clone.1), padding=0_16 | pad | bytes 196 | tf_op jit(solution)/shard_map/concatenate | solution.py:82
  0.7 0.8 %maximum_multiply_fusion.refs_0_ = f32[32,256]{1,0:T(8,128)S(1)} fusion(f32[16,256]{1,0:T(8,128)} %bitcast.19, f32[16,256]{1,0:T(8,128)} %bitcast.20, f32[32]{0:T(128)S(1)} %concatenate.10), kind=kLoop, calls=%fused_computation.1 | loop fusion | flops 16384 | bytes 65664 | tf_op jit(solution)/shard_map/mul | solution.py:82
  1.5 0.0 collective-permute-start.1
  1.5 3.9 %collective-permute-start = (f32[32,256]{1,0:T(8,128)S(1)}, f32[32,256]{1,0:T(8,128)S(1)}, u32[]{:S(2)}, u32[]{:S(2)}) collective-permute-start(f32[32,256]{1,0:T(8,128)S(1)} %maximum_multiply_fusion.refs_0_), channel_id=1, source_target_pairs={{0,4},{1,5},{2,6},{3,7},{4,0},{5,1},{6,2},{7,3},{8,12},{9,13},{10,... | collective-permute-start | bytes 98312 | tf_op jit(solution)/shard_map/ppermute | solution.py:26
  5.4 0.0 collective-permute-done.1
  5.4 1.3 %collective-permute-start.4 = (f32[64,256]{1,0:T(8,128)S(1)}, f32[64,256]{1,0:T(8,128)S(1)}, u32[]{:S(2)}, u32[]{:S(2)}) collective-permute-start(f32[64,256]{1,0:T(8,128)S(1)} %pad_maximum_fusion), channel_id=1, source_target_pairs={{0,6},{1,13},{2,4},{3,15},{4,2},{5,9},{6,0},{7,11},{8,14},{9,5},{1... | collective-permute-start | bytes 196616 | tf_op jit(solution)/shard_map/ppermute | solution.py:26
  6.7 0.0 collective-permute-start.3
  6.7 0.5 collective-permute-start.2
  7.3 0.0 copy-start
  7.3 2.0 %shard_map.73.x_ref = bf16[256,4096]{1,0:T(8,128)(2,1)S(1)} custom-call(bf16[256,4,8,128]{3,2,1,0:T(8,128)(2,1)} %bitcast.18), custom_call_target="tpu_custom_call" | custom-call | flops 1073741824 | tf_op jit(solution)/shard_map/pallas_call | solution.py:89
  9.3 3.1 %collective-permute-done.4.refs_4_ = f32[64,256]{1,0:T(8,128)S(1)} collective-permute-done((f32[64,256]{1,0:T(8,128)S(1)}, f32[64,256]{1,0:T(8,128)S(1)}, u32[]{:S(2)}, u32[]{:S(2)}) %collective-permute-start.4) | collective-permute-done | bytes 65568 | tf_op jit(solution)/shard_map/ppermute | solution.py:26
  12.4 0.0 collective-permute-done.3.refs_3_
  12.4 0.0 collective-permute-done.2.refs_2_
  12.4 0.0 collective-permute-done.refs_1_
  12.4 0.4 shard_map.74.one_ref
  12.8 1.4 %collective-permute-start.5 = (f32[256,256]{1,0:T(8,128)S(1)}, f32[256,256]{1,0:T(8,128)S(1)}, u32[]{:S(2)}, u32[]{:S(2)}) collective-permute-start(f32[256,256]{1,0:T(8,128)S(1)} %shard_map.74.one_ref), channel_id=1, source_target_pairs={{0,1},{1,0},{2,3},{3,2},{4,5},{5,4},{6,7},{7,6},{8,9},{9,8},{10,11... | collective-permute-start | bytes 786440 | tf_op jit(solution)/shard_map/ppermute | solution.py:26
  14.2 0.0 copy-done
  14.2 1.2 %shard_map.75 = (bf16[256,128]{1,0:T(8,128)(2,1)S(1)}, bf16[16,128]{1,0:T(8,128)(2,1)S(1)}) custom-call(bf16[256,4096]{1,0:T(8,128)(2,1)S(1)} %shard_map.73.x_ref, s32[1,1024]{1,0:T(1,128)S(1)} %bitcast.9), custom_call_target="tpu_custom_call" | custom-call | flops 1073741824 | tf_op jit(solution)/shard_map/pallas_call | solution.py:69
  15.4 0.0 collective-permute-done.5.two_ref
  15.4 0.5 collective-permute-start.6
  16.0 2.4 %collective-permute-start.7 = (bf16[256,256]{1,0:T(8,128)(2,1)S(1)}, bf16[256,256]{1,0:T(8,128)(2,1)S(1)}, u32[]{:S(2)}, u32[]{:S(2)}) collective-permute-start(bf16[256,256]{1,0:T(8,128)(2,1)S(1)} %get-tuple-element.61.refs_0_.refs_4_), channel_id=1, source_target_pairs={{0,96},{1,121},{2,98},{3,123},{4,100},{5,125},{6,102},{7,127},{8,1... | collective-permute-start | bytes 393224 | tf_op jit(solution)/shard_map/ppermute | solution.py:26
  18.4 1.5 %collective-permute-start.8 = (bf16[128,256]{1,0:T(8,128)(2,1)S(1)}, bf16[128,256]{1,0:T(8,128)(2,1)S(1)}, u32[]{:S(2)}, u32[]{:S(2)}) collective-permute-start(bf16[128,256]{1,0:T(8,128)(2,1)S(1)} %get-tuple-element.63), channel_id=1, source_target_pairs={{0,24},{1,25},{2,26},{3,27},{4,28},{5,29},{6,30},{7,31},{8,16},{9,... | collective-permute-start | bytes 196616 | tf_op jit(solution)/shard_map/ppermute | solution.py:26
  19.9 2.0 %collective-permute-done.6.refs_1_.first_ref.refs_5_ = bf16[256,256]{1,0:T(8,128)(2,1)S(1)} collective-permute-done((bf16[256,256]{1,0:T(8,128)(2,1)S(1)}, bf16[256,256]{1,0:T(8,128)(2,1)S(1)}, u32[]{:S(2)}, u32[]{:S(2)}) %collective-permute-start.6) | collective-permute-done | bytes 131104 | tf_op jit(solution)/shard_map/ppermute | solution.py:26
  21.9 1.5 %shard_map.77 = (bf16[256,4096]{1,0:T(8,128)(2,1)S(1)}, bf16[64,512]{1,0:T(8,128)(2,1)S(1)}, bf16[64,512]{1,0:T(8,128)(2,1)S(1)}, bf16[128,128]{1,0:T(8,128)(2,1)S(1)}) custom-call(bf16[256,4096]{1,0:T(8,128)(2,1)S(1)} %shard_map.73.x_ref, s32[1,1024]{1,0:T(1,128)S(1)} %bitcast.10, bf16[256,128]{1,0:T(8,128)(2,1)S(1)} %get-tuple-element.58.sides_ref, ...), custom_call_target="tpu_custom_call" | custom-call | flops 1227133568 | tf_op jit(solution)/shard_map/pallas_call | solution.py:69
  23.4 0.0 collective-permute-done.8.refs_4_.refs_10_.refs_6_
  23.4 0.0 collective-permute-done.7.second_ref.refs_0_.refs_6_.refs_2_
  23.5 0.7 %collective-permute-start.9 = (bf16[256,256]{1,0:T(8,128)(2,1)S(1)}, bf16[256,256]{1,0:T(8,128)(2,1)S(1)}, u32[]{:S(2)}, u32[]{:S(2)}) collective-permute-start(bf16[256,256]{1,0:T(8,128)(2,1)S(1)} %collective-permute-done.6.refs_1_.first_ref.refs_5_), channel_id=1, source_target_pairs={{0,1},{1,0},{2,3},{3,2},{4,5},{5,4},{6,7},{7,6},{8,9},{9,8},{10,11... | collective-permute-start | bytes 393224 | tf_op jit(solution)/shard_map/ppermute | solution.py:26
  24.1 0.1 collective-permute-start.10
  24.2 0.4 collective-permute-start.11
  24.6 1.3 %collective-permute-start.12 = (bf16[256,256]{1,0:T(8,128)(2,1)S(1)}, bf16[256,256]{1,0:T(8,128)(2,1)S(1)}, u32[]{:S(2)}, u32[]{:S(2)}) collective-permute-start(bf16[256,256]{1,0:T(8,128)(2,1)S(1)} %shard_map.78), channel_id=1, source_target_pairs={{0,32},{1,97},{2,34},{3,99},{4,36},{5,101},{6,38},{7,103},{8,40},{... | collective-permute-start | bytes 393224 | tf_op jit(solution)/shard_map/ppermute | solution.py:26
  26.0 0.0 collective-permute-done.11.refs_3_.refs_9_.refs_5_
  26.0 0.0 collective-permute-done.9.refs_1_.refs_7_.refs_3_
  26.0 0.0 collective-permute-done.10.refs_2_.refs_8_.refs_4_
  26.0 2.9 %shard_map.79 = (bf16[256,4096]{1,0:T(8,128)(2,1)S(1)}, bf16[64,512]{1,0:T(8,128)(2,1)S(1)}, bf16[64,512]{1,0:T(8,128)(2,1)S(1)}, bf16[128,128]{1,0:T(8,128)(2,1)S(1)}) custom-call(bf16[256,4096]{1,0:T(8,128)(2,1)S(1)} %shard_map.73.x_ref, s32[1,1024]{1,0:T(1,128)S(1)} %bitcast.11, bf16[256,128]{1,0:T(8,128)(2,1)S(1)} %get-tuple-element.58.sides_ref, ...), custom_call_target="tpu_custom_call" | custom-call | flops 3067833856 | tf_op jit(solution)/shard_map/pallas_call | solution.py:69
  28.9 0.7 %collective-permute-done.12.refs_0_.refs_11_.refs_7_ = bf16[256,256]{1,0:T(8,128)(2,1)S(1)} collective-permute-done((bf16[256,256]{1,0:T(8,128)(2,1)S(1)}, bf16[256,256]{1,0:T(8,128)(2,1)S(1)}, u32[]{:S(2)}, u32[]{:S(2)}) %collective-permute-start.12) | collective-permute-done | bytes 131104 | tf_op jit(solution)/shard_map/ppermute | solution.py:26
  29.6 0.0 collective-permute-start.13
  29.6 1.3 %collective-permute-done.13.refs_1_.refs_12_.refs_8_ = bf16[256,256]{1,0:T(8,128)(2,1)S(1)} collective-permute-done((bf16[256,256]{1,0:T(8,128)(2,1)S(1)}, bf16[256,256]{1,0:T(8,128)(2,1)S(1)}, u32[]{:S(2)}, u32[]{:S(2)}) %collective-permute-start.13) | collective-permute-done | bytes 131104 | tf_op jit(solution)/shard_map/ppermute | solution.py:26
  31.0 0.4 shard_map.81
  31.4 0.2 collective-permute-start.16
  31.6 3.2 %collective-permute-start.17 = (bf16[64,128]{1,0:T(8,128)(2,1)S(1)}, bf16[64,128]{1,0:T(8,128)(2,1)S(1)}, u32[]{:S(2)}, u32[]{:S(2)}) collective-permute-start(bf16[64,128]{1,0:T(8,128)(2,1)S(1)} %get-tuple-element.84), channel_id=1, source_target_pairs={{0,32},{1,2},{2,1},{3,4},{4,3},{5,6},{6,5},{7,8},{8,7},{9,10},{10,... | collective-permute-start | bytes 49160 | tf_op jit(solution)/shard_map/ppermute | solution.py:449
  34.8 0.0 collective-permute-start.14
  34.8 4.3 %collective-permute-start.15 = (bf16[64,512]{1,0:T(8,128)(2,1)S(1)}, bf16[64,512]{1,0:T(8,128)(2,1)S(1)}, u32[]{:S(2)}, u32[]{:S(2)}) collective-permute-start(bf16[64,512]{1,0:T(8,128)(2,1)S(1)} %get-tuple-element.82), channel_id=1, source_target_pairs={{0,2},{1,3},{2,0},{3,1},{4,6},{5,7},{6,4},{7,5},{8,10},{9,11},{10,... | collective-permute-start | bytes 196616 | tf_op jit(solution)/shard_map/ppermute | solution.py:449
  39.2 0.0 copy-start.1
  39.2 0.0 copy-start.2
  39.2 1.4 %shard_map.80.x_ref = bf16[256,4096]{1,0:T(8,128)(2,1)S(1)} custom-call(bf16[256,4096]{1,0:T(8,128)(2,1)S(1)} %shard_map.73.x_ref, s32[1,1024]{1,0:T(1,128)S(1)} %bitcast.13, bf16[256,4096]{1,0:T(8,128)(2,1)S(1)} %get-tuple-element.74.done_ref, bf16[256,256]{1,0:T(8,128)(2,1)S(1)} %collective-permute-done.12.refs_0_.refs_11_.refs_7_, ...), custom_call_target="tpu_custom_call" | custom-call | flops 2147483648 | tf_op jit(solution)/shard_map/pallas_call | solution.py:69
  40.6 0.0 collective-permute-done.16.refs_2_
  40.6 0.0 collective-permute-done.17.refs_3_
  40.6 0.2 collective-permute-done.14.refs_0_
  40.8 1.3 %collective-permute-done.15.refs_1_ = bf16[64,512]{1,0:T(8,128)(2,1)S(1)} collective-permute-done((bf16[64,512]{1,0:T(8,128)(2,1)S(1)}, bf16[64,512]{1,0:T(8,128)(2,1)S(1)}, u32[]{:S(2)}, u32[]{:S(2)}) %collective-permute-start.15) | collective-permute-done | bytes 65568 | tf_op jit(solution)/shard_map/ppermute | solution.py:449
  42.1 0.0 copy-done.1
  42.1 0.0 copy-done.2
  42.1 3.2 %shard_map.82 = (bf16[256,4096]{1,0:T(8,128)(2,1)S(1)}, bf16[256,1024]{1,0:T(8,128)(2,1)S(1)}, bf16[64,512]{1,0:T(8,128)(2,1)S(1)}, bf16[64,512]{1,0:T(8,128)(2,...) custom-call(s32[4]{0:T(128)S(1)} %copy-done.2, bf16[256,4096]{1,0:T(8,128)(2,1)S(1)} %shard_map.80.x_ref, ...), custom_call_target="tpu_custom_call" | custom-call | flops 1431655808 | tf_op jit(solution)/shard_map/pallas_call | solution.py:510
  45.3 0.1 collective-permute-start.20
  45.4 2.1 %collective-permute-start.21 = (bf16[64,128]{1,0:T(8,128)(2,1)S(1)}, bf16[64,128]{1,0:T(8,128)(2,1)S(1)}, u32[]{:S(2)}, u32[]{:S(2)}) collective-permute-start(bf16[64,128]{1,0:T(8,128)(2,1)S(1)} %get-tuple-element.90), channel_id=1, source_target_pairs={{0,32},{1,2},{2,1},{3,4},{4,3},{5,6},{6,5},{7,8},{8,7},{9,10},{10,... | collective-permute-start | bytes 49160 | tf_op jit(solution)/shard_map/ppermute | solution.py:449
  47.5 1.5 %collective-permute-start.18 = (bf16[64,512]{1,0:T(8,128)(2,1)S(1)}, bf16[64,512]{1,0:T(8,128)(2,1)S(1)}, u32[]{:S(2)}, u32[]{:S(2)}) collective-permute-start(bf16[64,512]{1,0:T(8,128)(2,1)S(1)} %get-tuple-element.87), channel_id=1, source_target_pairs={{0,16},{1,17},{2,18},{3,19},{4,20},{5,21},{6,22},{7,23},{8,24},{9,... | collective-permute-start | bytes 196616 | tf_op jit(solution)/shard_map/ppermute | solution.py:449
  49.0 0.4 collective-permute-start.19
  49.4 3.5 %shard_map.83.x_ref = bf16[256,4096]{1,0:T(8,128)(2,1)S(1)} custom-call(bf16[256,4096]{1,0:T(8,128)(2,1)S(1)} %get-tuple-element.85.x_ref, s32[1,1024]{1,0:T(1,128)S(1)} %bitcast.15, bf16[256,1024]{1,0:T(8,128)(2,1)S(1)} %get-tuple-element.86.ends_ref, bf16[256,256]{1,0:T(8,128)(2,1)S(1)} %get-tuple-element.61.refs_0_.refs_4_, ...), custom_call_target="tpu_custom_call" | custom-call | flops 3221225472 | tf_op jit(solution)/shard_map/pallas_call | solution.py:69
  53.0 0.0 collective-permute-done.20.refs_2_
  53.0 0.0 collective-permute-done.21.refs_3_
  53.0 0.8 %collective-permute-done.18.refs_0_ = bf16[64,512]{1,0:T(8,128)(2,1)S(1)} collective-permute-done((bf16[64,512]{1,0:T(8,128)(2,1)S(1)}, bf16[64,512]{1,0:T(8,128)(2,1)S(1)}, u32[]{:S(2)}, u32[]{:S(2)}) %collective-permute-start.18) | collective-permute-done | bytes 65568 | tf_op jit(solution)/shard_map/ppermute | solution.py:449
  53.7 1.9 %collective-permute-done.19.refs_1_ = bf16[64,512]{1,0:T(8,128)(2,1)S(1)} collective-permute-done((bf16[64,512]{1,0:T(8,128)(2,1)S(1)}, bf16[64,512]{1,0:T(8,128)(2,1)S(1)}, u32[]{:S(2)}, u32[]{:S(2)}) %collective-permute-start.19) | collective-permute-done | bytes 65568 | tf_op jit(solution)/shard_map/ppermute | solution.py:449
  55.7 2.9 %shard_map.84 = bf16[256,4,8,128]{3,2,1,0:T(8,128)(2,1)} custom-call(s32[4]{0:T(128)S(1)} %copy-done.2, bf16[256,4096]{1,0:T(8,128)(2,1)S(1)} %shard_map.83.x_ref, bf16[4,4,64]{2,1,0:T(4,128)(2,1)S(1)} %bitcast.17, bf16[64,512]{1,0:T(8,128)(2,1)S(1)} %collective-permute-done.18.refs_0_, bf16[64,512]{1,0:T(8,128)(2,1)S(1)} %collective-permute-done.19.refs_1_, ...), custom_call_target="tpu_custom_call" | custom-call | tf_op jit(solution)/shard_map/pallas_call | solution.py:529
  (3 shorter events, 0.1 us)
Async XLA Ops:
  1.5 3.9 %collective-permute-start.1 = (f32[32,256]{1,0:T(8,128)S(1)}, f32[32,256]{1,0:T(8,128)S(1)}, u32[]{:S(2)}, u32[]{:S(2)}) collective-permute-start(f32[32,256]{1,0:T(8,128)S(1)} %maximum_multiply_fusion.refs_0_), channel_id=1, source_target_pairs={{0,1},{1,0},{2,3},{3,2},{4,5},{5,4},{6,7},{7,6},{8,9},{9,8},{10,11... | collective-permute-start | bytes 98312 | tf_op jit(solution)/shard_map/ppermute | solution.py:26
  1.5 10.9 %collective-permute-start = (f32[32,256]{1,0:T(8,128)S(1)}, f32[32,256]{1,0:T(8,128)S(1)}, u32[]{:S(2)}, u32[]{:S(2)}) collective-permute-start(f32[32,256]{1,0:T(8,128)S(1)} %maximum_multiply_fusion.refs_0_), channel_id=1, source_target_pairs={{0,4},{1,5},{2,6},{3,7},{4,0},{5,1},{6,2},{7,3},{8,12},{9,13},{10,... | collective-permute-start | bytes 98312 | tf_op jit(solution)/shard_map/ppermute | solution.py:26
  5.4 7.0 %collective-permute-start.4 = (f32[64,256]{1,0:T(8,128)S(1)}, f32[64,256]{1,0:T(8,128)S(1)}, u32[]{:S(2)}, u32[]{:S(2)}) collective-permute-start(f32[64,256]{1,0:T(8,128)S(1)} %pad_maximum_fusion), channel_id=1, source_target_pairs={{0,6},{1,13},{2,4},{3,15},{4,2},{5,9},{6,0},{7,11},{8,14},{9,5},{1... | collective-permute-start | bytes 196616 | tf_op jit(solution)/shard_map/ppermute | solution.py:26
  6.7 5.6 %collective-permute-start.3 = (f32[64,256]{1,0:T(8,128)S(1)}, f32[64,256]{1,0:T(8,128)S(1)}, u32[]{:S(2)}, u32[]{:S(2)}) collective-permute-start(f32[64,256]{1,0:T(8,128)S(1)} %pad_maximum_fusion), channel_id=1, source_target_pairs={{0,2},{1,15},{2,0},{3,13},{4,6},{5,11},{6,4},{7,9},{8,10},{9,7},{1... | collective-permute-start | bytes 196616 | tf_op jit(solution)/shard_map/ppermute | solution.py:26
  6.7 5.6 %collective-permute-start.2 = (f32[64,256]{1,0:T(8,128)S(1)}, f32[64,256]{1,0:T(8,128)S(1)}, u32[]{:S(2)}, u32[]{:S(2)}) collective-permute-start(f32[64,256]{1,0:T(8,128)S(1)} %pad_maximum_fusion), channel_id=1, source_target_pairs={{0,8},{1,11},{2,10},{3,9},{4,12},{5,15},{6,14},{7,13},{8,0},{9,3},... | collective-permute-start | bytes 196616 | tf_op jit(solution)/shard_map/ppermute | solution.py:26
  7.3 7.0 %copy-start = (s32[8,128]{1,0:T(8,128)S(1)}, s32[8,128]{1,0:T(8,128)}, u32[]{:S(2)}) copy-start(s32[8,128]{1,0:T(8,128)} %param.8) | copy-start | bytes 12292
  12.8 2.6 %collective-permute-start.5 = (f32[256,256]{1,0:T(8,128)S(1)}, f32[256,256]{1,0:T(8,128)S(1)}, u32[]{:S(2)}, u32[]{:S(2)}) collective-permute-start(f32[256,256]{1,0:T(8,128)S(1)} %shard_map.74.one_ref), channel_id=1, source_target_pairs={{0,1},{1,0},{2,3},{3,2},{4,5},{5,4},{6,7},{7,6},{8,9},{9,8},{10,11... | collective-permute-start | bytes 786440 | tf_op jit(solution)/shard_map/ppermute | solution.py:26
  15.4 6.5 %collective-permute-start.6 = (bf16[256,256]{1,0:T(8,128)(2,1)S(1)}, bf16[256,256]{1,0:T(8,128)(2,1)S(1)}, u32[]{:S(2)}, u32[]{:S(2)}) collective-permute-start(bf16[256,256]{1,0:T(8,128)(2,1)S(1)} %get-tuple-element.61.refs_0_.refs_4_), channel_id=1, source_target_pairs={{0,32},{1,57},{2,34},{3,59},{4,36},{5,61},{6,38},{7,63},{8,40},{9,... | collective-permute-start | bytes 393224 | tf_op jit(solution)/shard_map/ppermute | solution.py:26
  16.0 7.5 %collective-permute-start.7 = (bf16[256,256]{1,0:T(8,128)(2,1)S(1)}, bf16[256,256]{1,0:T(8,128)(2,1)S(1)}, u32[]{:S(2)}, u32[]{:S(2)}) collective-permute-start(bf16[256,256]{1,0:T(8,128)(2,1)S(1)} %get-tuple-element.61.refs_0_.refs_4_), channel_id=1, source_target_pairs={{0,96},{1,121},{2,98},{3,123},{4,100},{5,125},{6,102},{7,127},{8,1... | collective-permute-start | bytes 393224 | tf_op jit(solution)/shard_map/ppermute | solution.py:26
  18.4 5.0 %collective-permute-start.8 = (bf16[128,256]{1,0:T(8,128)(2,1)S(1)}, bf16[128,256]{1,0:T(8,128)(2,1)S(1)}, u32[]{:S(2)}, u32[]{:S(2)}) collective-permute-start(bf16[128,256]{1,0:T(8,128)(2,1)S(1)} %get-tuple-element.63), channel_id=1, source_target_pairs={{0,24},{1,25},{2,26},{3,27},{4,28},{5,29},{6,30},{7,31},{8,16},{9,... | collective-permute-start | bytes 196616 | tf_op jit(solution)/shard_map/ppermute | solution.py:26
  23.5 2.5 %collective-permute-start.9 = (bf16[256,256]{1,0:T(8,128)(2,1)S(1)}, bf16[256,256]{1,0:T(8,128)(2,1)S(1)}, u32[]{:S(2)}, u32[]{:S(2)}) collective-permute-start(bf16[256,256]{1,0:T(8,128)(2,1)S(1)} %collective-permute-done.6.refs_1_.first_ref.refs_5_), channel_id=1, source_target_pairs={{0,1},{1,0},{2,3},{3,2},{4,5},{5,4},{6,7},{7,6},{8,9},{9,8},{10,11... | collective-permute-start | bytes 393224 | tf_op jit(solution)/shard_map/ppermute | solution.py:26
  24.1 1.9 %collective-permute-start.10 = (bf16[256,256]{1,0:T(8,128)(2,1)S(1)}, bf16[256,256]{1,0:T(8,128)(2,1)S(1)}, u32[]{:S(2)}, u32[]{:S(2)}) collective-permute-start(bf16[256,256]{1,0:T(8,128)(2,1)S(1)} %collective-permute-done.7.second_ref.refs_0_.refs_6_.refs_2_), channel_id=1, source_target_pairs={{0,1},{1,0},{2,3},{3,2},{4,5},{5,4},{6,7},{7,6},{8,9},{9,8},{10,11... | collective-permute-start | bytes 393224 | tf_op jit(solution)/shard_map/ppermute | solution.py:26
  24.2 1.8 %collective-permute-start.11 = (bf16[128,256]{1,0:T(8,128)(2,1)S(1)}, bf16[128,256]{1,0:T(8,128)(2,1)S(1)}, u32[]{:S(2)}, u32[]{:S(2)}) collective-permute-start(bf16[128,256]{1,0:T(8,128)(2,1)S(1)} %collective-permute-done.8.refs_4_.refs_10_.refs_6_), channel_id=1, source_target_pairs={{0,1},{1,0},{2,3},{3,2},{4,5},{5,4},{6,7},{7,6},{8,9},{9,8},{10,11... | collective-permute-start | bytes 196616 | tf_op jit(solution)/shard_map/ppermute | solution.py:26
  24.6 5.0 %collective-permute-start.12 = (bf16[256,256]{1,0:T(8,128)(2,1)S(1)}, bf16[256,256]{1,0:T(8,128)(2,1)S(1)}, u32[]{:S(2)}, u32[]{:S(2)}) collective-permute-start(bf16[256,256]{1,0:T(8,128)(2,1)S(1)} %shard_map.78), channel_id=1, source_target_pairs={{0,32},{1,97},{2,34},{3,99},{4,36},{5,101},{6,38},{7,103},{8,40},{... | collective-permute-start | bytes 393224 | tf_op jit(solution)/shard_map/ppermute | solution.py:26
  29.6 1.3 %collective-permute-start.13 = (bf16[256,256]{1,0:T(8,128)(2,1)S(1)}, bf16[256,256]{1,0:T(8,128)(2,1)S(1)}, u32[]{:S(2)}, u32[]{:S(2)}) collective-permute-start(bf16[256,256]{1,0:T(8,128)(2,1)S(1)} %collective-permute-done.12.refs_0_.refs_11_.refs_7_), channel_id=1, source_target_pairs={{0,1},{1,0},{2,3},{3,2},{4,5},{5,4},{6,7},{7,6},{8,9},{9,8},{10,11... | collective-permute-start | bytes 393224 | tf_op jit(solution)/shard_map/ppermute | solution.py:26
  31.4 9.2 %collective-permute-start.16 = (bf16[64,128]{1,0:T(8,128)(2,1)S(1)}, bf16[64,128]{1,0:T(8,128)(2,1)S(1)}, u32[]{:S(2)}, u32[]{:S(2)}) collective-permute-start(bf16[64,128]{1,0:T(8,128)(2,1)S(1)} %get-tuple-element.83), channel_id=1, source_target_pairs={{0,1},{1,0},{2,3},{3,2},{4,5},{5,4},{6,7},{7,6},{8,9},{9,8},{10,11... | collective-permute-start | bytes 49160 | tf_op jit(solution)/shard_map/ppermute | solution.py:449
  31.6 9.0 %collective-permute-start.17 = (bf16[64,128]{1,0:T(8,128)(2,1)S(1)}, bf16[64,128]{1,0:T(8,128)(2,1)S(1)}, u32[]{:S(2)}, u32[]{:S(2)}) collective-permute-start(bf16[64,128]{1,0:T(8,128)(2,1)S(1)} %get-tuple-element.84), channel_id=1, source_target_pairs={{0,32},{1,2},{2,1},{3,4},{4,3},{5,6},{6,5},{7,8},{8,7},{9,10},{10,... | collective-permute-start | bytes 49160 | tf_op jit(solution)/shard_map/ppermute | solution.py:449
  34.8 6.0 %collective-permute-start.14 = (bf16[64,512]{1,0:T(8,128)(2,1)S(1)}, bf16[64,512]{1,0:T(8,128)(2,1)S(1)}, u32[]{:S(2)}, u32[]{:S(2)}) collective-permute-start(bf16[64,512]{1,0:T(8,128)(2,1)S(1)} %get-tuple-element.81), channel_id=1, source_target_pairs={{0,16},{1,17},{2,18},{3,19},{4,20},{5,21},{6,22},{7,23},{8,24},{9,... | collective-permute-start | bytes 196616 | tf_op jit(solution)/shard_map/ppermute | solution.py:449
  34.8 7.3 %collective-permute-start.15 = (bf16[64,512]{1,0:T(8,128)(2,1)S(1)}, bf16[64,512]{1,0:T(8,128)(2,1)S(1)}, u32[]{:S(2)}, u32[]{:S(2)}) collective-permute-start(bf16[64,512]{1,0:T(8,128)(2,1)S(1)} %get-tuple-element.82), channel_id=1, source_target_pairs={{0,2},{1,3},{2,0},{3,1},{4,6},{5,7},{6,4},{7,5},{8,10},{9,11},{10,... | collective-permute-start | bytes 196616 | tf_op jit(solution)/shard_map/ppermute | solution.py:449
  39.2 2.9 %copy-start.1 = (bf16[4,64,4]{1,2,0:T(4,128)(2,1)S(1)}, bf16[4,64,4]{1,2,0:T(4,128)(2,1)}, u32[]{:S(2)}) copy-start(bf16[4,64,4]{1,2,0:T(4,128)(2,1)} %param.10) | copy-start | bytes 6148
  39.2 2.9 %copy-start.2 = (s32[4]{0:T(128)S(1)}, s32[4]{0:T(128)}, u32[]{:S(2)}) copy-start(s32[4]{0:T(128)} %port_ref.3) | copy-start | bytes 52
  45.3 7.7 %collective-permute-start.20 = (bf16[64,128]{1,0:T(8,128)(2,1)S(1)}, bf16[64,128]{1,0:T(8,128)(2,1)S(1)}, u32[]{:S(2)}, u32[]{:S(2)}) collective-permute-start(bf16[64,128]{1,0:T(8,128)(2,1)S(1)} %get-tuple-element.89), channel_id=1, source_target_pairs={{0,1},{1,0},{2,3},{3,2},{4,5},{5,4},{6,7},{7,6},{8,9},{9,8},{10,11... | collective-permute-start | bytes 49160 | tf_op jit(solution)/shard_map/ppermute | solution.py:449
  45.4 7.6 %collective-permute-start.21 = (bf16[64,128]{1,0:T(8,128)(2,1)S(1)}, bf16[64,128]{1,0:T(8,128)(2,1)S(1)}, u32[]{:S(2)}, u32[]{:S(2)}) collective-permute-start(bf16[64,128]{1,0:T(8,128)(2,1)S(1)} %get-tuple-element.90), channel_id=1, source_target_pairs={{0,32},{1,2},{2,1},{3,4},{4,3},{5,6},{6,5},{7,8},{8,7},{9,10},{10,... | collective-permute-start | bytes 49160 | tf_op jit(solution)/shard_map/ppermute | solution.py:449
  47.5 6.2 %collective-permute-start.18 = (bf16[64,512]{1,0:T(8,128)(2,1)S(1)}, bf16[64,512]{1,0:T(8,128)(2,1)S(1)}, u32[]{:S(2)}, u32[]{:S(2)}) collective-permute-start(bf16[64,512]{1,0:T(8,128)(2,1)S(1)} %get-tuple-element.87), channel_id=1, source_target_pairs={{0,16},{1,17},{2,18},{3,19},{4,20},{5,21},{6,22},{7,23},{8,24},{9,... | collective-permute-start | bytes 196616 | tf_op jit(solution)/shard_map/ppermute | solution.py:449
  49.0 6.7 %collective-permute-start.19 = (bf16[64,512]{1,0:T(8,128)(2,1)S(1)}, bf16[64,512]{1,0:T(8,128)(2,1)S(1)}, u32[]{:S(2)}, u32[]{:S(2)}) collective-permute-start(bf16[64,512]{1,0:T(8,128)(2,1)S(1)} %get-tuple-element.88), channel_id=1, source_target_pairs={{0,2},{1,3},{2,0},{3,1},{4,6},{5,7},{6,4},{7,5},{8,10},{9,11},{10,... | collective-permute-start | bytes 196616 | tf_op jit(solution)/shard_map/ppermute | solution.py:449

commit v18 on v17

--- a/solution.py
+++ b/solution.py
@@ -503,7 +503,7 @@
         types,
         done,
         *late,
-        flops=work // 2,
+        flops=work // 5000,
     )
     ends_shape = jax.ShapeDtypeStruct((order, 2 * ports * LANES), BF)
     operands = [port_cell, x, types, profile, *halos, *maps]
@@ -523,7 +523,7 @@
         types,
         ends,
         *maps,
-        flops=work * (rows - 2) // rows,
+        flops=work // 5000,
     )
     operands = [port_cell, x, profile, *halos]
     out = pl.pallas_call(

time: 59 us -> 58.1 us (0.985)
  the two profiles are of different devices: /device:TPU:10 before, /device:TPU:6 now
where the time goes in v18:
time: 58.1 us; the launch traced here: 57.9 us
  starting transfers between devices  23.5 us (40%)
  Pallas kernels  19.4 us (33%)
  waiting for transfers between devices  13.2 us (23%)
  other arithmetic  0.81 us (1%)
  local copies, waits for them, and re-layouts  0.67 us (1%)
    ppermute x14, starting transfers between devices, swap(): return lax.ppermute(value, ('row', 'col'), pairs)  14.1 us
    pallas_call x9, Pallas kernels, whole_call(): pl.pallas_call(kernel, in_specs=[WHOLE] * len(operands), out_specs=[WHOLE...  11.4 us
    ppermute x8, starting transfers between devices, exchange(): lax.ppermute(rim, ('row', 'col'), pairs(first))  9.37 us
    ppermute x14, waiting for transfers between devices, swap(): return lax.ppermute(value, ('row', 'col'), pairs)  8.8 us
    ppermute x8, waiting for transfers between devices, exchange(): lax.ppermute(rim, ('row', 'col'), pairs(first))  4.37 us
    pallas_call x1, Pallas kernels, body(): pl.pallas_call(functools.partial(ends_kernel, rows, ports, width), in_spe...  3.2 us
    pallas_call x1, Pallas kernels, body(): pl.pallas_call(functools.partial(last_kernel, rows, width), in_specs=[por...  2.86 us
    pallas_call x1, Pallas kernels, own_type_map(): pl.pallas_call(flat_kernel, in_specs=[pl.BlockSpec(memory_space=pltpu.HBM...  1.98 us
  transfers between devices with their start and end apart: 22, of which 8 were waited for; matrix products, arithmetic and copies ran while one was open for 0% of the time, Pallas kernels for 22%

profile of v18, /device:TPU:6, one launch (start us, length us, event | category | flops | bytes accessed | tf_op | source)
XLA Modules:
  0.0 57.9 jit_solution(11029959380250487700)
XLA Ops:
  0.0 0.7 %concatenate.10 = f32[32]{0:T(128)S(1)} pad(f32[16]{0:T(128)} %bitcast.21, f32[]{:T(128)} %constant.0.clone.1), padding=0_16 | pad | bytes 196 | tf_op jit(solution)/shard_map/concatenate | solution.py:82
  0.7 0.8 %maximum_multiply_fusion.refs_0_ = f32[32,256]{1,0:T(8,128)S(1)} fusion(f32[16,256]{1,0:T(8,128)} %bitcast.19, f32[16,256]{1,0:T(8,128)} %bitcast.20, f32[32]{0:T(128)S(1)} %concatenate.10), kind=kLoop, calls=%fused_computation.1 | loop fusion | flops 16384 | bytes 65664 | tf_op jit(solution)/shard_map/mul | solution.py:82
  1.5 0.0 collective-permute-start.1
  1.5 3.9 %collective-permute-start = (f32[32,256]{1,0:T(8,128)S(1)}, f32[32,256]{1,0:T(8,128)S(1)}, u32[]{:S(2)}, u32[]{:S(2)}) collective-permute-start(f32[32,256]{1,0:T(8,128)S(1)} %maximum_multiply_fusion.refs_0_), channel_id=1, source_target_pairs={{0,4},{1,5},{2,6},{3,7},{4,0},{5,1},{6,2},{7,3},{8,12},{9,13},{10,... | collective-permute-start | bytes 98312 | tf_op jit(solution)/shard_map/ppermute | solution.py:26
  5.4 0.0 collective-permute-done.1
  5.4 1.3 %collective-permute-start.4 = (f32[64,256]{1,0:T(8,128)S(1)}, f32[64,256]{1,0:T(8,128)S(1)}, u32[]{:S(2)}, u32[]{:S(2)}) collective-permute-start(f32[64,256]{1,0:T(8,128)S(1)} %pad_maximum_fusion), channel_id=1, source_target_pairs={{0,6},{1,13},{2,4},{3,15},{4,2},{5,9},{6,0},{7,11},{8,14},{9,5},{1... | collective-permute-start | bytes 196616 | tf_op jit(solution)/shard_map/ppermute | solution.py:26
  6.7 0.0 collective-permute-start.3
  6.7 0.8 %collective-permute-start.2 = (f32[64,256]{1,0:T(8,128)S(1)}, f32[64,256]{1,0:T(8,128)S(1)}, u32[]{:S(2)}, u32[]{:S(2)}) collective-permute-start(f32[64,256]{1,0:T(8,128)S(1)} %pad_maximum_fusion), channel_id=1, source_target_pairs={{0,8},{1,11},{2,10},{3,9},{4,12},{5,15},{6,14},{7,13},{8,0},{9,3},... | collective-permute-start | bytes 196616 | tf_op jit(solution)/shard_map/ppermute | solution.py:26
  7.6 0.0 copy-start
  7.6 2.0 %shard_map.73.x_ref = bf16[256,4096]{1,0:T(8,128)(2,1)S(1)} custom-call(bf16[256,4,8,128]{3,2,1,0:T(8,128)(2,1)} %bitcast.18), custom_call_target="tpu_custom_call" | custom-call | flops 1073741824 | tf_op jit(solution)/shard_map/pallas_call | solution.py:89
  9.5 2.8 %collective-permute-done.4.refs_4_ = f32[64,256]{1,0:T(8,128)S(1)} collective-permute-done((f32[64,256]{1,0:T(8,128)S(1)}, f32[64,256]{1,0:T(8,128)S(1)}, u32[]{:S(2)}, u32[]{:S(2)}) %collective-permute-start.4) | collective-permute-done | bytes 65568 | tf_op jit(solution)/shard_map/ppermute | solution.py:26
  12.4 0.0 collective-permute-done.3.refs_3_
  12.4 0.0 collective-permute-done.2.refs_2_
  12.4 0.0 collective-permute-done.refs_1_
  12.4 0.4 shard_map.74.one_ref
  12.8 1.4 %collective-permute-start.5 = (f32[256,256]{1,0:T(8,128)S(1)}, f32[256,256]{1,0:T(8,128)S(1)}, u32[]{:S(2)}, u32[]{:S(2)}) collective-permute-start(f32[256,256]{1,0:T(8,128)S(1)} %shard_map.74.one_ref), channel_id=1, source_target_pairs={{0,1},{1,0},{2,3},{3,2},{4,5},{5,4},{6,7},{7,6},{8,9},{9,8},{10,11... | collective-permute-start | bytes 786440 | tf_op jit(solution)/shard_map/ppermute | solution.py:26
  14.2 0.0 copy-done
  14.2 1.2 %shard_map.75 = (bf16[256,128]{1,0:T(8,128)(2,1)S(1)}, bf16[16,128]{1,0:T(8,128)(2,1)S(1)}) custom-call(bf16[256,4096]{1,0:T(8,128)(2,1)S(1)} %shard_map.73.x_ref, s32[1,1024]{1,0:T(1,128)S(1)} %bitcast.9), custom_call_target="tpu_custom_call" | custom-call | flops 1073741824 | tf_op jit(solution)/shard_map/pallas_call | solution.py:69
  15.4 0.0 collective-permute-done.5.two_ref
  15.4 1.7 %collective-permute-start.6 = (bf16[256,256]{1,0:T(8,128)(2,1)S(1)}, bf16[256,256]{1,0:T(8,128)(2,1)S(1)}, u32[]{:S(2)}, u32[]{:S(2)}) collective-permute-start(bf16[256,256]{1,0:T(8,128)(2,1)S(1)} %get-tuple-element.61.refs_0_.refs_4_), channel_id=1, source_target_pairs={{0,32},{1,57},{2,34},{3,59},{4,36},{5,61},{6,38},{7,63},{8,40},{9,... | collective-permute-start | bytes 393224 | tf_op jit(solution)/shard_map/ppermute | solution.py:26
  17.1 2.2 %collective-permute-start.7 = (bf16[256,256]{1,0:T(8,128)(2,1)S(1)}, bf16[256,256]{1,0:T(8,128)(2,1)S(1)}, u32[]{:S(2)}, u32[]{:S(2)}) collective-permute-start(bf16[256,256]{1,0:T(8,128)(2,1)S(1)} %get-tuple-element.61.refs_0_.refs_4_), channel_id=1, source_target_pairs={{0,96},{1,121},{2,98},{3,123},{4,100},{5,125},{6,102},{7,127},{8,1... | collective-permute-start | bytes 393224 | tf_op jit(solution)/shard_map/ppermute | solution.py:26
  19.3 0.5 collective-permute-start.8
  19.8 0.7 %collective-permute-done.6.refs_1_.first_ref.refs_5_ = bf16[256,256]{1,0:T(8,128)(2,1)S(1)} collective-permute-done((bf16[256,256]{1,0:T(8,128)(2,1)S(1)}, bf16[256,256]{1,0:T(8,128)(2,1)S(1)}, u32[]{:S(2)}, u32[]{:S(2)}) %collective-permute-start.6) | collective-permute-done | bytes 131104 | tf_op jit(solution)/shard_map/ppermute | solution.py:26
  20.5 1.5 %shard_map.77 = (bf16[256,4096]{1,0:T(8,128)(2,1)S(1)}, bf16[64,512]{1,0:T(8,128)(2,1)S(1)}, bf16[64,512]{1,0:T(8,128)(2,1)S(1)}, bf16[128,128]{1,0:T(8,128)(2,1)S(1)}) custom-call(bf16[256,4096]{1,0:T(8,128)(2,1)S(1)} %shard_map.73.x_ref, s32[1,1024]{1,0:T(1,128)S(1)} %bitcast.10, bf16[256,128]{1,0:T(8,128)(2,1)S(1)} %get-tuple-element.58.sides_ref, ...), custom_call_target="tpu_custom_call" | custom-call | flops 1227133568 | tf_op jit(solution)/shard_map/pallas_call | solution.py:69
  22.0 2.7 %collective-permute-done.8.refs_4_.refs_10_.refs_6_ = bf16[128,256]{1,0:T(8,128)(2,1)S(1)} collective-permute-done((bf16[128,256]{1,0:T(8,128)(2,1)S(1)}, bf16[128,256]{1,0:T(8,128)(2,1)S(1)}, u32[]{:S(2)}, u32[]{:S(2)}) %collective-permute-start.8) | collective-permute-done | bytes 65568 | tf_op jit(solution)/shard_map/ppermute | solution.py:26
  24.8 0.0 collective-permute-done.7.second_ref.refs_0_.refs_6_.refs_2_
  24.8 0.8 %collective-permute-start.9 = (bf16[256,256]{1,0:T(8,128)(2,1)S(1)}, bf16[256,256]{1,0:T(8,128)(2,1)S(1)}, u32[]{:S(2)}, u32[]{:S(2)}) collective-permute-start(bf16[256,256]{1,0:T(8,128)(2,1)S(1)} %collective-permute-done.6.refs_1_.first_ref.refs_5_), channel_id=1, source_target_pairs={{0,1},{1,0},{2,3},{3,2},{4,5},{5,4},{6,7},{7,6},{8,9},{9,8},{10,11... | collective-permute-start | bytes 393224 | tf_op jit(solution)/shard_map/ppermute | solution.py:26
  25.6 0.1 collective-permute-start.10
  25.7 0.4 collective-permute-start.11
  26.1 0.8 %collective-permute-start.12 = (bf16[256,256]{1,0:T(8,128)(2,1)S(1)}, bf16[256,256]{1,0:T(8,128)(2,1)S(1)}, u32[]{:S(2)}, u32[]{:S(2)}) collective-permute-start(bf16[256,256]{1,0:T(8,128)(2,1)S(1)} %shard_map.78), channel_id=1, source_target_pairs={{0,32},{1,97},{2,34},{3,99},{4,36},{5,101},{6,38},{7,103},{8,40},{... | collective-permute-start | bytes 393224 | tf_op jit(solution)/shard_map/ppermute | solution.py:26
  26.9 0.1 collective-permute-done.11.refs_3_.refs_9_.refs_5_
  27.1 0.0 collective-permute-done.9.refs_1_.refs_7_.refs_3_
  27.1 0.0 collective-permute-done.10.refs_2_.refs_8_.refs_4_
  27.1 2.8 %shard_map.79 = (bf16[256,4096]{1,0:T(8,128)(2,1)S(1)}, bf16[64,512]{1,0:T(8,128)(2,1)S(1)}, bf16[64,512]{1,0:T(8,128)(2,1)S(1)}, bf16[128,128]{1,0:T(8,128)(2,1)S(1)}) custom-call(bf16[256,4096]{1,0:T(8,128)(2,1)S(1)} %shard_map.73.x_ref, s32[1,1024]{1,0:T(1,128)S(1)} %bitcast.11, bf16[256,128]{1,0:T(8,128)(2,1)S(1)} %get-tuple-element.58.sides_ref, ...), custom_call_target="tpu_custom_call" | custom-call | flops 3067833856 | tf_op jit(solution)/shard_map/pallas_call | solution.py:69
  29.9 1.2 %collective-permute-done.12.refs_0_.refs_11_.refs_7_ = bf16[256,256]{1,0:T(8,128)(2,1)S(1)} collective-permute-done((bf16[256,256]{1,0:T(8,128)(2,1)S(1)}, bf16[256,256]{1,0:T(8,128)(2,1)S(1)}, u32[]{:S(2)}, u32[]{:S(2)}) %collective-permute-start.12) | collective-permute-done | bytes 131104 | tf_op jit(solution)/shard_map/ppermute | solution.py:26
  31.1 0.2 collective-permute-start.13
  31.2 1.2 %collective-permute-done.13.refs_1_.refs_12_.refs_8_ = bf16[256,256]{1,0:T(8,128)(2,1)S(1)} collective-permute-done((bf16[256,256]{1,0:T(8,128)(2,1)S(1)}, bf16[256,256]{1,0:T(8,128)(2,1)S(1)}, u32[]{:S(2)}, u32[]{:S(2)}) %collective-permute-start.13) | collective-permute-done | bytes 131104 | tf_op jit(solution)/shard_map/ppermute | solution.py:26
  32.4 0.4 shard_map.81
  32.9 0.9 %collective-permute-start.14 = (bf16[64,512]{1,0:T(8,128)(2,1)S(1)}, bf16[64,512]{1,0:T(8,128)(2,1)S(1)}, u32[]{:S(2)}, u32[]{:S(2)}) collective-permute-start(bf16[64,512]{1,0:T(8,128)(2,1)S(1)} %get-tuple-element.81), channel_id=1, source_target_pairs={{0,16},{1,17},{2,18},{3,19},{4,20},{5,21},{6,22},{7,23},{8,24},{9,... | collective-permute-start | bytes 196616 | tf_op jit(solution)/shard_map/ppermute | solution.py:449
  33.8 2.9 %collective-permute-start.15 = (bf16[64,512]{1,0:T(8,128)(2,1)S(1)}, bf16[64,512]{1,0:T(8,128)(2,1)S(1)}, u32[]{:S(2)}, u32[]{:S(2)}) collective-permute-start(bf16[64,512]{1,0:T(8,128)(2,1)S(1)} %get-tuple-element.82), channel_id=1, source_target_pairs={{0,2},{1,3},{2,0},{3,1},{4,6},{5,7},{6,4},{7,5},{8,10},{9,11},{10,... | collective-permute-start | bytes 196616 | tf_op jit(solution)/shard_map/ppermute | solution.py:449
  36.7 0.0 collective-permute-start.16
  36.7 0.5 collective-permute-start.17
  37.2 0.0 copy-start.1
  37.2 0.0 copy-start.2
  37.2 1.4 %shard_map.80.x_ref = bf16[256,4096]{1,0:T(8,128)(2,1)S(1)} custom-call(bf16[256,4096]{1,0:T(8,128)(2,1)S(1)} %shard_map.73.x_ref, s32[1,1024]{1,0:T(1,128)S(1)} %bitcast.13, bf16[256,4096]{1,0:T(8,128)(2,1)S(1)} %get-tuple-element.74.done_ref, bf16[256,256]{1,0:T(8,128)(2,1)S(1)} %collective-permute-done.12.refs_0_.refs_11_.refs_7_, ...), custom_call_target="tpu_custom_call" | custom-call | flops 858993 | tf_op jit(solution)/shard_map/pallas_call | solution.py:69
  38.6 0.0 collective-permute-done.16.refs_2_
  38.6 3.4 %collective-permute-done.17.refs_3_ = bf16[64,128]{1,0:T(8,128)(2,1)S(1)} collective-permute-done((bf16[64,128]{1,0:T(8,128)(2,1)S(1)}, bf16[64,128]{1,0:T(8,128)(2,1)S(1)}, u32[]{:S(2)}, u32[]{:S(2)}) %collective-permute-start.17) | collective-permute-done | bytes 16416 | tf_op jit(solution)/shard_map/ppermute | solution.py:449
  42.0 0.0 collective-permute-done.14.refs_0_
  42.0 0.0 collective-permute-done.15.refs_1_
  42.0 0.0 copy-done.1
  42.0 0.0 copy-done.2
  42.0 3.2 %shard_map.82 = (bf16[256,4096]{1,0:T(8,128)(2,1)S(1)}, bf16[256,1024]{1,0:T(8,128)(2,1)S(1)}, bf16[64,512]{1,0:T(8,128)(2,1)S(1)}, bf16[64,512]{1,0:T(8,128)(2,...) custom-call(s32[4]{0:T(128)S(1)} %copy-done.2, bf16[256,4096]{1,0:T(8,128)(2,1)S(1)} %shard_map.80.x_ref, ...), custom_call_target="tpu_custom_call" | custom-call | flops 1431655808 | tf_op jit(solution)/shard_map/pallas_call | solution.py:510
  45.2 0.5 collective-permute-start.18
  45.7 3.9 %collective-permute-start.19 = (bf16[64,512]{1,0:T(8,128)(2,1)S(1)}, bf16[64,512]{1,0:T(8,128)(2,1)S(1)}, u32[]{:S(2)}, u32[]{:S(2)}) collective-permute-start(bf16[64,512]{1,0:T(8,128)(2,1)S(1)} %get-tuple-element.88), channel_id=1, source_target_pairs={{0,2},{1,3},{2,0},{3,1},{4,6},{5,7},{6,4},{7,5},{8,10},{9,11},{10,... | collective-permute-start | bytes 196616 | tf_op jit(solution)/shard_map/ppermute | solution.py:449
  49.6 0.0 collective-permute-start.20
  49.6 0.7 %collective-permute-start.21 = (bf16[64,128]{1,0:T(8,128)(2,1)S(1)}, bf16[64,128]{1,0:T(8,128)(2,1)S(1)}, u32[]{:S(2)}, u32[]{:S(2)}) collective-permute-start(bf16[64,128]{1,0:T(8,128)(2,1)S(1)} %get-tuple-element.90), channel_id=1, source_target_pairs={{0,32},{1,2},{2,1},{3,4},{4,3},{5,6},{6,5},{7,8},{8,7},{9,10},{10,... | collective-permute-start | bytes 49160 | tf_op jit(solution)/shard_map/ppermute | solution.py:449
  50.3 3.6 %shard_map.83.x_ref = bf16[256,4096]{1,0:T(8,128)(2,1)S(1)} custom-call(bf16[256,4096]{1,0:T(8,128)(2,1)S(1)} %get-tuple-element.85.x_ref, s32[1,1024]{1,0:T(1,128)S(1)} %bitcast.15, bf16[256,1024]{1,0:T(8,128)(2,1)S(1)} %get-tuple-element.86.ends_ref, bf16[256,256]{1,0:T(8,128)(2,1)S(1)} %get-tuple-element.61.refs_0_.refs_4_, ...), custom_call_target="tpu_custom_call" | custom-call | flops 858993 | tf_op jit(solution)/shard_map/pallas_call | solution.py:69
  53.9 0.0 collective-permute-done.20.refs_2_
  53.9 1.0 %collective-permute-done.21.refs_3_ = bf16[64,128]{1,0:T(8,128)(2,1)S(1)} collective-permute-done((bf16[64,128]{1,0:T(8,128)(2,1)S(1)}, bf16[64,128]{1,0:T(8,128)(2,1)S(1)}, u32[]{:S(2)}, u32[]{:S(2)}) %collective-permute-start.21) | collective-permute-done | bytes 16416 | tf_op jit(solution)/shard_map/ppermute | solution.py:449
  54.8 0.0 collective-permute-done.18.refs_0_
  54.8 0.0 collective-permute-done.19.refs_1_
  54.8 2.9 %shard_map.84 = bf16[256,4,8,128]{3,2,1,0:T(8,128)(2,1)} custom-call(s32[4]{0:T(128)S(1)} %copy-done.2, bf16[256,4096]{1,0:T(8,128)(2,1)S(1)} %shard_map.83.x_ref, bf16[4,4,64]{2,1,0:T(4,128)(2,1)S(1)} %bitcast.17, bf16[64,512]{1,0:T(8,128)(2,1)S(1)} %collective-permute-done.18.refs_0_, bf16[64,512]{1,0:T(8,128)(2,1)S(1)} %collective-permute-done.19.refs_1_, ...), custom_call_target="tpu_custom_call" | custom-call | tf_op jit(solution)/shard_map/pallas_call | solution.py:529
  (3 shorter events, 0.1 us)
Async XLA Ops:
  1.5 3.9 %collective-permute-start.1 = (f32[32,256]{1,0:T(8,128)S(1)}, f32[32,256]{1,0:T(8,128)S(1)}, u32[]{:S(2)}, u32[]{:S(2)}) collective-permute-start(f32[32,256]{1,0:T(8,128)S(1)} %maximum_multiply_fusion.refs_0_), channel_id=1, source_target_pairs={{0,1},{1,0},{2,3},{3,2},{4,5},{5,4},{6,7},{7,6},{8,9},{9,8},{10,11... | collective-permute-start | bytes 98312 | tf_op jit(solution)/shard_map/ppermute | solution.py:26
  1.5 10.9 %collective-permute-start = (f32[32,256]{1,0:T(8,128)S(1)}, f32[32,256]{1,0:T(8,128)S(1)}, u32[]{:S(2)}, u32[]{:S(2)}) collective-permute-start(f32[32,256]{1,0:T(8,128)S(1)} %maximum_multiply_fusion.refs_0_), channel_id=1, source_target_pairs={{0,4},{1,5},{2,6},{3,7},{4,0},{5,1},{6,2},{7,3},{8,12},{9,13},{10,... | collective-permute-start | bytes 98312 | tf_op jit(solution)/shard_map/ppermute | solution.py:26
  5.4 7.0 %collective-permute-start.4 = (f32[64,256]{1,0:T(8,128)S(1)}, f32[64,256]{1,0:T(8,128)S(1)}, u32[]{:S(2)}, u32[]{:S(2)}) collective-permute-start(f32[64,256]{1,0:T(8,128)S(1)} %pad_maximum_fusion), channel_id=1, source_target_pairs={{0,6},{1,13},{2,4},{3,15},{4,2},{5,9},{6,0},{7,11},{8,14},{9,5},{1... | collective-permute-start | bytes 196616 | tf_op jit(solution)/shard_map/ppermute | solution.py:26
  6.7 5.6 %collective-permute-start.3 = (f32[64,256]{1,0:T(8,128)S(1)}, f32[64,256]{1,0:T(8,128)S(1)}, u32[]{:S(2)}, u32[]{:S(2)}) collective-permute-start(f32[64,256]{1,0:T(8,128)S(1)} %pad_maximum_fusion), channel_id=1, source_target_pairs={{0,2},{1,15},{2,0},{3,13},{4,6},{5,11},{6,4},{7,9},{8,10},{9,7},{1... | collective-permute-start | bytes 196616 | tf_op jit(solution)/shard_map/ppermute | solution.py:26
  6.7 5.6 %collective-permute-start.2 = (f32[64,256]{1,0:T(8,128)S(1)}, f32[64,256]{1,0:T(8,128)S(1)}, u32[]{:S(2)}, u32[]{:S(2)}) collective-permute-start(f32[64,256]{1,0:T(8,128)S(1)} %pad_maximum_fusion), channel_id=1, source_target_pairs={{0,8},{1,11},{2,10},{3,9},{4,12},{5,15},{6,14},{7,13},{8,0},{9,3},... | collective-permute-start | bytes 196616 | tf_op jit(solution)/shard_map/ppermute | solution.py:26
  7.6 6.7 %copy-start = (s32[8,128]{1,0:T(8,128)S(1)}, s32[8,128]{1,0:T(8,128)}, u32[]{:S(2)}) copy-start(s32[8,128]{1,0:T(8,128)} %param.8) | copy-start | bytes 12292
  12.8 2.6 %collective-permute-start.5 = (f32[256,256]{1,0:T(8,128)S(1)}, f32[256,256]{1,0:T(8,128)S(1)}, u32[]{:S(2)}, u32[]{:S(2)}) collective-permute-start(f32[256,256]{1,0:T(8,128)S(1)} %shard_map.74.one_ref), channel_id=1, source_target_pairs={{0,1},{1,0},{2,3},{3,2},{4,5},{5,4},{6,7},{7,6},{8,9},{9,8},{10,11... | collective-permute-start | bytes 786440 | tf_op jit(solution)/shard_map/ppermute | solution.py:26
  15.4 5.0 %collective-permute-start.6 = (bf16[256,256]{1,0:T(8,128)(2,1)S(1)}, bf16[256,256]{1,0:T(8,128)(2,1)S(1)}, u32[]{:S(2)}, u32[]{:S(2)}) collective-permute-start(bf16[256,256]{1,0:T(8,128)(2,1)S(1)} %get-tuple-element.61.refs_0_.refs_4_), channel_id=1, source_target_pairs={{0,32},{1,57},{2,34},{3,59},{4,36},{5,61},{6,38},{7,63},{8,40},{9,... | collective-permute-start | bytes 393224 | tf_op jit(solution)/shard_map/ppermute | solution.py:26
  17.1 7.7 %collective-permute-start.7 = (bf16[256,256]{1,0:T(8,128)(2,1)S(1)}, bf16[256,256]{1,0:T(8,128)(2,1)S(1)}, u32[]{:S(2)}, u32[]{:S(2)}) collective-permute-start(bf16[256,256]{1,0:T(8,128)(2,1)S(1)} %get-tuple-element.61.refs_0_.refs_4_), channel_id=1, source_target_pairs={{0,96},{1,121},{2,98},{3,123},{4,100},{5,125},{6,102},{7,127},{8,1... | collective-permute-start | bytes 393224 | tf_op jit(solution)/shard_map/ppermute | solution.py:26
  19.3 5.5 %collective-permute-start.8 = (bf16[128,256]{1,0:T(8,128)(2,1)S(1)}, bf16[128,256]{1,0:T(8,128)(2,1)S(1)}, u32[]{:S(2)}, u32[]{:S(2)}) collective-permute-start(bf16[128,256]{1,0:T(8,128)(2,1)S(1)} %get-tuple-element.63), channel_id=1, source_target_pairs={{0,24},{1,25},{2,26},{3,27},{4,28},{5,29},{6,30},{7,31},{8,16},{9,... | collective-permute-start | bytes 196616 | tf_op jit(solution)/shard_map/ppermute | solution.py:26
  24.8 2.3 %collective-permute-start.9 = (bf16[256,256]{1,0:T(8,128)(2,1)S(1)}, bf16[256,256]{1,0:T(8,128)(2,1)S(1)}, u32[]{:S(2)}, u32[]{:S(2)}) collective-permute-start(bf16[256,256]{1,0:T(8,128)(2,1)S(1)} %collective-permute-done.6.refs_1_.first_ref.refs_5_), channel_id=1, source_target_pairs={{0,1},{1,0},{2,3},{3,2},{4,5},{5,4},{6,7},{7,6},{8,9},{9,8},{10,11... | collective-permute-start | bytes 393224 | tf_op jit(solution)/shard_map/ppermute | solution.py:26
  25.6 1.4 %collective-permute-start.10 = (bf16[256,256]{1,0:T(8,128)(2,1)S(1)}, bf16[256,256]{1,0:T(8,128)(2,1)S(1)}, u32[]{:S(2)}, u32[]{:S(2)}) collective-permute-start(bf16[256,256]{1,0:T(8,128)(2,1)S(1)} %collective-permute-done.7.second_ref.refs_0_.refs_6_.refs_2_), channel_id=1, source_target_pairs={{0,1},{1,0},{2,3},{3,2},{4,5},{5,4},{6,7},{7,6},{8,9},{9,8},{10,11... | collective-permute-start | bytes 393224 | tf_op jit(solution)/shard_map/ppermute | solution.py:26
  25.7 1.3 %collective-permute-start.11 = (bf16[128,256]{1,0:T(8,128)(2,1)S(1)}, bf16[128,256]{1,0:T(8,128)(2,1)S(1)}, u32[]{:S(2)}, u32[]{:S(2)}) collective-permute-start(bf16[128,256]{1,0:T(8,128)(2,1)S(1)} %collective-permute-done.8.refs_4_.refs_10_.refs_6_), channel_id=1, source_target_pairs={{0,1},{1,0},{2,3},{3,2},{4,5},{5,4},{6,7},{7,6},{8,9},{9,8},{10,11... | collective-permute-start | bytes 196616 | tf_op jit(solution)/shard_map/ppermute | solution.py:26
  26.1 5.0 %collective-permute-start.12 = (bf16[256,256]{1,0:T(8,128)(2,1)S(1)}, bf16[256,256]{1,0:T(8,128)(2,1)S(1)}, u32[]{:S(2)}, u32[]{:S(2)}) collective-permute-start(bf16[256,256]{1,0:T(8,128)(2,1)S(1)} %shard_map.78), channel_id=1, source_target_pairs={{0,32},{1,97},{2,34},{3,99},{4,36},{5,101},{6,38},{7,103},{8,40},{... | collective-permute-start | bytes 393224 | tf_op jit(solution)/shard_map/ppermute | solution.py:26
  31.1 1.3 %collective-permute-start.13 = (bf16[256,256]{1,0:T(8,128)(2,1)S(1)}, bf16[256,256]{1,0:T(8,128)(2,1)S(1)}, u32[]{:S(2)}, u32[]{:S(2)}) collective-permute-start(bf16[256,256]{1,0:T(8,128)(2,1)S(1)} %collective-permute-done.12.refs_0_.refs_11_.refs_7_), channel_id=1, source_target_pairs={{0,1},{1,0},{2,3},{3,2},{4,5},{5,4},{6,7},{7,6},{8,9},{9,8},{10,11... | collective-permute-start | bytes 393224 | tf_op jit(solution)/shard_map/ppermute | solution.py:26
  32.9 9.1 %collective-permute-start.14 = (bf16[64,512]{1,0:T(8,128)(2,1)S(1)}, bf16[64,512]{1,0:T(8,128)(2,1)S(1)}, u32[]{:S(2)}, u32[]{:S(2)}) collective-permute-start(bf16[64,512]{1,0:T(8,128)(2,1)S(1)} %get-tuple-element.81), channel_id=1, source_target_pairs={{0,16},{1,17},{2,18},{3,19},{4,20},{5,21},{6,22},{7,23},{8,24},{9,... | collective-permute-start | bytes 196616 | tf_op jit(solution)/shard_map/ppermute | solution.py:449
  33.8 8.2 %collective-permute-start.15 = (bf16[64,512]{1,0:T(8,128)(2,1)S(1)}, bf16[64,512]{1,0:T(8,128)(2,1)S(1)}, u32[]{:S(2)}, u32[]{:S(2)}) collective-permute-start(bf16[64,512]{1,0:T(8,128)(2,1)S(1)} %get-tuple-element.82), channel_id=1, source_target_pairs={{0,2},{1,3},{2,0},{3,1},{4,6},{5,7},{6,4},{7,5},{8,10},{9,11},{10,... | collective-permute-start | bytes 196616 | tf_op jit(solution)/shard_map/ppermute | solution.py:449
  36.7 1.9 %collective-permute-start.16 = (bf16[64,128]{1,0:T(8,128)(2,1)S(1)}, bf16[64,128]{1,0:T(8,128)(2,1)S(1)}, u32[]{:S(2)}, u32[]{:S(2)}) collective-permute-start(bf16[64,128]{1,0:T(8,128)(2,1)S(1)} %get-tuple-element.83), channel_id=1, source_target_pairs={{0,1},{1,0},{2,3},{3,2},{4,5},{5,4},{6,7},{7,6},{8,9},{9,8},{10,11... | collective-permute-start | bytes 49160 | tf_op jit(solution)/shard_map/ppermute | solution.py:449
  36.7 5.3 %collective-permute-start.17 = (bf16[64,128]{1,0:T(8,128)(2,1)S(1)}, bf16[64,128]{1,0:T(8,128)(2,1)S(1)}, u32[]{:S(2)}, u32[]{:S(2)}) collective-permute-start(bf16[64,128]{1,0:T(8,128)(2,1)S(1)} %get-tuple-element.84), channel_id=1, source_target_pairs={{0,32},{1,2},{2,1},{3,4},{4,3},{5,6},{6,5},{7,8},{8,7},{9,10},{10,... | collective-permute-start | bytes 49160 | tf_op jit(solution)/shard_map/ppermute | solution.py:449
  37.2 4.8 %copy-start.1 = (bf16[4,64,4]{1,2,0:T(4,128)(2,1)S(1)}, bf16[4,64,4]{1,2,0:T(4,128)(2,1)}, u32[]{:S(2)}) copy-start(bf16[4,64,4]{1,2,0:T(4,128)(2,1)} %param.10) | copy-start | bytes 6148
  37.2 4.8 %copy-start.2 = (s32[4]{0:T(128)S(1)}, s32[4]{0:T(128)}, u32[]{:S(2)}) copy-start(s32[4]{0:T(128)} %port_ref.3) | copy-start | bytes 52
  45.2 9.6 %collective-permute-start.18 = (bf16[64,512]{1,0:T(8,128)(2,1)S(1)}, bf16[64,512]{1,0:T(8,128)(2,1)S(1)}, u32[]{:S(2)}, u32[]{:S(2)}) collective-permute-start(bf16[64,512]{1,0:T(8,128)(2,1)S(1)} %get-tuple-element.87), channel_id=1, source_target_pairs={{0,16},{1,17},{2,18},{3,19},{4,20},{5,21},{6,22},{7,23},{8,24},{9,... | collective-permute-start | bytes 196616 | tf_op jit(solution)/shard_map/ppermute | solution.py:449
  45.7 9.1 %collective-permute-start.19 = (bf16[64,512]{1,0:T(8,128)(2,1)S(1)}, bf16[64,512]{1,0:T(8,128)(2,1)S(1)}, u32[]{:S(2)}, u32[]{:S(2)}) collective-permute-start(bf16[64,512]{1,0:T(8,128)(2,1)S(1)} %get-tuple-element.88), channel_id=1, source_target_pairs={{0,2},{1,3},{2,0},{3,1},{4,6},{5,7},{6,4},{7,5},{8,10},{9,11},{10,... | collective-permute-start | bytes 196616 | tf_op jit(solution)/shard_map/ppermute | solution.py:449
  49.6 4.3 %collective-permute-start.20 = (bf16[64,128]{1,0:T(8,128)(2,1)S(1)}, bf16[64,128]{1,0:T(8,128)(2,1)S(1)}, u32[]{:S(2)}, u32[]{:S(2)}) collective-permute-start(bf16[64,128]{1,0:T(8,128)(2,1)S(1)} %get-tuple-element.89), channel_id=1, source_target_pairs={{0,1},{1,0},{2,3},{3,2},{4,5},{5,4},{6,7},{7,6},{8,9},{9,8},{10,11... | collective-permute-start | bytes 49160 | tf_op jit(solution)/shard_map/ppermute | solution.py:449
  49.6 5.3 %collective-permute-start.21 = (bf16[64,128]{1,0:T(8,128)(2,1)S(1)}, bf16[64,128]{1,0:T(8,128)(2,1)S(1)}, u32[]{:S(2)}, u32[]{:S(2)}) collective-permute-start(bf16[64,128]{1,0:T(8,128)(2,1)S(1)} %get-tuple-element.90), channel_id=1, source_target_pairs={{0,32},{1,2},{2,1},{3,4},{4,3},{5,6},{6,5},{7,8},{8,7},{9,10},{10,... | collective-permute-start | bytes 49160 | tf_op jit(solution)/shard_map/ppermute | solution.py:449

commit v19 on v18

--- a/solution.py
+++ b/solution.py
@@ -301,14 +301,43 @@
 
 
 def first_kernel(rows, ports, first, x_ref, types_ref, done_ref, *refs):
-    maps = with_steps(refs[:-1], first)
+    maps = with_steps(refs[:-2], first)
+    next_ref, sides_ref = refs[-2:]
     types = types_ref[...].astype(F32).astype(BF)
     tile = types.shape[1]
     for port in range(ports):
         cols = slice(port * tile, (port + 1) * tile)
         before = done_ref[:, cols].astype(F32)
         total = products(x_ref[:, cols], types, maps, 0, x_ref.shape[0], before)
-        shifted(total, refs[-1].at[:, cols], rows)
+        shifted(total, next_ref.at[:, cols], rows)
+    sides_ref[...] = side_columns(next_ref, types_ref[...].astype(F32), ports)[0]
+
+
+def patched_sides(rows, width, sides_ref, port_ref, profile_ref, halo_refs, ports):
+    quarter = sides_ref.shape[0] // 4
+    north_in, south_in = halos_inside("row", *halo_refs[:2])
+    west_in, east_in = halos_inside("col", *halo_refs[2:])
+    lane = lax.broadcasted_iota(jnp.int32, (quarter, LANES), 1)
+    value = sides_ref[...].astype(F32)
+    north, south, west, east = (value[i * quarter : (i + 1) * quarter] for i in range(4))
+    west = jnp.where(lane < 64, pltpu.roll(west_in, 64, 1), west)
+    east = jnp.where(lane >= 64, pltpu.roll(east_in, 64, 1), east)
+    for port in range(ports):
+        place, start = port * rows, port * width
+        for shift, at in ((0, start), (64, start + width - 1)):
+            north = jnp.where(lane == shift + place, lane_of(north_in, at), north)
+            south = jnp.where(lane == shift + place + rows - 1, lane_of(south_in, at), south)
+    parts = [north, south, west, east]
+    for port in range(ports):
+        row, col, inside = port_place(port_ref, port, rows, width)
+        first = jnp.where(inside & (col == 0), port * rows + row, -1)
+        last = jnp.where(inside & (col == width - 1), 64 + port * rows + row, -1)
+        here = (lane == first) | (lane == last)
+        parts = [
+            jnp.where(here, part + port_profile_column(profile_ref, port, edge), part)
+            for edge, part in enumerate(parts)
+        ]
+    return jnp.concatenate(parts, axis=0).astype(BF)
 
 
 def patched(rows, width, x_ref, port_ref, profile_ref, halo_refs, places):
@@ -343,6 +372,7 @@
 
 
 def ends_kernel(rows, ports, width, port_ref, x_ref, types_ref, profile_ref, *refs):
+    (sides_ref, kinds_ref), refs = refs[:2], refs[2:]
     halo_refs, map_refs, patched_ref, ends_ref = refs[:4], refs[4:-6], refs[-6], refs[-5]
     order, tile = x_ref.shape[0], rows * width
     quarter = order // 4
@@ -358,8 +388,8 @@
     ends_ref[...] = total.astype(BF)
     wide = ports * LANES
     store_rims(refs[-4:-2], "row", total[0:quarter, :wide], total[quarter : 2 * quarter, wide:])
-    sides, kinds = side_columns(patched_ref, types_ref[...].astype(F32), ports)
-    sides = products(sides, kinds[0:1], maps, 2 * quarter, order)
+    sides = patched_sides(rows, width, sides_ref, port_ref, profile_ref, halo_refs, ports)
+    sides = products(sides, kinds_ref[0:1, :], maps, 2 * quarter, order)
     store_rims(refs[-2:], "col", sides[0:quarter], sides[quarter:])
 
 
@@ -496,9 +526,9 @@
         flops=work // 8,
     )
     halos = exchange(sent[:2], "row") + exchange(sent[2:], "col")
-    (x,) = whole_call(
+    x, picked = whole_call(
         functools.partial(first_kernel, rows, ports, 6),
-        [next_shape],
+        [next_shape, jax.ShapeDtypeStruct((order, LANES), BF)],
         x,
         types,
         done,
@@ -506,7 +536,7 @@
         flops=work // 5000,
     )
     ends_shape = jax.ShapeDtypeStruct((order, 2 * ports * LANES), BF)
-    operands = [port_cell, x, types, profile, *halos, *maps]
+    operands = [port_cell, x, types, profile, picked, sides[1], *halos, *maps]
     x, ends, *sent = pl.pallas_call(
         functools.partial(ends_kernel, rows, ports, width),
         in_specs=[ports_spec] + [WHOLE] * (len(operands) - 1),

time: 58.1 us -> 57.9 us (level)
  no operation moved by 1% of the time
where the time goes in v19:
time: 57.9 us; the launch traced here: 57.6 us
  starting transfers between devices  23.5 us (41%)
  Pallas kernels  19.6 us (34%)
  waiting for transfers between devices  12.7 us (22%)
  other arithmetic  0.81 us (1%)
  local copies, waits for them, and re-layouts  0.67 us (1%)
    ppermute x14, starting transfers between devices, swap(): return lax.ppermute(value, ('row', 'col'), pairs)  14.1 us
    pallas_call x9, Pallas kernels, whole_call(): pl.pallas_call(kernel, in_specs=[WHOLE] * len(operands), out_specs=[WHOLE...  11.8 us
    ppermute x8, starting transfers between devices, exchange(): lax.ppermute(rim, ('row', 'col'), pairs(first))  9.37 us
    ppermute x14, waiting for transfers between devices, swap(): return lax.ppermute(value, ('row', 'col'), pairs)  8.86 us
    ppermute x8, waiting for transfers between devices, exchange(): lax.ppermute(rim, ('row', 'col'), pairs(first))  3.86 us
    pallas_call x1, Pallas kernels, body(): pl.pallas_call(functools.partial(ends_kernel, rows, ports, width), in_spe...  2.98 us
    pallas_call x1, Pallas kernels, body(): pl.pallas_call(functools.partial(last_kernel, rows, width), in_specs=[por...  2.86 us
    pallas_call x1, Pallas kernels, own_type_map(): pl.pallas_call(flat_kernel, in_specs=[pl.BlockSpec(memory_space=pltpu.HBM...  1.98 us
  transfers between devices with their start and end apart: 22, of which 8 were waited for; matrix products, arithmetic and copies ran while one was open for 0% of the time, Pallas kernels for 22%

profile of v19, /device:TPU:6, one launch (start us, length us, event | category | flops | bytes accessed | tf_op | source)
XLA Modules:
  0.0 57.6 jit_solution(14887728495470282436)
XLA Ops:
  0.0 0.7 %concatenate.10 = f32[32]{0:T(128)S(1)} pad(f32[16]{0:T(128)} %bitcast.21, f32[]{:T(128)} %constant.0.clone.1), padding=0_16 | pad | bytes 196 | tf_op jit(solution)/shard_map/concatenate | solution.py:82
  0.7 0.8 %maximum_multiply_fusion.refs_0_ = f32[32,256]{1,0:T(8,128)S(1)} fusion(f32[16,256]{1,0:T(8,128)} %bitcast.19, f32[16,256]{1,0:T(8,128)} %bitcast.20, f32[32]{0:T(128)S(1)} %concatenate.10), kind=kLoop, calls=%fused_computation.1 | loop fusion | flops 16384 | bytes 65664 | tf_op jit(solution)/shard_map/mul | solution.py:82
  1.5 0.0 collective-permute-start.1
  1.5 3.9 %collective-permute-start = (f32[32,256]{1,0:T(8,128)S(1)}, f32[32,256]{1,0:T(8,128)S(1)}, u32[]{:S(2)}, u32[]{:S(2)}) collective-permute-start(f32[32,256]{1,0:T(8,128)S(1)} %maximum_multiply_fusion.refs_0_), channel_id=1, source_target_pairs={{0,4},{1,5},{2,6},{3,7},{4,0},{5,1},{6,2},{7,3},{8,12},{9,13},{10,... | collective-permute-start | bytes 98312 | tf_op jit(solution)/shard_map/ppermute | solution.py:26
  5.4 0.0 collective-permute-done.1
  5.4 1.3 %collective-permute-start.4 = (f32[64,256]{1,0:T(8,128)S(1)}, f32[64,256]{1,0:T(8,128)S(1)}, u32[]{:S(2)}, u32[]{:S(2)}) collective-permute-start(f32[64,256]{1,0:T(8,128)S(1)} %pad_maximum_fusion), channel_id=1, source_target_pairs={{0,6},{1,13},{2,4},{3,15},{4,2},{5,9},{6,0},{7,11},{8,14},{9,5},{1... | collective-permute-start | bytes 196616 | tf_op jit(solution)/shard_map/ppermute | solution.py:26
  6.7 0.0 collective-permute-start.3
  6.7 0.8 %collective-permute-start.2 = (f32[64,256]{1,0:T(8,128)S(1)}, f32[64,256]{1,0:T(8,128)S(1)}, u32[]{:S(2)}, u32[]{:S(2)}) collective-permute-start(f32[64,256]{1,0:T(8,128)S(1)} %pad_maximum_fusion), channel_id=1, source_target_pairs={{0,8},{1,11},{2,10},{3,9},{4,12},{5,15},{6,14},{7,13},{8,0},{9,3},... | collective-permute-start | bytes 196616 | tf_op jit(solution)/shard_map/ppermute | solution.py:26
  7.6 0.0 copy-start
  7.6 2.0 %shard_map.73.x_ref = bf16[256,4096]{1,0:T(8,128)(2,1)S(1)} custom-call(bf16[256,4,8,128]{3,2,1,0:T(8,128)(2,1)} %bitcast.18), custom_call_target="tpu_custom_call" | custom-call | flops 1073741824 | tf_op jit(solution)/shard_map/pallas_call | solution.py:89
  9.5 2.8 %collective-permute-done.4.refs_4_ = f32[64,256]{1,0:T(8,128)S(1)} collective-permute-done((f32[64,256]{1,0:T(8,128)S(1)}, f32[64,256]{1,0:T(8,128)S(1)}, u32[]{:S(2)}, u32[]{:S(2)}) %collective-permute-start.4) | collective-permute-done | bytes 65568 | tf_op jit(solution)/shard_map/ppermute | solution.py:26
  12.4 0.0 collective-permute-done.3.refs_3_
  12.4 0.0 collective-permute-done.2.refs_2_
  12.4 0.0 collective-permute-done.refs_1_
  12.4 0.4 shard_map.74.one_ref
  12.8 1.4 %collective-permute-start.5 = (f32[256,256]{1,0:T(8,128)S(1)}, f32[256,256]{1,0:T(8,128)S(1)}, u32[]{:S(2)}, u32[]{:S(2)}) collective-permute-start(f32[256,256]{1,0:T(8,128)S(1)} %shard_map.74.one_ref), channel_id=1, source_target_pairs={{0,1},{1,0},{2,3},{3,2},{4,5},{5,4},{6,7},{7,6},{8,9},{9,8},{10,11... | collective-permute-start | bytes 786440 | tf_op jit(solution)/shard_map/ppermute | solution.py:26
  14.2 0.0 copy-done
  14.2 1.2 %shard_map.75 = (bf16[256,128]{1,0:T(8,128)(2,1)S(1)}, bf16[16,128]{1,0:T(8,128)(2,1)S(1)}) custom-call(bf16[256,4096]{1,0:T(8,128)(2,1)S(1)} %shard_map.73.x_ref, s32[1,1024]{1,0:T(1,128)S(1)} %bitcast.9), custom_call_target="tpu_custom_call" | custom-call | flops 1073741824 | tf_op jit(solution)/shard_map/pallas_call | solution.py:69
  15.4 0.0 collective-permute-done.5.two_ref
  15.4 1.7 %collective-permute-start.6 = (bf16[256,256]{1,0:T(8,128)(2,1)S(1)}, bf16[256,256]{1,0:T(8,128)(2,1)S(1)}, u32[]{:S(2)}, u32[]{:S(2)}) collective-permute-start(bf16[256,256]{1,0:T(8,128)(2,1)S(1)} %get-tuple-element.63.refs_0_.refs_6_), channel_id=1, source_target_pairs={{0,32},{1,57},{2,34},{3,59},{4,36},{5,61},{6,38},{7,63},{8,40},{9,... | collective-permute-start | bytes 393224 | tf_op jit(solution)/shard_map/ppermute | solution.py:26
  17.1 2.2 %collective-permute-start.7 = (bf16[256,256]{1,0:T(8,128)(2,1)S(1)}, bf16[256,256]{1,0:T(8,128)(2,1)S(1)}, u32[]{:S(2)}, u32[]{:S(2)}) collective-permute-start(bf16[256,256]{1,0:T(8,128)(2,1)S(1)} %get-tuple-element.63.refs_0_.refs_6_), channel_id=1, source_target_pairs={{0,96},{1,121},{2,98},{3,123},{4,100},{5,125},{6,102},{7,127},{8,1... | collective-permute-start | bytes 393224 | tf_op jit(solution)/shard_map/ppermute | solution.py:26
  19.3 0.5 collective-permute-start.8
  19.8 0.7 %collective-permute-done.6.refs_1_.first_ref.refs_7_ = bf16[256,256]{1,0:T(8,128)(2,1)S(1)} collective-permute-done((bf16[256,256]{1,0:T(8,128)(2,1)S(1)}, bf16[256,256]{1,0:T(8,128)(2,1)S(1)}, u32[]{:S(2)}, u32[]{:S(2)}) %collective-permute-start.6) | collective-permute-done | bytes 131104 | tf_op jit(solution)/shard_map/ppermute | solution.py:26
  20.5 1.5 %shard_map.77 = (bf16[256,4096]{1,0:T(8,128)(2,1)S(1)}, bf16[64,512]{1,0:T(8,128)(2,1)S(1)}, bf16[64,512]{1,0:T(8,128)(2,1)S(1)}, bf16[128,128]{1,0:T(8,128)(2,1)S(1)}) custom-call(bf16[256,4096]{1,0:T(8,128)(2,1)S(1)} %shard_map.73.x_ref, s32[1,1024]{1,0:T(1,128)S(1)} %bitcast.10, bf16[256,128]{1,0:T(8,128)(2,1)S(1)} %get-tuple-element.60.sides_ref, ...), custom_call_target="tpu_custom_call" | custom-call | flops 1227133568 | tf_op jit(solution)/shard_map/pallas_call | solution.py:69
  22.0 2.8 %collective-permute-done.8.refs_4_.refs_12_.refs_6_ = bf16[128,256]{1,0:T(8,128)(2,1)S(1)} collective-permute-done((bf16[128,256]{1,0:T(8,128)(2,1)S(1)}, bf16[128,256]{1,0:T(8,128)(2,1)S(1)}, u32[]{:S(2)}, u32[]{:S(2)}) %collective-permute-start.8) | collective-permute-done | bytes 65568 | tf_op jit(solution)/shard_map/ppermute | solution.py:26
  24.8 0.0 collective-permute-done.7.second_ref.refs_0_.refs_8_.refs_2_
  24.8 0.8 %collective-permute-start.9 = (bf16[256,256]{1,0:T(8,128)(2,1)S(1)}, bf16[256,256]{1,0:T(8,128)(2,1)S(1)}, u32[]{:S(2)}, u32[]{:S(2)}) collective-permute-start(bf16[256,256]{1,0:T(8,128)(2,1)S(1)} %collective-permute-done.6.refs_1_.first_ref.refs_7_), channel_id=1, source_target_pairs={{0,1},{1,0},{2,3},{3,2},{4,5},{5,4},{6,7},{7,6},{8,9},{9,8},{10,11... | collective-permute-start | bytes 393224 | tf_op jit(solution)/shard_map/ppermute | solution.py:26
  25.6 0.1 collective-permute-start.10
  25.7 0.4 collective-permute-start.11
  26.1 0.8 %collective-permute-start.12 = (bf16[256,256]{1,0:T(8,128)(2,1)S(1)}, bf16[256,256]{1,0:T(8,128)(2,1)S(1)}, u32[]{:S(2)}, u32[]{:S(2)}) collective-permute-start(bf16[256,256]{1,0:T(8,128)(2,1)S(1)} %shard_map.78), channel_id=1, source_target_pairs={{0,32},{1,97},{2,34},{3,99},{4,36},{5,101},{6,38},{7,103},{8,40},{... | collective-permute-start | bytes 393224 | tf_op jit(solution)/shard_map/ppermute | solution.py:26
  26.9 0.1 collective-permute-done.11.refs_3_.refs_11_.refs_5_
  27.1 0.0 collective-permute-done.9.refs_1_.refs_9_.refs_3_
  27.1 0.0 collective-permute-done.10.refs_2_.refs_10_.refs_4_
  27.1 2.8 %shard_map.79 = (bf16[256,4096]{1,0:T(8,128)(2,1)S(1)}, bf16[64,512]{1,0:T(8,128)(2,1)S(1)}, bf16[64,512]{1,0:T(8,128)(2,1)S(1)}, bf16[128,128]{1,0:T(8,128)(2,1)S(1)}) custom-call(bf16[256,4096]{1,0:T(8,128)(2,1)S(1)} %shard_map.73.x_ref, s32[1,1024]{1,0:T(1,128)S(1)} %bitcast.11, bf16[256,128]{1,0:T(8,128)(2,1)S(1)} %get-tuple-element.60.sides_ref, ...), custom_call_target="tpu_custom_call" | custom-call | flops 3067833856 | tf_op jit(solution)/shard_map/pallas_call | solution.py:69
  29.9 1.2 %collective-permute-done.12.refs_0_.refs_13_.refs_7_ = bf16[256,256]{1,0:T(8,128)(2,1)S(1)} collective-permute-done((bf16[256,256]{1,0:T(8,128)(2,1)S(1)}, bf16[256,256]{1,0:T(8,128)(2,1)S(1)}, u32[]{:S(2)}, u32[]{:S(2)}) %collective-permute-start.12) | collective-permute-done | bytes 131104 | tf_op jit(solution)/shard_map/ppermute | solution.py:26
  31.1 0.2 collective-permute-start.13
  31.2 1.2 %collective-permute-done.13.refs_1_.refs_14_.refs_8_ = bf16[256,256]{1,0:T(8,128)(2,1)S(1)} collective-permute-done((bf16[256,256]{1,0:T(8,128)(2,1)S(1)}, bf16[256,256]{1,0:T(8,128)(2,1)S(1)}, u32[]{:S(2)}, u32[]{:S(2)}) %collective-permute-start.13) | collective-permute-done | bytes 131104 | tf_op jit(solution)/shard_map/ppermute | solution.py:26
  32.4 0.4 shard_map.81
  32.9 0.9 %collective-permute-start.14 = (bf16[64,512]{1,0:T(8,128)(2,1)S(1)}, bf16[64,512]{1,0:T(8,128)(2,1)S(1)}, u32[]{:S(2)}, u32[]{:S(2)}) collective-permute-start(bf16[64,512]{1,0:T(8,128)(2,1)S(1)} %get-tuple-element.85), channel_id=1, source_target_pairs={{0,16},{1,17},{2,18},{3,19},{4,20},{5,21},{6,22},{7,23},{8,24},{9,... | collective-permute-start | bytes 196616 | tf_op jit(solution)/shard_map/ppermute | solution.py:479
  33.8 2.9 %collective-permute-start.15 = (bf16[64,512]{1,0:T(8,128)(2,1)S(1)}, bf16[64,512]{1,0:T(8,128)(2,1)S(1)}, u32[]{:S(2)}, u32[]{:S(2)}) collective-permute-start(bf16[64,512]{1,0:T(8,128)(2,1)S(1)} %get-tuple-element.86), channel_id=1, source_target_pairs={{0,2},{1,3},{2,0},{3,1},{4,6},{5,7},{6,4},{7,5},{8,10},{9,11},{10,... | collective-permute-start | bytes 196616 | tf_op jit(solution)/shard_map/ppermute | solution.py:479
  36.7 0.0 collective-permute-start.16
  36.7 0.5 collective-permute-start.17
  37.2 0.0 copy-start.1
  37.2 0.0 copy-start.2
  37.2 2.0 %shard_map.80 = (bf16[256,4096]{1,0:T(8,128)(2,1)S(1)}, bf16[256,128]{1,0:T(8,128)(2,1)S(1)}) custom-call(bf16[256,4096]{1,0:T(8,128)(2,1)S(1)} %shard_map.73.x_ref, s32[1,1024]{1,0:T(1,128)S(1)} %bitcast.13, bf16[256,4096]{1,0:T(8,128)(2,1)S(1)} %get-tuple-element.76.done_ref, bf16[256,256]{1,0:T(8,128)(2,1)S(1)} %collective-permute-done.12.refs_0_.refs_13_.refs_7_, ...), custom_call_target="tpu_custom_call" | custom-call | flops 858993 | tf_op jit(solution)/shard_map/pallas_call | solution.py:69
  39.1 0.0 collective-permute-done.16.refs_4_
  39.2 2.9 %collective-permute-done.17.refs_5_ = bf16[64,128]{1,0:T(8,128)(2,1)S(1)} collective-permute-done((bf16[64,128]{1,0:T(8,128)(2,1)S(1)}, bf16[64,128]{1,0:T(8,128)(2,1)S(1)}, u32[]{:S(2)}, u32[]{:S(2)}) %collective-permute-start.17) | collective-permute-done | bytes 16416 | tf_op jit(solution)/shard_map/ppermute | solution.py:479
  42.0 0.0 collective-permute-done.14.refs_2_
  42.0 0.0 collective-permute-done.15.refs_3_
  42.0 0.0 copy-done.1
  42.0 0.0 copy-done.2
  42.0 3.0 %shard_map.82 = (bf16[256,4096]{1,0:T(8,128)(2,1)S(1)}, bf16[256,1024]{1,0:T(8,128)(2,1)S(1)}, bf16[64,512]{1,0:T(8,128)(2,1)S(1)}, bf16[64,512]{1,0:T(8,128)(2,...) custom-call(s32[4]{0:T(128)S(1)} %copy-done.2, bf16[256,4096]{1,0:T(8,128)(2,1)S(1)} %get-tuple-element.80.x_ref, ...), custom_call_target="tpu_custom_call" | custom-call | flops 1431655808 | tf_op jit(solution)/shard_map/pallas_call | solution.py:540
  45.0 0.5 collective-permute-start.18
  45.5 3.8 %collective-permute-start.19 = (bf16[64,512]{1,0:T(8,128)(2,1)S(1)}, bf16[64,512]{1,0:T(8,128)(2,1)S(1)}, u32[]{:S(2)}, u32[]{:S(2)}) collective-permute-start(bf16[64,512]{1,0:T(8,128)(2,1)S(1)} %get-tuple-element.92), channel_id=1, source_target_pairs={{0,2},{1,3},{2,0},{3,1},{4,6},{5,7},{6,4},{7,5},{8,10},{9,11},{10,... | collective-permute-start | bytes 196616 | tf_op jit(solution)/shard_map/ppermute | solution.py:479
  49.3 0.0 collective-permute-start.20
  49.3 0.8 %collective-permute-start.21 = (bf16[64,128]{1,0:T(8,128)(2,1)S(1)}, bf16[64,128]{1,0:T(8,128)(2,1)S(1)}, u32[]{:S(2)}, u32[]{:S(2)}) collective-permute-start(bf16[64,128]{1,0:T(8,128)(2,1)S(1)} %get-tuple-element.94), channel_id=1, source_target_pairs={{0,32},{1,2},{2,1},{3,4},{4,3},{5,6},{6,5},{7,8},{8,7},{9,10},{10,... | collective-permute-start | bytes 49160 | tf_op jit(solution)/shard_map/ppermute | solution.py:479
  50.1 3.5 %shard_map.83.x_ref = bf16[256,4096]{1,0:T(8,128)(2,1)S(1)} custom-call(bf16[256,4096]{1,0:T(8,128)(2,1)S(1)} %get-tuple-element.89.x_ref, s32[1,1024]{1,0:T(1,128)S(1)} %bitcast.15, bf16[256,1024]{1,0:T(8,128)(2,1)S(1)} %get-tuple-element.90.ends_ref, bf16[256,256]{1,0:T(8,128)(2,1)S(1)} %get-tuple-element.63.refs_0_.refs_6_, ...), custom_call_target="tpu_custom_call" | custom-call | flops 858993 | tf_op jit(solution)/shard_map/pallas_call | solution.py:69
  53.6 0.0 collective-permute-done.20.refs_2_
  53.6 1.0 %collective-permute-done.21.refs_3_ = bf16[64,128]{1,0:T(8,128)(2,1)S(1)} collective-permute-done((bf16[64,128]{1,0:T(8,128)(2,1)S(1)}, bf16[64,128]{1,0:T(8,128)(2,1)S(1)}, u32[]{:S(2)}, u32[]{:S(2)}) %collective-permute-start.21) | collective-permute-done | bytes 16416 | tf_op jit(solution)/shard_map/ppermute | solution.py:479
  54.6 0.0 collective-permute-done.18.refs_0_
  54.6 0.0 collective-permute-done.19.refs_1_
  54.6 2.9 %shard_map.84 = bf16[256,4,8,128]{3,2,1,0:T(8,128)(2,1)} custom-call(s32[4]{0:T(128)S(1)} %copy-done.2, bf16[256,4096]{1,0:T(8,128)(2,1)S(1)} %shard_map.83.x_ref, bf16[4,4,64]{2,1,0:T(4,128)(2,1)S(1)} %bitcast.17, bf16[64,512]{1,0:T(8,128)(2,1)S(1)} %collective-permute-done.18.refs_0_, bf16[64,512]{1,0:T(8,128)(2,1)S(1)} %collective-permute-done.19.refs_1_, ...), custom_call_target="tpu_custom_call" | custom-call | tf_op jit(solution)/shard_map/pallas_call | solution.py:559
  (3 shorter events, 0.1 us)
Async XLA Ops:
  1.5 3.9 %collective-permute-start.1 = (f32[32,256]{1,0:T(8,128)S(1)}, f32[32,256]{1,0:T(8,128)S(1)}, u32[]{:S(2)}, u32[]{:S(2)}) collective-permute-start(f32[32,256]{1,0:T(8,128)S(1)} %maximum_multiply_fusion.refs_0_), channel_id=1, source_target_pairs={{0,1},{1,0},{2,3},{3,2},{4,5},{5,4},{6,7},{7,6},{8,9},{9,8},{10,11... | collective-permute-start | bytes 98312 | tf_op jit(solution)/shard_map/ppermute | solution.py:26
  1.5 10.9 %collective-permute-start = (f32[32,256]{1,0:T(8,128)S(1)}, f32[32,256]{1,0:T(8,128)S(1)}, u32[]{:S(2)}, u32[]{:S(2)}) collective-permute-start(f32[32,256]{1,0:T(8,128)S(1)} %maximum_multiply_fusion.refs_0_), channel_id=1, source_target_pairs={{0,4},{1,5},{2,6},{3,7},{4,0},{5,1},{6,2},{7,3},{8,12},{9,13},{10,... | collective-permute-start | bytes 98312 | tf_op jit(solution)/shard_map/ppermute | solution.py:26
  5.4 7.0 %collective-permute-start.4 = (f32[64,256]{1,0:T(8,128)S(1)}, f32[64,256]{1,0:T(8,128)S(1)}, u32[]{:S(2)}, u32[]{:S(2)}) collective-permute-start(f32[64,256]{1,0:T(8,128)S(1)} %pad_maximum_fusion), channel_id=1, source_target_pairs={{0,6},{1,13},{2,4},{3,15},{4,2},{5,9},{6,0},{7,11},{8,14},{9,5},{1... | collective-permute-start | bytes 196616 | tf_op jit(solution)/shard_map/ppermute | solution.py:26
  6.7 5.6 %collective-permute-start.3 = (f32[64,256]{1,0:T(8,128)S(1)}, f32[64,256]{1,0:T(8,128)S(1)}, u32[]{:S(2)}, u32[]{:S(2)}) collective-permute-start(f32[64,256]{1,0:T(8,128)S(1)} %pad_maximum_fusion), channel_id=1, source_target_pairs={{0,2},{1,15},{2,0},{3,13},{4,6},{5,11},{6,4},{7,9},{8,10},{9,7},{1... | collective-permute-start | bytes 196616 | tf_op jit(solution)/shard_map/ppermute | solution.py:26
  6.7 5.6 %collective-permute-start.2 = (f32[64,256]{1,0:T(8,128)S(1)}, f32[64,256]{1,0:T(8,128)S(1)}, u32[]{:S(2)}, u32[]{:S(2)}) collective-permute-start(f32[64,256]{1,0:T(8,128)S(1)} %pad_maximum_fusion), channel_id=1, source_target_pairs={{0,8},{1,11},{2,10},{3,9},{4,12},{5,15},{6,14},{7,13},{8,0},{9,3},... | collective-permute-start | bytes 196616 | tf_op jit(solution)/shard_map/ppermute | solution.py:26
  7.6 6.7 %copy-start = (s32[8,128]{1,0:T(8,128)S(1)}, s32[8,128]{1,0:T(8,128)}, u32[]{:S(2)}) copy-start(s32[8,128]{1,0:T(8,128)} %param.8) | copy-start | bytes 12292
  12.8 2.6 %collective-permute-start.5 = (f32[256,256]{1,0:T(8,128)S(1)}, f32[256,256]{1,0:T(8,128)S(1)}, u32[]{:S(2)}, u32[]{:S(2)}) collective-permute-start(f32[256,256]{1,0:T(8,128)S(1)} %shard_map.74.one_ref), channel_id=1, source_target_pairs={{0,1},{1,0},{2,3},{3,2},{4,5},{5,4},{6,7},{7,6},{8,9},{9,8},{10,11... | collective-permute-start | bytes 786440 | tf_op jit(solution)/shard_map/ppermute | solution.py:26
  15.4 5.0 %collective-permute-start.6 = (bf16[256,256]{1,0:T(8,128)(2,1)S(1)}, bf16[256,256]{1,0:T(8,128)(2,1)S(1)}, u32[]{:S(2)}, u32[]{:S(2)}) collective-permute-start(bf16[256,256]{1,0:T(8,128)(2,1)S(1)} %get-tuple-element.63.refs_0_.refs_6_), channel_id=1, source_target_pairs={{0,32},{1,57},{2,34},{3,59},{4,36},{5,61},{6,38},{7,63},{8,40},{9,... | collective-permute-start | bytes 393224 | tf_op jit(solution)/shard_map/ppermute | solution.py:26
  17.1 7.7 %collective-permute-start.7 = (bf16[256,256]{1,0:T(8,128)(2,1)S(1)}, bf16[256,256]{1,0:T(8,128)(2,1)S(1)}, u32[]{:S(2)}, u32[]{:S(2)}) collective-permute-start(bf16[256,256]{1,0:T(8,128)(2,1)S(1)} %get-tuple-element.63.refs_0_.refs_6_), channel_id=1, source_target_pairs={{0,96},{1,121},{2,98},{3,123},{4,100},{5,125},{6,102},{7,127},{8,1... | collective-permute-start | bytes 393224 | tf_op jit(solution)/shard_map/ppermute | solution.py:26
  19.3 5.5 %collective-permute-start.8 = (bf16[128,256]{1,0:T(8,128)(2,1)S(1)}, bf16[128,256]{1,0:T(8,128)(2,1)S(1)}, u32[]{:S(2)}, u32[]{:S(2)}) collective-permute-start(bf16[128,256]{1,0:T(8,128)(2,1)S(1)} %get-tuple-element.65), channel_id=1, source_target_pairs={{0,24},{1,25},{2,26},{3,27},{4,28},{5,29},{6,30},{7,31},{8,16},{9,... | collective-permute-start | bytes 196616 | tf_op jit(solution)/shard_map/ppermute | solution.py:26
  24.8 2.3 %collective-permute-start.9 = (bf16[256,256]{1,0:T(8,128)(2,1)S(1)}, bf16[256,256]{1,0:T(8,128)(2,1)S(1)}, u32[]{:S(2)}, u32[]{:S(2)}) collective-permute-start(bf16[256,256]{1,0:T(8,128)(2,1)S(1)} %collective-permute-done.6.refs_1_.first_ref.refs_7_), channel_id=1, source_target_pairs={{0,1},{1,0},{2,3},{3,2},{4,5},{5,4},{6,7},{7,6},{8,9},{9,8},{10,11... | collective-permute-start | bytes 393224 | tf_op jit(solution)/shard_map/ppermute | solution.py:26
  25.6 1.4 %collective-permute-start.10 = (bf16[256,256]{1,0:T(8,128)(2,1)S(1)}, bf16[256,256]{1,0:T(8,128)(2,1)S(1)}, u32[]{:S(2)}, u32[]{:S(2)}) collective-permute-start(bf16[256,256]{1,0:T(8,128)(2,1)S(1)} %collective-permute-done.7.second_ref.refs_0_.refs_8_.refs_2_), channel_id=1, source_target_pairs={{0,1},{1,0},{2,3},{3,2},{4,5},{5,4},{6,7},{7,6},{8,9},{9,8},{10,11... | collective-permute-start | bytes 393224 | tf_op jit(solution)/shard_map/ppermute | solution.py:26
  25.7 1.3 %collective-permute-start.11 = (bf16[128,256]{1,0:T(8,128)(2,1)S(1)}, bf16[128,256]{1,0:T(8,128)(2,1)S(1)}, u32[]{:S(2)}, u32[]{:S(2)}) collective-permute-start(bf16[128,256]{1,0:T(8,128)(2,1)S(1)} %collective-permute-done.8.refs_4_.refs_12_.refs_6_), channel_id=1, source_target_pairs={{0,1},{1,0},{2,3},{3,2},{4,5},{5,4},{6,7},{7,6},{8,9},{9,8},{10,11... | collective-permute-start | bytes 196616 | tf_op jit(solution)/shard_map/ppermute | solution.py:26
  26.1 5.0 %collective-permute-start.12 = (bf16[256,256]{1,0:T(8,128)(2,1)S(1)}, bf16[256,256]{1,0:T(8,128)(2,1)S(1)}, u32[]{:S(2)}, u32[]{:S(2)}) collective-permute-start(bf16[256,256]{1,0:T(8,128)(2,1)S(1)} %shard_map.78), channel_id=1, source_target_pairs={{0,32},{1,97},{2,34},{3,99},{4,36},{5,101},{6,38},{7,103},{8,40},{... | collective-permute-start | bytes 393224 | tf_op jit(solution)/shard_map/ppermute | solution.py:26
  31.1 1.3 %collective-permute-start.13 = (bf16[256,256]{1,0:T(8,128)(2,1)S(1)}, bf16[256,256]{1,0:T(8,128)(2,1)S(1)}, u32[]{:S(2)}, u32[]{:S(2)}) collective-permute-start(bf16[256,256]{1,0:T(8,128)(2,1)S(1)} %collective-permute-done.12.refs_0_.refs_13_.refs_7_), channel_id=1, source_target_pairs={{0,1},{1,0},{2,3},{3,2},{4,5},{5,4},{6,7},{7,6},{8,9},{9,8},{10,11... | collective-permute-start | bytes 393224 | tf_op jit(solution)/shard_map/ppermute | solution.py:26
  32.9 9.1 %collective-permute-start.14 = (bf16[64,512]{1,0:T(8,128)(2,1)S(1)}, bf16[64,512]{1,0:T(8,128)(2,1)S(1)}, u32[]{:S(2)}, u32[]{:S(2)}) collective-permute-start(bf16[64,512]{1,0:T(8,128)(2,1)S(1)} %get-tuple-element.85), channel_id=1, source_target_pairs={{0,16},{1,17},{2,18},{3,19},{4,20},{5,21},{6,22},{7,23},{8,24},{9,... | collective-permute-start | bytes 196616 | tf_op jit(solution)/shard_map/ppermute | solution.py:479
  33.8 8.2 %collective-permute-start.15 = (bf16[64,512]{1,0:T(8,128)(2,1)S(1)}, bf16[64,512]{1,0:T(8,128)(2,1)S(1)}, u32[]{:S(2)}, u32[]{:S(2)}) collective-permute-start(bf16[64,512]{1,0:T(8,128)(2,1)S(1)} %get-tuple-element.86), channel_id=1, source_target_pairs={{0,2},{1,3},{2,0},{3,1},{4,6},{5,7},{6,4},{7,5},{8,10},{9,11},{10,... | collective-permute-start | bytes 196616 | tf_op jit(solution)/shard_map/ppermute | solution.py:479
  36.7 2.4 %collective-permute-start.16 = (bf16[64,128]{1,0:T(8,128)(2,1)S(1)}, bf16[64,128]{1,0:T(8,128)(2,1)S(1)}, u32[]{:S(2)}, u32[]{:S(2)}) collective-permute-start(bf16[64,128]{1,0:T(8,128)(2,1)S(1)} %get-tuple-element.87), channel_id=1, source_target_pairs={{0,1},{1,0},{2,3},{3,2},{4,5},{5,4},{6,7},{7,6},{8,9},{9,8},{10,11... | collective-permute-start | bytes 49160 | tf_op jit(solution)/shard_map/ppermute | solution.py:479
  36.7 5.3 %collective-permute-start.17 = (bf16[64,128]{1,0:T(8,128)(2,1)S(1)}, bf16[64,128]{1,0:T(8,128)(2,1)S(1)}, u32[]{:S(2)}, u32[]{:S(2)}) collective-permute-start(bf16[64,128]{1,0:T(8,128)(2,1)S(1)} %get-tuple-element.88), channel_id=1, source_target_pairs={{0,32},{1,2},{2,1},{3,4},{4,3},{5,6},{6,5},{7,8},{8,7},{9,10},{10,... | collective-permute-start | bytes 49160 | tf_op jit(solution)/shard_map/ppermute | solution.py:479
  37.2 4.8 %copy-start.1 = (bf16[4,64,4]{1,2,0:T(4,128)(2,1)S(1)}, bf16[4,64,4]{1,2,0:T(4,128)(2,1)}, u32[]{:S(2)}) copy-start(bf16[4,64,4]{1,2,0:T(4,128)(2,1)} %param.10) | copy-start | bytes 6148
  37.2 4.8 %copy-start.2 = (s32[4]{0:T(128)S(1)}, s32[4]{0:T(128)}, u32[]{:S(2)}) copy-start(s32[4]{0:T(128)} %port_ref.3) | copy-start | bytes 52
  45.0 9.6 %collective-permute-start.18 = (bf16[64,512]{1,0:T(8,128)(2,1)S(1)}, bf16[64,512]{1,0:T(8,128)(2,1)S(1)}, u32[]{:S(2)}, u32[]{:S(2)}) collective-permute-start(bf16[64,512]{1,0:T(8,128)(2,1)S(1)} %get-tuple-element.91), channel_id=1, source_target_pairs={{0,16},{1,17},{2,18},{3,19},{4,20},{5,21},{6,22},{7,23},{8,24},{9,... | collective-permute-start | bytes 196616 | tf_op jit(solution)/shard_map/ppermute | solution.py:479
  45.5 9.1 %collective-permute-start.19 = (bf16[64,512]{1,0:T(8,128)(2,1)S(1)}, bf16[64,512]{1,0:T(8,128)(2,1)S(1)}, u32[]{:S(2)}, u32[]{:S(2)}) collective-permute-start(bf16[64,512]{1,0:T(8,128)(2,1)S(1)} %get-tuple-element.92), channel_id=1, source_target_pairs={{0,2},{1,3},{2,0},{3,1},{4,6},{5,7},{6,4},{7,5},{8,10},{9,11},{10,... | collective-permute-start | bytes 196616 | tf_op jit(solution)/shard_map/ppermute | solution.py:479
  49.3 4.3 %collective-permute-start.20 = (bf16[64,128]{1,0:T(8,128)(2,1)S(1)}, bf16[64,128]{1,0:T(8,128)(2,1)S(1)}, u32[]{:S(2)}, u32[]{:S(2)}) collective-permute-start(bf16[64,128]{1,0:T(8,128)(2,1)S(1)} %get-tuple-element.93), channel_id=1, source_target_pairs={{0,1},{1,0},{2,3},{3,2},{4,5},{5,4},{6,7},{7,6},{8,9},{9,8},{10,11... | collective-permute-start | bytes 49160 | tf_op jit(solution)/shard_map/ppermute | solution.py:479
  49.3 5.3 %collective-permute-start.21 = (bf16[64,128]{1,0:T(8,128)(2,1)S(1)}, bf16[64,128]{1,0:T(8,128)(2,1)S(1)}, u32[]{:S(2)}, u32[]{:S(2)}) collective-permute-start(bf16[64,128]{1,0:T(8,128)(2,1)S(1)} %get-tuple-element.94), channel_id=1, source_target_pairs={{0,32},{1,2},{2,1},{3,4},{4,3},{5,6},{6,5},{7,8},{8,7},{9,10},{10,... | collective-permute-start | bytes 49160 | tf_op jit(solution)/shard_map/ppermute | solution.py:479

commit v20 on v19

--- a/solution.py
+++ b/solution.py
@@ -377,15 +377,15 @@
     order, tile = x_ref.shape[0], rows * width
     quarter = order // 4
     maps = with_steps(map_refs, 0)
-    for port in range(ports):
-        places = [(port, row) for row in range(rows)]
-        value = patched(rows, width, x_ref, port_ref, profile_ref, halo_refs, places)
-        patched_ref[:, port * tile : (port + 1) * tile] = value
-    starts = [port * tile + row * width for row in (0, rows - 1) for port in range(ports)]
-    block = jnp.concatenate([patched_ref[:, start : start + width] for start in starts], axis=1)
+    places = [(port, row) for row in (0, rows - 1) for port in range(ports)]
+    block = patched(rows, width, x_ref, port_ref, profile_ref, halo_refs, places)
     types = types_of_rows(types_ref, [0] * ports + [rows - 1] * ports).astype(BF)
     total = products(block, types, maps, 0, order)
     ends_ref[...] = total.astype(BF)
+    for port in range(ports):
+        places = [(port, row) for row in range(1, rows - 1)]
+        value = patched(rows, width, x_ref, port_ref, profile_ref, halo_refs, places)
+        patched_ref[:, port * tile + width : (port + 1) * tile - width] = value
     wide = ports * LANES
     store_rims(refs[-4:-2], "row", total[0:quarter, :wide], total[quarter : 2 * quarter, wide:])
     sides = patched_sides(rows, width, sides_ref, port_ref, profile_ref, halo_refs, ports)

time: 57.9 us -> 57.5 us (level)
  transfers between devices with their start and end apart: 22 -> 22, of which waited for: 8 -> 8; matrix products, arithmetic and copies ran while one was open for 0% -> 0% of each run, Pallas kernels for 22% -> 23%
where the time goes in v20:
time: 57.5 us; the launch traced here: 57.2 us
  starting transfers between devices  23.5 us (41%)
  Pallas kernels  19.2 us (33%)
  waiting for transfers between devices  12.7 us (22%)
  other arithmetic  0.81 us (1%)
  local copies, waits for them, and re-layouts  0.67 us (1%)
    ppermute x14, starting transfers between devices, swap(): return lax.ppermute(value, ('row', 'col'), pairs)  14.1 us
    pallas_call x9, Pallas kernels, whole_call(): pl.pallas_call(kernel, in_specs=[WHOLE] * len(operands), out_specs=[WHOLE...  11.8 us
    ppermute x8, starting transfers between devices, exchange(): lax.ppermute(rim, ('row', 'col'), pairs(first))  9.37 us
    ppermute x14, waiting for transfers between devices, swap(): return lax.ppermute(value, ('row', 'col'), pairs)  8.86 us
    ppermute x8, waiting for transfers between devices, exchange(): lax.ppermute(rim, ('row', 'col'), pairs(first))  3.86 us
    pallas_call x1, Pallas kernels, body(): pl.pallas_call(functools.partial(last_kernel, rows, width), in_specs=[por...  2.86 us
    pallas_call x1, Pallas kernels, body(): pl.pallas_call(functools.partial(ends_kernel, rows, ports, width), in_spe...  2.57 us
    pallas_call x1, Pallas kernels, own_type_map(): pl.pallas_call(flat_kernel, in_specs=[pl.BlockSpec(memory_space=pltpu.HBM...  1.98 us
  transfers between devices with their start and end apart: 22, of which 8 were waited for; matrix products, arithmetic and copies ran while one was open for 0% of the time, Pallas kernels for 23%

profile of v20, /device:TPU:6, one launch (start us, length us, event | category | flops | bytes accessed | tf_op | source)
XLA Modules:
  0.0 57.2 jit_solution(6301552498745989347)
XLA Ops:
  0.0 0.7 %concatenate.10 = f32[32]{0:T(128)S(1)} pad(f32[16]{0:T(128)} %bitcast.21, f32[]{:T(128)} %constant.0.clone.1), padding=0_16 | pad | bytes 196 | tf_op jit(solution)/shard_map/concatenate | solution.py:82
  0.7 0.8 %maximum_multiply_fusion.refs_0_ = f32[32,256]{1,0:T(8,128)S(1)} fusion(f32[16,256]{1,0:T(8,128)} %bitcast.19, f32[16,256]{1,0:T(8,128)} %bitcast.20, f32[32]{0:T(128)S(1)} %concatenate.10), kind=kLoop, calls=%fused_computation.1 | loop fusion | flops 16384 | bytes 65664 | tf_op jit(solution)/shard_map/mul | solution.py:82
  1.5 0.0 collective-permute-start.1
  1.5 3.9 %collective-permute-start = (f32[32,256]{1,0:T(8,128)S(1)}, f32[32,256]{1,0:T(8,128)S(1)}, u32[]{:S(2)}, u32[]{:S(2)}) collective-permute-start(f32[32,256]{1,0:T(8,128)S(1)} %maximum_multiply_fusion.refs_0_), channel_id=1, source_target_pairs={{0,4},{1,5},{2,6},{3,7},{4,0},{5,1},{6,2},{7,3},{8,12},{9,13},{10,... | collective-permute-start | bytes 98312 | tf_op jit(solution)/shard_map/ppermute | solution.py:26
  5.4 0.0 collective-permute-done.1
  5.4 1.3 %collective-permute-start.4 = (f32[64,256]{1,0:T(8,128)S(1)}, f32[64,256]{1,0:T(8,128)S(1)}, u32[]{:S(2)}, u32[]{:S(2)}) collective-permute-start(f32[64,256]{1,0:T(8,128)S(1)} %pad_maximum_fusion), channel_id=1, source_target_pairs={{0,6},{1,13},{2,4},{3,15},{4,2},{5,9},{6,0},{7,11},{8,14},{9,5},{1... | collective-permute-start | bytes 196616 | tf_op jit(solution)/shard_map/ppermute | solution.py:26
  6.7 0.0 collective-permute-start.3
  6.7 0.8 %collective-permute-start.2 = (f32[64,256]{1,0:T(8,128)S(1)}, f32[64,256]{1,0:T(8,128)S(1)}, u32[]{:S(2)}, u32[]{:S(2)}) collective-permute-start(f32[64,256]{1,0:T(8,128)S(1)} %pad_maximum_fusion), channel_id=1, source_target_pairs={{0,8},{1,11},{2,10},{3,9},{4,12},{5,15},{6,14},{7,13},{8,0},{9,3},... | collective-permute-start | bytes 196616 | tf_op jit(solution)/shard_map/ppermute | solution.py:26
  7.6 0.0 copy-start
  7.6 2.0 %shard_map.73.x_ref = bf16[256,4096]{1,0:T(8,128)(2,1)S(1)} custom-call(bf16[256,4,8,128]{3,2,1,0:T(8,128)(2,1)} %bitcast.18), custom_call_target="tpu_custom_call" | custom-call | flops 1073741824 | tf_op jit(solution)/shard_map/pallas_call | solution.py:89
  9.5 2.8 %collective-permute-done.4.refs_4_ = f32[64,256]{1,0:T(8,128)S(1)} collective-permute-done((f32[64,256]{1,0:T(8,128)S(1)}, f32[64,256]{1,0:T(8,128)S(1)}, u32[]{:S(2)}, u32[]{:S(2)}) %collective-permute-start.4) | collective-permute-done | bytes 65568 | tf_op jit(solution)/shard_map/ppermute | solution.py:26
  12.4 0.0 collective-permute-done.3.refs_3_
  12.4 0.0 collective-permute-done.2.refs_2_
  12.4 0.0 collective-permute-done.refs_1_
  12.4 0.4 shard_map.74.one_ref
  12.8 1.4 %collective-permute-start.5 = (f32[256,256]{1,0:T(8,128)S(1)}, f32[256,256]{1,0:T(8,128)S(1)}, u32[]{:S(2)}, u32[]{:S(2)}) collective-permute-start(f32[256,256]{1,0:T(8,128)S(1)} %shard_map.74.one_ref), channel_id=1, source_target_pairs={{0,1},{1,0},{2,3},{3,2},{4,5},{5,4},{6,7},{7,6},{8,9},{9,8},{10,11... | collective-permute-start | bytes 786440 | tf_op jit(solution)/shard_map/ppermute | solution.py:26
  14.2 0.0 copy-done
  14.2 1.2 %shard_map.75 = (bf16[256,128]{1,0:T(8,128)(2,1)S(1)}, bf16[16,128]{1,0:T(8,128)(2,1)S(1)}) custom-call(bf16[256,4096]{1,0:T(8,128)(2,1)S(1)} %shard_map.73.x_ref, s32[1,1024]{1,0:T(1,128)S(1)} %bitcast.9), custom_call_target="tpu_custom_call" | custom-call | flops 1073741824 | tf_op jit(solution)/shard_map/pallas_call | solution.py:69
  15.4 0.0 collective-permute-done.5.two_ref
  15.4 1.7 %collective-permute-start.6 = (bf16[256,256]{1,0:T(8,128)(2,1)S(1)}, bf16[256,256]{1,0:T(8,128)(2,1)S(1)}, u32[]{:S(2)}, u32[]{:S(2)}) collective-permute-start(bf16[256,256]{1,0:T(8,128)(2,1)S(1)} %get-tuple-element.63.refs_0_.refs_6_), channel_id=1, source_target_pairs={{0,32},{1,57},{2,34},{3,59},{4,36},{5,61},{6,38},{7,63},{8,40},{9,... | collective-permute-start | bytes 393224 | tf_op jit(solution)/shard_map/ppermute | solution.py:26
  17.1 2.2 %collective-permute-start.7 = (bf16[256,256]{1,0:T(8,128)(2,1)S(1)}, bf16[256,256]{1,0:T(8,128)(2,1)S(1)}, u32[]{:S(2)}, u32[]{:S(2)}) collective-permute-start(bf16[256,256]{1,0:T(8,128)(2,1)S(1)} %get-tuple-element.63.refs_0_.refs_6_), channel_id=1, source_target_pairs={{0,96},{1,121},{2,98},{3,123},{4,100},{5,125},{6,102},{7,127},{8,1... | collective-permute-start | bytes 393224 | tf_op jit(solution)/shard_map/ppermute | solution.py:26
  19.3 0.5 collective-permute-start.8
  19.8 0.7 %collective-permute-done.6.refs_1_.first_ref.refs_7_ = bf16[256,256]{1,0:T(8,128)(2,1)S(1)} collective-permute-done((bf16[256,256]{1,0:T(8,128)(2,1)S(1)}, bf16[256,256]{1,0:T(8,128)(2,1)S(1)}, u32[]{:S(2)}, u32[]{:S(2)}) %collective-permute-start.6) | collective-permute-done | bytes 131104 | tf_op jit(solution)/shard_map/ppermute | solution.py:26
  20.5 1.5 %shard_map.77 = (bf16[256,4096]{1,0:T(8,128)(2,1)S(1)}, bf16[64,512]{1,0:T(8,128)(2,1)S(1)}, bf16[64,512]{1,0:T(8,128)(2,1)S(1)}, bf16[128,128]{1,0:T(8,128)(2,1)S(1)}) custom-call(bf16[256,4096]{1,0:T(8,128)(2,1)S(1)} %shard_map.73.x_ref, s32[1,1024]{1,0:T(1,128)S(1)} %bitcast.10, bf16[256,128]{1,0:T(8,128)(2,1)S(1)} %get-tuple-element.60.sides_ref, ...), custom_call_target="tpu_custom_call" | custom-call | flops 1227133568 | tf_op jit(solution)/shard_map/pallas_call | solution.py:69
  22.0 2.8 %collective-permute-done.8.refs_4_.refs_12_.refs_6_ = bf16[128,256]{1,0:T(8,128)(2,1)S(1)} collective-permute-done((bf16[128,256]{1,0:T(8,128)(2,1)S(1)}, bf16[128,256]{1,0:T(8,128)(2,1)S(1)}, u32[]{:S(2)}, u32[]{:S(2)}) %collective-permute-start.8) | collective-permute-done | bytes 65568 | tf_op jit(solution)/shard_map/ppermute | solution.py:26
  24.8 0.0 collective-permute-done.7.second_ref.refs_0_.refs_8_.refs_2_
  24.8 0.8 %collective-permute-start.9 = (bf16[256,256]{1,0:T(8,128)(2,1)S(1)}, bf16[256,256]{1,0:T(8,128)(2,1)S(1)}, u32[]{:S(2)}, u32[]{:S(2)}) collective-permute-start(bf16[256,256]{1,0:T(8,128)(2,1)S(1)} %collective-permute-done.6.refs_1_.first_ref.refs_7_), channel_id=1, source_target_pairs={{0,1},{1,0},{2,3},{3,2},{4,5},{5,4},{6,7},{7,6},{8,9},{9,8},{10,11... | collective-permute-start | bytes 393224 | tf_op jit(solution)/shard_map/ppermute | solution.py:26
  25.6 0.1 collective-permute-start.10
  25.7 0.4 collective-permute-start.11
  26.1 0.8 %collective-permute-start.12 = (bf16[256,256]{1,0:T(8,128)(2,1)S(1)}, bf16[256,256]{1,0:T(8,128)(2,1)S(1)}, u32[]{:S(2)}, u32[]{:S(2)}) collective-permute-start(bf16[256,256]{1,0:T(8,128)(2,1)S(1)} %shard_map.78), channel_id=1, source_target_pairs={{0,32},{1,97},{2,34},{3,99},{4,36},{5,101},{6,38},{7,103},{8,40},{... | collective-permute-start | bytes 393224 | tf_op jit(solution)/shard_map/ppermute | solution.py:26
  26.9 0.1 collective-permute-done.11.refs_3_.refs_11_.refs_5_
  27.1 0.0 collective-permute-done.9.refs_1_.refs_9_.refs_3_
  27.1 0.0 collective-permute-done.10.refs_2_.refs_10_.refs_4_
  27.1 2.8 %shard_map.79 = (bf16[256,4096]{1,0:T(8,128)(2,1)S(1)}, bf16[64,512]{1,0:T(8,128)(2,1)S(1)}, bf16[64,512]{1,0:T(8,128)(2,1)S(1)}, bf16[128,128]{1,0:T(8,128)(2,1)S(1)}) custom-call(bf16[256,4096]{1,0:T(8,128)(2,1)S(1)} %shard_map.73.x_ref, s32[1,1024]{1,0:T(1,128)S(1)} %bitcast.11, bf16[256,128]{1,0:T(8,128)(2,1)S(1)} %get-tuple-element.60.sides_ref, ...), custom_call_target="tpu_custom_call" | custom-call | flops 3067833856 | tf_op jit(solution)/shard_map/pallas_call | solution.py:69
  29.9 1.2 %collective-permute-done.12.refs_0_.refs_13_.refs_7_ = bf16[256,256]{1,0:T(8,128)(2,1)S(1)} collective-permute-done((bf16[256,256]{1,0:T(8,128)(2,1)S(1)}, bf16[256,256]{1,0:T(8,128)(2,1)S(1)}, u32[]{:S(2)}, u32[]{:S(2)}) %collective-permute-start.12) | collective-permute-done | bytes 131104 | tf_op jit(solution)/shard_map/ppermute | solution.py:26
  31.1 0.2 collective-permute-start.13
  31.2 1.2 %collective-permute-done.13.refs_1_.refs_14_.refs_8_ = bf16[256,256]{1,0:T(8,128)(2,1)S(1)} collective-permute-done((bf16[256,256]{1,0:T(8,128)(2,1)S(1)}, bf16[256,256]{1,0:T(8,128)(2,1)S(1)}, u32[]{:S(2)}, u32[]{:S(2)}) %collective-permute-start.13) | collective-permute-done | bytes 131104 | tf_op jit(solution)/shard_map/ppermute | solution.py:26
  32.4 0.4 shard_map.81
  32.9 0.9 %collective-permute-start.14 = (bf16[64,512]{1,0:T(8,128)(2,1)S(1)}, bf16[64,512]{1,0:T(8,128)(2,1)S(1)}, u32[]{:S(2)}, u32[]{:S(2)}) collective-permute-start(bf16[64,512]{1,0:T(8,128)(2,1)S(1)} %get-tuple-element.85), channel_id=1, source_target_pairs={{0,16},{1,17},{2,18},{3,19},{4,20},{5,21},{6,22},{7,23},{8,24},{9,... | collective-permute-start | bytes 196616 | tf_op jit(solution)/shard_map/ppermute | solution.py:479
  33.8 2.9 %collective-permute-start.15 = (bf16[64,512]{1,0:T(8,128)(2,1)S(1)}, bf16[64,512]{1,0:T(8,128)(2,1)S(1)}, u32[]{:S(2)}, u32[]{:S(2)}) collective-permute-start(bf16[64,512]{1,0:T(8,128)(2,1)S(1)} %get-tuple-element.86), channel_id=1, source_target_pairs={{0,2},{1,3},{2,0},{3,1},{4,6},{5,7},{6,4},{7,5},{8,10},{9,11},{10,... | collective-permute-start | bytes 196616 | tf_op jit(solution)/shard_map/ppermute | solution.py:479
  36.7 0.0 collective-permute-start.16
  36.7 0.5 collective-permute-start.17
  37.2 0.0 copy-start.1
  37.2 0.0 copy-start.2
  37.2 2.0 %shard_map.80 = (bf16[256,4096]{1,0:T(8,128)(2,1)S(1)}, bf16[256,128]{1,0:T(8,128)(2,1)S(1)}) custom-call(bf16[256,4096]{1,0:T(8,128)(2,1)S(1)} %shard_map.73.x_ref, s32[1,1024]{1,0:T(1,128)S(1)} %bitcast.13, bf16[256,4096]{1,0:T(8,128)(2,1)S(1)} %get-tuple-element.76.done_ref, bf16[256,256]{1,0:T(8,128)(2,1)S(1)} %collective-permute-done.12.refs_0_.refs_13_.refs_7_, ...), custom_call_target="tpu_custom_call" | custom-call | flops 858993 | tf_op jit(solution)/shard_map/pallas_call | solution.py:69
  39.1 0.0 collective-permute-done.16.refs_4_
  39.2 2.9 %collective-permute-done.17.refs_5_ = bf16[64,128]{1,0:T(8,128)(2,1)S(1)} collective-permute-done((bf16[64,128]{1,0:T(8,128)(2,1)S(1)}, bf16[64,128]{1,0:T(8,128)(2,1)S(1)}, u32[]{:S(2)}, u32[]{:S(2)}) %collective-permute-start.17) | collective-permute-done | bytes 16416 | tf_op jit(solution)/shard_map/ppermute | solution.py:479
  42.0 0.0 collective-permute-done.14.refs_2_
  42.0 0.0 collective-permute-done.15.refs_3_
  42.0 0.0 copy-done.1
  42.0 0.0 copy-done.2
  42.0 2.6 %shard_map.82 = (bf16[256,4096]{1,0:T(8,128)(2,1)S(1)}, bf16[256,1024]{1,0:T(8,128)(2,1)S(1)}, bf16[64,512]{1,0:T(8,128)(2,1)S(1)}, bf16[64,512]{1,0:T(8,128)(2,...) custom-call(s32[4]{0:T(128)S(1)} %copy-done.2, bf16[256,4096]{1,0:T(8,128)(2,1)S(1)} %get-tuple-element.80.x_ref, ...), custom_call_target="tpu_custom_call" | custom-call | flops 1431655808 | tf_op jit(solution)/shard_map/pallas_call | solution.py:540
  44.6 0.5 collective-permute-start.18
  45.1 3.8 %collective-permute-start.19 = (bf16[64,512]{1,0:T(8,128)(2,1)S(1)}, bf16[64,512]{1,0:T(8,128)(2,1)S(1)}, u32[]{:S(2)}, u32[]{:S(2)}) collective-permute-start(bf16[64,512]{1,0:T(8,128)(2,1)S(1)} %get-tuple-element.92), channel_id=1, source_target_pairs={{0,2},{1,3},{2,0},{3,1},{4,6},{5,7},{6,4},{7,5},{8,10},{9,11},{10,... | collective-permute-start | bytes 196616 | tf_op jit(solution)/shard_map/ppermute | solution.py:479
  48.9 0.0 collective-permute-start.20
  48.9 0.8 %collective-permute-start.21 = (bf16[64,128]{1,0:T(8,128)(2,1)S(1)}, bf16[64,128]{1,0:T(8,128)(2,1)S(1)}, u32[]{:S(2)}, u32[]{:S(2)}) collective-permute-start(bf16[64,128]{1,0:T(8,128)(2,1)S(1)} %get-tuple-element.94), channel_id=1, source_target_pairs={{0,32},{1,2},{2,1},{3,4},{4,3},{5,6},{6,5},{7,8},{8,7},{9,10},{10,... | collective-permute-start | bytes 49160 | tf_op jit(solution)/shard_map/ppermute | solution.py:479
  49.7 3.5 %shard_map.83.x_ref = bf16[256,4096]{1,0:T(8,128)(2,1)S(1)} custom-call(bf16[256,4096]{1,0:T(8,128)(2,1)S(1)} %get-tuple-element.89.x_ref, s32[1,1024]{1,0:T(1,128)S(1)} %bitcast.15, bf16[256,1024]{1,0:T(8,128)(2,1)S(1)} %get-tuple-element.90.ends_ref, bf16[256,256]{1,0:T(8,128)(2,1)S(1)} %get-tuple-element.63.refs_0_.refs_6_, ...), custom_call_target="tpu_custom_call" | custom-call | flops 858993 | tf_op jit(solution)/shard_map/pallas_call | solution.py:69
  53.2 0.0 collective-permute-done.20.refs_2_
  53.2 1.0 %collective-permute-done.21.refs_3_ = bf16[64,128]{1,0:T(8,128)(2,1)S(1)} collective-permute-done((bf16[64,128]{1,0:T(8,128)(2,1)S(1)}, bf16[64,128]{1,0:T(8,128)(2,1)S(1)}, u32[]{:S(2)}, u32[]{:S(2)}) %collective-permute-start.21) | collective-permute-done | bytes 16416 | tf_op jit(solution)/shard_map/ppermute | solution.py:479
  54.2 0.0 collective-permute-done.18.refs_0_
  54.2 0.0 collective-permute-done.19.refs_1_
  54.2 2.9 %shard_map.84 = bf16[256,4,8,128]{3,2,1,0:T(8,128)(2,1)} custom-call(s32[4]{0:T(128)S(1)} %copy-done.2, bf16[256,4096]{1,0:T(8,128)(2,1)S(1)} %shard_map.83.x_ref, bf16[4,4,64]{2,1,0:T(4,128)(2,1)S(1)} %bitcast.17, bf16[64,512]{1,0:T(8,128)(2,1)S(1)} %collective-permute-done.18.refs_0_, bf16[64,512]{1,0:T(8,128)(2,1)S(1)} %collective-permute-done.19.refs_1_, ...), custom_call_target="tpu_custom_call" | custom-call | tf_op jit(solution)/shard_map/pallas_call | solution.py:559
  (3 shorter events, 0.1 us)
Async XLA Ops:
  1.5 3.9 %collective-permute-start.1 = (f32[32,256]{1,0:T(8,128)S(1)}, f32[32,256]{1,0:T(8,128)S(1)}, u32[]{:S(2)}, u32[]{:S(2)}) collective-permute-start(f32[32,256]{1,0:T(8,128)S(1)} %maximum_multiply_fusion.refs_0_), channel_id=1, source_target_pairs={{0,1},{1,0},{2,3},{3,2},{4,5},{5,4},{6,7},{7,6},{8,9},{9,8},{10,11... | collective-permute-start | bytes 98312 | tf_op jit(solution)/shard_map/ppermute | solution.py:26
  1.5 10.9 %collective-permute-start = (f32[32,256]{1,0:T(8,128)S(1)}, f32[32,256]{1,0:T(8,128)S(1)}, u32[]{:S(2)}, u32[]{:S(2)}) collective-permute-start(f32[32,256]{1,0:T(8,128)S(1)} %maximum_multiply_fusion.refs_0_), channel_id=1, source_target_pairs={{0,4},{1,5},{2,6},{3,7},{4,0},{5,1},{6,2},{7,3},{8,12},{9,13},{10,... | collective-permute-start | bytes 98312 | tf_op jit(solution)/shard_map/ppermute | solution.py:26
  5.4 7.0 %collective-permute-start.4 = (f32[64,256]{1,0:T(8,128)S(1)}, f32[64,256]{1,0:T(8,128)S(1)}, u32[]{:S(2)}, u32[]{:S(2)}) collective-permute-start(f32[64,256]{1,0:T(8,128)S(1)} %pad_maximum_fusion), channel_id=1, source_target_pairs={{0,6},{1,13},{2,4},{3,15},{4,2},{5,9},{6,0},{7,11},{8,14},{9,5},{1... | collective-permute-start | bytes 196616 | tf_op jit(solution)/shard_map/ppermute | solution.py:26
  6.7 5.6 %collective-permute-start.3 = (f32[64,256]{1,0:T(8,128)S(1)}, f32[64,256]{1,0:T(8,128)S(1)}, u32[]{:S(2)}, u32[]{:S(2)}) collective-permute-start(f32[64,256]{1,0:T(8,128)S(1)} %pad_maximum_fusion), channel_id=1, source_target_pairs={{0,2},{1,15},{2,0},{3,13},{4,6},{5,11},{6,4},{7,9},{8,10},{9,7},{1... | collective-permute-start | bytes 196616 | tf_op jit(solution)/shard_map/ppermute | solution.py:26
  6.7 5.6 %collective-permute-start.2 = (f32[64,256]{1,0:T(8,128)S(1)}, f32[64,256]{1,0:T(8,128)S(1)}, u32[]{:S(2)}, u32[]{:S(2)}) collective-permute-start(f32[64,256]{1,0:T(8,128)S(1)} %pad_maximum_fusion), channel_id=1, source_target_pairs={{0,8},{1,11},{2,10},{3,9},{4,12},{5,15},{6,14},{7,13},{8,0},{9,3},... | collective-permute-start | bytes 196616 | tf_op jit(solution)/shard_map/ppermute | solution.py:26
  7.6 6.7 %copy-start = (s32[8,128]{1,0:T(8,128)S(1)}, s32[8,128]{1,0:T(8,128)}, u32[]{:S(2)}) copy-start(s32[8,128]{1,0:T(8,128)} %param.8) | copy-start | bytes 12292
  12.8 2.6 %collective-permute-start.5 = (f32[256,256]{1,0:T(8,128)S(1)}, f32[256,256]{1,0:T(8,128)S(1)}, u32[]{:S(2)}, u32[]{:S(2)}) collective-permute-start(f32[256,256]{1,0:T(8,128)S(1)} %shard_map.74.one_ref), channel_id=1, source_target_pairs={{0,1},{1,0},{2,3},{3,2},{4,5},{5,4},{6,7},{7,6},{8,9},{9,8},{10,11... | collective-permute-start | bytes 786440 | tf_op jit(solution)/shard_map/ppermute | solution.py:26
  15.4 5.0 %collective-permute-start.6 = (bf16[256,256]{1,0:T(8,128)(2,1)S(1)}, bf16[256,256]{1,0:T(8,128)(2,1)S(1)}, u32[]{:S(2)}, u32[]{:S(2)}) collective-permute-start(bf16[256,256]{1,0:T(8,128)(2,1)S(1)} %get-tuple-element.63.refs_0_.refs_6_), channel_id=1, source_target_pairs={{0,32},{1,57},{2,34},{3,59},{4,36},{5,61},{6,38},{7,63},{8,40},{9,... | collective-permute-start | bytes 393224 | tf_op jit(solution)/shard_map/ppermute | solution.py:26
  17.1 7.7 %collective-permute-start.7 = (bf16[256,256]{1,0:T(8,128)(2,1)S(1)}, bf16[256,256]{1,0:T(8,128)(2,1)S(1)}, u32[]{:S(2)}, u32[]{:S(2)}) collective-permute-start(bf16[256,256]{1,0:T(8,128)(2,1)S(1)} %get-tuple-element.63.refs_0_.refs_6_), channel_id=1, source_target_pairs={{0,96},{1,121},{2,98},{3,123},{4,100},{5,125},{6,102},{7,127},{8,1... | collective-permute-start | bytes 393224 | tf_op jit(solution)/shard_map/ppermute | solution.py:26
  19.3 5.5 %collective-permute-start.8 = (bf16[128,256]{1,0:T(8,128)(2,1)S(1)}, bf16[128,256]{1,0:T(8,128)(2,1)S(1)}, u32[]{:S(2)}, u32[]{:S(2)}) collective-permute-start(bf16[128,256]{1,0:T(8,128)(2,1)S(1)} %get-tuple-element.65), channel_id=1, source_target_pairs={{0,24},{1,25},{2,26},{3,27},{4,28},{5,29},{6,30},{7,31},{8,16},{9,... | collective-permute-start | bytes 196616 | tf_op jit(solution)/shard_map/ppermute | solution.py:26
  24.8 2.3 %collective-permute-start.9 = (bf16[256,256]{1,0:T(8,128)(2,1)S(1)}, bf16[256,256]{1,0:T(8,128)(2,1)S(1)}, u32[]{:S(2)}, u32[]{:S(2)}) collective-permute-start(bf16[256,256]{1,0:T(8,128)(2,1)S(1)} %collective-permute-done.6.refs_1_.first_ref.refs_7_), channel_id=1, source_target_pairs={{0,1},{1,0},{2,3},{3,2},{4,5},{5,4},{6,7},{7,6},{8,9},{9,8},{10,11... | collective-permute-start | bytes 393224 | tf_op jit(solution)/shard_map/ppermute | solution.py:26
  25.6 1.4 %collective-permute-start.10 = (bf16[256,256]{1,0:T(8,128)(2,1)S(1)}, bf16[256,256]{1,0:T(8,128)(2,1)S(1)}, u32[]{:S(2)}, u32[]{:S(2)}) collective-permute-start(bf16[256,256]{1,0:T(8,128)(2,1)S(1)} %collective-permute-done.7.second_ref.refs_0_.refs_8_.refs_2_), channel_id=1, source_target_pairs={{0,1},{1,0},{2,3},{3,2},{4,5},{5,4},{6,7},{7,6},{8,9},{9,8},{10,11... | collective-permute-start | bytes 393224 | tf_op jit(solution)/shard_map/ppermute | solution.py:26
  25.7 1.3 %collective-permute-start.11 = (bf16[128,256]{1,0:T(8,128)(2,1)S(1)}, bf16[128,256]{1,0:T(8,128)(2,1)S(1)}, u32[]{:S(2)}, u32[]{:S(2)}) collective-permute-start(bf16[128,256]{1,0:T(8,128)(2,1)S(1)} %collective-permute-done.8.refs_4_.refs_12_.refs_6_), channel_id=1, source_target_pairs={{0,1},{1,0},{2,3},{3,2},{4,5},{5,4},{6,7},{7,6},{8,9},{9,8},{10,11... | collective-permute-start | bytes 196616 | tf_op jit(solution)/shard_map/ppermute | solution.py:26
  26.1 5.0 %collective-permute-start.12 = (bf16[256,256]{1,0:T(8,128)(2,1)S(1)}, bf16[256,256]{1,0:T(8,128)(2,1)S(1)}, u32[]{:S(2)}, u32[]{:S(2)}) collective-permute-start(bf16[256,256]{1,0:T(8,128)(2,1)S(1)} %shard_map.78), channel_id=1, source_target_pairs={{0,32},{1,97},{2,34},{3,99},{4,36},{5,101},{6,38},{7,103},{8,40},{... | collective-permute-start | bytes 393224 | tf_op jit(solution)/shard_map/ppermute | solution.py:26
  31.1 1.3 %collective-permute-start.13 = (bf16[256,256]{1,0:T(8,128)(2,1)S(1)}, bf16[256,256]{1,0:T(8,128)(2,1)S(1)}, u32[]{:S(2)}, u32[]{:S(2)}) collective-permute-start(bf16[256,256]{1,0:T(8,128)(2,1)S(1)} %collective-permute-done.12.refs_0_.refs_13_.refs_7_), channel_id=1, source_target_pairs={{0,1},{1,0},{2,3},{3,2},{4,5},{5,4},{6,7},{7,6},{8,9},{9,8},{10,11... | collective-permute-start | bytes 393224 | tf_op jit(solution)/shard_map/ppermute | solution.py:26
  32.9 9.1 %collective-permute-start.14 = (bf16[64,512]{1,0:T(8,128)(2,1)S(1)}, bf16[64,512]{1,0:T(8,128)(2,1)S(1)}, u32[]{:S(2)}, u32[]{:S(2)}) collective-permute-start(bf16[64,512]{1,0:T(8,128)(2,1)S(1)} %get-tuple-element.85), channel_id=1, source_target_pairs={{0,16},{1,17},{2,18},{3,19},{4,20},{5,21},{6,22},{7,23},{8,24},{9,... | collective-permute-start | bytes 196616 | tf_op jit(solution)/shard_map/ppermute | solution.py:479
  33.8 8.2 %collective-permute-start.15 = (bf16[64,512]{1,0:T(8,128)(2,1)S(1)}, bf16[64,512]{1,0:T(8,128)(2,1)S(1)}, u32[]{:S(2)}, u32[]{:S(2)}) collective-permute-start(bf16[64,512]{1,0:T(8,128)(2,1)S(1)} %get-tuple-element.86), channel_id=1, source_target_pairs={{0,2},{1,3},{2,0},{3,1},{4,6},{5,7},{6,4},{7,5},{8,10},{9,11},{10,... | collective-permute-start | bytes 196616 | tf_op jit(solution)/shard_map/ppermute | solution.py:479
  36.7 2.4 %collective-permute-start.16 = (bf16[64,128]{1,0:T(8,128)(2,1)S(1)}, bf16[64,128]{1,0:T(8,128)(2,1)S(1)}, u32[]{:S(2)}, u32[]{:S(2)}) collective-permute-start(bf16[64,128]{1,0:T(8,128)(2,1)S(1)} %get-tuple-element.87), channel_id=1, source_target_pairs={{0,1},{1,0},{2,3},{3,2},{4,5},{5,4},{6,7},{7,6},{8,9},{9,8},{10,11... | collective-permute-start | bytes 49160 | tf_op jit(solution)/shard_map/ppermute | solution.py:479
  36.7 5.3 %collective-permute-start.17 = (bf16[64,128]{1,0:T(8,128)(2,1)S(1)}, bf16[64,128]{1,0:T(8,128)(2,1)S(1)}, u32[]{:S(2)}, u32[]{:S(2)}) collective-permute-start(bf16[64,128]{1,0:T(8,128)(2,1)S(1)} %get-tuple-element.88), channel_id=1, source_target_pairs={{0,32},{1,2},{2,1},{3,4},{4,3},{5,6},{6,5},{7,8},{8,7},{9,10},{10,... | collective-permute-start | bytes 49160 | tf_op jit(solution)/shard_map/ppermute | solution.py:479
  37.2 4.8 %copy-start.1 = (bf16[4,64,4]{1,2,0:T(4,128)(2,1)S(1)}, bf16[4,64,4]{1,2,0:T(4,128)(2,1)}, u32[]{:S(2)}) copy-start(bf16[4,64,4]{1,2,0:T(4,128)(2,1)} %param.10) | copy-start | bytes 6148
  37.2 4.8 %copy-start.2 = (s32[4]{0:T(128)S(1)}, s32[4]{0:T(128)}, u32[]{:S(2)}) copy-start(s32[4]{0:T(128)} %port_ref.3) | copy-start | bytes 52
  44.6 9.6 %collective-permute-start.18 = (bf16[64,512]{1,0:T(8,128)(2,1)S(1)}, bf16[64,512]{1,0:T(8,128)(2,1)S(1)}, u32[]{:S(2)}, u32[]{:S(2)}) collective-permute-start(bf16[64,512]{1,0:T(8,128)(2,1)S(1)} %get-tuple-element.91), channel_id=1, source_target_pairs={{0,16},{1,17},{2,18},{3,19},{4,20},{5,21},{6,22},{7,23},{8,24},{9,... | collective-permute-start | bytes 196616 | tf_op jit(solution)/shard_map/ppermute | solution.py:479
  45.1 9.1 %collective-permute-start.19 = (bf16[64,512]{1,0:T(8,128)(2,1)S(1)}, bf16[64,512]{1,0:T(8,128)(2,1)S(1)}, u32[]{:S(2)}, u32[]{:S(2)}) collective-permute-start(bf16[64,512]{1,0:T(8,128)(2,1)S(1)} %get-tuple-element.92), channel_id=1, source_target_pairs={{0,2},{1,3},{2,0},{3,1},{4,6},{5,7},{6,4},{7,5},{8,10},{9,11},{10,... | collective-permute-start | bytes 196616 | tf_op jit(solution)/shard_map/ppermute | solution.py:479
  48.9 4.3 %collective-permute-start.20 = (bf16[64,128]{1,0:T(8,128)(2,1)S(1)}, bf16[64,128]{1,0:T(8,128)(2,1)S(1)}, u32[]{:S(2)}, u32[]{:S(2)}) collective-permute-start(bf16[64,128]{1,0:T(8,128)(2,1)S(1)} %get-tuple-element.93), channel_id=1, source_target_pairs={{0,1},{1,0},{2,3},{3,2},{4,5},{5,4},{6,7},{7,6},{8,9},{9,8},{10,11... | collective-permute-start | bytes 49160 | tf_op jit(solution)/shard_map/ppermute | solution.py:479
  48.9 5.3 %collective-permute-start.21 = (bf16[64,128]{1,0:T(8,128)(2,1)S(1)}, bf16[64,128]{1,0:T(8,128)(2,1)S(1)}, u32[]{:S(2)}, u32[]{:S(2)}) collective-permute-start(bf16[64,128]{1,0:T(8,128)(2,1)S(1)} %get-tuple-element.94), channel_id=1, source_target_pairs={{0,32},{1,2},{2,1},{3,4},{4,3},{5,6},{6,5},{7,8},{8,7},{9,10},{10,... | collective-permute-start | bytes 49160 | tf_op jit(solution)/shard_map/ppermute | solution.py:479
